TPU v7x, 32 devices: a whole 2x2x4 slice. The times are simulated.
32 devices in a mesh: groups: 2 (over y), batch: 4 (over z), pair: 2 (over x), orb: 2 (over core).
Axes of the slice: x: 2, y: 2, z: 4, core: 2. Of those that a mesh axis runs over, the one named last changes fastest.
Arguments:
- basis_values: bfloat16 [64, 256, 512], P(('groups', 'batch', 'pair')), parts along dimension 0, may hold values from -6 to 6
- point_weights: float32 [64, 256], P(('groups', 'batch', 'pair')), parts along dimension 0, may hold values from 0.005 to 0.05
- slot_ids: int32 [64, 8, 8], P(('groups', 'batch', 'pair'), None, 'orb'), parts along dimension 0, may hold values from 0 to 63, as said below
- fetch_rows: int32 [16, 2, 8, 8], P(('groups', 'batch', 'pair'), 'orb'), parts along dimension 0, may hold values from 0 to 15, as said below
- density_blocks: bfloat16 [256, 4096], P(('groups', 'batch', 'pair')), parts along dimension 0, may hold values from -0.01171875 to 0.01171875
- core_blocks: bfloat16 [256, 4096], P(('groups', 'batch', 'pair')), parts along dimension 0, may hold values from -3 to 3
Outputs:
- kohn_sham: float32 [256, 4096], P(('groups', 'batch', 'pair')), parts along dimension 0
There are 2 independent parts, one for each index of `groups`. A program takes and returns all parts, laid end to end along the dimension named above; each array names one. Nothing has to cross between parts.
Inputs may be any that keep to these rules, and one draw needn't show every extreme that they name: `fetch_rows`: within one share the 32 slots named by slot_ids name distinct stored rows; the 8 rows of one owner in one share's table are distinct. `slot_ids`: each share's entries name exactly 32 distinct slots of its table; one owner has all 8 of its slots named in every share.
All inputs are finite; a program needn't handle non-finite values.
Results may differ from a plain program's by a relative error of at most 0.004.
Values may be sent and summed in bfloat16 or wider, within the bound.
No kernel may reach another device: no remote copies, remote signals or barrier semaphores. Data moves between devices by JAX's collectives and lax.ppermute only.
A program may use at most 64 MiB of HBM per device.

v0:
```python
import jax
import jax.numpy as jnp
from jax import lax
from jax.sharding import PartitionSpec as P

GO = 64


def per_device(basis_values, point_weights, slot_ids, fetch_rows, density_blocks, core_blocks):
    owners = lax.axis_size(("batch", "pair"))
    orb_index = lax.axis_index("orb")
    batches, points, columns = basis_values.shape
    groups = slot_ids.shape[1]
    own_groups = slot_ids.shape[2]
    held_blocks = density_blocks.shape[0]
    square = density_blocks.shape[1]
    capacity = fetch_rows.shape[3]
    entries = batches * groups * own_groups
    slot_flat = slot_ids.reshape(-1)
    wanted = fetch_rows.reshape(owners, capacity)
    asked_ids = lax.all_to_all(wanted, ("batch", "pair"), split_axis=0, concat_axis=0, tiled=True)
    served = density_blocks[asked_ids.reshape(-1)].reshape(owners, capacity, square)
    arrived = lax.all_to_all(
        served, ("batch", "pair"), split_axis=0, concat_axis=0, tiled=True
    ).reshape(owners * capacity, square)
    needed = arrived[slot_flat].reshape(batches, groups, own_groups, GO, GO)
    dense_cols = needed.transpose(0, 1, 3, 2, 4).reshape(batches, groups * GO, own_groups * GO)
    own_values = lax.dynamic_slice_in_dim(
        basis_values, orb_index * own_groups * GO, own_groups * GO, 2
    )
    product = jnp.einsum(
        "bpc,bcd->bpd", basis_values, dense_cols, preferred_element_type=jnp.float32
    )
    partial_sum = jnp.sum(product * own_values.astype(jnp.float32), axis=2)
    density = lax.psum(partial_sum, "orb")
    potential = point_weights * jnp.tanh(density)
    weighted = (own_values.astype(jnp.float32) * potential[:, :, None]).astype(jnp.bfloat16)
    hamil = jnp.einsum("bpc,bpd->bcd", basis_values, weighted, preferred_element_type=jnp.float32)
    pieces = hamil.reshape(batches, groups, GO, own_groups, GO)
    pieces = pieces.transpose(0, 1, 3, 2, 4).reshape(entries, square)
    table_sum = jnp.zeros((owners * capacity, square), jnp.float32).at[slot_flat].add(pieces)
    outgoing = table_sum.astype(jnp.bfloat16)
    returned = lax.all_to_all(
        outgoing.reshape(owners, capacity, square),
        ("batch", "pair"),
        split_axis=0,
        concat_axis=0,
        tiled=True,
    )
    selector = (
        asked_ids.reshape(-1)[None, :] == jnp.arange(held_blocks, dtype=jnp.int32)[:, None]
    ).astype(jnp.bfloat16)
    plane_sum = jnp.dot(
        selector, returned.reshape(owners * capacity, square), preferred_element_type=jnp.float32
    )
    total = lax.psum(plane_sum, "orb")
    return total + core_blocks.astype(jnp.float32)


def solution(mesh):
    placed = (
        P(("groups", "batch", "pair"), None, None),
        P(("groups", "batch", "pair"), None),
        P(("groups", "batch", "pair"), None, "orb"),
        P(("groups", "batch", "pair"), "orb", None, None),
        P(("groups", "batch", "pair"), None),
        P(("groups", "batch", "pair"), None),
    )
    return jax.shard_map(
        per_device,
        mesh=mesh,
        in_specs=placed,
        out_specs=P(("groups", "batch", "pair"), None),
        check_vma=False,
    )
```

profile of v0, /device:TPU:0, one launch (start us, length us, event | category | flops | bytes accessed | tf_op | source)
XLA Modules:
  0.0 119.3 jit_solution(7338338615750078686)
XLA Ops:
  6.5 0.0 copy-start
  6.5 13.8 %all_to_all.19 = s32[8,1,8]{2,1,0:T(1,128)S(1)} all-to-all(s32[8,1,8]{2,1,0:T(1,128)} %bitcast.40), channel_id=1, replica_groups=mesh['groups'=2,'batch'=4,'pair'=2,'orb'=2] {'batch','pair'}, dimensions={0} | all-to-all | bytes 512 | tf_op jit(solution)/shard_map/all_to_all | solution.py:21
  20.3 0.1 reshape.95
  20.4 0.0 copy-start.3
  20.4 3.1 %gather_fusion = bf16[64,4096]{1,0:T(8,128)(2,1)} fusion(bf16[16,4096]{1,0:T(8,128)(2,1)} %param.10, s32[1024]{0:T(1024)S(1)} %pad_clamp_fusion.1), kind=kCustom, calls=%fused_computation | custom fusion | bytes 1048832 | tf_op jit(solution)/shard_map/gather | solution.py:22
  23.5 3.5 %all-to-all-start.1 = ((bf16[8,8,4096]{2,1,0:T(8,128)(2,1)}), bf16[8,8,4096]{2,1,0:T(8,128)(2,1)S(1)}, u32[]{:S(2)}, u32[]{:S(2)}) async-start(bf16[8,8,4096]{2,1,0:T(8,128)(2,1)} %bitcast.4), calls=%async_computation.1 | async-start | bytes 1048576 | tf_op jit(solution)/shard_map/all_to_all | solution.py:23
  27.0 0.0 copy-done.3
  27.0 0.1 copy.14
  27.1 0.1 reshape.94
  27.2 0.0 copy-done
  27.3 1.0 copy.18
  28.3 12.0 %all-to-all-done.1 = bf16[8,8,4096]{2,1,0:T(8,128)(2,1)S(1)} async-done(((bf16[8,8,4096]{2,1,0:T(8,128)(2,1)}), bf16[8,8,4096]{2,1,0:T(8,128)(2,1)S(1)}, u32[]{:S(2)}, u32[]{:S(2)}) %all-to-all-start.1) | async-done | bytes 524320 | tf_op jit(solution)/shard_map/all_to_all | solution.py:23
  40.3 2.2 %gather_fusion.1 = bf16[128,4096]{1,0:T(8,128)(2,1)} fusion(bf16[64,4096]{1,0:T(8,128)(2,1)S(1)} %bitcast.36, s32[1024]{0:T(1024)S(1)} %pad_clamp_fusion), kind=kCustom, calls=%fused_computation.1 | custom fusion | bytes 2097664 | tf_op jit(solution)/shard_map/gather | solution.py:26
  42.4 3.3 %reshape.98 = bf16[4,8,4,64,64]{4,3,2,1,0:T(8,128)(2,1)S(1)} reshape(bf16[128,4096]{1,0:T(8,128)(2,1)} %gather_fusion.1) | data formatting | bytes 2097152 | tf_op jit(solution)/shard_map/reshape | solution.py:26
  45.7 2.6 %copy.16 = bf16[4,8,4,64,64]{3,1,4,2,0:T(8,128)(2,1)} copy(bf16[4,8,4,64,64]{4,3,2,1,0:T(8,128)(2,1)S(1)} %reshape.98) | data formatting | bytes 2097152 | tf_op jit(solution)/shard_map/reshape | solution.py:26
  48.3 0.0 copy-start.1
  48.3 3.2 %reshape.99 = bf16[4,512,256]{1,2,0:T(8,128)(2,1)S(1)} reshape(bf16[4,8,64,4,64]{2,1,4,3,0:T(8,128)(2,1)} %bitcast.38) | data formatting | bytes 2097152 | tf_op jit(solution)/shard_map/reshape | solution.py:27
  51.6 0.0 copy-done.1
  51.6 0.0 copy-start.4
  51.6 0.5 fusion.1
  52.1 2.5 %psum.14 = f32[4,256]{1,0:T(4,128)S(1)} all-reduce(f32[4,256]{1,0:T(4,128)S(1)} %fusion.1), channel_id=1, replica_groups=mesh['groups'=2,'batch'=4,'pair'=2,'orb'=2] {'orb'}, use_global_device_ids=true, to_apply=%region_1.0 | all-reduce | flops 1024 | bytes 8192 | tf_op jit(solution)/shard_map/psum | solution.py:35
  54.5 0.0 copy-done.4
  54.6 1.5 %convolution_bitcast_fusion = f32[4,512,256]{1,2,0:T(8,128)S(1)} fusion(bf16[4,256,512]{2,1,0:T(8,128)(2,1)S(1)} %copy-done, bf16[4,256,256]{1,2,0:T(8,128)(2,1)} %copy.18, f32[4,256]{1,0:T(4,128)S(1)} %tanh_multiply_fusion), kind=kOutput, calls=%fused_computation.3 | convolution fusion | flops 269221888 | bytes 3674112 | tf_op jit(solution)/shard_map/bpc,bpd->bcd/dot_general | solution.py:38
  56.1 2.4 %reshape.100 = f32[4,8,64,4,64]{2,1,4,3,0:T(8,128)} reshape(f32[4,512,256]{1,2,0:T(8,128)S(1)} %convolution_bitcast_fusion) | data formatting | bytes 4194304 | tf_op jit(solution)/shard_map/reshape | solution.py:39
  58.5 5.2 %copy.17 = f32[4,8,64,4,64]{4,2,3,1,0:T(8,128)} copy(f32[4,8,64,4,64]{2,1,4,3,0:T(8,128)} %reshape.100) | data formatting | bytes 4194304 | tf_op jit(solution)/shard_map/reshape | solution.py:39
  63.7 4.8 %reshape.124 = f32[128,4096]{1,0:T(8,128)} reshape(f32[4,8,4,64,64]{4,3,2,1,0:T(8,128)} %bitcast.37) | data formatting | bytes 4194304 | tf_op jit(solution)/shard_map/reshape | solution.py:40
  68.5 4.5 %scatter_custom_fusion = f32[64,4096]{1,0:T(8,128)S(1)} fusion(s32[128]{0:T(128)S(1)} %fusion.10, f32[128,4096]{1,0:T(8,128)} %reshape.124, f32[]{:T(128)} %constant.7.clone.1), kind=kCustom, calls=%fused_computation.13 | custom fusion | flops 524288 | bytes 1049088 | tf_op jit(solution)/shard_map/scatter-add | solution.py:41
  73.0 0.0 copy-start.2
  73.0 0.8 convert_bitcast_fusion
  73.9 3.7 %all-to-all-start.2 = ((bf16[8,8,4096]{2,1,0:T(8,128)(2,1)}), bf16[8,8,4096]{2,1,0:T(8,128)(2,1)S(1)}, u32[]{:S(2)}, u32[]{:S(2)}) async-start(bf16[8,8,4096]{2,1,0:T(8,128)(2,1)} %convert_bitcast_fusion), calls=%async_computation.2 | async-start | bytes 1048576 | tf_op jit(solution)/shard_map/all_to_all | solution.py:43
  77.5 0.0 all-reduce.2.cloned.1.call-start
  77.6 0.5 broadcast.52
  78.1 0.7 reduce.5
  78.8 0.1 eq.15
  78.8 13.5 %all-to-all-done.2 = bf16[8,8,4096]{2,1,0:T(8,128)(2,1)S(1)} async-done(((bf16[8,8,4096]{2,1,0:T(8,128)(2,1)}), bf16[8,8,4096]{2,1,0:T(8,128)(2,1)S(1)}, u32[]{:S(2)}, u32[]{:S(2)}) %all-to-all-start.2) | async-done | bytes 524320 | tf_op jit(solution)/shard_map/all_to_all | solution.py:43
  92.4 0.9 fusion.4
  93.3 0.0 all-reduce.2.cloned.1.call-update
  93.3 17.5 %all-reduce.2.cloned.1.call-done = f32[16,4096]{1,0:T(8,128)} async-done(((f32[16,4096]{1,0:T(8,128)}), f32[16,4096]{1,0:T(8,128)}) %all-reduce.2.cloned.1.call-update) | async-done | bytes 262160 | tf_op jit(solution)/shard_map/psum | solution.py:56
  110.8 0.0 copy-done.2
  110.8 1.7 %convert_add_fusion = f32[16,4096]{1,0:T(8,128)} fusion(f32[16,4096]{1,0:T(8,128)} %all-reduce.2.cloned.1.call-done, bf16[16,4096]{1,0:T(8,128)(2,1)S(1)} %copy-done.2), kind=kLoop, calls=%fused_computation.15 | loop fusion | flops 131072 | bytes 655360 | tf_op jit(solution)/shard_map/add | solution.py:57
  (6 shorter events, 0.1 us)
Async XLA Ops:
  6.5 20.7 %copy-start = (bf16[4,256,512]{2,1,0:T(8,128)(2,1)S(1)}, bf16[4,256,512]{2,1,0:T(8,128)(2,1)}, u32[]{:S(2)}) copy-start(bf16[4,256,512]{2,1,0:T(8,128)(2,1)} %param.6) | copy-start | bytes 3145732
  20.4 6.6 %copy-start.3 = (s32[4,8,4]{1,2,0:T(4,128)S(1)}, s32[4,8,4]{1,2,0:T(4,128)}, u32[]{:S(2)}) copy-start(s32[4,8,4]{1,2,0:T(4,128)} %param.8) | copy-start | bytes 1540
  23.5 16.8 %all-to-all-start.1 = ((bf16[8,8,4096]{2,1,0:T(8,128)(2,1)}), bf16[8,8,4096]{2,1,0:T(8,128)(2,1)S(1)}, u32[]{:S(2)}, u32[]{:S(2)}) async-start(bf16[8,8,4096]{2,1,0:T(8,128)(2,1)} %bitcast.4), calls=%async_computation.1 | async-start | bytes 1048576 | tf_op jit(solution)/shard_map/all_to_all | solution.py:23
  48.3 3.3 %copy-start.1 = (bf16[4,256,256]{1,2,0:T(8,128)(2,1)S(1)}, bf16[4,256,256]{1,2,0:T(8,128)(2,1)}, u32[]{:S(2)}) copy-start(bf16[4,256,256]{1,2,0:T(8,128)(2,1)} %copy.18) | copy-start | bytes 1572868
  51.6 3.0 %copy-start.4 = (f32[4,256]{1,0:T(4,128)S(1)}, f32[4,256]{1,0:T(4,128)}, u32[]{:S(2)}) copy-start(f32[4,256]{1,0:T(4,128)} %param.7) | copy-start | bytes 12292
  73.0 37.8 %copy-start.2 = (bf16[16,4096]{1,0:T(8,128)(2,1)S(1)}, bf16[16,4096]{1,0:T(8,128)(2,1)}, u32[]{:S(2)}) copy-start(bf16[16,4096]{1,0:T(8,128)(2,1)} %param.11) | copy-start | bytes 393220
  73.9 18.5 %all-to-all-start.2 = ((bf16[8,8,4096]{2,1,0:T(8,128)(2,1)}), bf16[8,8,4096]{2,1,0:T(8,128)(2,1)S(1)}, u32[]{:S(2)}, u32[]{:S(2)}) async-start(bf16[8,8,4096]{2,1,0:T(8,128)(2,1)} %convert_bitcast_fusion), calls=%async_computation.2 | async-start | bytes 1048576 | tf_op jit(solution)/shard_map/all_to_all | solution.py:43
  77.5 33.2 %all-reduce.2.cloned.1.call-start = ((), (), s32[]{:S(2)}) async-start(), calls=%async_computation.3 | async-start | bytes 524288 | tf_op jit(solution)/shard_map/psum | solution.py:56
Sparse Core Ops, SparseCore 0:
  93.4 17.3 all-reduce.1
where the time goes:
time: 120 us; the launch traced here: 119 us
  waiting for transfers between devices  43 us (36%)
  local copies, waits for them, and re-layouts  28.7 us (24%)
  blocking collectives  16.2 us (14%)
  between operations  13.5 us (11%)
  other arithmetic  7.74 us (6%)
  starting transfers between devices  7.19 us (6%)
  matrix products  2.87 us (2%)
    psum x1, waiting for transfers between devices, per_device(): total = lax.psum(plane_sum, 'orb')  17.5 us
    all_to_all x1, blocking collectives, per_device(): lax.all_to_all(wanted, ('batch', 'pair'), split_axis=0, concat_axis=0, ti...  13.8 us
    all_to_all x1, waiting for transfers between devices, per_device(): lax.all_to_all(outgoing.reshape(owners, capacity, square), ('batch', 'pai...  13.5 us
    all_to_all x1, waiting for transfers between devices, per_device(): lax.all_to_all(served, ('batch', 'pair'), split_axis=0, concat_axis=0, ti...  12 us
    reshape x2, local copies, waits for them, and re-layouts, per_device(): pieces = hamil.reshape(batches, groups, GO, own_groups, GO)  7.65 us
    reshape x2, local copies, waits for them, and re-layouts, per_device(): needed = arrived[slot_flat].reshape(batches, groups, own_groups, GO, GO)  5.86 us
    reshape x1, local copies, waits for them, and re-layouts, per_device(): pieces = pieces.transpose(0, 1, 3, 2, 4).reshape(entries, square)  4.77 us
    scatter-add x1, other arithmetic, per_device(): jnp.zeros((owners * capacity, square), jnp.float32).at[slot_flat]  4.53 us
  transfers between devices with their start and end apart: 3, of which 3 were waited for; matrix products, arithmetic and copies ran while one was open for 2% of the time, Pallas kernels for 0%

commit v1 on v0

v1 whole, which is shorter than its diff:
```python
import functools

import jax
import jax.numpy as jnp
from jax import lax
from jax.experimental import pallas as pl
from jax.experimental.pallas import tpu as pltpu
from jax.sharding import PartitionSpec as P

GO = 64
VMEM_LIMIT = 50 * 1024 * 1024
NT = (((1,), (1,)), ((), ()))


def split_dot(left, right, dims=None):
    if dims is None:
        return jnp.dot(left, right, preferred_element_type=jnp.float32)
    return lax.dot_general(left, right, dims, preferred_element_type=jnp.float32)


def prepare_kernel(half_ref, rows_ref, values_ref, left_ref, left_t_ref, pick_ref, put_ref):
    batches, points, columns = values_ref.shape
    groups = columns // GO
    kept = left_ref.shape[2]
    per_half = kept // groups
    first = half_ref[0] * per_half
    at = lax.broadcasted_iota(jnp.int32, (kept, columns), 0)
    lane = lax.broadcasted_iota(jnp.int32, (kept, columns), 1)
    wanted = (at % groups) * GO + first + at // groups
    select = jnp.where(lane == wanted, 1.0, 0.0).astype(jnp.bfloat16)
    for t in range(batches):
        left_ref[t] = split_dot(values_ref[t], select, NT).astype(jnp.bfloat16)
        left_t_ref[t] = split_dot(select, values_ref[t], NT).astype(jnp.bfloat16)
    table_rows, entries = put_ref.shape
    row = lax.broadcasted_iota(jnp.int32, (table_rows, entries), 0)
    hot = jnp.where(row == rows_ref[...], 1.0, 0.0)
    put_ref[...] = hot.astype(jnp.bfloat16)
    pick_ref[...] = hot.T.astype(jnp.bfloat16)


def density_kernel(pieces, *refs):
    piece_refs = refs[:pieces]
    pick_ref, left_ref, values_ref, out_ref, table, dense = refs[pieces:]
    held = piece_refs[0].shape[0]
    batches, points, columns = values_ref.shape
    groups = columns // GO
    for k in range(pieces):
        table[k * held:(k + 1) * held, :] = piece_refs[k][...]
    low = lax.broadcasted_iota(jnp.int32, (1, 1, groups, 128), 3) < GO
    for j in range(table.shape[1] // 128):
        lanes = slice(j * 128, (j + 1) * 128)
        got = split_dot(pick_ref[...], table[:, lanes])
        got = got.reshape(batches, groups // 2, 2, groups, 128)
        even, odd = got[:, :, 0], got[:, :, 1]
        first = jnp.where(low, even, pltpu.roll(odd, GO, 3))
        second = jnp.where(low, pltpu.roll(even, GO, 3), odd)
        for t in range(batches):
            for q in range(groups // 2):
                both = jnp.concatenate([first[t, q], second[t, q]], axis=0)
                dense[t, j * 2 * groups:(j + 1) * 2 * groups, q * 128:(q + 1) * 128] = both.astype(jnp.bfloat16)
    for t in range(batches):
        product = split_dot(left_ref[t], dense[t]) * values_ref[t].astype(jnp.float32)
        folded = product[:, :128]
        for q in range(1, columns // 128):
            folded = folded + product[:, q * 128:(q + 1) * 128]
        out_ref[t:t + 1, :] = jnp.sum(folded.T, axis=0, keepdims=True)


def scatter_kernel(pieces, *refs):
    mine_ref, other_ref, weight_ref, values_ref, left_t_ref, put_ref = refs[:6]
    out_refs = refs[6:6 + pieces]
    high, rest = refs[6 + pieces:]
    held = out_refs[0].shape[0]
    batches, points, columns = values_ref.shape
    groups = columns // GO
    kept = left_t_ref.shape[1]
    steps = kept // (2 * groups)
    potential = weight_ref[...] * jnp.tanh(mine_ref[...] + other_ref[...])
    low = lax.broadcasted_iota(jnp.int32, (1, groups, 128), 2) < GO
    for t in range(batches):
        factor = jnp.broadcast_to(potential[t:t + 1, :], (128, points)).T
        factor = jnp.concatenate([factor] * (columns // 128), axis=1)
        weighted = (values_ref[t].astype(jnp.float32) * factor).astype(jnp.bfloat16)
        part = split_dot(left_t_ref[t], weighted)
        for q in range(groups // 2):
            cut = part[:, q * 128:(q + 1) * 128].reshape(steps, 2, groups, 128)
            first, second = cut[:, 0], cut[:, 1]
            even = jnp.where(low, first, pltpu.roll(second, GO, 2))
            odd = jnp.where(low, pltpu.roll(first, GO, 2), second)
            at = (t * groups + 2 * q) * groups
            for j in range(steps):
                both = jnp.concatenate([even[j], odd[j]], axis=0)
                top = both.astype(jnp.bfloat16)
                high[at:at + 2 * groups, j * 128:(j + 1) * 128] = top
                rest[at:at + 2 * groups, j * 128:(j + 1) * 128] = (both - top.astype(jnp.float32)).astype(jnp.bfloat16)
    step = max(1, min(pieces, 128 // held))
    for k in range(0, pieces, step):
        some = put_ref[k * held:(k + step) * held, :]
        total = split_dot(some, high[...]) + split_dot(some, rest[...])
        for i in range(step):
            out_refs[k + i][...] = total[i * held:(i + 1) * held, :].astype(jnp.bfloat16)


def sum_kernel(*refs):
    out_ref = refs[-1]
    total = refs[0][...].astype(jnp.float32)
    for ref in refs[1:-1]:
        total = total + ref[...].astype(jnp.float32)
    out_ref[...] = total.astype(out_ref.dtype)


def finish_kernel(half_ref, mine_ref, other_ref, core_ref, out_ref):
    wide = mine_ref.shape[1]
    own = pl.multiple_of(half_ref[0] * wide, wide)
    far = pl.multiple_of((1 - half_ref[0]) * wide, wide)
    out_ref[:, pl.ds(own, wide)] = core_ref[:, pl.ds(own, wide)].astype(jnp.float32) + mine_ref[...]
    out_ref[:, pl.ds(far, wide)] = core_ref[:, pl.ds(far, wide)].astype(jnp.float32) + other_ref[...]


def call(kernel, outs, count, scratch=(), scalar=False, flops=0, moved=0):
    specs = [pl.BlockSpec(memory_space=pltpu.VMEM)] * count
    if scalar:
        specs = [pl.BlockSpec(memory_space=pltpu.SMEM)] + specs
    out_specs = jax.tree.map(lambda _: pl.BlockSpec(memory_space=pltpu.VMEM), outs)
    return pl.pallas_call(
        kernel,
        out_shape=outs,
        in_specs=specs,
        out_specs=out_specs,
        scratch_shapes=list(scratch),
        compiler_params=pltpu.CompilerParams(vmem_limit_bytes=VMEM_LIMIT),
        cost_estimate=pl.CostEstimate(flops=flops, bytes_accessed=moved, transcendentals=0),
    )


def from_ahead(array, axis, count, step):
    return lax.ppermute(array, axis, [((i + step) % count, i) for i in range(count)])


def to_ahead(array, axis, count, step):
    return lax.ppermute(array, axis, [(i, (i + step) % count) for i in range(count)])


def per_device(basis_values, point_weights, slot_ids, fetch_rows, density_blocks, core_blocks):
    rows_z, rows_x = lax.axis_size("batch"), lax.axis_size("pair")
    z, x, half = lax.axis_index("batch"), lax.axis_index("pair"), lax.axis_index("orb")
    owners = rows_z * rows_x
    batches, points, columns = basis_values.shape
    groups, own_groups = slot_ids.shape[1], slot_ids.shape[2]
    held, square = density_blocks.shape
    capacity = fetch_rows.shape[3]
    wide = square // 2
    table_rows = owners * held
    entries = batches * groups * groups
    kept = columns // 2
    bf16, f32 = jnp.bfloat16, jnp.float32

    owner = jnp.arange(owners, dtype=jnp.int32)
    ahead = ((owner // rows_x - z) % rows_z) * rows_x + (owner % rows_x - x) % rows_x
    home = (ahead[:, None] * held + fetch_rows.reshape(owners, capacity)).reshape(-1)
    slots = jnp.arange(owners * capacity, dtype=jnp.int32)
    own_rows = jnp.sum(jnp.where(slot_ids[..., None] == slots, home, 0), axis=-1)
    own_rows = own_rows.transpose(0, 2, 1).astype(jnp.int32)
    other_rows = lax.ppermute(own_rows, "orb", [(0, 1), (1, 0)])
    rows = jnp.concatenate(
        [jnp.where(half == 0, own_rows, other_rows), jnp.where(half == 0, other_rows, own_rows)], axis=1
    ).reshape(1, entries)
    half_at = half.reshape(1).astype(jnp.int32)

    mine = lax.dynamic_slice_in_dim(density_blocks, half * wide, wide, 1)
    pieces = []
    for dz in range(rows_z):
        base = mine if dz == 0 else from_ahead(mine, "batch", rows_z, dz)
        pieces.append(base)
        for dx in range(1, rows_x):
            pieces.append(from_ahead(base, "pair", rows_x, dx))
    count = len(pieces)

    left, left_t, pick, put = call(
        prepare_kernel,
        (
            jax.ShapeDtypeStruct((batches, points, kept), bf16),
            jax.ShapeDtypeStruct((batches, kept, points), bf16),
            jax.ShapeDtypeStruct((entries, table_rows), bf16),
            jax.ShapeDtypeStruct((table_rows, entries), bf16),
        ),
        2,
        scalar=True,
        flops=4 * batches * points * columns * kept,
        moved=3 * batches * points * columns * 2,
    )(half_at, rows, basis_values)

    partial = call(
        functools.partial(density_kernel, count),
        jax.ShapeDtypeStruct((batches, points), f32),
        count + 3,
        scratch=(pltpu.VMEM((table_rows, wide), bf16), pltpu.VMEM((batches, kept, columns), bf16)),
        flops=2 * batches * points * columns * kept,
        moved=2 * batches * points * columns * 2,
    )(*pieces, pick, left, basis_values)
    partial_other = lax.ppermute(partial, "orb", [(0, 1), (1, 0)])

    sums = call(
        functools.partial(scatter_kernel, count),
        [jax.ShapeDtypeStruct((held, wide), bf16)] * count,
        6,
        scratch=(pltpu.VMEM((entries, wide), bf16), pltpu.VMEM((entries, wide), bf16)),
        flops=2 * batches * points * columns * kept,
        moved=2 * batches * points * columns * 2,
    )(partial, partial_other, point_weights, basis_values, left_t, put)

    landed = []
    for dz in range(rows_z - 1, -1, -1):
        terms = [sums[dz * rows_x]]
        for dx in range(1, rows_x):
            terms.append(to_ahead(sums[dz * rows_x + dx], "pair", rows_x, dx))
        if dz == 0:
            landed.extend(terms)
            continue
        joined = terms[0].astype(f32)
        for term in terms[1:]:
            joined = joined + term.astype(f32)
        landed.append(to_ahead(joined.astype(bf16), "batch", rows_z, dz))
    total = call(
        sum_kernel, jax.ShapeDtypeStruct((held, wide), f32), len(landed), moved=len(landed) * held * wide * 2
    )(*landed)
    total_other = lax.ppermute(total, "orb", [(0, 1), (1, 0)])
    return call(
        finish_kernel, jax.ShapeDtypeStruct((held, square), f32), 3, scalar=True, moved=held * square * 12
    )(half_at, total, total_other, core_blocks)


def solution(mesh):
    placed = (
        P(("groups", "batch", "pair"), None, None),
        P(("groups", "batch", "pair"), None),
        P(("groups", "batch", "pair"), None, "orb"),
        P(("groups", "batch", "pair"), "orb", None, None),
        P(("groups", "batch", "pair"), None),
        P(("groups", "batch", "pair"), None),
    )
    return jax.shard_map(
        per_device,
        mesh=mesh,
        in_specs=placed,
        out_specs=P(("groups", "batch", "pair"), None),
        check_vma=False,
    )
```

time: 120 us -> 38.8 us (0.32)
  waiting for transfers between devices: 43 us -> 10.5 us
  local copies, waits for them, and re-layouts: 28.7 us -> 2.72 us
  blocking collectives: 16.2 us -> 0 us
  starting transfers between devices: 7.19 us -> 20.8 us
  between operations: 13.5 us -> 0.13 us
  other arithmetic: 7.74 us -> 0.52 us
  Pallas kernels: 0 us -> 3.95 us
  matrix products: 2.87 us -> 0 us
    all_to_all x2 -> x0, waiting for transfers between devices: 25.5 us -> none  [the longest x1 13.5 us: per_device(): lax.all_to_all(outgoing.reshape(owners, capacity, square), ('batch', 'pai...]
    reshape x8 -> x2, local copies, waits for them, and re-layouts: 21.7 us -> 0.17 us  [the longest x1 0.09 us: per_device(): rows = jnp.concatenate([jnp.where(half == 0, own_rows, other_rows), jnp.w...]
    ppermute x0 -> x17, starting transfers between devices: none -> 20.8 us  [the longest x7 11.1 us: from_ahead(): lax.ppermute(array, axis, [((i + step) % count, i) for i in range(count)])]
    psum x1 -> x0, waiting for transfers between devices: 17.5 us -> none  [per_device(): total = lax.psum(plane_sum, 'orb')]
    all_to_all x1 -> x0, blocking collectives: 13.8 us -> none  [per_device(): lax.all_to_all(wanted, ('batch', 'pair'), split_axis=0, concat_axis=0, ti...]
    ppermute x0 -> x17, waiting for transfers between devices: none -> 10.5 us  [the longest x7 5.09 us: to_ahead(): lax.ppermute(array, axis, [(i, (i + step) % count) for i in range(count)])]
    all_to_all x2 -> x0, starting transfers between devices: 7.15 us -> none  [the longest x1 3.66 us: per_device(): lax.all_to_all(outgoing.reshape(owners, capacity, square), ('batch', 'pai...]
    gather x2 -> x0, local copies, waits for them, and re-layouts: 5.27 us -> none  [the longest x1 3.09 us: per_device(): density_blocks[asked_ids.reshape(-1)].reshape(owners, capacity, square)]
  transfers between devices with their start and end apart: 3 -> 17, of which waited for: 3 -> 8; matrix products, arithmetic and copies ran while one was open for 2% -> 0% of each run, Pallas kernels for 0% -> 2%
where the time goes in v1:
time: 38.8 us; the launch traced here: 38.6 us
  starting transfers between devices  20.8 us (54%)
  waiting for transfers between devices  10.5 us (27%)
  Pallas kernels  3.95 us (10%)
  local copies, waits for them, and re-layouts  2.72 us (7%)
  other arithmetic  0.52 us (1%)
    ppermute x7, starting transfers between devices, from_ahead(): lax.ppermute(array, axis, [((i + step) % count, i) for i in range(count)])  11.1 us
    ppermute x7, starting transfers between devices, to_ahead(): lax.ppermute(array, axis, [(i, (i + step) % count) for i in range(count)])  9.08 us
    ppermute x7, waiting for transfers between devices, to_ahead(): lax.ppermute(array, axis, [(i, (i + step) % count) for i in range(count)])  5.09 us
    ppermute x7, waiting for transfers between devices, from_ahead(): lax.ppermute(array, axis, [((i + step) % count, i) for i in range(count)])  2.88 us
    unnamed x14, local copies, waits for them, and re-layouts  2.4 us
    pallas_call x1, Pallas kernels, per_device(): call(functools.partial(scatter_kernel, count), [jax.ShapeDtypeStruct((hel...  1.39 us
    ppermute x1, waiting for transfers between devices, per_device(): total_other = lax.ppermute(total, 'orb', [(0, 1), (1, 0)])  1.33 us
    ppermute x1, waiting for transfers between devices, per_device(): partial_other = lax.ppermute(partial, 'orb', [(0, 1), (1, 0)])  1.15 us
  transfers between devices with their start and end apart: 17, of which 8 were waited for; matrix products, arithmetic and copies ran while one was open for 0% of the time, Pallas kernels for 2%

profile of v1, /device:TPU:0, one launch (start us, length us, event | category | flops | bytes accessed | tf_op | source)
XLA Modules:
  0.0 38.6 jit_solution(13757246932506170838)
XLA Ops:
  0.0 0.0 copy-start
  0.0 0.7 %copy-done.6 = s32[1,1,8,8]{3,2,1,0:T(8,128)S(1)} copy-done((s32[1,1,8,8]{3,2,1,0:T(8,128)S(1)}, s32[1,1,8,8]{3,2,1,0:T(8,128)}, u32[]{:S(2)}) %copy-start.6) | copy-done | bytes 280
  0.7 0.1 reshape.62
  0.8 0.1 add.66
  0.9 0.1 add.67
  1.0 0.4 %copy-done.5 = s32[4,8,4]{1,2,0:T(4,128)S(1)} copy-done((s32[4,8,4]{1,2,0:T(4,128)S(1)}, s32[4,8,4]{1,2,0:T(4,128)}, u32[]{:S(2)}) %copy-start.5) | copy-done | bytes 536
  1.4 0.4 %select_reduce_fusion = s32[4,8,4]{1,2,0:T(4,128)S(1)} fusion(s32[64]{0:T(128)S(1)} %add.68, s32[4,8,4]{1,2,0:T(4,128)S(1)} %copy-done.5), kind=kLoop, calls=%fused_computation.3 | loop fusion | flops 24448 | bytes 1280 | tf_op jit(solution)/shard_map/reduce_sum | solution.py:162
  1.8 0.5 %collective-permute-start.7 = (s32[4,4,8]{2,1,0:T(4,128)S(1)}, s32[4,4,8]{2,1,0:T(4,128)S(1)}, u32[]{:S(2)}, u32[]{:S(2)}) collective-permute-start(s32[4,4,8]{2,1,0:T(4,128)S(1)} %bitcast.6), channel_id=1, source_target_pairs={{0,1},{1,0},{2,3},{3,2},{4,5},{5,4},{6,7},{7,6},{8,9},{9,8},{10,11... | collective-permute-start | bytes 1544 | tf_op jit(solution)/shard_map/ppermute | solution.py:164
  2.4 2.7 %collective-permute-start.5 = (bf16[16,2048]{1,0:T(8,128)(2,1)S(1)}, bf16[16,2048]{1,0:T(8,128)(2,1)S(1)}, u32[]{:S(2)}, u32[]{:S(2)}) collective-permute-start(bf16[16,2048]{1,0:T(8,128)(2,1)S(1)} %constant_dynamic-slice_fusion.refs_0_), channel_id=1, source_target_pairs={{12,0},{0,4},{4,8},{8,12},{13,1},{1,5},{5,9},{9,13},{14,2},{2,6},{... | collective-permute-start | bytes 196616 | tf_op jit(solution)/shard_map/ppermute | solution.py:137
  5.0 2.6 %collective-permute-start.3 = (bf16[16,2048]{1,0:T(8,128)(2,1)S(1)}, bf16[16,2048]{1,0:T(8,128)(2,1)S(1)}, u32[]{:S(2)}, u32[]{:S(2)}) collective-permute-start(bf16[16,2048]{1,0:T(8,128)(2,1)S(1)} %constant_dynamic-slice_fusion.refs_0_), channel_id=1, source_target_pairs={{8,0},{12,4},{0,8},{4,12},{9,1},{13,5},{1,9},{5,13},{10,2},{14,6},... | collective-permute-start | bytes 196616 | tf_op jit(solution)/shard_map/ppermute | solution.py:137
  7.6 1.3 %collective-permute-start.1 = (bf16[16,2048]{1,0:T(8,128)(2,1)S(1)}, bf16[16,2048]{1,0:T(8,128)(2,1)S(1)}, u32[]{:S(2)}, u32[]{:S(2)}) collective-permute-start(bf16[16,2048]{1,0:T(8,128)(2,1)S(1)} %constant_dynamic-slice_fusion.refs_0_), channel_id=1, source_target_pairs={{4,0},{8,4},{12,8},{0,12},{5,1},{9,5},{13,9},{1,13},{6,2},{10,6},{... | collective-permute-start | bytes 196616 | tf_op jit(solution)/shard_map/ppermute | solution.py:137
  9.0 1.5 %collective-permute-start = (bf16[16,2048]{1,0:T(8,128)(2,1)S(1)}, bf16[16,2048]{1,0:T(8,128)(2,1)S(1)}, u32[]{:S(2)}, u32[]{:S(2)}) collective-permute-start(bf16[16,2048]{1,0:T(8,128)(2,1)S(1)} %constant_dynamic-slice_fusion.refs_0_), channel_id=1, source_target_pairs={{2,0},{0,2},{3,1},{1,3},{6,4},{4,6},{7,5},{5,7},{10,8},{8,10},{11,... | collective-permute-start | bytes 196616 | tf_op jit(solution)/shard_map/ppermute | solution.py:137
  10.5 0.0 collective-permute-done.7
  10.5 0.0 collective-permute-done.5.refs_6_
  10.5 1.0 %collective-permute-start.6 = (bf16[16,2048]{1,0:T(8,128)(2,1)S(1)}, bf16[16,2048]{1,0:T(8,128)(2,1)S(1)}, u32[]{:S(2)}, u32[]{:S(2)}) collective-permute-start(bf16[16,2048]{1,0:T(8,128)(2,1)S(1)} %collective-permute-done.5.refs_6_), channel_id=1, source_target_pairs={{2,0},{0,2},{3,1},{1,3},{6,4},{4,6},{7,5},{5,7},{10,8},{8,10},{11,... | collective-permute-start | bytes 196616 | tf_op jit(solution)/shard_map/ppermute | solution.py:137
  11.5 1.3 %collective-permute-done.3.refs_4_ = bf16[16,2048]{1,0:T(8,128)(2,1)S(1)} collective-permute-done((bf16[16,2048]{1,0:T(8,128)(2,1)S(1)}, bf16[16,2048]{1,0:T(8,128)(2,1)S(1)}, u32[]{:S(2)}, u32[]{:S(2)}) %collective-permute-start.3) | collective-permute-done | bytes 65568 | tf_op jit(solution)/shard_map/ppermute | solution.py:137
  12.7 1.5 %collective-permute-start.4 = (bf16[16,2048]{1,0:T(8,128)(2,1)S(1)}, bf16[16,2048]{1,0:T(8,128)(2,1)S(1)}, u32[]{:S(2)}, u32[]{:S(2)}) collective-permute-start(bf16[16,2048]{1,0:T(8,128)(2,1)S(1)} %collective-permute-done.3.refs_4_), channel_id=1, source_target_pairs={{2,0},{0,2},{3,1},{1,3},{6,4},{4,6},{7,5},{5,7},{10,8},{8,10},{11,... | collective-permute-start | bytes 196616 | tf_op jit(solution)/shard_map/ppermute | solution.py:137
  14.2 0.0 collective-permute-done.1.refs_2_
  14.2 0.5 %collective-permute-start.2 = (bf16[16,2048]{1,0:T(8,128)(2,1)S(1)}, bf16[16,2048]{1,0:T(8,128)(2,1)S(1)}, u32[]{:S(2)}, u32[]{:S(2)}) collective-permute-start(bf16[16,2048]{1,0:T(8,128)(2,1)S(1)} %collective-permute-done.1.refs_2_), channel_id=1, source_target_pairs={{2,0},{0,2},{3,1},{1,3},{6,4},{4,6},{7,5},{5,7},{10,8},{8,10},{11,... | collective-permute-start | bytes 196616 | tf_op jit(solution)/shard_map/ppermute | solution.py:137
  14.8 0.1 reshape.63.rows_ref
  14.8 0.0 copy-start.1
  14.8 1.2 %copy-done.1 = bf16[4,256,512]{2,1,0:T(8,128)(2,1)S(1)} copy-done((bf16[4,256,512]{2,1,0:T(8,128)(2,1)S(1)}, bf16[4,256,512]{2,1,0:T(8,128)(2,1)}, u32[]{:S(2)}) %copy-start.1) | copy-done | bytes 1048600
  16.1 0.8 %shard_map.64 = (bf16[4,256,256]{2,1,0:T(8,128)(2,1)S(1)}, bf16[4,256,256]{2,1,0:T(8,128)(2,1)S(1)}, bf16[256,128]{1,0:T(8,128)(2,1)S(1)}, bf16[128,256]{1,0:T(8,128)(2,1)S(1)}) custom-call(s32[1]{0:T(128)} %bitcast.half_ref, s32[1,256]{1,0:T(1,128)S(1)} %reshape.63.rows_ref, bf16[4,256,512]{2,1,0:T(8,128)(2,1)S(1)} %copy-done.1), custom_call_target="tpu_custom_call" | custom-call | flops 536870912 | bytes 3145728 | tf_op jit(solution)/shard_map/pallas_call | solution.py:179
  16.8 0.0 collective-permute-done.refs_1_
  16.8 0.0 collective-permute-done.6.refs_7_
  16.9 0.6 %collective-permute-done.4.refs_5_ = bf16[16,2048]{1,0:T(8,128)(2,1)S(1)} collective-permute-done((bf16[16,2048]{1,0:T(8,128)(2,1)S(1)}, bf16[16,2048]{1,0:T(8,128)(2,1)S(1)}, u32[]{:S(2)}, u32[]{:S(2)}) %collective-permute-start.4) | collective-permute-done | bytes 65568 | tf_op jit(solution)/shard_map/ppermute | solution.py:137
  17.5 1.0 %collective-permute-done.2.refs_3_ = bf16[16,2048]{1,0:T(8,128)(2,1)S(1)} collective-permute-done((bf16[16,2048]{1,0:T(8,128)(2,1)S(1)}, bf16[16,2048]{1,0:T(8,128)(2,1)S(1)}, u32[]{:S(2)}, u32[]{:S(2)}) %collective-permute-start.2) | collective-permute-done | bytes 65568 | tf_op jit(solution)/shard_map/ppermute | solution.py:137
  18.5 1.0 %shard_map.65.refs_0_ = f32[4,256]{1,0:T(4,128)S(1)} custom-call(bf16[16,2048]{1,0:T(8,128)(2,1)S(1)} %constant_dynamic-slice_fusion.refs_0_, bf16[16,2048]{1,0:T(8,128)(2,1)S(1)} %collective-permute-done.refs_1_, bf16[16,2048]{1,0:T(8,128)(2,1)S(1)} %collective-permute-done.1.refs_2_, bf16[16,2048]{1,0:T(8,128)(2,1)S(1)} %collective-permute-done.2.refs_3_, ...), custom_call_target="tpu_custom_call" | custom-call | flops 268435456 | bytes 2097152 | tf_op jit(solution)/shard_map/pallas_call | solution.py:193
  19.5 0.1 collective-permute-start.8
  19.6 1.2 %collective-permute-done.8.refs_1_ = f32[4,256]{1,0:T(4,128)S(1)} collective-permute-done((f32[4,256]{1,0:T(4,128)S(1)}, f32[4,256]{1,0:T(4,128)S(1)}, u32[]{:S(2)}, u32[]{:S(2)}) %collective-permute-start.8) | collective-permute-done | bytes 4128 | tf_op jit(solution)/shard_map/ppermute | solution.py:201
  20.7 1.4 %shard_map.66 = (bf16[16,2048]{1,0:T(8,128)(2,1)S(1)}, bf16[16,2048]{1,0:T(8,128)(2,1)S(1)}, bf16[16,2048]{1,0:T(8,128)(2,1)S(1)}, bf16[16,2048]{1,0:T(8,128)(2,...) custom-call(f32[4,256]{1,0:T(4,128)S(1)} %shard_map.65.refs_0_, ...), custom_call_target="tpu_custom_call" | custom-call | flops 268435456 | bytes 2097152 | tf_op jit(solution)/shard_map/pallas_call | solution.py:203
  22.1 1.1 %collective-permute-start.9 = (bf16[16,2048]{1,0:T(8,128)(2,1)S(1)}, bf16[16,2048]{1,0:T(8,128)(2,1)S(1)}, u32[]{:S(2)}, u32[]{:S(2)}) collective-permute-start(bf16[16,2048]{1,0:T(8,128)(2,1)S(1)} %get-tuple-element.22), channel_id=1, source_target_pairs={{0,2},{2,0},{1,3},{3,1},{4,6},{6,4},{5,7},{7,5},{8,10},{10,8},{9,1... | collective-permute-start | bytes 196616 | tf_op jit(solution)/shard_map/ppermute | solution.py:141
  23.3 1.0 %collective-permute-start.11 = (bf16[16,2048]{1,0:T(8,128)(2,1)S(1)}, bf16[16,2048]{1,0:T(8,128)(2,1)S(1)}, u32[]{:S(2)}, u32[]{:S(2)}) collective-permute-start(bf16[16,2048]{1,0:T(8,128)(2,1)S(1)} %get-tuple-element.24), channel_id=1, source_target_pairs={{0,2},{2,0},{1,3},{3,1},{4,6},{6,4},{5,7},{7,5},{8,10},{10,8},{9,1... | collective-permute-start | bytes 196616 | tf_op jit(solution)/shard_map/ppermute | solution.py:141
  24.2 1.1 %collective-permute-start.13 = (bf16[16,2048]{1,0:T(8,128)(2,1)S(1)}, bf16[16,2048]{1,0:T(8,128)(2,1)S(1)}, u32[]{:S(2)}, u32[]{:S(2)}) collective-permute-start(bf16[16,2048]{1,0:T(8,128)(2,1)S(1)} %get-tuple-element.26), channel_id=1, source_target_pairs={{0,2},{2,0},{1,3},{3,1},{4,6},{6,4},{5,7},{7,5},{8,10},{10,8},{9,1... | collective-permute-start | bytes 196616 | tf_op jit(solution)/shard_map/ppermute | solution.py:141
  25.3 1.0 %collective-permute-start.15 = (bf16[16,2048]{1,0:T(8,128)(2,1)S(1)}, bf16[16,2048]{1,0:T(8,128)(2,1)S(1)}, u32[]{:S(2)}, u32[]{:S(2)}) collective-permute-start(bf16[16,2048]{1,0:T(8,128)(2,1)S(1)} %get-tuple-element.28), channel_id=1, source_target_pairs={{0,2},{2,0},{1,3},{3,1},{4,6},{6,4},{5,7},{7,5},{8,10},{10,8},{9,1... | collective-permute-start | bytes 196616 | tf_op jit(solution)/shard_map/ppermute | solution.py:141
  26.3 0.9 %collective-permute-done.9 = bf16[16,2048]{1,0:T(8,128)(2,1)S(1)} collective-permute-done((bf16[16,2048]{1,0:T(8,128)(2,1)S(1)}, bf16[16,2048]{1,0:T(8,128)(2,1)S(1)}, u32[]{:S(2)}, u32[]{:S(2)}) %collective-permute-start.9) | collective-permute-done | bytes 65568 | tf_op jit(solution)/shard_map/ppermute | solution.py:141
  27.2 3.0 %collective-permute-start.10 = (bf16[16,2048]{1,0:T(8,128)(2,1)S(1)}, bf16[16,2048]{1,0:T(8,128)(2,1)S(1)}, u32[]{:S(2)}, u32[]{:S(2)}) collective-permute-start(bf16[16,2048]{1,0:T(8,128)(2,1)S(1)} %add_convert_fusion.2), channel_id=1, source_target_pairs={{0,12},{4,0},{8,4},{12,8},{1,13},{5,1},{9,5},{13,9},{2,14},{6,2},{... | collective-permute-start | bytes 196616 | tf_op jit(solution)/shard_map/ppermute | solution.py:141
  30.2 0.0 collective-permute-done.11
  30.2 0.1 collective-permute-start.12
  30.3 0.0 collective-permute-done.13
  30.3 1.9 %collective-permute-start.14 = (bf16[16,2048]{1,0:T(8,128)(2,1)S(1)}, bf16[16,2048]{1,0:T(8,128)(2,1)S(1)}, u32[]{:S(2)}, u32[]{:S(2)}) collective-permute-start(bf16[16,2048]{1,0:T(8,128)(2,1)S(1)} %add_convert_fusion), channel_id=1, source_target_pairs={{0,4},{4,8},{8,12},{12,0},{1,5},{5,9},{9,13},{13,1},{2,6},{6,10},{... | collective-permute-start | bytes 196616 | tf_op jit(solution)/shard_map/ppermute | solution.py:141
  32.2 0.0 collective-permute-done.15.refs_4_
  32.2 0.0 collective-permute-done.10.refs_0_
  32.2 3.2 %collective-permute-done.12.refs_1_ = bf16[16,2048]{1,0:T(8,128)(2,1)S(1)} collective-permute-done((bf16[16,2048]{1,0:T(8,128)(2,1)S(1)}, bf16[16,2048]{1,0:T(8,128)(2,1)S(1)}, u32[]{:S(2)}, u32[]{:S(2)}) %collective-permute-start.12) | collective-permute-done | bytes 65568 | tf_op jit(solution)/shard_map/ppermute | solution.py:141
  35.4 1.0 %collective-permute-done.14.refs_2_ = bf16[16,2048]{1,0:T(8,128)(2,1)S(1)} collective-permute-done((bf16[16,2048]{1,0:T(8,128)(2,1)S(1)}, bf16[16,2048]{1,0:T(8,128)(2,1)S(1)}, u32[]{:S(2)}, u32[]{:S(2)}) %collective-permute-start.14) | collective-permute-done | bytes 65568 | tf_op jit(solution)/shard_map/ppermute | solution.py:141
  36.5 0.1 collective-permute-start.16
  36.5 1.3 %collective-permute-done.16.other_ref = f32[16,2048]{1,0:T(8,128)S(1)} collective-permute-done((f32[16,2048]{1,0:T(8,128)S(1)}, f32[16,2048]{1,0:T(8,128)S(1)}, u32[]{:S(2)}, u32[]{:S(2)}) %collective-permute-start.16) | collective-permute-done | bytes 131104 | tf_op jit(solution)/shard_map/ppermute | solution.py:227
  37.9 0.7 %shard_map.68 = f32[16,4096]{1,0:T(8,128)} custom-call(s32[1]{0:T(128)} %bitcast.half_ref, f32[16,2048]{1,0:T(8,128)S(1)} %shard_map.67.mine_ref, f32[16,2048]{1,0:T(8,128)S(1)} %collective-permute-done.16.other_ref, bf16[16,4096]{1,0:T(8,128)(2,1)S(1)} %copy-done.3), custom_call_target="tpu_custom_call" | custom-call | bytes 786432 | tf_op jit(solution)/shard_map/pallas_call | solution.py:228
  (18 shorter events, 0.2 us)
Async XLA Ops:
  0.0 2.4 %copy-start = (bf16[16,4096]{1,0:T(8,128)(2,1)S(1)}, bf16[16,4096]{1,0:T(8,128)(2,1)}, u32[]{:S(2)}) copy-start(bf16[16,4096]{1,0:T(8,128)(2,1)} %param.10) | copy-start | bytes 393220
  0.0 0.7 %copy-start.6 = (s32[1,1,8,8]{3,2,1,0:T(8,128)S(1)}, s32[1,1,8,8]{3,2,1,0:T(8,128)}, u32[]{:S(2)}) copy-start(s32[1,1,8,8]{3,2,1,0:T(8,128)} %param.9) | copy-start | bytes 772
  0.7 0.7 %copy-start.5 = (s32[4,8,4]{1,2,0:T(4,128)S(1)}, s32[4,8,4]{1,2,0:T(4,128)}, u32[]{:S(2)}) copy-start(s32[4,8,4]{1,2,0:T(4,128)} %param.8) | copy-start | bytes 1540
  1.8 8.6 %collective-permute-start.7 = (s32[4,4,8]{2,1,0:T(4,128)S(1)}, s32[4,4,8]{2,1,0:T(4,128)S(1)}, u32[]{:S(2)}, u32[]{:S(2)}) collective-permute-start(s32[4,4,8]{2,1,0:T(4,128)S(1)} %bitcast.6), channel_id=1, source_target_pairs={{0,1},{1,0},{2,3},{3,2},{4,5},{5,4},{6,7},{7,6},{8,9},{9,8},{10,11... | collective-permute-start | bytes 1544 | tf_op jit(solution)/shard_map/ppermute | solution.py:164
  2.4 8.1 %collective-permute-start.5 = (bf16[16,2048]{1,0:T(8,128)(2,1)S(1)}, bf16[16,2048]{1,0:T(8,128)(2,1)S(1)}, u32[]{:S(2)}, u32[]{:S(2)}) collective-permute-start(bf16[16,2048]{1,0:T(8,128)(2,1)S(1)} %constant_dynamic-slice_fusion.refs_0_), channel_id=1, source_target_pairs={{12,0},{0,4},{4,8},{8,12},{13,1},{1,5},{5,9},{9,13},{14,2},{2,6},{... | collective-permute-start | bytes 196616 | tf_op jit(solution)/shard_map/ppermute | solution.py:137
  5.0 7.7 %collective-permute-start.3 = (bf16[16,2048]{1,0:T(8,128)(2,1)S(1)}, bf16[16,2048]{1,0:T(8,128)(2,1)S(1)}, u32[]{:S(2)}, u32[]{:S(2)}) collective-permute-start(bf16[16,2048]{1,0:T(8,128)(2,1)S(1)} %constant_dynamic-slice_fusion.refs_0_), channel_id=1, source_target_pairs={{8,0},{12,4},{0,8},{4,12},{9,1},{13,5},{1,9},{5,13},{10,2},{14,6},... | collective-permute-start | bytes 196616 | tf_op jit(solution)/shard_map/ppermute | solution.py:137
  7.6 6.6 %collective-permute-start.1 = (bf16[16,2048]{1,0:T(8,128)(2,1)S(1)}, bf16[16,2048]{1,0:T(8,128)(2,1)S(1)}, u32[]{:S(2)}, u32[]{:S(2)}) collective-permute-start(bf16[16,2048]{1,0:T(8,128)(2,1)S(1)} %constant_dynamic-slice_fusion.refs_0_), channel_id=1, source_target_pairs={{4,0},{8,4},{12,8},{0,12},{5,1},{9,5},{13,9},{1,13},{6,2},{10,6},{... | collective-permute-start | bytes 196616 | tf_op jit(solution)/shard_map/ppermute | solution.py:137
  9.0 7.9 %collective-permute-start = (bf16[16,2048]{1,0:T(8,128)(2,1)S(1)}, bf16[16,2048]{1,0:T(8,128)(2,1)S(1)}, u32[]{:S(2)}, u32[]{:S(2)}) collective-permute-start(bf16[16,2048]{1,0:T(8,128)(2,1)S(1)} %constant_dynamic-slice_fusion.refs_0_), channel_id=1, source_target_pairs={{2,0},{0,2},{3,1},{1,3},{6,4},{4,6},{7,5},{5,7},{10,8},{8,10},{11,... | collective-permute-start | bytes 196616 | tf_op jit(solution)/shard_map/ppermute | solution.py:137
  10.5 6.4 %collective-permute-start.6 = (bf16[16,2048]{1,0:T(8,128)(2,1)S(1)}, bf16[16,2048]{1,0:T(8,128)(2,1)S(1)}, u32[]{:S(2)}, u32[]{:S(2)}) collective-permute-start(bf16[16,2048]{1,0:T(8,128)(2,1)S(1)} %collective-permute-done.5.refs_6_), channel_id=1, source_target_pairs={{2,0},{0,2},{3,1},{1,3},{6,4},{4,6},{7,5},{5,7},{10,8},{8,10},{11,... | collective-permute-start | bytes 196616 | tf_op jit(solution)/shard_map/ppermute | solution.py:137
  12.7 4.8 %collective-permute-start.4 = (bf16[16,2048]{1,0:T(8,128)(2,1)S(1)}, bf16[16,2048]{1,0:T(8,128)(2,1)S(1)}, u32[]{:S(2)}, u32[]{:S(2)}) collective-permute-start(bf16[16,2048]{1,0:T(8,128)(2,1)S(1)} %collective-permute-done.3.refs_4_), channel_id=1, source_target_pairs={{2,0},{0,2},{3,1},{1,3},{6,4},{4,6},{7,5},{5,7},{10,8},{8,10},{11,... | collective-permute-start | bytes 196616 | tf_op jit(solution)/shard_map/ppermute | solution.py:137
  14.2 4.3 %collective-permute-start.2 = (bf16[16,2048]{1,0:T(8,128)(2,1)S(1)}, bf16[16,2048]{1,0:T(8,128)(2,1)S(1)}, u32[]{:S(2)}, u32[]{:S(2)}) collective-permute-start(bf16[16,2048]{1,0:T(8,128)(2,1)S(1)} %collective-permute-done.1.refs_2_), channel_id=1, source_target_pairs={{2,0},{0,2},{3,1},{1,3},{6,4},{4,6},{7,5},{5,7},{10,8},{8,10},{11,... | collective-permute-start | bytes 196616 | tf_op jit(solution)/shard_map/ppermute | solution.py:137
  14.8 1.2 %copy-start.1 = (bf16[4,256,512]{2,1,0:T(8,128)(2,1)S(1)}, bf16[4,256,512]{2,1,0:T(8,128)(2,1)}, u32[]{:S(2)}) copy-start(bf16[4,256,512]{2,1,0:T(8,128)(2,1)} %refs_3_.1) | copy-start | bytes 3145732
  16.1 2.4 %copy-start.2 = (bf16[4,256,512]{2,1,0:T(8,128)(2,1)S(1)}, bf16[4,256,512]{2,1,0:T(8,128)(2,1)}, u32[]{:S(2)}) copy-start(bf16[4,256,512]{2,1,0:T(8,128)(2,1)} %refs_3_.1) | copy-start | bytes 3145732
  18.5 2.3 %copy-start.4 = (f32[4,256]{1,0:T(4,128)S(1)}, f32[4,256]{1,0:T(4,128)}, u32[]{:S(2)}) copy-start(f32[4,256]{1,0:T(4,128)} %refs_2_.1) | copy-start | bytes 12292
  19.5 1.2 %collective-permute-start.8 = (f32[4,256]{1,0:T(4,128)S(1)}, f32[4,256]{1,0:T(4,128)S(1)}, u32[]{:S(2)}, u32[]{:S(2)}) collective-permute-start(f32[4,256]{1,0:T(4,128)S(1)} %shard_map.65.refs_0_), channel_id=1, source_target_pairs={{0,1},{1,0},{2,3},{3,2},{4,5},{5,4},{6,7},{7,6},{8,9},{9,8},{10,11... | collective-permute-start | bytes 12296 | tf_op jit(solution)/shard_map/ppermute | solution.py:201
  22.1 5.0 %collective-permute-start.9 = (bf16[16,2048]{1,0:T(8,128)(2,1)S(1)}, bf16[16,2048]{1,0:T(8,128)(2,1)S(1)}, u32[]{:S(2)}, u32[]{:S(2)}) collective-permute-start(bf16[16,2048]{1,0:T(8,128)(2,1)S(1)} %get-tuple-element.22), channel_id=1, source_target_pairs={{0,2},{2,0},{1,3},{3,1},{4,6},{6,4},{5,7},{7,5},{8,10},{10,8},{9,1... | collective-permute-start | bytes 196616 | tf_op jit(solution)/shard_map/ppermute | solution.py:141
  23.3 6.9 %collective-permute-start.11 = (bf16[16,2048]{1,0:T(8,128)(2,1)S(1)}, bf16[16,2048]{1,0:T(8,128)(2,1)S(1)}, u32[]{:S(2)}, u32[]{:S(2)}) collective-permute-start(bf16[16,2048]{1,0:T(8,128)(2,1)S(1)} %get-tuple-element.24), channel_id=1, source_target_pairs={{0,2},{2,0},{1,3},{3,1},{4,6},{6,4},{5,7},{7,5},{8,10},{10,8},{9,1... | collective-permute-start | bytes 196616 | tf_op jit(solution)/shard_map/ppermute | solution.py:141
  24.2 6.0 %collective-permute-start.13 = (bf16[16,2048]{1,0:T(8,128)(2,1)S(1)}, bf16[16,2048]{1,0:T(8,128)(2,1)S(1)}, u32[]{:S(2)}, u32[]{:S(2)}) collective-permute-start(bf16[16,2048]{1,0:T(8,128)(2,1)S(1)} %get-tuple-element.26), channel_id=1, source_target_pairs={{0,2},{2,0},{1,3},{3,1},{4,6},{6,4},{5,7},{7,5},{8,10},{10,8},{9,1... | collective-permute-start | bytes 196616 | tf_op jit(solution)/shard_map/ppermute | solution.py:141
  25.3 6.9 %collective-permute-start.15 = (bf16[16,2048]{1,0:T(8,128)(2,1)S(1)}, bf16[16,2048]{1,0:T(8,128)(2,1)S(1)}, u32[]{:S(2)}, u32[]{:S(2)}) collective-permute-start(bf16[16,2048]{1,0:T(8,128)(2,1)S(1)} %get-tuple-element.28), channel_id=1, source_target_pairs={{0,2},{2,0},{1,3},{3,1},{4,6},{6,4},{5,7},{7,5},{8,10},{10,8},{9,1... | collective-permute-start | bytes 196616 | tf_op jit(solution)/shard_map/ppermute | solution.py:141
  27.2 5.0 %collective-permute-start.10 = (bf16[16,2048]{1,0:T(8,128)(2,1)S(1)}, bf16[16,2048]{1,0:T(8,128)(2,1)S(1)}, u32[]{:S(2)}, u32[]{:S(2)}) collective-permute-start(bf16[16,2048]{1,0:T(8,128)(2,1)S(1)} %add_convert_fusion.2), channel_id=1, source_target_pairs={{0,12},{4,0},{8,4},{12,8},{1,13},{5,1},{9,5},{13,9},{2,14},{6,2},{... | collective-permute-start | bytes 196616 | tf_op jit(solution)/shard_map/ppermute | solution.py:141
  30.2 5.2 %collective-permute-start.12 = (bf16[16,2048]{1,0:T(8,128)(2,1)S(1)}, bf16[16,2048]{1,0:T(8,128)(2,1)S(1)}, u32[]{:S(2)}, u32[]{:S(2)}) collective-permute-start(bf16[16,2048]{1,0:T(8,128)(2,1)S(1)} %add_convert_fusion.1), channel_id=1, source_target_pairs={{0,8},{4,12},{8,0},{12,4},{1,9},{5,13},{9,1},{13,5},{2,10},{6,14},... | collective-permute-start | bytes 196616 | tf_op jit(solution)/shard_map/ppermute | solution.py:141
  30.3 6.1 %collective-permute-start.14 = (bf16[16,2048]{1,0:T(8,128)(2,1)S(1)}, bf16[16,2048]{1,0:T(8,128)(2,1)S(1)}, u32[]{:S(2)}, u32[]{:S(2)}) collective-permute-start(bf16[16,2048]{1,0:T(8,128)(2,1)S(1)} %add_convert_fusion), channel_id=1, source_target_pairs={{0,4},{4,8},{8,12},{12,0},{1,5},{5,9},{9,13},{13,1},{2,6},{6,10},{... | collective-permute-start | bytes 196616 | tf_op jit(solution)/shard_map/ppermute | solution.py:141
  36.4 1.5 %copy-start.3 = (bf16[16,4096]{1,0:T(8,128)(2,1)S(1)}, bf16[16,4096]{1,0:T(8,128)(2,1)}, u32[]{:S(2)}) copy-start(bf16[16,4096]{1,0:T(8,128)(2,1)} %core_ref.1) | copy-start | bytes 393220
  36.5 1.4 %collective-permute-start.16 = (f32[16,2048]{1,0:T(8,128)S(1)}, f32[16,2048]{1,0:T(8,128)S(1)}, u32[]{:S(2)}, u32[]{:S(2)}) collective-permute-start(f32[16,2048]{1,0:T(8,128)S(1)} %shard_map.67.mine_ref), channel_id=1, source_target_pairs={{0,1},{1,0},{2,3},{3,2},{4,5},{5,4},{6,7},{7,6},{8,9},{9,8},{10,11... | collective-permute-start | bytes 393224 | tf_op jit(solution)/shard_map/ppermute | solution.py:227

commit v2 on v1

--- a/solution.py
+++ b/solution.py
@@ -38,14 +38,15 @@
     pick_ref[...] = hot.T.astype(jnp.bfloat16)
 
 
-def density_kernel(pieces, *refs):
-    piece_refs = refs[:pieces]
-    pick_ref, left_ref, values_ref, out_ref, table, dense = refs[pieces:]
-    held = piece_refs[0].shape[0]
+def density_kernel(places, *refs):
+    piece_refs = refs[:len(places)]
+    pick_ref, left_ref, values_ref, out_ref, table, dense = refs[len(places):]
     batches, points, columns = values_ref.shape
     groups = columns // GO
-    for k in range(pieces):
-        table[k * held:(k + 1) * held, :] = piece_refs[k][...]
+    for ref, blocks in zip(piece_refs, places):
+        held = ref.shape[0] // len(blocks)
+        for i, k in enumerate(blocks):
+            table[k * held:(k + 1) * held, :] = ref[i * held:(i + 1) * held, :]
     low = lax.broadcasted_iota(jnp.int32, (1, 1, groups, 128), 3) < GO
     for j in range(table.shape[1] // 128):
         lanes = slice(j * 128, (j + 1) * 128)
@@ -66,11 +67,16 @@
         out_ref[t:t + 1, :] = jnp.sum(folded.T, axis=0, keepdims=True)
 
 
-def scatter_kernel(pieces, *refs):
+def scatter_kernel(places, *refs):
     mine_ref, other_ref, weight_ref, values_ref, left_t_ref, put_ref = refs[:6]
-    out_refs = refs[6:6 + pieces]
-    high, rest = refs[6 + pieces:]
-    held = out_refs[0].shape[0]
+    out_refs = refs[6:6 + len(places)]
+    high, rest = refs[6 + len(places):]
+    target = {}
+    for ref, blocks in zip(out_refs, places):
+        for i, k in enumerate(blocks):
+            target[k] = (ref, i)
+    pieces = len(target)
+    held = put_ref.shape[0] // pieces
     batches, points, columns = values_ref.shape
     groups = columns // GO
     kept = left_t_ref.shape[1]
@@ -98,7 +104,8 @@
         some = put_ref[k * held:(k + step) * held, :]
         total = split_dot(some, high[...]) + split_dot(some, rest[...])
         for i in range(step):
-            out_refs[k + i][...] = total[i * held:(i + 1) * held, :].astype(jnp.bfloat16)
+            ref, at = target[k + i]
+            ref[at * held:(at + 1) * held, :] = total[i * held:(i + 1) * held, :].astype(jnp.bfloat16)
 
 
 def sum_kernel(*refs):
@@ -133,12 +140,8 @@
     )
 
 
-def from_ahead(array, axis, count, step):
-    return lax.ppermute(array, axis, [((i + step) % count, i) for i in range(count)])
-
-
-def to_ahead(array, axis, count, step):
-    return lax.ppermute(array, axis, [(i, (i + step) % count) for i in range(count)])
+def swap(array, axis, count, step):
+    return lax.ppermute(array, axis, [(i, i ^ step) for i in range(count)])
 
 
 def per_device(basis_values, point_weights, slot_ids, fetch_rows, density_blocks, core_blocks):
@@ -155,26 +158,38 @@
     kept = columns // 2
     bf16, f32 = jnp.bfloat16, jnp.float32
 
+    upper = list(range(rows_z // 2, rows_z))
+    lower = list(range(1, rows_z // 2))
+    cut = (len(upper) + 1) // 2
+    groups_in = [[0], upper[:cut] + lower, upper[cut:]]
+    groups_in = [group for group in groups_in if group]
+
+    mine = lax.dynamic_slice_in_dim(density_blocks, half * wide, wide, 1)
+    held_z = {0: mine}
+    for dz in upper + lower:
+        held_z[dz] = swap(mine, "batch", rows_z, dz)
+    arrays, places = [], []
+    for dz in [0] + upper + lower:
+        arrays.append(held_z[dz])
+        places.append([dz * rows_x])
+    for group in groups_in:
+        sent = jnp.concatenate([held_z[dz] for dz in group], axis=0) if len(group) > 1 else held_z[group[0]]
+        for dx in range(1, rows_x):
+            arrays.append(swap(sent, "pair", rows_x, dx))
+            places.append([dz * rows_x + dx for dz in group])
+
+    slot_ids, fetch_rows, _ = lax.optimization_barrier((slot_ids, fetch_rows, held_z[upper[0]]))
     owner = jnp.arange(owners, dtype=jnp.int32)
-    ahead = ((owner // rows_x - z) % rows_z) * rows_x + (owner % rows_x - x) % rows_x
-    home = (ahead[:, None] * held + fetch_rows.reshape(owners, capacity)).reshape(-1)
+    apart = ((owner // rows_x) ^ z) * rows_x + ((owner % rows_x) ^ x)
+    home = (apart[:, None] * held + fetch_rows.reshape(owners, capacity)).reshape(-1)
     slots = jnp.arange(owners * capacity, dtype=jnp.int32)
     own_rows = jnp.sum(jnp.where(slot_ids[..., None] == slots, home, 0), axis=-1)
     own_rows = own_rows.transpose(0, 2, 1).astype(jnp.int32)
-    other_rows = lax.ppermute(own_rows, "orb", [(0, 1), (1, 0)])
+    other_rows = swap(own_rows, "orb", 2, 1)
     rows = jnp.concatenate(
         [jnp.where(half == 0, own_rows, other_rows), jnp.where(half == 0, other_rows, own_rows)], axis=1
     ).reshape(1, entries)
     half_at = half.reshape(1).astype(jnp.int32)
-
-    mine = lax.dynamic_slice_in_dim(density_blocks, half * wide, wide, 1)
-    pieces = []
-    for dz in range(rows_z):
-        base = mine if dz == 0 else from_ahead(mine, "batch", rows_z, dz)
-        pieces.append(base)
-        for dx in range(1, rows_x):
-            pieces.append(from_ahead(base, "pair", rows_x, dx))
-    count = len(pieces)
 
     left, left_t, pick, put = call(
         prepare_kernel,
@@ -191,40 +206,47 @@
     )(half_at, rows, basis_values)
 
     partial = call(
-        functools.partial(density_kernel, count),
+        functools.partial(density_kernel, places),
         jax.ShapeDtypeStruct((batches, points), f32),
-        count + 3,
+        len(arrays) + 3,
         scratch=(pltpu.VMEM((table_rows, wide), bf16), pltpu.VMEM((batches, kept, columns), bf16)),
         flops=2 * batches * points * columns * kept,
         moved=2 * batches * points * columns * 2,
-    )(*pieces, pick, left, basis_values)
-    partial_other = lax.ppermute(partial, "orb", [(0, 1), (1, 0)])
-
+    )(*arrays, pick, left, basis_values)
+    partial_other = swap(partial, "orb", 2, 1)
+
+    groups_out = [group for group in (upper[::-1], lower[::-1] + [0]) if group]
+    kept_places = [[dz * rows_x] for dz in range(rows_z)]
+    sent_places = [[dz * rows_x + dx for dz in group] for group in groups_out for dx in range(1, rows_x)]
+    out_places = kept_places + sent_places
     sums = call(
-        functools.partial(scatter_kernel, count),
-        [jax.ShapeDtypeStruct((held, wide), bf16)] * count,
+        functools.partial(scatter_kernel, out_places),
+        [jax.ShapeDtypeStruct((held * len(blocks), wide), bf16) for blocks in out_places],
         6,
         scratch=(pltpu.VMEM((entries, wide), bf16), pltpu.VMEM((entries, wide), bf16)),
         flops=2 * batches * points * columns * kept,
         moved=2 * batches * points * columns * 2,
     )(partial, partial_other, point_weights, basis_values, left_t, put)
-
     landed = []
-    for dz in range(rows_z - 1, -1, -1):
-        terms = [sums[dz * rows_x]]
+    at = rows_z
+    for group in groups_out:
+        came = []
         for dx in range(1, rows_x):
-            terms.append(to_ahead(sums[dz * rows_x + dx], "pair", rows_x, dx))
-        if dz == 0:
-            landed.extend(terms)
-            continue
-        joined = terms[0].astype(f32)
-        for term in terms[1:]:
-            joined = joined + term.astype(f32)
-        landed.append(to_ahead(joined.astype(bf16), "batch", rows_z, dz))
+            came.append(swap(sums[at], "pair", rows_x, dx))
+            at += 1
+        for i, dz in enumerate(group):
+            terms = [sums[dz]] + [array[i * held:(i + 1) * held] for array in came]
+            if dz == 0:
+                landed.extend(terms)
+                continue
+            joined = terms[0].astype(f32)
+            for term in terms[1:]:
+                joined = joined + term.astype(f32)
+            landed.append(swap(joined.astype(bf16), "batch", rows_z, dz))
     total = call(
         sum_kernel, jax.ShapeDtypeStruct((held, wide), f32), len(landed), moved=len(landed) * held * wide * 2
     )(*landed)
-    total_other = lax.ppermute(total, "orb", [(0, 1), (1, 0)])
+    total_other = swap(total, "orb", 2, 1)
     return call(
         finish_kernel, jax.ShapeDtypeStruct((held, square), f32), 3, scalar=True, moved=held * square * 12
     )(half_at, total, total_other, core_blocks)

time: 38.8 us -> 41.9 us (1.080)
  waiting for transfers between devices: 10.5 us -> 19.5 us
  starting transfers between devices: 20.8 us -> 15.1 us
    ppermute x17 -> x14, waiting for transfers between devices: 10.5 us -> 19.5 us  [swap(): return lax.ppermute(array, axis, [(i, i ^ step) for i in range(count)])]
    ppermute x17 -> x14, starting transfers between devices: 20.8 us -> 15.1 us  [swap(): return lax.ppermute(array, axis, [(i, i ^ step) for i in range(count)])]
  transfers between devices with their start and end apart: 17 -> 14, of which waited for: 8 -> 7; matrix products, arithmetic and copies ran while one was open for 0% -> 2% of each run, Pallas kernels for 2% -> 2%
where the time goes in v2:
time: 41.9 us; the launch traced here: 41.7 us
  waiting for transfers between devices  19.5 us (47%)
  starting transfers between devices  15.1 us (36%)
  Pallas kernels  3.97 us (9%)
  local copies, waits for them, and re-layouts  2.47 us (6%)
  other arithmetic  0.52 us (1%)
    ppermute x14, waiting for transfers between devices, swap(): return lax.ppermute(array, axis, [(i, i ^ step) for i in range(count)])  19.5 us
    ppermute x14, starting transfers between devices, swap(): return lax.ppermute(array, axis, [(i, i ^ step) for i in range(count)])  15.1 us
    unnamed x14, local copies, waits for them, and re-layouts  2.14 us
    pallas_call x1, Pallas kernels, per_device(): call(functools.partial(scatter_kernel, out_places), [jax.ShapeDtypeStruct...  1.4 us
    pallas_call x1, Pallas kernels, per_device(): call(functools.partial(density_kernel, places), jax.ShapeDtypeStruct((bat...  1.04 us
  transfers between devices with their start and end apart: 14, of which 7 were waited for; matrix products, arithmetic and copies ran while one was open for 2% of the time, Pallas kernels for 2%

profile of v2, /device:TPU:0, one launch (start us, length us, event | category | flops | bytes accessed | tf_op | source)
XLA Modules:
  0.0 41.7 jit_solution(4361366783551214059)
XLA Ops:
  0.0 0.0 copy-start
  0.0 0.9 %copy-done = bf16[16,4096]{1,0:T(8,128)(2,1)S(1)} copy-done((bf16[16,4096]{1,0:T(8,128)(2,1)S(1)}, bf16[16,4096]{1,0:T(8,128)(2,1)}, u32[]{:S(2)}) %copy-start) | copy-done | bytes 131096
  0.9 2.9 %collective-permute-start.3 = (bf16[16,2048]{1,0:T(8,128)(2,1)S(1)}, bf16[16,2048]{1,0:T(8,128)(2,1)S(1)}, u32[]{:S(2)}, u32[]{:S(2)}) collective-permute-start(bf16[16,2048]{1,0:T(8,128)(2,1)S(1)} %constant_dynamic-slice_fusion.refs_0_), channel_id=1, source_target_pairs={{0,2},{2,0},{1,3},{3,1},{4,6},{6,4},{5,7},{7,5},{8,10},{10,8},{9,1... | collective-permute-start | bytes 196616 | tf_op jit(solution)/shard_map/ppermute | solution.py:144
  3.9 1.6 %collective-permute-start.2 = (bf16[16,2048]{1,0:T(8,128)(2,1)S(1)}, bf16[16,2048]{1,0:T(8,128)(2,1)S(1)}, u32[]{:S(2)}, u32[]{:S(2)}) collective-permute-start(bf16[16,2048]{1,0:T(8,128)(2,1)S(1)} %constant_dynamic-slice_fusion.refs_0_), channel_id=1, source_target_pairs={{0,4},{4,0},{8,12},{12,8},{1,5},{5,1},{9,13},{13,9},{2,6},{6,2},{1... | collective-permute-start | bytes 196616 | tf_op jit(solution)/shard_map/ppermute | solution.py:144
  5.4 2.5 %collective-permute-start.1 = (bf16[16,2048]{1,0:T(8,128)(2,1)S(1)}, bf16[16,2048]{1,0:T(8,128)(2,1)S(1)}, u32[]{:S(2)}, u32[]{:S(2)}) collective-permute-start(bf16[16,2048]{1,0:T(8,128)(2,1)S(1)} %constant_dynamic-slice_fusion.refs_0_), channel_id=1, source_target_pairs={{0,12},{4,8},{8,4},{12,0},{1,13},{5,9},{9,5},{13,1},{2,14},{6,10},... | collective-permute-start | bytes 196616 | tf_op jit(solution)/shard_map/ppermute | solution.py:144
  7.9 0.1 collective-permute-start
  8.0 0.0 copy-start.6
  8.0 0.0 copy-start.5
  8.0 0.1 add.48
  8.1 0.1 add.49
  8.2 5.9 %collective-permute-done.refs_1_ = bf16[16,2048]{1,0:T(8,128)(2,1)S(1)} collective-permute-done((bf16[16,2048]{1,0:T(8,128)(2,1)S(1)}, bf16[16,2048]{1,0:T(8,128)(2,1)S(1)}, u32[]{:S(2)}, u32[]{:S(2)}) %collective-permute-start) | collective-permute-done | bytes 65568 | tf_op jit(solution)/shard_map/ppermute | solution.py:144
  14.1 0.0 copy-done.6
  14.1 0.1 reshape.40
  14.2 0.0 copy-done.5
  14.2 0.4 %select_reduce_fusion = s32[4,8,4]{1,2,0:T(4,128)S(1)} fusion(s32[64]{0:T(128)S(1)} %add.50, s32[4,8,4]{1,2,0:T(4,128)S(1)} %copy-done.5), kind=kLoop, calls=%fused_computation.4 | loop fusion | flops 24448 | bytes 1280 | tf_op jit(solution)/shard_map/reduce_sum | solution.py:186
  14.6 0.1 collective-permute-start.6
  14.7 0.0 collective-permute-done.2.refs_3_
  14.7 0.6 %collective-permute-start.4 = (bf16[32,2048]{1,0:T(8,128)(2,1)S(1)}, bf16[32,2048]{1,0:T(8,128)(2,1)S(1)}, u32[]{:S(2)}, u32[]{:S(2)}) collective-permute-start(bf16[32,2048]{1,0:T(8,128)(2,1)S(1)} %pad_maximum_fusion), channel_id=1, source_target_pairs={{0,2},{2,0},{1,3},{3,1},{4,6},{6,4},{5,7},{7,5},{8,10},{10,8},{9,1... | collective-permute-start | bytes 393224 | tf_op jit(solution)/shard_map/ppermute | solution.py:144
  15.3 0.0 collective-permute-done.1.refs_2_
  15.3 1.5 %collective-permute-start.5 = (bf16[16,2048]{1,0:T(8,128)(2,1)S(1)}, bf16[16,2048]{1,0:T(8,128)(2,1)S(1)}, u32[]{:S(2)}, u32[]{:S(2)}) collective-permute-start(bf16[16,2048]{1,0:T(8,128)(2,1)S(1)} %collective-permute-done.1.refs_2_), channel_id=1, source_target_pairs={{0,2},{2,0},{1,3},{3,1},{4,6},{6,4},{5,7},{7,5},{8,10},{10,8},{9,1... | collective-permute-start | bytes 196616 | tf_op jit(solution)/shard_map/ppermute | solution.py:144
  16.8 0.0 collective-permute-done.6
  16.9 0.1 reshape.41.rows_ref
  17.0 0.0 copy-start.1
  17.0 1.2 %copy-done.1 = bf16[4,256,512]{2,1,0:T(8,128)(2,1)S(1)} copy-done((bf16[4,256,512]{2,1,0:T(8,128)(2,1)S(1)}, bf16[4,256,512]{2,1,0:T(8,128)(2,1)}, u32[]{:S(2)}) %copy-start.1) | copy-done | bytes 1048600
  18.2 0.8 %shard_map.64 = (bf16[4,256,256]{2,1,0:T(8,128)(2,1)S(1)}, bf16[4,256,256]{2,1,0:T(8,128)(2,1)S(1)}, bf16[256,128]{1,0:T(8,128)(2,1)S(1)}, bf16[128,256]{1,0:T(8,128)(2,1)S(1)}) custom-call(s32[1]{0:T(128)} %bitcast.half_ref, s32[1,256]{1,0:T(1,128)S(1)} %reshape.41.rows_ref, bf16[4,256,512]{2,1,0:T(8,128)(2,1)S(1)} %copy-done.1), custom_call_target="tpu_custom_call" | custom-call | flops 536870912 | bytes 3145728 | tf_op jit(solution)/shard_map/pallas_call | solution.py:194
  19.0 0.0 collective-permute-done.3.refs_4_
  19.0 3.1 %collective-permute-done.5.refs_6_ = bf16[16,2048]{1,0:T(8,128)(2,1)S(1)} collective-permute-done((bf16[16,2048]{1,0:T(8,128)(2,1)S(1)}, bf16[16,2048]{1,0:T(8,128)(2,1)S(1)}, u32[]{:S(2)}, u32[]{:S(2)}) %collective-permute-start.5) | collective-permute-done | bytes 65568 | tf_op jit(solution)/shard_map/ppermute | solution.py:144
  22.1 0.0 collective-permute-done.4.refs_5_
  22.1 0.0 copy-done.2
  22.1 1.0 %shard_map.65.refs_0_ = f32[4,256]{1,0:T(4,128)S(1)} custom-call(bf16[16,2048]{1,0:T(8,128)(2,1)S(1)} %constant_dynamic-slice_fusion.refs_0_, bf16[16,2048]{1,0:T(8,128)(2,1)S(1)} %collective-permute-done.refs_1_, bf16[16,2048]{1,0:T(8,128)(2,1)S(1)} %collective-permute-done.1.refs_2_, bf16[16,2048]{1,0:T(8,128)(2,1)S(1)} %collective-permute-done.2.refs_3_, ...), custom_call_target="tpu_custom_call" | custom-call | flops 268435456 | bytes 2097152 | tf_op jit(solution)/shard_map/pallas_call | solution.py:208
  23.2 0.1 collective-permute-start.7
  23.2 1.2 %collective-permute-done.7.refs_1_ = f32[4,256]{1,0:T(4,128)S(1)} collective-permute-done((f32[4,256]{1,0:T(4,128)S(1)}, f32[4,256]{1,0:T(4,128)S(1)}, u32[]{:S(2)}, u32[]{:S(2)}) %collective-permute-start.7) | collective-permute-done | bytes 4128 | tf_op jit(solution)/shard_map/ppermute | solution.py:144
  24.4 0.0 copy-done.4
  24.4 1.4 %shard_map.66 = (bf16[16,2048]{1,0:T(8,128)(2,1)S(1)}, bf16[16,2048]{1,0:T(8,128)(2,1)S(1)}, bf16[16,2048]{1,0:T(8,128)(2,1)S(1)}, bf16[16,2048]{1,0:T(8,128)(2,...) custom-call(f32[4,256]{1,0:T(4,128)S(1)} %shard_map.65.refs_0_, ...), custom_call_target="tpu_custom_call" | custom-call | flops 268435456 | bytes 2097152 | tf_op jit(solution)/shard_map/pallas_call | solution.py:222
  25.8 0.6 %collective-permute-start.8 = (bf16[32,2048]{1,0:T(8,128)(2,1)S(1)}, bf16[32,2048]{1,0:T(8,128)(2,1)S(1)}, u32[]{:S(2)}, u32[]{:S(2)}) collective-permute-start(bf16[32,2048]{1,0:T(8,128)(2,1)S(1)} %get-tuple-element.24), channel_id=1, source_target_pairs={{0,2},{2,0},{1,3},{3,1},{4,6},{6,4},{5,7},{7,5},{8,10},{10,8},{9,1... | collective-permute-start | bytes 393224 | tf_op jit(solution)/shard_map/ppermute | solution.py:144
  26.4 1.5 %collective-permute-start.11 = (bf16[32,2048]{1,0:T(8,128)(2,1)S(1)}, bf16[32,2048]{1,0:T(8,128)(2,1)S(1)}, u32[]{:S(2)}, u32[]{:S(2)}) collective-permute-start(bf16[32,2048]{1,0:T(8,128)(2,1)S(1)} %get-tuple-element.27), channel_id=1, source_target_pairs={{0,2},{2,0},{1,3},{3,1},{4,6},{6,4},{5,7},{7,5},{8,10},{10,8},{9,1... | collective-permute-start | bytes 393224 | tf_op jit(solution)/shard_map/ppermute | solution.py:144
  27.9 4.3 %collective-permute-done.8 = bf16[32,2048]{1,0:T(8,128)(2,1)S(1)} collective-permute-done((bf16[32,2048]{1,0:T(8,128)(2,1)S(1)}, bf16[32,2048]{1,0:T(8,128)(2,1)S(1)}, u32[]{:S(2)}, u32[]{:S(2)}) %collective-permute-start.8) | collective-permute-done | bytes 131104 | tf_op jit(solution)/shard_map/ppermute | solution.py:144
  32.2 0.1 collective-permute-start.10
  32.3 2.4 %collective-permute-start.9 = (bf16[16,2048]{1,0:T(8,128)(2,1)S(1)}, bf16[16,2048]{1,0:T(8,128)(2,1)S(1)}, u32[]{:S(2)}, u32[]{:S(2)}) collective-permute-start(bf16[16,2048]{1,0:T(8,128)(2,1)S(1)} %get-tuple-element.30), channel_id=1, source_target_pairs={{0,12},{4,8},{8,4},{12,0},{1,13},{5,9},{9,5},{13,1},{2,14},{6,10},... | collective-permute-start | bytes 196616 | tf_op jit(solution)/shard_map/ppermute | solution.py:144
  34.8 0.0 collective-permute-done.11
  34.8 1.1 %collective-permute-start.12 = (bf16[16,2048]{1,0:T(8,128)(2,1)S(1)}, bf16[16,2048]{1,0:T(8,128)(2,1)S(1)}, u32[]{:S(2)}, u32[]{:S(2)}) collective-permute-start(bf16[16,2048]{1,0:T(8,128)(2,1)S(1)} %add_convert_fusion), channel_id=1, source_target_pairs={{0,4},{4,0},{8,12},{12,8},{1,5},{5,1},{9,13},{13,9},{2,6},{6,2},{1... | collective-permute-start | bytes 196616 | tf_op jit(solution)/shard_map/ppermute | solution.py:144
  35.9 3.1 %collective-permute-done.10.refs_1_ = bf16[16,2048]{1,0:T(8,128)(2,1)S(1)} collective-permute-done((bf16[16,2048]{1,0:T(8,128)(2,1)S(1)}, bf16[16,2048]{1,0:T(8,128)(2,1)S(1)}, u32[]{:S(2)}, u32[]{:S(2)}) %collective-permute-start.10) | collective-permute-done | bytes 65568 | tf_op jit(solution)/shard_map/ppermute | solution.py:144
  39.0 0.0 collective-permute-done.9.refs_0_
  39.0 0.5 %collective-permute-done.12.refs_2_ = bf16[16,2048]{1,0:T(8,128)(2,1)S(1)} collective-permute-done((bf16[16,2048]{1,0:T(8,128)(2,1)S(1)}, bf16[16,2048]{1,0:T(8,128)(2,1)S(1)}, u32[]{:S(2)}, u32[]{:S(2)}) %collective-permute-start.12) | collective-permute-done | bytes 65568 | tf_op jit(solution)/shard_map/ppermute | solution.py:144
  39.6 0.1 collective-permute-start.13
  39.7 1.3 %collective-permute-done.13.other_ref = f32[16,2048]{1,0:T(8,128)S(1)} collective-permute-done((f32[16,2048]{1,0:T(8,128)S(1)}, f32[16,2048]{1,0:T(8,128)S(1)}, u32[]{:S(2)}, u32[]{:S(2)}) %collective-permute-start.13) | collective-permute-done | bytes 131104 | tf_op jit(solution)/shard_map/ppermute | solution.py:144
  41.0 0.0 copy-done.3
  41.0 0.7 %shard_map.68 = f32[16,4096]{1,0:T(8,128)} custom-call(s32[1]{0:T(128)} %bitcast.half_ref, f32[16,2048]{1,0:T(8,128)S(1)} %shard_map.67.mine_ref, f32[16,2048]{1,0:T(8,128)S(1)} %collective-permute-done.13.other_ref, bf16[16,4096]{1,0:T(8,128)(2,1)S(1)} %copy-done.3), custom_call_target="tpu_custom_call" | custom-call | bytes 786432 | tf_op jit(solution)/shard_map/pallas_call | solution.py:250
  (13 shorter events, 0.2 us)
Async XLA Ops:
  0.0 0.9 %copy-start = (bf16[16,4096]{1,0:T(8,128)(2,1)S(1)}, bf16[16,4096]{1,0:T(8,128)(2,1)}, u32[]{:S(2)}) copy-start(bf16[16,4096]{1,0:T(8,128)(2,1)} %param.10) | copy-start | bytes 393220
  0.9 18.0 %collective-permute-start.3 = (bf16[16,2048]{1,0:T(8,128)(2,1)S(1)}, bf16[16,2048]{1,0:T(8,128)(2,1)S(1)}, u32[]{:S(2)}, u32[]{:S(2)}) collective-permute-start(bf16[16,2048]{1,0:T(8,128)(2,1)S(1)} %constant_dynamic-slice_fusion.refs_0_), channel_id=1, source_target_pairs={{0,2},{2,0},{1,3},{3,1},{4,6},{6,4},{5,7},{7,5},{8,10},{10,8},{9,1... | collective-permute-start | bytes 196616 | tf_op jit(solution)/shard_map/ppermute | solution.py:144
  3.9 10.9 %collective-permute-start.2 = (bf16[16,2048]{1,0:T(8,128)(2,1)S(1)}, bf16[16,2048]{1,0:T(8,128)(2,1)S(1)}, u32[]{:S(2)}, u32[]{:S(2)}) collective-permute-start(bf16[16,2048]{1,0:T(8,128)(2,1)S(1)} %constant_dynamic-slice_fusion.refs_0_), channel_id=1, source_target_pairs={{0,4},{4,0},{8,12},{12,8},{1,5},{5,1},{9,13},{13,9},{2,6},{6,2},{1... | collective-permute-start | bytes 196616 | tf_op jit(solution)/shard_map/ppermute | solution.py:144
  5.4 9.9 %collective-permute-start.1 = (bf16[16,2048]{1,0:T(8,128)(2,1)S(1)}, bf16[16,2048]{1,0:T(8,128)(2,1)S(1)}, u32[]{:S(2)}, u32[]{:S(2)}) collective-permute-start(bf16[16,2048]{1,0:T(8,128)(2,1)S(1)} %constant_dynamic-slice_fusion.refs_0_), channel_id=1, source_target_pairs={{0,12},{4,8},{8,4},{12,0},{1,13},{5,9},{9,5},{13,1},{2,14},{6,10},... | collective-permute-start | bytes 196616 | tf_op jit(solution)/shard_map/ppermute | solution.py:144
  7.9 6.2 %collective-permute-start = (bf16[16,2048]{1,0:T(8,128)(2,1)S(1)}, bf16[16,2048]{1,0:T(8,128)(2,1)S(1)}, u32[]{:S(2)}, u32[]{:S(2)}) collective-permute-start(bf16[16,2048]{1,0:T(8,128)(2,1)S(1)} %constant_dynamic-slice_fusion.refs_0_), channel_id=1, source_target_pairs={{0,8},{4,12},{8,0},{12,4},{1,9},{5,13},{9,1},{13,5},{2,10},{6,14},... | collective-permute-start | bytes 196616 | tf_op jit(solution)/shard_map/ppermute | solution.py:144
  8.0 6.1 %copy-start.6 = (s32[1,1,8,8]{3,2,1,0:T(8,128)S(1)}, s32[1,1,8,8]{3,2,1,0:T(8,128)}, u32[]{:S(2)}) copy-start(s32[1,1,8,8]{3,2,1,0:T(8,128)} %param.9) | copy-start | bytes 772
  8.0 6.2 %copy-start.5 = (s32[4,8,4]{1,2,0:T(4,128)S(1)}, s32[4,8,4]{1,2,0:T(4,128)}, u32[]{:S(2)}) copy-start(s32[4,8,4]{1,2,0:T(4,128)} %param.8) | copy-start | bytes 1540
  14.6 2.2 %collective-permute-start.6 = (s32[4,4,8]{2,1,0:T(4,128)S(1)}, s32[4,4,8]{2,1,0:T(4,128)S(1)}, u32[]{:S(2)}, u32[]{:S(2)}) collective-permute-start(s32[4,4,8]{2,1,0:T(4,128)S(1)} %bitcast.6), channel_id=1, source_target_pairs={{0,1},{1,0},{2,3},{3,2},{4,5},{5,4},{6,7},{7,6},{8,9},{9,8},{10,11... | collective-permute-start | bytes 1544 | tf_op jit(solution)/shard_map/ppermute | solution.py:144
  14.7 7.4 %collective-permute-start.4 = (bf16[32,2048]{1,0:T(8,128)(2,1)S(1)}, bf16[32,2048]{1,0:T(8,128)(2,1)S(1)}, u32[]{:S(2)}, u32[]{:S(2)}) collective-permute-start(bf16[32,2048]{1,0:T(8,128)(2,1)S(1)} %pad_maximum_fusion), channel_id=1, source_target_pairs={{0,2},{2,0},{1,3},{3,1},{4,6},{6,4},{5,7},{7,5},{8,10},{10,8},{9,1... | collective-permute-start | bytes 393224 | tf_op jit(solution)/shard_map/ppermute | solution.py:144
  15.3 6.8 %collective-permute-start.5 = (bf16[16,2048]{1,0:T(8,128)(2,1)S(1)}, bf16[16,2048]{1,0:T(8,128)(2,1)S(1)}, u32[]{:S(2)}, u32[]{:S(2)}) collective-permute-start(bf16[16,2048]{1,0:T(8,128)(2,1)S(1)} %collective-permute-done.1.refs_2_), channel_id=1, source_target_pairs={{0,2},{2,0},{1,3},{3,1},{4,6},{6,4},{5,7},{7,5},{8,10},{10,8},{9,1... | collective-permute-start | bytes 196616 | tf_op jit(solution)/shard_map/ppermute | solution.py:144
  17.0 1.2 %copy-start.1 = (bf16[4,256,512]{2,1,0:T(8,128)(2,1)S(1)}, bf16[4,256,512]{2,1,0:T(8,128)(2,1)}, u32[]{:S(2)}) copy-start(bf16[4,256,512]{2,1,0:T(8,128)(2,1)} %refs_3_.1) | copy-start | bytes 3145732
  18.2 3.9 %copy-start.2 = (bf16[4,256,512]{2,1,0:T(8,128)(2,1)S(1)}, bf16[4,256,512]{2,1,0:T(8,128)(2,1)}, u32[]{:S(2)}) copy-start(bf16[4,256,512]{2,1,0:T(8,128)(2,1)} %refs_3_.1) | copy-start | bytes 3145732
  22.1 2.3 %copy-start.4 = (f32[4,256]{1,0:T(4,128)S(1)}, f32[4,256]{1,0:T(4,128)}, u32[]{:S(2)}) copy-start(f32[4,256]{1,0:T(4,128)} %refs_2_.1) | copy-start | bytes 12292
  23.2 1.2 %collective-permute-start.7 = (f32[4,256]{1,0:T(4,128)S(1)}, f32[4,256]{1,0:T(4,128)S(1)}, u32[]{:S(2)}, u32[]{:S(2)}) collective-permute-start(f32[4,256]{1,0:T(4,128)S(1)} %shard_map.65.refs_0_), channel_id=1, source_target_pairs={{0,1},{1,0},{2,3},{3,2},{4,5},{5,4},{6,7},{7,6},{8,9},{9,8},{10,11... | collective-permute-start | bytes 12296 | tf_op jit(solution)/shard_map/ppermute | solution.py:144
  25.8 6.4 %collective-permute-start.8 = (bf16[32,2048]{1,0:T(8,128)(2,1)S(1)}, bf16[32,2048]{1,0:T(8,128)(2,1)S(1)}, u32[]{:S(2)}, u32[]{:S(2)}) collective-permute-start(bf16[32,2048]{1,0:T(8,128)(2,1)S(1)} %get-tuple-element.24), channel_id=1, source_target_pairs={{0,2},{2,0},{1,3},{3,1},{4,6},{6,4},{5,7},{7,5},{8,10},{10,8},{9,1... | collective-permute-start | bytes 393224 | tf_op jit(solution)/shard_map/ppermute | solution.py:144
  26.4 8.4 %collective-permute-start.11 = (bf16[32,2048]{1,0:T(8,128)(2,1)S(1)}, bf16[32,2048]{1,0:T(8,128)(2,1)S(1)}, u32[]{:S(2)}, u32[]{:S(2)}) collective-permute-start(bf16[32,2048]{1,0:T(8,128)(2,1)S(1)} %get-tuple-element.27), channel_id=1, source_target_pairs={{0,2},{2,0},{1,3},{3,1},{4,6},{6,4},{5,7},{7,5},{8,10},{10,8},{9,1... | collective-permute-start | bytes 393224 | tf_op jit(solution)/shard_map/ppermute | solution.py:144
  32.2 6.8 %collective-permute-start.10 = (bf16[16,2048]{1,0:T(8,128)(2,1)S(1)}, bf16[16,2048]{1,0:T(8,128)(2,1)S(1)}, u32[]{:S(2)}, u32[]{:S(2)}) collective-permute-start(bf16[16,2048]{1,0:T(8,128)(2,1)S(1)} %get-tuple-element.29), channel_id=1, source_target_pairs={{0,8},{4,12},{8,0},{12,4},{1,9},{5,13},{9,1},{13,5},{2,10},{6,14},... | collective-permute-start | bytes 196616 | tf_op jit(solution)/shard_map/ppermute | solution.py:144
  32.3 6.7 %collective-permute-start.9 = (bf16[16,2048]{1,0:T(8,128)(2,1)S(1)}, bf16[16,2048]{1,0:T(8,128)(2,1)S(1)}, u32[]{:S(2)}, u32[]{:S(2)}) collective-permute-start(bf16[16,2048]{1,0:T(8,128)(2,1)S(1)} %get-tuple-element.30), channel_id=1, source_target_pairs={{0,12},{4,8},{8,4},{12,0},{1,13},{5,9},{9,5},{13,1},{2,14},{6,10},... | collective-permute-start | bytes 196616 | tf_op jit(solution)/shard_map/ppermute | solution.py:144
  34.8 4.8 %collective-permute-start.12 = (bf16[16,2048]{1,0:T(8,128)(2,1)S(1)}, bf16[16,2048]{1,0:T(8,128)(2,1)S(1)}, u32[]{:S(2)}, u32[]{:S(2)}) collective-permute-start(bf16[16,2048]{1,0:T(8,128)(2,1)S(1)} %add_convert_fusion), channel_id=1, source_target_pairs={{0,4},{4,0},{8,12},{12,8},{1,5},{5,1},{9,13},{13,9},{2,6},{6,2},{1... | collective-permute-start | bytes 196616 | tf_op jit(solution)/shard_map/ppermute | solution.py:144
  39.5 1.5 %copy-start.3 = (bf16[16,4096]{1,0:T(8,128)(2,1)S(1)}, bf16[16,4096]{1,0:T(8,128)(2,1)}, u32[]{:S(2)}) copy-start(bf16[16,4096]{1,0:T(8,128)(2,1)} %core_ref.1) | copy-start | bytes 393220
  39.6 1.4 %collective-permute-start.13 = (f32[16,2048]{1,0:T(8,128)S(1)}, f32[16,2048]{1,0:T(8,128)S(1)}, u32[]{:S(2)}, u32[]{:S(2)}) collective-permute-start(f32[16,2048]{1,0:T(8,128)S(1)} %shard_map.67.mine_ref), channel_id=1, source_target_pairs={{0,1},{1,0},{2,3},{3,2},{4,5},{5,4},{6,7},{7,6},{8,9},{9,8},{10,11... | collective-permute-start | bytes 393224 | tf_op jit(solution)/shard_map/ppermute | solution.py:144

commit v3 on v1

v3 whole, which is shorter than its diff:
```python
import functools

import jax
import jax.numpy as jnp
from jax import lax
from jax.experimental import pallas as pl
from jax.experimental.pallas import tpu as pltpu
from jax.sharding import PartitionSpec as P

GO = 64
VMEM_LIMIT = 50 * 1024 * 1024
NT = (((1,), (1,)), ((), ()))


def split_dot(left, right, dims=None):
    if dims is None:
        return jnp.dot(left, right, preferred_element_type=jnp.float32)
    return lax.dot_general(left, right, dims, preferred_element_type=jnp.float32)


def prepare_kernel(half_ref, values_hbm, left_ref, left_t_ref, values, arrived):
    batches, points, columns = values.shape
    copies = [pltpu.make_async_copy(values_hbm.at[t], values.at[t], arrived.at[t]) for t in range(batches)]
    for copy in copies:
        copy.start()
    groups = columns // GO
    kept = left_ref.shape[2]
    first = half_ref[0] * (kept // groups)
    at = lax.broadcasted_iota(jnp.int32, (kept, columns), 0)
    lane = lax.broadcasted_iota(jnp.int32, (kept, columns), 1)
    wanted = (at % groups) * GO + first + at // groups
    select = jnp.where(lane == wanted, 1.0, 0.0).astype(jnp.bfloat16)
    for t in range(batches):
        copies[t].wait()
        left_ref[t] = split_dot(values[t], select, NT).astype(jnp.bfloat16)
        left_t_ref[t] = split_dot(select, values[t], NT).astype(jnp.bfloat16)


def index_kernel(held, fetch_ref, slots_ref, rows_ref):
    owners, capacity = fetch_ref.shape
    slots = slots_ref[...]
    rows = jnp.zeros(slots.shape, jnp.int32)
    for owner in range(owners):
        for at in range(capacity):
            rows = jnp.where(slots == owner * capacity + at, fetch_ref[owner, at] + owner * held, rows)
    rows_ref[...] = rows


def row_table(place_ref, rows_ref, held, owners):
    rows = lax.bitwise_xor(rows_ref[...], place_ref[0] * held)
    row = lax.broadcasted_iota(jnp.int32, (owners * held, rows.shape[1]), 0)
    return jnp.where(row == rows, 1.0, 0.0)


def density_kernel(places, place_ref, *refs):
    piece_refs = refs[:len(places)]
    rows_ref, left_ref, values_ref, out_ref, table, dense = refs[len(places):]
    batches, points, columns = values_ref.shape
    groups = columns // GO
    held = piece_refs[0].shape[0]
    for ref, k in zip(piece_refs, places):
        table[k * held:(k + 1) * held, :] = ref[...]
    pick = row_table(place_ref, rows_ref, held, len(places)).T.astype(jnp.bfloat16)
    low = lax.broadcasted_iota(jnp.int32, (1, 1, groups, 128), 3) < GO
    for j in range(table.shape[1] // 128):
        lanes = slice(j * 128, (j + 1) * 128)
        got = split_dot(pick, table[:, lanes])
        got = got.reshape(batches, groups // 2, 2, groups, 128)
        even, odd = got[:, :, 0], got[:, :, 1]
        first = jnp.where(low, even, pltpu.roll(odd, GO, 3))
        second = jnp.where(low, pltpu.roll(even, GO, 3), odd)
        for t in range(batches):
            for q in range(groups // 2):
                both = jnp.concatenate([first[t, q], second[t, q]], axis=0)
                dense[t, j * 2 * groups:(j + 1) * 2 * groups, q * 128:(q + 1) * 128] = both.astype(jnp.bfloat16)
    for t in range(batches):
        product = split_dot(left_ref[t], dense[t]) * values_ref[t].astype(jnp.float32)
        folded = product[:, :128]
        for q in range(1, columns // 128):
            folded = folded + product[:, q * 128:(q + 1) * 128]
        out_ref[t:t + 1, :] = jnp.sum(folded.T, axis=0, keepdims=True)


def scatter_kernel(place_ref, *refs):
    mine_ref, other_ref, weight_ref, values_ref, left_t_ref, rows_ref = refs[:6]
    out_refs = refs[6:-2]
    high, rest = refs[-2:]
    pieces = len(out_refs)
    held = out_refs[0].shape[0]
    put = row_table(place_ref, rows_ref, held, pieces).astype(jnp.bfloat16)
    batches, points, columns = values_ref.shape
    groups = columns // GO
    kept = left_t_ref.shape[1]
    steps = kept // (2 * groups)
    potential = weight_ref[...] * jnp.tanh(mine_ref[...] + other_ref[...])
    low = lax.broadcasted_iota(jnp.int32, (1, groups, 128), 2) < GO
    for t in range(batches):
        factor = jnp.broadcast_to(potential[t:t + 1, :], (128, points)).T
        factor = jnp.concatenate([factor] * (columns // 128), axis=1)
        weighted = (values_ref[t].astype(jnp.float32) * factor).astype(jnp.bfloat16)
        part = split_dot(left_t_ref[t], weighted)
        for q in range(groups // 2):
            cut = part[:, q * 128:(q + 1) * 128].reshape(steps, 2, groups, 128)
            first, second = cut[:, 0], cut[:, 1]
            even = jnp.where(low, first, pltpu.roll(second, GO, 2))
            odd = jnp.where(low, pltpu.roll(first, GO, 2), second)
            at = (t * groups + 2 * q) * groups
            for j in range(steps):
                both = jnp.concatenate([even[j], odd[j]], axis=0)
                top = both.astype(jnp.bfloat16)
                high[at:at + 2 * groups, j * 128:(j + 1) * 128] = top
                rest[at:at + 2 * groups, j * 128:(j + 1) * 128] = (both - top.astype(jnp.float32)).astype(jnp.bfloat16)
    step = max(1, min(pieces, 128 // held))
    for k in range(0, pieces, step):
        some = put[k * held:(k + step) * held, :]
        total = split_dot(some, high[...]) + split_dot(some, rest[...])
        for i in range(step):
            out_refs[k + i][...] = total[i * held:(i + 1) * held, :].astype(jnp.bfloat16)


def sum_kernel(*refs):
    out_ref = refs[-1]
    total = refs[0][...].astype(jnp.float32)
    for ref in refs[1:-1]:
        total = total + ref[...].astype(jnp.float32)
    out_ref[...] = total.astype(out_ref.dtype)


def finish_kernel(half_ref, mine_ref, other_ref, core_ref, out_ref):
    wide = mine_ref.shape[1]
    own = pl.multiple_of(half_ref[0] * wide, wide)
    far = pl.multiple_of((1 - half_ref[0]) * wide, wide)
    out_ref[:, pl.ds(own, wide)] = core_ref[:, pl.ds(own, wide)].astype(jnp.float32) + mine_ref[...]
    out_ref[:, pl.ds(far, wide)] = core_ref[:, pl.ds(far, wide)].astype(jnp.float32) + other_ref[...]


def call(kernel, outs, count, scratch=(), scalar=False, flops=0, moved=0, space=pltpu.VMEM):
    specs = [pl.BlockSpec(memory_space=space)] * count
    if scalar:
        specs = [pl.BlockSpec(memory_space=pltpu.SMEM)] + specs
    out_specs = jax.tree.map(lambda _: pl.BlockSpec(memory_space=pltpu.VMEM), outs)
    return pl.pallas_call(
        kernel,
        out_shape=outs,
        in_specs=specs,
        out_specs=out_specs,
        scratch_shapes=list(scratch),
        compiler_params=pltpu.CompilerParams(vmem_limit_bytes=VMEM_LIMIT),
        cost_estimate=pl.CostEstimate(flops=flops, bytes_accessed=moved, transcendentals=0),
    )


def swap(array, axis, count, step):
    return lax.ppermute(array, axis, [(i, i ^ step) for i in range(count)])


def per_device(basis_values, point_weights, slot_ids, fetch_rows, density_blocks, core_blocks):
    rows_z, rows_x = lax.axis_size("batch"), lax.axis_size("pair")
    z, x, half = lax.axis_index("batch"), lax.axis_index("pair"), lax.axis_index("orb")
    owners = rows_z * rows_x
    batches, points, columns = basis_values.shape
    groups, own_groups = slot_ids.shape[1], slot_ids.shape[2]
    held, square = density_blocks.shape
    capacity = fetch_rows.shape[3]
    wide = square // 2
    table_rows = owners * held
    entries = batches * groups * groups
    kept = columns // 2
    bf16, f32 = jnp.bfloat16, jnp.float32

    far = rows_z // 2
    upper = [dz for dz in range(far + 1, rows_z)]
    lower = [dz for dz in range(1, far)]
    side = list(range(1, rows_x))
    direct = (
        [far * rows_x]
        + [dz * rows_x for dz in upper]
        + [dz * rows_x + dx for dz in upper for dx in side]
        + side
        + [dz * rows_x + dx for dz in lower for dx in [0] + side]
    )
    grid = ("batch", "pair")

    mine = lax.dynamic_slice_in_dim(density_blocks, half * wide, wide, 1)
    pieces = {0: mine}
    for k in reversed(direct):
        pieces[k] = swap(mine, grid, owners, k)
    for dx in side:
        pieces[far * rows_x + dx] = swap(pieces[far * rows_x], "pair", rows_x, dx)
    order = [0] + direct[::-1] + [far * rows_x + dx for dx in side]

    half_at = half.reshape(1).astype(jnp.int32)
    left, left_t = call(
        prepare_kernel,
        (
            jax.ShapeDtypeStruct((batches, points, kept), bf16),
            jax.ShapeDtypeStruct((batches, kept, points), bf16),
        ),
        1,
        scratch=(pltpu.VMEM(basis_values.shape, bf16), pltpu.SemaphoreType.DMA((batches,))),
        scalar=True,
        space=pl.ANY,
        flops=4 * batches * points * columns * kept,
        moved=3 * batches * points * columns * 2,
    )(half_at, basis_values)

    own_rows = pl.pallas_call(
        functools.partial(index_kernel, held),
        out_shape=jax.ShapeDtypeStruct((batches, own_groups, groups), jnp.int32),
        in_specs=[pl.BlockSpec(memory_space=pltpu.SMEM), pl.BlockSpec(memory_space=pltpu.VMEM)],
        out_specs=pl.BlockSpec(memory_space=pltpu.VMEM),
    )(fetch_rows.reshape(owners, capacity), slot_ids.transpose(0, 2, 1))
    other_rows = swap(own_rows, "orb", 2, 1)
    rows = jnp.concatenate(
        [jnp.where(half == 0, own_rows, other_rows), jnp.where(half == 0, other_rows, own_rows)], axis=1
    ).reshape(1, entries)
    place = (z * rows_x + x).reshape(1).astype(jnp.int32)

    partial = call(
        functools.partial(density_kernel, order),
        jax.ShapeDtypeStruct((batches, points), f32),
        owners + 3,
        scalar=True,
        scratch=(pltpu.VMEM((table_rows, wide), bf16), pltpu.VMEM((batches, kept, columns), bf16)),
        flops=2 * batches * points * columns * kept,
        moved=2 * batches * points * columns * 2,
    )(place, *[pieces[k] for k in order], rows, left, basis_values)
    partial_other = swap(partial, "orb", 2, 1)

    sums = call(
        scatter_kernel,
        [jax.ShapeDtypeStruct((held, wide), bf16)] * owners,
        6,
        scalar=True,
        scratch=(pltpu.VMEM((entries, wide), bf16), pltpu.VMEM((entries, wide), bf16)),
        flops=2 * batches * points * columns * kept,
        moved=2 * batches * points * columns * 2,
    )(place, partial, partial_other, point_weights, basis_values, left_t, rows)

    landed = []
    for k in direct[1:]:
        landed.append(swap(sums[k], grid, owners, k))
    joined = sums[far * rows_x].astype(f32)
    for dx in side:
        joined = joined + swap(sums[far * rows_x + dx], "pair", rows_x, dx).astype(f32)
    landed.append(swap(joined.astype(bf16), "batch", rows_z, far))
    landed.append(sums[0])
    total = call(
        sum_kernel, jax.ShapeDtypeStruct((held, wide), f32), len(landed), moved=len(landed) * held * wide * 2
    )(*landed)
    total_other = swap(total, "orb", 2, 1)
    return call(
        finish_kernel, jax.ShapeDtypeStruct((held, square), f32), 3, scalar=True, moved=held * square * 12
    )(half_at, total, total_other, core_blocks)


def solution(mesh):
    placed = (
        P(("groups", "batch", "pair"), None, None),
        P(("groups", "batch", "pair"), None),
        P(("groups", "batch", "pair"), None, "orb"),
        P(("groups", "batch", "pair"), "orb", None, None),
        P(("groups", "batch", "pair"), None),
        P(("groups", "batch", "pair"), None),
    )
    return jax.shard_map(
        per_device,
        mesh=mesh,
        in_specs=placed,
        out_specs=P(("groups", "batch", "pair"), None),
        check_vma=False,
    )
```

time: 38.8 us -> 43 us (1.11)
  Pallas kernels: 3.95 us -> 6.13 us
  waiting for transfers between devices: 10.5 us -> 12.2 us
  starting transfers between devices: 20.8 us -> 21.4 us
  other arithmetic: 0.52 us -> 0.03 us
    ppermute x17, waiting for transfers between devices: 10.5 us -> 12.2 us  [swap(): return lax.ppermute(array, axis, [(i, i ^ step) for i in range(count)])]
    pallas_call x2 -> x3, Pallas kernels: 2.43 us -> 3.82 us  [the longest x1 1.41 us: per_device(): pl.pallas_call(functools.partial(index_kernel, held), out_shape=jax.Shape...]
    pallas_call x1, Pallas kernels: 0.75 us -> 1.52 us  [per_device(): call(prepare_kernel, (jax.ShapeDtypeStruct((batches, points, kept), bf16)...]
    ppermute x17, starting transfers between devices: 20.8 us -> 21.4 us  [swap(): return lax.ppermute(array, axis, [(i, i ^ step) for i in range(count)])]
    unnamed x14 -> x12, local copies, waits for them, and re-layouts: 2.4 us -> 2.74 us
  transfers between devices with their start and end apart: 17 -> 17, of which waited for: 8 -> 9; matrix products, arithmetic and copies ran while one was open for 0% -> 0% of each run, Pallas kernels for 2% -> 7%
where the time goes in v3:
time: 43 us; the launch traced here: 42.7 us
  starting transfers between devices  21.4 us (50%)
  waiting for transfers between devices  12.2 us (28%)
  Pallas kernels  6.13 us (14%)
  local copies, waits for them, and re-layouts  2.83 us (7%)
    ppermute x17, starting transfers between devices, swap(): return lax.ppermute(array, axis, [(i, i ^ step) for i in range(count)])  21.4 us
    ppermute x17, waiting for transfers between devices, swap(): return lax.ppermute(array, axis, [(i, i ^ step) for i in range(count)])  12.2 us
    unnamed x12, local copies, waits for them, and re-layouts  2.74 us
    pallas_call x1, Pallas kernels, per_device(): call(prepare_kernel, (jax.ShapeDtypeStruct((batches, points, kept), bf16)...  1.52 us
    pallas_call x1, Pallas kernels, per_device(): pl.pallas_call(functools.partial(index_kernel, held), out_shape=jax.Shape...  1.41 us
    pallas_call x1, Pallas kernels, per_device(): call(scatter_kernel, [jax.ShapeDtypeStruct((held, wide), bf16)] * owners,...  1.35 us
    pallas_call x1, Pallas kernels, per_device(): call(functools.partial(density_kernel, order), jax.ShapeDtypeStruct((batc...  1.07 us
  transfers between devices with their start and end apart: 17, of which 9 were waited for; matrix products, arithmetic and copies ran while one was open for 0% of the time, Pallas kernels for 7%

profile of v3, /device:TPU:0, one launch (start us, length us, event | category | flops | bytes accessed | tf_op | source)
XLA Modules:
  0.0 42.7 jit_solution(2126014165284959743)
XLA Ops:
  0.0 0.0 copy-start
  0.0 0.9 %copy-done = bf16[16,4096]{1,0:T(8,128)(2,1)S(1)} copy-done((bf16[16,4096]{1,0:T(8,128)(2,1)S(1)}, bf16[16,4096]{1,0:T(8,128)(2,1)}, u32[]{:S(2)}) %copy-start) | copy-done | bytes 131096
  0.9 4.0 %collective-permute-start.5 = (bf16[16,2048]{1,0:T(8,128)(2,1)S(1)}, bf16[16,2048]{1,0:T(8,128)(2,1)S(1)}, u32[]{:S(2)}, u32[]{:S(2)}) collective-permute-start(bf16[16,2048]{1,0:T(8,128)(2,1)S(1)} %constant_dynamic-slice_fusion.refs_0_), channel_id=1, source_target_pairs={{0,8},{2,10},{4,12},{6,14},{8,0},{10,2},{12,4},{14,6},{1,9},{3,11}... | collective-permute-start | bytes 196616 | tf_op jit(solution)/shard_map/ppermute | solution.py:154
  4.9 1.3 %collective-permute-start.4 = (bf16[16,2048]{1,0:T(8,128)(2,1)S(1)}, bf16[16,2048]{1,0:T(8,128)(2,1)S(1)}, u32[]{:S(2)}, u32[]{:S(2)}) collective-permute-start(bf16[16,2048]{1,0:T(8,128)(2,1)S(1)} %constant_dynamic-slice_fusion.refs_0_), channel_id=1, source_target_pairs={{0,12},{2,14},{4,8},{6,10},{8,4},{10,6},{12,0},{14,2},{1,13},{3,15... | collective-permute-start | bytes 196616 | tf_op jit(solution)/shard_map/ppermute | solution.py:154
  6.3 3.4 %collective-permute-start.3 = (bf16[16,2048]{1,0:T(8,128)(2,1)S(1)}, bf16[16,2048]{1,0:T(8,128)(2,1)S(1)}, u32[]{:S(2)}, u32[]{:S(2)}) collective-permute-start(bf16[16,2048]{1,0:T(8,128)(2,1)S(1)} %constant_dynamic-slice_fusion.refs_0_), channel_id=1, source_target_pairs={{0,14},{2,12},{4,10},{6,8},{8,6},{10,4},{12,2},{14,0},{1,15},{3,13... | collective-permute-start | bytes 196616 | tf_op jit(solution)/shard_map/ppermute | solution.py:154
  9.7 0.5 %collective-permute-start.2 = (bf16[16,2048]{1,0:T(8,128)(2,1)S(1)}, bf16[16,2048]{1,0:T(8,128)(2,1)S(1)}, u32[]{:S(2)}, u32[]{:S(2)}) collective-permute-start(bf16[16,2048]{1,0:T(8,128)(2,1)S(1)} %constant_dynamic-slice_fusion.refs_0_), channel_id=1, source_target_pairs={{0,2},{2,0},{4,6},{6,4},{8,10},{10,8},{12,14},{14,12},{1,3},{3,1},... | collective-permute-start | bytes 196616 | tf_op jit(solution)/shard_map/ppermute | solution.py:154
  10.2 1.4 %shard_map.64 = s32[4,4,8]{2,1,0:T(4,128)} custom-call(s32[8,8]{1,0:T(8,128)} %bitcast.13, s32[4,4,8]{2,1,0:T(4,128)} %bitcast.11), custom_call_target="tpu_custom_call" | custom-call | tf_op jit(solution)/shard_map/pallas_call | solution.py:207
  11.6 0.0 collective-permute-start.7
  11.7 1.2 %copy-done.1 = bf16[4,256,512]{2,1,0:T(8,128)(2,1)S(1)} copy-done((bf16[4,256,512]{2,1,0:T(8,128)(2,1)S(1)}, bf16[4,256,512]{2,1,0:T(8,128)(2,1)}, u32[]{:S(2)}) %copy-start.1) | copy-done | bytes 1048600
  12.9 1.5 %shard_map.65 = (bf16[4,256,256]{2,1,0:T(8,128)(2,1)S(1)}, bf16[4,256,256]{2,1,0:T(8,128)(2,1)S(1)}) custom-call(s32[1]{0:T(128)} %bitcast.half_ref, bf16[4,256,512]{2,1,0:T(8,128)(2,1)S(1)} %copy-done.1), custom_call_target="tpu_custom_call" | custom-call | flops 536870912 | bytes 3145728 | tf_op jit(solution)/shard_map/pallas_call | solution.py:193
  14.4 0.0 copy-start.5
  14.4 0.0 collective-permute-done.7
  14.4 0.1 collective-permute-start.1
  14.5 0.6 %copy-done.5 = s32[4,4,8]{2,1,0:T(4,128)S(1)} copy-done((s32[4,4,8]{2,1,0:T(4,128)S(1)}, s32[4,4,8]{2,1,0:T(4,128)}, u32[]{:S(2)}) %copy-start.5) | copy-done | bytes 536
  15.1 0.0 collective-permute-done.5.refs_6_
  15.1 2.4 %collective-permute-start = (bf16[16,2048]{1,0:T(8,128)(2,1)S(1)}, bf16[16,2048]{1,0:T(8,128)(2,1)S(1)}, u32[]{:S(2)}, u32[]{:S(2)}) collective-permute-start(bf16[16,2048]{1,0:T(8,128)(2,1)S(1)} %constant_dynamic-slice_fusion.refs_0_), channel_id=1, source_target_pairs={{0,6},{2,4},{4,2},{6,0},{8,14},{10,12},{12,10},{14,8},{1,7},{3,5},... | collective-permute-start | bytes 196616 | tf_op jit(solution)/shard_map/ppermute | solution.py:154
  17.5 0.0 collective-permute-done.4.refs_5_
  17.5 0.5 %collective-permute-start.6 = (bf16[16,2048]{1,0:T(8,128)(2,1)S(1)}, bf16[16,2048]{1,0:T(8,128)(2,1)S(1)}, u32[]{:S(2)}, u32[]{:S(2)}) collective-permute-start(bf16[16,2048]{1,0:T(8,128)(2,1)S(1)} %collective-permute-done.5.refs_6_), channel_id=1, source_target_pairs={{0,2},{2,0},{1,3},{3,1},{4,6},{6,4},{5,7},{7,5},{8,10},{10,8},{9,1... | collective-permute-start | bytes 196616 | tf_op jit(solution)/shard_map/ppermute | solution.py:154
  18.1 0.1 reshape.15.refs_8_.refs_5_
  18.2 0.0 collective-permute-done.3.refs_4_
  18.2 0.0 collective-permute-done.2.refs_3_
  18.2 0.8 %collective-permute-done.1.refs_2_ = bf16[16,2048]{1,0:T(8,128)(2,1)S(1)} collective-permute-done((bf16[16,2048]{1,0:T(8,128)(2,1)S(1)}, bf16[16,2048]{1,0:T(8,128)(2,1)S(1)}, u32[]{:S(2)}, u32[]{:S(2)}) %collective-permute-start.1) | collective-permute-done | bytes 65568 | tf_op jit(solution)/shard_map/ppermute | solution.py:154
  19.0 2.4 %collective-permute-done.refs_1_ = bf16[16,2048]{1,0:T(8,128)(2,1)S(1)} collective-permute-done((bf16[16,2048]{1,0:T(8,128)(2,1)S(1)}, bf16[16,2048]{1,0:T(8,128)(2,1)S(1)}, u32[]{:S(2)}, u32[]{:S(2)}) %collective-permute-start) | collective-permute-done | bytes 65568 | tf_op jit(solution)/shard_map/ppermute | solution.py:154
  21.4 1.2 %collective-permute-done.6.refs_7_ = bf16[16,2048]{1,0:T(8,128)(2,1)S(1)} collective-permute-done((bf16[16,2048]{1,0:T(8,128)(2,1)S(1)}, bf16[16,2048]{1,0:T(8,128)(2,1)S(1)}, u32[]{:S(2)}, u32[]{:S(2)}) %collective-permute-start.6) | collective-permute-done | bytes 65568 | tf_op jit(solution)/shard_map/ppermute | solution.py:154
  22.6 0.0 copy-done.2
  22.6 1.1 %shard_map.66.refs_0_ = f32[4,256]{1,0:T(4,128)S(1)} custom-call(s32[1]{0:T(128)} %bitcast.1.place_ref, bf16[16,2048]{1,0:T(8,128)(2,1)S(1)} %constant_dynamic-slice_fusion.refs_0_, bf16[16,2048]{1,0:T(8,128)(2,1)S(1)} %collective-permute-done.refs_1_, bf16[16,2048]{1,0:T(8,128)(2,1)S(1)} %collective-permute-done.1.refs_2_, ...), custom_call_target="tpu_custom_call" | custom-call | flops 268435456 | bytes 2097152 | tf_op jit(solution)/shard_map/pallas_call | solution.py:219
  23.7 0.1 collective-permute-start.8
  23.8 1.2 %collective-permute-done.8.refs_1_ = f32[4,256]{1,0:T(4,128)S(1)} collective-permute-done((f32[4,256]{1,0:T(4,128)S(1)}, f32[4,256]{1,0:T(4,128)S(1)}, u32[]{:S(2)}, u32[]{:S(2)}) %collective-permute-start.8) | collective-permute-done | bytes 4128 | tf_op jit(solution)/shard_map/ppermute | solution.py:154
  24.9 0.0 copy-done.4
  24.9 1.3 %shard_map.67 = (bf16[16,2048]{1,0:T(8,128)(2,1)S(1)}, bf16[16,2048]{1,0:T(8,128)(2,1)S(1)}, bf16[16,2048]{1,0:T(8,128)(2,1)S(1)}, bf16[16,2048]{1,0:T(8,128)(2,...) custom-call(s32[1]{0:T(128)} %bitcast.1.place_ref, ...), custom_call_target="tpu_custom_call" | custom-call | flops 268435456 | bytes 2097152 | tf_op jit(solution)/shard_map/pallas_call | solution.py:230
  26.3 0.9 %collective-permute-start.14 = (bf16[16,2048]{1,0:T(8,128)(2,1)S(1)}, bf16[16,2048]{1,0:T(8,128)(2,1)S(1)}, u32[]{:S(2)}, u32[]{:S(2)}) collective-permute-start(bf16[16,2048]{1,0:T(8,128)(2,1)S(1)} %get-tuple-element.23), channel_id=1, source_target_pairs={{0,2},{2,0},{1,3},{3,1},{4,6},{6,4},{5,7},{7,5},{8,10},{10,8},{9,1... | collective-permute-start | bytes 196616 | tf_op jit(solution)/shard_map/ppermute | solution.py:154
  27.1 1.3 %collective-permute-start.9 = (bf16[16,2048]{1,0:T(8,128)(2,1)S(1)}, bf16[16,2048]{1,0:T(8,128)(2,1)S(1)}, u32[]{:S(2)}, u32[]{:S(2)}) collective-permute-start(bf16[16,2048]{1,0:T(8,128)(2,1)S(1)} %get-tuple-element.17), channel_id=1, source_target_pairs={{0,12},{2,14},{4,8},{6,10},{8,4},{10,6},{12,0},{14,2},{1,13},{3,15... | collective-permute-start | bytes 196616 | tf_op jit(solution)/shard_map/ppermute | solution.py:154
  28.5 3.1 %collective-permute-start.10 = (bf16[16,2048]{1,0:T(8,128)(2,1)S(1)}, bf16[16,2048]{1,0:T(8,128)(2,1)S(1)}, u32[]{:S(2)}, u32[]{:S(2)}) collective-permute-start(bf16[16,2048]{1,0:T(8,128)(2,1)S(1)} %get-tuple-element.18), channel_id=1, source_target_pairs={{0,14},{2,12},{4,10},{6,8},{8,6},{10,4},{12,2},{14,0},{1,15},{3,13... | collective-permute-start | bytes 196616 | tf_op jit(solution)/shard_map/ppermute | solution.py:154
  31.6 0.8 %collective-permute-start.11 = (bf16[16,2048]{1,0:T(8,128)(2,1)S(1)}, bf16[16,2048]{1,0:T(8,128)(2,1)S(1)}, u32[]{:S(2)}, u32[]{:S(2)}) collective-permute-start(bf16[16,2048]{1,0:T(8,128)(2,1)S(1)} %get-tuple-element.19), channel_id=1, source_target_pairs={{0,2},{2,0},{4,6},{6,4},{8,10},{10,8},{12,14},{14,12},{1,3},{3,1},... | collective-permute-start | bytes 196616 | tf_op jit(solution)/shard_map/ppermute | solution.py:154
  32.4 0.0 collective-permute-start.12
  32.4 0.0 collective-permute-done.14
  32.4 2.7 %collective-permute-start.13 = (bf16[16,2048]{1,0:T(8,128)(2,1)S(1)}, bf16[16,2048]{1,0:T(8,128)(2,1)S(1)}, u32[]{:S(2)}, u32[]{:S(2)}) collective-permute-start(bf16[16,2048]{1,0:T(8,128)(2,1)S(1)} %get-tuple-element.21), channel_id=1, source_target_pairs={{0,6},{2,4},{4,2},{6,0},{8,14},{10,12},{12,10},{14,8},{1,7},{3,5},... | collective-permute-start | bytes 196616 | tf_op jit(solution)/shard_map/ppermute | solution.py:154
  35.1 0.0 collective-permute-done.9.refs_0_
  35.2 0.1 collective-permute-start.15
  35.2 0.8 %collective-permute-done.10.refs_1_ = bf16[16,2048]{1,0:T(8,128)(2,1)S(1)} collective-permute-done((bf16[16,2048]{1,0:T(8,128)(2,1)S(1)}, bf16[16,2048]{1,0:T(8,128)(2,1)S(1)}, u32[]{:S(2)}, u32[]{:S(2)}) %collective-permute-start.10) | collective-permute-done | bytes 65568 | tf_op jit(solution)/shard_map/ppermute | solution.py:154
  36.0 1.1 %collective-permute-done.11.refs_2_ = bf16[16,2048]{1,0:T(8,128)(2,1)S(1)} collective-permute-done((bf16[16,2048]{1,0:T(8,128)(2,1)S(1)}, bf16[16,2048]{1,0:T(8,128)(2,1)S(1)}, u32[]{:S(2)}, u32[]{:S(2)}) %collective-permute-start.11) | collective-permute-done | bytes 65568 | tf_op jit(solution)/shard_map/ppermute | solution.py:154
  37.1 0.0 collective-permute-done.12.refs_3_
  37.1 1.8 %collective-permute-done.13.refs_4_ = bf16[16,2048]{1,0:T(8,128)(2,1)S(1)} collective-permute-done((bf16[16,2048]{1,0:T(8,128)(2,1)S(1)}, bf16[16,2048]{1,0:T(8,128)(2,1)S(1)}, u32[]{:S(2)}, u32[]{:S(2)}) %collective-permute-start.13) | collective-permute-done | bytes 65568 | tf_op jit(solution)/shard_map/ppermute | solution.py:154
  39.0 1.6 %collective-permute-done.15.refs_5_ = bf16[16,2048]{1,0:T(8,128)(2,1)S(1)} collective-permute-done((bf16[16,2048]{1,0:T(8,128)(2,1)S(1)}, bf16[16,2048]{1,0:T(8,128)(2,1)S(1)}, u32[]{:S(2)}, u32[]{:S(2)}) %collective-permute-start.15) | collective-permute-done | bytes 65568 | tf_op jit(solution)/shard_map/ppermute | solution.py:154
  40.5 0.1 shard_map.68.mine_ref
  40.6 0.1 collective-permute-start.16
  40.7 1.3 %collective-permute-done.16.other_ref = f32[16,2048]{1,0:T(8,128)S(1)} collective-permute-done((f32[16,2048]{1,0:T(8,128)S(1)}, f32[16,2048]{1,0:T(8,128)S(1)}, u32[]{:S(2)}, u32[]{:S(2)}) %collective-permute-start.16) | collective-permute-done | bytes 131104 | tf_op jit(solution)/shard_map/ppermute | solution.py:154
  42.0 0.7 %shard_map.69 = f32[16,4096]{1,0:T(8,128)} custom-call(s32[1]{0:T(128)} %bitcast.half_ref, f32[16,2048]{1,0:T(8,128)S(1)} %shard_map.68.mine_ref, f32[16,2048]{1,0:T(8,128)S(1)} %collective-permute-done.16.other_ref, bf16[16,4096]{1,0:T(8,128)(2,1)S(1)} %copy-done.3), custom_call_target="tpu_custom_call" | custom-call | bytes 786432 | tf_op jit(solution)/shard_map/pallas_call | solution.py:252
  (9 shorter events, 0.0 us)
Async XLA Ops:
  0.0 0.9 %copy-start = (bf16[16,4096]{1,0:T(8,128)(2,1)S(1)}, bf16[16,4096]{1,0:T(8,128)(2,1)}, u32[]{:S(2)}) copy-start(bf16[16,4096]{1,0:T(8,128)(2,1)} %param.10) | copy-start | bytes 393220
  0.9 14.2 %collective-permute-start.5 = (bf16[16,2048]{1,0:T(8,128)(2,1)S(1)}, bf16[16,2048]{1,0:T(8,128)(2,1)S(1)}, u32[]{:S(2)}, u32[]{:S(2)}) collective-permute-start(bf16[16,2048]{1,0:T(8,128)(2,1)S(1)} %constant_dynamic-slice_fusion.refs_0_), channel_id=1, source_target_pairs={{0,8},{2,10},{4,12},{6,14},{8,0},{10,2},{12,4},{14,6},{1,9},{3,11}... | collective-permute-start | bytes 196616 | tf_op jit(solution)/shard_map/ppermute | solution.py:154
  4.9 12.6 %collective-permute-start.4 = (bf16[16,2048]{1,0:T(8,128)(2,1)S(1)}, bf16[16,2048]{1,0:T(8,128)(2,1)S(1)}, u32[]{:S(2)}, u32[]{:S(2)}) collective-permute-start(bf16[16,2048]{1,0:T(8,128)(2,1)S(1)} %constant_dynamic-slice_fusion.refs_0_), channel_id=1, source_target_pairs={{0,12},{2,14},{4,8},{6,10},{8,4},{10,6},{12,0},{14,2},{1,13},{3,15... | collective-permute-start | bytes 196616 | tf_op jit(solution)/shard_map/ppermute | solution.py:154
  6.3 11.9 %collective-permute-start.3 = (bf16[16,2048]{1,0:T(8,128)(2,1)S(1)}, bf16[16,2048]{1,0:T(8,128)(2,1)S(1)}, u32[]{:S(2)}, u32[]{:S(2)}) collective-permute-start(bf16[16,2048]{1,0:T(8,128)(2,1)S(1)} %constant_dynamic-slice_fusion.refs_0_), channel_id=1, source_target_pairs={{0,14},{2,12},{4,10},{6,8},{8,6},{10,4},{12,2},{14,0},{1,15},{3,13... | collective-permute-start | bytes 196616 | tf_op jit(solution)/shard_map/ppermute | solution.py:154
  9.7 8.5 %collective-permute-start.2 = (bf16[16,2048]{1,0:T(8,128)(2,1)S(1)}, bf16[16,2048]{1,0:T(8,128)(2,1)S(1)}, u32[]{:S(2)}, u32[]{:S(2)}) collective-permute-start(bf16[16,2048]{1,0:T(8,128)(2,1)S(1)} %constant_dynamic-slice_fusion.refs_0_), channel_id=1, source_target_pairs={{0,2},{2,0},{4,6},{6,4},{8,10},{10,8},{12,14},{14,12},{1,3},{3,1},... | collective-permute-start | bytes 196616 | tf_op jit(solution)/shard_map/ppermute | solution.py:154
  11.6 2.8 %collective-permute-start.7 = (s32[4,4,8]{2,1,0:T(4,128)}, s32[4,4,8]{2,1,0:T(4,128)S(1)}, u32[]{:S(2)}, u32[]{:S(2)}) collective-permute-start(s32[4,4,8]{2,1,0:T(4,128)} %shard_map.64), channel_id=1, source_target_pairs={{0,1},{1,0},{2,3},{3,2},{4,5},{5,4},{6,7},{7,6},{8,9},{9,8},{10,11... | collective-permute-start | bytes 1544 | tf_op jit(solution)/shard_map/ppermute | solution.py:154
  11.7 1.2 %copy-start.1 = (bf16[4,256,512]{2,1,0:T(8,128)(2,1)S(1)}, bf16[4,256,512]{2,1,0:T(8,128)(2,1)}, u32[]{:S(2)}) copy-start(bf16[4,256,512]{2,1,0:T(8,128)(2,1)} %refs_3_.1) | copy-start | bytes 3145732
  12.9 9.7 %copy-start.2 = (bf16[4,256,512]{2,1,0:T(8,128)(2,1)S(1)}, bf16[4,256,512]{2,1,0:T(8,128)(2,1)}, u32[]{:S(2)}) copy-start(bf16[4,256,512]{2,1,0:T(8,128)(2,1)} %refs_3_.1) | copy-start | bytes 3145732
  14.4 0.7 %copy-start.5 = (s32[4,4,8]{2,1,0:T(4,128)S(1)}, s32[4,4,8]{2,1,0:T(4,128)}, u32[]{:S(2)}) copy-start(s32[4,4,8]{2,1,0:T(4,128)} %shard_map.64) | copy-start | bytes 1540
  14.4 4.6 %collective-permute-start.1 = (bf16[16,2048]{1,0:T(8,128)(2,1)S(1)}, bf16[16,2048]{1,0:T(8,128)(2,1)S(1)}, u32[]{:S(2)}, u32[]{:S(2)}) collective-permute-start(bf16[16,2048]{1,0:T(8,128)(2,1)S(1)} %constant_dynamic-slice_fusion.refs_0_), channel_id=1, source_target_pairs={{0,4},{2,6},{4,0},{6,2},{8,12},{10,14},{12,8},{14,10},{1,5},{3,7},... | collective-permute-start | bytes 196616 | tf_op jit(solution)/shard_map/ppermute | solution.py:154
  15.1 6.3 %collective-permute-start = (bf16[16,2048]{1,0:T(8,128)(2,1)S(1)}, bf16[16,2048]{1,0:T(8,128)(2,1)S(1)}, u32[]{:S(2)}, u32[]{:S(2)}) collective-permute-start(bf16[16,2048]{1,0:T(8,128)(2,1)S(1)} %constant_dynamic-slice_fusion.refs_0_), channel_id=1, source_target_pairs={{0,6},{2,4},{4,2},{6,0},{8,14},{10,12},{12,10},{14,8},{1,7},{3,5},... | collective-permute-start | bytes 196616 | tf_op jit(solution)/shard_map/ppermute | solution.py:154
  17.5 5.1 %collective-permute-start.6 = (bf16[16,2048]{1,0:T(8,128)(2,1)S(1)}, bf16[16,2048]{1,0:T(8,128)(2,1)S(1)}, u32[]{:S(2)}, u32[]{:S(2)}) collective-permute-start(bf16[16,2048]{1,0:T(8,128)(2,1)S(1)} %collective-permute-done.5.refs_6_), channel_id=1, source_target_pairs={{0,2},{2,0},{1,3},{3,1},{4,6},{6,4},{5,7},{7,5},{8,10},{10,8},{9,1... | collective-permute-start | bytes 196616 | tf_op jit(solution)/shard_map/ppermute | solution.py:154
  22.6 2.3 %copy-start.4 = (f32[4,256]{1,0:T(4,128)S(1)}, f32[4,256]{1,0:T(4,128)}, u32[]{:S(2)}) copy-start(f32[4,256]{1,0:T(4,128)} %refs_2_.1) | copy-start | bytes 12292
  23.7 1.2 %collective-permute-start.8 = (f32[4,256]{1,0:T(4,128)S(1)}, f32[4,256]{1,0:T(4,128)S(1)}, u32[]{:S(2)}, u32[]{:S(2)}) collective-permute-start(f32[4,256]{1,0:T(4,128)S(1)} %shard_map.66.refs_0_), channel_id=1, source_target_pairs={{0,1},{1,0},{2,3},{3,2},{4,5},{5,4},{6,7},{7,6},{8,9},{9,8},{10,11... | collective-permute-start | bytes 12296 | tf_op jit(solution)/shard_map/ppermute | solution.py:154
  26.3 6.2 %collective-permute-start.14 = (bf16[16,2048]{1,0:T(8,128)(2,1)S(1)}, bf16[16,2048]{1,0:T(8,128)(2,1)S(1)}, u32[]{:S(2)}, u32[]{:S(2)}) collective-permute-start(bf16[16,2048]{1,0:T(8,128)(2,1)S(1)} %get-tuple-element.23), channel_id=1, source_target_pairs={{0,2},{2,0},{1,3},{3,1},{4,6},{6,4},{5,7},{7,5},{8,10},{10,8},{9,1... | collective-permute-start | bytes 196616 | tf_op jit(solution)/shard_map/ppermute | solution.py:154
  27.1 8.0 %collective-permute-start.9 = (bf16[16,2048]{1,0:T(8,128)(2,1)S(1)}, bf16[16,2048]{1,0:T(8,128)(2,1)S(1)}, u32[]{:S(2)}, u32[]{:S(2)}) collective-permute-start(bf16[16,2048]{1,0:T(8,128)(2,1)S(1)} %get-tuple-element.17), channel_id=1, source_target_pairs={{0,12},{2,14},{4,8},{6,10},{8,4},{10,6},{12,0},{14,2},{1,13},{3,15... | collective-permute-start | bytes 196616 | tf_op jit(solution)/shard_map/ppermute | solution.py:154
  28.5 7.5 %collective-permute-start.10 = (bf16[16,2048]{1,0:T(8,128)(2,1)S(1)}, bf16[16,2048]{1,0:T(8,128)(2,1)S(1)}, u32[]{:S(2)}, u32[]{:S(2)}) collective-permute-start(bf16[16,2048]{1,0:T(8,128)(2,1)S(1)} %get-tuple-element.18), channel_id=1, source_target_pairs={{0,14},{2,12},{4,10},{6,8},{8,6},{10,4},{12,2},{14,0},{1,15},{3,13... | collective-permute-start | bytes 196616 | tf_op jit(solution)/shard_map/ppermute | solution.py:154
  31.6 5.5 %collective-permute-start.11 = (bf16[16,2048]{1,0:T(8,128)(2,1)S(1)}, bf16[16,2048]{1,0:T(8,128)(2,1)S(1)}, u32[]{:S(2)}, u32[]{:S(2)}) collective-permute-start(bf16[16,2048]{1,0:T(8,128)(2,1)S(1)} %get-tuple-element.19), channel_id=1, source_target_pairs={{0,2},{2,0},{4,6},{6,4},{8,10},{10,8},{12,14},{14,12},{1,3},{3,1},... | collective-permute-start | bytes 196616 | tf_op jit(solution)/shard_map/ppermute | solution.py:154
  32.4 4.7 %collective-permute-start.12 = (bf16[16,2048]{1,0:T(8,128)(2,1)S(1)}, bf16[16,2048]{1,0:T(8,128)(2,1)S(1)}, u32[]{:S(2)}, u32[]{:S(2)}) collective-permute-start(bf16[16,2048]{1,0:T(8,128)(2,1)S(1)} %get-tuple-element.20), channel_id=1, source_target_pairs={{0,4},{2,6},{4,0},{6,2},{8,12},{10,14},{12,8},{14,10},{1,5},{3,7},... | collective-permute-start | bytes 196616 | tf_op jit(solution)/shard_map/ppermute | solution.py:154
  32.4 6.5 %collective-permute-start.13 = (bf16[16,2048]{1,0:T(8,128)(2,1)S(1)}, bf16[16,2048]{1,0:T(8,128)(2,1)S(1)}, u32[]{:S(2)}, u32[]{:S(2)}) collective-permute-start(bf16[16,2048]{1,0:T(8,128)(2,1)S(1)} %get-tuple-element.21), channel_id=1, source_target_pairs={{0,6},{2,4},{4,2},{6,0},{8,14},{10,12},{12,10},{14,8},{1,7},{3,5},... | collective-permute-start | bytes 196616 | tf_op jit(solution)/shard_map/ppermute | solution.py:154
  35.2 5.4 %collective-permute-start.15 = (bf16[16,2048]{1,0:T(8,128)(2,1)S(1)}, bf16[16,2048]{1,0:T(8,128)(2,1)S(1)}, u32[]{:S(2)}, u32[]{:S(2)}) collective-permute-start(bf16[16,2048]{1,0:T(8,128)(2,1)S(1)} %add_convert_fusion), channel_id=1, source_target_pairs={{0,8},{4,12},{8,0},{12,4},{1,9},{5,13},{9,1},{13,5},{2,10},{6,14},... | collective-permute-start | bytes 196616 | tf_op jit(solution)/shard_map/ppermute | solution.py:154
  40.5 1.5 %copy-start.3 = (bf16[16,4096]{1,0:T(8,128)(2,1)S(1)}, bf16[16,4096]{1,0:T(8,128)(2,1)}, u32[]{:S(2)}) copy-start(bf16[16,4096]{1,0:T(8,128)(2,1)} %core_ref.1) | copy-start | bytes 393220
  40.6 1.4 %collective-permute-start.16 = (f32[16,2048]{1,0:T(8,128)S(1)}, f32[16,2048]{1,0:T(8,128)S(1)}, u32[]{:S(2)}, u32[]{:S(2)}) collective-permute-start(f32[16,2048]{1,0:T(8,128)S(1)} %shard_map.68.mine_ref), channel_id=1, source_target_pairs={{0,1},{1,0},{2,3},{3,2},{4,5},{5,4},{6,7},{7,6},{8,9},{9,8},{10,11... | collective-permute-start | bytes 393224 | tf_op jit(solution)/shard_map/ppermute | solution.py:154

commit v4 on v3

--- a/solution.py
+++ b/solution.py
@@ -40,9 +40,11 @@
     owners, capacity = fetch_ref.shape
     slots = slots_ref[...]
     rows = jnp.zeros(slots.shape, jnp.int32)
+    stored = fetch_ref[...] + held * lax.broadcasted_iota(jnp.int32, (owners, capacity), 0)
     for owner in range(owners):
         for at in range(capacity):
-            rows = jnp.where(slots == owner * capacity + at, fetch_ref[owner, at] + owner * held, rows)
+            home = stored[owner:owner + 1, at:at + 1].reshape(1, 1, 1)
+            rows = jnp.where(slots == owner * capacity + at, home, rows)
     rows_ref[...] = rows
 
 
@@ -168,28 +170,21 @@
     kept = columns // 2
     bf16, f32 = jnp.bfloat16, jnp.float32
 
-    far = rows_z // 2
-    upper = [dz for dz in range(far + 1, rows_z)]
-    lower = [dz for dz in range(1, far)]
+    steps = list(range(rows_z // 2, rows_z)) + list(range(1, rows_z // 2))
     side = list(range(1, rows_x))
-    direct = (
-        [far * rows_x]
-        + [dz * rows_x for dz in upper]
-        + [dz * rows_x + dx for dz in upper for dx in side]
-        + side
-        + [dz * rows_x + dx for dz in lower for dx in [0] + side]
-    )
-    grid = ("batch", "pair")
 
     mine = lax.dynamic_slice_in_dim(density_blocks, half * wide, wide, 1)
     pieces = {0: mine}
-    for k in reversed(direct):
-        pieces[k] = swap(mine, grid, owners, k)
     for dx in side:
-        pieces[far * rows_x + dx] = swap(pieces[far * rows_x], "pair", rows_x, dx)
-    order = [0] + direct[::-1] + [far * rows_x + dx for dx in side]
-
-    half_at = half.reshape(1).astype(jnp.int32)
+        pieces[dx] = swap(mine, "pair", rows_x, dx)
+    for dz in steps[::-1]:
+        pieces[dz * rows_x] = swap(mine, "batch", rows_z, dz)
+    for dz in steps[rows_z // 2:] + steps[:rows_z // 2]:
+        for dx in side:
+            pieces[dz * rows_x + dx] = swap(pieces[dz * rows_x], "pair", rows_x, dx)
+    order = list(pieces)
+
+    half_at, _ = lax.optimization_barrier((half.reshape(1).astype(jnp.int32), pieces[(rows_z - 1) * rows_x]))
     left, left_t = call(
         prepare_kernel,
         (
@@ -207,7 +202,7 @@
     own_rows = pl.pallas_call(
         functools.partial(index_kernel, held),
         out_shape=jax.ShapeDtypeStruct((batches, own_groups, groups), jnp.int32),
-        in_specs=[pl.BlockSpec(memory_space=pltpu.SMEM), pl.BlockSpec(memory_space=pltpu.VMEM)],
+        in_specs=[pl.BlockSpec(memory_space=pltpu.VMEM)] * 2,
         out_specs=pl.BlockSpec(memory_space=pltpu.VMEM),
     )(fetch_rows.reshape(owners, capacity), slot_ids.transpose(0, 2, 1))
     other_rows = swap(own_rows, "orb", 2, 1)
@@ -238,13 +233,18 @@
     )(place, partial, partial_other, point_weights, basis_values, left_t, rows)
 
     landed = []
-    for k in direct[1:]:
-        landed.append(swap(sums[k], grid, owners, k))
-    joined = sums[far * rows_x].astype(f32)
+    own = sums[:rows_x]
+    for dz in steps:
+        joined = sums[dz * rows_x].astype(f32)
+        for dx in side:
+            joined = joined + swap(sums[dz * rows_x + dx], "pair", rows_x, dx).astype(f32)
+        joined = joined.astype(bf16)
+        if dz == steps[0]:
+            joined, *own = lax.optimization_barrier((joined, *own))
+        landed.append(swap(joined, "batch", rows_z, dz))
     for dx in side:
-        joined = joined + swap(sums[far * rows_x + dx], "pair", rows_x, dx).astype(f32)
-    landed.append(swap(joined.astype(bf16), "batch", rows_z, far))
-    landed.append(sums[0])
+        landed.append(swap(own[dx], "pair", rows_x, dx))
+    landed.append(own[0])
     total = call(
         sum_kernel, jax.ShapeDtypeStruct((held, wide), f32), len(landed), moved=len(landed) * held * wide * 2
     )(*landed)

time: 43 us -> 38.7 us (0.900)
  starting transfers between devices: 21.4 us -> 17.8 us
  local copies, waits for them, and re-layouts: 2.83 us -> 2.24 us
    ppermute x17, starting transfers between devices: 21.4 us -> 17.8 us  [swap(): return lax.ppermute(array, axis, [(i, i ^ step) for i in range(count)])]
    unnamed x12, local copies, waits for them, and re-layouts: 2.74 us -> 2.14 us
  transfers between devices with their start and end apart: 17 -> 17, of which waited for: 9 -> 9; matrix products, arithmetic and copies ran while one was open for 0% -> 0% of each run, Pallas kernels for 7% -> 8%
where the time goes in v4:
time: 38.7 us; the launch traced here: 38.5 us
  starting transfers between devices  17.8 us (46%)
  waiting for transfers between devices  12 us (31%)
  Pallas kernels  6.21 us (16%)
  local copies, waits for them, and re-layouts  2.24 us (6%)
    ppermute x17, starting transfers between devices, swap(): return lax.ppermute(array, axis, [(i, i ^ step) for i in range(count)])  17.8 us
    ppermute x17, waiting for transfers between devices, swap(): return lax.ppermute(array, axis, [(i, i ^ step) for i in range(count)])  12 us
    unnamed x12, local copies, waits for them, and re-layouts  2.14 us
    pallas_call x1, Pallas kernels, per_device(): call(prepare_kernel, (jax.ShapeDtypeStruct((batches, points, kept), bf16)...  1.52 us
    pallas_call x1, Pallas kernels, per_device(): pl.pallas_call(functools.partial(index_kernel, held), out_shape=jax.Shape...  1.5 us
    pallas_call x1, Pallas kernels, per_device(): call(scatter_kernel, [jax.ShapeDtypeStruct((held, wide), bf16)] * owners,...  1.35 us
    pallas_call x1, Pallas kernels, per_device(): call(functools.partial(density_kernel, order), jax.ShapeDtypeStruct((batc...  1.07 us
  transfers between devices with their start and end apart: 17, of which 9 were waited for; matrix products, arithmetic and copies ran while one was open for 0% of the time, Pallas kernels for 8%

profile of v4, /device:TPU:0, one launch (start us, length us, event | category | flops | bytes accessed | tf_op | source)
XLA Modules:
  0.0 38.5 jit_solution(9521164357274515169)
XLA Ops:
  0.0 0.0 copy-start
  0.0 0.9 %copy-done = bf16[16,4096]{1,0:T(8,128)(2,1)S(1)} copy-done((bf16[16,4096]{1,0:T(8,128)(2,1)S(1)}, bf16[16,4096]{1,0:T(8,128)(2,1)}, u32[]{:S(2)}) %copy-start) | copy-done | bytes 131096
  0.9 4.0 %collective-permute-start.3 = (bf16[16,2048]{1,0:T(8,128)(2,1)S(1)}, bf16[16,2048]{1,0:T(8,128)(2,1)S(1)}, u32[]{:S(2)}, u32[]{:S(2)}) collective-permute-start(bf16[16,2048]{1,0:T(8,128)(2,1)S(1)} %constant_dynamic-slice_fusion.refs_0_), channel_id=1, source_target_pairs={{0,8},{4,12},{8,0},{12,4},{1,9},{5,13},{9,1},{13,5},{2,10},{6,14},... | collective-permute-start | bytes 196616 | tf_op jit(solution)/shard_map/ppermute | solution.py:156
  4.9 1.6 %collective-permute-start.2 = (bf16[16,2048]{1,0:T(8,128)(2,1)S(1)}, bf16[16,2048]{1,0:T(8,128)(2,1)S(1)}, u32[]{:S(2)}, u32[]{:S(2)}) collective-permute-start(bf16[16,2048]{1,0:T(8,128)(2,1)S(1)} %constant_dynamic-slice_fusion.refs_0_), channel_id=1, source_target_pairs={{0,4},{4,0},{8,12},{12,8},{1,5},{5,1},{9,13},{13,9},{2,6},{6,2},{1... | collective-permute-start | bytes 196616 | tf_op jit(solution)/shard_map/ppermute | solution.py:156
  6.5 1.5 %collective-permute-start.1 = (bf16[16,2048]{1,0:T(8,128)(2,1)S(1)}, bf16[16,2048]{1,0:T(8,128)(2,1)S(1)}, u32[]{:S(2)}, u32[]{:S(2)}) collective-permute-start(bf16[16,2048]{1,0:T(8,128)(2,1)S(1)} %constant_dynamic-slice_fusion.refs_0_), channel_id=1, source_target_pairs={{0,2},{2,0},{1,3},{3,1},{4,6},{6,4},{5,7},{7,5},{8,10},{10,8},{9,1... | collective-permute-start | bytes 196616 | tf_op jit(solution)/shard_map/ppermute | solution.py:156
  8.0 0.2 collective-permute-start
  8.2 1.5 %shard_map.64 = s32[4,4,8]{2,1,0:T(4,128)} custom-call(s32[8,8]{1,0:T(8,128)} %bitcast.13, s32[4,4,8]{2,1,0:T(4,128)} %bitcast.11), custom_call_target="tpu_custom_call" | custom-call | tf_op jit(solution)/shard_map/pallas_call | solution.py:202
  9.7 0.0 collective-permute-start.7
  9.7 1.4 %collective-permute-done.7 = s32[4,4,8]{2,1,0:T(4,128)S(1)} collective-permute-done((s32[4,4,8]{2,1,0:T(4,128)}, s32[4,4,8]{2,1,0:T(4,128)S(1)}, u32[]{:S(2)}, u32[]{:S(2)}) %collective-permute-start.7) | collective-permute-done | bytes 544 | tf_op jit(solution)/shard_map/ppermute | solution.py:156
  11.1 0.0 copy-done.5
  11.1 0.0 collective-permute-done.3.refs_4_
  11.1 0.4 collective-permute-start.5
  11.5 0.0 collective-permute-done.2.refs_2_
  11.5 1.7 %collective-permute-start.4 = (bf16[16,2048]{1,0:T(8,128)(2,1)S(1)}, bf16[16,2048]{1,0:T(8,128)(2,1)S(1)}, u32[]{:S(2)}, u32[]{:S(2)}) collective-permute-start(bf16[16,2048]{1,0:T(8,128)(2,1)S(1)} %collective-permute-done.2.refs_2_), channel_id=1, source_target_pairs={{0,2},{2,0},{1,3},{3,1},{4,6},{6,4},{5,7},{7,5},{8,10},{10,8},{9,1... | collective-permute-start | bytes 196616 | tf_op jit(solution)/shard_map/ppermute | solution.py:156
  13.2 0.8 %collective-permute-done.refs_3_ = bf16[16,2048]{1,0:T(8,128)(2,1)S(1)} collective-permute-done((bf16[16,2048]{1,0:T(8,128)(2,1)S(1)}, bf16[16,2048]{1,0:T(8,128)(2,1)S(1)}, u32[]{:S(2)}, u32[]{:S(2)}) %collective-permute-start) | collective-permute-done | bytes 65568 | tf_op jit(solution)/shard_map/ppermute | solution.py:156
  14.1 0.5 %collective-permute-start.6 = (bf16[16,2048]{1,0:T(8,128)(2,1)S(1)}, bf16[16,2048]{1,0:T(8,128)(2,1)S(1)}, u32[]{:S(2)}, u32[]{:S(2)}) collective-permute-start(bf16[16,2048]{1,0:T(8,128)(2,1)S(1)} %collective-permute-done.refs_3_), channel_id=1, source_target_pairs={{0,2},{2,0},{1,3},{3,1},{4,6},{6,4},{5,7},{7,5},{8,10},{10,8},{9,1... | collective-permute-start | bytes 196616 | tf_op jit(solution)/shard_map/ppermute | solution.py:156
  14.6 0.1 reshape.15.refs_8_.refs_5_
  14.7 0.0 copy-start.1
  14.7 1.2 %copy-done.1 = bf16[4,256,512]{2,1,0:T(8,128)(2,1)S(1)} copy-done((bf16[4,256,512]{2,1,0:T(8,128)(2,1)S(1)}, bf16[4,256,512]{2,1,0:T(8,128)(2,1)}, u32[]{:S(2)}) %copy-start.1) | copy-done | bytes 1048600
  15.9 1.5 %shard_map.65 = (bf16[4,256,256]{2,1,0:T(8,128)(2,1)S(1)}, bf16[4,256,256]{2,1,0:T(8,128)(2,1)S(1)}) custom-call(s32[1]{0:T(128)} %bitcast.half_ref, bf16[4,256,512]{2,1,0:T(8,128)(2,1)S(1)} %copy-done.1), custom_call_target="tpu_custom_call" | custom-call | flops 536870912 | bytes 3145728 | tf_op jit(solution)/shard_map/pallas_call | solution.py:188
  17.5 0.0 collective-permute-done.1.refs_1_
  17.5 0.0 collective-permute-done.5.refs_6_
  17.5 0.0 collective-permute-done.4.refs_5_
  17.5 0.8 %collective-permute-done.6.refs_7_ = bf16[16,2048]{1,0:T(8,128)(2,1)S(1)} collective-permute-done((bf16[16,2048]{1,0:T(8,128)(2,1)S(1)}, bf16[16,2048]{1,0:T(8,128)(2,1)S(1)}, u32[]{:S(2)}, u32[]{:S(2)}) %collective-permute-start.6) | collective-permute-done | bytes 65568 | tf_op jit(solution)/shard_map/ppermute | solution.py:156
  18.3 0.0 copy-done.2
  18.4 1.1 %shard_map.66.refs_0_ = f32[4,256]{1,0:T(4,128)S(1)} custom-call(s32[1]{0:T(128)} %bitcast.1.place_ref, bf16[16,2048]{1,0:T(8,128)(2,1)S(1)} %constant_dynamic-slice_fusion.refs_0_, bf16[16,2048]{1,0:T(8,128)(2,1)S(1)} %collective-permute-done.1.refs_1_, bf16[16,2048]{1,0:T(8,128)(2,1)S(1)} %collective-permute-done.2.refs_2_, ...), custom_call_target="tpu_custom_call" | custom-call | flops 268435456 | bytes 2097152 | tf_op jit(solution)/shard_map/pallas_call | solution.py:214
  19.4 0.1 collective-permute-start.8
  19.5 1.2 %collective-permute-done.8.refs_1_ = f32[4,256]{1,0:T(4,128)S(1)} collective-permute-done((f32[4,256]{1,0:T(4,128)S(1)}, f32[4,256]{1,0:T(4,128)S(1)}, u32[]{:S(2)}, u32[]{:S(2)}) %collective-permute-start.8) | collective-permute-done | bytes 4128 | tf_op jit(solution)/shard_map/ppermute | solution.py:156
  20.7 0.0 copy-done.4
  20.7 1.3 %shard_map.67 = (bf16[16,2048]{1,0:T(8,128)(2,1)S(1)}, bf16[16,2048]{1,0:T(8,128)(2,1)S(1)}, bf16[16,2048]{1,0:T(8,128)(2,1)S(1)}, bf16[16,2048]{1,0:T(8,128)(2,...) custom-call(s32[1]{0:T(128)} %bitcast.1.place_ref, ...), custom_call_target="tpu_custom_call" | custom-call | flops 268435456 | bytes 2097152 | tf_op jit(solution)/shard_map/pallas_call | solution.py:225
  22.0 0.7 %collective-permute-start.9 = (bf16[16,2048]{1,0:T(8,128)(2,1)S(1)}, bf16[16,2048]{1,0:T(8,128)(2,1)S(1)}, u32[]{:S(2)}, u32[]{:S(2)}) collective-permute-start(bf16[16,2048]{1,0:T(8,128)(2,1)S(1)} %get-tuple-element.23), channel_id=1, source_target_pairs={{0,2},{2,0},{1,3},{3,1},{4,6},{6,4},{5,7},{7,5},{8,10},{10,8},{9,1... | collective-permute-start | bytes 196616 | tf_op jit(solution)/shard_map/ppermute | solution.py:156
  22.8 1.3 %collective-permute-start.11 = (bf16[16,2048]{1,0:T(8,128)(2,1)S(1)}, bf16[16,2048]{1,0:T(8,128)(2,1)S(1)}, u32[]{:S(2)}, u32[]{:S(2)}) collective-permute-start(bf16[16,2048]{1,0:T(8,128)(2,1)S(1)} %get-tuple-element.28), channel_id=1, source_target_pairs={{0,2},{2,0},{1,3},{3,1},{4,6},{6,4},{5,7},{7,5},{8,10},{10,8},{9,1... | collective-permute-start | bytes 196616 | tf_op jit(solution)/shard_map/ppermute | solution.py:156
  24.1 0.7 %collective-permute-start.13 = (bf16[16,2048]{1,0:T(8,128)(2,1)S(1)}, bf16[16,2048]{1,0:T(8,128)(2,1)S(1)}, u32[]{:S(2)}, u32[]{:S(2)}) collective-permute-start(bf16[16,2048]{1,0:T(8,128)(2,1)S(1)} %get-tuple-element.30), channel_id=1, source_target_pairs={{0,2},{2,0},{1,3},{3,1},{4,6},{6,4},{5,7},{7,5},{8,10},{10,8},{9,1... | collective-permute-start | bytes 196616 | tf_op jit(solution)/shard_map/ppermute | solution.py:156
  24.8 2.2 %collective-permute-done.9 = bf16[16,2048]{1,0:T(8,128)(2,1)S(1)} collective-permute-done((bf16[16,2048]{1,0:T(8,128)(2,1)S(1)}, bf16[16,2048]{1,0:T(8,128)(2,1)S(1)}, u32[]{:S(2)}, u32[]{:S(2)}) %collective-permute-start.9) | collective-permute-done | bytes 65568 | tf_op jit(solution)/shard_map/ppermute | solution.py:156
  27.0 1.6 %collective-permute-start.10 = (bf16[16,2048]{1,0:T(8,128)(2,1)S(1)}, bf16[16,2048]{1,0:T(8,128)(2,1)S(1)}, u32[]{:S(2)}, u32[]{:S(2)}) collective-permute-start(bf16[16,2048]{1,0:T(8,128)(2,1)S(1)} %add_convert_fusion.2), channel_id=1, source_target_pairs={{0,8},{4,12},{8,0},{12,4},{1,9},{5,13},{9,1},{13,5},{2,10},{6,14},... | collective-permute-start | bytes 196616 | tf_op jit(solution)/shard_map/ppermute | solution.py:156
  28.6 0.4 collective-permute-start.15
  29.0 0.0 collective-permute-done.11
  29.0 2.9 %collective-permute-start.12 = (bf16[16,2048]{1,0:T(8,128)(2,1)S(1)}, bf16[16,2048]{1,0:T(8,128)(2,1)S(1)}, u32[]{:S(2)}, u32[]{:S(2)}) collective-permute-start(bf16[16,2048]{1,0:T(8,128)(2,1)S(1)} %add_convert_fusion.1), channel_id=1, source_target_pairs={{0,12},{4,8},{8,4},{12,0},{1,13},{5,9},{9,5},{13,1},{2,14},{6,10},... | collective-permute-start | bytes 196616 | tf_op jit(solution)/shard_map/ppermute | solution.py:156
  31.9 0.0 collective-permute-done.13
  32.0 0.0 copy-start.3
  32.0 0.1 collective-permute-start.14
  32.0 2.3 %collective-permute-done.10.refs_0_ = bf16[16,2048]{1,0:T(8,128)(2,1)S(1)} collective-permute-done((bf16[16,2048]{1,0:T(8,128)(2,1)S(1)}, bf16[16,2048]{1,0:T(8,128)(2,1)S(1)}, u32[]{:S(2)}, u32[]{:S(2)}) %collective-permute-start.10) | collective-permute-done | bytes 65568 | tf_op jit(solution)/shard_map/ppermute | solution.py:156
  34.3 0.0 collective-permute-done.15.refs_3_
  34.3 0.9 %collective-permute-done.12.refs_1_ = bf16[16,2048]{1,0:T(8,128)(2,1)S(1)} collective-permute-done((bf16[16,2048]{1,0:T(8,128)(2,1)S(1)}, bf16[16,2048]{1,0:T(8,128)(2,1)S(1)}, u32[]{:S(2)}, u32[]{:S(2)}) %collective-permute-start.12) | collective-permute-done | bytes 65568 | tf_op jit(solution)/shard_map/ppermute | solution.py:156
  35.2 1.1 %collective-permute-done.14.refs_2_ = bf16[16,2048]{1,0:T(8,128)(2,1)S(1)} collective-permute-done((bf16[16,2048]{1,0:T(8,128)(2,1)S(1)}, bf16[16,2048]{1,0:T(8,128)(2,1)S(1)}, u32[]{:S(2)}, u32[]{:S(2)}) %collective-permute-start.14) | collective-permute-done | bytes 65568 | tf_op jit(solution)/shard_map/ppermute | solution.py:156
  36.3 0.1 collective-permute-start.16
  36.4 1.3 %collective-permute-done.16.other_ref = f32[16,2048]{1,0:T(8,128)S(1)} collective-permute-done((f32[16,2048]{1,0:T(8,128)S(1)}, f32[16,2048]{1,0:T(8,128)S(1)}, u32[]{:S(2)}, u32[]{:S(2)}) %collective-permute-start.16) | collective-permute-done | bytes 131104 | tf_op jit(solution)/shard_map/ppermute | solution.py:156
  37.8 0.7 %shard_map.69 = f32[16,4096]{1,0:T(8,128)} custom-call(s32[1]{0:T(128)} %bitcast.half_ref, f32[16,2048]{1,0:T(8,128)S(1)} %shard_map.68.mine_ref, f32[16,2048]{1,0:T(8,128)S(1)} %collective-permute-done.16.other_ref, bf16[16,4096]{1,0:T(8,128)(2,1)S(1)} %copy-done.3), custom_call_target="tpu_custom_call" | custom-call | bytes 786432 | tf_op jit(solution)/shard_map/pallas_call | solution.py:252
  (11 shorter events, 0.1 us)
Async XLA Ops:
  0.0 0.9 %copy-start = (bf16[16,4096]{1,0:T(8,128)(2,1)S(1)}, bf16[16,4096]{1,0:T(8,128)(2,1)}, u32[]{:S(2)}) copy-start(bf16[16,4096]{1,0:T(8,128)(2,1)} %param.10) | copy-start | bytes 393220
  0.9 10.2 %collective-permute-start.3 = (bf16[16,2048]{1,0:T(8,128)(2,1)S(1)}, bf16[16,2048]{1,0:T(8,128)(2,1)S(1)}, u32[]{:S(2)}, u32[]{:S(2)}) collective-permute-start(bf16[16,2048]{1,0:T(8,128)(2,1)S(1)} %constant_dynamic-slice_fusion.refs_0_), channel_id=1, source_target_pairs={{0,8},{4,12},{8,0},{12,4},{1,9},{5,13},{9,1},{13,5},{2,10},{6,14},... | collective-permute-start | bytes 196616 | tf_op jit(solution)/shard_map/ppermute | solution.py:156
  4.9 6.6 %collective-permute-start.2 = (bf16[16,2048]{1,0:T(8,128)(2,1)S(1)}, bf16[16,2048]{1,0:T(8,128)(2,1)S(1)}, u32[]{:S(2)}, u32[]{:S(2)}) collective-permute-start(bf16[16,2048]{1,0:T(8,128)(2,1)S(1)} %constant_dynamic-slice_fusion.refs_0_), channel_id=1, source_target_pairs={{0,4},{4,0},{8,12},{12,8},{1,5},{5,1},{9,13},{13,9},{2,6},{6,2},{1... | collective-permute-start | bytes 196616 | tf_op jit(solution)/shard_map/ppermute | solution.py:156
  6.5 11.0 %collective-permute-start.1 = (bf16[16,2048]{1,0:T(8,128)(2,1)S(1)}, bf16[16,2048]{1,0:T(8,128)(2,1)S(1)}, u32[]{:S(2)}, u32[]{:S(2)}) collective-permute-start(bf16[16,2048]{1,0:T(8,128)(2,1)S(1)} %constant_dynamic-slice_fusion.refs_0_), channel_id=1, source_target_pairs={{0,2},{2,0},{1,3},{3,1},{4,6},{6,4},{5,7},{7,5},{8,10},{10,8},{9,1... | collective-permute-start | bytes 196616 | tf_op jit(solution)/shard_map/ppermute | solution.py:156
  8.0 6.1 %collective-permute-start = (bf16[16,2048]{1,0:T(8,128)(2,1)S(1)}, bf16[16,2048]{1,0:T(8,128)(2,1)S(1)}, u32[]{:S(2)}, u32[]{:S(2)}) collective-permute-start(bf16[16,2048]{1,0:T(8,128)(2,1)S(1)} %constant_dynamic-slice_fusion.refs_0_), channel_id=1, source_target_pairs={{0,12},{4,8},{8,4},{12,0},{1,13},{5,9},{9,5},{13,1},{2,14},{6,10},... | collective-permute-start | bytes 196616 | tf_op jit(solution)/shard_map/ppermute | solution.py:156
  9.7 1.4 %collective-permute-start.7 = (s32[4,4,8]{2,1,0:T(4,128)}, s32[4,4,8]{2,1,0:T(4,128)S(1)}, u32[]{:S(2)}, u32[]{:S(2)}) collective-permute-start(s32[4,4,8]{2,1,0:T(4,128)} %shard_map.64), channel_id=1, source_target_pairs={{0,1},{1,0},{2,3},{3,2},{4,5},{5,4},{6,7},{7,6},{8,9},{9,8},{10,11... | collective-permute-start | bytes 1544 | tf_op jit(solution)/shard_map/ppermute | solution.py:156
  9.7 1.4 %copy-start.5 = (s32[4,4,8]{2,1,0:T(4,128)S(1)}, s32[4,4,8]{2,1,0:T(4,128)}, u32[]{:S(2)}) copy-start(s32[4,4,8]{2,1,0:T(4,128)} %shard_map.64) | copy-start | bytes 1540
  11.1 6.3 %collective-permute-start.5 = (bf16[16,2048]{1,0:T(8,128)(2,1)S(1)}, bf16[16,2048]{1,0:T(8,128)(2,1)S(1)}, u32[]{:S(2)}, u32[]{:S(2)}) collective-permute-start(bf16[16,2048]{1,0:T(8,128)(2,1)S(1)} %collective-permute-done.3.refs_4_), channel_id=1, source_target_pairs={{0,2},{2,0},{1,3},{3,1},{4,6},{6,4},{5,7},{7,5},{8,10},{10,8},{9,1... | collective-permute-start | bytes 196616 | tf_op jit(solution)/shard_map/ppermute | solution.py:156
  11.5 6.0 %collective-permute-start.4 = (bf16[16,2048]{1,0:T(8,128)(2,1)S(1)}, bf16[16,2048]{1,0:T(8,128)(2,1)S(1)}, u32[]{:S(2)}, u32[]{:S(2)}) collective-permute-start(bf16[16,2048]{1,0:T(8,128)(2,1)S(1)} %collective-permute-done.2.refs_2_), channel_id=1, source_target_pairs={{0,2},{2,0},{1,3},{3,1},{4,6},{6,4},{5,7},{7,5},{8,10},{10,8},{9,1... | collective-permute-start | bytes 196616 | tf_op jit(solution)/shard_map/ppermute | solution.py:156
  14.1 4.3 %collective-permute-start.6 = (bf16[16,2048]{1,0:T(8,128)(2,1)S(1)}, bf16[16,2048]{1,0:T(8,128)(2,1)S(1)}, u32[]{:S(2)}, u32[]{:S(2)}) collective-permute-start(bf16[16,2048]{1,0:T(8,128)(2,1)S(1)} %collective-permute-done.refs_3_), channel_id=1, source_target_pairs={{0,2},{2,0},{1,3},{3,1},{4,6},{6,4},{5,7},{7,5},{8,10},{10,8},{9,1... | collective-permute-start | bytes 196616 | tf_op jit(solution)/shard_map/ppermute | solution.py:156
  14.7 1.2 %copy-start.1 = (bf16[4,256,512]{2,1,0:T(8,128)(2,1)S(1)}, bf16[4,256,512]{2,1,0:T(8,128)(2,1)}, u32[]{:S(2)}) copy-start(bf16[4,256,512]{2,1,0:T(8,128)(2,1)} %refs_3_.1) | copy-start | bytes 3145732
  15.9 2.4 %copy-start.2 = (bf16[4,256,512]{2,1,0:T(8,128)(2,1)S(1)}, bf16[4,256,512]{2,1,0:T(8,128)(2,1)}, u32[]{:S(2)}) copy-start(bf16[4,256,512]{2,1,0:T(8,128)(2,1)} %refs_3_.1) | copy-start | bytes 3145732
  18.4 2.3 %copy-start.4 = (f32[4,256]{1,0:T(4,128)S(1)}, f32[4,256]{1,0:T(4,128)}, u32[]{:S(2)}) copy-start(f32[4,256]{1,0:T(4,128)} %refs_2_.1) | copy-start | bytes 12292
  19.4 1.2 %collective-permute-start.8 = (f32[4,256]{1,0:T(4,128)S(1)}, f32[4,256]{1,0:T(4,128)S(1)}, u32[]{:S(2)}, u32[]{:S(2)}) collective-permute-start(f32[4,256]{1,0:T(4,128)S(1)} %shard_map.66.refs_0_), channel_id=1, source_target_pairs={{0,1},{1,0},{2,3},{3,2},{4,5},{5,4},{6,7},{7,6},{8,9},{9,8},{10,11... | collective-permute-start | bytes 12296 | tf_op jit(solution)/shard_map/ppermute | solution.py:156
  22.0 5.0 %collective-permute-start.9 = (bf16[16,2048]{1,0:T(8,128)(2,1)S(1)}, bf16[16,2048]{1,0:T(8,128)(2,1)S(1)}, u32[]{:S(2)}, u32[]{:S(2)}) collective-permute-start(bf16[16,2048]{1,0:T(8,128)(2,1)S(1)} %get-tuple-element.23), channel_id=1, source_target_pairs={{0,2},{2,0},{1,3},{3,1},{4,6},{6,4},{5,7},{7,5},{8,10},{10,8},{9,1... | collective-permute-start | bytes 196616 | tf_op jit(solution)/shard_map/ppermute | solution.py:156
  22.8 6.2 %collective-permute-start.11 = (bf16[16,2048]{1,0:T(8,128)(2,1)S(1)}, bf16[16,2048]{1,0:T(8,128)(2,1)S(1)}, u32[]{:S(2)}, u32[]{:S(2)}) collective-permute-start(bf16[16,2048]{1,0:T(8,128)(2,1)S(1)} %get-tuple-element.28), channel_id=1, source_target_pairs={{0,2},{2,0},{1,3},{3,1},{4,6},{6,4},{5,7},{7,5},{8,10},{10,8},{9,1... | collective-permute-start | bytes 196616 | tf_op jit(solution)/shard_map/ppermute | solution.py:156
  24.1 7.8 %collective-permute-start.13 = (bf16[16,2048]{1,0:T(8,128)(2,1)S(1)}, bf16[16,2048]{1,0:T(8,128)(2,1)S(1)}, u32[]{:S(2)}, u32[]{:S(2)}) collective-permute-start(bf16[16,2048]{1,0:T(8,128)(2,1)S(1)} %get-tuple-element.30), channel_id=1, source_target_pairs={{0,2},{2,0},{1,3},{3,1},{4,6},{6,4},{5,7},{7,5},{8,10},{10,8},{9,1... | collective-permute-start | bytes 196616 | tf_op jit(solution)/shard_map/ppermute | solution.py:156
  27.0 7.3 %collective-permute-start.10 = (bf16[16,2048]{1,0:T(8,128)(2,1)S(1)}, bf16[16,2048]{1,0:T(8,128)(2,1)S(1)}, u32[]{:S(2)}, u32[]{:S(2)}) collective-permute-start(bf16[16,2048]{1,0:T(8,128)(2,1)S(1)} %add_convert_fusion.2), channel_id=1, source_target_pairs={{0,8},{4,12},{8,0},{12,4},{1,9},{5,13},{9,1},{13,5},{2,10},{6,14},... | collective-permute-start | bytes 196616 | tf_op jit(solution)/shard_map/ppermute | solution.py:156
  28.6 5.7 %collective-permute-start.15 = (bf16[16,2048]{1,0:T(8,128)(2,1)S(1)}, bf16[16,2048]{1,0:T(8,128)(2,1)S(1)}, u32[]{:S(2)}, u32[]{:S(2)}) collective-permute-start(bf16[16,2048]{1,0:T(8,128)(2,1)S(1)} %get-tuple-element.31), channel_id=1, source_target_pairs={{0,2},{2,0},{1,3},{3,1},{4,6},{6,4},{5,7},{7,5},{8,10},{10,8},{9,1... | collective-permute-start | bytes 196616 | tf_op jit(solution)/shard_map/ppermute | solution.py:156
  29.0 6.2 %collective-permute-start.12 = (bf16[16,2048]{1,0:T(8,128)(2,1)S(1)}, bf16[16,2048]{1,0:T(8,128)(2,1)S(1)}, u32[]{:S(2)}, u32[]{:S(2)}) collective-permute-start(bf16[16,2048]{1,0:T(8,128)(2,1)S(1)} %add_convert_fusion.1), channel_id=1, source_target_pairs={{0,12},{4,8},{8,4},{12,0},{1,13},{5,9},{9,5},{13,1},{2,14},{6,10},... | collective-permute-start | bytes 196616 | tf_op jit(solution)/shard_map/ppermute | solution.py:156
  32.0 5.8 %copy-start.3 = (bf16[16,4096]{1,0:T(8,128)(2,1)S(1)}, bf16[16,4096]{1,0:T(8,128)(2,1)}, u32[]{:S(2)}) copy-start(bf16[16,4096]{1,0:T(8,128)(2,1)} %core_ref.1) | copy-start | bytes 393220
  32.0 4.3 %collective-permute-start.14 = (bf16[16,2048]{1,0:T(8,128)(2,1)S(1)}, bf16[16,2048]{1,0:T(8,128)(2,1)S(1)}, u32[]{:S(2)}, u32[]{:S(2)}) collective-permute-start(bf16[16,2048]{1,0:T(8,128)(2,1)S(1)} %add_convert_fusion), channel_id=1, source_target_pairs={{0,4},{4,0},{8,12},{12,8},{1,5},{5,1},{9,13},{13,9},{2,6},{6,2},{1... | collective-permute-start | bytes 196616 | tf_op jit(solution)/shard_map/ppermute | solution.py:156
  36.3 1.4 %collective-permute-start.16 = (f32[16,2048]{1,0:T(8,128)S(1)}, f32[16,2048]{1,0:T(8,128)S(1)}, u32[]{:S(2)}, u32[]{:S(2)}) collective-permute-start(f32[16,2048]{1,0:T(8,128)S(1)} %shard_map.68.mine_ref), channel_id=1, source_target_pairs={{0,1},{1,0},{2,3},{3,2},{4,5},{5,4},{6,7},{7,6},{8,9},{9,8},{10,11... | collective-permute-start | bytes 393224 | tf_op jit(solution)/shard_map/ppermute | solution.py:156

commit v5 on v4

--- a/solution.py
+++ b/solution.py
@@ -18,11 +18,8 @@
     return lax.dot_general(left, right, dims, preferred_element_type=jnp.float32)
 
 
-def prepare_kernel(half_ref, values_hbm, left_ref, left_t_ref, values, arrived):
-    batches, points, columns = values.shape
-    copies = [pltpu.make_async_copy(values_hbm.at[t], values.at[t], arrived.at[t]) for t in range(batches)]
-    for copy in copies:
-        copy.start()
+def prepare_kernel(half_ref, values_ref, left_ref, left_t_ref):
+    batches, points, columns = values_ref.shape
     groups = columns // GO
     kept = left_ref.shape[2]
     first = half_ref[0] * (kept // groups)
@@ -31,49 +28,54 @@
     wanted = (at % groups) * GO + first + at // groups
     select = jnp.where(lane == wanted, 1.0, 0.0).astype(jnp.bfloat16)
     for t in range(batches):
-        copies[t].wait()
-        left_ref[t] = split_dot(values[t], select, NT).astype(jnp.bfloat16)
-        left_t_ref[t] = split_dot(select, values[t], NT).astype(jnp.bfloat16)
+        left_ref[t] = split_dot(values_ref[t], select, NT).astype(jnp.bfloat16)
+        left_t_ref[t] = split_dot(select, values_ref[t], NT).astype(jnp.bfloat16)
 
 
 def index_kernel(held, fetch_ref, slots_ref, rows_ref):
     owners, capacity = fetch_ref.shape
     slots = slots_ref[...]
-    rows = jnp.zeros(slots.shape, jnp.int32)
-    stored = fetch_ref[...] + held * lax.broadcasted_iota(jnp.int32, (owners, capacity), 0)
-    for owner in range(owners):
-        for at in range(capacity):
-            home = stored[owner:owner + 1, at:at + 1].reshape(1, 1, 1)
-            rows = jnp.where(slots == owner * capacity + at, home, rows)
-    rows_ref[...] = rows
-
-
-def row_table(place_ref, rows_ref, held, owners):
-    rows = lax.bitwise_xor(rows_ref[...], place_ref[0] * held)
+    entries = slots.shape[1]
+    owner = slots // capacity
+    owner_hot = jnp.where(lax.broadcasted_iota(jnp.int32, (owners, entries), 0) == owner, 1.0, 0.0)
+    stored = fetch_ref[...].astype(jnp.float32).T.astype(jnp.bfloat16)
+    listed = split_dot(stored, owner_hot.astype(jnp.bfloat16)).astype(jnp.int32)
+    at = lax.broadcasted_iota(jnp.int32, (capacity, entries), 0)
+    chosen = jnp.where(at == slots - owner * capacity, listed, 0)
+    rows_ref[...] = jnp.sum(chosen, axis=0, keepdims=True) + owner * held
+
+
+def row_table(place_ref, own_ref, other_ref, held, owners):
+    low = place_ref[1] == 0
+    rows = jnp.concatenate(
+        [jnp.where(low, own_ref[...], other_ref[...]), jnp.where(low, other_ref[...], own_ref[...])], axis=1
+    )
+    rows = lax.bitwise_xor(rows, place_ref[0] * held)
     row = lax.broadcasted_iota(jnp.int32, (owners * held, rows.shape[1]), 0)
     return jnp.where(row == rows, 1.0, 0.0)
 
 
 def density_kernel(places, place_ref, *refs):
     piece_refs = refs[:len(places)]
-    rows_ref, left_ref, values_ref, out_ref, table, dense = refs[len(places):]
+    own_ref, other_ref, left_ref, values_ref, out_ref, table, dense = refs[len(places):]
     batches, points, columns = values_ref.shape
     groups = columns // GO
     held = piece_refs[0].shape[0]
     for ref, k in zip(piece_refs, places):
         table[k * held:(k + 1) * held, :] = ref[...]
-    pick = row_table(place_ref, rows_ref, held, len(places)).T.astype(jnp.bfloat16)
-    low = lax.broadcasted_iota(jnp.int32, (1, 1, groups, 128), 3) < GO
+    pick = row_table(place_ref, own_ref, other_ref, held, len(places)).T.astype(jnp.bfloat16)
+    low = lax.broadcasted_iota(jnp.int32, (1, 1, 1, groups, 128), 4) < GO
     for j in range(table.shape[1] // 128):
         lanes = slice(j * 128, (j + 1) * 128)
         got = split_dot(pick, table[:, lanes])
-        got = got.reshape(batches, groups // 2, 2, groups, 128)
-        even, odd = got[:, :, 0], got[:, :, 1]
-        first = jnp.where(low, even, pltpu.roll(odd, GO, 3))
-        second = jnp.where(low, pltpu.roll(even, GO, 3), odd)
+        got = got.reshape(2, batches, groups // 4, 2, groups, 128)
+        even, odd = got[:, :, :, 0], got[:, :, :, 1]
+        first = jnp.where(low, even, pltpu.roll(odd, GO, 4))
+        second = jnp.where(low, pltpu.roll(even, GO, 4), odd)
         for t in range(batches):
             for q in range(groups // 2):
-                both = jnp.concatenate([first[t, q], second[t, q]], axis=0)
+                at = (q // (groups // 4), t, q % (groups // 4))
+                both = jnp.concatenate([first[at], second[at]], axis=0)
                 dense[t, j * 2 * groups:(j + 1) * 2 * groups, q * 128:(q + 1) * 128] = both.astype(jnp.bfloat16)
     for t in range(batches):
         product = split_dot(left_ref[t], dense[t]) * values_ref[t].astype(jnp.float32)
@@ -84,17 +86,17 @@
 
 
 def scatter_kernel(place_ref, *refs):
-    mine_ref, other_ref, weight_ref, values_ref, left_t_ref, rows_ref = refs[:6]
-    out_refs = refs[6:-2]
+    mine_ref, far_ref, weight_ref, values_ref, left_t_ref, own_ref, other_ref = refs[:7]
+    out_refs = refs[7:-2]
     high, rest = refs[-2:]
     pieces = len(out_refs)
     held = out_refs[0].shape[0]
-    put = row_table(place_ref, rows_ref, held, pieces).astype(jnp.bfloat16)
+    put = row_table(place_ref, own_ref, other_ref, held, pieces).astype(jnp.bfloat16)
     batches, points, columns = values_ref.shape
     groups = columns // GO
     kept = left_t_ref.shape[1]
     steps = kept // (2 * groups)
-    potential = weight_ref[...] * jnp.tanh(mine_ref[...] + other_ref[...])
+    potential = weight_ref[...] * jnp.tanh(mine_ref[...] + far_ref[...])
     low = lax.broadcasted_iota(jnp.int32, (1, groups, 128), 2) < GO
     for t in range(batches):
         factor = jnp.broadcast_to(potential[t:t + 1, :], (128, points)).T
@@ -106,7 +108,8 @@
             first, second = cut[:, 0], cut[:, 1]
             even = jnp.where(low, first, pltpu.roll(second, GO, 2))
             odd = jnp.where(low, pltpu.roll(first, GO, 2), second)
-            at = (t * groups + 2 * q) * groups
+            side, pair = q // (groups // 4), q % (groups // 4)
+            at = ((side * batches + t) * (groups // 2) + 2 * pair) * groups
             for j in range(steps):
                 both = jnp.concatenate([even[j], odd[j]], axis=0)
                 top = both.astype(jnp.bfloat16)
@@ -136,8 +139,8 @@
     out_ref[:, pl.ds(far, wide)] = core_ref[:, pl.ds(far, wide)].astype(jnp.float32) + other_ref[...]
 
 
-def call(kernel, outs, count, scratch=(), scalar=False, flops=0, moved=0, space=pltpu.VMEM):
-    specs = [pl.BlockSpec(memory_space=space)] * count
+def call(kernel, outs, count, scratch=(), scalar=False, flops=0, moved=0):
+    specs = [pl.BlockSpec(memory_space=pltpu.VMEM)] * count
     if scalar:
         specs = [pl.BlockSpec(memory_space=pltpu.SMEM)] + specs
     out_specs = jax.tree.map(lambda _: pl.BlockSpec(memory_space=pltpu.VMEM), outs)
@@ -192,45 +195,39 @@
             jax.ShapeDtypeStruct((batches, kept, points), bf16),
         ),
         1,
-        scratch=(pltpu.VMEM(basis_values.shape, bf16), pltpu.SemaphoreType.DMA((batches,))),
         scalar=True,
-        space=pl.ANY,
         flops=4 * batches * points * columns * kept,
         moved=3 * batches * points * columns * 2,
     )(half_at, basis_values)
 
-    own_rows = pl.pallas_call(
+    own_rows = call(
         functools.partial(index_kernel, held),
-        out_shape=jax.ShapeDtypeStruct((batches, own_groups, groups), jnp.int32),
-        in_specs=[pl.BlockSpec(memory_space=pltpu.VMEM)] * 2,
-        out_specs=pl.BlockSpec(memory_space=pltpu.VMEM),
-    )(fetch_rows.reshape(owners, capacity), slot_ids.transpose(0, 2, 1))
+        jax.ShapeDtypeStruct((1, batches * own_groups * groups), jnp.int32),
+        2,
+    )(fetch_rows.reshape(owners, capacity), slot_ids.transpose(0, 2, 1).reshape(1, -1))
     other_rows = swap(own_rows, "orb", 2, 1)
-    rows = jnp.concatenate(
-        [jnp.where(half == 0, own_rows, other_rows), jnp.where(half == 0, other_rows, own_rows)], axis=1
-    ).reshape(1, entries)
-    place = (z * rows_x + x).reshape(1).astype(jnp.int32)
+    place = jnp.stack([z * rows_x + x, half]).astype(jnp.int32)
 
     partial = call(
         functools.partial(density_kernel, order),
         jax.ShapeDtypeStruct((batches, points), f32),
-        owners + 3,
+        owners + 4,
         scalar=True,
         scratch=(pltpu.VMEM((table_rows, wide), bf16), pltpu.VMEM((batches, kept, columns), bf16)),
         flops=2 * batches * points * columns * kept,
         moved=2 * batches * points * columns * 2,
-    )(place, *[pieces[k] for k in order], rows, left, basis_values)
+    )(place, *[pieces[k] for k in order], own_rows, other_rows, left, basis_values)
     partial_other = swap(partial, "orb", 2, 1)
 
     sums = call(
         scatter_kernel,
         [jax.ShapeDtypeStruct((held, wide), bf16)] * owners,
-        6,
+        7,
         scalar=True,
         scratch=(pltpu.VMEM((entries, wide), bf16), pltpu.VMEM((entries, wide), bf16)),
         flops=2 * batches * points * columns * kept,
         moved=2 * batches * points * columns * 2,
-    )(place, partial, partial_other, point_weights, basis_values, left_t, rows)
+    )(place, partial, partial_other, point_weights, basis_values, left_t, own_rows, other_rows)
 
     landed = []
     own = sums[:rows_x]
@@ -239,7 +236,7 @@
         for dx in side:
             joined = joined + swap(sums[dz * rows_x + dx], "pair", rows_x, dx).astype(f32)
         joined = joined.astype(bf16)
-        if dz == steps[0]:
+        if dz == steps[:2][-1]:
             joined, *own = lax.optimization_barrier((joined, *own))
         landed.append(swap(joined, "batch", rows_z, dz))
     for dx in side:

time: 38.7 us -> 39.7 us (1.026)
  starting transfers between devices: 17.8 us -> 20.8 us
  waiting for transfers between devices: 12 us -> 10.3 us
  Pallas kernels: 6.21 us -> 5.3 us
  local copies, waits for them, and re-layouts: 2.24 us -> 2.83 us
    ppermute x17, starting transfers between devices: 17.8 us -> 20.8 us  [swap(): return lax.ppermute(array, axis, [(i, i ^ step) for i in range(count)])]
    ppermute x17, waiting for transfers between devices: 12 us -> 10.3 us  [swap(): return lax.ppermute(array, axis, [(i, i ^ step) for i in range(count)])]
    pallas_call x1, Pallas kernels: 1.5 us -> 0.19 us  [per_device(): call(functools.partial(index_kernel, held), jax.ShapeDtypeStruct((1, batc...]
    pallas_call x1, Pallas kernels: 1.52 us -> 0.76 us  [per_device(): call(prepare_kernel, (jax.ShapeDtypeStruct((batches, points, kept), bf16)...]
    pallas_call x1, Pallas kernels: 1.35 us -> 1.94 us  [per_device(): call(scatter_kernel, [jax.ShapeDtypeStruct((held, wide), bf16)] * owners,...]
    unnamed x12, local copies, waits for them, and re-layouts: 2.14 us -> 2.74 us
    pallas_call x1, Pallas kernels: 1.07 us -> 1.64 us  [per_device(): call(functools.partial(density_kernel, order), jax.ShapeDtypeStruct((batc...]
  transfers between devices with their start and end apart: 17 -> 17, of which waited for: 9 -> 10; matrix products, arithmetic and copies ran while one was open for 0% -> 1% of each run, Pallas kernels for 8% -> 2%
where the time goes in v5:
time: 39.7 us; the launch traced here: 39.5 us
  starting transfers between devices  20.8 us (52%)
  waiting for transfers between devices  10.3 us (26%)
  Pallas kernels  5.3 us (13%)
  local copies, waits for them, and re-layouts  2.83 us (7%)
    ppermute x17, starting transfers between devices, swap(): return lax.ppermute(array, axis, [(i, i ^ step) for i in range(count)])  20.8 us
    ppermute x17, waiting for transfers between devices, swap(): return lax.ppermute(array, axis, [(i, i ^ step) for i in range(count)])  10.3 us
    unnamed x12, local copies, waits for them, and re-layouts  2.74 us
    pallas_call x1, Pallas kernels, per_device(): call(scatter_kernel, [jax.ShapeDtypeStruct((held, wide), bf16)] * owners,...  1.94 us
    pallas_call x1, Pallas kernels, per_device(): call(functools.partial(density_kernel, order), jax.ShapeDtypeStruct((batc...  1.64 us
  transfers between devices with their start and end apart: 17, of which 10 were waited for; matrix products, arithmetic and copies ran while one was open for 1% of the time, Pallas kernels for 2%

profile of v5, /device:TPU:0, one launch (start us, length us, event | category | flops | bytes accessed | tf_op | source)
XLA Modules:
  0.0 39.5 jit_solution(11298098277888187173)
XLA Ops:
  0.0 0.0 copy-start
  0.0 0.9 %copy-done = bf16[16,4096]{1,0:T(8,128)(2,1)S(1)} copy-done((bf16[16,4096]{1,0:T(8,128)(2,1)S(1)}, bf16[16,4096]{1,0:T(8,128)(2,1)}, u32[]{:S(2)}) %copy-start) | copy-done | bytes 131096
  0.9 4.1 %collective-permute-start.3 = (bf16[16,2048]{1,0:T(8,128)(2,1)S(1)}, bf16[16,2048]{1,0:T(8,128)(2,1)S(1)}, u32[]{:S(2)}, u32[]{:S(2)}) collective-permute-start(bf16[16,2048]{1,0:T(8,128)(2,1)S(1)} %constant_dynamic-slice_fusion.refs_0_), channel_id=1, source_target_pairs={{0,8},{4,12},{8,0},{12,4},{1,9},{5,13},{9,1},{13,5},{2,10},{6,14},... | collective-permute-start | bytes 196616 | tf_op jit(solution)/shard_map/ppermute | solution.py:159
  5.0 1.6 %collective-permute-start.2 = (bf16[16,2048]{1,0:T(8,128)(2,1)S(1)}, bf16[16,2048]{1,0:T(8,128)(2,1)S(1)}, u32[]{:S(2)}, u32[]{:S(2)}) collective-permute-start(bf16[16,2048]{1,0:T(8,128)(2,1)S(1)} %constant_dynamic-slice_fusion.refs_0_), channel_id=1, source_target_pairs={{0,4},{4,0},{8,12},{12,8},{1,5},{5,1},{9,13},{13,9},{2,6},{6,2},{1... | collective-permute-start | bytes 196616 | tf_op jit(solution)/shard_map/ppermute | solution.py:159
  6.6 0.0 collective-permute-start
  6.6 1.7 %collective-permute-start.1 = (bf16[16,2048]{1,0:T(8,128)(2,1)S(1)}, bf16[16,2048]{1,0:T(8,128)(2,1)S(1)}, u32[]{:S(2)}, u32[]{:S(2)}) collective-permute-start(bf16[16,2048]{1,0:T(8,128)(2,1)S(1)} %constant_dynamic-slice_fusion.refs_0_), channel_id=1, source_target_pairs={{0,2},{2,0},{1,3},{3,1},{4,6},{6,4},{5,7},{7,5},{8,10},{10,8},{9,1... | collective-permute-start | bytes 196616 | tf_op jit(solution)/shard_map/ppermute | solution.py:159
  8.3 0.0 copy-done.5
  8.3 0.1 reshape.11.slots_ref
  8.4 0.6 %copy-done.4 = s32[1,1,8,8]{3,2,1,0:T(8,128)S(1)} copy-done((s32[1,1,8,8]{3,2,1,0:T(8,128)S(1)}, s32[1,1,8,8]{3,2,1,0:T(8,128)}, u32[]{:S(2)}) %copy-start.4) | copy-done | bytes 280
  9.0 0.2 shard_map.64.refs_8_.refs_5_
  9.2 0.0 collective-permute-start.7
  9.2 0.0 collective-permute-done.3.refs_4_
  9.2 0.7 %collective-permute-start.5 = (bf16[16,2048]{1,0:T(8,128)(2,1)S(1)}, bf16[16,2048]{1,0:T(8,128)(2,1)S(1)}, u32[]{:S(2)}, u32[]{:S(2)}) collective-permute-start(bf16[16,2048]{1,0:T(8,128)(2,1)S(1)} %collective-permute-done.3.refs_4_), channel_id=1, source_target_pairs={{0,2},{2,0},{1,3},{3,1},{4,6},{6,4},{5,7},{7,5},{8,10},{10,8},{9,1... | collective-permute-start | bytes 196616 | tf_op jit(solution)/shard_map/ppermute | solution.py:159
  9.9 0.0 collective-permute-done.2.refs_2_
  9.9 1.4 %collective-permute-start.4 = (bf16[16,2048]{1,0:T(8,128)(2,1)S(1)}, bf16[16,2048]{1,0:T(8,128)(2,1)S(1)}, u32[]{:S(2)}, u32[]{:S(2)}) collective-permute-start(bf16[16,2048]{1,0:T(8,128)(2,1)S(1)} %collective-permute-done.2.refs_2_), channel_id=1, source_target_pairs={{0,2},{2,0},{1,3},{3,1},{4,6},{6,4},{5,7},{7,5},{8,10},{10,8},{9,1... | collective-permute-start | bytes 196616 | tf_op jit(solution)/shard_map/ppermute | solution.py:159
  11.3 1.4 %collective-permute-done.refs_3_ = bf16[16,2048]{1,0:T(8,128)(2,1)S(1)} collective-permute-done((bf16[16,2048]{1,0:T(8,128)(2,1)S(1)}, bf16[16,2048]{1,0:T(8,128)(2,1)S(1)}, u32[]{:S(2)}, u32[]{:S(2)}) %collective-permute-start) | collective-permute-done | bytes 65568 | tf_op jit(solution)/shard_map/ppermute | solution.py:159
  12.7 1.5 %collective-permute-start.6 = (bf16[16,2048]{1,0:T(8,128)(2,1)S(1)}, bf16[16,2048]{1,0:T(8,128)(2,1)S(1)}, u32[]{:S(2)}, u32[]{:S(2)}) collective-permute-start(bf16[16,2048]{1,0:T(8,128)(2,1)S(1)} %collective-permute-done.refs_3_), channel_id=1, source_target_pairs={{0,2},{2,0},{1,3},{3,1},{4,6},{6,4},{5,7},{7,5},{8,10},{10,8},{9,1... | collective-permute-start | bytes 196616 | tf_op jit(solution)/shard_map/ppermute | solution.py:159
  14.1 0.1 pad_add_fusion.place_ref
  14.2 1.2 %copy-done.1 = bf16[4,256,512]{2,1,0:T(8,128)(2,1)S(1)} copy-done((bf16[4,256,512]{2,1,0:T(8,128)(2,1)S(1)}, bf16[4,256,512]{2,1,0:T(8,128)(2,1)}, u32[]{:S(2)}) %copy-start.1) | copy-done | bytes 1048600
  15.4 0.8 %shard_map.65 = (bf16[4,256,256]{2,1,0:T(8,128)(2,1)S(1)}, bf16[4,256,256]{2,1,0:T(8,128)(2,1)S(1)}) custom-call(s32[1]{0:T(128)} %bitcast.half_ref, bf16[4,256,512]{2,1,0:T(8,128)(2,1)S(1)} %copy-done.1), custom_call_target="tpu_custom_call" | custom-call | flops 536870912 | bytes 3145728 | tf_op jit(solution)/shard_map/pallas_call | solution.py:191
  16.2 0.0 collective-permute-done.7.refs_9_.refs_6_
  16.2 0.0 collective-permute-done.1.refs_1_
  16.2 0.0 collective-permute-done.5.refs_6_
  16.2 0.0 collective-permute-done.4.refs_5_
  16.2 0.7 %collective-permute-done.6.refs_7_ = bf16[16,2048]{1,0:T(8,128)(2,1)S(1)} collective-permute-done((bf16[16,2048]{1,0:T(8,128)(2,1)S(1)}, bf16[16,2048]{1,0:T(8,128)(2,1)S(1)}, u32[]{:S(2)}, u32[]{:S(2)}) %collective-permute-start.6) | collective-permute-done | bytes 65568 | tf_op jit(solution)/shard_map/ppermute | solution.py:159
  16.9 1.6 %shard_map.66.refs_0_ = f32[4,256]{1,0:T(4,128)S(1)} custom-call(s32[2]{0:T(128)S(1)} %pad_add_fusion.place_ref, bf16[16,2048]{1,0:T(8,128)(2,1)S(1)} %constant_dynamic-slice_fusion.refs_0_, bf16[16,2048]{1,0:T(8,128)(2,1)S(1)} %collective-permute-done.1.refs_1_, bf16[16,2048]{1,0:T(8,128)(2,1)S(1)} %collective-permute-done.2.refs_2_, ...), custom_call_target="tpu_custom_call" | custom-call | flops 268435456 | bytes 2097152 | tf_op jit(solution)/shard_map/pallas_call | solution.py:211
  18.6 0.1 collective-permute-start.8
  18.6 1.2 %collective-permute-done.8.refs_1_ = f32[4,256]{1,0:T(4,128)S(1)} collective-permute-done((f32[4,256]{1,0:T(4,128)S(1)}, f32[4,256]{1,0:T(4,128)S(1)}, u32[]{:S(2)}, u32[]{:S(2)}) %collective-permute-start.8) | collective-permute-done | bytes 4128 | tf_op jit(solution)/shard_map/ppermute | solution.py:159
  19.8 1.9 %shard_map.67 = (bf16[16,2048]{1,0:T(8,128)(2,1)S(1)}, bf16[16,2048]{1,0:T(8,128)(2,1)S(1)}, bf16[16,2048]{1,0:T(8,128)(2,1)S(1)}, bf16[16,2048]{1,0:T(8,128)(2,...) custom-call(s32[2]{0:T(128)S(1)} %pad_add_fusion.place_ref, ...), custom_call_target="tpu_custom_call" | custom-call | flops 268435456 | bytes 2097152 | tf_op jit(solution)/shard_map/pallas_call | solution.py:222
  21.7 1.6 %collective-permute-start.9 = (bf16[16,2048]{1,0:T(8,128)(2,1)S(1)}, bf16[16,2048]{1,0:T(8,128)(2,1)S(1)}, u32[]{:S(2)}, u32[]{:S(2)}) collective-permute-start(bf16[16,2048]{1,0:T(8,128)(2,1)S(1)} %get-tuple-element.23), channel_id=1, source_target_pairs={{0,2},{2,0},{1,3},{3,1},{4,6},{6,4},{5,7},{7,5},{8,10},{10,8},{9,1... | collective-permute-start | bytes 196616 | tf_op jit(solution)/shard_map/ppermute | solution.py:159
  23.3 0.5 %collective-permute-start.11 = (bf16[16,2048]{1,0:T(8,128)(2,1)S(1)}, bf16[16,2048]{1,0:T(8,128)(2,1)S(1)}, u32[]{:S(2)}, u32[]{:S(2)}) collective-permute-start(bf16[16,2048]{1,0:T(8,128)(2,1)S(1)} %get-tuple-element.25), channel_id=1, source_target_pairs={{0,2},{2,0},{1,3},{3,1},{4,6},{6,4},{5,7},{7,5},{8,10},{10,8},{9,1... | collective-permute-start | bytes 196616 | tf_op jit(solution)/shard_map/ppermute | solution.py:159
  23.8 1.5 %collective-permute-start.13 = (bf16[16,2048]{1,0:T(8,128)(2,1)S(1)}, bf16[16,2048]{1,0:T(8,128)(2,1)S(1)}, u32[]{:S(2)}, u32[]{:S(2)}) collective-permute-start(bf16[16,2048]{1,0:T(8,128)(2,1)S(1)} %get-tuple-element.30), channel_id=1, source_target_pairs={{0,2},{2,0},{1,3},{3,1},{4,6},{6,4},{5,7},{7,5},{8,10},{10,8},{9,1... | collective-permute-start | bytes 196616 | tf_op jit(solution)/shard_map/ppermute | solution.py:159
  25.3 1.1 %collective-permute-done.9 = bf16[16,2048]{1,0:T(8,128)(2,1)S(1)} collective-permute-done((bf16[16,2048]{1,0:T(8,128)(2,1)S(1)}, bf16[16,2048]{1,0:T(8,128)(2,1)S(1)}, u32[]{:S(2)}, u32[]{:S(2)}) %collective-permute-start.9) | collective-permute-done | bytes 65568 | tf_op jit(solution)/shard_map/ppermute | solution.py:159
  26.5 1.4 %collective-permute-start.10 = (bf16[16,2048]{1,0:T(8,128)(2,1)S(1)}, bf16[16,2048]{1,0:T(8,128)(2,1)S(1)}, u32[]{:S(2)}, u32[]{:S(2)}) collective-permute-start(bf16[16,2048]{1,0:T(8,128)(2,1)S(1)} %add_convert_fusion.2), channel_id=1, source_target_pairs={{0,8},{4,12},{8,0},{12,4},{1,9},{5,13},{9,1},{13,5},{2,10},{6,14},... | collective-permute-start | bytes 196616 | tf_op jit(solution)/shard_map/ppermute | solution.py:159
  27.8 0.3 collective-permute-done.11
  28.2 3.4 %collective-permute-start.12 = (bf16[16,2048]{1,0:T(8,128)(2,1)S(1)}, bf16[16,2048]{1,0:T(8,128)(2,1)S(1)}, u32[]{:S(2)}, u32[]{:S(2)}) collective-permute-start(bf16[16,2048]{1,0:T(8,128)(2,1)S(1)} %add_convert_fusion.1), channel_id=1, source_target_pairs={{0,12},{4,8},{8,4},{12,0},{1,13},{5,9},{9,5},{13,1},{2,14},{6,10},... | collective-permute-start | bytes 196616 | tf_op jit(solution)/shard_map/ppermute | solution.py:159
  31.6 1.3 %collective-permute-start.15 = (bf16[16,2048]{1,0:T(8,128)(2,1)S(1)}, bf16[16,2048]{1,0:T(8,128)(2,1)S(1)}, u32[]{:S(2)}, u32[]{:S(2)}) collective-permute-start(bf16[16,2048]{1,0:T(8,128)(2,1)S(1)} %get-tuple-element.31), channel_id=1, source_target_pairs={{0,2},{2,0},{1,3},{3,1},{4,6},{6,4},{5,7},{7,5},{8,10},{10,8},{9,1... | collective-permute-start | bytes 196616 | tf_op jit(solution)/shard_map/ppermute | solution.py:159
  32.9 0.0 collective-permute-done.13
  33.0 0.0 copy-start.2
  33.0 0.1 collective-permute-start.14
  33.0 1.0 %collective-permute-done.10.refs_0_ = bf16[16,2048]{1,0:T(8,128)(2,1)S(1)} collective-permute-done((bf16[16,2048]{1,0:T(8,128)(2,1)S(1)}, bf16[16,2048]{1,0:T(8,128)(2,1)S(1)}, u32[]{:S(2)}, u32[]{:S(2)}) %collective-permute-start.10) | collective-permute-done | bytes 65568 | tf_op jit(solution)/shard_map/ppermute | solution.py:159
  34.0 0.9 %collective-permute-done.12.refs_1_ = bf16[16,2048]{1,0:T(8,128)(2,1)S(1)} collective-permute-done((bf16[16,2048]{1,0:T(8,128)(2,1)S(1)}, bf16[16,2048]{1,0:T(8,128)(2,1)S(1)}, u32[]{:S(2)}, u32[]{:S(2)}) %collective-permute-start.12) | collective-permute-done | bytes 65568 | tf_op jit(solution)/shard_map/ppermute | solution.py:159
  34.9 1.0 %collective-permute-done.15.refs_3_ = bf16[16,2048]{1,0:T(8,128)(2,1)S(1)} collective-permute-done((bf16[16,2048]{1,0:T(8,128)(2,1)S(1)}, bf16[16,2048]{1,0:T(8,128)(2,1)S(1)}, u32[]{:S(2)}, u32[]{:S(2)}) %collective-permute-start.15) | collective-permute-done | bytes 65568 | tf_op jit(solution)/shard_map/ppermute | solution.py:159
  35.9 1.4 %collective-permute-done.14.refs_2_ = bf16[16,2048]{1,0:T(8,128)(2,1)S(1)} collective-permute-done((bf16[16,2048]{1,0:T(8,128)(2,1)S(1)}, bf16[16,2048]{1,0:T(8,128)(2,1)S(1)}, u32[]{:S(2)}, u32[]{:S(2)}) %collective-permute-start.14) | collective-permute-done | bytes 65568 | tf_op jit(solution)/shard_map/ppermute | solution.py:159
  37.3 0.1 collective-permute-start.16
  37.4 1.3 %collective-permute-done.16.other_ref = f32[16,2048]{1,0:T(8,128)S(1)} collective-permute-done((f32[16,2048]{1,0:T(8,128)S(1)}, f32[16,2048]{1,0:T(8,128)S(1)}, u32[]{:S(2)}, u32[]{:S(2)}) %collective-permute-start.16) | collective-permute-done | bytes 131104 | tf_op jit(solution)/shard_map/ppermute | solution.py:159
  38.8 0.0 copy-done.2
  38.8 0.7 %shard_map.69 = f32[16,4096]{1,0:T(8,128)} custom-call(s32[1]{0:T(128)} %bitcast.half_ref, f32[16,2048]{1,0:T(8,128)S(1)} %shard_map.68.mine_ref, f32[16,2048]{1,0:T(8,128)S(1)} %collective-permute-done.16.other_ref, bf16[16,4096]{1,0:T(8,128)(2,1)S(1)} %copy-done.2), custom_call_target="tpu_custom_call" | custom-call | bytes 786432 | tf_op jit(solution)/shard_map/pallas_call | solution.py:249
  (10 shorter events, 0.1 us)
Async XLA Ops:
  0.0 0.9 %copy-start = (bf16[16,4096]{1,0:T(8,128)(2,1)S(1)}, bf16[16,4096]{1,0:T(8,128)(2,1)}, u32[]{:S(2)}) copy-start(bf16[16,4096]{1,0:T(8,128)(2,1)} %param.10) | copy-start | bytes 393220
  0.9 7.4 %copy-start.5 = (s32[4,8,4]{1,2,0:T(4,128)S(1)}, s32[4,8,4]{1,2,0:T(4,128)}, u32[]{:S(2)}) copy-start(s32[4,8,4]{1,2,0:T(4,128)} %param.8) | copy-start | bytes 1540
  0.9 8.3 %collective-permute-start.3 = (bf16[16,2048]{1,0:T(8,128)(2,1)S(1)}, bf16[16,2048]{1,0:T(8,128)(2,1)S(1)}, u32[]{:S(2)}, u32[]{:S(2)}) collective-permute-start(bf16[16,2048]{1,0:T(8,128)(2,1)S(1)} %constant_dynamic-slice_fusion.refs_0_), channel_id=1, source_target_pairs={{0,8},{4,12},{8,0},{12,4},{1,9},{5,13},{9,1},{13,5},{2,10},{6,14},... | collective-permute-start | bytes 196616 | tf_op jit(solution)/shard_map/ppermute | solution.py:159
  5.0 4.9 %collective-permute-start.2 = (bf16[16,2048]{1,0:T(8,128)(2,1)S(1)}, bf16[16,2048]{1,0:T(8,128)(2,1)S(1)}, u32[]{:S(2)}, u32[]{:S(2)}) collective-permute-start(bf16[16,2048]{1,0:T(8,128)(2,1)S(1)} %constant_dynamic-slice_fusion.refs_0_), channel_id=1, source_target_pairs={{0,4},{4,0},{8,12},{12,8},{1,5},{5,1},{9,13},{13,9},{2,6},{6,2},{1... | collective-permute-start | bytes 196616 | tf_op jit(solution)/shard_map/ppermute | solution.py:159
  6.6 6.1 %collective-permute-start = (bf16[16,2048]{1,0:T(8,128)(2,1)S(1)}, bf16[16,2048]{1,0:T(8,128)(2,1)S(1)}, u32[]{:S(2)}, u32[]{:S(2)}) collective-permute-start(bf16[16,2048]{1,0:T(8,128)(2,1)S(1)} %constant_dynamic-slice_fusion.refs_0_), channel_id=1, source_target_pairs={{0,12},{4,8},{8,4},{12,0},{1,13},{5,9},{9,5},{13,1},{2,14},{6,10},... | collective-permute-start | bytes 196616 | tf_op jit(solution)/shard_map/ppermute | solution.py:159
  6.6 9.6 %collective-permute-start.1 = (bf16[16,2048]{1,0:T(8,128)(2,1)S(1)}, bf16[16,2048]{1,0:T(8,128)(2,1)S(1)}, u32[]{:S(2)}, u32[]{:S(2)}) collective-permute-start(bf16[16,2048]{1,0:T(8,128)(2,1)S(1)} %constant_dynamic-slice_fusion.refs_0_), channel_id=1, source_target_pairs={{0,2},{2,0},{1,3},{3,1},{4,6},{6,4},{5,7},{7,5},{8,10},{10,8},{9,1... | collective-permute-start | bytes 196616 | tf_op jit(solution)/shard_map/ppermute | solution.py:159
  8.3 0.7 %copy-start.4 = (s32[1,1,8,8]{3,2,1,0:T(8,128)S(1)}, s32[1,1,8,8]{3,2,1,0:T(8,128)}, u32[]{:S(2)}) copy-start(s32[1,1,8,8]{3,2,1,0:T(8,128)} %param.9) | copy-start | bytes 772
  9.2 7.0 %collective-permute-start.7 = (s32[1,128]{1,0:T(1,128)S(1)}, s32[1,128]{1,0:T(1,128)S(1)}, u32[]{:S(2)}, u32[]{:S(2)}) collective-permute-start(s32[1,128]{1,0:T(1,128)S(1)} %shard_map.64.refs_8_.refs_5_), channel_id=1, source_target_pairs={{0,1},{1,0},{2,3},{3,2},{4,5},{5,4},{6,7},{7,6},{8,9},{9,8},{10,11... | collective-permute-start | bytes 1544 | tf_op jit(solution)/shard_map/ppermute | solution.py:159
  9.2 7.0 %collective-permute-start.5 = (bf16[16,2048]{1,0:T(8,128)(2,1)S(1)}, bf16[16,2048]{1,0:T(8,128)(2,1)S(1)}, u32[]{:S(2)}, u32[]{:S(2)}) collective-permute-start(bf16[16,2048]{1,0:T(8,128)(2,1)S(1)} %collective-permute-done.3.refs_4_), channel_id=1, source_target_pairs={{0,2},{2,0},{1,3},{3,1},{4,6},{6,4},{5,7},{7,5},{8,10},{10,8},{9,1... | collective-permute-start | bytes 196616 | tf_op jit(solution)/shard_map/ppermute | solution.py:159
  9.9 6.3 %collective-permute-start.4 = (bf16[16,2048]{1,0:T(8,128)(2,1)S(1)}, bf16[16,2048]{1,0:T(8,128)(2,1)S(1)}, u32[]{:S(2)}, u32[]{:S(2)}) collective-permute-start(bf16[16,2048]{1,0:T(8,128)(2,1)S(1)} %collective-permute-done.2.refs_2_), channel_id=1, source_target_pairs={{0,2},{2,0},{1,3},{3,1},{4,6},{6,4},{5,7},{7,5},{8,10},{10,8},{9,1... | collective-permute-start | bytes 196616 | tf_op jit(solution)/shard_map/ppermute | solution.py:159
  12.7 4.3 %collective-permute-start.6 = (bf16[16,2048]{1,0:T(8,128)(2,1)S(1)}, bf16[16,2048]{1,0:T(8,128)(2,1)S(1)}, u32[]{:S(2)}, u32[]{:S(2)}) collective-permute-start(bf16[16,2048]{1,0:T(8,128)(2,1)S(1)} %collective-permute-done.refs_3_), channel_id=1, source_target_pairs={{0,2},{2,0},{1,3},{3,1},{4,6},{6,4},{5,7},{7,5},{8,10},{10,8},{9,1... | collective-permute-start | bytes 196616 | tf_op jit(solution)/shard_map/ppermute | solution.py:159
  14.2 1.2 %copy-start.1 = (bf16[4,256,512]{2,1,0:T(8,128)(2,1)S(1)}, bf16[4,256,512]{2,1,0:T(8,128)(2,1)}, u32[]{:S(2)}) copy-start(bf16[4,256,512]{2,1,0:T(8,128)(2,1)} %refs_3_.1) | copy-start | bytes 3145732
  16.9 2.9 %copy-start.3 = (f32[4,256]{1,0:T(4,128)S(1)}, f32[4,256]{1,0:T(4,128)}, u32[]{:S(2)}) copy-start(f32[4,256]{1,0:T(4,128)} %refs_2_.1) | copy-start | bytes 12292
  18.6 1.2 %collective-permute-start.8 = (f32[4,256]{1,0:T(4,128)S(1)}, f32[4,256]{1,0:T(4,128)S(1)}, u32[]{:S(2)}, u32[]{:S(2)}) collective-permute-start(f32[4,256]{1,0:T(4,128)S(1)} %shard_map.66.refs_0_), channel_id=1, source_target_pairs={{0,1},{1,0},{2,3},{3,2},{4,5},{5,4},{6,7},{7,6},{8,9},{9,8},{10,11... | collective-permute-start | bytes 12296 | tf_op jit(solution)/shard_map/ppermute | solution.py:159
  21.7 4.7 %collective-permute-start.9 = (bf16[16,2048]{1,0:T(8,128)(2,1)S(1)}, bf16[16,2048]{1,0:T(8,128)(2,1)S(1)}, u32[]{:S(2)}, u32[]{:S(2)}) collective-permute-start(bf16[16,2048]{1,0:T(8,128)(2,1)S(1)} %get-tuple-element.23), channel_id=1, source_target_pairs={{0,2},{2,0},{1,3},{3,1},{4,6},{6,4},{5,7},{7,5},{8,10},{10,8},{9,1... | collective-permute-start | bytes 196616 | tf_op jit(solution)/shard_map/ppermute | solution.py:159
  23.3 4.9 %collective-permute-start.11 = (bf16[16,2048]{1,0:T(8,128)(2,1)S(1)}, bf16[16,2048]{1,0:T(8,128)(2,1)S(1)}, u32[]{:S(2)}, u32[]{:S(2)}) collective-permute-start(bf16[16,2048]{1,0:T(8,128)(2,1)S(1)} %get-tuple-element.25), channel_id=1, source_target_pairs={{0,2},{2,0},{1,3},{3,1},{4,6},{6,4},{5,7},{7,5},{8,10},{10,8},{9,1... | collective-permute-start | bytes 196616 | tf_op jit(solution)/shard_map/ppermute | solution.py:159
  23.8 9.1 %collective-permute-start.13 = (bf16[16,2048]{1,0:T(8,128)(2,1)S(1)}, bf16[16,2048]{1,0:T(8,128)(2,1)S(1)}, u32[]{:S(2)}, u32[]{:S(2)}) collective-permute-start(bf16[16,2048]{1,0:T(8,128)(2,1)S(1)} %get-tuple-element.30), channel_id=1, source_target_pairs={{0,2},{2,0},{1,3},{3,1},{4,6},{6,4},{5,7},{7,5},{8,10},{10,8},{9,1... | collective-permute-start | bytes 196616 | tf_op jit(solution)/shard_map/ppermute | solution.py:159
  26.5 7.5 %collective-permute-start.10 = (bf16[16,2048]{1,0:T(8,128)(2,1)S(1)}, bf16[16,2048]{1,0:T(8,128)(2,1)S(1)}, u32[]{:S(2)}, u32[]{:S(2)}) collective-permute-start(bf16[16,2048]{1,0:T(8,128)(2,1)S(1)} %add_convert_fusion.2), channel_id=1, source_target_pairs={{0,8},{4,12},{8,0},{12,4},{1,9},{5,13},{9,1},{13,5},{2,10},{6,14},... | collective-permute-start | bytes 196616 | tf_op jit(solution)/shard_map/ppermute | solution.py:159
  28.2 6.7 %collective-permute-start.12 = (bf16[16,2048]{1,0:T(8,128)(2,1)S(1)}, bf16[16,2048]{1,0:T(8,128)(2,1)S(1)}, u32[]{:S(2)}, u32[]{:S(2)}) collective-permute-start(bf16[16,2048]{1,0:T(8,128)(2,1)S(1)} %add_convert_fusion.1), channel_id=1, source_target_pairs={{0,12},{4,8},{8,4},{12,0},{1,13},{5,9},{9,5},{13,1},{2,14},{6,10},... | collective-permute-start | bytes 196616 | tf_op jit(solution)/shard_map/ppermute | solution.py:159
  31.6 4.3 %collective-permute-start.15 = (bf16[16,2048]{1,0:T(8,128)(2,1)S(1)}, bf16[16,2048]{1,0:T(8,128)(2,1)S(1)}, u32[]{:S(2)}, u32[]{:S(2)}) collective-permute-start(bf16[16,2048]{1,0:T(8,128)(2,1)S(1)} %get-tuple-element.31), channel_id=1, source_target_pairs={{0,2},{2,0},{1,3},{3,1},{4,6},{6,4},{5,7},{7,5},{8,10},{10,8},{9,1... | collective-permute-start | bytes 196616 | tf_op jit(solution)/shard_map/ppermute | solution.py:159
  33.0 5.8 %copy-start.2 = (bf16[16,4096]{1,0:T(8,128)(2,1)S(1)}, bf16[16,4096]{1,0:T(8,128)(2,1)}, u32[]{:S(2)}) copy-start(bf16[16,4096]{1,0:T(8,128)(2,1)} %core_ref.1) | copy-start | bytes 393220
  33.0 4.3 %collective-permute-start.14 = (bf16[16,2048]{1,0:T(8,128)(2,1)S(1)}, bf16[16,2048]{1,0:T(8,128)(2,1)S(1)}, u32[]{:S(2)}, u32[]{:S(2)}) collective-permute-start(bf16[16,2048]{1,0:T(8,128)(2,1)S(1)} %add_convert_fusion), channel_id=1, source_target_pairs={{0,4},{4,0},{8,12},{12,8},{1,5},{5,1},{9,13},{13,9},{2,6},{6,2},{1... | collective-permute-start | bytes 196616 | tf_op jit(solution)/shard_map/ppermute | solution.py:159
  37.3 1.4 %collective-permute-start.16 = (f32[16,2048]{1,0:T(8,128)S(1)}, f32[16,2048]{1,0:T(8,128)S(1)}, u32[]{:S(2)}, u32[]{:S(2)}) collective-permute-start(f32[16,2048]{1,0:T(8,128)S(1)} %shard_map.68.mine_ref), channel_id=1, source_target_pairs={{0,1},{1,0},{2,3},{3,2},{4,5},{5,4},{6,7},{7,6},{8,9},{9,8},{10,11... | collective-permute-start | bytes 393224 | tf_op jit(solution)/shard_map/ppermute | solution.py:159

commit v6 on v5

--- a/solution.py
+++ b/solution.py
@@ -45,8 +45,8 @@
     rows_ref[...] = jnp.sum(chosen, axis=0, keepdims=True) + owner * held
 
 
-def row_table(place_ref, own_ref, other_ref, held, owners):
-    low = place_ref[1] == 0
+def row_table(place_ref, half_ref, own_ref, other_ref, held, owners):
+    low = half_ref[0] == 0
     rows = jnp.concatenate(
         [jnp.where(low, own_ref[...], other_ref[...]), jnp.where(low, other_ref[...], own_ref[...])], axis=1
     )
@@ -55,7 +55,7 @@
     return jnp.where(row == rows, 1.0, 0.0)
 
 
-def density_kernel(places, place_ref, *refs):
+def density_kernel(places, place_ref, half_ref, *refs):
     piece_refs = refs[:len(places)]
     own_ref, other_ref, left_ref, values_ref, out_ref, table, dense = refs[len(places):]
     batches, points, columns = values_ref.shape
@@ -63,7 +63,7 @@
     held = piece_refs[0].shape[0]
     for ref, k in zip(piece_refs, places):
         table[k * held:(k + 1) * held, :] = ref[...]
-    pick = row_table(place_ref, own_ref, other_ref, held, len(places)).T.astype(jnp.bfloat16)
+    pick = row_table(place_ref, half_ref, own_ref, other_ref, held, len(places)).T.astype(jnp.bfloat16)
     low = lax.broadcasted_iota(jnp.int32, (1, 1, 1, groups, 128), 4) < GO
     for j in range(table.shape[1] // 128):
         lanes = slice(j * 128, (j + 1) * 128)
@@ -85,13 +85,13 @@
         out_ref[t:t + 1, :] = jnp.sum(folded.T, axis=0, keepdims=True)
 
 
-def scatter_kernel(place_ref, *refs):
+def scatter_kernel(place_ref, half_ref, *refs):
     mine_ref, far_ref, weight_ref, values_ref, left_t_ref, own_ref, other_ref = refs[:7]
     out_refs = refs[7:-2]
     high, rest = refs[-2:]
     pieces = len(out_refs)
     held = out_refs[0].shape[0]
-    put = row_table(place_ref, own_ref, other_ref, held, pieces).astype(jnp.bfloat16)
+    put = row_table(place_ref, half_ref, own_ref, other_ref, held, pieces).astype(jnp.bfloat16)
     batches, points, columns = values_ref.shape
     groups = columns // GO
     kept = left_t_ref.shape[1]
@@ -123,14 +123,6 @@
             out_refs[k + i][...] = total[i * held:(i + 1) * held, :].astype(jnp.bfloat16)
 
 
-def sum_kernel(*refs):
-    out_ref = refs[-1]
-    total = refs[0][...].astype(jnp.float32)
-    for ref in refs[1:-1]:
-        total = total + ref[...].astype(jnp.float32)
-    out_ref[...] = total.astype(out_ref.dtype)
-
-
 def finish_kernel(half_ref, mine_ref, other_ref, core_ref, out_ref):
     wide = mine_ref.shape[1]
     own = pl.multiple_of(half_ref[0] * wide, wide)
@@ -139,10 +131,9 @@
     out_ref[:, pl.ds(far, wide)] = core_ref[:, pl.ds(far, wide)].astype(jnp.float32) + other_ref[...]
 
 
-def call(kernel, outs, count, scratch=(), scalar=False, flops=0, moved=0):
+def call(kernel, outs, count, scratch=(), scalars=0, flops=0, moved=0):
     specs = [pl.BlockSpec(memory_space=pltpu.VMEM)] * count
-    if scalar:
-        specs = [pl.BlockSpec(memory_space=pltpu.SMEM)] + specs
+    specs = [pl.BlockSpec(memory_space=pltpu.SMEM)] * scalars + specs
     out_specs = jax.tree.map(lambda _: pl.BlockSpec(memory_space=pltpu.VMEM), outs)
     return pl.pallas_call(
         kernel,
@@ -157,6 +148,13 @@
 
 def swap(array, axis, count, step):
     return lax.ppermute(array, axis, [(i, i ^ step) for i in range(count)])
+
+
+def add_all(terms):
+    total = terms[0]
+    for term in terms[1:]:
+        total = total + term
+    return total
 
 
 def per_device(basis_values, point_weights, slot_ids, fetch_rows, density_blocks, core_blocks):
@@ -173,16 +171,32 @@
     kept = columns // 2
     bf16, f32 = jnp.bfloat16, jnp.float32
 
-    steps = list(range(rows_z // 2, rows_z)) + list(range(1, rows_z // 2))
+    own_rows = call(
+        functools.partial(index_kernel, held),
+        jax.ShapeDtypeStruct((1, batches * own_groups * groups), jnp.int32),
+        2,
+    )(fetch_rows.reshape(owners, capacity), slot_ids.transpose(0, 2, 1).reshape(1, -1))
+    other_rows = swap(own_rows, "orb", 2, 1)
+
+    bits = [1 << i for i in reversed(range(rows_z.bit_length() - 1))]
     side = list(range(1, rows_x))
 
     mine = lax.dynamic_slice_in_dim(density_blocks, half * wide, wide, 1)
     pieces = {0: mine}
-    for dx in side:
-        pieces[dx] = swap(mine, "pair", rows_x, dx)
-    for dz in steps[::-1]:
-        pieces[dz * rows_x] = swap(mine, "batch", rows_z, dz)
-    for dz in steps[rows_z // 2:] + steps[:rows_z // 2]:
+    have = [0]
+    for bit in bits:
+        for dz in have:
+            pieces[(dz | bit) * rows_x] = swap(pieces[dz * rows_x], "batch", rows_z, bit)
+        if bit == bits[0]:
+            for dx in side:
+                pieces[dx] = swap(mine, "pair", rows_x, dx)
+            ready = side + [bit * rows_x]
+            ordered = lax.optimization_barrier([pieces[k] for k in ready])
+            pieces.update(zip(ready, ordered))
+        have = have + [dz | bit for dz in have]
+    first = bits[0] * rows_x
+    pieces[first], other_rows = lax.optimization_barrier((pieces[first], other_rows))
+    for dz in have[1:]:
         for dx in side:
             pieces[dz * rows_x + dx] = swap(pieces[dz * rows_x], "pair", rows_x, dx)
     order = list(pieces)
@@ -195,59 +209,52 @@
             jax.ShapeDtypeStruct((batches, kept, points), bf16),
         ),
         1,
-        scalar=True,
+        scalars=1,
         flops=4 * batches * points * columns * kept,
         moved=3 * batches * points * columns * 2,
     )(half_at, basis_values)
 
-    own_rows = call(
-        functools.partial(index_kernel, held),
-        jax.ShapeDtypeStruct((1, batches * own_groups * groups), jnp.int32),
-        2,
-    )(fetch_rows.reshape(owners, capacity), slot_ids.transpose(0, 2, 1).reshape(1, -1))
-    other_rows = swap(own_rows, "orb", 2, 1)
-    place = jnp.stack([z * rows_x + x, half]).astype(jnp.int32)
+    place = (z * rows_x + x).reshape(1).astype(jnp.int32)
+    side_at = half.reshape(1).astype(jnp.int32)
 
     partial = call(
         functools.partial(density_kernel, order),
         jax.ShapeDtypeStruct((batches, points), f32),
         owners + 4,
-        scalar=True,
+        scalars=2,
         scratch=(pltpu.VMEM((table_rows, wide), bf16), pltpu.VMEM((batches, kept, columns), bf16)),
         flops=2 * batches * points * columns * kept,
         moved=2 * batches * points * columns * 2,
-    )(place, *[pieces[k] for k in order], own_rows, other_rows, left, basis_values)
+    )(place, side_at, *[pieces[k] for k in order], own_rows, other_rows, left, basis_values)
     partial_other = swap(partial, "orb", 2, 1)
 
     sums = call(
         scatter_kernel,
         [jax.ShapeDtypeStruct((held, wide), bf16)] * owners,
         7,
-        scalar=True,
+        scalars=2,
         scratch=(pltpu.VMEM((entries, wide), bf16), pltpu.VMEM((entries, wide), bf16)),
         flops=2 * batches * points * columns * kept,
         moved=2 * batches * points * columns * 2,
-    )(place, partial, partial_other, point_weights, basis_values, left_t, own_rows, other_rows)
-
-    landed = []
-    own = sums[:rows_x]
-    for dz in steps:
-        joined = sums[dz * rows_x].astype(f32)
-        for dx in side:
-            joined = joined + swap(sums[dz * rows_x + dx], "pair", rows_x, dx).astype(f32)
-        joined = joined.astype(bf16)
-        if dz == steps[:2][-1]:
-            joined, *own = lax.optimization_barrier((joined, *own))
-        landed.append(swap(joined, "batch", rows_z, dz))
-    for dx in side:
-        landed.append(swap(own[dx], "pair", rows_x, dx))
-    landed.append(own[0])
-    total = call(
-        sum_kernel, jax.ShapeDtypeStruct((held, wide), f32), len(landed), moved=len(landed) * held * wide * 2
-    )(*landed)
+    )(place, side_at, partial, partial_other, point_weights, basis_values, left_t, own_rows, other_rows)
+
+    sums = list(sums)
+    joined = {}
+    for dz in reversed(have):
+        terms = [sums[dz * rows_x]] + [swap(sums[dz * rows_x + dx], "pair", rows_x, dx) for dx in side]
+        if dz == rows_z - 1:
+            terms[-1], *sums[1:rows_x] = lax.optimization_barrier((terms[-1], *sums[1:rows_x]))
+        joined[dz] = [term.astype(f32) for term in terms]
+    for bit in reversed(bits):
+        for dz in range(rows_z - bit, 0, -2 * bit):
+            sent = add_all(joined.pop(dz)).astype(bf16)
+            came = swap(sent, "batch", rows_z, bit)
+            joined[dz ^ bit].append(came.astype(f32))
+    landed = joined[0]
+    total = add_all(landed)
     total_other = swap(total, "orb", 2, 1)
     return call(
-        finish_kernel, jax.ShapeDtypeStruct((held, square), f32), 3, scalar=True, moved=held * square * 12
+        finish_kernel, jax.ShapeDtypeStruct((held, square), f32), 3, scalars=1, moved=held * square * 12
     )(half_at, total, total_other, core_blocks)
 
 

time: 39.7 us -> 41.2 us (1.038)
  waiting for transfers between devices: 10.3 us -> 12.2 us
  Pallas kernels: 5.3 us -> 4.18 us
  starting transfers between devices: 20.8 us -> 21.5 us
    ppermute x17, waiting for transfers between devices: 10.3 us -> 12.2 us  [swap(): return lax.ppermute(array, axis, [(i, i ^ step) for i in range(count)])]
    ppermute x17, starting transfers between devices: 20.8 us -> 21.5 us  [swap(): return lax.ppermute(array, axis, [(i, i ^ step) for i in range(count)])]
    pallas_call x1, Pallas kernels: 1.64 us -> 1.1 us  [per_device(): call(functools.partial(density_kernel, order), jax.ShapeDtypeStruct((batc...]
    pallas_call x1, Pallas kernels: 1.94 us -> 1.4 us  [per_device(): call(scatter_kernel, [jax.ShapeDtypeStruct((held, wide), bf16)] * owners,...]
    unnamed x12 -> x14, local copies, waits for them, and re-layouts: 2.74 us -> 2.74 us
  transfers between devices with their start and end apart: 17 -> 17, of which waited for: 10 -> 11; matrix products, arithmetic and copies ran while one was open for 1% -> 0% of each run, Pallas kernels for 2% -> 2%
where the time goes in v6:
time: 41.2 us; the launch traced here: 41 us
  starting transfers between devices  21.5 us (52%)
  waiting for transfers between devices  12.2 us (30%)
  Pallas kernels  4.18 us (10%)
  local copies, waits for them, and re-layouts  2.83 us (7%)
    ppermute x17, starting transfers between devices, swap(): return lax.ppermute(array, axis, [(i, i ^ step) for i in range(count)])  21.5 us
    ppermute x17, waiting for transfers between devices, swap(): return lax.ppermute(array, axis, [(i, i ^ step) for i in range(count)])  12.2 us
    unnamed x14, local copies, waits for them, and re-layouts  2.74 us
    pallas_call x1, Pallas kernels, per_device(): call(scatter_kernel, [jax.ShapeDtypeStruct((held, wide), bf16)] * owners,...  1.4 us
    pallas_call x1, Pallas kernels, per_device(): call(functools.partial(density_kernel, order), jax.ShapeDtypeStruct((batc...  1.1 us
  transfers between devices with their start and end apart: 17, of which 11 were waited for; matrix products, arithmetic and copies ran while one was open for 0% of the time, Pallas kernels for 2%

profile of v6, /device:TPU:0, one launch (start us, length us, event | category | flops | bytes accessed | tf_op | source)
XLA Modules:
  0.0 41.0 jit_solution(619993531429895311)
XLA Ops:
  0.0 0.0 copy-start
  0.0 0.9 %copy-done = bf16[16,4096]{1,0:T(8,128)(2,1)S(1)} copy-done((bf16[16,4096]{1,0:T(8,128)(2,1)S(1)}, bf16[16,4096]{1,0:T(8,128)(2,1)}, u32[]{:S(2)}) %copy-start) | copy-done | bytes 131096
  0.9 4.1 %collective-permute-start.1 = (bf16[16,2048]{1,0:T(8,128)(2,1)S(1)}, bf16[16,2048]{1,0:T(8,128)(2,1)S(1)}, u32[]{:S(2)}, u32[]{:S(2)}) collective-permute-start(bf16[16,2048]{1,0:T(8,128)(2,1)S(1)} %constant_dynamic-slice_fusion.refs_0_), channel_id=1, source_target_pairs={{0,8},{4,12},{8,0},{12,4},{1,9},{5,13},{9,1},{13,5},{2,10},{6,14},... | collective-permute-start | bytes 196616 | tf_op jit(solution)/shard_map/ppermute | solution.py:150
  5.0 1.5 %collective-permute-start = (bf16[16,2048]{1,0:T(8,128)(2,1)S(1)}, bf16[16,2048]{1,0:T(8,128)(2,1)S(1)}, u32[]{:S(2)}, u32[]{:S(2)}) collective-permute-start(bf16[16,2048]{1,0:T(8,128)(2,1)S(1)} %constant_dynamic-slice_fusion.refs_0_), channel_id=1, source_target_pairs={{0,2},{2,0},{1,3},{3,1},{4,6},{6,4},{5,7},{7,5},{8,10},{10,8},{9,1... | collective-permute-start | bytes 196616 | tf_op jit(solution)/shard_map/ppermute | solution.py:150
  6.5 1.6 %collective-permute-start.4 = (bf16[16,2048]{1,0:T(8,128)(2,1)S(1)}, bf16[16,2048]{1,0:T(8,128)(2,1)S(1)}, u32[]{:S(2)}, u32[]{:S(2)}) collective-permute-start(bf16[16,2048]{1,0:T(8,128)(2,1)S(1)} %constant_dynamic-slice_fusion.refs_0_), channel_id=1, source_target_pairs={{0,4},{4,0},{8,12},{12,8},{1,5},{5,1},{9,13},{13,9},{2,6},{6,2},{1... | collective-permute-start | bytes 196616 | tf_op jit(solution)/shard_map/ppermute | solution.py:150
  8.1 0.2 collective-permute-done.1.refs_1_
  8.3 1.0 %collective-permute-done.refs_2_ = bf16[16,2048]{1,0:T(8,128)(2,1)S(1)} collective-permute-done((bf16[16,2048]{1,0:T(8,128)(2,1)S(1)}, bf16[16,2048]{1,0:T(8,128)(2,1)S(1)}, u32[]{:S(2)}, u32[]{:S(2)}) %collective-permute-start) | collective-permute-done | bytes 65568 | tf_op jit(solution)/shard_map/ppermute | solution.py:150
  9.3 1.6 %collective-permute-start.2 = (bf16[16,2048]{1,0:T(8,128)(2,1)S(1)}, bf16[16,2048]{1,0:T(8,128)(2,1)S(1)}, u32[]{:S(2)}, u32[]{:S(2)}) collective-permute-start(bf16[16,2048]{1,0:T(8,128)(2,1)S(1)} %collective-permute-done.1.refs_1_), channel_id=1, source_target_pairs={{0,4},{4,0},{8,12},{12,8},{1,5},{5,1},{9,13},{13,9},{2,6},{6,2},{1... | collective-permute-start | bytes 196616 | tf_op jit(solution)/shard_map/ppermute | solution.py:150
  10.9 0.0 copy-done.6
  10.9 0.1 reshape.16.slots_ref
  11.0 0.6 %copy-done.5 = s32[1,1,8,8]{3,2,1,0:T(8,128)S(1)} copy-done((s32[1,1,8,8]{3,2,1,0:T(8,128)S(1)}, s32[1,1,8,8]{3,2,1,0:T(8,128)}, u32[]{:S(2)}) %copy-start.5) | copy-done | bytes 280
  11.5 0.2 shard_map.64.refs_8_.refs_5_
  11.7 0.0 collective-permute-start.3
  11.7 1.1 %collective-permute-done.3.refs_9_.refs_6_ = s32[1,128]{1,0:T(1,128)S(1)} collective-permute-done((s32[1,128]{1,0:T(1,128)S(1)}, s32[1,128]{1,0:T(1,128)S(1)}, u32[]{:S(2)}, u32[]{:S(2)}) %collective-permute-start.3) | collective-permute-done | bytes 544 | tf_op jit(solution)/shard_map/ppermute | solution.py:150
  12.9 1.5 %collective-permute-start.5 = (bf16[16,2048]{1,0:T(8,128)(2,1)S(1)}, bf16[16,2048]{1,0:T(8,128)(2,1)S(1)}, u32[]{:S(2)}, u32[]{:S(2)}) collective-permute-start(bf16[16,2048]{1,0:T(8,128)(2,1)S(1)} %collective-permute-done.1.refs_1_), channel_id=1, source_target_pairs={{0,2},{2,0},{1,3},{3,1},{4,6},{6,4},{5,7},{7,5},{8,10},{10,8},{9,1... | collective-permute-start | bytes 196616 | tf_op jit(solution)/shard_map/ppermute | solution.py:150
  14.4 0.0 collective-permute-done.4.refs_3_
  14.4 0.5 %collective-permute-start.6 = (bf16[16,2048]{1,0:T(8,128)(2,1)S(1)}, bf16[16,2048]{1,0:T(8,128)(2,1)S(1)}, u32[]{:S(2)}, u32[]{:S(2)}) collective-permute-start(bf16[16,2048]{1,0:T(8,128)(2,1)S(1)} %collective-permute-done.4.refs_3_), channel_id=1, source_target_pairs={{0,2},{2,0},{1,3},{3,1},{4,6},{6,4},{5,7},{7,5},{8,10},{10,8},{9,1... | collective-permute-start | bytes 196616 | tf_op jit(solution)/shard_map/ppermute | solution.py:150
  14.9 0.0 collective-permute-done.2.refs_4_
  14.9 1.5 %collective-permute-start.7 = (bf16[16,2048]{1,0:T(8,128)(2,1)S(1)}, bf16[16,2048]{1,0:T(8,128)(2,1)S(1)}, u32[]{:S(2)}, u32[]{:S(2)}) collective-permute-start(bf16[16,2048]{1,0:T(8,128)(2,1)S(1)} %collective-permute-done.2.refs_4_), channel_id=1, source_target_pairs={{0,2},{2,0},{1,3},{3,1},{4,6},{6,4},{5,7},{7,5},{8,10},{10,8},{9,1... | collective-permute-start | bytes 196616 | tf_op jit(solution)/shard_map/ppermute | solution.py:150
  16.4 1.2 %copy-done.1 = bf16[4,256,512]{2,1,0:T(8,128)(2,1)S(1)} copy-done((bf16[4,256,512]{2,1,0:T(8,128)(2,1)S(1)}, bf16[4,256,512]{2,1,0:T(8,128)(2,1)}, u32[]{:S(2)}) %copy-start.1) | copy-done | bytes 1048600
  17.6 0.8 %shard_map.65 = (bf16[4,256,256]{2,1,0:T(8,128)(2,1)S(1)}, bf16[4,256,256]{2,1,0:T(8,128)(2,1)S(1)}) custom-call(s32[1]{0:T(128)} %bitcast.half_ref, bf16[4,256,512]{2,1,0:T(8,128)(2,1)S(1)} %copy-done.1), custom_call_target="tpu_custom_call" | custom-call | flops 536870912 | bytes 3145728 | tf_op jit(solution)/shard_map/pallas_call | solution.py:205
  18.4 0.9 %collective-permute-done.6.refs_6_ = bf16[16,2048]{1,0:T(8,128)(2,1)S(1)} collective-permute-done((bf16[16,2048]{1,0:T(8,128)(2,1)S(1)}, bf16[16,2048]{1,0:T(8,128)(2,1)S(1)}, u32[]{:S(2)}, u32[]{:S(2)}) %collective-permute-start.6) | collective-permute-done | bytes 65568 | tf_op jit(solution)/shard_map/ppermute | solution.py:150
  19.2 0.0 collective-permute-done.5.refs_5_
  19.2 0.7 %collective-permute-done.7.refs_7_ = bf16[16,2048]{1,0:T(8,128)(2,1)S(1)} collective-permute-done((bf16[16,2048]{1,0:T(8,128)(2,1)S(1)}, bf16[16,2048]{1,0:T(8,128)(2,1)S(1)}, u32[]{:S(2)}, u32[]{:S(2)}) %collective-permute-start.7) | collective-permute-done | bytes 65568 | tf_op jit(solution)/shard_map/ppermute | solution.py:150
  19.9 0.0 copy-done.2
  19.9 1.1 %shard_map.66.refs_0_ = f32[4,256]{1,0:T(4,128)S(1)} custom-call(s32[1]{0:T(128)} %bitcast.1.place_ref, s32[1]{0:T(128)} %bitcast.half_ref, bf16[16,2048]{1,0:T(8,128)(2,1)S(1)} %constant_dynamic-slice_fusion.refs_0_, bf16[16,2048]{1,0:T(8,128)(2,1)S(1)} %collective-permute-done.1.refs_1_, bf16[16,2048]{1,0:T(8,128)(2,1)S(1)} %collective-permute-done.refs_2_, ...), custom_call_target="tpu_custom_call" | custom-call | flops 268435456 | bytes 2097152 | tf_op jit(solution)/shard_map/pallas_call | solution.py:220
  21.0 0.1 collective-permute-start.8
  21.1 1.2 %collective-permute-done.8.refs_1_ = f32[4,256]{1,0:T(4,128)S(1)} collective-permute-done((f32[4,256]{1,0:T(4,128)S(1)}, f32[4,256]{1,0:T(4,128)S(1)}, u32[]{:S(2)}, u32[]{:S(2)}) %collective-permute-start.8) | collective-permute-done | bytes 4128 | tf_op jit(solution)/shard_map/ppermute | solution.py:150
  22.3 0.0 copy-done.4
  22.3 1.4 %shard_map.67 = (bf16[16,2048]{1,0:T(8,128)(2,1)S(1)}, bf16[16,2048]{1,0:T(8,128)(2,1)S(1)}, bf16[16,2048]{1,0:T(8,128)(2,1)S(1)}, bf16[16,2048]{1,0:T(8,128)(2,...) custom-call(s32[1]{0:T(128)} %bitcast.1.place_ref, ...), custom_call_target="tpu_custom_call" | custom-call | flops 268435456 | bytes 2097152 | tf_op jit(solution)/shard_map/pallas_call | solution.py:231
  23.7 1.5 %collective-permute-start.9 = (bf16[16,2048]{1,0:T(8,128)(2,1)S(1)}, bf16[16,2048]{1,0:T(8,128)(2,1)S(1)}, u32[]{:S(2)}, u32[]{:S(2)}) collective-permute-start(bf16[16,2048]{1,0:T(8,128)(2,1)S(1)} %get-tuple-element.30), channel_id=1, source_target_pairs={{0,2},{2,0},{1,3},{3,1},{4,6},{6,4},{5,7},{7,5},{8,10},{10,8},{9,1... | collective-permute-start | bytes 196616 | tf_op jit(solution)/shard_map/ppermute | solution.py:150
  25.2 0.6 %collective-permute-start.11 = (bf16[16,2048]{1,0:T(8,128)(2,1)S(1)}, bf16[16,2048]{1,0:T(8,128)(2,1)S(1)}, u32[]{:S(2)}, u32[]{:S(2)}) collective-permute-start(bf16[16,2048]{1,0:T(8,128)(2,1)S(1)} %get-tuple-element.34), channel_id=1, source_target_pairs={{0,2},{2,0},{1,3},{3,1},{4,6},{6,4},{5,7},{7,5},{8,10},{10,8},{9,1... | collective-permute-start | bytes 196616 | tf_op jit(solution)/shard_map/ppermute | solution.py:150
  25.8 1.4 %collective-permute-start.13 = (bf16[16,2048]{1,0:T(8,128)(2,1)S(1)}, bf16[16,2048]{1,0:T(8,128)(2,1)S(1)}, u32[]{:S(2)}, u32[]{:S(2)}) collective-permute-start(bf16[16,2048]{1,0:T(8,128)(2,1)S(1)} %get-tuple-element.36), channel_id=1, source_target_pairs={{0,2},{2,0},{1,3},{3,1},{4,6},{6,4},{5,7},{7,5},{8,10},{10,8},{9,1... | collective-permute-start | bytes 196616 | tf_op jit(solution)/shard_map/ppermute | solution.py:150
  27.2 1.3 %collective-permute-done.9 = bf16[16,2048]{1,0:T(8,128)(2,1)S(1)} collective-permute-done((bf16[16,2048]{1,0:T(8,128)(2,1)S(1)}, bf16[16,2048]{1,0:T(8,128)(2,1)S(1)}, u32[]{:S(2)}, u32[]{:S(2)}) %collective-permute-start.9) | collective-permute-done | bytes 65568 | tf_op jit(solution)/shard_map/ppermute | solution.py:150
  28.5 0.5 %collective-permute-start.14 = (bf16[16,2048]{1,0:T(8,128)(2,1)S(1)}, bf16[16,2048]{1,0:T(8,128)(2,1)S(1)}, u32[]{:S(2)}, u32[]{:S(2)}) collective-permute-start(bf16[16,2048]{1,0:T(8,128)(2,1)S(1)} %add_convert_fusion.1), channel_id=1, source_target_pairs={{0,4},{4,0},{8,12},{12,8},{1,5},{5,1},{9,13},{13,9},{2,6},{6,2},{1... | collective-permute-start | bytes 196616 | tf_op jit(solution)/shard_map/ppermute | solution.py:150
  29.0 1.7 %collective-permute-start.10 = (bf16[16,2048]{1,0:T(8,128)(2,1)S(1)}, bf16[16,2048]{1,0:T(8,128)(2,1)S(1)}, u32[]{:S(2)}, u32[]{:S(2)}) collective-permute-start(bf16[16,2048]{1,0:T(8,128)(2,1)S(1)} %get-tuple-element.32), channel_id=1, source_target_pairs={{0,2},{2,0},{1,3},{3,1},{4,6},{6,4},{5,7},{7,5},{8,10},{10,8},{9,1... | collective-permute-start | bytes 196616 | tf_op jit(solution)/shard_map/ppermute | solution.py:150
  30.7 0.0 collective-permute-done.11
  30.7 1.6 %collective-permute-start.12 = (bf16[16,2048]{1,0:T(8,128)(2,1)S(1)}, bf16[16,2048]{1,0:T(8,128)(2,1)S(1)}, u32[]{:S(2)}, u32[]{:S(2)}) collective-permute-start(bf16[16,2048]{1,0:T(8,128)(2,1)S(1)} %add_convert_fusion.2), channel_id=1, source_target_pairs={{0,4},{4,0},{8,12},{12,8},{1,5},{5,1},{9,13},{13,9},{2,6},{6,2},{1... | collective-permute-start | bytes 196616 | tf_op jit(solution)/shard_map/ppermute | solution.py:150
  32.3 0.0 collective-permute-done.13
  32.3 0.5 %collective-permute-done.14 = bf16[16,2048]{1,0:T(8,128)(2,1)S(1)} collective-permute-done((bf16[16,2048]{1,0:T(8,128)(2,1)S(1)}, bf16[16,2048]{1,0:T(8,128)(2,1)S(1)}, u32[]{:S(2)}, u32[]{:S(2)}) %collective-permute-start.14) | collective-permute-done | bytes 65568 | tf_op jit(solution)/shard_map/ppermute | solution.py:150
  32.8 1.8 %collective-permute-start.15 = (bf16[16,2048]{1,0:T(8,128)(2,1)S(1)}, bf16[16,2048]{1,0:T(8,128)(2,1)S(1)}, u32[]{:S(2)}, u32[]{:S(2)}) collective-permute-start(bf16[16,2048]{1,0:T(8,128)(2,1)S(1)} %add_convert_fusion), channel_id=1, source_target_pairs={{0,8},{4,12},{8,0},{12,4},{1,9},{5,13},{9,1},{13,5},{2,10},{6,14},... | collective-permute-start | bytes 196616 | tf_op jit(solution)/shard_map/ppermute | solution.py:150
  34.7 0.0 collective-permute-done.10
  34.7 1.0 %collective-permute-done.12 = bf16[16,2048]{1,0:T(8,128)(2,1)S(1)} collective-permute-done((bf16[16,2048]{1,0:T(8,128)(2,1)S(1)}, bf16[16,2048]{1,0:T(8,128)(2,1)S(1)}, u32[]{:S(2)}, u32[]{:S(2)}) %collective-permute-start.12) | collective-permute-done | bytes 65568 | tf_op jit(solution)/shard_map/ppermute | solution.py:150
  35.7 3.1 %collective-permute-done.15 = bf16[16,2048]{1,0:T(8,128)(2,1)S(1)} collective-permute-done((bf16[16,2048]{1,0:T(8,128)(2,1)S(1)}, bf16[16,2048]{1,0:T(8,128)(2,1)S(1)}, u32[]{:S(2)}, u32[]{:S(2)}) %collective-permute-start.15) | collective-permute-done | bytes 65568 | tf_op jit(solution)/shard_map/ppermute | solution.py:150
  38.8 0.1 collective-permute-start.16
  38.9 1.3 %collective-permute-done.16.other_ref = f32[16,2048]{1,0:T(8,128)S(1)} collective-permute-done((f32[16,2048]{1,0:T(8,128)S(1)}, f32[16,2048]{1,0:T(8,128)S(1)}, u32[]{:S(2)}, u32[]{:S(2)}) %collective-permute-start.16) | collective-permute-done | bytes 131104 | tf_op jit(solution)/shard_map/ppermute | solution.py:150
  40.2 0.0 copy-done.3
  40.2 0.7 %shard_map.68 = f32[16,4096]{1,0:T(8,128)} custom-call(s32[1]{0:T(128)} %bitcast.half_ref, f32[16,2048]{1,0:T(8,128)S(1)} %convert_add_fusion.mine_ref, f32[16,2048]{1,0:T(8,128)S(1)} %collective-permute-done.16.other_ref, bf16[16,4096]{1,0:T(8,128)(2,1)S(1)} %copy-done.3), custom_call_target="tpu_custom_call" | custom-call | bytes 786432 | tf_op jit(solution)/shard_map/pallas_call | solution.py:256
  (11 shorter events, 0.1 us)
Async XLA Ops:
  0.0 0.9 %copy-start = (bf16[16,4096]{1,0:T(8,128)(2,1)S(1)}, bf16[16,4096]{1,0:T(8,128)(2,1)}, u32[]{:S(2)}) copy-start(bf16[16,4096]{1,0:T(8,128)(2,1)} %param.10) | copy-start | bytes 393220
  0.9 10.0 %copy-start.6 = (s32[4,8,4]{1,2,0:T(4,128)S(1)}, s32[4,8,4]{1,2,0:T(4,128)}, u32[]{:S(2)}) copy-start(s32[4,8,4]{1,2,0:T(4,128)} %param.8) | copy-start | bytes 1540
  0.9 7.4 %collective-permute-start.1 = (bf16[16,2048]{1,0:T(8,128)(2,1)S(1)}, bf16[16,2048]{1,0:T(8,128)(2,1)S(1)}, u32[]{:S(2)}, u32[]{:S(2)}) collective-permute-start(bf16[16,2048]{1,0:T(8,128)(2,1)S(1)} %constant_dynamic-slice_fusion.refs_0_), channel_id=1, source_target_pairs={{0,8},{4,12},{8,0},{12,4},{1,9},{5,13},{9,1},{13,5},{2,10},{6,14},... | collective-permute-start | bytes 196616 | tf_op jit(solution)/shard_map/ppermute | solution.py:150
  5.0 4.3 %collective-permute-start = (bf16[16,2048]{1,0:T(8,128)(2,1)S(1)}, bf16[16,2048]{1,0:T(8,128)(2,1)S(1)}, u32[]{:S(2)}, u32[]{:S(2)}) collective-permute-start(bf16[16,2048]{1,0:T(8,128)(2,1)S(1)} %constant_dynamic-slice_fusion.refs_0_), channel_id=1, source_target_pairs={{0,2},{2,0},{1,3},{3,1},{4,6},{6,4},{5,7},{7,5},{8,10},{10,8},{9,1... | collective-permute-start | bytes 196616 | tf_op jit(solution)/shard_map/ppermute | solution.py:150
  6.5 7.9 %collective-permute-start.4 = (bf16[16,2048]{1,0:T(8,128)(2,1)S(1)}, bf16[16,2048]{1,0:T(8,128)(2,1)S(1)}, u32[]{:S(2)}, u32[]{:S(2)}) collective-permute-start(bf16[16,2048]{1,0:T(8,128)(2,1)S(1)} %constant_dynamic-slice_fusion.refs_0_), channel_id=1, source_target_pairs={{0,4},{4,0},{8,12},{12,8},{1,5},{5,1},{9,13},{13,9},{2,6},{6,2},{1... | collective-permute-start | bytes 196616 | tf_op jit(solution)/shard_map/ppermute | solution.py:150
  9.3 5.6 %collective-permute-start.2 = (bf16[16,2048]{1,0:T(8,128)(2,1)S(1)}, bf16[16,2048]{1,0:T(8,128)(2,1)S(1)}, u32[]{:S(2)}, u32[]{:S(2)}) collective-permute-start(bf16[16,2048]{1,0:T(8,128)(2,1)S(1)} %collective-permute-done.1.refs_1_), channel_id=1, source_target_pairs={{0,4},{4,0},{8,12},{12,8},{1,5},{5,1},{9,13},{13,9},{2,6},{6,2},{1... | collective-permute-start | bytes 196616 | tf_op jit(solution)/shard_map/ppermute | solution.py:150
  10.9 0.7 %copy-start.5 = (s32[1,1,8,8]{3,2,1,0:T(8,128)S(1)}, s32[1,1,8,8]{3,2,1,0:T(8,128)}, u32[]{:S(2)}) copy-start(s32[1,1,8,8]{3,2,1,0:T(8,128)} %param.9) | copy-start | bytes 772
  11.7 1.1 %collective-permute-start.3 = (s32[1,128]{1,0:T(1,128)S(1)}, s32[1,128]{1,0:T(1,128)S(1)}, u32[]{:S(2)}, u32[]{:S(2)}) collective-permute-start(s32[1,128]{1,0:T(1,128)S(1)} %shard_map.64.refs_8_.refs_5_), channel_id=1, source_target_pairs={{0,1},{1,0},{2,3},{3,2},{4,5},{5,4},{6,7},{7,6},{8,9},{9,8},{10,11... | collective-permute-start | bytes 1544 | tf_op jit(solution)/shard_map/ppermute | solution.py:150
  12.9 6.4 %collective-permute-start.5 = (bf16[16,2048]{1,0:T(8,128)(2,1)S(1)}, bf16[16,2048]{1,0:T(8,128)(2,1)S(1)}, u32[]{:S(2)}, u32[]{:S(2)}) collective-permute-start(bf16[16,2048]{1,0:T(8,128)(2,1)S(1)} %collective-permute-done.1.refs_1_), channel_id=1, source_target_pairs={{0,2},{2,0},{1,3},{3,1},{4,6},{6,4},{5,7},{7,5},{8,10},{10,8},{9,1... | collective-permute-start | bytes 196616 | tf_op jit(solution)/shard_map/ppermute | solution.py:150
  14.4 4.9 %collective-permute-start.6 = (bf16[16,2048]{1,0:T(8,128)(2,1)S(1)}, bf16[16,2048]{1,0:T(8,128)(2,1)S(1)}, u32[]{:S(2)}, u32[]{:S(2)}) collective-permute-start(bf16[16,2048]{1,0:T(8,128)(2,1)S(1)} %collective-permute-done.4.refs_3_), channel_id=1, source_target_pairs={{0,2},{2,0},{1,3},{3,1},{4,6},{6,4},{5,7},{7,5},{8,10},{10,8},{9,1... | collective-permute-start | bytes 196616 | tf_op jit(solution)/shard_map/ppermute | solution.py:150
  14.9 5.0 %collective-permute-start.7 = (bf16[16,2048]{1,0:T(8,128)(2,1)S(1)}, bf16[16,2048]{1,0:T(8,128)(2,1)S(1)}, u32[]{:S(2)}, u32[]{:S(2)}) collective-permute-start(bf16[16,2048]{1,0:T(8,128)(2,1)S(1)} %collective-permute-done.2.refs_4_), channel_id=1, source_target_pairs={{0,2},{2,0},{1,3},{3,1},{4,6},{6,4},{5,7},{7,5},{8,10},{10,8},{9,1... | collective-permute-start | bytes 196616 | tf_op jit(solution)/shard_map/ppermute | solution.py:150
  16.4 1.2 %copy-start.1 = (bf16[4,256,512]{2,1,0:T(8,128)(2,1)S(1)}, bf16[4,256,512]{2,1,0:T(8,128)(2,1)}, u32[]{:S(2)}) copy-start(bf16[4,256,512]{2,1,0:T(8,128)(2,1)} %refs_3_.1) | copy-start | bytes 3145732
  17.6 2.3 %copy-start.2 = (bf16[4,256,512]{2,1,0:T(8,128)(2,1)S(1)}, bf16[4,256,512]{2,1,0:T(8,128)(2,1)}, u32[]{:S(2)}) copy-start(bf16[4,256,512]{2,1,0:T(8,128)(2,1)} %refs_3_.1) | copy-start | bytes 3145732
  19.9 2.3 %copy-start.4 = (f32[4,256]{1,0:T(4,128)S(1)}, f32[4,256]{1,0:T(4,128)}, u32[]{:S(2)}) copy-start(f32[4,256]{1,0:T(4,128)} %refs_2_.1) | copy-start | bytes 12292
  21.0 1.2 %collective-permute-start.8 = (f32[4,256]{1,0:T(4,128)S(1)}, f32[4,256]{1,0:T(4,128)S(1)}, u32[]{:S(2)}, u32[]{:S(2)}) collective-permute-start(f32[4,256]{1,0:T(4,128)S(1)} %shard_map.66.refs_0_), channel_id=1, source_target_pairs={{0,1},{1,0},{2,3},{3,2},{4,5},{5,4},{6,7},{7,6},{8,9},{9,8},{10,11... | collective-permute-start | bytes 12296 | tf_op jit(solution)/shard_map/ppermute | solution.py:150
  23.7 4.8 %collective-permute-start.9 = (bf16[16,2048]{1,0:T(8,128)(2,1)S(1)}, bf16[16,2048]{1,0:T(8,128)(2,1)S(1)}, u32[]{:S(2)}, u32[]{:S(2)}) collective-permute-start(bf16[16,2048]{1,0:T(8,128)(2,1)S(1)} %get-tuple-element.30), channel_id=1, source_target_pairs={{0,2},{2,0},{1,3},{3,1},{4,6},{6,4},{5,7},{7,5},{8,10},{10,8},{9,1... | collective-permute-start | bytes 196616 | tf_op jit(solution)/shard_map/ppermute | solution.py:150
  25.2 5.5 %collective-permute-start.11 = (bf16[16,2048]{1,0:T(8,128)(2,1)S(1)}, bf16[16,2048]{1,0:T(8,128)(2,1)S(1)}, u32[]{:S(2)}, u32[]{:S(2)}) collective-permute-start(bf16[16,2048]{1,0:T(8,128)(2,1)S(1)} %get-tuple-element.34), channel_id=1, source_target_pairs={{0,2},{2,0},{1,3},{3,1},{4,6},{6,4},{5,7},{7,5},{8,10},{10,8},{9,1... | collective-permute-start | bytes 196616 | tf_op jit(solution)/shard_map/ppermute | solution.py:150
  25.8 6.6 %collective-permute-start.13 = (bf16[16,2048]{1,0:T(8,128)(2,1)S(1)}, bf16[16,2048]{1,0:T(8,128)(2,1)S(1)}, u32[]{:S(2)}, u32[]{:S(2)}) collective-permute-start(bf16[16,2048]{1,0:T(8,128)(2,1)S(1)} %get-tuple-element.36), channel_id=1, source_target_pairs={{0,2},{2,0},{1,3},{3,1},{4,6},{6,4},{5,7},{7,5},{8,10},{10,8},{9,1... | collective-permute-start | bytes 196616 | tf_op jit(solution)/shard_map/ppermute | solution.py:150
  28.5 4.3 %collective-permute-start.14 = (bf16[16,2048]{1,0:T(8,128)(2,1)S(1)}, bf16[16,2048]{1,0:T(8,128)(2,1)S(1)}, u32[]{:S(2)}, u32[]{:S(2)}) collective-permute-start(bf16[16,2048]{1,0:T(8,128)(2,1)S(1)} %add_convert_fusion.1), channel_id=1, source_target_pairs={{0,4},{4,0},{8,12},{12,8},{1,5},{5,1},{9,13},{13,9},{2,6},{6,2},{1... | collective-permute-start | bytes 196616 | tf_op jit(solution)/shard_map/ppermute | solution.py:150
  29.0 5.7 %collective-permute-start.10 = (bf16[16,2048]{1,0:T(8,128)(2,1)S(1)}, bf16[16,2048]{1,0:T(8,128)(2,1)S(1)}, u32[]{:S(2)}, u32[]{:S(2)}) collective-permute-start(bf16[16,2048]{1,0:T(8,128)(2,1)S(1)} %get-tuple-element.32), channel_id=1, source_target_pairs={{0,2},{2,0},{1,3},{3,1},{4,6},{6,4},{5,7},{7,5},{8,10},{10,8},{9,1... | collective-permute-start | bytes 196616 | tf_op jit(solution)/shard_map/ppermute | solution.py:150
  30.7 5.0 %collective-permute-start.12 = (bf16[16,2048]{1,0:T(8,128)(2,1)S(1)}, bf16[16,2048]{1,0:T(8,128)(2,1)S(1)}, u32[]{:S(2)}, u32[]{:S(2)}) collective-permute-start(bf16[16,2048]{1,0:T(8,128)(2,1)S(1)} %add_convert_fusion.2), channel_id=1, source_target_pairs={{0,4},{4,0},{8,12},{12,8},{1,5},{5,1},{9,13},{13,9},{2,6},{6,2},{1... | collective-permute-start | bytes 196616 | tf_op jit(solution)/shard_map/ppermute | solution.py:150
  32.8 5.9 %collective-permute-start.15 = (bf16[16,2048]{1,0:T(8,128)(2,1)S(1)}, bf16[16,2048]{1,0:T(8,128)(2,1)S(1)}, u32[]{:S(2)}, u32[]{:S(2)}) collective-permute-start(bf16[16,2048]{1,0:T(8,128)(2,1)S(1)} %add_convert_fusion), channel_id=1, source_target_pairs={{0,8},{4,12},{8,0},{12,4},{1,9},{5,13},{9,1},{13,5},{2,10},{6,14},... | collective-permute-start | bytes 196616 | tf_op jit(solution)/shard_map/ppermute | solution.py:150
  38.8 1.5 %copy-start.3 = (bf16[16,4096]{1,0:T(8,128)(2,1)S(1)}, bf16[16,4096]{1,0:T(8,128)(2,1)}, u32[]{:S(2)}) copy-start(bf16[16,4096]{1,0:T(8,128)(2,1)} %core_ref.1) | copy-start | bytes 393220
  38.8 1.4 %collective-permute-start.16 = (f32[16,2048]{1,0:T(8,128)S(1)}, f32[16,2048]{1,0:T(8,128)S(1)}, u32[]{:S(2)}, u32[]{:S(2)}) collective-permute-start(f32[16,2048]{1,0:T(8,128)S(1)} %convert_add_fusion.mine_ref), channel_id=1, source_target_pairs={{0,1},{1,0},{2,3},{3,2},{4,5},{5,4},{6,7},{7,6},{8,9},{9,8},{10,11... | collective-permute-start | bytes 393224 | tf_op jit(solution)/shard_map/ppermute | solution.py:150

commit v7 on v6

--- a/solution.py
+++ b/solution.py
@@ -45,8 +45,8 @@
     rows_ref[...] = jnp.sum(chosen, axis=0, keepdims=True) + owner * held
 
 
-def row_table(place_ref, half_ref, own_ref, other_ref, held, owners):
-    low = half_ref[0] == 0
+def row_table(place_ref, core_ref, own_ref, other_ref, held, owners):
+    low = core_ref[0] == 0
     rows = jnp.concatenate(
         [jnp.where(low, own_ref[...], other_ref[...]), jnp.where(low, other_ref[...], own_ref[...])], axis=1
     )
@@ -55,7 +55,7 @@
     return jnp.where(row == rows, 1.0, 0.0)
 
 
-def density_kernel(places, place_ref, half_ref, *refs):
+def density_kernel(places, place_ref, core_ref, *refs):
     piece_refs = refs[:len(places)]
     own_ref, other_ref, left_ref, values_ref, out_ref, table, dense = refs[len(places):]
     batches, points, columns = values_ref.shape
@@ -63,7 +63,7 @@
     held = piece_refs[0].shape[0]
     for ref, k in zip(piece_refs, places):
         table[k * held:(k + 1) * held, :] = ref[...]
-    pick = row_table(place_ref, half_ref, own_ref, other_ref, held, len(places)).T.astype(jnp.bfloat16)
+    pick = row_table(place_ref, core_ref, own_ref, other_ref, held, len(places)).T.astype(jnp.bfloat16)
     low = lax.broadcasted_iota(jnp.int32, (1, 1, 1, groups, 128), 4) < GO
     for j in range(table.shape[1] // 128):
         lanes = slice(j * 128, (j + 1) * 128)
@@ -85,13 +85,13 @@
         out_ref[t:t + 1, :] = jnp.sum(folded.T, axis=0, keepdims=True)
 
 
-def scatter_kernel(place_ref, half_ref, *refs):
+def scatter_kernel(place_ref, core_ref, *refs):
     mine_ref, far_ref, weight_ref, values_ref, left_t_ref, own_ref, other_ref = refs[:7]
     out_refs = refs[7:-2]
     high, rest = refs[-2:]
     pieces = len(out_refs)
     held = out_refs[0].shape[0]
-    put = row_table(place_ref, half_ref, own_ref, other_ref, held, pieces).astype(jnp.bfloat16)
+    put = row_table(place_ref, core_ref, own_ref, other_ref, held, pieces).astype(jnp.bfloat16)
     batches, points, columns = values_ref.shape
     groups = columns // GO
     kept = left_t_ref.shape[1]
@@ -146,8 +146,22 @@
     )
 
 
-def swap(array, axis, count, step):
-    return lax.ppermute(array, axis, [(i, i ^ step) for i in range(count)])
+def odd_bits(number, count):
+    parity = number & 1
+    for shift in range(1, (count - 1).bit_length()):
+        parity = parity ^ ((number >> shift) & 1)
+    return parity
+
+
+def swap(array, sizes, dz, dx):
+    rows_z, rows_x = sizes
+    turn = odd_bits(dz, rows_z) ^ odd_bits(dx, rows_x)
+    step = (dz * rows_x + dx) * 2 + turn
+    return lax.ppermute(array, ("batch", "pair", "orb"), [(i, i ^ step) for i in range(rows_z * rows_x * 2)])
+
+
+def swap_cores(array):
+    return lax.ppermute(array, "orb", [(0, 1), (1, 0)])
 
 
 def add_all(terms):
@@ -159,7 +173,9 @@
 
 def per_device(basis_values, point_weights, slot_ids, fetch_rows, density_blocks, core_blocks):
     rows_z, rows_x = lax.axis_size("batch"), lax.axis_size("pair")
-    z, x, half = lax.axis_index("batch"), lax.axis_index("pair"), lax.axis_index("orb")
+    z, x, core = lax.axis_index("batch"), lax.axis_index("pair"), lax.axis_index("orb")
+    sizes = (rows_z, rows_x)
+    half = core ^ odd_bits(z, rows_z) ^ odd_bits(x, rows_x)
     owners = rows_z * rows_x
     batches, points, columns = basis_values.shape
     groups, own_groups = slot_ids.shape[1], slot_ids.shape[2]
@@ -176,32 +192,26 @@
         jax.ShapeDtypeStruct((1, batches * own_groups * groups), jnp.int32),
         2,
     )(fetch_rows.reshape(owners, capacity), slot_ids.transpose(0, 2, 1).reshape(1, -1))
-    other_rows = swap(own_rows, "orb", 2, 1)
-
-    bits = [1 << i for i in reversed(range(rows_z.bit_length() - 1))]
+    other_rows = swap_cores(own_rows)
+
+    steps = list(range(rows_z // 2, rows_z)) + list(range(1, rows_z // 2))
     side = list(range(1, rows_x))
 
     mine = lax.dynamic_slice_in_dim(density_blocks, half * wide, wide, 1)
     pieces = {0: mine}
-    have = [0]
-    for bit in bits:
-        for dz in have:
-            pieces[(dz | bit) * rows_x] = swap(pieces[dz * rows_x], "batch", rows_z, bit)
-        if bit == bits[0]:
-            for dx in side:
-                pieces[dx] = swap(mine, "pair", rows_x, dx)
-            ready = side + [bit * rows_x]
-            ordered = lax.optimization_barrier([pieces[k] for k in ready])
-            pieces.update(zip(ready, ordered))
-        have = have + [dz | bit for dz in have]
-    first = bits[0] * rows_x
-    pieces[first], other_rows = lax.optimization_barrier((pieces[first], other_rows))
-    for dz in have[1:]:
+    for dx in side:
+        pieces[dx] = swap(mine, sizes, 0, dx)
+    for dz in steps[::-1]:
+        pieces[dz * rows_x] = swap(mine, sizes, dz, 0)
+    first, last = steps[0] * rows_x, (rows_z - 1) * rows_x
+    pieces[first], own_rows = lax.optimization_barrier((pieces[first], own_rows))
+    pieces[last], other_rows = lax.optimization_barrier((pieces[last], other_rows))
+    for dz in steps[rows_z // 2:] + steps[:rows_z // 2]:
         for dx in side:
-            pieces[dz * rows_x + dx] = swap(pieces[dz * rows_x], "pair", rows_x, dx)
+            pieces[dz * rows_x + dx] = swap(pieces[dz * rows_x], sizes, 0, dx)
     order = list(pieces)
 
-    half_at, _ = lax.optimization_barrier((half.reshape(1).astype(jnp.int32), pieces[(rows_z - 1) * rows_x]))
+    half_at, _ = lax.optimization_barrier((half.reshape(1).astype(jnp.int32), pieces[last]))
     left, left_t = call(
         prepare_kernel,
         (
@@ -215,7 +225,7 @@
     )(half_at, basis_values)
 
     place = (z * rows_x + x).reshape(1).astype(jnp.int32)
-    side_at = half.reshape(1).astype(jnp.int32)
+    core_at = core.reshape(1).astype(jnp.int32)
 
     partial = call(
         functools.partial(density_kernel, order),
@@ -225,8 +235,8 @@
         scratch=(pltpu.VMEM((table_rows, wide), bf16), pltpu.VMEM((batches, kept, columns), bf16)),
         flops=2 * batches * points * columns * kept,
         moved=2 * batches * points * columns * 2,
-    )(place, side_at, *[pieces[k] for k in order], own_rows, other_rows, left, basis_values)
-    partial_other = swap(partial, "orb", 2, 1)
+    )(place, core_at, *[pieces[k] for k in order], own_rows, other_rows, left, basis_values)
+    partial_other = swap_cores(partial)
 
     sums = call(
         scatter_kernel,
@@ -236,23 +246,23 @@
         scratch=(pltpu.VMEM((entries, wide), bf16), pltpu.VMEM((entries, wide), bf16)),
         flops=2 * batches * points * columns * kept,
         moved=2 * batches * points * columns * 2,
-    )(place, side_at, partial, partial_other, point_weights, basis_values, left_t, own_rows, other_rows)
-
-    sums = list(sums)
-    joined = {}
-    for dz in reversed(have):
-        terms = [sums[dz * rows_x]] + [swap(sums[dz * rows_x + dx], "pair", rows_x, dx) for dx in side]
-        if dz == rows_z - 1:
-            terms[-1], *sums[1:rows_x] = lax.optimization_barrier((terms[-1], *sums[1:rows_x]))
-        joined[dz] = [term.astype(f32) for term in terms]
-    for bit in reversed(bits):
-        for dz in range(rows_z - bit, 0, -2 * bit):
-            sent = add_all(joined.pop(dz)).astype(bf16)
-            came = swap(sent, "batch", rows_z, bit)
-            joined[dz ^ bit].append(came.astype(f32))
-    landed = joined[0]
-    total = add_all(landed)
-    total_other = swap(total, "orb", 2, 1)
+    )(place, core_at, partial, partial_other, point_weights, basis_values, left_t, own_rows, other_rows)
+
+    landed = []
+    own = sums[:rows_x]
+    for dz in steps:
+        joined = sums[dz * rows_x].astype(f32)
+        for dx in side:
+            joined = joined + swap(sums[dz * rows_x + dx], sizes, 0, dx).astype(f32)
+        joined = joined.astype(bf16)
+        if dz == steps[0]:
+            joined, *own = lax.optimization_barrier((joined, *own))
+        landed.append(swap(joined, sizes, dz, 0))
+    for dx in side:
+        landed.append(swap(own[dx], sizes, 0, dx))
+    landed.append(own[0])
+    total = add_all([term.astype(f32) for term in landed])
+    total_other = swap_cores(total)
     return call(
         finish_kernel, jax.ShapeDtypeStruct((held, square), f32), 3, scalars=1, moved=held * square * 12
     )(half_at, total, total_other, core_blocks)

time: 41.2 us -> 39.2 us (0.951)
  starting transfers between devices: 21.5 us -> 19.9 us
    ppermute x17, starting transfers between devices: 21.5 us -> 19.9 us  [the longest x14 19.4 us: swap(): lax.ppermute(array, ('batch', 'pair', 'orb'), [(i, i ^ step) for i in ran...]
    unnamed x14 -> x12, local copies, waits for them, and re-layouts: 2.74 us -> 2.74 us
where the time goes in v7:
time: 39.2 us; the launch traced here: 39 us
  starting transfers between devices  19.9 us (51%)
  waiting for transfers between devices  12 us (31%)
  Pallas kernels  4.19 us (11%)
  local copies, waits for them, and re-layouts  2.83 us (7%)
    ppermute x14, starting transfers between devices, swap(): lax.ppermute(array, ('batch', 'pair', 'orb'), [(i, i ^ step) for i in ran...  19.4 us
    ppermute x14, waiting for transfers between devices, swap(): lax.ppermute(array, ('batch', 'pair', 'orb'), [(i, i ^ step) for i in ran...  9.73 us
    unnamed x12, local copies, waits for them, and re-layouts  2.74 us
    ppermute x3, waiting for transfers between devices, swap_cores(): return lax.ppermute(array, 'orb', [(0, 1), (1, 0)])  2.22 us
    pallas_call x1, Pallas kernels, per_device(): call(scatter_kernel, [jax.ShapeDtypeStruct((held, wide), bf16)] * owners,...  1.41 us
    pallas_call x1, Pallas kernels, per_device(): call(functools.partial(density_kernel, order), jax.ShapeDtypeStruct((batc...  1.09 us
  transfers between devices with their start and end apart: 17, of which 11 were waited for; matrix products, arithmetic and copies ran while one was open for 0% of the time, Pallas kernels for 2%

profile of v7, /device:TPU:0, one launch (start us, length us, event | category | flops | bytes accessed | tf_op | source)
XLA Modules:
  0.0 39.0 jit_solution(3068185400253900501)
XLA Ops:
  0.0 0.0 copy-start
  0.0 0.9 %copy-done = bf16[16,4096]{1,0:T(8,128)(2,1)S(1)} copy-done((bf16[16,4096]{1,0:T(8,128)(2,1)S(1)}, bf16[16,4096]{1,0:T(8,128)(2,1)}, u32[]{:S(2)}) %copy-start) | copy-done | bytes 131096
  0.9 3.5 %collective-permute-start.4 = (bf16[16,2048]{1,0:T(8,128)(2,1)S(1)}, bf16[16,2048]{1,0:T(8,128)(2,1)S(1)}, u32[]{:S(2)}, u32[]{:S(2)}) collective-permute-start(bf16[16,2048]{1,0:T(8,128)(2,1)S(1)} %constant_dynamic-slice_fusion.refs_0_), channel_id=1, source_target_pairs={{0,9},{1,8},{2,11},{3,10},{4,13},{5,12},{6,15},{7,14},{8,1},{9,0},... | collective-permute-start | bytes 196616 | tf_op jit(solution)/shard_map/ppermute | solution.py:160
  4.5 1.7 %collective-permute-start = (bf16[16,2048]{1,0:T(8,128)(2,1)S(1)}, bf16[16,2048]{1,0:T(8,128)(2,1)S(1)}, u32[]{:S(2)}, u32[]{:S(2)}) collective-permute-start(bf16[16,2048]{1,0:T(8,128)(2,1)S(1)} %constant_dynamic-slice_fusion.refs_0_), channel_id=1, source_target_pairs={{0,12},{1,13},{2,14},{3,15},{4,8},{5,9},{6,10},{7,11},{8,4},{9,5},... | collective-permute-start | bytes 196616 | tf_op jit(solution)/shard_map/ppermute | solution.py:160
  6.1 0.2 collective-permute-start.3
  6.3 0.0 copy-done.5
  6.3 0.1 reshape.17.slots_ref
  6.4 0.6 %copy-done.4 = s32[1,1,8,8]{3,2,1,0:T(8,128)S(1)} copy-done((s32[1,1,8,8]{3,2,1,0:T(8,128)S(1)}, s32[1,1,8,8]{3,2,1,0:T(8,128)}, u32[]{:S(2)}) %copy-start.4) | copy-done | bytes 280
  7.0 0.2 shard_map.64.refs_8_.refs_5_
  7.2 0.0 collective-permute-start.1
  7.2 1.6 %collective-permute-start.2 = (bf16[16,2048]{1,0:T(8,128)(2,1)S(1)}, bf16[16,2048]{1,0:T(8,128)(2,1)S(1)}, u32[]{:S(2)}, u32[]{:S(2)}) collective-permute-start(bf16[16,2048]{1,0:T(8,128)(2,1)S(1)} %constant_dynamic-slice_fusion.refs_0_), channel_id=1, source_target_pairs={{0,3},{1,2},{2,1},{3,0},{4,7},{5,6},{6,5},{7,4},{8,11},{9,10},{10,... | collective-permute-start | bytes 196616 | tf_op jit(solution)/shard_map/ppermute | solution.py:160
  8.8 0.0 collective-permute-done.4.refs_4_
  8.8 1.5 %collective-permute-start.6 = (bf16[16,2048]{1,0:T(8,128)(2,1)S(1)}, bf16[16,2048]{1,0:T(8,128)(2,1)S(1)}, u32[]{:S(2)}, u32[]{:S(2)}) collective-permute-start(bf16[16,2048]{1,0:T(8,128)(2,1)S(1)} %collective-permute-done.4.refs_4_), channel_id=1, source_target_pairs={{0,3},{1,2},{2,1},{3,0},{4,7},{5,6},{6,5},{7,4},{8,11},{9,10},{10,... | collective-permute-start | bytes 196616 | tf_op jit(solution)/shard_map/ppermute | solution.py:160
  10.3 0.0 collective-permute-done.1.refs_9_.refs_6_
  10.3 1.0 %collective-permute-done.refs_3_ = bf16[16,2048]{1,0:T(8,128)(2,1)S(1)} collective-permute-done((bf16[16,2048]{1,0:T(8,128)(2,1)S(1)}, bf16[16,2048]{1,0:T(8,128)(2,1)S(1)}, u32[]{:S(2)}, u32[]{:S(2)}) %collective-permute-start) | collective-permute-done | bytes 65568 | tf_op jit(solution)/shard_map/ppermute | solution.py:160
  11.3 0.4 collective-permute-done.3.refs_2_
  11.7 1.6 %collective-permute-start.5 = (bf16[16,2048]{1,0:T(8,128)(2,1)S(1)}, bf16[16,2048]{1,0:T(8,128)(2,1)S(1)}, u32[]{:S(2)}, u32[]{:S(2)}) collective-permute-start(bf16[16,2048]{1,0:T(8,128)(2,1)S(1)} %collective-permute-done.3.refs_2_), channel_id=1, source_target_pairs={{0,3},{1,2},{2,1},{3,0},{4,7},{5,6},{6,5},{7,4},{8,11},{9,10},{10,... | collective-permute-start | bytes 196616 | tf_op jit(solution)/shard_map/ppermute | solution.py:160
  13.3 0.2 collective-permute-start.7
  13.4 1.2 %copy-done.1 = bf16[4,256,512]{2,1,0:T(8,128)(2,1)S(1)} copy-done((bf16[4,256,512]{2,1,0:T(8,128)(2,1)S(1)}, bf16[4,256,512]{2,1,0:T(8,128)(2,1)}, u32[]{:S(2)}) %copy-start.1) | copy-done | bytes 1048600
  14.7 0.8 %shard_map.65 = (bf16[4,256,256]{2,1,0:T(8,128)(2,1)S(1)}, bf16[4,256,256]{2,1,0:T(8,128)(2,1)S(1)}) custom-call(s32[1]{0:T(128)} %bitcast.half_ref, bf16[4,256,512]{2,1,0:T(8,128)(2,1)S(1)} %copy-done.1), custom_call_target="tpu_custom_call" | custom-call | flops 536870912 | bytes 3145728 | tf_op jit(solution)/shard_map/pallas_call | solution.py:215
  15.4 0.0 collective-permute-done.2.refs_1_
  15.4 0.0 collective-permute-done.6.refs_6_
  15.4 0.2 collective-permute-done.5.refs_5_
  15.7 1.6 %collective-permute-done.7.refs_7_ = bf16[16,2048]{1,0:T(8,128)(2,1)S(1)} collective-permute-done((bf16[16,2048]{1,0:T(8,128)(2,1)S(1)}, bf16[16,2048]{1,0:T(8,128)(2,1)S(1)}, u32[]{:S(2)}, u32[]{:S(2)}) %collective-permute-start.7) | collective-permute-done | bytes 65568 | tf_op jit(solution)/shard_map/ppermute | solution.py:160
  17.3 1.1 %shard_map.66.refs_0_ = f32[4,256]{1,0:T(4,128)S(1)} custom-call(s32[1]{0:T(128)} %bitcast.3.place_ref, s32[1]{0:T(128)} %bitcast.4.core_ref, bf16[16,2048]{1,0:T(8,128)(2,1)S(1)} %constant_dynamic-slice_fusion.refs_0_, bf16[16,2048]{1,0:T(8,128)(2,1)S(1)} %collective-permute-done.2.refs_1_, bf16[16,2048]{1,0:T(8,128)(2,1)S(1)} %collective-permute-done.3.refs_2_, ...), custom_call_target="tpu_custom_call" | custom-call | flops 268435456 | bytes 2097152 | tf_op jit(solution)/shard_map/pallas_call | solution.py:230
  18.4 0.2 collective-permute-start.8
  18.6 1.0 %collective-permute-done.8.refs_1_ = f32[4,256]{1,0:T(4,128)S(1)} collective-permute-done((f32[4,256]{1,0:T(4,128)S(1)}, f32[4,256]{1,0:T(4,128)S(1)}, u32[]{:S(2)}, u32[]{:S(2)}) %collective-permute-start.8) | collective-permute-done | bytes 4128 | tf_op jit(solution)/shard_map/ppermute | solution.py:164
  19.6 0.0 copy-done.3
  19.6 1.4 %shard_map.67 = (bf16[16,2048]{1,0:T(8,128)(2,1)S(1)}, bf16[16,2048]{1,0:T(8,128)(2,1)S(1)}, bf16[16,2048]{1,0:T(8,128)(2,1)S(1)}, bf16[16,2048]{1,0:T(8,128)(2,...) custom-call(s32[1]{0:T(128)} %bitcast.3.place_ref, ...), custom_call_target="tpu_custom_call" | custom-call | flops 268435456 | bytes 2097152 | tf_op jit(solution)/shard_map/pallas_call | solution.py:241
  21.0 1.4 %collective-permute-start.9 = (bf16[16,2048]{1,0:T(8,128)(2,1)S(1)}, bf16[16,2048]{1,0:T(8,128)(2,1)S(1)}, u32[]{:S(2)}, u32[]{:S(2)}) collective-permute-start(bf16[16,2048]{1,0:T(8,128)(2,1)S(1)} %get-tuple-element.31), channel_id=1, source_target_pairs={{0,3},{1,2},{2,1},{3,0},{4,7},{5,6},{6,5},{7,4},{8,11},{9,10},{10,... | collective-permute-start | bytes 196616 | tf_op jit(solution)/shard_map/ppermute | solution.py:160
  22.4 0.4 %collective-permute-start.11 = (bf16[16,2048]{1,0:T(8,128)(2,1)S(1)}, bf16[16,2048]{1,0:T(8,128)(2,1)S(1)}, u32[]{:S(2)}, u32[]{:S(2)}) collective-permute-start(bf16[16,2048]{1,0:T(8,128)(2,1)S(1)} %get-tuple-element.36), channel_id=1, source_target_pairs={{0,3},{1,2},{2,1},{3,0},{4,7},{5,6},{6,5},{7,4},{8,11},{9,10},{10,... | collective-permute-start | bytes 196616 | tf_op jit(solution)/shard_map/ppermute | solution.py:160
  22.8 1.3 %collective-permute-start.13 = (bf16[16,2048]{1,0:T(8,128)(2,1)S(1)}, bf16[16,2048]{1,0:T(8,128)(2,1)S(1)}, u32[]{:S(2)}, u32[]{:S(2)}) collective-permute-start(bf16[16,2048]{1,0:T(8,128)(2,1)S(1)} %get-tuple-element.38), channel_id=1, source_target_pairs={{0,3},{1,2},{2,1},{3,0},{4,7},{5,6},{6,5},{7,4},{8,11},{9,10},{10,... | collective-permute-start | bytes 196616 | tf_op jit(solution)/shard_map/ppermute | solution.py:160
  24.2 1.0 %collective-permute-done.9 = bf16[16,2048]{1,0:T(8,128)(2,1)S(1)} collective-permute-done((bf16[16,2048]{1,0:T(8,128)(2,1)S(1)}, bf16[16,2048]{1,0:T(8,128)(2,1)S(1)}, u32[]{:S(2)}, u32[]{:S(2)}) %collective-permute-start.9) | collective-permute-done | bytes 65568 | tf_op jit(solution)/shard_map/ppermute | solution.py:160
  25.2 2.9 %collective-permute-start.10 = (bf16[16,2048]{1,0:T(8,128)(2,1)S(1)}, bf16[16,2048]{1,0:T(8,128)(2,1)S(1)}, u32[]{:S(2)}, u32[]{:S(2)}) collective-permute-start(bf16[16,2048]{1,0:T(8,128)(2,1)S(1)} %add_convert_fusion.2), channel_id=1, source_target_pairs={{0,9},{1,8},{2,11},{3,10},{4,13},{5,12},{6,15},{7,14},{8,1},{9,0},... | collective-permute-start | bytes 196616 | tf_op jit(solution)/shard_map/ppermute | solution.py:160
  28.2 1.0 %collective-permute-start.15 = (bf16[16,2048]{1,0:T(8,128)(2,1)S(1)}, bf16[16,2048]{1,0:T(8,128)(2,1)S(1)}, u32[]{:S(2)}, u32[]{:S(2)}) collective-permute-start(bf16[16,2048]{1,0:T(8,128)(2,1)S(1)} %get-tuple-element.39), channel_id=1, source_target_pairs={{0,3},{1,2},{2,1},{3,0},{4,7},{5,6},{6,5},{7,4},{8,11},{9,10},{10,... | collective-permute-start | bytes 196616 | tf_op jit(solution)/shard_map/ppermute | solution.py:160
  29.2 0.0 collective-permute-done.11
  29.2 1.8 %collective-permute-start.12 = (bf16[16,2048]{1,0:T(8,128)(2,1)S(1)}, bf16[16,2048]{1,0:T(8,128)(2,1)S(1)}, u32[]{:S(2)}, u32[]{:S(2)}) collective-permute-start(bf16[16,2048]{1,0:T(8,128)(2,1)S(1)} %add_convert_fusion.1), channel_id=1, source_target_pairs={{0,12},{1,13},{2,14},{3,15},{4,8},{5,9},{6,10},{7,11},{8,4},{9,5},... | collective-permute-start | bytes 196616 | tf_op jit(solution)/shard_map/ppermute | solution.py:160
  31.0 0.0 collective-permute-done.13
  31.0 0.0 copy-start.2
  31.1 0.3 collective-permute-start.14
  31.4 0.6 %collective-permute-done.10 = bf16[16,2048]{1,0:T(8,128)(2,1)S(1)} collective-permute-done((bf16[16,2048]{1,0:T(8,128)(2,1)S(1)}, bf16[16,2048]{1,0:T(8,128)(2,1)S(1)}, u32[]{:S(2)}, u32[]{:S(2)}) %collective-permute-start.10) | collective-permute-done | bytes 65568 | tf_op jit(solution)/shard_map/ppermute | solution.py:160
  31.9 0.4 collective-permute-done.15
  32.3 3.8 %collective-permute-done.12 = bf16[16,2048]{1,0:T(8,128)(2,1)S(1)} collective-permute-done((bf16[16,2048]{1,0:T(8,128)(2,1)S(1)}, bf16[16,2048]{1,0:T(8,128)(2,1)S(1)}, u32[]{:S(2)}, u32[]{:S(2)}) %collective-permute-start.12) | collective-permute-done | bytes 65568 | tf_op jit(solution)/shard_map/ppermute | solution.py:160
  36.1 0.7 %collective-permute-done.14 = bf16[16,2048]{1,0:T(8,128)(2,1)S(1)} collective-permute-done((bf16[16,2048]{1,0:T(8,128)(2,1)S(1)}, bf16[16,2048]{1,0:T(8,128)(2,1)S(1)}, u32[]{:S(2)}, u32[]{:S(2)}) %collective-permute-start.14) | collective-permute-done | bytes 65568 | tf_op jit(solution)/shard_map/ppermute | solution.py:160
  36.9 0.2 collective-permute-start.16
  37.1 1.2 %collective-permute-done.16.other_ref = f32[16,2048]{1,0:T(8,128)S(1)} collective-permute-done((f32[16,2048]{1,0:T(8,128)S(1)}, f32[16,2048]{1,0:T(8,128)S(1)}, u32[]{:S(2)}, u32[]{:S(2)}) %collective-permute-start.16) | collective-permute-done | bytes 131104 | tf_op jit(solution)/shard_map/ppermute | solution.py:164
  38.3 0.0 copy-done.2
  38.3 0.7 %shard_map.68 = f32[16,4096]{1,0:T(8,128)} custom-call(s32[1]{0:T(128)} %bitcast.half_ref, f32[16,2048]{1,0:T(8,128)S(1)} %convert_add_fusion.mine_ref, f32[16,2048]{1,0:T(8,128)S(1)} %collective-permute-done.16.other_ref, bf16[16,4096]{1,0:T(8,128)(2,1)S(1)} %copy-done.2), custom_call_target="tpu_custom_call" | custom-call | bytes 786432 | tf_op jit(solution)/shard_map/pallas_call | solution.py:266
  (9 shorter events, 0.1 us)
Async XLA Ops:
  0.0 0.9 %copy-start = (bf16[16,4096]{1,0:T(8,128)(2,1)S(1)}, bf16[16,4096]{1,0:T(8,128)(2,1)}, u32[]{:S(2)}) copy-start(bf16[16,4096]{1,0:T(8,128)(2,1)} %param.10) | copy-start | bytes 393220
  0.9 5.4 %copy-start.5 = (s32[4,8,4]{1,2,0:T(4,128)S(1)}, s32[4,8,4]{1,2,0:T(4,128)}, u32[]{:S(2)}) copy-start(s32[4,8,4]{1,2,0:T(4,128)} %param.8) | copy-start | bytes 1540
  0.9 7.9 %collective-permute-start.4 = (bf16[16,2048]{1,0:T(8,128)(2,1)S(1)}, bf16[16,2048]{1,0:T(8,128)(2,1)S(1)}, u32[]{:S(2)}, u32[]{:S(2)}) collective-permute-start(bf16[16,2048]{1,0:T(8,128)(2,1)S(1)} %constant_dynamic-slice_fusion.refs_0_), channel_id=1, source_target_pairs={{0,9},{1,8},{2,11},{3,10},{4,13},{5,12},{6,15},{7,14},{8,1},{9,0},... | collective-permute-start | bytes 196616 | tf_op jit(solution)/shard_map/ppermute | solution.py:160
  4.5 6.8 %collective-permute-start = (bf16[16,2048]{1,0:T(8,128)(2,1)S(1)}, bf16[16,2048]{1,0:T(8,128)(2,1)S(1)}, u32[]{:S(2)}, u32[]{:S(2)}) collective-permute-start(bf16[16,2048]{1,0:T(8,128)(2,1)S(1)} %constant_dynamic-slice_fusion.refs_0_), channel_id=1, source_target_pairs={{0,12},{1,13},{2,14},{3,15},{4,8},{5,9},{6,10},{7,11},{8,4},{9,5},... | collective-permute-start | bytes 196616 | tf_op jit(solution)/shard_map/ppermute | solution.py:160
  6.1 5.5 %collective-permute-start.3 = (bf16[16,2048]{1,0:T(8,128)(2,1)S(1)}, bf16[16,2048]{1,0:T(8,128)(2,1)S(1)}, u32[]{:S(2)}, u32[]{:S(2)}) collective-permute-start(bf16[16,2048]{1,0:T(8,128)(2,1)S(1)} %constant_dynamic-slice_fusion.refs_0_), channel_id=1, source_target_pairs={{0,5},{1,4},{2,7},{3,6},{4,1},{5,0},{6,3},{7,2},{8,13},{9,12},{10,... | collective-permute-start | bytes 196616 | tf_op jit(solution)/shard_map/ppermute | solution.py:160
  6.3 0.7 %copy-start.4 = (s32[1,1,8,8]{3,2,1,0:T(8,128)S(1)}, s32[1,1,8,8]{3,2,1,0:T(8,128)}, u32[]{:S(2)}) copy-start(s32[1,1,8,8]{3,2,1,0:T(8,128)} %param.9) | copy-start | bytes 772
  7.2 3.1 %collective-permute-start.1 = (s32[1,128]{1,0:T(1,128)S(1)}, s32[1,128]{1,0:T(1,128)S(1)}, u32[]{:S(2)}, u32[]{:S(2)}) collective-permute-start(s32[1,128]{1,0:T(1,128)S(1)} %shard_map.64.refs_8_.refs_5_), channel_id=1, source_target_pairs={{0,1},{1,0},{2,3},{3,2},{4,5},{5,4},{6,7},{7,6},{8,9},{9,8},{10,11... | collective-permute-start | bytes 1544 | tf_op jit(solution)/shard_map/ppermute | solution.py:164
  7.2 8.2 %collective-permute-start.2 = (bf16[16,2048]{1,0:T(8,128)(2,1)S(1)}, bf16[16,2048]{1,0:T(8,128)(2,1)S(1)}, u32[]{:S(2)}, u32[]{:S(2)}) collective-permute-start(bf16[16,2048]{1,0:T(8,128)(2,1)S(1)} %constant_dynamic-slice_fusion.refs_0_), channel_id=1, source_target_pairs={{0,3},{1,2},{2,1},{3,0},{4,7},{5,6},{6,5},{7,4},{8,11},{9,10},{10,... | collective-permute-start | bytes 196616 | tf_op jit(solution)/shard_map/ppermute | solution.py:160
  8.8 6.6 %collective-permute-start.6 = (bf16[16,2048]{1,0:T(8,128)(2,1)S(1)}, bf16[16,2048]{1,0:T(8,128)(2,1)S(1)}, u32[]{:S(2)}, u32[]{:S(2)}) collective-permute-start(bf16[16,2048]{1,0:T(8,128)(2,1)S(1)} %collective-permute-done.4.refs_4_), channel_id=1, source_target_pairs={{0,3},{1,2},{2,1},{3,0},{4,7},{5,6},{6,5},{7,4},{8,11},{9,10},{10,... | collective-permute-start | bytes 196616 | tf_op jit(solution)/shard_map/ppermute | solution.py:160
  11.7 4.0 %collective-permute-start.5 = (bf16[16,2048]{1,0:T(8,128)(2,1)S(1)}, bf16[16,2048]{1,0:T(8,128)(2,1)S(1)}, u32[]{:S(2)}, u32[]{:S(2)}) collective-permute-start(bf16[16,2048]{1,0:T(8,128)(2,1)S(1)} %collective-permute-done.3.refs_2_), channel_id=1, source_target_pairs={{0,3},{1,2},{2,1},{3,0},{4,7},{5,6},{6,5},{7,4},{8,11},{9,10},{10,... | collective-permute-start | bytes 196616 | tf_op jit(solution)/shard_map/ppermute | solution.py:160
  13.3 4.0 %collective-permute-start.7 = (bf16[16,2048]{1,0:T(8,128)(2,1)S(1)}, bf16[16,2048]{1,0:T(8,128)(2,1)S(1)}, u32[]{:S(2)}, u32[]{:S(2)}) collective-permute-start(bf16[16,2048]{1,0:T(8,128)(2,1)S(1)} %collective-permute-done.refs_3_), channel_id=1, source_target_pairs={{0,3},{1,2},{2,1},{3,0},{4,7},{5,6},{6,5},{7,4},{8,11},{9,10},{10,... | collective-permute-start | bytes 196616 | tf_op jit(solution)/shard_map/ppermute | solution.py:160
  13.4 1.2 %copy-start.1 = (bf16[4,256,512]{2,1,0:T(8,128)(2,1)S(1)}, bf16[4,256,512]{2,1,0:T(8,128)(2,1)}, u32[]{:S(2)}) copy-start(bf16[4,256,512]{2,1,0:T(8,128)(2,1)} %refs_3_.1) | copy-start | bytes 3145732
  17.3 2.3 %copy-start.3 = (f32[4,256]{1,0:T(4,128)S(1)}, f32[4,256]{1,0:T(4,128)}, u32[]{:S(2)}) copy-start(f32[4,256]{1,0:T(4,128)} %refs_2_.1) | copy-start | bytes 12292
  18.4 1.2 %collective-permute-start.8 = (f32[4,256]{1,0:T(4,128)S(1)}, f32[4,256]{1,0:T(4,128)S(1)}, u32[]{:S(2)}, u32[]{:S(2)}) collective-permute-start(f32[4,256]{1,0:T(4,128)S(1)} %shard_map.66.refs_0_), channel_id=1, source_target_pairs={{0,1},{1,0},{2,3},{3,2},{4,5},{5,4},{6,7},{7,6},{8,9},{9,8},{10,11... | collective-permute-start | bytes 12296 | tf_op jit(solution)/shard_map/ppermute | solution.py:164
  21.0 4.2 %collective-permute-start.9 = (bf16[16,2048]{1,0:T(8,128)(2,1)S(1)}, bf16[16,2048]{1,0:T(8,128)(2,1)S(1)}, u32[]{:S(2)}, u32[]{:S(2)}) collective-permute-start(bf16[16,2048]{1,0:T(8,128)(2,1)S(1)} %get-tuple-element.31), channel_id=1, source_target_pairs={{0,3},{1,2},{2,1},{3,0},{4,7},{5,6},{6,5},{7,4},{8,11},{9,10},{10,... | collective-permute-start | bytes 196616 | tf_op jit(solution)/shard_map/ppermute | solution.py:160
  22.4 6.8 %collective-permute-start.11 = (bf16[16,2048]{1,0:T(8,128)(2,1)S(1)}, bf16[16,2048]{1,0:T(8,128)(2,1)S(1)}, u32[]{:S(2)}, u32[]{:S(2)}) collective-permute-start(bf16[16,2048]{1,0:T(8,128)(2,1)S(1)} %get-tuple-element.36), channel_id=1, source_target_pairs={{0,3},{1,2},{2,1},{3,0},{4,7},{5,6},{6,5},{7,4},{8,11},{9,10},{10,... | collective-permute-start | bytes 196616 | tf_op jit(solution)/shard_map/ppermute | solution.py:160
  22.8 8.2 %collective-permute-start.13 = (bf16[16,2048]{1,0:T(8,128)(2,1)S(1)}, bf16[16,2048]{1,0:T(8,128)(2,1)S(1)}, u32[]{:S(2)}, u32[]{:S(2)}) collective-permute-start(bf16[16,2048]{1,0:T(8,128)(2,1)S(1)} %get-tuple-element.38), channel_id=1, source_target_pairs={{0,3},{1,2},{2,1},{3,0},{4,7},{5,6},{6,5},{7,4},{8,11},{9,10},{10,... | collective-permute-start | bytes 196616 | tf_op jit(solution)/shard_map/ppermute | solution.py:160
  25.2 6.7 %collective-permute-start.10 = (bf16[16,2048]{1,0:T(8,128)(2,1)S(1)}, bf16[16,2048]{1,0:T(8,128)(2,1)S(1)}, u32[]{:S(2)}, u32[]{:S(2)}) collective-permute-start(bf16[16,2048]{1,0:T(8,128)(2,1)S(1)} %add_convert_fusion.2), channel_id=1, source_target_pairs={{0,9},{1,8},{2,11},{3,10},{4,13},{5,12},{6,15},{7,14},{8,1},{9,0},... | collective-permute-start | bytes 196616 | tf_op jit(solution)/shard_map/ppermute | solution.py:160
  28.2 4.1 %collective-permute-start.15 = (bf16[16,2048]{1,0:T(8,128)(2,1)S(1)}, bf16[16,2048]{1,0:T(8,128)(2,1)S(1)}, u32[]{:S(2)}, u32[]{:S(2)}) collective-permute-start(bf16[16,2048]{1,0:T(8,128)(2,1)S(1)} %get-tuple-element.39), channel_id=1, source_target_pairs={{0,3},{1,2},{2,1},{3,0},{4,7},{5,6},{6,5},{7,4},{8,11},{9,10},{10,... | collective-permute-start | bytes 196616 | tf_op jit(solution)/shard_map/ppermute | solution.py:160
  29.2 6.9 %collective-permute-start.12 = (bf16[16,2048]{1,0:T(8,128)(2,1)S(1)}, bf16[16,2048]{1,0:T(8,128)(2,1)S(1)}, u32[]{:S(2)}, u32[]{:S(2)}) collective-permute-start(bf16[16,2048]{1,0:T(8,128)(2,1)S(1)} %add_convert_fusion.1), channel_id=1, source_target_pairs={{0,12},{1,13},{2,14},{3,15},{4,8},{5,9},{6,10},{7,11},{8,4},{9,5},... | collective-permute-start | bytes 196616 | tf_op jit(solution)/shard_map/ppermute | solution.py:160
  31.0 7.2 %copy-start.2 = (bf16[16,4096]{1,0:T(8,128)(2,1)S(1)}, bf16[16,4096]{1,0:T(8,128)(2,1)}, u32[]{:S(2)}) copy-start(bf16[16,4096]{1,0:T(8,128)(2,1)} %core_ref.1) | copy-start | bytes 393220
  31.1 5.8 %collective-permute-start.14 = (bf16[16,2048]{1,0:T(8,128)(2,1)S(1)}, bf16[16,2048]{1,0:T(8,128)(2,1)S(1)}, u32[]{:S(2)}, u32[]{:S(2)}) collective-permute-start(bf16[16,2048]{1,0:T(8,128)(2,1)S(1)} %add_convert_fusion), channel_id=1, source_target_pairs={{0,5},{1,4},{2,7},{3,6},{4,1},{5,0},{6,3},{7,2},{8,13},{9,12},{10,... | collective-permute-start | bytes 196616 | tf_op jit(solution)/shard_map/ppermute | solution.py:160
  36.9 1.4 %collective-permute-start.16 = (f32[16,2048]{1,0:T(8,128)S(1)}, f32[16,2048]{1,0:T(8,128)S(1)}, u32[]{:S(2)}, u32[]{:S(2)}) collective-permute-start(f32[16,2048]{1,0:T(8,128)S(1)} %convert_add_fusion.mine_ref), channel_id=1, source_target_pairs={{0,1},{1,0},{2,3},{3,2},{4,5},{5,4},{6,7},{7,6},{8,9},{9,8},{10,11... | collective-permute-start | bytes 393224 | tf_op jit(solution)/shard_map/ppermute | solution.py:164

commit v8 on v7

--- a/solution.py
+++ b/solution.py
@@ -45,25 +45,19 @@
     rows_ref[...] = jnp.sum(chosen, axis=0, keepdims=True) + owner * held
 
 
-def row_table(place_ref, core_ref, own_ref, other_ref, held, owners):
+def row_table(core_ref, own_ref, other_ref, table_rows):
     low = core_ref[0] == 0
     rows = jnp.concatenate(
         [jnp.where(low, own_ref[...], other_ref[...]), jnp.where(low, other_ref[...], own_ref[...])], axis=1
     )
-    rows = lax.bitwise_xor(rows, place_ref[0] * held)
-    row = lax.broadcasted_iota(jnp.int32, (owners * held, rows.shape[1]), 0)
+    row = lax.broadcasted_iota(jnp.int32, (table_rows, rows.shape[1]), 0)
     return jnp.where(row == rows, 1.0, 0.0)
 
 
-def density_kernel(places, place_ref, core_ref, *refs):
-    piece_refs = refs[:len(places)]
-    own_ref, other_ref, left_ref, values_ref, out_ref, table, dense = refs[len(places):]
+def density_kernel(core_ref, table, own_ref, other_ref, left_ref, values_ref, out_ref, dense):
     batches, points, columns = values_ref.shape
     groups = columns // GO
-    held = piece_refs[0].shape[0]
-    for ref, k in zip(piece_refs, places):
-        table[k * held:(k + 1) * held, :] = ref[...]
-    pick = row_table(place_ref, core_ref, own_ref, other_ref, held, len(places)).T.astype(jnp.bfloat16)
+    pick = row_table(core_ref, own_ref, other_ref, table.shape[0]).T.astype(jnp.bfloat16)
     low = lax.broadcasted_iota(jnp.int32, (1, 1, 1, groups, 128), 4) < GO
     for j in range(table.shape[1] // 128):
         lanes = slice(j * 128, (j + 1) * 128)
@@ -85,13 +79,10 @@
         out_ref[t:t + 1, :] = jnp.sum(folded.T, axis=0, keepdims=True)
 
 
-def scatter_kernel(place_ref, core_ref, *refs):
-    mine_ref, far_ref, weight_ref, values_ref, left_t_ref, own_ref, other_ref = refs[:7]
-    out_refs = refs[7:-2]
-    high, rest = refs[-2:]
-    pieces = len(out_refs)
-    held = out_refs[0].shape[0]
-    put = row_table(place_ref, core_ref, own_ref, other_ref, held, pieces).astype(jnp.bfloat16)
+def scatter_kernel(
+    core_ref, mine_ref, far_ref, weight_ref, values_ref, left_t_ref, own_ref, other_ref, out_ref, high, rest
+):
+    put = row_table(core_ref, own_ref, other_ref, out_ref.shape[0]).astype(jnp.bfloat16)
     batches, points, columns = values_ref.shape
     groups = columns // GO
     kept = left_t_ref.shape[1]
@@ -115,12 +106,11 @@
                 top = both.astype(jnp.bfloat16)
                 high[at:at + 2 * groups, j * 128:(j + 1) * 128] = top
                 rest[at:at + 2 * groups, j * 128:(j + 1) * 128] = (both - top.astype(jnp.float32)).astype(jnp.bfloat16)
-    step = max(1, min(pieces, 128 // held))
-    for k in range(0, pieces, step):
-        some = put[k * held:(k + step) * held, :]
+    step = min(out_ref.shape[0], 128)
+    for at in range(0, out_ref.shape[0], step):
+        some = put[at:at + step, :]
         total = split_dot(some, high[...]) + split_dot(some, rest[...])
-        for i in range(step):
-            out_refs[k + i][...] = total[i * held:(i + 1) * held, :].astype(jnp.bfloat16)
+        out_ref[at:at + step, :] = total.astype(jnp.bfloat16)
 
 
 def finish_kernel(half_ref, mine_ref, other_ref, core_ref, out_ref):
@@ -146,37 +136,14 @@
     )
 
 
-def odd_bits(number, count):
-    parity = number & 1
-    for shift in range(1, (count - 1).bit_length()):
-        parity = parity ^ ((number >> shift) & 1)
-    return parity
-
-
-def swap(array, sizes, dz, dx):
-    rows_z, rows_x = sizes
-    turn = odd_bits(dz, rows_z) ^ odd_bits(dx, rows_x)
-    step = (dz * rows_x + dx) * 2 + turn
-    return lax.ppermute(array, ("batch", "pair", "orb"), [(i, i ^ step) for i in range(rows_z * rows_x * 2)])
-
-
 def swap_cores(array):
     return lax.ppermute(array, "orb", [(0, 1), (1, 0)])
 
 
-def add_all(terms):
-    total = terms[0]
-    for term in terms[1:]:
-        total = total + term
-    return total
-
-
 def per_device(basis_values, point_weights, slot_ids, fetch_rows, density_blocks, core_blocks):
-    rows_z, rows_x = lax.axis_size("batch"), lax.axis_size("pair")
-    z, x, core = lax.axis_index("batch"), lax.axis_index("pair"), lax.axis_index("orb")
-    sizes = (rows_z, rows_x)
-    half = core ^ odd_bits(z, rows_z) ^ odd_bits(x, rows_x)
-    owners = rows_z * rows_x
+    grid = ("batch", "pair")
+    owners = lax.axis_size(grid)
+    half = lax.axis_index("orb")
     batches, points, columns = basis_values.shape
     groups, own_groups = slot_ids.shape[1], slot_ids.shape[2]
     held, square = density_blocks.shape
@@ -194,24 +161,10 @@
     )(fetch_rows.reshape(owners, capacity), slot_ids.transpose(0, 2, 1).reshape(1, -1))
     other_rows = swap_cores(own_rows)
 
-    steps = list(range(rows_z // 2, rows_z)) + list(range(1, rows_z // 2))
-    side = list(range(1, rows_x))
-
+    half_at = half.reshape(1).astype(jnp.int32)
     mine = lax.dynamic_slice_in_dim(density_blocks, half * wide, wide, 1)
-    pieces = {0: mine}
-    for dx in side:
-        pieces[dx] = swap(mine, sizes, 0, dx)
-    for dz in steps[::-1]:
-        pieces[dz * rows_x] = swap(mine, sizes, dz, 0)
-    first, last = steps[0] * rows_x, (rows_z - 1) * rows_x
-    pieces[first], own_rows = lax.optimization_barrier((pieces[first], own_rows))
-    pieces[last], other_rows = lax.optimization_barrier((pieces[last], other_rows))
-    for dz in steps[rows_z // 2:] + steps[:rows_z // 2]:
-        for dx in side:
-            pieces[dz * rows_x + dx] = swap(pieces[dz * rows_x], sizes, 0, dx)
-    order = list(pieces)
-
-    half_at, _ = lax.optimization_barrier((half.reshape(1).astype(jnp.int32), pieces[last]))
+    table = lax.all_to_all(jnp.tile(mine, (owners, 1)), grid, split_axis=0, concat_axis=0, tiled=True)
+
     left, left_t = call(
         prepare_kernel,
         (
@@ -224,44 +177,28 @@
         moved=3 * batches * points * columns * 2,
     )(half_at, basis_values)
 
-    place = (z * rows_x + x).reshape(1).astype(jnp.int32)
-    core_at = core.reshape(1).astype(jnp.int32)
-
     partial = call(
-        functools.partial(density_kernel, order),
+        density_kernel,
         jax.ShapeDtypeStruct((batches, points), f32),
-        owners + 4,
-        scalars=2,
-        scratch=(pltpu.VMEM((table_rows, wide), bf16), pltpu.VMEM((batches, kept, columns), bf16)),
+        5,
+        scalars=1,
+        scratch=(pltpu.VMEM((batches, kept, columns), bf16),),
         flops=2 * batches * points * columns * kept,
         moved=2 * batches * points * columns * 2,
-    )(place, core_at, *[pieces[k] for k in order], own_rows, other_rows, left, basis_values)
+    )(half_at, table, own_rows, other_rows, left, basis_values)
     partial_other = swap_cores(partial)
 
     sums = call(
         scatter_kernel,
-        [jax.ShapeDtypeStruct((held, wide), bf16)] * owners,
+        jax.ShapeDtypeStruct((table_rows, wide), bf16),
         7,
-        scalars=2,
+        scalars=1,
         scratch=(pltpu.VMEM((entries, wide), bf16), pltpu.VMEM((entries, wide), bf16)),
         flops=2 * batches * points * columns * kept,
         moved=2 * batches * points * columns * 2,
-    )(place, core_at, partial, partial_other, point_weights, basis_values, left_t, own_rows, other_rows)
-
-    landed = []
-    own = sums[:rows_x]
-    for dz in steps:
-        joined = sums[dz * rows_x].astype(f32)
-        for dx in side:
-            joined = joined + swap(sums[dz * rows_x + dx], sizes, 0, dx).astype(f32)
-        joined = joined.astype(bf16)
-        if dz == steps[0]:
-            joined, *own = lax.optimization_barrier((joined, *own))
-        landed.append(swap(joined, sizes, dz, 0))
-    for dx in side:
-        landed.append(swap(own[dx], sizes, 0, dx))
-    landed.append(own[0])
-    total = add_all([term.astype(f32) for term in landed])
+    )(half_at, partial, partial_other, point_weights, basis_values, left_t, own_rows, other_rows)
+    landed = lax.all_to_all(sums, grid, split_axis=0, concat_axis=0, tiled=True)
+    total = jnp.sum(landed.reshape(owners, held, wide).astype(f32), axis=0)
     total_other = swap_cores(total)
     return call(
         finish_kernel, jax.ShapeDtypeStruct((held, square), f32), 3, scalars=1, moved=held * square * 12

time: 39.2 us -> 48.1 us (1.23)
  blocking collectives: 0 us -> 18.3 us
  starting transfers between devices: 19.9 us -> 7.53 us
  waiting for transfers between devices: 12 us -> 15.3 us
    ppermute x14 -> x0, starting transfers between devices: 19.4 us -> none  [swap(): lax.ppermute(array, ('batch', 'pair', 'orb'), [(i, i ^ step) for i in ran...]
    all_to_all x0 -> x1, blocking collectives: none -> 18.3 us  [per_device(): landed = lax.all_to_all(sums, grid, split_axis=0, concat_axis=0, tiled=True)]
    all_to_all x0 -> x1, waiting for transfers between devices: none -> 12.5 us  [per_device(): lax.all_to_all(jnp.tile(mine, (owners, 1)), grid, split_axis=0, concat_ax...]
    ppermute x14 -> x0, waiting for transfers between devices: 9.73 us -> none  [swap(): lax.ppermute(array, ('batch', 'pair', 'orb'), [(i, i ^ step) for i in ran...]
    all_to_all x0 -> x1, starting transfers between devices: none -> 7.38 us  [per_device(): lax.all_to_all(jnp.tile(mine, (owners, 1)), grid, split_axis=0, concat_ax...]
    unnamed x12, local copies, waits for them, and re-layouts: 2.74 us -> 1.51 us
    another operation x0 -> x1, local copies, waits for them, and re-layouts: none -> 0.85 us  [per_device(): jnp.tile(mine, (owners, 1))]
    ppermute x3, waiting for transfers between devices: 2.22 us -> 2.83 us  [swap_cores(): return lax.ppermute(array, 'orb', [(0, 1), (1, 0)])]
  transfers between devices with their start and end apart: 17 -> 4, of which waited for: 11 -> 4; matrix products, arithmetic and copies ran while one was open for 0% -> 0% of each run, Pallas kernels for 2% -> 2%
where the time goes in v8:
time: 48.1 us; the launch traced here: 47.8 us
  blocking collectives  18.3 us (38%)
  waiting for transfers between devices  15.3 us (32%)
  starting transfers between devices  7.53 us (16%)
  Pallas kernels  4.13 us (9%)
  local copies, waits for them, and re-layouts  2.45 us (5%)
    all_to_all x1, blocking collectives, per_device(): landed = lax.all_to_all(sums, grid, split_axis=0, concat_axis=0, tiled=True)  18.3 us
    all_to_all x1, waiting for transfers between devices, per_device(): lax.all_to_all(jnp.tile(mine, (owners, 1)), grid, split_axis=0, concat_ax...  12.5 us
    all_to_all x1, starting transfers between devices, per_device(): lax.all_to_all(jnp.tile(mine, (owners, 1)), grid, split_axis=0, concat_ax...  7.38 us
    ppermute x3, waiting for transfers between devices, swap_cores(): return lax.ppermute(array, 'orb', [(0, 1), (1, 0)])  2.83 us
    unnamed x12, local copies, waits for them, and re-layouts  1.51 us
    pallas_call x1, Pallas kernels, per_device(): call(scatter_kernel, jax.ShapeDtypeStruct((table_rows, wide), bf16), 7, s...  1.39 us
    pallas_call x1, Pallas kernels, per_device(): call(density_kernel, jax.ShapeDtypeStruct((batches, points), f32), 5, sca...  1.06 us
  transfers between devices with their start and end apart: 4, of which 4 were waited for; matrix products, arithmetic and copies ran while one was open for 0% of the time, Pallas kernels for 2%

profile of v8, /device:TPU:0, one launch (start us, length us, event | category | flops | bytes accessed | tf_op | source)
XLA Modules:
  0.0 47.8 jit_solution(2814085008481946649)
XLA Ops:
  0.0 0.0 copy-start
  0.0 0.0 copy-start.1
  0.0 0.9 %copy-done = bf16[16,4096]{1,0:T(8,128)(2,1)S(1)} copy-done((bf16[16,4096]{1,0:T(8,128)(2,1)S(1)}, bf16[16,4096]{1,0:T(8,128)(2,1)}, u32[]{:S(2)}) %copy-start) | copy-done | bytes 131096
  0.9 0.8 %tile.2 = bf16[8,16,2048]{2,1,0:T(8,128)(2,1)} broadcast(bf16[16,2048]{1,0:T(8,128)(2,1)S(1)} %constant_dynamic-slice_fusion), dimensions={1,2} | broadcast | bytes 589824 | tf_op jit(solution)/shard_map/tile | solution.py:166
  1.8 0.0 copy-start.5
  1.8 7.4 %all-to-all-start = ((bf16[8,16,2048]{2,1,0:T(8,128)(2,1)}), bf16[8,16,2048]{2,1,0:T(8,128)(2,1)S(1)}, u32[]{:S(2)}, u32[]{:S(2)}) async-start(bf16[8,16,2048]{2,1,0:T(8,128)(2,1)} %tile.2), calls=%async_computation | async-start | bytes 1048576 | tf_op jit(solution)/shard_map/all_to_all | solution.py:166
  9.1 0.0 copy-done.5
  9.2 0.0 copy-start.4
  9.2 0.1 reshape.22.slots_ref
  9.3 0.6 %copy-done.4 = s32[1,1,8,8]{3,2,1,0:T(8,128)S(1)} copy-done((s32[1,1,8,8]{3,2,1,0:T(8,128)S(1)}, s32[1,1,8,8]{3,2,1,0:T(8,128)}, u32[]{:S(2)}) %copy-start.4) | copy-done | bytes 280
  9.8 0.2 shard_map.64.own_ref
  10.0 0.0 collective-permute-start
  10.0 0.0 copy-done.1
  10.0 0.8 %shard_map.65 = (bf16[4,256,256]{2,1,0:T(8,128)(2,1)S(1)}, bf16[4,256,256]{2,1,0:T(8,128)(2,1)S(1)}) custom-call(s32[1]{0:T(128)} %bitcast.half_ref.core_ref, bf16[4,256,512]{2,1,0:T(8,128)(2,1)S(1)} %copy-done.1), custom_call_target="tpu_custom_call" | custom-call | flops 536870912 | bytes 3145728 | tf_op jit(solution)/shard_map/pallas_call | solution.py:168
  10.8 0.3 collective-permute-done.other_ref
  11.2 12.5 %all-to-all-done = bf16[8,16,2048]{2,1,0:T(8,128)(2,1)S(1)} async-done(((bf16[8,16,2048]{2,1,0:T(8,128)(2,1)}), bf16[8,16,2048]{2,1,0:T(8,128)(2,1)S(1)}, u32[]{:S(2)}, u32[]{:S(2)}) %all-to-all-start) | async-done | bytes 524320 | tf_op jit(solution)/shard_map/all_to_all | solution.py:166
  23.6 0.0 copy-start.3
  23.6 1.1 %shard_map.66.mine_ref = f32[4,256]{1,0:T(4,128)S(1)} custom-call(s32[1]{0:T(128)} %bitcast.half_ref.core_ref, bf16[128,2048]{1,0:T(8,128)(2,1)S(1)} %bitcast.5, s32[1,128]{1,0:T(1,128)S(1)} %shard_map.64.own_ref, s32[1,128]{1,0:T(1,128)S(1)} %collective-permute-done.other_ref, bf16[4,256,256]{2,1,0:T(8,128)(2,1)S(1)} %get-tuple-element.7.left_ref, ...), custom_call_target="tpu_custom_call" | custom-call | flops 268435456 | bytes 2097152 | tf_op jit(solution)/shard_map/pallas_call | solution.py:180
  24.7 0.1 collective-permute-start.1
  24.8 1.2 %collective-permute-done.1.far_ref = f32[4,256]{1,0:T(4,128)S(1)} collective-permute-done((f32[4,256]{1,0:T(4,128)S(1)}, f32[4,256]{1,0:T(4,128)S(1)}, u32[]{:S(2)}, u32[]{:S(2)}) %collective-permute-start.1) | collective-permute-done | bytes 4128 | tf_op jit(solution)/shard_map/ppermute | solution.py:140
  25.9 0.0 copy-done.3
  25.9 1.4 %shard_map.67 = bf16[128,2048]{1,0:T(8,128)(2,1)S(1)} custom-call(s32[1]{0:T(128)} %bitcast.half_ref.core_ref, f32[4,256]{1,0:T(4,128)S(1)} %shard_map.66.mine_ref, f32[4,256]{1,0:T(4,128)S(1)} %collective-permute-done.1.far_ref, f32[4,256]{1,0:T(4,128)S(1)} %copy-done.3, bf16[4,256,512]{2,1,0:T(8,128)(2,1)S(1)} %copy-done.1, ...), custom_call_target="tpu_custom_call" | custom-call | flops 268435456 | bytes 2097152 | tf_op jit(solution)/shard_map/pallas_call | solution.py:191
  27.3 18.3 %all_to_all.17 = bf16[8,16,2048]{2,1,0:T(8,128)(2,1)S(1)} all-to-all(bf16[8,16,2048]{2,1,0:T(8,128)(2,1)S(1)} %bitcast.6), channel_id=1, replica_groups=mesh['groups'=2,'batch'=4,'pair'=2,'orb'=2] {'batch','pair'}, dimensions={0} | all-to-all | bytes 1048576 | tf_op jit(solution)/shard_map/all_to_all | solution.py:200
  45.6 0.0 copy-start.2
  45.6 0.1 convert_reduce_fusion.mine_ref
  45.7 0.1 collective-permute-start.2
  45.7 1.3 %collective-permute-done.2.other_ref = f32[16,2048]{1,0:T(8,128)S(1)} collective-permute-done((f32[16,2048]{1,0:T(8,128)S(1)}, f32[16,2048]{1,0:T(8,128)S(1)}, u32[]{:S(2)}, u32[]{:S(2)}) %collective-permute-start.2) | collective-permute-done | bytes 131104 | tf_op jit(solution)/shard_map/ppermute | solution.py:140
  47.1 0.0 copy-done.2
  47.1 0.7 %shard_map.68 = f32[16,4096]{1,0:T(8,128)} custom-call(s32[1]{0:T(128)} %bitcast.half_ref.core_ref, f32[16,2048]{1,0:T(8,128)S(1)} %convert_reduce_fusion.mine_ref, f32[16,2048]{1,0:T(8,128)S(1)} %collective-permute-done.2.other_ref, bf16[16,4096]{1,0:T(8,128)(2,1)S(1)} %copy-done.2), custom_call_target="tpu_custom_call" | custom-call | bytes 786432 | tf_op jit(solution)/shard_map/pallas_call | solution.py:203
  (1 shorter events, 0.0 us)
Async XLA Ops:
  0.0 0.9 %copy-start = (bf16[16,4096]{1,0:T(8,128)(2,1)S(1)}, bf16[16,4096]{1,0:T(8,128)(2,1)}, u32[]{:S(2)}) copy-start(bf16[16,4096]{1,0:T(8,128)(2,1)} %param.10) | copy-start | bytes 393220
  0.0 10.0 %copy-start.1 = (bf16[4,256,512]{2,1,0:T(8,128)(2,1)S(1)}, bf16[4,256,512]{2,1,0:T(8,128)(2,1)}, u32[]{:S(2)}) copy-start(bf16[4,256,512]{2,1,0:T(8,128)(2,1)} %values_ref.5) | copy-start | bytes 3145732
  1.8 7.4 %copy-start.5 = (s32[4,8,4]{1,2,0:T(4,128)S(1)}, s32[4,8,4]{1,2,0:T(4,128)}, u32[]{:S(2)}) copy-start(s32[4,8,4]{1,2,0:T(4,128)} %param.8) | copy-start | bytes 1540
  1.8 21.9 %all-to-all-start = ((bf16[8,16,2048]{2,1,0:T(8,128)(2,1)}), bf16[8,16,2048]{2,1,0:T(8,128)(2,1)S(1)}, u32[]{:S(2)}, u32[]{:S(2)}) async-start(bf16[8,16,2048]{2,1,0:T(8,128)(2,1)} %tile.2), calls=%async_computation | async-start | bytes 1048576 | tf_op jit(solution)/shard_map/all_to_all | solution.py:166
  9.2 0.7 %copy-start.4 = (s32[1,1,8,8]{3,2,1,0:T(8,128)S(1)}, s32[1,1,8,8]{3,2,1,0:T(8,128)}, u32[]{:S(2)}) copy-start(s32[1,1,8,8]{3,2,1,0:T(8,128)} %param.9) | copy-start | bytes 772
  10.0 1.1 %collective-permute-start = (s32[1,128]{1,0:T(1,128)S(1)}, s32[1,128]{1,0:T(1,128)S(1)}, u32[]{:S(2)}, u32[]{:S(2)}) collective-permute-start(s32[1,128]{1,0:T(1,128)S(1)} %shard_map.64.own_ref), channel_id=1, source_target_pairs={{0,1},{1,0},{2,3},{3,2},{4,5},{5,4},{6,7},{7,6},{8,9},{9,8},{10,11... | collective-permute-start | bytes 1544 | tf_op jit(solution)/shard_map/ppermute | solution.py:140
  23.6 2.3 %copy-start.3 = (f32[4,256]{1,0:T(4,128)S(1)}, f32[4,256]{1,0:T(4,128)}, u32[]{:S(2)}) copy-start(f32[4,256]{1,0:T(4,128)} %weight_ref.1) | copy-start | bytes 12292
  24.7 1.2 %collective-permute-start.1 = (f32[4,256]{1,0:T(4,128)S(1)}, f32[4,256]{1,0:T(4,128)S(1)}, u32[]{:S(2)}, u32[]{:S(2)}) collective-permute-start(f32[4,256]{1,0:T(4,128)S(1)} %shard_map.66.mine_ref), channel_id=1, source_target_pairs={{0,1},{1,0},{2,3},{3,2},{4,5},{5,4},{6,7},{7,6},{8,9},{9,8},{10,11... | collective-permute-start | bytes 12296 | tf_op jit(solution)/shard_map/ppermute | solution.py:140
  45.6 1.5 %copy-start.2 = (bf16[16,4096]{1,0:T(8,128)(2,1)S(1)}, bf16[16,4096]{1,0:T(8,128)(2,1)}, u32[]{:S(2)}) copy-start(bf16[16,4096]{1,0:T(8,128)(2,1)} %core_ref.1) | copy-start | bytes 393220
  45.7 1.4 %collective-permute-start.2 = (f32[16,2048]{1,0:T(8,128)S(1)}, f32[16,2048]{1,0:T(8,128)S(1)}, u32[]{:S(2)}, u32[]{:S(2)}) collective-permute-start(f32[16,2048]{1,0:T(8,128)S(1)} %convert_reduce_fusion.mine_ref), channel_id=1, source_target_pairs={{0,1},{1,0},{2,3},{3,2},{4,5},{5,4},{6,7},{7,6},{8,9},{9,8},{10,11... | collective-permute-start | bytes 393224 | tf_op jit(solution)/shard_map/ppermute | solution.py:140

commit v9 on v8

--- a/solution.py
+++ b/solution.py
@@ -45,19 +45,35 @@
     rows_ref[...] = jnp.sum(chosen, axis=0, keepdims=True) + owner * held
 
 
-def row_table(core_ref, own_ref, other_ref, table_rows):
-    low = core_ref[0] == 0
+def row_table(stages, place_ref, core_ref, own_ref, other_ref, held):
+    first_core = core_ref[0] == 0
     rows = jnp.concatenate(
-        [jnp.where(low, own_ref[...], other_ref[...]), jnp.where(low, other_ref[...], own_ref[...])], axis=1
-    )
-    row = lax.broadcasted_iota(jnp.int32, (table_rows, rows.shape[1]), 0)
-    return jnp.where(row == rows, 1.0, 0.0)
-
-
-def density_kernel(core_ref, table, own_ref, other_ref, left_ref, values_ref, out_ref, dense):
+        [
+            jnp.where(first_core, own_ref[...], other_ref[...]),
+            jnp.where(first_core, other_ref[...], own_ref[...]),
+        ],
+        axis=1,
+    )
+    owner = lax.bitwise_xor(rows // held, place_ref[0])
+    at = rows % held
+    for i, steps in enumerate(stages):
+        here = [(owner // step) % 2 for step in steps]
+        at = at + jnp.where(first_core, here[0], here[1]) * (held << i)
+    row = lax.broadcasted_iota(jnp.int32, (held << len(stages), rows.shape[1]), 0)
+    return jnp.where(row == at, 1.0, 0.0)
+
+
+def density_kernel(stages, place_ref, core_ref, *refs):
+    piece_refs = refs[:-7]
+    own_ref, other_ref, left_ref, values_ref, out_ref, table, dense = refs[-7:]
     batches, points, columns = values_ref.shape
     groups = columns // GO
-    pick = row_table(core_ref, own_ref, other_ref, table.shape[0]).T.astype(jnp.bfloat16)
+    held = table.shape[0] >> len(stages)
+    at = 0
+    for ref in piece_refs:
+        table[at:at + ref.shape[0], :] = ref[...]
+        at += ref.shape[0]
+    pick = row_table(stages, place_ref, core_ref, own_ref, other_ref, held).T.astype(jnp.bfloat16)
     low = lax.broadcasted_iota(jnp.int32, (1, 1, 1, groups, 128), 4) < GO
     for j in range(table.shape[1] // 128):
         lanes = slice(j * 128, (j + 1) * 128)
@@ -79,10 +95,13 @@
         out_ref[t:t + 1, :] = jnp.sum(folded.T, axis=0, keepdims=True)
 
 
-def scatter_kernel(
-    core_ref, mine_ref, far_ref, weight_ref, values_ref, left_t_ref, own_ref, other_ref, out_ref, high, rest
-):
-    put = row_table(core_ref, own_ref, other_ref, out_ref.shape[0]).astype(jnp.bfloat16)
+def scatter_kernel(stages, place_ref, core_ref, *refs):
+    mine_ref, far_ref, weight_ref, values_ref, left_t_ref, own_ref, other_ref = refs[:7]
+    out_refs = refs[7:-2]
+    high, rest = refs[-2:]
+    part_rows = out_refs[0].shape[0]
+    held = len(out_refs) * part_rows >> len(stages)
+    put = row_table(stages, place_ref, core_ref, own_ref, other_ref, held).astype(jnp.bfloat16)
     batches, points, columns = values_ref.shape
     groups = columns // GO
     kept = left_t_ref.shape[1]
@@ -106,11 +125,14 @@
                 top = both.astype(jnp.bfloat16)
                 high[at:at + 2 * groups, j * 128:(j + 1) * 128] = top
                 rest[at:at + 2 * groups, j * 128:(j + 1) * 128] = (both - top.astype(jnp.float32)).astype(jnp.bfloat16)
-    step = min(out_ref.shape[0], 128)
-    for at in range(0, out_ref.shape[0], step):
+    step = min(put.shape[0], 128)
+    for at in range(0, put.shape[0], step):
         some = put[at:at + step, :]
-        total = split_dot(some, high[...]) + split_dot(some, rest[...])
-        out_ref[at:at + step, :] = total.astype(jnp.bfloat16)
+        total = (split_dot(some, high[...]) + split_dot(some, rest[...])).astype(jnp.bfloat16)
+        size = min(step, part_rows)
+        for i in range(0, step, size):
+            part, begin = divmod(at + i, part_rows)
+            out_refs[part][begin:begin + size, :] = total[i:i + size, :]
 
 
 def finish_kernel(half_ref, mine_ref, other_ref, core_ref, out_ref):
@@ -136,14 +158,19 @@
     )
 
 
+def swap(array, owners, steps):
+    pairs = [(i * 2 + core, (i ^ steps[core]) * 2 + core) for i in range(owners) for core in range(2)]
+    return lax.ppermute(array, ("batch", "pair", "orb"), pairs)
+
+
 def swap_cores(array):
     return lax.ppermute(array, "orb", [(0, 1), (1, 0)])
 
 
 def per_device(basis_values, point_weights, slot_ids, fetch_rows, density_blocks, core_blocks):
-    grid = ("batch", "pair")
-    owners = lax.axis_size(grid)
-    half = lax.axis_index("orb")
+    rows_z, rows_x = lax.axis_size("batch"), lax.axis_size("pair")
+    z, x, core = lax.axis_index("batch"), lax.axis_index("pair"), lax.axis_index("orb")
+    owners = rows_z * rows_x
     batches, points, columns = basis_values.shape
     groups, own_groups = slot_ids.shape[1], slot_ids.shape[2]
     held, square = density_blocks.shape
@@ -161,10 +188,24 @@
     )(fetch_rows.reshape(owners, capacity), slot_ids.transpose(0, 2, 1).reshape(1, -1))
     other_rows = swap_cores(own_rows)
 
-    half_at = half.reshape(1).astype(jnp.int32)
-    mine = lax.dynamic_slice_in_dim(density_blocks, half * wide, wide, 1)
-    table = lax.all_to_all(jnp.tile(mine, (owners, 1)), grid, split_axis=0, concat_axis=0, tiled=True)
-
+    along_z = [rows_x << i for i in reversed(range(rows_z.bit_length() - 1))]
+    along_x = [1 << i for i in reversed(range(rows_x.bit_length() - 1))]
+    stages = list(zip(along_z + along_x, along_z[:-1] + along_x + along_z[-1:]))
+
+    mine = lax.dynamic_slice_in_dim(density_blocks, core * wide, wide, 1)
+    pieces = [mine, swap(mine, owners, stages[0])]
+    early = swap(mine, owners, stages[-1])
+    early, pieces[-1], own_rows = lax.optimization_barrier((early, pieces[-1], own_rows))
+    for steps in stages[1:-1]:
+        pieces.append(swap(jnp.concatenate(pieces, axis=0), owners, steps))
+    middle = pieces[1:-1]
+    middle = middle[0] if len(middle) == 1 else jnp.concatenate(middle, axis=0)
+    middle = swap(middle, owners, stages[-1])
+    pieces[-1], middle, other_rows = lax.optimization_barrier((pieces[-1], middle, other_rows))
+    pieces = pieces + [early, middle, swap(pieces[-1], owners, stages[-1])]
+
+    core_at = core.reshape(1).astype(jnp.int32)
+    half_at, _ = lax.optimization_barrier((core_at, pieces[-4]))
     left, left_t = call(
         prepare_kernel,
         (
@@ -177,32 +218,39 @@
         moved=3 * batches * points * columns * 2,
     )(half_at, basis_values)
 
+    place = (z * rows_x + x).reshape(1).astype(jnp.int32)
     partial = call(
-        density_kernel,
+        functools.partial(density_kernel, stages),
         jax.ShapeDtypeStruct((batches, points), f32),
-        5,
-        scalars=1,
-        scratch=(pltpu.VMEM((batches, kept, columns), bf16),),
+        len(pieces) + 4,
+        scalars=2,
+        scratch=(pltpu.VMEM((table_rows, wide), bf16), pltpu.VMEM((batches, kept, columns), bf16)),
         flops=2 * batches * points * columns * kept,
         moved=2 * batches * points * columns * 2,
-    )(half_at, table, own_rows, other_rows, left, basis_values)
+    )(place, core_at, *pieces, own_rows, other_rows, left, basis_values)
     partial_other = swap_cores(partial)
 
-    sums = call(
-        scatter_kernel,
-        jax.ShapeDtypeStruct((table_rows, wide), bf16),
+    quarter = jax.ShapeDtypeStruct((table_rows // 4, wide), bf16)
+    none, upper, last, both = call(
+        functools.partial(scatter_kernel, stages),
+        [quarter] * 4,
         7,
-        scalars=1,
+        scalars=2,
         scratch=(pltpu.VMEM((entries, wide), bf16), pltpu.VMEM((entries, wide), bf16)),
         flops=2 * batches * points * columns * kept,
         moved=2 * batches * points * columns * 2,
-    )(half_at, partial, partial_other, point_weights, basis_values, left_t, own_rows, other_rows)
-    landed = lax.all_to_all(sums, grid, split_axis=0, concat_axis=0, tiled=True)
-    total = jnp.sum(landed.reshape(owners, held, wide).astype(f32), axis=0)
+    )(place, core_at, partial, partial_other, point_weights, basis_values, left_t, own_rows, other_rows)
+
+    upper = upper.astype(f32) + swap(both, owners, stages[-1]).astype(f32)
+    total = none.astype(f32) + swap(last, owners, stages[-1]).astype(f32)
+    total = total + swap(upper.astype(bf16), owners, stages[-2]).astype(f32)
+    for steps in reversed(stages[:-2]):
+        rows = total.shape[0] // 2
+        total = total[:rows] + swap(total[rows:].astype(bf16), owners, steps).astype(f32)
     total_other = swap_cores(total)
     return call(
         finish_kernel, jax.ShapeDtypeStruct((held, square), f32), 3, scalars=1, moved=held * square * 12
-    )(half_at, total, total_other, core_blocks)
+    )(core_at, total, total_other, core_blocks)
 
 
 def solution(mesh):

time: 48.1 us -> 42.4 us (0.88)
  blocking collectives: 18.3 us -> 0 us
  starting transfers between devices: 7.53 us -> 15 us
  waiting for transfers between devices: 15.3 us -> 19.9 us
    all_to_all x1 -> x0, blocking collectives: 18.3 us -> none  [per_device(): landed = lax.all_to_all(sums, grid, split_axis=0, concat_axis=0, tiled=True)]
    ppermute x0 -> x9, waiting for transfers between devices: none -> 16.3 us  [swap(): return lax.ppermute(array, ('batch', 'pair', 'orb'), pairs)]
    ppermute x0 -> x9, starting transfers between devices: none -> 14.9 us  [swap(): return lax.ppermute(array, ('batch', 'pair', 'orb'), pairs)]
    all_to_all x1 -> x0, waiting for transfers between devices: 12.5 us -> none  [per_device(): lax.all_to_all(jnp.tile(mine, (owners, 1)), grid, split_axis=0, concat_ax...]
    all_to_all x1 -> x0, starting transfers between devices: 7.38 us -> none  [per_device(): lax.all_to_all(jnp.tile(mine, (owners, 1)), grid, split_axis=0, concat_ax...]
    unnamed x12 -> x14, local copies, waits for them, and re-layouts: 1.51 us -> 2.74 us
    another operation x1 -> x0, local copies, waits for them, and re-layouts: 0.85 us -> none  [per_device(): jnp.tile(mine, (owners, 1))]
    ppermute x3, waiting for transfers between devices: 2.83 us -> 3.61 us  [swap_cores(): return lax.ppermute(array, 'orb', [(0, 1), (1, 0)])]
  transfers between devices with their start and end apart: 4 -> 12, of which waited for: 4 -> 11; matrix products, arithmetic and copies ran while one was open for 0% -> 0% of each run, Pallas kernels for 2% -> 2%
where the time goes in v9:
time: 42.4 us; the launch traced here: 42.2 us
  waiting for transfers between devices  19.9 us (47%)
  starting transfers between devices  15 us (35%)
  Pallas kernels  4.2 us (10%)
  local copies, waits for them, and re-layouts  2.84 us (7%)
    ppermute x9, waiting for transfers between devices, swap(): return lax.ppermute(array, ('batch', 'pair', 'orb'), pairs)  16.3 us
    ppermute x9, starting transfers between devices, swap(): return lax.ppermute(array, ('batch', 'pair', 'orb'), pairs)  14.9 us
    ppermute x3, waiting for transfers between devices, swap_cores(): return lax.ppermute(array, 'orb', [(0, 1), (1, 0)])  3.61 us
    unnamed x14, local copies, waits for them, and re-layouts  2.74 us
    pallas_call x1, Pallas kernels, per_device(): call(functools.partial(scatter_kernel, stages), [quarter] * 4, 7, scalars...  1.4 us
    pallas_call x1, Pallas kernels, per_device(): call(functools.partial(density_kernel, stages), jax.ShapeDtypeStruct((bat...  1.12 us
  transfers between devices with their start and end apart: 12, of which 11 were waited for; matrix products, arithmetic and copies ran while one was open for 0% of the time, Pallas kernels for 2%

profile of v9, /device:TPU:0, one launch (start us, length us, event | category | flops | bytes accessed | tf_op | source)
XLA Modules:
  0.0 42.2 jit_solution(14240447111933089980)
XLA Ops:
  0.0 0.0 copy-start
  0.0 0.9 %copy-done = bf16[16,4096]{1,0:T(8,128)(2,1)S(1)} copy-done((bf16[16,4096]{1,0:T(8,128)(2,1)S(1)}, bf16[16,4096]{1,0:T(8,128)(2,1)}, u32[]{:S(2)}) %copy-start) | copy-done | bytes 131096
  0.9 0.0 copy-start.6
  0.9 4.1 %collective-permute-start.1 = (bf16[16,2048]{1,0:T(8,128)(2,1)S(1)}, bf16[16,2048]{1,0:T(8,128)(2,1)S(1)}, u32[]{:S(2)}, u32[]{:S(2)}) collective-permute-start(bf16[16,2048]{1,0:T(8,128)(2,1)S(1)} %constant_dynamic-slice_fusion.refs_0_), channel_id=1, source_target_pairs={{0,8},{1,9},{2,10},{3,11},{4,12},{5,13},{6,14},{7,15},{8,0},{9,1},... | collective-permute-start | bytes 196616 | tf_op jit(solution)/shard_map/ppermute | solution.py:163
  5.0 1.5 %collective-permute-start = (bf16[16,2048]{1,0:T(8,128)(2,1)S(1)}, bf16[16,2048]{1,0:T(8,128)(2,1)S(1)}, u32[]{:S(2)}, u32[]{:S(2)}) collective-permute-start(bf16[16,2048]{1,0:T(8,128)(2,1)S(1)} %constant_dynamic-slice_fusion.refs_0_), channel_id=1, source_target_pairs={{0,2},{1,5},{2,0},{3,7},{4,6},{5,1},{6,4},{7,3},{8,10},{9,13},{10,... | collective-permute-start | bytes 196616 | tf_op jit(solution)/shard_map/ppermute | solution.py:163
  6.5 0.0 copy-done.6
  6.5 0.0 copy-start.5
  6.5 0.1 reshape.15.slots_ref
  6.6 0.6 %copy-done.5 = s32[1,1,8,8]{3,2,1,0:T(8,128)S(1)} copy-done((s32[1,1,8,8]{3,2,1,0:T(8,128)S(1)}, s32[1,1,8,8]{3,2,1,0:T(8,128)}, u32[]{:S(2)}) %copy-start.5) | copy-done | bytes 280
  7.2 0.2 shard_map.64.refs_6_.refs_5_
  7.4 0.7 %collective-permute-done.1.refs_1_ = bf16[16,2048]{1,0:T(8,128)(2,1)S(1)} collective-permute-done((bf16[16,2048]{1,0:T(8,128)(2,1)S(1)}, bf16[16,2048]{1,0:T(8,128)(2,1)S(1)}, u32[]{:S(2)}, u32[]{:S(2)}) %collective-permute-start.1) | collective-permute-done | bytes 65568 | tf_op jit(solution)/shard_map/ppermute | solution.py:163
  8.1 1.2 %collective-permute-done.refs_3_ = bf16[16,2048]{1,0:T(8,128)(2,1)S(1)} collective-permute-done((bf16[16,2048]{1,0:T(8,128)(2,1)S(1)}, bf16[16,2048]{1,0:T(8,128)(2,1)S(1)}, u32[]{:S(2)}, u32[]{:S(2)}) %collective-permute-start) | collective-permute-done | bytes 65568 | tf_op jit(solution)/shard_map/ppermute | solution.py:163
  9.3 1.6 %collective-permute-start.2 = (bf16[32,2048]{1,0:T(8,128)(2,1)S(1)}, bf16[32,2048]{1,0:T(8,128)(2,1)S(1)}, u32[]{:S(2)}, u32[]{:S(2)}) collective-permute-start(bf16[32,2048]{1,0:T(8,128)(2,1)S(1)} %pad_maximum_fusion), channel_id=1, source_target_pairs={{0,4},{1,3},{2,6},{3,1},{4,0},{5,7},{6,2},{7,5},{8,12},{9,11},{10,... | collective-permute-start | bytes 393224 | tf_op jit(solution)/shard_map/ppermute | solution.py:163
  10.9 1.5 %collective-permute-start.3 = (bf16[16,2048]{1,0:T(8,128)(2,1)S(1)}, bf16[16,2048]{1,0:T(8,128)(2,1)S(1)}, u32[]{:S(2)}, u32[]{:S(2)}) collective-permute-start(bf16[16,2048]{1,0:T(8,128)(2,1)S(1)} %collective-permute-done.1.refs_1_), channel_id=1, source_target_pairs={{0,2},{1,5},{2,0},{3,7},{4,6},{5,1},{6,4},{7,3},{8,10},{9,13},{10,... | collective-permute-start | bytes 196616 | tf_op jit(solution)/shard_map/ppermute | solution.py:163
  12.4 0.0 collective-permute-start.4
  12.4 1.1 %collective-permute-done.4.refs_7_.refs_6_ = s32[1,128]{1,0:T(1,128)S(1)} collective-permute-done((s32[1,128]{1,0:T(1,128)S(1)}, s32[1,128]{1,0:T(1,128)S(1)}, u32[]{:S(2)}, u32[]{:S(2)}) %collective-permute-start.4) | collective-permute-done | bytes 544 | tf_op jit(solution)/shard_map/ppermute | solution.py:167
  13.5 1.7 %collective-permute-done.3.refs_4_ = bf16[16,2048]{1,0:T(8,128)(2,1)S(1)} collective-permute-done((bf16[16,2048]{1,0:T(8,128)(2,1)S(1)}, bf16[16,2048]{1,0:T(8,128)(2,1)S(1)}, u32[]{:S(2)}, u32[]{:S(2)}) %collective-permute-start.3) | collective-permute-done | bytes 65568 | tf_op jit(solution)/shard_map/ppermute | solution.py:163
  15.2 0.0 collective-permute-done.2.refs_2_
  15.2 1.5 %collective-permute-start.5 = (bf16[32,2048]{1,0:T(8,128)(2,1)S(1)}, bf16[32,2048]{1,0:T(8,128)(2,1)S(1)}, u32[]{:S(2)}, u32[]{:S(2)}) collective-permute-start(bf16[32,2048]{1,0:T(8,128)(2,1)S(1)} %collective-permute-done.2.refs_2_), channel_id=1, source_target_pairs={{0,2},{1,5},{2,0},{3,7},{4,6},{5,1},{6,4},{7,3},{8,10},{9,13},{10,... | collective-permute-start | bytes 393224 | tf_op jit(solution)/shard_map/ppermute | solution.py:163
  16.7 0.0 copy-start.1
  16.7 1.2 %copy-done.1 = bf16[4,256,512]{2,1,0:T(8,128)(2,1)S(1)} copy-done((bf16[4,256,512]{2,1,0:T(8,128)(2,1)S(1)}, bf16[4,256,512]{2,1,0:T(8,128)(2,1)}, u32[]{:S(2)}) %copy-start.1) | copy-done | bytes 1048600
  17.9 0.0 copy-start.2
  17.9 0.8 %shard_map.65 = (bf16[4,256,256]{2,1,0:T(8,128)(2,1)S(1)}, bf16[4,256,256]{2,1,0:T(8,128)(2,1)S(1)}) custom-call(s32[1]{0:T(128)} %bitcast.half_ref.core_ref, bf16[4,256,512]{2,1,0:T(8,128)(2,1)S(1)} %copy-done.1), custom_call_target="tpu_custom_call" | custom-call | flops 536870912 | bytes 3145728 | tf_op jit(solution)/shard_map/pallas_call | solution.py:209
  18.7 1.5 %collective-permute-done.5.refs_5_ = bf16[32,2048]{1,0:T(8,128)(2,1)S(1)} collective-permute-done((bf16[32,2048]{1,0:T(8,128)(2,1)S(1)}, bf16[32,2048]{1,0:T(8,128)(2,1)S(1)}, u32[]{:S(2)}, u32[]{:S(2)}) %collective-permute-start.5) | collective-permute-done | bytes 131104 | tf_op jit(solution)/shard_map/ppermute | solution.py:163
  20.2 0.0 copy-done.2
  20.2 0.0 copy-start.4
  20.2 1.1 %shard_map.66.refs_0_ = f32[4,256]{1,0:T(4,128)S(1)} custom-call(s32[1]{0:T(128)} %bitcast.1.place_ref, s32[1]{0:T(128)} %bitcast.half_ref.core_ref, bf16[16,2048]{1,0:T(8,128)(2,1)S(1)} %constant_dynamic-slice_fusion.refs_0_, bf16[16,2048]{1,0:T(8,128)(2,1)S(1)} %collective-permute-done.1.refs_1_, bf16[32,2048]{1,0:T(8,128)(2,1)S(1)} %collective-permute-done.2.refs_2_, ...), custom_call_target="tpu_custom_call" | custom-call | flops 268435456 | bytes 2097152 | tf_op jit(solution)/shard_map/pallas_call | solution.py:222
  21.3 0.1 collective-permute-start.6
  21.4 1.2 %collective-permute-done.6.refs_1_ = f32[4,256]{1,0:T(4,128)S(1)} collective-permute-done((f32[4,256]{1,0:T(4,128)S(1)}, f32[4,256]{1,0:T(4,128)S(1)}, u32[]{:S(2)}, u32[]{:S(2)}) %collective-permute-start.6) | collective-permute-done | bytes 4128 | tf_op jit(solution)/shard_map/ppermute | solution.py:167
  22.5 0.0 copy-done.4
  22.5 1.4 %shard_map.67 = (bf16[32,2048]{1,0:T(8,128)(2,1)S(1)}, bf16[32,2048]{1,0:T(8,128)(2,1)S(1)}, bf16[32,2048]{1,0:T(8,128)(2,1)S(1)}, bf16[32,2048]{1,0:T(8,128)(2,1)S(1)}) custom-call(s32[1]{0:T(128)} %bitcast.1.place_ref, s32[1]{0:T(128)} %bitcast.half_ref.core_ref, f32[4,256]{1,0:T(4,128)S(1)} %shard_map.66.refs_0_, ...), custom_call_target="tpu_custom_call" | custom-call | flops 268435456 | bytes 2097152 | tf_op jit(solution)/shard_map/pallas_call | solution.py:234
  23.9 1.6 %collective-permute-start.8 = (bf16[32,2048]{1,0:T(8,128)(2,1)S(1)}, bf16[32,2048]{1,0:T(8,128)(2,1)S(1)}, u32[]{:S(2)}, u32[]{:S(2)}) collective-permute-start(bf16[32,2048]{1,0:T(8,128)(2,1)S(1)} %get-tuple-element.30), channel_id=1, source_target_pairs={{0,2},{1,5},{2,0},{3,7},{4,6},{5,1},{6,4},{7,3},{8,10},{9,13},{10,... | collective-permute-start | bytes 393224 | tf_op jit(solution)/shard_map/ppermute | solution.py:163
  25.5 0.5 %collective-permute-start.7 = (bf16[32,2048]{1,0:T(8,128)(2,1)S(1)}, bf16[32,2048]{1,0:T(8,128)(2,1)S(1)}, u32[]{:S(2)}, u32[]{:S(2)}) collective-permute-start(bf16[32,2048]{1,0:T(8,128)(2,1)S(1)} %get-tuple-element.28), channel_id=1, source_target_pairs={{0,2},{1,5},{2,0},{3,7},{4,6},{5,1},{6,4},{7,3},{8,10},{9,13},{10,... | collective-permute-start | bytes 393224 | tf_op jit(solution)/shard_map/ppermute | solution.py:163
  26.0 2.9 %collective-permute-done.8 = bf16[32,2048]{1,0:T(8,128)(2,1)S(1)} collective-permute-done((bf16[32,2048]{1,0:T(8,128)(2,1)S(1)}, bf16[32,2048]{1,0:T(8,128)(2,1)S(1)}, u32[]{:S(2)}, u32[]{:S(2)}) %collective-permute-start.8) | collective-permute-done | bytes 131104 | tf_op jit(solution)/shard_map/ppermute | solution.py:163
  29.0 0.8 %collective-permute-start.9 = (bf16[32,2048]{1,0:T(8,128)(2,1)S(1)}, bf16[32,2048]{1,0:T(8,128)(2,1)S(1)}, u32[]{:S(2)}, u32[]{:S(2)}) collective-permute-start(bf16[32,2048]{1,0:T(8,128)(2,1)S(1)} %add_convert_fusion), channel_id=1, source_target_pairs={{0,4},{1,3},{2,6},{3,1},{4,0},{5,7},{6,2},{7,5},{8,12},{9,11},{10,... | collective-permute-start | bytes 393224 | tf_op jit(solution)/shard_map/ppermute | solution.py:163
  29.8 0.7 %collective-permute-done.7 = bf16[32,2048]{1,0:T(8,128)(2,1)S(1)} collective-permute-done((bf16[32,2048]{1,0:T(8,128)(2,1)S(1)}, bf16[32,2048]{1,0:T(8,128)(2,1)S(1)}, u32[]{:S(2)}, u32[]{:S(2)}) %collective-permute-start.7) | collective-permute-done | bytes 131104 | tf_op jit(solution)/shard_map/ppermute | solution.py:163
  30.5 3.6 %collective-permute-done.9 = bf16[32,2048]{1,0:T(8,128)(2,1)S(1)} collective-permute-done((bf16[32,2048]{1,0:T(8,128)(2,1)S(1)}, bf16[32,2048]{1,0:T(8,128)(2,1)S(1)}, u32[]{:S(2)}, u32[]{:S(2)}) %collective-permute-start.9) | collective-permute-done | bytes 131104 | tf_op jit(solution)/shard_map/ppermute | solution.py:163
  34.1 0.0 copy-start.3
  34.1 1.8 %collective-permute-start.10 = (bf16[16,2048]{1,0:T(8,128)(2,1)S(1)}, bf16[16,2048]{1,0:T(8,128)(2,1)S(1)}, u32[]{:S(2)}, u32[]{:S(2)}) collective-permute-start(bf16[16,2048]{1,0:T(8,128)(2,1)S(1)} %slice.13), channel_id=1, source_target_pairs={{0,8},{1,9},{2,10},{3,11},{4,12},{5,13},{6,14},{7,15},{8,0},{9,1},... | collective-permute-start | bytes 196616 | tf_op jit(solution)/shard_map/ppermute | solution.py:163
  36.0 4.1 %collective-permute-done.10 = bf16[16,2048]{1,0:T(8,128)(2,1)S(1)} collective-permute-done((bf16[16,2048]{1,0:T(8,128)(2,1)S(1)}, bf16[16,2048]{1,0:T(8,128)(2,1)S(1)}, u32[]{:S(2)}, u32[]{:S(2)}) %collective-permute-start.10) | collective-permute-done | bytes 65568 | tf_op jit(solution)/shard_map/ppermute | solution.py:163
  40.1 0.1 collective-permute-start.11
  40.2 1.3 %collective-permute-done.11.other_ref = f32[16,2048]{1,0:T(8,128)S(1)} collective-permute-done((f32[16,2048]{1,0:T(8,128)S(1)}, f32[16,2048]{1,0:T(8,128)S(1)}, u32[]{:S(2)}, u32[]{:S(2)}) %collective-permute-start.11) | collective-permute-done | bytes 131104 | tf_op jit(solution)/shard_map/ppermute | solution.py:167
  41.5 0.0 copy-done.3
  41.5 0.7 %shard_map.68 = f32[16,4096]{1,0:T(8,128)} custom-call(s32[1]{0:T(128)} %bitcast.half_ref.core_ref, f32[16,2048]{1,0:T(8,128)S(1)} %slice_add_fusion.mine_ref, f32[16,2048]{1,0:T(8,128)S(1)} %collective-permute-done.11.other_ref, bf16[16,4096]{1,0:T(8,128)(2,1)S(1)} %copy-done.3), custom_call_target="tpu_custom_call" | custom-call | bytes 786432 | tf_op jit(solution)/shard_map/pallas_call | solution.py:251
  (6 shorter events, 0.1 us)
Async XLA Ops:
  0.0 0.9 %copy-start = (bf16[16,4096]{1,0:T(8,128)(2,1)S(1)}, bf16[16,4096]{1,0:T(8,128)(2,1)}, u32[]{:S(2)}) copy-start(bf16[16,4096]{1,0:T(8,128)(2,1)} %param.10) | copy-start | bytes 393220
  0.9 5.6 %copy-start.6 = (s32[4,8,4]{1,2,0:T(4,128)S(1)}, s32[4,8,4]{1,2,0:T(4,128)}, u32[]{:S(2)}) copy-start(s32[4,8,4]{1,2,0:T(4,128)} %param.8) | copy-start | bytes 1540
  0.9 7.2 %collective-permute-start.1 = (bf16[16,2048]{1,0:T(8,128)(2,1)S(1)}, bf16[16,2048]{1,0:T(8,128)(2,1)S(1)}, u32[]{:S(2)}, u32[]{:S(2)}) collective-permute-start(bf16[16,2048]{1,0:T(8,128)(2,1)S(1)} %constant_dynamic-slice_fusion.refs_0_), channel_id=1, source_target_pairs={{0,8},{1,9},{2,10},{3,11},{4,12},{5,13},{6,14},{7,15},{8,0},{9,1},... | collective-permute-start | bytes 196616 | tf_op jit(solution)/shard_map/ppermute | solution.py:163
  5.0 4.3 %collective-permute-start = (bf16[16,2048]{1,0:T(8,128)(2,1)S(1)}, bf16[16,2048]{1,0:T(8,128)(2,1)S(1)}, u32[]{:S(2)}, u32[]{:S(2)}) collective-permute-start(bf16[16,2048]{1,0:T(8,128)(2,1)S(1)} %constant_dynamic-slice_fusion.refs_0_), channel_id=1, source_target_pairs={{0,2},{1,5},{2,0},{3,7},{4,6},{5,1},{6,4},{7,3},{8,10},{9,13},{10,... | collective-permute-start | bytes 196616 | tf_op jit(solution)/shard_map/ppermute | solution.py:163
  6.5 0.7 %copy-start.5 = (s32[1,1,8,8]{3,2,1,0:T(8,128)S(1)}, s32[1,1,8,8]{3,2,1,0:T(8,128)}, u32[]{:S(2)}) copy-start(s32[1,1,8,8]{3,2,1,0:T(8,128)} %param.9) | copy-start | bytes 772
  9.3 5.9 %collective-permute-start.2 = (bf16[32,2048]{1,0:T(8,128)(2,1)S(1)}, bf16[32,2048]{1,0:T(8,128)(2,1)S(1)}, u32[]{:S(2)}, u32[]{:S(2)}) collective-permute-start(bf16[32,2048]{1,0:T(8,128)(2,1)S(1)} %pad_maximum_fusion), channel_id=1, source_target_pairs={{0,4},{1,3},{2,6},{3,1},{4,0},{5,7},{6,2},{7,5},{8,12},{9,11},{10,... | collective-permute-start | bytes 393224 | tf_op jit(solution)/shard_map/ppermute | solution.py:163
  10.9 4.3 %collective-permute-start.3 = (bf16[16,2048]{1,0:T(8,128)(2,1)S(1)}, bf16[16,2048]{1,0:T(8,128)(2,1)S(1)}, u32[]{:S(2)}, u32[]{:S(2)}) collective-permute-start(bf16[16,2048]{1,0:T(8,128)(2,1)S(1)} %collective-permute-done.1.refs_1_), channel_id=1, source_target_pairs={{0,2},{1,5},{2,0},{3,7},{4,6},{5,1},{6,4},{7,3},{8,10},{9,13},{10,... | collective-permute-start | bytes 196616 | tf_op jit(solution)/shard_map/ppermute | solution.py:163
  12.4 1.1 %collective-permute-start.4 = (s32[1,128]{1,0:T(1,128)S(1)}, s32[1,128]{1,0:T(1,128)S(1)}, u32[]{:S(2)}, u32[]{:S(2)}) collective-permute-start(s32[1,128]{1,0:T(1,128)S(1)} %shard_map.64.refs_6_.refs_5_), channel_id=1, source_target_pairs={{0,1},{1,0},{2,3},{3,2},{4,5},{5,4},{6,7},{7,6},{8,9},{9,8},{10,11... | collective-permute-start | bytes 1544 | tf_op jit(solution)/shard_map/ppermute | solution.py:167
  15.2 5.0 %collective-permute-start.5 = (bf16[32,2048]{1,0:T(8,128)(2,1)S(1)}, bf16[32,2048]{1,0:T(8,128)(2,1)S(1)}, u32[]{:S(2)}, u32[]{:S(2)}) collective-permute-start(bf16[32,2048]{1,0:T(8,128)(2,1)S(1)} %collective-permute-done.2.refs_2_), channel_id=1, source_target_pairs={{0,2},{1,5},{2,0},{3,7},{4,6},{5,1},{6,4},{7,3},{8,10},{9,13},{10,... | collective-permute-start | bytes 393224 | tf_op jit(solution)/shard_map/ppermute | solution.py:163
  16.7 1.2 %copy-start.1 = (bf16[4,256,512]{2,1,0:T(8,128)(2,1)S(1)}, bf16[4,256,512]{2,1,0:T(8,128)(2,1)}, u32[]{:S(2)}) copy-start(bf16[4,256,512]{2,1,0:T(8,128)(2,1)} %refs_3_.1) | copy-start | bytes 3145732
  17.9 2.3 %copy-start.2 = (bf16[4,256,512]{2,1,0:T(8,128)(2,1)S(1)}, bf16[4,256,512]{2,1,0:T(8,128)(2,1)}, u32[]{:S(2)}) copy-start(bf16[4,256,512]{2,1,0:T(8,128)(2,1)} %refs_3_.1) | copy-start | bytes 3145732
  20.2 2.4 %copy-start.4 = (f32[4,256]{1,0:T(4,128)S(1)}, f32[4,256]{1,0:T(4,128)}, u32[]{:S(2)}) copy-start(f32[4,256]{1,0:T(4,128)} %refs_2_.1) | copy-start | bytes 12292
  21.3 1.2 %collective-permute-start.6 = (f32[4,256]{1,0:T(4,128)S(1)}, f32[4,256]{1,0:T(4,128)S(1)}, u32[]{:S(2)}, u32[]{:S(2)}) collective-permute-start(f32[4,256]{1,0:T(4,128)S(1)} %shard_map.66.refs_0_), channel_id=1, source_target_pairs={{0,1},{1,0},{2,3},{3,2},{4,5},{5,4},{6,7},{7,6},{8,9},{9,8},{10,11... | collective-permute-start | bytes 12296 | tf_op jit(solution)/shard_map/ppermute | solution.py:167
  23.9 5.0 %collective-permute-start.8 = (bf16[32,2048]{1,0:T(8,128)(2,1)S(1)}, bf16[32,2048]{1,0:T(8,128)(2,1)S(1)}, u32[]{:S(2)}, u32[]{:S(2)}) collective-permute-start(bf16[32,2048]{1,0:T(8,128)(2,1)S(1)} %get-tuple-element.30), channel_id=1, source_target_pairs={{0,2},{1,5},{2,0},{3,7},{4,6},{5,1},{6,4},{7,3},{8,10},{9,13},{10,... | collective-permute-start | bytes 393224 | tf_op jit(solution)/shard_map/ppermute | solution.py:163
  25.5 5.0 %collective-permute-start.7 = (bf16[32,2048]{1,0:T(8,128)(2,1)S(1)}, bf16[32,2048]{1,0:T(8,128)(2,1)S(1)}, u32[]{:S(2)}, u32[]{:S(2)}) collective-permute-start(bf16[32,2048]{1,0:T(8,128)(2,1)S(1)} %get-tuple-element.28), channel_id=1, source_target_pairs={{0,2},{1,5},{2,0},{3,7},{4,6},{5,1},{6,4},{7,3},{8,10},{9,13},{10,... | collective-permute-start | bytes 393224 | tf_op jit(solution)/shard_map/ppermute | solution.py:163
  29.0 5.0 %collective-permute-start.9 = (bf16[32,2048]{1,0:T(8,128)(2,1)S(1)}, bf16[32,2048]{1,0:T(8,128)(2,1)S(1)}, u32[]{:S(2)}, u32[]{:S(2)}) collective-permute-start(bf16[32,2048]{1,0:T(8,128)(2,1)S(1)} %add_convert_fusion), channel_id=1, source_target_pairs={{0,4},{1,3},{2,6},{3,1},{4,0},{5,7},{6,2},{7,5},{8,12},{9,11},{10,... | collective-permute-start | bytes 393224 | tf_op jit(solution)/shard_map/ppermute | solution.py:163
  34.1 7.4 %copy-start.3 = (bf16[16,4096]{1,0:T(8,128)(2,1)S(1)}, bf16[16,4096]{1,0:T(8,128)(2,1)}, u32[]{:S(2)}) copy-start(bf16[16,4096]{1,0:T(8,128)(2,1)} %core_ref.1) | copy-start | bytes 393220
  34.1 5.9 %collective-permute-start.10 = (bf16[16,2048]{1,0:T(8,128)(2,1)S(1)}, bf16[16,2048]{1,0:T(8,128)(2,1)S(1)}, u32[]{:S(2)}, u32[]{:S(2)}) collective-permute-start(bf16[16,2048]{1,0:T(8,128)(2,1)S(1)} %slice.13), channel_id=1, source_target_pairs={{0,8},{1,9},{2,10},{3,11},{4,12},{5,13},{6,14},{7,15},{8,0},{9,1},... | collective-permute-start | bytes 196616 | tf_op jit(solution)/shard_map/ppermute | solution.py:163
  40.1 1.4 %collective-permute-start.11 = (f32[16,2048]{1,0:T(8,128)S(1)}, f32[16,2048]{1,0:T(8,128)S(1)}, u32[]{:S(2)}, u32[]{:S(2)}) collective-permute-start(f32[16,2048]{1,0:T(8,128)S(1)} %slice_add_fusion.mine_ref), channel_id=1, source_target_pairs={{0,1},{1,0},{2,3},{3,2},{4,5},{5,4},{6,7},{7,6},{8,9},{9,8},{10,11... | collective-permute-start | bytes 393224 | tf_op jit(solution)/shard_map/ppermute | solution.py:167

commit v10 on v7

--- a/solution.py
+++ b/solution.py
@@ -146,36 +146,13 @@
     )
 
 
-def odd_bits(number, count):
-    parity = number & 1
-    for shift in range(1, (count - 1).bit_length()):
-        parity = parity ^ ((number >> shift) & 1)
-    return parity
-
-
-def swap(array, sizes, dz, dx):
-    rows_z, rows_x = sizes
-    turn = odd_bits(dz, rows_z) ^ odd_bits(dx, rows_x)
-    step = (dz * rows_x + dx) * 2 + turn
-    return lax.ppermute(array, ("batch", "pair", "orb"), [(i, i ^ step) for i in range(rows_z * rows_x * 2)])
-
-
-def swap_cores(array):
-    return lax.ppermute(array, "orb", [(0, 1), (1, 0)])
-
-
-def add_all(terms):
-    total = terms[0]
-    for term in terms[1:]:
-        total = total + term
-    return total
+def swap(array, axis, count, step):
+    return lax.ppermute(array, axis, [(i, i ^ step) for i in range(count)])
 
 
 def per_device(basis_values, point_weights, slot_ids, fetch_rows, density_blocks, core_blocks):
     rows_z, rows_x = lax.axis_size("batch"), lax.axis_size("pair")
-    z, x, core = lax.axis_index("batch"), lax.axis_index("pair"), lax.axis_index("orb")
-    sizes = (rows_z, rows_x)
-    half = core ^ odd_bits(z, rows_z) ^ odd_bits(x, rows_x)
+    z, x, half = lax.axis_index("batch"), lax.axis_index("pair"), lax.axis_index("orb")
     owners = rows_z * rows_x
     batches, points, columns = basis_values.shape
     groups, own_groups = slot_ids.shape[1], slot_ids.shape[2]
@@ -192,7 +169,7 @@
         jax.ShapeDtypeStruct((1, batches * own_groups * groups), jnp.int32),
         2,
     )(fetch_rows.reshape(owners, capacity), slot_ids.transpose(0, 2, 1).reshape(1, -1))
-    other_rows = swap_cores(own_rows)
+    other_rows = swap(own_rows, "orb", 2, 1)
 
     steps = list(range(rows_z // 2, rows_z)) + list(range(1, rows_z // 2))
     side = list(range(1, rows_x))
@@ -200,18 +177,18 @@
     mine = lax.dynamic_slice_in_dim(density_blocks, half * wide, wide, 1)
     pieces = {0: mine}
     for dx in side:
-        pieces[dx] = swap(mine, sizes, 0, dx)
+        pieces[dx] = swap(mine, "pair", rows_x, dx)
     for dz in steps[::-1]:
-        pieces[dz * rows_x] = swap(mine, sizes, dz, 0)
-    first, last = steps[0] * rows_x, (rows_z - 1) * rows_x
+        pieces[dz * rows_x] = swap(mine, "batch", rows_z, dz)
+    first, last = steps[0] * rows_x, steps[-1] * rows_x
     pieces[first], own_rows = lax.optimization_barrier((pieces[first], own_rows))
     pieces[last], other_rows = lax.optimization_barrier((pieces[last], other_rows))
     for dz in steps[rows_z // 2:] + steps[:rows_z // 2]:
         for dx in side:
-            pieces[dz * rows_x + dx] = swap(pieces[dz * rows_x], sizes, 0, dx)
+            pieces[dz * rows_x + dx] = swap(pieces[dz * rows_x], "pair", rows_x, dx)
     order = list(pieces)
 
-    half_at, _ = lax.optimization_barrier((half.reshape(1).astype(jnp.int32), pieces[last]))
+    half_at, _ = lax.optimization_barrier((half.reshape(1).astype(jnp.int32), pieces[(rows_z - 1) * rows_x]))
     left, left_t = call(
         prepare_kernel,
         (
@@ -225,7 +202,7 @@
     )(half_at, basis_values)
 
     place = (z * rows_x + x).reshape(1).astype(jnp.int32)
-    core_at = core.reshape(1).astype(jnp.int32)
+    core_at = half.reshape(1).astype(jnp.int32)
 
     partial = call(
         functools.partial(density_kernel, order),
@@ -236,7 +213,7 @@
         flops=2 * batches * points * columns * kept,
         moved=2 * batches * points * columns * 2,
     )(place, core_at, *[pieces[k] for k in order], own_rows, other_rows, left, basis_values)
-    partial_other = swap_cores(partial)
+    partial_other = swap(partial, "orb", 2, 1)
 
     sums = call(
         scatter_kernel,
@@ -253,16 +230,18 @@
     for dz in steps:
         joined = sums[dz * rows_x].astype(f32)
         for dx in side:
-            joined = joined + swap(sums[dz * rows_x + dx], sizes, 0, dx).astype(f32)
+            joined = joined + swap(sums[dz * rows_x + dx], "pair", rows_x, dx).astype(f32)
         joined = joined.astype(bf16)
         if dz == steps[0]:
             joined, *own = lax.optimization_barrier((joined, *own))
-        landed.append(swap(joined, sizes, dz, 0))
+        landed.append(swap(joined, "batch", rows_z, dz))
     for dx in side:
-        landed.append(swap(own[dx], sizes, 0, dx))
+        landed.append(swap(own[dx], "pair", rows_x, dx))
     landed.append(own[0])
-    total = add_all([term.astype(f32) for term in landed])
-    total_other = swap_cores(total)
+    total = landed[0].astype(f32)
+    for term in landed[1:]:
+        total = total + term.astype(f32)
+    total_other = swap(total, "orb", 2, 1)
     return call(
         finish_kernel, jax.ShapeDtypeStruct((held, square), f32), 3, scalars=1, moved=held * square * 12
     )(half_at, total, total_other, core_blocks)

time: 39.2 us -> 37.8 us (0.964)
  waiting for transfers between devices: 12 us -> 9.84 us
  starting transfers between devices: 19.9 us -> 20.6 us
    ppermute x17, waiting for transfers between devices: 12 us -> 9.84 us  [swap(): return lax.ppermute(array, axis, [(i, i ^ step) for i in range(count)])]
    ppermute x17, starting transfers between devices: 19.9 us -> 20.6 us  [swap(): return lax.ppermute(array, axis, [(i, i ^ step) for i in range(count)])]
    unnamed x12 -> x14, local copies, waits for them, and re-layouts: 2.74 us -> 2.74 us
  transfers between devices with their start and end apart: 17 -> 17, of which waited for: 11 -> 7; matrix products, arithmetic and copies ran while one was open for 0% -> 0% of each run, Pallas kernels for 2% -> 3%
where the time goes in v10:
time: 37.8 us; the launch traced here: 37.6 us
  starting transfers between devices  20.6 us (54%)
  waiting for transfers between devices  9.84 us (26%)
  Pallas kernels  4.18 us (11%)
  local copies, waits for them, and re-layouts  2.84 us (8%)
    ppermute x17, starting transfers between devices, swap(): return lax.ppermute(array, axis, [(i, i ^ step) for i in range(count)])  20.6 us
    ppermute x17, waiting for transfers between devices, swap(): return lax.ppermute(array, axis, [(i, i ^ step) for i in range(count)])  9.84 us
    unnamed x14, local copies, waits for them, and re-layouts  2.74 us
    pallas_call x1, Pallas kernels, per_device(): call(scatter_kernel, [jax.ShapeDtypeStruct((held, wide), bf16)] * owners,...  1.41 us
    pallas_call x1, Pallas kernels, per_device(): call(functools.partial(density_kernel, order), jax.ShapeDtypeStruct((batc...  1.09 us
  transfers between devices with their start and end apart: 17, of which 7 were waited for; matrix products, arithmetic and copies ran while one was open for 0% of the time, Pallas kernels for 3%

profile of v10, /device:TPU:0, one launch (start us, length us, event | category | flops | bytes accessed | tf_op | source)
XLA Modules:
  0.0 37.6 jit_solution(8062417348851341965)
XLA Ops:
  0.0 0.0 copy-start
  0.0 0.9 %copy-done = bf16[16,4096]{1,0:T(8,128)(2,1)S(1)} copy-done((bf16[16,4096]{1,0:T(8,128)(2,1)S(1)}, bf16[16,4096]{1,0:T(8,128)(2,1)}, u32[]{:S(2)}) %copy-start) | copy-done | bytes 131096
  0.9 4.1 %collective-permute-start.4 = (bf16[16,2048]{1,0:T(8,128)(2,1)S(1)}, bf16[16,2048]{1,0:T(8,128)(2,1)S(1)}, u32[]{:S(2)}, u32[]{:S(2)}) collective-permute-start(bf16[16,2048]{1,0:T(8,128)(2,1)S(1)} %constant_dynamic-slice_fusion.refs_0_), channel_id=1, source_target_pairs={{0,8},{4,12},{8,0},{12,4},{1,9},{5,13},{9,1},{13,5},{2,10},{6,14},... | collective-permute-start | bytes 196616 | tf_op jit(solution)/shard_map/ppermute | solution.py:150
  5.0 1.6 %collective-permute-start.2 = (bf16[16,2048]{1,0:T(8,128)(2,1)S(1)}, bf16[16,2048]{1,0:T(8,128)(2,1)S(1)}, u32[]{:S(2)}, u32[]{:S(2)}) collective-permute-start(bf16[16,2048]{1,0:T(8,128)(2,1)S(1)} %constant_dynamic-slice_fusion.refs_0_), channel_id=1, source_target_pairs={{0,4},{4,0},{8,12},{12,8},{1,5},{5,1},{9,13},{13,9},{2,6},{6,2},{1... | collective-permute-start | bytes 196616 | tf_op jit(solution)/shard_map/ppermute | solution.py:150
  6.6 0.0 collective-permute-start
  6.6 0.0 copy-done.6
  6.6 0.1 reshape.16.slots_ref
  6.7 0.6 %copy-done.5 = s32[1,1,8,8]{3,2,1,0:T(8,128)S(1)} copy-done((s32[1,1,8,8]{3,2,1,0:T(8,128)S(1)}, s32[1,1,8,8]{3,2,1,0:T(8,128)}, u32[]{:S(2)}) %copy-start.5) | copy-done | bytes 280
  7.3 0.2 shard_map.64.refs_8_.refs_5_
  7.5 0.0 collective-permute-start.3
  7.5 1.8 %collective-permute-start.1 = (bf16[16,2048]{1,0:T(8,128)(2,1)S(1)}, bf16[16,2048]{1,0:T(8,128)(2,1)S(1)}, u32[]{:S(2)}, u32[]{:S(2)}) collective-permute-start(bf16[16,2048]{1,0:T(8,128)(2,1)S(1)} %constant_dynamic-slice_fusion.refs_0_), channel_id=1, source_target_pairs={{0,2},{2,0},{1,3},{3,1},{4,6},{6,4},{5,7},{7,5},{8,10},{10,8},{9,1... | collective-permute-start | bytes 196616 | tf_op jit(solution)/shard_map/ppermute | solution.py:150
  9.3 0.0 collective-permute-done.4.refs_4_
  9.3 0.7 %collective-permute-start.6 = (bf16[16,2048]{1,0:T(8,128)(2,1)S(1)}, bf16[16,2048]{1,0:T(8,128)(2,1)S(1)}, u32[]{:S(2)}, u32[]{:S(2)}) collective-permute-start(bf16[16,2048]{1,0:T(8,128)(2,1)S(1)} %collective-permute-done.4.refs_4_), channel_id=1, source_target_pairs={{0,2},{2,0},{1,3},{3,1},{4,6},{6,4},{5,7},{7,5},{8,10},{10,8},{9,1... | collective-permute-start | bytes 196616 | tf_op jit(solution)/shard_map/ppermute | solution.py:150
  9.9 0.0 collective-permute-done.3.refs_9_.refs_6_
  9.9 0.0 collective-permute-done.2.refs_2_
  9.9 1.4 %collective-permute-start.5 = (bf16[16,2048]{1,0:T(8,128)(2,1)S(1)}, bf16[16,2048]{1,0:T(8,128)(2,1)S(1)}, u32[]{:S(2)}, u32[]{:S(2)}) collective-permute-start(bf16[16,2048]{1,0:T(8,128)(2,1)S(1)} %collective-permute-done.2.refs_2_), channel_id=1, source_target_pairs={{0,2},{2,0},{1,3},{3,1},{4,6},{6,4},{5,7},{7,5},{8,10},{10,8},{9,1... | collective-permute-start | bytes 196616 | tf_op jit(solution)/shard_map/ppermute | solution.py:150
  11.3 1.4 %collective-permute-done.refs_3_ = bf16[16,2048]{1,0:T(8,128)(2,1)S(1)} collective-permute-done((bf16[16,2048]{1,0:T(8,128)(2,1)S(1)}, bf16[16,2048]{1,0:T(8,128)(2,1)S(1)}, u32[]{:S(2)}, u32[]{:S(2)}) %collective-permute-start) | collective-permute-done | bytes 65568 | tf_op jit(solution)/shard_map/ppermute | solution.py:150
  12.7 1.5 %collective-permute-start.7 = (bf16[16,2048]{1,0:T(8,128)(2,1)S(1)}, bf16[16,2048]{1,0:T(8,128)(2,1)S(1)}, u32[]{:S(2)}, u32[]{:S(2)}) collective-permute-start(bf16[16,2048]{1,0:T(8,128)(2,1)S(1)} %collective-permute-done.refs_3_), channel_id=1, source_target_pairs={{0,2},{2,0},{1,3},{3,1},{4,6},{6,4},{5,7},{7,5},{8,10},{10,8},{9,1... | collective-permute-start | bytes 196616 | tf_op jit(solution)/shard_map/ppermute | solution.py:150
  14.1 1.2 %copy-done.1 = bf16[4,256,512]{2,1,0:T(8,128)(2,1)S(1)} copy-done((bf16[4,256,512]{2,1,0:T(8,128)(2,1)S(1)}, bf16[4,256,512]{2,1,0:T(8,128)(2,1)}, u32[]{:S(2)}) %copy-start.1) | copy-done | bytes 1048600
  15.4 0.8 %shard_map.65 = (bf16[4,256,256]{2,1,0:T(8,128)(2,1)S(1)}, bf16[4,256,256]{2,1,0:T(8,128)(2,1)S(1)}) custom-call(s32[1]{0:T(128)} %bitcast.half_ref.core_ref, bf16[4,256,512]{2,1,0:T(8,128)(2,1)S(1)} %copy-done.1), custom_call_target="tpu_custom_call" | custom-call | flops 536870912 | bytes 3145728 | tf_op jit(solution)/shard_map/pallas_call | solution.py:192
  16.1 0.0 collective-permute-done.1.refs_1_
  16.1 0.0 collective-permute-done.6.refs_6_
  16.2 0.0 collective-permute-done.5.refs_5_
  16.2 0.8 %collective-permute-done.7.refs_7_ = bf16[16,2048]{1,0:T(8,128)(2,1)S(1)} collective-permute-done((bf16[16,2048]{1,0:T(8,128)(2,1)S(1)}, bf16[16,2048]{1,0:T(8,128)(2,1)S(1)}, u32[]{:S(2)}, u32[]{:S(2)}) %collective-permute-start.7) | collective-permute-done | bytes 65568 | tf_op jit(solution)/shard_map/ppermute | solution.py:150
  16.9 0.0 copy-done.2
  16.9 1.1 %shard_map.66.refs_0_ = f32[4,256]{1,0:T(4,128)S(1)} custom-call(s32[1]{0:T(128)} %bitcast.1.place_ref, s32[1]{0:T(128)} %bitcast.half_ref.core_ref, bf16[16,2048]{1,0:T(8,128)(2,1)S(1)} %constant_dynamic-slice_fusion.refs_0_, bf16[16,2048]{1,0:T(8,128)(2,1)S(1)} %collective-permute-done.1.refs_1_, bf16[16,2048]{1,0:T(8,128)(2,1)S(1)} %collective-permute-done.2.refs_2_, ...), custom_call_target="tpu_custom_call" | custom-call | flops 268435456 | bytes 2097152 | tf_op jit(solution)/shard_map/pallas_call | solution.py:207
  18.0 0.1 collective-permute-start.8
  18.1 1.2 %collective-permute-done.8.refs_1_ = f32[4,256]{1,0:T(4,128)S(1)} collective-permute-done((f32[4,256]{1,0:T(4,128)S(1)}, f32[4,256]{1,0:T(4,128)S(1)}, u32[]{:S(2)}, u32[]{:S(2)}) %collective-permute-start.8) | collective-permute-done | bytes 4128 | tf_op jit(solution)/shard_map/ppermute | solution.py:150
  19.2 0.0 copy-done.4
  19.3 1.4 %shard_map.67 = (bf16[16,2048]{1,0:T(8,128)(2,1)S(1)}, bf16[16,2048]{1,0:T(8,128)(2,1)S(1)}, bf16[16,2048]{1,0:T(8,128)(2,1)S(1)}, bf16[16,2048]{1,0:T(8,128)(2,...) custom-call(s32[1]{0:T(128)} %bitcast.1.place_ref, ...), custom_call_target="tpu_custom_call" | custom-call | flops 268435456 | bytes 2097152 | tf_op jit(solution)/shard_map/pallas_call | solution.py:218
  20.7 1.6 %collective-permute-start.9 = (bf16[16,2048]{1,0:T(8,128)(2,1)S(1)}, bf16[16,2048]{1,0:T(8,128)(2,1)S(1)}, u32[]{:S(2)}, u32[]{:S(2)}) collective-permute-start(bf16[16,2048]{1,0:T(8,128)(2,1)S(1)} %get-tuple-element.31), channel_id=1, source_target_pairs={{0,2},{2,0},{1,3},{3,1},{4,6},{6,4},{5,7},{7,5},{8,10},{10,8},{9,1... | collective-permute-start | bytes 196616 | tf_op jit(solution)/shard_map/ppermute | solution.py:150
  22.2 0.5 %collective-permute-start.11 = (bf16[16,2048]{1,0:T(8,128)(2,1)S(1)}, bf16[16,2048]{1,0:T(8,128)(2,1)S(1)}, u32[]{:S(2)}, u32[]{:S(2)}) collective-permute-start(bf16[16,2048]{1,0:T(8,128)(2,1)S(1)} %get-tuple-element.36), channel_id=1, source_target_pairs={{0,2},{2,0},{1,3},{3,1},{4,6},{6,4},{5,7},{7,5},{8,10},{10,8},{9,1... | collective-permute-start | bytes 196616 | tf_op jit(solution)/shard_map/ppermute | solution.py:150
  22.8 1.5 %collective-permute-start.13 = (bf16[16,2048]{1,0:T(8,128)(2,1)S(1)}, bf16[16,2048]{1,0:T(8,128)(2,1)S(1)}, u32[]{:S(2)}, u32[]{:S(2)}) collective-permute-start(bf16[16,2048]{1,0:T(8,128)(2,1)S(1)} %get-tuple-element.38), channel_id=1, source_target_pairs={{0,2},{2,0},{1,3},{3,1},{4,6},{6,4},{5,7},{7,5},{8,10},{10,8},{9,1... | collective-permute-start | bytes 196616 | tf_op jit(solution)/shard_map/ppermute | solution.py:150
  24.2 1.1 %collective-permute-done.9 = bf16[16,2048]{1,0:T(8,128)(2,1)S(1)} collective-permute-done((bf16[16,2048]{1,0:T(8,128)(2,1)S(1)}, bf16[16,2048]{1,0:T(8,128)(2,1)S(1)}, u32[]{:S(2)}, u32[]{:S(2)}) %collective-permute-start.9) | collective-permute-done | bytes 65568 | tf_op jit(solution)/shard_map/ppermute | solution.py:150
  25.4 1.4 %collective-permute-start.10 = (bf16[16,2048]{1,0:T(8,128)(2,1)S(1)}, bf16[16,2048]{1,0:T(8,128)(2,1)S(1)}, u32[]{:S(2)}, u32[]{:S(2)}) collective-permute-start(bf16[16,2048]{1,0:T(8,128)(2,1)S(1)} %add_convert_fusion.2), channel_id=1, source_target_pairs={{0,8},{4,12},{8,0},{12,4},{1,9},{5,13},{9,1},{13,5},{2,10},{6,14},... | collective-permute-start | bytes 196616 | tf_op jit(solution)/shard_map/ppermute | solution.py:150
  26.8 1.8 %collective-permute-start.15 = (bf16[16,2048]{1,0:T(8,128)(2,1)S(1)}, bf16[16,2048]{1,0:T(8,128)(2,1)S(1)}, u32[]{:S(2)}, u32[]{:S(2)}) collective-permute-start(bf16[16,2048]{1,0:T(8,128)(2,1)S(1)} %get-tuple-element.39), channel_id=1, source_target_pairs={{0,2},{2,0},{1,3},{3,1},{4,6},{6,4},{5,7},{7,5},{8,10},{10,8},{9,1... | collective-permute-start | bytes 196616 | tf_op jit(solution)/shard_map/ppermute | solution.py:150
  28.5 0.0 collective-permute-done.11
  28.6 2.1 %collective-permute-start.12 = (bf16[16,2048]{1,0:T(8,128)(2,1)S(1)}, bf16[16,2048]{1,0:T(8,128)(2,1)S(1)}, u32[]{:S(2)}, u32[]{:S(2)}) collective-permute-start(bf16[16,2048]{1,0:T(8,128)(2,1)S(1)} %add_convert_fusion.1), channel_id=1, source_target_pairs={{0,12},{4,8},{8,4},{12,0},{1,13},{5,9},{9,5},{13,1},{2,14},{6,10},... | collective-permute-start | bytes 196616 | tf_op jit(solution)/shard_map/ppermute | solution.py:150
  30.7 0.0 collective-permute-done.13
  30.7 0.0 copy-start.3
  30.7 0.6 %collective-permute-start.14 = (bf16[16,2048]{1,0:T(8,128)(2,1)S(1)}, bf16[16,2048]{1,0:T(8,128)(2,1)S(1)}, u32[]{:S(2)}, u32[]{:S(2)}) collective-permute-start(bf16[16,2048]{1,0:T(8,128)(2,1)S(1)} %add_convert_fusion), channel_id=1, source_target_pairs={{0,4},{4,0},{8,12},{12,8},{1,5},{5,1},{9,13},{13,9},{2,6},{6,2},{1... | collective-permute-start | bytes 196616 | tf_op jit(solution)/shard_map/ppermute | solution.py:150
  31.3 0.0 collective-permute-done.10
  31.3 0.0 collective-permute-done.15
  31.3 3.4 %collective-permute-done.12 = bf16[16,2048]{1,0:T(8,128)(2,1)S(1)} collective-permute-done((bf16[16,2048]{1,0:T(8,128)(2,1)S(1)}, bf16[16,2048]{1,0:T(8,128)(2,1)S(1)}, u32[]{:S(2)}, u32[]{:S(2)}) %collective-permute-start.12) | collective-permute-done | bytes 65568 | tf_op jit(solution)/shard_map/ppermute | solution.py:150
  34.8 0.7 %collective-permute-done.14 = bf16[16,2048]{1,0:T(8,128)(2,1)S(1)} collective-permute-done((bf16[16,2048]{1,0:T(8,128)(2,1)S(1)}, bf16[16,2048]{1,0:T(8,128)(2,1)S(1)}, u32[]{:S(2)}, u32[]{:S(2)}) %collective-permute-start.14) | collective-permute-done | bytes 65568 | tf_op jit(solution)/shard_map/ppermute | solution.py:150
  35.5 0.1 collective-permute-start.16
  35.5 1.3 %collective-permute-done.16.other_ref = f32[16,2048]{1,0:T(8,128)S(1)} collective-permute-done((f32[16,2048]{1,0:T(8,128)S(1)}, f32[16,2048]{1,0:T(8,128)S(1)}, u32[]{:S(2)}, u32[]{:S(2)}) %collective-permute-start.16) | collective-permute-done | bytes 131104 | tf_op jit(solution)/shard_map/ppermute | solution.py:150
  36.9 0.7 %shard_map.68 = f32[16,4096]{1,0:T(8,128)} custom-call(s32[1]{0:T(128)} %bitcast.half_ref.core_ref, f32[16,2048]{1,0:T(8,128)S(1)} %convert_add_fusion.mine_ref, f32[16,2048]{1,0:T(8,128)S(1)} %collective-permute-done.16.other_ref, bf16[16,4096]{1,0:T(8,128)(2,1)S(1)} %copy-done.3), custom_call_target="tpu_custom_call" | custom-call | bytes 786432 | tf_op jit(solution)/shard_map/pallas_call | solution.py:245
  (11 shorter events, 0.1 us)
Async XLA Ops:
  0.0 0.9 %copy-start = (bf16[16,4096]{1,0:T(8,128)(2,1)S(1)}, bf16[16,4096]{1,0:T(8,128)(2,1)}, u32[]{:S(2)}) copy-start(bf16[16,4096]{1,0:T(8,128)(2,1)} %param.10) | copy-start | bytes 393220
  0.9 5.7 %copy-start.6 = (s32[4,8,4]{1,2,0:T(4,128)S(1)}, s32[4,8,4]{1,2,0:T(4,128)}, u32[]{:S(2)}) copy-start(s32[4,8,4]{1,2,0:T(4,128)} %param.8) | copy-start | bytes 1540
  0.9 8.3 %collective-permute-start.4 = (bf16[16,2048]{1,0:T(8,128)(2,1)S(1)}, bf16[16,2048]{1,0:T(8,128)(2,1)S(1)}, u32[]{:S(2)}, u32[]{:S(2)}) collective-permute-start(bf16[16,2048]{1,0:T(8,128)(2,1)S(1)} %constant_dynamic-slice_fusion.refs_0_), channel_id=1, source_target_pairs={{0,8},{4,12},{8,0},{12,4},{1,9},{5,13},{9,1},{13,5},{2,10},{6,14},... | collective-permute-start | bytes 196616 | tf_op jit(solution)/shard_map/ppermute | solution.py:150
  5.0 4.9 %collective-permute-start.2 = (bf16[16,2048]{1,0:T(8,128)(2,1)S(1)}, bf16[16,2048]{1,0:T(8,128)(2,1)S(1)}, u32[]{:S(2)}, u32[]{:S(2)}) collective-permute-start(bf16[16,2048]{1,0:T(8,128)(2,1)S(1)} %constant_dynamic-slice_fusion.refs_0_), channel_id=1, source_target_pairs={{0,4},{4,0},{8,12},{12,8},{1,5},{5,1},{9,13},{13,9},{2,6},{6,2},{1... | collective-permute-start | bytes 196616 | tf_op jit(solution)/shard_map/ppermute | solution.py:150
  6.6 6.1 %collective-permute-start = (bf16[16,2048]{1,0:T(8,128)(2,1)S(1)}, bf16[16,2048]{1,0:T(8,128)(2,1)S(1)}, u32[]{:S(2)}, u32[]{:S(2)}) collective-permute-start(bf16[16,2048]{1,0:T(8,128)(2,1)S(1)} %constant_dynamic-slice_fusion.refs_0_), channel_id=1, source_target_pairs={{0,12},{4,8},{8,4},{12,0},{1,13},{5,9},{9,5},{13,1},{2,14},{6,10},... | collective-permute-start | bytes 196616 | tf_op jit(solution)/shard_map/ppermute | solution.py:150
  6.6 0.7 %copy-start.5 = (s32[1,1,8,8]{3,2,1,0:T(8,128)S(1)}, s32[1,1,8,8]{3,2,1,0:T(8,128)}, u32[]{:S(2)}) copy-start(s32[1,1,8,8]{3,2,1,0:T(8,128)} %param.9) | copy-start | bytes 772
  7.5 2.4 %collective-permute-start.3 = (s32[1,128]{1,0:T(1,128)S(1)}, s32[1,128]{1,0:T(1,128)S(1)}, u32[]{:S(2)}, u32[]{:S(2)}) collective-permute-start(s32[1,128]{1,0:T(1,128)S(1)} %shard_map.64.refs_8_.refs_5_), channel_id=1, source_target_pairs={{0,1},{1,0},{2,3},{3,2},{4,5},{5,4},{6,7},{7,6},{8,9},{9,8},{10,11... | collective-permute-start | bytes 1544 | tf_op jit(solution)/shard_map/ppermute | solution.py:150
  7.5 8.7 %collective-permute-start.1 = (bf16[16,2048]{1,0:T(8,128)(2,1)S(1)}, bf16[16,2048]{1,0:T(8,128)(2,1)S(1)}, u32[]{:S(2)}, u32[]{:S(2)}) collective-permute-start(bf16[16,2048]{1,0:T(8,128)(2,1)S(1)} %constant_dynamic-slice_fusion.refs_0_), channel_id=1, source_target_pairs={{0,2},{2,0},{1,3},{3,1},{4,6},{6,4},{5,7},{7,5},{8,10},{10,8},{9,1... | collective-permute-start | bytes 196616 | tf_op jit(solution)/shard_map/ppermute | solution.py:150
  9.3 6.9 %collective-permute-start.6 = (bf16[16,2048]{1,0:T(8,128)(2,1)S(1)}, bf16[16,2048]{1,0:T(8,128)(2,1)S(1)}, u32[]{:S(2)}, u32[]{:S(2)}) collective-permute-start(bf16[16,2048]{1,0:T(8,128)(2,1)S(1)} %collective-permute-done.4.refs_4_), channel_id=1, source_target_pairs={{0,2},{2,0},{1,3},{3,1},{4,6},{6,4},{5,7},{7,5},{8,10},{10,8},{9,1... | collective-permute-start | bytes 196616 | tf_op jit(solution)/shard_map/ppermute | solution.py:150
  9.9 6.2 %collective-permute-start.5 = (bf16[16,2048]{1,0:T(8,128)(2,1)S(1)}, bf16[16,2048]{1,0:T(8,128)(2,1)S(1)}, u32[]{:S(2)}, u32[]{:S(2)}) collective-permute-start(bf16[16,2048]{1,0:T(8,128)(2,1)S(1)} %collective-permute-done.2.refs_2_), channel_id=1, source_target_pairs={{0,2},{2,0},{1,3},{3,1},{4,6},{6,4},{5,7},{7,5},{8,10},{10,8},{9,1... | collective-permute-start | bytes 196616 | tf_op jit(solution)/shard_map/ppermute | solution.py:150
  12.7 4.3 %collective-permute-start.7 = (bf16[16,2048]{1,0:T(8,128)(2,1)S(1)}, bf16[16,2048]{1,0:T(8,128)(2,1)S(1)}, u32[]{:S(2)}, u32[]{:S(2)}) collective-permute-start(bf16[16,2048]{1,0:T(8,128)(2,1)S(1)} %collective-permute-done.refs_3_), channel_id=1, source_target_pairs={{0,2},{2,0},{1,3},{3,1},{4,6},{6,4},{5,7},{7,5},{8,10},{10,8},{9,1... | collective-permute-start | bytes 196616 | tf_op jit(solution)/shard_map/ppermute | solution.py:150
  14.1 1.2 %copy-start.1 = (bf16[4,256,512]{2,1,0:T(8,128)(2,1)S(1)}, bf16[4,256,512]{2,1,0:T(8,128)(2,1)}, u32[]{:S(2)}) copy-start(bf16[4,256,512]{2,1,0:T(8,128)(2,1)} %refs_3_.1) | copy-start | bytes 3145732
  15.4 1.6 %copy-start.2 = (bf16[4,256,512]{2,1,0:T(8,128)(2,1)S(1)}, bf16[4,256,512]{2,1,0:T(8,128)(2,1)}, u32[]{:S(2)}) copy-start(bf16[4,256,512]{2,1,0:T(8,128)(2,1)} %refs_3_.1) | copy-start | bytes 3145732
  16.9 2.3 %copy-start.4 = (f32[4,256]{1,0:T(4,128)S(1)}, f32[4,256]{1,0:T(4,128)}, u32[]{:S(2)}) copy-start(f32[4,256]{1,0:T(4,128)} %refs_2_.1) | copy-start | bytes 12292
  18.0 1.2 %collective-permute-start.8 = (f32[4,256]{1,0:T(4,128)S(1)}, f32[4,256]{1,0:T(4,128)S(1)}, u32[]{:S(2)}, u32[]{:S(2)}) collective-permute-start(f32[4,256]{1,0:T(4,128)S(1)} %shard_map.66.refs_0_), channel_id=1, source_target_pairs={{0,1},{1,0},{2,3},{3,2},{4,5},{5,4},{6,7},{7,6},{8,9},{9,8},{10,11... | collective-permute-start | bytes 12296 | tf_op jit(solution)/shard_map/ppermute | solution.py:150
  20.7 4.7 %collective-permute-start.9 = (bf16[16,2048]{1,0:T(8,128)(2,1)S(1)}, bf16[16,2048]{1,0:T(8,128)(2,1)S(1)}, u32[]{:S(2)}, u32[]{:S(2)}) collective-permute-start(bf16[16,2048]{1,0:T(8,128)(2,1)S(1)} %get-tuple-element.31), channel_id=1, source_target_pairs={{0,2},{2,0},{1,3},{3,1},{4,6},{6,4},{5,7},{7,5},{8,10},{10,8},{9,1... | collective-permute-start | bytes 196616 | tf_op jit(solution)/shard_map/ppermute | solution.py:150
  22.2 6.3 %collective-permute-start.11 = (bf16[16,2048]{1,0:T(8,128)(2,1)S(1)}, bf16[16,2048]{1,0:T(8,128)(2,1)S(1)}, u32[]{:S(2)}, u32[]{:S(2)}) collective-permute-start(bf16[16,2048]{1,0:T(8,128)(2,1)S(1)} %get-tuple-element.36), channel_id=1, source_target_pairs={{0,2},{2,0},{1,3},{3,1},{4,6},{6,4},{5,7},{7,5},{8,10},{10,8},{9,1... | collective-permute-start | bytes 196616 | tf_op jit(solution)/shard_map/ppermute | solution.py:150
  22.8 7.9 %collective-permute-start.13 = (bf16[16,2048]{1,0:T(8,128)(2,1)S(1)}, bf16[16,2048]{1,0:T(8,128)(2,1)S(1)}, u32[]{:S(2)}, u32[]{:S(2)}) collective-permute-start(bf16[16,2048]{1,0:T(8,128)(2,1)S(1)} %get-tuple-element.38), channel_id=1, source_target_pairs={{0,2},{2,0},{1,3},{3,1},{4,6},{6,4},{5,7},{7,5},{8,10},{10,8},{9,1... | collective-permute-start | bytes 196616 | tf_op jit(solution)/shard_map/ppermute | solution.py:150
  25.4 5.9 %collective-permute-start.10 = (bf16[16,2048]{1,0:T(8,128)(2,1)S(1)}, bf16[16,2048]{1,0:T(8,128)(2,1)S(1)}, u32[]{:S(2)}, u32[]{:S(2)}) collective-permute-start(bf16[16,2048]{1,0:T(8,128)(2,1)S(1)} %add_convert_fusion.2), channel_id=1, source_target_pairs={{0,8},{4,12},{8,0},{12,4},{1,9},{5,13},{9,1},{13,5},{2,10},{6,14},... | collective-permute-start | bytes 196616 | tf_op jit(solution)/shard_map/ppermute | solution.py:150
  26.8 4.6 %collective-permute-start.15 = (bf16[16,2048]{1,0:T(8,128)(2,1)S(1)}, bf16[16,2048]{1,0:T(8,128)(2,1)S(1)}, u32[]{:S(2)}, u32[]{:S(2)}) collective-permute-start(bf16[16,2048]{1,0:T(8,128)(2,1)S(1)} %get-tuple-element.39), channel_id=1, source_target_pairs={{0,2},{2,0},{1,3},{3,1},{4,6},{6,4},{5,7},{7,5},{8,10},{10,8},{9,1... | collective-permute-start | bytes 196616 | tf_op jit(solution)/shard_map/ppermute | solution.py:150
  28.6 6.2 %collective-permute-start.12 = (bf16[16,2048]{1,0:T(8,128)(2,1)S(1)}, bf16[16,2048]{1,0:T(8,128)(2,1)S(1)}, u32[]{:S(2)}, u32[]{:S(2)}) collective-permute-start(bf16[16,2048]{1,0:T(8,128)(2,1)S(1)} %add_convert_fusion.1), channel_id=1, source_target_pairs={{0,12},{4,8},{8,4},{12,0},{1,13},{5,9},{9,5},{13,1},{2,14},{6,10},... | collective-permute-start | bytes 196616 | tf_op jit(solution)/shard_map/ppermute | solution.py:150
  30.7 6.2 %copy-start.3 = (bf16[16,4096]{1,0:T(8,128)(2,1)S(1)}, bf16[16,4096]{1,0:T(8,128)(2,1)}, u32[]{:S(2)}) copy-start(bf16[16,4096]{1,0:T(8,128)(2,1)} %core_ref.1) | copy-start | bytes 393220
  30.7 4.7 %collective-permute-start.14 = (bf16[16,2048]{1,0:T(8,128)(2,1)S(1)}, bf16[16,2048]{1,0:T(8,128)(2,1)S(1)}, u32[]{:S(2)}, u32[]{:S(2)}) collective-permute-start(bf16[16,2048]{1,0:T(8,128)(2,1)S(1)} %add_convert_fusion), channel_id=1, source_target_pairs={{0,4},{4,0},{8,12},{12,8},{1,5},{5,1},{9,13},{13,9},{2,6},{6,2},{1... | collective-permute-start | bytes 196616 | tf_op jit(solution)/shard_map/ppermute | solution.py:150
  35.5 1.4 %collective-permute-start.16 = (f32[16,2048]{1,0:T(8,128)S(1)}, f32[16,2048]{1,0:T(8,128)S(1)}, u32[]{:S(2)}, u32[]{:S(2)}) collective-permute-start(f32[16,2048]{1,0:T(8,128)S(1)} %convert_add_fusion.mine_ref), channel_id=1, source_target_pairs={{0,1},{1,0},{2,3},{3,2},{4,5},{5,4},{6,7},{7,6},{8,9},{9,8},{10,11... | collective-permute-start | bytes 393224 | tf_op jit(solution)/shard_map/ppermute | solution.py:150

commit v11 on v10

--- a/solution.py
+++ b/solution.py
@@ -60,10 +60,11 @@
     own_ref, other_ref, left_ref, values_ref, out_ref, table, dense = refs[len(places):]
     batches, points, columns = values_ref.shape
     groups = columns // GO
-    held = piece_refs[0].shape[0]
-    for ref, k in zip(piece_refs, places):
-        table[k * held:(k + 1) * held, :] = ref[...]
-    pick = row_table(place_ref, core_ref, own_ref, other_ref, held, len(places)).T.astype(jnp.bfloat16)
+    owners = sum(len(blocks) for blocks in places)
+    held = table.shape[0] // owners
+    for ref, blocks in zip(piece_refs, places):
+        table[blocks[0] * held:(blocks[-1] + 1) * held, :] = ref[...]
+    pick = row_table(place_ref, core_ref, own_ref, other_ref, held, owners).T.astype(jnp.bfloat16)
     low = lax.broadcasted_iota(jnp.int32, (1, 1, 1, groups, 128), 4) < GO
     for j in range(table.shape[1] // 128):
         lanes = slice(j * 128, (j + 1) * 128)
@@ -85,12 +86,13 @@
         out_ref[t:t + 1, :] = jnp.sum(folded.T, axis=0, keepdims=True)
 
 
-def scatter_kernel(place_ref, core_ref, *refs):
+def scatter_kernel(places, place_ref, core_ref, *refs):
     mine_ref, far_ref, weight_ref, values_ref, left_t_ref, own_ref, other_ref = refs[:7]
     out_refs = refs[7:-2]
     high, rest = refs[-2:]
-    pieces = len(out_refs)
-    held = out_refs[0].shape[0]
+    target = {k: (ref, i) for ref, blocks in zip(out_refs, places) for i, k in enumerate(blocks)}
+    pieces = len(target)
+    held = out_refs[0].shape[0] // len(places[0])
     put = row_table(place_ref, core_ref, own_ref, other_ref, held, pieces).astype(jnp.bfloat16)
     batches, points, columns = values_ref.shape
     groups = columns // GO
@@ -120,7 +122,8 @@
         some = put[k * held:(k + step) * held, :]
         total = split_dot(some, high[...]) + split_dot(some, rest[...])
         for i in range(step):
-            out_refs[k + i][...] = total[i * held:(i + 1) * held, :].astype(jnp.bfloat16)
+            ref, at = target[k + i]
+            ref[at * held:(at + 1) * held, :] = total[i * held:(i + 1) * held, :].astype(jnp.bfloat16)
 
 
 def finish_kernel(half_ref, mine_ref, other_ref, core_ref, out_ref):
@@ -171,24 +174,28 @@
     )(fetch_rows.reshape(owners, capacity), slot_ids.transpose(0, 2, 1).reshape(1, -1))
     other_rows = swap(own_rows, "orb", 2, 1)
 
-    steps = list(range(rows_z // 2, rows_z)) + list(range(1, rows_z // 2))
+    far = list(range(rows_z // 2, rows_z))
+    near = list(range(1, rows_z // 2))
     side = list(range(1, rows_x))
 
     mine = lax.dynamic_slice_in_dim(density_blocks, half * wide, wide, 1)
-    pieces = {0: mine}
-    for dx in side:
-        pieces[dx] = swap(mine, "pair", rows_x, dx)
-    for dz in steps[::-1]:
-        pieces[dz * rows_x] = swap(mine, "batch", rows_z, dz)
-    first, last = steps[0] * rows_x, steps[-1] * rows_x
-    pieces[first], own_rows = lax.optimization_barrier((pieces[first], own_rows))
-    pieces[last], other_rows = lax.optimization_barrier((pieces[last], other_rows))
-    for dz in steps[rows_z // 2:] + steps[:rows_z // 2]:
+    direct = {dz: swap(mine, "batch", rows_z, dz) for dz in far}
+    beside = [swap(mine, "pair", rows_x, dx) for dx in side]
+    *beside, own_rows = lax.optimization_barrier((*beside, own_rows))
+    cluster = jnp.concatenate([mine, *beside], axis=0)
+    arrays, places = [cluster], [list(range(rows_x))]
+    for dz in near:
+        arrays.append(swap(cluster, "batch", rows_z, dz))
+        places.append(list(range(dz * rows_x, (dz + 1) * rows_x)))
+    direct[far[0]], other_rows = lax.optimization_barrier((direct[far[0]], other_rows))
+    for dz in far:
+        arrays.append(direct[dz])
+        places.append([dz * rows_x])
         for dx in side:
-            pieces[dz * rows_x + dx] = swap(pieces[dz * rows_x], "pair", rows_x, dx)
-    order = list(pieces)
-
-    half_at, _ = lax.optimization_barrier((half.reshape(1).astype(jnp.int32), pieces[(rows_z - 1) * rows_x]))
+            arrays.append(swap(direct[dz], "pair", rows_x, dx))
+            places.append([dz * rows_x + dx])
+
+    half_at, _ = lax.optimization_barrier((half.reshape(1).astype(jnp.int32), direct[far[-1]]))
     left, left_t = call(
         prepare_kernel,
         (
@@ -205,19 +212,21 @@
     core_at = half.reshape(1).astype(jnp.int32)
 
     partial = call(
-        functools.partial(density_kernel, order),
+        functools.partial(density_kernel, places),
         jax.ShapeDtypeStruct((batches, points), f32),
-        owners + 4,
+        len(arrays) + 4,
         scalars=2,
         scratch=(pltpu.VMEM((table_rows, wide), bf16), pltpu.VMEM((batches, kept, columns), bf16)),
         flops=2 * batches * points * columns * kept,
         moved=2 * batches * points * columns * 2,
-    )(place, core_at, *[pieces[k] for k in order], own_rows, other_rows, left, basis_values)
+    )(place, core_at, *arrays, own_rows, other_rows, left, basis_values)
     partial_other = swap(partial, "orb", 2, 1)
 
+    out_places = [list(range(dz * rows_x, (dz + 1) * rows_x)) for dz in [0] + near]
+    out_places += [[dz * rows_x + dx] for dz in far for dx in [0] + side]
     sums = call(
-        scatter_kernel,
-        [jax.ShapeDtypeStruct((held, wide), bf16)] * owners,
+        functools.partial(scatter_kernel, out_places),
+        [jax.ShapeDtypeStruct((held * len(blocks), wide), bf16) for blocks in out_places],
         7,
         scalars=2,
         scratch=(pltpu.VMEM((entries, wide), bf16), pltpu.VMEM((entries, wide), bf16)),
@@ -225,22 +234,21 @@
         moved=2 * batches * points * columns * 2,
     )(place, core_at, partial, partial_other, point_weights, basis_values, left_t, own_rows, other_rows)
 
+    clusters, singles = sums[:len(near) + 1], sums[len(near) + 1:]
     landed = []
-    own = sums[:rows_x]
-    for dz in steps:
-        joined = sums[dz * rows_x].astype(f32)
+    for i, dz in enumerate(far):
+        joined = singles[i * rows_x].astype(f32)
         for dx in side:
-            joined = joined + swap(sums[dz * rows_x + dx], "pair", rows_x, dx).astype(f32)
-        joined = joined.astype(bf16)
-        if dz == steps[0]:
-            joined, *own = lax.optimization_barrier((joined, *own))
-        landed.append(swap(joined, "batch", rows_z, dz))
+            joined = joined + swap(singles[i * rows_x + dx], "pair", rows_x, dx).astype(f32)
+        landed.append(swap(joined.astype(bf16), "batch", rows_z, dz).astype(f32))
+    cluster = clusters[0].astype(f32)
+    for dz, array in zip(near, clusters[1:]):
+        cluster = cluster + swap(array, "batch", rows_z, dz).astype(f32)
+    total = cluster[:held]
     for dx in side:
-        landed.append(swap(own[dx], "pair", rows_x, dx))
-    landed.append(own[0])
-    total = landed[0].astype(f32)
-    for term in landed[1:]:
-        total = total + term.astype(f32)
+        total = total + swap(cluster[dx * held:(dx + 1) * held].astype(bf16), "pair", rows_x, dx).astype(f32)
+    for term in landed:
+        total = total + term
     total_other = swap(total, "orb", 2, 1)
     return call(
         finish_kernel, jax.ShapeDtypeStruct((held, square), f32), 3, scalars=1, moved=held * square * 12

time: 37.8 us -> 36.8 us (0.974)
  starting transfers between devices: 20.6 us -> 15.5 us
  waiting for transfers between devices: 9.84 us -> 13.8 us
    ppermute x17 -> x15, starting transfers between devices: 20.6 us -> 15.5 us  [swap(): return lax.ppermute(array, axis, [(i, i ^ step) for i in range(count)])]
    ppermute x17 -> x15, waiting for transfers between devices: 9.84 us -> 13.8 us  [swap(): return lax.ppermute(array, axis, [(i, i ^ step) for i in range(count)])]
  transfers between devices with their start and end apart: 17 -> 15, of which waited for: 7 -> 8; matrix products, arithmetic and copies ran while one was open for 0% -> 0% of each run, Pallas kernels for 3% -> 3%
where the time goes in v11:
time: 36.8 us; the launch traced here: 36.6 us
  starting transfers between devices  15.5 us (42%)
  waiting for transfers between devices  13.8 us (38%)
  Pallas kernels  4.19 us (11%)
  local copies, waits for them, and re-layouts  2.84 us (8%)
    ppermute x15, starting transfers between devices, swap(): return lax.ppermute(array, axis, [(i, i ^ step) for i in range(count)])  15.5 us
    ppermute x15, waiting for transfers between devices, swap(): return lax.ppermute(array, axis, [(i, i ^ step) for i in range(count)])  13.8 us
    unnamed x14, local copies, waits for them, and re-layouts  2.74 us
    pallas_call x1, Pallas kernels, per_device(): call(functools.partial(scatter_kernel, out_places), [jax.ShapeDtypeStruct...  1.4 us
    pallas_call x1, Pallas kernels, per_device(): call(functools.partial(density_kernel, places), jax.ShapeDtypeStruct((bat...  1.1 us
    pallas_call x1, Pallas kernels, per_device(): call(prepare_kernel, (jax.ShapeDtypeStruct((batches, points, kept), bf16)...  0.76 us
  transfers between devices with their start and end apart: 15, of which 8 were waited for; matrix products, arithmetic and copies ran while one was open for 0% of the time, Pallas kernels for 3%

profile of v11, /device:TPU:0, one launch (start us, length us, event | category | flops | bytes accessed | tf_op | source)
XLA Modules:
  0.0 36.6 jit_solution(6196155802958742305)
XLA Ops:
  0.0 0.0 copy-start
  0.0 0.9 %copy-done = bf16[16,4096]{1,0:T(8,128)(2,1)S(1)} copy-done((bf16[16,4096]{1,0:T(8,128)(2,1)S(1)}, bf16[16,4096]{1,0:T(8,128)(2,1)}, u32[]{:S(2)}) %copy-start) | copy-done | bytes 131096
  0.9 0.0 copy-start.6
  0.9 3.0 %collective-permute-start.1 = (bf16[16,2048]{1,0:T(8,128)(2,1)S(1)}, bf16[16,2048]{1,0:T(8,128)(2,1)S(1)}, u32[]{:S(2)}, u32[]{:S(2)}) collective-permute-start(bf16[16,2048]{1,0:T(8,128)(2,1)S(1)} %constant_dynamic-slice_fusion), channel_id=1, source_target_pairs={{0,2},{2,0},{1,3},{3,1},{4,6},{6,4},{5,7},{7,5},{8,10},{10,8},{9,1... | collective-permute-start | bytes 196616 | tf_op jit(solution)/shard_map/ppermute | solution.py:153
  3.9 2.6 %collective-permute-start.3 = (bf16[16,2048]{1,0:T(8,128)(2,1)S(1)}, bf16[16,2048]{1,0:T(8,128)(2,1)S(1)}, u32[]{:S(2)}, u32[]{:S(2)}) collective-permute-start(bf16[16,2048]{1,0:T(8,128)(2,1)S(1)} %constant_dynamic-slice_fusion), channel_id=1, source_target_pairs={{0,8},{4,12},{8,0},{12,4},{1,9},{5,13},{9,1},{13,5},{2,10},{6,14},... | collective-permute-start | bytes 196616 | tf_op jit(solution)/shard_map/ppermute | solution.py:153
  6.5 1.3 %collective-permute-start = (bf16[16,2048]{1,0:T(8,128)(2,1)S(1)}, bf16[16,2048]{1,0:T(8,128)(2,1)S(1)}, u32[]{:S(2)}, u32[]{:S(2)}) collective-permute-start(bf16[16,2048]{1,0:T(8,128)(2,1)S(1)} %constant_dynamic-slice_fusion), channel_id=1, source_target_pairs={{0,12},{4,8},{8,4},{12,0},{1,13},{5,9},{9,5},{13,1},{2,14},{6,10},... | collective-permute-start | bytes 196616 | tf_op jit(solution)/shard_map/ppermute | solution.py:153
  7.9 0.0 copy-done.6
  7.9 0.1 reshape.16.slots_ref
  7.9 0.6 %copy-done.5 = s32[1,1,8,8]{3,2,1,0:T(8,128)S(1)} copy-done((s32[1,1,8,8]{3,2,1,0:T(8,128)S(1)}, s32[1,1,8,8]{3,2,1,0:T(8,128)}, u32[]{:S(2)}) %copy-start.5) | copy-done | bytes 280
  8.5 0.2 shard_map.64.refs_6_.refs_5_
  8.7 0.0 collective-permute-done.1
  8.8 0.3 collective-permute-start.2
  9.1 0.0 collective-permute-start.4
  9.1 1.1 %collective-permute-done.4.refs_7_.refs_6_ = s32[1,128]{1,0:T(1,128)S(1)} collective-permute-done((s32[1,128]{1,0:T(1,128)S(1)}, s32[1,128]{1,0:T(1,128)S(1)}, u32[]{:S(2)}, u32[]{:S(2)}) %collective-permute-start.4) | collective-permute-done | bytes 544 | tf_op jit(solution)/shard_map/ppermute | solution.py:153
  10.2 0.0 collective-permute-done.3.refs_2_
  10.2 0.8 %collective-permute-start.5 = (bf16[16,2048]{1,0:T(8,128)(2,1)S(1)}, bf16[16,2048]{1,0:T(8,128)(2,1)S(1)}, u32[]{:S(2)}, u32[]{:S(2)}) collective-permute-start(bf16[16,2048]{1,0:T(8,128)(2,1)S(1)} %collective-permute-done.3.refs_2_), channel_id=1, source_target_pairs={{0,2},{2,0},{1,3},{3,1},{4,6},{6,4},{5,7},{7,5},{8,10},{10,8},{9,1... | collective-permute-start | bytes 196616 | tf_op jit(solution)/shard_map/ppermute | solution.py:153
  11.0 2.3 %collective-permute-done.refs_4_ = bf16[16,2048]{1,0:T(8,128)(2,1)S(1)} collective-permute-done((bf16[16,2048]{1,0:T(8,128)(2,1)S(1)}, bf16[16,2048]{1,0:T(8,128)(2,1)S(1)}, u32[]{:S(2)}, u32[]{:S(2)}) %collective-permute-start) | collective-permute-done | bytes 65568 | tf_op jit(solution)/shard_map/ppermute | solution.py:153
  13.3 0.5 %collective-permute-start.6 = (bf16[16,2048]{1,0:T(8,128)(2,1)S(1)}, bf16[16,2048]{1,0:T(8,128)(2,1)S(1)}, u32[]{:S(2)}, u32[]{:S(2)}) collective-permute-start(bf16[16,2048]{1,0:T(8,128)(2,1)S(1)} %collective-permute-done.refs_4_), channel_id=1, source_target_pairs={{0,2},{2,0},{1,3},{3,1},{4,6},{6,4},{5,7},{7,5},{8,10},{10,8},{9,1... | collective-permute-start | bytes 196616 | tf_op jit(solution)/shard_map/ppermute | solution.py:153
  13.8 0.0 copy-start.1
  13.8 1.2 %copy-done.1 = bf16[4,256,512]{2,1,0:T(8,128)(2,1)S(1)} copy-done((bf16[4,256,512]{2,1,0:T(8,128)(2,1)S(1)}, bf16[4,256,512]{2,1,0:T(8,128)(2,1)}, u32[]{:S(2)}) %copy-start.1) | copy-done | bytes 1048600
  15.0 0.0 copy-start.2
  15.0 0.8 %shard_map.65 = (bf16[4,256,256]{2,1,0:T(8,128)(2,1)S(1)}, bf16[4,256,256]{2,1,0:T(8,128)(2,1)S(1)}) custom-call(s32[1]{0:T(128)} %bitcast.half_ref.core_ref, bf16[4,256,512]{2,1,0:T(8,128)(2,1)S(1)} %copy-done.1), custom_call_target="tpu_custom_call" | custom-call | flops 536870912 | bytes 3145728 | tf_op jit(solution)/shard_map/pallas_call | solution.py:199
  15.8 0.0 collective-permute-done.5.refs_3_
  15.8 1.7 %collective-permute-done.6.refs_5_ = bf16[16,2048]{1,0:T(8,128)(2,1)S(1)} collective-permute-done((bf16[16,2048]{1,0:T(8,128)(2,1)S(1)}, bf16[16,2048]{1,0:T(8,128)(2,1)S(1)}, u32[]{:S(2)}, u32[]{:S(2)}) %collective-permute-start.6) | collective-permute-done | bytes 65568 | tf_op jit(solution)/shard_map/ppermute | solution.py:153
  17.5 0.0 collective-permute-done.2.refs_1_
  17.5 0.0 copy-done.2
  17.5 1.1 %shard_map.66.refs_0_ = f32[4,256]{1,0:T(4,128)S(1)} custom-call(s32[1]{0:T(128)} %bitcast.1.place_ref, s32[1]{0:T(128)} %bitcast.half_ref.core_ref, bf16[32,2048]{1,0:T(8,128)(2,1)S(1)} %pad_maximum_fusion.refs_0_, bf16[32,2048]{1,0:T(8,128)(2,1)S(1)} %collective-permute-done.2.refs_1_, bf16[16,2048]{1,0:T(8,128)(2,1)S(1)} %collective-permute-done.3.refs_2_, ...), custom_call_target="tpu_custom_call" | custom-call | flops 268435456 | bytes 2097152 | tf_op jit(solution)/shard_map/pallas_call | solution.py:214
  18.6 0.1 collective-permute-start.7
  18.7 1.2 %collective-permute-done.7.refs_1_ = f32[4,256]{1,0:T(4,128)S(1)} collective-permute-done((f32[4,256]{1,0:T(4,128)S(1)}, f32[4,256]{1,0:T(4,128)S(1)}, u32[]{:S(2)}, u32[]{:S(2)}) %collective-permute-start.7) | collective-permute-done | bytes 4128 | tf_op jit(solution)/shard_map/ppermute | solution.py:153
  19.9 0.0 copy-done.4
  19.9 1.4 %shard_map.67 = (bf16[32,2048]{1,0:T(8,128)(2,1)S(1)}, bf16[32,2048]{1,0:T(8,128)(2,1)S(1)}, bf16[16,2048]{1,0:T(8,128)(2,1)S(1)}, bf16[16,2048]{1,0:T(8,128)(2,...) custom-call(s32[1]{0:T(128)} %bitcast.1.place_ref, s32[1]{0:T(128)} %bitcast.half_ref.core_ref, ...), custom_call_target="tpu_custom_call" | custom-call | flops 268435456 | bytes 2097152 | tf_op jit(solution)/shard_map/pallas_call | solution.py:227
  21.3 0.6 %collective-permute-start.10 = (bf16[16,2048]{1,0:T(8,128)(2,1)S(1)}, bf16[16,2048]{1,0:T(8,128)(2,1)S(1)}, u32[]{:S(2)}, u32[]{:S(2)}) collective-permute-start(bf16[16,2048]{1,0:T(8,128)(2,1)S(1)} %get-tuple-element.28), channel_id=1, source_target_pairs={{0,2},{2,0},{1,3},{3,1},{4,6},{6,4},{5,7},{7,5},{8,10},{10,8},{9,1... | collective-permute-start | bytes 196616 | tf_op jit(solution)/shard_map/ppermute | solution.py:153
  21.9 1.5 %collective-permute-start.12 = (bf16[16,2048]{1,0:T(8,128)(2,1)S(1)}, bf16[16,2048]{1,0:T(8,128)(2,1)S(1)}, u32[]{:S(2)}, u32[]{:S(2)}) collective-permute-start(bf16[16,2048]{1,0:T(8,128)(2,1)S(1)} %get-tuple-element.30), channel_id=1, source_target_pairs={{0,2},{2,0},{1,3},{3,1},{4,6},{6,4},{5,7},{7,5},{8,10},{10,8},{9,1... | collective-permute-start | bytes 196616 | tf_op jit(solution)/shard_map/ppermute | solution.py:153
  23.4 0.1 collective-permute-start.8
  23.5 2.7 %collective-permute-done.10 = bf16[16,2048]{1,0:T(8,128)(2,1)S(1)} collective-permute-done((bf16[16,2048]{1,0:T(8,128)(2,1)S(1)}, bf16[16,2048]{1,0:T(8,128)(2,1)S(1)}, u32[]{:S(2)}, u32[]{:S(2)}) %collective-permute-start.10) | collective-permute-done | bytes 65568 | tf_op jit(solution)/shard_map/ppermute | solution.py:153
  26.2 2.0 %collective-permute-start.11 = (bf16[16,2048]{1,0:T(8,128)(2,1)S(1)}, bf16[16,2048]{1,0:T(8,128)(2,1)S(1)}, u32[]{:S(2)}, u32[]{:S(2)}) collective-permute-start(bf16[16,2048]{1,0:T(8,128)(2,1)S(1)} %add_convert_fusion.1), channel_id=1, source_target_pairs={{0,8},{4,12},{8,0},{12,4},{1,9},{5,13},{9,1},{13,5},{2,10},{6,14},... | collective-permute-start | bytes 196616 | tf_op jit(solution)/shard_map/ppermute | solution.py:153
  28.2 0.0 collective-permute-done.12
  28.2 1.4 %collective-permute-start.13 = (bf16[16,2048]{1,0:T(8,128)(2,1)S(1)}, bf16[16,2048]{1,0:T(8,128)(2,1)S(1)}, u32[]{:S(2)}, u32[]{:S(2)}) collective-permute-start(bf16[16,2048]{1,0:T(8,128)(2,1)S(1)} %add_convert_fusion), channel_id=1, source_target_pairs={{0,12},{4,8},{8,4},{12,0},{1,13},{5,9},{9,5},{13,1},{2,14},{6,10},... | collective-permute-start | bytes 196616 | tf_op jit(solution)/shard_map/ppermute | solution.py:153
  29.6 0.0 collective-permute-done.8
  29.7 0.0 copy-start.3
  29.7 1.3 %collective-permute-start.9 = (bf16[16,2048]{1,0:T(8,128)(2,1)S(1)}, bf16[16,2048]{1,0:T(8,128)(2,1)S(1)}, u32[]{:S(2)}, u32[]{:S(2)}) collective-permute-start(bf16[16,2048]{1,0:T(8,128)(2,1)S(1)} %slice.17), channel_id=1, source_target_pairs={{0,2},{2,0},{1,3},{3,1},{4,6},{6,4},{5,7},{7,5},{8,10},{10,8},{9,1... | collective-permute-start | bytes 196616 | tf_op jit(solution)/shard_map/ppermute | solution.py:153
  31.0 1.6 %collective-permute-done.11 = bf16[16,2048]{1,0:T(8,128)(2,1)S(1)} collective-permute-done((bf16[16,2048]{1,0:T(8,128)(2,1)S(1)}, bf16[16,2048]{1,0:T(8,128)(2,1)S(1)}, u32[]{:S(2)}, u32[]{:S(2)}) %collective-permute-start.11) | collective-permute-done | bytes 65568 | tf_op jit(solution)/shard_map/ppermute | solution.py:153
  32.5 1.8 %collective-permute-done.13 = bf16[16,2048]{1,0:T(8,128)(2,1)S(1)} collective-permute-done((bf16[16,2048]{1,0:T(8,128)(2,1)S(1)}, bf16[16,2048]{1,0:T(8,128)(2,1)S(1)}, u32[]{:S(2)}, u32[]{:S(2)}) %collective-permute-start.13) | collective-permute-done | bytes 65568 | tf_op jit(solution)/shard_map/ppermute | solution.py:153
  34.4 0.0 collective-permute-done.9
  34.4 0.1 collective-permute-start.14
  34.5 1.3 %collective-permute-done.14.other_ref = f32[16,2048]{1,0:T(8,128)S(1)} collective-permute-done((f32[16,2048]{1,0:T(8,128)S(1)}, f32[16,2048]{1,0:T(8,128)S(1)}, u32[]{:S(2)}, u32[]{:S(2)}) %collective-permute-start.14) | collective-permute-done | bytes 131104 | tf_op jit(solution)/shard_map/ppermute | solution.py:153
  35.8 0.0 copy-done.3
  35.8 0.7 %shard_map.68 = f32[16,4096]{1,0:T(8,128)} custom-call(s32[1]{0:T(128)} %bitcast.half_ref.core_ref, f32[16,2048]{1,0:T(8,128)S(1)} %fusion.1.mine_ref, f32[16,2048]{1,0:T(8,128)S(1)} %collective-permute-done.14.other_ref, bf16[16,4096]{1,0:T(8,128)(2,1)S(1)} %copy-done.3), custom_call_target="tpu_custom_call" | custom-call | bytes 786432 | tf_op jit(solution)/shard_map/pallas_call | solution.py:253
  (9 shorter events, 0.1 us)
Async XLA Ops:
  0.0 0.9 %copy-start = (bf16[16,4096]{1,0:T(8,128)(2,1)S(1)}, bf16[16,4096]{1,0:T(8,128)(2,1)}, u32[]{:S(2)}) copy-start(bf16[16,4096]{1,0:T(8,128)(2,1)} %param.10) | copy-start | bytes 393220
  0.9 6.9 %copy-start.6 = (s32[4,8,4]{1,2,0:T(4,128)S(1)}, s32[4,8,4]{1,2,0:T(4,128)}, u32[]{:S(2)}) copy-start(s32[4,8,4]{1,2,0:T(4,128)} %param.8) | copy-start | bytes 1540
  0.9 7.8 %collective-permute-start.1 = (bf16[16,2048]{1,0:T(8,128)(2,1)S(1)}, bf16[16,2048]{1,0:T(8,128)(2,1)S(1)}, u32[]{:S(2)}, u32[]{:S(2)}) collective-permute-start(bf16[16,2048]{1,0:T(8,128)(2,1)S(1)} %constant_dynamic-slice_fusion), channel_id=1, source_target_pairs={{0,2},{2,0},{1,3},{3,1},{4,6},{6,4},{5,7},{7,5},{8,10},{10,8},{9,1... | collective-permute-start | bytes 196616 | tf_op jit(solution)/shard_map/ppermute | solution.py:153
  3.9 6.3 %collective-permute-start.3 = (bf16[16,2048]{1,0:T(8,128)(2,1)S(1)}, bf16[16,2048]{1,0:T(8,128)(2,1)S(1)}, u32[]{:S(2)}, u32[]{:S(2)}) collective-permute-start(bf16[16,2048]{1,0:T(8,128)(2,1)S(1)} %constant_dynamic-slice_fusion), channel_id=1, source_target_pairs={{0,8},{4,12},{8,0},{12,4},{1,9},{5,13},{9,1},{13,5},{2,10},{6,14},... | collective-permute-start | bytes 196616 | tf_op jit(solution)/shard_map/ppermute | solution.py:153
  6.5 6.8 %collective-permute-start = (bf16[16,2048]{1,0:T(8,128)(2,1)S(1)}, bf16[16,2048]{1,0:T(8,128)(2,1)S(1)}, u32[]{:S(2)}, u32[]{:S(2)}) collective-permute-start(bf16[16,2048]{1,0:T(8,128)(2,1)S(1)} %constant_dynamic-slice_fusion), channel_id=1, source_target_pairs={{0,12},{4,8},{8,4},{12,0},{1,13},{5,9},{9,5},{13,1},{2,14},{6,10},... | collective-permute-start | bytes 196616 | tf_op jit(solution)/shard_map/ppermute | solution.py:153
  7.9 0.7 %copy-start.5 = (s32[1,1,8,8]{3,2,1,0:T(8,128)S(1)}, s32[1,1,8,8]{3,2,1,0:T(8,128)}, u32[]{:S(2)}) copy-start(s32[1,1,8,8]{3,2,1,0:T(8,128)} %param.9) | copy-start | bytes 772
  8.8 8.8 %collective-permute-start.2 = (bf16[32,2048]{1,0:T(8,128)(2,1)S(1)}, bf16[32,2048]{1,0:T(8,128)(2,1)S(1)}, u32[]{:S(2)}, u32[]{:S(2)}) collective-permute-start(bf16[32,2048]{1,0:T(8,128)(2,1)S(1)} %pad_maximum_fusion.refs_0_), channel_id=1, source_target_pairs={{0,4},{4,0},{8,12},{12,8},{1,5},{5,1},{9,13},{13,9},{2,6},{6,2},{1... | collective-permute-start | bytes 393224 | tf_op jit(solution)/shard_map/ppermute | solution.py:153
  9.1 1.1 %collective-permute-start.4 = (s32[1,128]{1,0:T(1,128)S(1)}, s32[1,128]{1,0:T(1,128)S(1)}, u32[]{:S(2)}, u32[]{:S(2)}) collective-permute-start(s32[1,128]{1,0:T(1,128)S(1)} %shard_map.64.refs_6_.refs_5_), channel_id=1, source_target_pairs={{0,1},{1,0},{2,3},{3,2},{4,5},{5,4},{6,7},{7,6},{8,9},{9,8},{10,11... | collective-permute-start | bytes 1544 | tf_op jit(solution)/shard_map/ppermute | solution.py:153
  10.2 5.6 %collective-permute-start.5 = (bf16[16,2048]{1,0:T(8,128)(2,1)S(1)}, bf16[16,2048]{1,0:T(8,128)(2,1)S(1)}, u32[]{:S(2)}, u32[]{:S(2)}) collective-permute-start(bf16[16,2048]{1,0:T(8,128)(2,1)S(1)} %collective-permute-done.3.refs_2_), channel_id=1, source_target_pairs={{0,2},{2,0},{1,3},{3,1},{4,6},{6,4},{5,7},{7,5},{8,10},{10,8},{9,1... | collective-permute-start | bytes 196616 | tf_op jit(solution)/shard_map/ppermute | solution.py:153
  13.3 4.3 %collective-permute-start.6 = (bf16[16,2048]{1,0:T(8,128)(2,1)S(1)}, bf16[16,2048]{1,0:T(8,128)(2,1)S(1)}, u32[]{:S(2)}, u32[]{:S(2)}) collective-permute-start(bf16[16,2048]{1,0:T(8,128)(2,1)S(1)} %collective-permute-done.refs_4_), channel_id=1, source_target_pairs={{0,2},{2,0},{1,3},{3,1},{4,6},{6,4},{5,7},{7,5},{8,10},{10,8},{9,1... | collective-permute-start | bytes 196616 | tf_op jit(solution)/shard_map/ppermute | solution.py:153
  13.8 1.2 %copy-start.1 = (bf16[4,256,512]{2,1,0:T(8,128)(2,1)S(1)}, bf16[4,256,512]{2,1,0:T(8,128)(2,1)}, u32[]{:S(2)}) copy-start(bf16[4,256,512]{2,1,0:T(8,128)(2,1)} %refs_3_.1) | copy-start | bytes 3145732
  15.0 2.5 %copy-start.2 = (bf16[4,256,512]{2,1,0:T(8,128)(2,1)S(1)}, bf16[4,256,512]{2,1,0:T(8,128)(2,1)}, u32[]{:S(2)}) copy-start(bf16[4,256,512]{2,1,0:T(8,128)(2,1)} %refs_3_.1) | copy-start | bytes 3145732
  17.5 2.3 %copy-start.4 = (f32[4,256]{1,0:T(4,128)S(1)}, f32[4,256]{1,0:T(4,128)}, u32[]{:S(2)}) copy-start(f32[4,256]{1,0:T(4,128)} %refs_2_.1) | copy-start | bytes 12292
  18.6 1.2 %collective-permute-start.7 = (f32[4,256]{1,0:T(4,128)S(1)}, f32[4,256]{1,0:T(4,128)S(1)}, u32[]{:S(2)}, u32[]{:S(2)}) collective-permute-start(f32[4,256]{1,0:T(4,128)S(1)} %shard_map.66.refs_0_), channel_id=1, source_target_pairs={{0,1},{1,0},{2,3},{3,2},{4,5},{5,4},{6,7},{7,6},{8,9},{9,8},{10,11... | collective-permute-start | bytes 12296 | tf_op jit(solution)/shard_map/ppermute | solution.py:153
  21.3 4.9 %collective-permute-start.10 = (bf16[16,2048]{1,0:T(8,128)(2,1)S(1)}, bf16[16,2048]{1,0:T(8,128)(2,1)S(1)}, u32[]{:S(2)}, u32[]{:S(2)}) collective-permute-start(bf16[16,2048]{1,0:T(8,128)(2,1)S(1)} %get-tuple-element.28), channel_id=1, source_target_pairs={{0,2},{2,0},{1,3},{3,1},{4,6},{6,4},{5,7},{7,5},{8,10},{10,8},{9,1... | collective-permute-start | bytes 196616 | tf_op jit(solution)/shard_map/ppermute | solution.py:153
  21.9 6.3 %collective-permute-start.12 = (bf16[16,2048]{1,0:T(8,128)(2,1)S(1)}, bf16[16,2048]{1,0:T(8,128)(2,1)S(1)}, u32[]{:S(2)}, u32[]{:S(2)}) collective-permute-start(bf16[16,2048]{1,0:T(8,128)(2,1)S(1)} %get-tuple-element.30), channel_id=1, source_target_pairs={{0,2},{2,0},{1,3},{3,1},{4,6},{6,4},{5,7},{7,5},{8,10},{10,8},{9,1... | collective-permute-start | bytes 196616 | tf_op jit(solution)/shard_map/ppermute | solution.py:153
  23.4 6.2 %collective-permute-start.8 = (bf16[32,2048]{1,0:T(8,128)(2,1)S(1)}, bf16[32,2048]{1,0:T(8,128)(2,1)S(1)}, u32[]{:S(2)}, u32[]{:S(2)}) collective-permute-start(bf16[32,2048]{1,0:T(8,128)(2,1)S(1)} %get-tuple-element.26), channel_id=1, source_target_pairs={{0,4},{4,0},{8,12},{12,8},{1,5},{5,1},{9,13},{13,9},{2,6},{6,2},{1... | collective-permute-start | bytes 393224 | tf_op jit(solution)/shard_map/ppermute | solution.py:153
  26.2 6.3 %collective-permute-start.11 = (bf16[16,2048]{1,0:T(8,128)(2,1)S(1)}, bf16[16,2048]{1,0:T(8,128)(2,1)S(1)}, u32[]{:S(2)}, u32[]{:S(2)}) collective-permute-start(bf16[16,2048]{1,0:T(8,128)(2,1)S(1)} %add_convert_fusion.1), channel_id=1, source_target_pairs={{0,8},{4,12},{8,0},{12,4},{1,9},{5,13},{9,1},{13,5},{2,10},{6,14},... | collective-permute-start | bytes 196616 | tf_op jit(solution)/shard_map/ppermute | solution.py:153
  28.2 6.1 %collective-permute-start.13 = (bf16[16,2048]{1,0:T(8,128)(2,1)S(1)}, bf16[16,2048]{1,0:T(8,128)(2,1)S(1)}, u32[]{:S(2)}, u32[]{:S(2)}) collective-permute-start(bf16[16,2048]{1,0:T(8,128)(2,1)S(1)} %add_convert_fusion), channel_id=1, source_target_pairs={{0,12},{4,8},{8,4},{12,0},{1,13},{5,9},{9,5},{13,1},{2,14},{6,10},... | collective-permute-start | bytes 196616 | tf_op jit(solution)/shard_map/ppermute | solution.py:153
  29.7 6.1 %copy-start.3 = (bf16[16,4096]{1,0:T(8,128)(2,1)S(1)}, bf16[16,4096]{1,0:T(8,128)(2,1)}, u32[]{:S(2)}) copy-start(bf16[16,4096]{1,0:T(8,128)(2,1)} %core_ref.1) | copy-start | bytes 393220
  29.7 4.7 %collective-permute-start.9 = (bf16[16,2048]{1,0:T(8,128)(2,1)S(1)}, bf16[16,2048]{1,0:T(8,128)(2,1)S(1)}, u32[]{:S(2)}, u32[]{:S(2)}) collective-permute-start(bf16[16,2048]{1,0:T(8,128)(2,1)S(1)} %slice.17), channel_id=1, source_target_pairs={{0,2},{2,0},{1,3},{3,1},{4,6},{6,4},{5,7},{7,5},{8,10},{10,8},{9,1... | collective-permute-start | bytes 196616 | tf_op jit(solution)/shard_map/ppermute | solution.py:153
  34.4 1.4 %collective-permute-start.14 = (f32[16,2048]{1,0:T(8,128)S(1)}, f32[16,2048]{1,0:T(8,128)S(1)}, u32[]{:S(2)}, u32[]{:S(2)}) collective-permute-start(f32[16,2048]{1,0:T(8,128)S(1)} %fusion.1.mine_ref), channel_id=1, source_target_pairs={{0,1},{1,0},{2,3},{3,2},{4,5},{5,4},{6,7},{7,6},{8,9},{9,8},{10,11... | collective-permute-start | bytes 393224 | tf_op jit(solution)/shard_map/ppermute | solution.py:153

commit v12 on v11

--- a/solution.py
+++ b/solution.py
@@ -10,6 +10,7 @@
 GO = 64
 VMEM_LIMIT = 50 * 1024 * 1024
 NT = (((1,), (1,)), ((), ()))
+TN = (((0,), (0,)), ((), ()))
 
 
 def split_dot(left, right, dims=None):
@@ -18,7 +19,14 @@
     return lax.dot_general(left, right, dims, preferred_element_type=jnp.float32)
 
 
-def prepare_kernel(half_ref, values_ref, left_ref, left_t_ref):
+def three_parts(values):
+    top = values.astype(jnp.bfloat16)
+    left = values - top.astype(jnp.float32)
+    middle = left.astype(jnp.bfloat16)
+    return top, middle, (left - middle.astype(jnp.float32)).astype(jnp.bfloat16)
+
+
+def prepare_kernel(place_ref, half_ref, values_ref, own_ref, other_ref, left_ref, left_t_ref, pick_ref, put_ref):
     batches, points, columns = values_ref.shape
     groups = columns // GO
     kept = left_ref.shape[2]
@@ -30,6 +38,9 @@
     for t in range(batches):
         left_ref[t] = split_dot(values_ref[t], select, NT).astype(jnp.bfloat16)
         left_t_ref[t] = split_dot(select, values_ref[t], NT).astype(jnp.bfloat16)
+    hot = row_table(place_ref, half_ref, own_ref, other_ref, put_ref.shape[0])
+    put_ref[...] = hot.astype(jnp.bfloat16)
+    pick_ref[...] = hot.T.astype(jnp.bfloat16)
 
 
 def index_kernel(held, fetch_ref, slots_ref, rows_ref):
@@ -45,63 +56,67 @@
     rows_ref[...] = jnp.sum(chosen, axis=0, keepdims=True) + owner * held
 
 
-def row_table(place_ref, core_ref, own_ref, other_ref, held, owners):
+def row_table(place_ref, core_ref, own_ref, other_ref, table_rows):
     low = core_ref[0] == 0
     rows = jnp.concatenate(
         [jnp.where(low, own_ref[...], other_ref[...]), jnp.where(low, other_ref[...], own_ref[...])], axis=1
     )
-    rows = lax.bitwise_xor(rows, place_ref[0] * held)
-    row = lax.broadcasted_iota(jnp.int32, (owners * held, rows.shape[1]), 0)
+    rows = lax.bitwise_xor(rows, place_ref[0])
+    row = lax.broadcasted_iota(jnp.int32, (table_rows, rows.shape[1]), 0)
     return jnp.where(row == rows, 1.0, 0.0)
 
 
-def density_kernel(places, place_ref, core_ref, *refs):
+def density_kernel(places, *refs):
     piece_refs = refs[:len(places)]
-    own_ref, other_ref, left_ref, values_ref, out_ref, table, dense = refs[len(places):]
+    pick_ref, left_ref, values_ref, out_ref, table, dense = refs[len(places):]
     batches, points, columns = values_ref.shape
     groups = columns // GO
     owners = sum(len(blocks) for blocks in places)
     held = table.shape[0] // owners
     for ref, blocks in zip(piece_refs, places):
         table[blocks[0] * held:(blocks[-1] + 1) * held, :] = ref[...]
-    pick = row_table(place_ref, core_ref, own_ref, other_ref, held, owners).T.astype(jnp.bfloat16)
     low = lax.broadcasted_iota(jnp.int32, (1, 1, 1, groups, 128), 4) < GO
-    for j in range(table.shape[1] // 128):
-        lanes = slice(j * 128, (j + 1) * 128)
-        got = split_dot(pick, table[:, lanes])
-        got = got.reshape(2, batches, groups // 4, 2, groups, 128)
-        even, odd = got[:, :, :, 0], got[:, :, :, 1]
-        first = jnp.where(low, even, pltpu.roll(odd, GO, 4))
-        second = jnp.where(low, pltpu.roll(even, GO, 4), odd)
-        for t in range(batches):
-            for q in range(groups // 2):
-                at = (q // (groups // 4), t, q % (groups // 4))
-                both = jnp.concatenate([first[at], second[at]], axis=0)
-                dense[t, j * 2 * groups:(j + 1) * 2 * groups, q * 128:(q + 1) * 128] = both.astype(jnp.bfloat16)
+    for chunk in range(table.shape[1] // 256):
+        wide = split_dot(pick_ref[...], table[:, chunk * 256:(chunk + 1) * 256])
+        for j in (2 * chunk, 2 * chunk + 1):
+            got = wide[:, (j % 2) * 128:(j % 2 + 1) * 128].reshape(2, batches, groups // 4, 2, groups, 128)
+            even, odd = got[:, :, :, 0], got[:, :, :, 1]
+            first = jnp.where(low, even, pltpu.roll(odd, GO, 4))
+            second = jnp.where(low, pltpu.roll(even, GO, 4), odd)
+            for t in range(batches):
+                for q in range(groups // 2):
+                    at = (q // (groups // 4), t, q % (groups // 4))
+                    both = jnp.concatenate([first[at], second[at]], axis=0)
+                    dense[t, j * 2 * groups:(j + 1) * 2 * groups, q * 128:(q + 1) * 128] = both.astype(jnp.bfloat16)
+    ones = jnp.ones((8, 128), jnp.bfloat16)
     for t in range(batches):
         product = split_dot(left_ref[t], dense[t]) * values_ref[t].astype(jnp.float32)
         folded = product[:, :128]
         for q in range(1, columns // 128):
             folded = folded + product[:, q * 128:(q + 1) * 128]
-        out_ref[t:t + 1, :] = jnp.sum(folded.T, axis=0, keepdims=True)
-
-
-def scatter_kernel(places, place_ref, core_ref, *refs):
-    mine_ref, far_ref, weight_ref, values_ref, left_t_ref, own_ref, other_ref = refs[:7]
-    out_refs = refs[7:-2]
+        top, middle, last = [split_dot(ones, part, NT) for part in three_parts(folded)]
+        out_ref[t:t + 1, :] = (top + middle + last)[:1]
+
+
+def scatter_kernel(places, *refs):
+    mine_ref, far_ref, weight_ref, values_ref, left_t_ref, put_ref = refs[:6]
+    out_refs = refs[6:-2]
     high, rest = refs[-2:]
     target = {k: (ref, i) for ref, blocks in zip(out_refs, places) for i, k in enumerate(blocks)}
     pieces = len(target)
     held = out_refs[0].shape[0] // len(places[0])
-    put = row_table(place_ref, core_ref, own_ref, other_ref, held, pieces).astype(jnp.bfloat16)
     batches, points, columns = values_ref.shape
     groups = columns // GO
     kept = left_t_ref.shape[1]
     steps = kept // (2 * groups)
     potential = weight_ref[...] * jnp.tanh(mine_ref[...] + far_ref[...])
     low = lax.broadcasted_iota(jnp.int32, (1, groups, 128), 2) < GO
+    row = lax.broadcasted_iota(jnp.int32, (8, points), 0)
+    ones = jnp.ones((8, 128), jnp.bfloat16)
     for t in range(batches):
-        factor = jnp.broadcast_to(potential[t:t + 1, :], (128, points)).T
+        top, middle, last = [part.astype(jnp.float32) for part in three_parts(potential[t:t + 1, :])]
+        stacked = jnp.where(row == 0, top, jnp.where(row == 1, middle, jnp.where(row == 2, last, 0.0)))
+        factor = split_dot(stacked.astype(jnp.bfloat16), ones, TN)
         factor = jnp.concatenate([factor] * (columns // 128), axis=1)
         weighted = (values_ref[t].astype(jnp.float32) * factor).astype(jnp.bfloat16)
         part = split_dot(left_t_ref[t], weighted)
@@ -119,7 +134,7 @@
                 rest[at:at + 2 * groups, j * 128:(j + 1) * 128] = (both - top.astype(jnp.float32)).astype(jnp.bfloat16)
     step = max(1, min(pieces, 128 // held))
     for k in range(0, pieces, step):
-        some = put[k * held:(k + step) * held, :]
+        some = put_ref[k * held:(k + step) * held, :]
         total = split_dot(some, high[...]) + split_dot(some, rest[...])
         for i in range(step):
             ref, at = target[k + i]
@@ -196,30 +211,30 @@
             places.append([dz * rows_x + dx])
 
     half_at, _ = lax.optimization_barrier((half.reshape(1).astype(jnp.int32), direct[far[-1]]))
-    left, left_t = call(
+    place = ((z * rows_x + x) * held).reshape(1).astype(jnp.int32)
+    left, left_t, pick, put = call(
         prepare_kernel,
         (
             jax.ShapeDtypeStruct((batches, points, kept), bf16),
             jax.ShapeDtypeStruct((batches, kept, points), bf16),
+            jax.ShapeDtypeStruct((entries, table_rows), bf16),
+            jax.ShapeDtypeStruct((table_rows, entries), bf16),
         ),
-        1,
-        scalars=1,
+        3,
+        scalars=2,
         flops=4 * batches * points * columns * kept,
         moved=3 * batches * points * columns * 2,
-    )(half_at, basis_values)
-
-    place = (z * rows_x + x).reshape(1).astype(jnp.int32)
-    core_at = half.reshape(1).astype(jnp.int32)
+    )(place, half_at, basis_values, own_rows, other_rows)
+
 
     partial = call(
         functools.partial(density_kernel, places),
         jax.ShapeDtypeStruct((batches, points), f32),
-        len(arrays) + 4,
-        scalars=2,
+        len(arrays) + 3,
         scratch=(pltpu.VMEM((table_rows, wide), bf16), pltpu.VMEM((batches, kept, columns), bf16)),
         flops=2 * batches * points * columns * kept,
         moved=2 * batches * points * columns * 2,
-    )(place, core_at, *arrays, own_rows, other_rows, left, basis_values)
+    )(*arrays, pick, left, basis_values)
     partial_other = swap(partial, "orb", 2, 1)
 
     out_places = [list(range(dz * rows_x, (dz + 1) * rows_x)) for dz in [0] + near]
@@ -227,12 +242,11 @@
     sums = call(
         functools.partial(scatter_kernel, out_places),
         [jax.ShapeDtypeStruct((held * len(blocks), wide), bf16) for blocks in out_places],
-        7,
-        scalars=2,
+        6,
         scratch=(pltpu.VMEM((entries, wide), bf16), pltpu.VMEM((entries, wide), bf16)),
         flops=2 * batches * points * columns * kept,
         moved=2 * batches * points * columns * 2,
-    )(place, core_at, partial, partial_other, point_weights, basis_values, left_t, own_rows, other_rows)
+    )(partial, partial_other, point_weights, basis_values, left_t, put)
 
     clusters, singles = sums[:len(near) + 1], sums[len(near) + 1:]
     landed = []

time: 36.8 us -> 37.6 us (1.022)
  Pallas kernels: 4.19 us -> 5.05 us
    pallas_call x1, Pallas kernels: 1.1 us -> 1.57 us  [per_device(): call(functools.partial(density_kernel, places), jax.ShapeDtypeStruct((bat...]
    pallas_call x1, Pallas kernels: 1.4 us -> 1.79 us  [per_device(): call(functools.partial(scatter_kernel, out_places), [jax.ShapeDtypeStruct...]
where the time goes in v12:
time: 37.6 us; the launch traced here: 37.4 us
  starting transfers between devices  15.5 us (41%)
  waiting for transfers between devices  13.8 us (37%)
  Pallas kernels  5.05 us (13%)
  local copies, waits for them, and re-layouts  2.84 us (8%)
    ppermute x15, starting transfers between devices, swap(): return lax.ppermute(array, axis, [(i, i ^ step) for i in range(count)])  15.5 us
    ppermute x15, waiting for transfers between devices, swap(): return lax.ppermute(array, axis, [(i, i ^ step) for i in range(count)])  13.8 us
    unnamed x14, local copies, waits for them, and re-layouts  2.74 us
    pallas_call x1, Pallas kernels, per_device(): call(functools.partial(scatter_kernel, out_places), [jax.ShapeDtypeStruct...  1.79 us
    pallas_call x1, Pallas kernels, per_device(): call(functools.partial(density_kernel, places), jax.ShapeDtypeStruct((bat...  1.57 us
    pallas_call x1, Pallas kernels, per_device(): call(prepare_kernel, (jax.ShapeDtypeStruct((batches, points, kept), bf16)...  0.77 us
  transfers between devices with their start and end apart: 15, of which 8 were waited for; matrix products, arithmetic and copies ran while one was open for 0% of the time, Pallas kernels for 3%

profile of v12, /device:TPU:0, one launch (start us, length us, event | category | flops | bytes accessed | tf_op | source)
XLA Modules:
  0.0 37.4 jit_solution(10086453272694152754)
XLA Ops:
  0.0 0.0 copy-start
  0.0 0.9 %copy-done = bf16[16,4096]{1,0:T(8,128)(2,1)S(1)} copy-done((bf16[16,4096]{1,0:T(8,128)(2,1)S(1)}, bf16[16,4096]{1,0:T(8,128)(2,1)}, u32[]{:S(2)}) %copy-start) | copy-done | bytes 131096
  0.9 0.0 copy-start.6
  0.9 3.0 %collective-permute-start.1 = (bf16[16,2048]{1,0:T(8,128)(2,1)S(1)}, bf16[16,2048]{1,0:T(8,128)(2,1)S(1)}, u32[]{:S(2)}, u32[]{:S(2)}) collective-permute-start(bf16[16,2048]{1,0:T(8,128)(2,1)S(1)} %constant_dynamic-slice_fusion), channel_id=1, source_target_pairs={{0,2},{2,0},{1,3},{3,1},{4,6},{6,4},{5,7},{7,5},{8,10},{10,8},{9,1... | collective-permute-start | bytes 196616 | tf_op jit(solution)/shard_map/ppermute | solution.py:168
  3.9 2.6 %collective-permute-start.3 = (bf16[16,2048]{1,0:T(8,128)(2,1)S(1)}, bf16[16,2048]{1,0:T(8,128)(2,1)S(1)}, u32[]{:S(2)}, u32[]{:S(2)}) collective-permute-start(bf16[16,2048]{1,0:T(8,128)(2,1)S(1)} %constant_dynamic-slice_fusion), channel_id=1, source_target_pairs={{0,8},{4,12},{8,0},{12,4},{1,9},{5,13},{9,1},{13,5},{2,10},{6,14},... | collective-permute-start | bytes 196616 | tf_op jit(solution)/shard_map/ppermute | solution.py:168
  6.5 1.3 %collective-permute-start = (bf16[16,2048]{1,0:T(8,128)(2,1)S(1)}, bf16[16,2048]{1,0:T(8,128)(2,1)S(1)}, u32[]{:S(2)}, u32[]{:S(2)}) collective-permute-start(bf16[16,2048]{1,0:T(8,128)(2,1)S(1)} %constant_dynamic-slice_fusion), channel_id=1, source_target_pairs={{0,12},{4,8},{8,4},{12,0},{1,13},{5,9},{9,5},{13,1},{2,14},{6,10},... | collective-permute-start | bytes 196616 | tf_op jit(solution)/shard_map/ppermute | solution.py:168
  7.9 0.0 copy-done.6
  7.9 0.0 copy-start.5
  7.9 0.1 reshape.14.slots_ref
  7.9 0.6 %copy-done.5 = s32[1,1,8,8]{3,2,1,0:T(8,128)S(1)} copy-done((s32[1,1,8,8]{3,2,1,0:T(8,128)S(1)}, s32[1,1,8,8]{3,2,1,0:T(8,128)}, u32[]{:S(2)}) %copy-start.5) | copy-done | bytes 280
  8.5 0.2 shard_map.64.own_ref
  8.7 0.0 collective-permute-done.1
  8.8 0.3 collective-permute-start.2
  9.1 0.0 collective-permute-start.4
  9.1 1.1 %collective-permute-done.4.other_ref = s32[1,128]{1,0:T(1,128)S(1)} collective-permute-done((s32[1,128]{1,0:T(1,128)S(1)}, s32[1,128]{1,0:T(1,128)S(1)}, u32[]{:S(2)}, u32[]{:S(2)}) %collective-permute-start.4) | collective-permute-done | bytes 544 | tf_op jit(solution)/shard_map/ppermute | solution.py:168
  10.2 0.0 collective-permute-done.3.refs_2_
  10.2 0.8 %collective-permute-start.5 = (bf16[16,2048]{1,0:T(8,128)(2,1)S(1)}, bf16[16,2048]{1,0:T(8,128)(2,1)S(1)}, u32[]{:S(2)}, u32[]{:S(2)}) collective-permute-start(bf16[16,2048]{1,0:T(8,128)(2,1)S(1)} %collective-permute-done.3.refs_2_), channel_id=1, source_target_pairs={{0,2},{2,0},{1,3},{3,1},{4,6},{6,4},{5,7},{7,5},{8,10},{10,8},{9,1... | collective-permute-start | bytes 196616 | tf_op jit(solution)/shard_map/ppermute | solution.py:168
  11.0 2.3 %collective-permute-done.refs_4_ = bf16[16,2048]{1,0:T(8,128)(2,1)S(1)} collective-permute-done((bf16[16,2048]{1,0:T(8,128)(2,1)S(1)}, bf16[16,2048]{1,0:T(8,128)(2,1)S(1)}, u32[]{:S(2)}, u32[]{:S(2)}) %collective-permute-start) | collective-permute-done | bytes 65568 | tf_op jit(solution)/shard_map/ppermute | solution.py:168
  13.3 0.5 %collective-permute-start.6 = (bf16[16,2048]{1,0:T(8,128)(2,1)S(1)}, bf16[16,2048]{1,0:T(8,128)(2,1)S(1)}, u32[]{:S(2)}, u32[]{:S(2)}) collective-permute-start(bf16[16,2048]{1,0:T(8,128)(2,1)S(1)} %collective-permute-done.refs_4_), channel_id=1, source_target_pairs={{0,2},{2,0},{1,3},{3,1},{4,6},{6,4},{5,7},{7,5},{8,10},{10,8},{9,1... | collective-permute-start | bytes 196616 | tf_op jit(solution)/shard_map/ppermute | solution.py:168
  13.8 0.0 copy-start.1
  13.8 1.2 %copy-done.1 = bf16[4,256,512]{2,1,0:T(8,128)(2,1)S(1)} copy-done((bf16[4,256,512]{2,1,0:T(8,128)(2,1)S(1)}, bf16[4,256,512]{2,1,0:T(8,128)(2,1)}, u32[]{:S(2)}) %copy-start.1) | copy-done | bytes 1048600
  15.0 0.8 %shard_map.65 = (bf16[4,256,256]{2,1,0:T(8,128)(2,1)S(1)}, bf16[4,256,256]{2,1,0:T(8,128)(2,1)S(1)}, bf16[256,128]{1,0:T(8,128)(2,1)S(1)}, bf16[128,256]{1,0:T(8,128)(2,1)S(1)}) custom-call(s32[1]{0:T(128)} %bitcast.3.place_ref, s32[1]{0:T(128)} %bitcast.half_ref, bf16[4,256,512]{2,1,0:T(8,128)(2,1)S(1)} %copy-done.1, s32[1,128]{1,0:T(1,128)S(1)} %shard_map.64.own_ref, ...), custom_call_target="tpu_custom_call" | custom-call | flops 536870912 | bytes 3145728 | tf_op jit(solution)/shard_map/pallas_call | solution.py:215
  15.8 0.0 collective-permute-done.5.refs_3_
  15.8 1.7 %collective-permute-done.6.refs_5_ = bf16[16,2048]{1,0:T(8,128)(2,1)S(1)} collective-permute-done((bf16[16,2048]{1,0:T(8,128)(2,1)S(1)}, bf16[16,2048]{1,0:T(8,128)(2,1)S(1)}, u32[]{:S(2)}, u32[]{:S(2)}) %collective-permute-start.6) | collective-permute-done | bytes 65568 | tf_op jit(solution)/shard_map/ppermute | solution.py:168
  17.5 0.0 collective-permute-done.2.refs_1_
  17.5 0.0 copy-done.2
  17.5 1.6 %shard_map.66.refs_0_ = f32[4,256]{1,0:T(4,128)S(1)} custom-call(bf16[32,2048]{1,0:T(8,128)(2,1)S(1)} %pad_maximum_fusion.refs_0_, bf16[32,2048]{1,0:T(8,128)(2,1)S(1)} %collective-permute-done.2.refs_1_, bf16[16,2048]{1,0:T(8,128)(2,1)S(1)} %collective-permute-done.3.refs_2_, bf16[16,2048]{1,0:T(8,128)(2,1)S(1)} %collective-permute-done.5.refs_3_, ...), custom_call_target="tpu_custom_call" | custom-call | flops 268435456 | bytes 2097152 | tf_op jit(solution)/shard_map/pallas_call | solution.py:230
  19.1 0.0 collective-permute-start.7
  19.1 1.2 %collective-permute-done.7.refs_1_ = f32[4,256]{1,0:T(4,128)S(1)} collective-permute-done((f32[4,256]{1,0:T(4,128)S(1)}, f32[4,256]{1,0:T(4,128)S(1)}, u32[]{:S(2)}, u32[]{:S(2)}) %collective-permute-start.7) | collective-permute-done | bytes 4128 | tf_op jit(solution)/shard_map/ppermute | solution.py:168
  20.3 0.0 copy-done.4
  20.4 1.8 %shard_map.67 = (bf16[32,2048]{1,0:T(8,128)(2,1)S(1)}, bf16[32,2048]{1,0:T(8,128)(2,1)S(1)}, bf16[16,2048]{1,0:T(8,128)(2,1)S(1)}, bf16[16,2048]{1,0:T(8,128)(2,...) custom-call(f32[4,256]{1,0:T(4,128)S(1)} %shard_map.66.refs_0_, ...), custom_call_target="tpu_custom_call" | custom-call | flops 268435456 | bytes 2097152 | tf_op jit(solution)/shard_map/pallas_call | solution.py:242
  22.2 0.6 %collective-permute-start.10 = (bf16[16,2048]{1,0:T(8,128)(2,1)S(1)}, bf16[16,2048]{1,0:T(8,128)(2,1)S(1)}, u32[]{:S(2)}, u32[]{:S(2)}) collective-permute-start(bf16[16,2048]{1,0:T(8,128)(2,1)S(1)} %get-tuple-element.32), channel_id=1, source_target_pairs={{0,2},{2,0},{1,3},{3,1},{4,6},{6,4},{5,7},{7,5},{8,10},{10,8},{9,1... | collective-permute-start | bytes 196616 | tf_op jit(solution)/shard_map/ppermute | solution.py:168
  22.8 1.5 %collective-permute-start.12 = (bf16[16,2048]{1,0:T(8,128)(2,1)S(1)}, bf16[16,2048]{1,0:T(8,128)(2,1)S(1)}, u32[]{:S(2)}, u32[]{:S(2)}) collective-permute-start(bf16[16,2048]{1,0:T(8,128)(2,1)S(1)} %get-tuple-element.34), channel_id=1, source_target_pairs={{0,2},{2,0},{1,3},{3,1},{4,6},{6,4},{5,7},{7,5},{8,10},{10,8},{9,1... | collective-permute-start | bytes 196616 | tf_op jit(solution)/shard_map/ppermute | solution.py:168
  24.2 0.1 collective-permute-start.8
  24.4 2.7 %collective-permute-done.10 = bf16[16,2048]{1,0:T(8,128)(2,1)S(1)} collective-permute-done((bf16[16,2048]{1,0:T(8,128)(2,1)S(1)}, bf16[16,2048]{1,0:T(8,128)(2,1)S(1)}, u32[]{:S(2)}, u32[]{:S(2)}) %collective-permute-start.10) | collective-permute-done | bytes 65568 | tf_op jit(solution)/shard_map/ppermute | solution.py:168
  27.1 2.0 %collective-permute-start.11 = (bf16[16,2048]{1,0:T(8,128)(2,1)S(1)}, bf16[16,2048]{1,0:T(8,128)(2,1)S(1)}, u32[]{:S(2)}, u32[]{:S(2)}) collective-permute-start(bf16[16,2048]{1,0:T(8,128)(2,1)S(1)} %add_convert_fusion.1), channel_id=1, source_target_pairs={{0,8},{4,12},{8,0},{12,4},{1,9},{5,13},{9,1},{13,5},{2,10},{6,14},... | collective-permute-start | bytes 196616 | tf_op jit(solution)/shard_map/ppermute | solution.py:168
  29.1 0.0 collective-permute-done.12
  29.1 1.4 %collective-permute-start.13 = (bf16[16,2048]{1,0:T(8,128)(2,1)S(1)}, bf16[16,2048]{1,0:T(8,128)(2,1)S(1)}, u32[]{:S(2)}, u32[]{:S(2)}) collective-permute-start(bf16[16,2048]{1,0:T(8,128)(2,1)S(1)} %add_convert_fusion), channel_id=1, source_target_pairs={{0,12},{4,8},{8,4},{12,0},{1,13},{5,9},{9,5},{13,1},{2,14},{6,10},... | collective-permute-start | bytes 196616 | tf_op jit(solution)/shard_map/ppermute | solution.py:168
  30.5 0.0 collective-permute-done.8
  30.5 0.0 copy-start.3
  30.6 1.3 %collective-permute-start.9 = (bf16[16,2048]{1,0:T(8,128)(2,1)S(1)}, bf16[16,2048]{1,0:T(8,128)(2,1)S(1)}, u32[]{:S(2)}, u32[]{:S(2)}) collective-permute-start(bf16[16,2048]{1,0:T(8,128)(2,1)S(1)} %slice.17), channel_id=1, source_target_pairs={{0,2},{2,0},{1,3},{3,1},{4,6},{6,4},{5,7},{7,5},{8,10},{10,8},{9,1... | collective-permute-start | bytes 196616 | tf_op jit(solution)/shard_map/ppermute | solution.py:168
  31.8 1.6 %collective-permute-done.11 = bf16[16,2048]{1,0:T(8,128)(2,1)S(1)} collective-permute-done((bf16[16,2048]{1,0:T(8,128)(2,1)S(1)}, bf16[16,2048]{1,0:T(8,128)(2,1)S(1)}, u32[]{:S(2)}, u32[]{:S(2)}) %collective-permute-start.11) | collective-permute-done | bytes 65568 | tf_op jit(solution)/shard_map/ppermute | solution.py:168
  33.4 1.8 %collective-permute-done.13 = bf16[16,2048]{1,0:T(8,128)(2,1)S(1)} collective-permute-done((bf16[16,2048]{1,0:T(8,128)(2,1)S(1)}, bf16[16,2048]{1,0:T(8,128)(2,1)S(1)}, u32[]{:S(2)}, u32[]{:S(2)}) %collective-permute-start.13) | collective-permute-done | bytes 65568 | tf_op jit(solution)/shard_map/ppermute | solution.py:168
  35.2 0.0 collective-permute-done.9
  35.3 0.1 collective-permute-start.14
  35.4 1.3 %collective-permute-done.14.other_ref = f32[16,2048]{1,0:T(8,128)S(1)} collective-permute-done((f32[16,2048]{1,0:T(8,128)S(1)}, f32[16,2048]{1,0:T(8,128)S(1)}, u32[]{:S(2)}, u32[]{:S(2)}) %collective-permute-start.14) | collective-permute-done | bytes 131104 | tf_op jit(solution)/shard_map/ppermute | solution.py:168
  36.7 0.0 copy-done.3
  36.7 0.7 %shard_map.68 = f32[16,4096]{1,0:T(8,128)} custom-call(s32[1]{0:T(128)} %bitcast.half_ref, f32[16,2048]{1,0:T(8,128)S(1)} %fusion.1.mine_ref, f32[16,2048]{1,0:T(8,128)S(1)} %collective-permute-done.14.other_ref, bf16[16,4096]{1,0:T(8,128)(2,1)S(1)} %copy-done.3), custom_call_target="tpu_custom_call" | custom-call | bytes 786432 | tf_op jit(solution)/shard_map/pallas_call | solution.py:267
  (9 shorter events, 0.1 us)
Async XLA Ops:
  0.0 0.9 %copy-start = (bf16[16,4096]{1,0:T(8,128)(2,1)S(1)}, bf16[16,4096]{1,0:T(8,128)(2,1)}, u32[]{:S(2)}) copy-start(bf16[16,4096]{1,0:T(8,128)(2,1)} %param.10) | copy-start | bytes 393220
  0.9 6.9 %copy-start.6 = (s32[4,8,4]{1,2,0:T(4,128)S(1)}, s32[4,8,4]{1,2,0:T(4,128)}, u32[]{:S(2)}) copy-start(s32[4,8,4]{1,2,0:T(4,128)} %param.8) | copy-start | bytes 1540
  0.9 7.8 %collective-permute-start.1 = (bf16[16,2048]{1,0:T(8,128)(2,1)S(1)}, bf16[16,2048]{1,0:T(8,128)(2,1)S(1)}, u32[]{:S(2)}, u32[]{:S(2)}) collective-permute-start(bf16[16,2048]{1,0:T(8,128)(2,1)S(1)} %constant_dynamic-slice_fusion), channel_id=1, source_target_pairs={{0,2},{2,0},{1,3},{3,1},{4,6},{6,4},{5,7},{7,5},{8,10},{10,8},{9,1... | collective-permute-start | bytes 196616 | tf_op jit(solution)/shard_map/ppermute | solution.py:168
  3.9 6.3 %collective-permute-start.3 = (bf16[16,2048]{1,0:T(8,128)(2,1)S(1)}, bf16[16,2048]{1,0:T(8,128)(2,1)S(1)}, u32[]{:S(2)}, u32[]{:S(2)}) collective-permute-start(bf16[16,2048]{1,0:T(8,128)(2,1)S(1)} %constant_dynamic-slice_fusion), channel_id=1, source_target_pairs={{0,8},{4,12},{8,0},{12,4},{1,9},{5,13},{9,1},{13,5},{2,10},{6,14},... | collective-permute-start | bytes 196616 | tf_op jit(solution)/shard_map/ppermute | solution.py:168
  6.5 6.8 %collective-permute-start = (bf16[16,2048]{1,0:T(8,128)(2,1)S(1)}, bf16[16,2048]{1,0:T(8,128)(2,1)S(1)}, u32[]{:S(2)}, u32[]{:S(2)}) collective-permute-start(bf16[16,2048]{1,0:T(8,128)(2,1)S(1)} %constant_dynamic-slice_fusion), channel_id=1, source_target_pairs={{0,12},{4,8},{8,4},{12,0},{1,13},{5,9},{9,5},{13,1},{2,14},{6,10},... | collective-permute-start | bytes 196616 | tf_op jit(solution)/shard_map/ppermute | solution.py:168
  7.9 0.7 %copy-start.5 = (s32[1,1,8,8]{3,2,1,0:T(8,128)S(1)}, s32[1,1,8,8]{3,2,1,0:T(8,128)}, u32[]{:S(2)}) copy-start(s32[1,1,8,8]{3,2,1,0:T(8,128)} %param.9) | copy-start | bytes 772
  8.8 8.8 %collective-permute-start.2 = (bf16[32,2048]{1,0:T(8,128)(2,1)S(1)}, bf16[32,2048]{1,0:T(8,128)(2,1)S(1)}, u32[]{:S(2)}, u32[]{:S(2)}) collective-permute-start(bf16[32,2048]{1,0:T(8,128)(2,1)S(1)} %pad_maximum_fusion.refs_0_), channel_id=1, source_target_pairs={{0,4},{4,0},{8,12},{12,8},{1,5},{5,1},{9,13},{13,9},{2,6},{6,2},{1... | collective-permute-start | bytes 393224 | tf_op jit(solution)/shard_map/ppermute | solution.py:168
  9.1 1.1 %collective-permute-start.4 = (s32[1,128]{1,0:T(1,128)S(1)}, s32[1,128]{1,0:T(1,128)S(1)}, u32[]{:S(2)}, u32[]{:S(2)}) collective-permute-start(s32[1,128]{1,0:T(1,128)S(1)} %shard_map.64.own_ref), channel_id=1, source_target_pairs={{0,1},{1,0},{2,3},{3,2},{4,5},{5,4},{6,7},{7,6},{8,9},{9,8},{10,11... | collective-permute-start | bytes 1544 | tf_op jit(solution)/shard_map/ppermute | solution.py:168
  10.2 5.6 %collective-permute-start.5 = (bf16[16,2048]{1,0:T(8,128)(2,1)S(1)}, bf16[16,2048]{1,0:T(8,128)(2,1)S(1)}, u32[]{:S(2)}, u32[]{:S(2)}) collective-permute-start(bf16[16,2048]{1,0:T(8,128)(2,1)S(1)} %collective-permute-done.3.refs_2_), channel_id=1, source_target_pairs={{0,2},{2,0},{1,3},{3,1},{4,6},{6,4},{5,7},{7,5},{8,10},{10,8},{9,1... | collective-permute-start | bytes 196616 | tf_op jit(solution)/shard_map/ppermute | solution.py:168
  13.3 4.3 %collective-permute-start.6 = (bf16[16,2048]{1,0:T(8,128)(2,1)S(1)}, bf16[16,2048]{1,0:T(8,128)(2,1)S(1)}, u32[]{:S(2)}, u32[]{:S(2)}) collective-permute-start(bf16[16,2048]{1,0:T(8,128)(2,1)S(1)} %collective-permute-done.refs_4_), channel_id=1, source_target_pairs={{0,2},{2,0},{1,3},{3,1},{4,6},{6,4},{5,7},{7,5},{8,10},{10,8},{9,1... | collective-permute-start | bytes 196616 | tf_op jit(solution)/shard_map/ppermute | solution.py:168
  13.8 1.2 %copy-start.1 = (bf16[4,256,512]{2,1,0:T(8,128)(2,1)S(1)}, bf16[4,256,512]{2,1,0:T(8,128)(2,1)}, u32[]{:S(2)}) copy-start(bf16[4,256,512]{2,1,0:T(8,128)(2,1)} %refs_3_.1) | copy-start | bytes 3145732
  15.0 2.5 %copy-start.2 = (bf16[4,256,512]{2,1,0:T(8,128)(2,1)S(1)}, bf16[4,256,512]{2,1,0:T(8,128)(2,1)}, u32[]{:S(2)}) copy-start(bf16[4,256,512]{2,1,0:T(8,128)(2,1)} %refs_3_.1) | copy-start | bytes 3145732
  17.5 2.8 %copy-start.4 = (f32[4,256]{1,0:T(4,128)S(1)}, f32[4,256]{1,0:T(4,128)}, u32[]{:S(2)}) copy-start(f32[4,256]{1,0:T(4,128)} %refs_2_.1) | copy-start | bytes 12292
  19.1 1.2 %collective-permute-start.7 = (f32[4,256]{1,0:T(4,128)S(1)}, f32[4,256]{1,0:T(4,128)S(1)}, u32[]{:S(2)}, u32[]{:S(2)}) collective-permute-start(f32[4,256]{1,0:T(4,128)S(1)} %shard_map.66.refs_0_), channel_id=1, source_target_pairs={{0,1},{1,0},{2,3},{3,2},{4,5},{5,4},{6,7},{7,6},{8,9},{9,8},{10,11... | collective-permute-start | bytes 12296 | tf_op jit(solution)/shard_map/ppermute | solution.py:168
  22.2 4.9 %collective-permute-start.10 = (bf16[16,2048]{1,0:T(8,128)(2,1)S(1)}, bf16[16,2048]{1,0:T(8,128)(2,1)S(1)}, u32[]{:S(2)}, u32[]{:S(2)}) collective-permute-start(bf16[16,2048]{1,0:T(8,128)(2,1)S(1)} %get-tuple-element.32), channel_id=1, source_target_pairs={{0,2},{2,0},{1,3},{3,1},{4,6},{6,4},{5,7},{7,5},{8,10},{10,8},{9,1... | collective-permute-start | bytes 196616 | tf_op jit(solution)/shard_map/ppermute | solution.py:168
  22.8 6.3 %collective-permute-start.12 = (bf16[16,2048]{1,0:T(8,128)(2,1)S(1)}, bf16[16,2048]{1,0:T(8,128)(2,1)S(1)}, u32[]{:S(2)}, u32[]{:S(2)}) collective-permute-start(bf16[16,2048]{1,0:T(8,128)(2,1)S(1)} %get-tuple-element.34), channel_id=1, source_target_pairs={{0,2},{2,0},{1,3},{3,1},{4,6},{6,4},{5,7},{7,5},{8,10},{10,8},{9,1... | collective-permute-start | bytes 196616 | tf_op jit(solution)/shard_map/ppermute | solution.py:168
  24.2 6.3 %collective-permute-start.8 = (bf16[32,2048]{1,0:T(8,128)(2,1)S(1)}, bf16[32,2048]{1,0:T(8,128)(2,1)S(1)}, u32[]{:S(2)}, u32[]{:S(2)}) collective-permute-start(bf16[32,2048]{1,0:T(8,128)(2,1)S(1)} %get-tuple-element.30), channel_id=1, source_target_pairs={{0,4},{4,0},{8,12},{12,8},{1,5},{5,1},{9,13},{13,9},{2,6},{6,2},{1... | collective-permute-start | bytes 393224 | tf_op jit(solution)/shard_map/ppermute | solution.py:168
  27.1 6.3 %collective-permute-start.11 = (bf16[16,2048]{1,0:T(8,128)(2,1)S(1)}, bf16[16,2048]{1,0:T(8,128)(2,1)S(1)}, u32[]{:S(2)}, u32[]{:S(2)}) collective-permute-start(bf16[16,2048]{1,0:T(8,128)(2,1)S(1)} %add_convert_fusion.1), channel_id=1, source_target_pairs={{0,8},{4,12},{8,0},{12,4},{1,9},{5,13},{9,1},{13,5},{2,10},{6,14},... | collective-permute-start | bytes 196616 | tf_op jit(solution)/shard_map/ppermute | solution.py:168
  29.1 6.1 %collective-permute-start.13 = (bf16[16,2048]{1,0:T(8,128)(2,1)S(1)}, bf16[16,2048]{1,0:T(8,128)(2,1)S(1)}, u32[]{:S(2)}, u32[]{:S(2)}) collective-permute-start(bf16[16,2048]{1,0:T(8,128)(2,1)S(1)} %add_convert_fusion), channel_id=1, source_target_pairs={{0,12},{4,8},{8,4},{12,0},{1,13},{5,9},{9,5},{13,1},{2,14},{6,10},... | collective-permute-start | bytes 196616 | tf_op jit(solution)/shard_map/ppermute | solution.py:168
  30.5 6.1 %copy-start.3 = (bf16[16,4096]{1,0:T(8,128)(2,1)S(1)}, bf16[16,4096]{1,0:T(8,128)(2,1)}, u32[]{:S(2)}) copy-start(bf16[16,4096]{1,0:T(8,128)(2,1)} %core_ref.1) | copy-start | bytes 393220
  30.6 4.7 %collective-permute-start.9 = (bf16[16,2048]{1,0:T(8,128)(2,1)S(1)}, bf16[16,2048]{1,0:T(8,128)(2,1)S(1)}, u32[]{:S(2)}, u32[]{:S(2)}) collective-permute-start(bf16[16,2048]{1,0:T(8,128)(2,1)S(1)} %slice.17), channel_id=1, source_target_pairs={{0,2},{2,0},{1,3},{3,1},{4,6},{6,4},{5,7},{7,5},{8,10},{10,8},{9,1... | collective-permute-start | bytes 196616 | tf_op jit(solution)/shard_map/ppermute | solution.py:168
  35.3 1.4 %collective-permute-start.14 = (f32[16,2048]{1,0:T(8,128)S(1)}, f32[16,2048]{1,0:T(8,128)S(1)}, u32[]{:S(2)}, u32[]{:S(2)}) collective-permute-start(f32[16,2048]{1,0:T(8,128)S(1)} %fusion.1.mine_ref), channel_id=1, source_target_pairs={{0,1},{1,0},{2,3},{3,2},{4,5},{5,4},{6,7},{7,6},{8,9},{9,8},{10,11... | collective-permute-start | bytes 393224 | tf_op jit(solution)/shard_map/ppermute | solution.py:168

commit v13 on v11

--- a/solution.py
+++ b/solution.py
@@ -66,18 +66,18 @@
         table[blocks[0] * held:(blocks[-1] + 1) * held, :] = ref[...]
     pick = row_table(place_ref, core_ref, own_ref, other_ref, held, owners).T.astype(jnp.bfloat16)
     low = lax.broadcasted_iota(jnp.int32, (1, 1, 1, groups, 128), 4) < GO
-    for j in range(table.shape[1] // 128):
-        lanes = slice(j * 128, (j + 1) * 128)
-        got = split_dot(pick, table[:, lanes])
-        got = got.reshape(2, batches, groups // 4, 2, groups, 128)
-        even, odd = got[:, :, :, 0], got[:, :, :, 1]
-        first = jnp.where(low, even, pltpu.roll(odd, GO, 4))
-        second = jnp.where(low, pltpu.roll(even, GO, 4), odd)
-        for t in range(batches):
-            for q in range(groups // 2):
-                at = (q // (groups // 4), t, q % (groups // 4))
-                both = jnp.concatenate([first[at], second[at]], axis=0)
-                dense[t, j * 2 * groups:(j + 1) * 2 * groups, q * 128:(q + 1) * 128] = both.astype(jnp.bfloat16)
+    for chunk in range(table.shape[1] // 256):
+        wide = split_dot(pick, table[:, chunk * 256:(chunk + 1) * 256])
+        for j in (2 * chunk, 2 * chunk + 1):
+            got = wide[:, (j % 2) * 128:(j % 2 + 1) * 128].reshape(2, batches, groups // 4, 2, groups, 128)
+            even, odd = got[:, :, :, 0], got[:, :, :, 1]
+            first = jnp.where(low, even, pltpu.roll(odd, GO, 4))
+            second = jnp.where(low, pltpu.roll(even, GO, 4), odd)
+            for t in range(batches):
+                for q in range(groups // 2):
+                    at = (q // (groups // 4), t, q % (groups // 4))
+                    both = jnp.concatenate([first[at], second[at]], axis=0)
+                    dense[t, j * 2 * groups:(j + 1) * 2 * groups, q * 128:(q + 1) * 128] = both.astype(jnp.bfloat16)
     for t in range(batches):
         product = split_dot(left_ref[t], dense[t]) * values_ref[t].astype(jnp.float32)
         folded = product[:, :128]
@@ -182,11 +182,11 @@
     direct = {dz: swap(mine, "batch", rows_z, dz) for dz in far}
     beside = [swap(mine, "pair", rows_x, dx) for dx in side]
     *beside, own_rows = lax.optimization_barrier((*beside, own_rows))
-    cluster = jnp.concatenate([mine, *beside], axis=0)
-    arrays, places = [cluster], [list(range(rows_x))]
+    arrays, places = [mine, *beside], [[dx] for dx in range(rows_x)]
     for dz in near:
-        arrays.append(swap(cluster, "batch", rows_z, dz))
-        places.append(list(range(dz * rows_x, (dz + 1) * rows_x)))
+        for dx, piece in enumerate([mine, *beside]):
+            arrays.append(swap(piece, "batch", rows_z, dz))
+            places.append([dz * rows_x + dx])
     direct[far[0]], other_rows = lax.optimization_barrier((direct[far[0]], other_rows))
     for dz in far:
         arrays.append(direct[dz])

time: 36.8 us -> 37.5 us (1.019)
  starting transfers between devices: 15.5 us -> 17 us
  waiting for transfers between devices: 13.8 us -> 13.1 us
    ppermute x15 -> x16, starting transfers between devices: 15.5 us -> 17 us  [swap(): return lax.ppermute(array, axis, [(i, i ^ step) for i in range(count)])]
    ppermute x15 -> x16, waiting for transfers between devices: 13.8 us -> 13.1 us  [swap(): return lax.ppermute(array, axis, [(i, i ^ step) for i in range(count)])]
  transfers between devices with their start and end apart: 15 -> 16, of which waited for: 8 -> 9; matrix products, arithmetic and copies ran while one was open for 0% -> 0% of each run, Pallas kernels for 3% -> 3%
where the time goes in v13:
time: 37.5 us; the launch traced here: 37.3 us
  starting transfers between devices  17 us (45%)
  waiting for transfers between devices  13.1 us (35%)
  Pallas kernels  4.15 us (11%)
  local copies, waits for them, and re-layouts  2.84 us (8%)
    ppermute x16, starting transfers between devices, swap(): return lax.ppermute(array, axis, [(i, i ^ step) for i in range(count)])  17 us
    ppermute x16, waiting for transfers between devices, swap(): return lax.ppermute(array, axis, [(i, i ^ step) for i in range(count)])  13.1 us
    unnamed x14, local copies, waits for them, and re-layouts  2.74 us
    pallas_call x1, Pallas kernels, per_device(): call(functools.partial(scatter_kernel, out_places), [jax.ShapeDtypeStruct...  1.4 us
    pallas_call x1, Pallas kernels, per_device(): call(functools.partial(density_kernel, places), jax.ShapeDtypeStruct((bat...  1.06 us
    pallas_call x1, Pallas kernels, per_device(): call(prepare_kernel, (jax.ShapeDtypeStruct((batches, points, kept), bf16)...  0.76 us
  transfers between devices with their start and end apart: 16, of which 9 were waited for; matrix products, arithmetic and copies ran while one was open for 0% of the time, Pallas kernels for 3%

profile of v13, /device:TPU:0, one launch (start us, length us, event | category | flops | bytes accessed | tf_op | source)
XLA Modules:
  0.0 37.3 jit_solution(14251738545891712763)
XLA Ops:
  0.0 0.0 copy-start
  0.0 0.9 %copy-done = bf16[16,4096]{1,0:T(8,128)(2,1)S(1)} copy-done((bf16[16,4096]{1,0:T(8,128)(2,1)S(1)}, bf16[16,4096]{1,0:T(8,128)(2,1)}, u32[]{:S(2)}) %copy-start) | copy-done | bytes 131096
  0.9 0.0 copy-start.6
  0.9 4.1 %collective-permute-start.4 = (bf16[16,2048]{1,0:T(8,128)(2,1)S(1)}, bf16[16,2048]{1,0:T(8,128)(2,1)S(1)}, u32[]{:S(2)}, u32[]{:S(2)}) collective-permute-start(bf16[16,2048]{1,0:T(8,128)(2,1)S(1)} %constant_dynamic-slice_fusion.refs_0_), channel_id=1, source_target_pairs={{0,8},{4,12},{8,0},{12,4},{1,9},{5,13},{9,1},{13,5},{2,10},{6,14},... | collective-permute-start | bytes 196616 | tf_op jit(solution)/shard_map/ppermute | solution.py:153
  5.0 1.5 %collective-permute-start.1 = (bf16[16,2048]{1,0:T(8,128)(2,1)S(1)}, bf16[16,2048]{1,0:T(8,128)(2,1)S(1)}, u32[]{:S(2)}, u32[]{:S(2)}) collective-permute-start(bf16[16,2048]{1,0:T(8,128)(2,1)S(1)} %constant_dynamic-slice_fusion.refs_0_), channel_id=1, source_target_pairs={{0,2},{2,0},{1,3},{3,1},{4,6},{6,4},{5,7},{7,5},{8,10},{10,8},{9,1... | collective-permute-start | bytes 196616 | tf_op jit(solution)/shard_map/ppermute | solution.py:153
  6.5 1.3 %collective-permute-start = (bf16[16,2048]{1,0:T(8,128)(2,1)S(1)}, bf16[16,2048]{1,0:T(8,128)(2,1)S(1)}, u32[]{:S(2)}, u32[]{:S(2)}) collective-permute-start(bf16[16,2048]{1,0:T(8,128)(2,1)S(1)} %constant_dynamic-slice_fusion.refs_0_), channel_id=1, source_target_pairs={{0,12},{4,8},{8,4},{12,0},{1,13},{5,9},{9,5},{13,1},{2,14},{6,10},... | collective-permute-start | bytes 196616 | tf_op jit(solution)/shard_map/ppermute | solution.py:153
  7.9 0.0 copy-done.6
  7.9 0.1 reshape.16.slots_ref
  7.9 0.6 %copy-done.5 = s32[1,1,8,8]{3,2,1,0:T(8,128)S(1)} copy-done((s32[1,1,8,8]{3,2,1,0:T(8,128)S(1)}, s32[1,1,8,8]{3,2,1,0:T(8,128)}, u32[]{:S(2)}) %copy-start.5) | copy-done | bytes 280
  8.5 0.2 shard_map.64.refs_8_.refs_5_
  8.7 0.0 collective-permute-start.5
  8.7 0.3 collective-permute-start.2
  9.0 0.8 %collective-permute-done.5.refs_9_.refs_6_ = s32[1,128]{1,0:T(1,128)S(1)} collective-permute-done((s32[1,128]{1,0:T(1,128)S(1)}, s32[1,128]{1,0:T(1,128)S(1)}, u32[]{:S(2)}, u32[]{:S(2)}) %collective-permute-start.5) | collective-permute-done | bytes 544 | tf_op jit(solution)/shard_map/ppermute | solution.py:153
  9.9 0.0 collective-permute-done.4.refs_4_
  9.9 0.7 %collective-permute-start.6 = (bf16[16,2048]{1,0:T(8,128)(2,1)S(1)}, bf16[16,2048]{1,0:T(8,128)(2,1)S(1)}, u32[]{:S(2)}, u32[]{:S(2)}) collective-permute-start(bf16[16,2048]{1,0:T(8,128)(2,1)S(1)} %collective-permute-done.4.refs_4_), channel_id=1, source_target_pairs={{0,2},{2,0},{1,3},{3,1},{4,6},{6,4},{5,7},{7,5},{8,10},{10,8},{9,1... | collective-permute-start | bytes 196616 | tf_op jit(solution)/shard_map/ppermute | solution.py:153
  10.6 0.0 collective-permute-done.1.refs_1_
  10.6 2.0 %collective-permute-start.3 = (bf16[16,2048]{1,0:T(8,128)(2,1)S(1)}, bf16[16,2048]{1,0:T(8,128)(2,1)S(1)}, u32[]{:S(2)}, u32[]{:S(2)}) collective-permute-start(bf16[16,2048]{1,0:T(8,128)(2,1)S(1)} %collective-permute-done.1.refs_1_), channel_id=1, source_target_pairs={{0,4},{4,0},{8,12},{12,8},{1,5},{5,1},{9,13},{13,9},{2,6},{6,2},{1... | collective-permute-start | bytes 196616 | tf_op jit(solution)/shard_map/ppermute | solution.py:153
  12.6 0.1 collective-permute-done.refs_6_
  12.7 0.6 %collective-permute-start.7 = (bf16[16,2048]{1,0:T(8,128)(2,1)S(1)}, bf16[16,2048]{1,0:T(8,128)(2,1)S(1)}, u32[]{:S(2)}, u32[]{:S(2)}) collective-permute-start(bf16[16,2048]{1,0:T(8,128)(2,1)S(1)} %collective-permute-done.refs_6_), channel_id=1, source_target_pairs={{0,2},{2,0},{1,3},{3,1},{4,6},{6,4},{5,7},{7,5},{8,10},{10,8},{9,1... | collective-permute-start | bytes 196616 | tf_op jit(solution)/shard_map/ppermute | solution.py:153
  13.2 1.2 %copy-done.1 = bf16[4,256,512]{2,1,0:T(8,128)(2,1)S(1)} copy-done((bf16[4,256,512]{2,1,0:T(8,128)(2,1)S(1)}, bf16[4,256,512]{2,1,0:T(8,128)(2,1)}, u32[]{:S(2)}) %copy-start.1) | copy-done | bytes 1048600
  14.5 0.8 %shard_map.65 = (bf16[4,256,256]{2,1,0:T(8,128)(2,1)S(1)}, bf16[4,256,256]{2,1,0:T(8,128)(2,1)S(1)}) custom-call(s32[1]{0:T(128)} %bitcast.half_ref.core_ref, bf16[4,256,512]{2,1,0:T(8,128)(2,1)S(1)} %copy-done.1), custom_call_target="tpu_custom_call" | custom-call | flops 536870912 | bytes 3145728 | tf_op jit(solution)/shard_map/pallas_call | solution.py:199
  15.2 0.0 collective-permute-done.2.refs_2_
  15.2 0.0 collective-permute-done.6.refs_5_
  15.2 0.1 collective-permute-done.3.refs_3_
  15.4 1.6 %collective-permute-done.7.refs_7_ = bf16[16,2048]{1,0:T(8,128)(2,1)S(1)} collective-permute-done((bf16[16,2048]{1,0:T(8,128)(2,1)S(1)}, bf16[16,2048]{1,0:T(8,128)(2,1)S(1)}, u32[]{:S(2)}, u32[]{:S(2)}) %collective-permute-start.7) | collective-permute-done | bytes 65568 | tf_op jit(solution)/shard_map/ppermute | solution.py:153
  16.9 0.0 copy-done.2
  16.9 1.1 %shard_map.66.refs_0_ = f32[4,256]{1,0:T(4,128)S(1)} custom-call(s32[1]{0:T(128)} %bitcast.1.place_ref, s32[1]{0:T(128)} %bitcast.half_ref.core_ref, bf16[16,2048]{1,0:T(8,128)(2,1)S(1)} %constant_dynamic-slice_fusion.refs_0_, bf16[16,2048]{1,0:T(8,128)(2,1)S(1)} %collective-permute-done.1.refs_1_, bf16[16,2048]{1,0:T(8,128)(2,1)S(1)} %collective-permute-done.2.refs_2_, ...), custom_call_target="tpu_custom_call" | custom-call | flops 268435456 | bytes 2097152 | tf_op jit(solution)/shard_map/pallas_call | solution.py:214
  18.0 0.1 collective-permute-start.8
  18.1 1.2 %collective-permute-done.8.refs_1_ = f32[4,256]{1,0:T(4,128)S(1)} collective-permute-done((f32[4,256]{1,0:T(4,128)S(1)}, f32[4,256]{1,0:T(4,128)S(1)}, u32[]{:S(2)}, u32[]{:S(2)}) %collective-permute-start.8) | collective-permute-done | bytes 4128 | tf_op jit(solution)/shard_map/ppermute | solution.py:153
  19.2 0.0 copy-done.4
  19.2 1.4 %shard_map.67 = (bf16[32,2048]{1,0:T(8,128)(2,1)S(1)}, bf16[32,2048]{1,0:T(8,128)(2,1)S(1)}, bf16[16,2048]{1,0:T(8,128)(2,1)S(1)}, bf16[16,2048]{1,0:T(8,128)(2,...) custom-call(s32[1]{0:T(128)} %bitcast.1.place_ref, s32[1]{0:T(128)} %bitcast.half_ref.core_ref, ...), custom_call_target="tpu_custom_call" | custom-call | flops 268435456 | bytes 2097152 | tf_op jit(solution)/shard_map/pallas_call | solution.py:227
  20.7 0.6 %collective-permute-start.11 = (bf16[16,2048]{1,0:T(8,128)(2,1)S(1)}, bf16[16,2048]{1,0:T(8,128)(2,1)S(1)}, u32[]{:S(2)}, u32[]{:S(2)}) collective-permute-start(bf16[16,2048]{1,0:T(8,128)(2,1)S(1)} %get-tuple-element.28), channel_id=1, source_target_pairs={{0,2},{2,0},{1,3},{3,1},{4,6},{6,4},{5,7},{7,5},{8,10},{10,8},{9,1... | collective-permute-start | bytes 196616 | tf_op jit(solution)/shard_map/ppermute | solution.py:153
  21.3 1.5 %collective-permute-start.13 = (bf16[16,2048]{1,0:T(8,128)(2,1)S(1)}, bf16[16,2048]{1,0:T(8,128)(2,1)S(1)}, u32[]{:S(2)}, u32[]{:S(2)}) collective-permute-start(bf16[16,2048]{1,0:T(8,128)(2,1)S(1)} %get-tuple-element.30), channel_id=1, source_target_pairs={{0,2},{2,0},{1,3},{3,1},{4,6},{6,4},{5,7},{7,5},{8,10},{10,8},{9,1... | collective-permute-start | bytes 196616 | tf_op jit(solution)/shard_map/ppermute | solution.py:153
  22.7 0.0 collective-permute-start.9
  22.8 2.8 %collective-permute-done.11 = bf16[16,2048]{1,0:T(8,128)(2,1)S(1)} collective-permute-done((bf16[16,2048]{1,0:T(8,128)(2,1)S(1)}, bf16[16,2048]{1,0:T(8,128)(2,1)S(1)}, u32[]{:S(2)}, u32[]{:S(2)}) %collective-permute-start.11) | collective-permute-done | bytes 65568 | tf_op jit(solution)/shard_map/ppermute | solution.py:153
  25.6 3.4 %collective-permute-start.12 = (bf16[16,2048]{1,0:T(8,128)(2,1)S(1)}, bf16[16,2048]{1,0:T(8,128)(2,1)S(1)}, u32[]{:S(2)}, u32[]{:S(2)}) collective-permute-start(bf16[16,2048]{1,0:T(8,128)(2,1)S(1)} %add_convert_fusion.1), channel_id=1, source_target_pairs={{0,8},{4,12},{8,0},{12,4},{1,9},{5,13},{9,1},{13,5},{2,10},{6,14},... | collective-permute-start | bytes 196616 | tf_op jit(solution)/shard_map/ppermute | solution.py:153
  29.0 0.0 collective-permute-done.13
  29.0 0.2 collective-permute-start.14
  29.2 0.0 collective-permute-done.9
  29.2 0.0 copy-start.3
  29.2 0.8 %collective-permute-start.10 = (bf16[16,2048]{1,0:T(8,128)(2,1)S(1)}, bf16[16,2048]{1,0:T(8,128)(2,1)S(1)}, u32[]{:S(2)}, u32[]{:S(2)}) collective-permute-start(bf16[16,2048]{1,0:T(8,128)(2,1)S(1)} %slice.17), channel_id=1, source_target_pairs={{0,2},{2,0},{1,3},{3,1},{4,6},{6,4},{5,7},{7,5},{8,10},{10,8},{9,1... | collective-permute-start | bytes 196616 | tf_op jit(solution)/shard_map/ppermute | solution.py:153
  30.0 3.0 %collective-permute-done.12 = bf16[16,2048]{1,0:T(8,128)(2,1)S(1)} collective-permute-done((bf16[16,2048]{1,0:T(8,128)(2,1)S(1)}, bf16[16,2048]{1,0:T(8,128)(2,1)S(1)}, u32[]{:S(2)}, u32[]{:S(2)}) %collective-permute-start.12) | collective-permute-done | bytes 65568 | tf_op jit(solution)/shard_map/ppermute | solution.py:153
  33.0 2.1 %collective-permute-done.14 = bf16[16,2048]{1,0:T(8,128)(2,1)S(1)} collective-permute-done((bf16[16,2048]{1,0:T(8,128)(2,1)S(1)}, bf16[16,2048]{1,0:T(8,128)(2,1)S(1)}, u32[]{:S(2)}, u32[]{:S(2)}) %collective-permute-start.14) | collective-permute-done | bytes 65568 | tf_op jit(solution)/shard_map/ppermute | solution.py:153
  35.1 0.0 collective-permute-done.10
  35.2 0.1 collective-permute-start.15
  35.2 1.3 %collective-permute-done.15.other_ref = f32[16,2048]{1,0:T(8,128)S(1)} collective-permute-done((f32[16,2048]{1,0:T(8,128)S(1)}, f32[16,2048]{1,0:T(8,128)S(1)}, u32[]{:S(2)}, u32[]{:S(2)}) %collective-permute-start.15) | collective-permute-done | bytes 131104 | tf_op jit(solution)/shard_map/ppermute | solution.py:153
  36.6 0.0 copy-done.3
  36.6 0.7 %shard_map.68 = f32[16,4096]{1,0:T(8,128)} custom-call(s32[1]{0:T(128)} %bitcast.half_ref.core_ref, f32[16,2048]{1,0:T(8,128)S(1)} %fusion.1.mine_ref, f32[16,2048]{1,0:T(8,128)S(1)} %collective-permute-done.15.other_ref, bf16[16,4096]{1,0:T(8,128)(2,1)S(1)} %copy-done.3), custom_call_target="tpu_custom_call" | custom-call | bytes 786432 | tf_op jit(solution)/shard_map/pallas_call | solution.py:253
  (10 shorter events, 0.1 us)
Async XLA Ops:
  0.0 0.9 %copy-start = (bf16[16,4096]{1,0:T(8,128)(2,1)S(1)}, bf16[16,4096]{1,0:T(8,128)(2,1)}, u32[]{:S(2)}) copy-start(bf16[16,4096]{1,0:T(8,128)(2,1)} %param.10) | copy-start | bytes 393220
  0.9 6.9 %copy-start.6 = (s32[4,8,4]{1,2,0:T(4,128)S(1)}, s32[4,8,4]{1,2,0:T(4,128)}, u32[]{:S(2)}) copy-start(s32[4,8,4]{1,2,0:T(4,128)} %param.8) | copy-start | bytes 1540
  0.9 8.9 %collective-permute-start.4 = (bf16[16,2048]{1,0:T(8,128)(2,1)S(1)}, bf16[16,2048]{1,0:T(8,128)(2,1)S(1)}, u32[]{:S(2)}, u32[]{:S(2)}) collective-permute-start(bf16[16,2048]{1,0:T(8,128)(2,1)S(1)} %constant_dynamic-slice_fusion.refs_0_), channel_id=1, source_target_pairs={{0,8},{4,12},{8,0},{12,4},{1,9},{5,13},{9,1},{13,5},{2,10},{6,14},... | collective-permute-start | bytes 196616 | tf_op jit(solution)/shard_map/ppermute | solution.py:153
  5.0 5.6 %collective-permute-start.1 = (bf16[16,2048]{1,0:T(8,128)(2,1)S(1)}, bf16[16,2048]{1,0:T(8,128)(2,1)S(1)}, u32[]{:S(2)}, u32[]{:S(2)}) collective-permute-start(bf16[16,2048]{1,0:T(8,128)(2,1)S(1)} %constant_dynamic-slice_fusion.refs_0_), channel_id=1, source_target_pairs={{0,2},{2,0},{1,3},{3,1},{4,6},{6,4},{5,7},{7,5},{8,10},{10,8},{9,1... | collective-permute-start | bytes 196616 | tf_op jit(solution)/shard_map/ppermute | solution.py:153
  6.5 6.2 %collective-permute-start = (bf16[16,2048]{1,0:T(8,128)(2,1)S(1)}, bf16[16,2048]{1,0:T(8,128)(2,1)S(1)}, u32[]{:S(2)}, u32[]{:S(2)}) collective-permute-start(bf16[16,2048]{1,0:T(8,128)(2,1)S(1)} %constant_dynamic-slice_fusion.refs_0_), channel_id=1, source_target_pairs={{0,12},{4,8},{8,4},{12,0},{1,13},{5,9},{9,5},{13,1},{2,14},{6,10},... | collective-permute-start | bytes 196616 | tf_op jit(solution)/shard_map/ppermute | solution.py:153
  7.9 0.7 %copy-start.5 = (s32[1,1,8,8]{3,2,1,0:T(8,128)S(1)}, s32[1,1,8,8]{3,2,1,0:T(8,128)}, u32[]{:S(2)}) copy-start(s32[1,1,8,8]{3,2,1,0:T(8,128)} %param.9) | copy-start | bytes 772
  8.7 1.1 %collective-permute-start.5 = (s32[1,128]{1,0:T(1,128)S(1)}, s32[1,128]{1,0:T(1,128)S(1)}, u32[]{:S(2)}, u32[]{:S(2)}) collective-permute-start(s32[1,128]{1,0:T(1,128)S(1)} %shard_map.64.refs_8_.refs_5_), channel_id=1, source_target_pairs={{0,1},{1,0},{2,3},{3,2},{4,5},{5,4},{6,7},{7,6},{8,9},{9,8},{10,11... | collective-permute-start | bytes 1544 | tf_op jit(solution)/shard_map/ppermute | solution.py:153
  8.7 6.5 %collective-permute-start.2 = (bf16[16,2048]{1,0:T(8,128)(2,1)S(1)}, bf16[16,2048]{1,0:T(8,128)(2,1)S(1)}, u32[]{:S(2)}, u32[]{:S(2)}) collective-permute-start(bf16[16,2048]{1,0:T(8,128)(2,1)S(1)} %constant_dynamic-slice_fusion.refs_0_), channel_id=1, source_target_pairs={{0,4},{4,0},{8,12},{12,8},{1,5},{5,1},{9,13},{13,9},{2,6},{6,2},{1... | collective-permute-start | bytes 196616 | tf_op jit(solution)/shard_map/ppermute | solution.py:153
  9.9 5.4 %collective-permute-start.6 = (bf16[16,2048]{1,0:T(8,128)(2,1)S(1)}, bf16[16,2048]{1,0:T(8,128)(2,1)S(1)}, u32[]{:S(2)}, u32[]{:S(2)}) collective-permute-start(bf16[16,2048]{1,0:T(8,128)(2,1)S(1)} %collective-permute-done.4.refs_4_), channel_id=1, source_target_pairs={{0,2},{2,0},{1,3},{3,1},{4,6},{6,4},{5,7},{7,5},{8,10},{10,8},{9,1... | collective-permute-start | bytes 196616 | tf_op jit(solution)/shard_map/ppermute | solution.py:153
  10.6 4.8 %collective-permute-start.3 = (bf16[16,2048]{1,0:T(8,128)(2,1)S(1)}, bf16[16,2048]{1,0:T(8,128)(2,1)S(1)}, u32[]{:S(2)}, u32[]{:S(2)}) collective-permute-start(bf16[16,2048]{1,0:T(8,128)(2,1)S(1)} %collective-permute-done.1.refs_1_), channel_id=1, source_target_pairs={{0,4},{4,0},{8,12},{12,8},{1,5},{5,1},{9,13},{13,9},{2,6},{6,2},{1... | collective-permute-start | bytes 196616 | tf_op jit(solution)/shard_map/ppermute | solution.py:153
  12.7 4.3 %collective-permute-start.7 = (bf16[16,2048]{1,0:T(8,128)(2,1)S(1)}, bf16[16,2048]{1,0:T(8,128)(2,1)S(1)}, u32[]{:S(2)}, u32[]{:S(2)}) collective-permute-start(bf16[16,2048]{1,0:T(8,128)(2,1)S(1)} %collective-permute-done.refs_6_), channel_id=1, source_target_pairs={{0,2},{2,0},{1,3},{3,1},{4,6},{6,4},{5,7},{7,5},{8,10},{10,8},{9,1... | collective-permute-start | bytes 196616 | tf_op jit(solution)/shard_map/ppermute | solution.py:153
  13.2 1.2 %copy-start.1 = (bf16[4,256,512]{2,1,0:T(8,128)(2,1)S(1)}, bf16[4,256,512]{2,1,0:T(8,128)(2,1)}, u32[]{:S(2)}) copy-start(bf16[4,256,512]{2,1,0:T(8,128)(2,1)} %refs_3_.1) | copy-start | bytes 3145732
  14.5 2.5 %copy-start.2 = (bf16[4,256,512]{2,1,0:T(8,128)(2,1)S(1)}, bf16[4,256,512]{2,1,0:T(8,128)(2,1)}, u32[]{:S(2)}) copy-start(bf16[4,256,512]{2,1,0:T(8,128)(2,1)} %refs_3_.1) | copy-start | bytes 3145732
  16.9 2.3 %copy-start.4 = (f32[4,256]{1,0:T(4,128)S(1)}, f32[4,256]{1,0:T(4,128)}, u32[]{:S(2)}) copy-start(f32[4,256]{1,0:T(4,128)} %refs_2_.1) | copy-start | bytes 12292
  18.0 1.2 %collective-permute-start.8 = (f32[4,256]{1,0:T(4,128)S(1)}, f32[4,256]{1,0:T(4,128)S(1)}, u32[]{:S(2)}, u32[]{:S(2)}) collective-permute-start(f32[4,256]{1,0:T(4,128)S(1)} %shard_map.66.refs_0_), channel_id=1, source_target_pairs={{0,1},{1,0},{2,3},{3,2},{4,5},{5,4},{6,7},{7,6},{8,9},{9,8},{10,11... | collective-permute-start | bytes 12296 | tf_op jit(solution)/shard_map/ppermute | solution.py:153
  20.7 4.9 %collective-permute-start.11 = (bf16[16,2048]{1,0:T(8,128)(2,1)S(1)}, bf16[16,2048]{1,0:T(8,128)(2,1)S(1)}, u32[]{:S(2)}, u32[]{:S(2)}) collective-permute-start(bf16[16,2048]{1,0:T(8,128)(2,1)S(1)} %get-tuple-element.28), channel_id=1, source_target_pairs={{0,2},{2,0},{1,3},{3,1},{4,6},{6,4},{5,7},{7,5},{8,10},{10,8},{9,1... | collective-permute-start | bytes 196616 | tf_op jit(solution)/shard_map/ppermute | solution.py:153
  21.3 7.7 %collective-permute-start.13 = (bf16[16,2048]{1,0:T(8,128)(2,1)S(1)}, bf16[16,2048]{1,0:T(8,128)(2,1)S(1)}, u32[]{:S(2)}, u32[]{:S(2)}) collective-permute-start(bf16[16,2048]{1,0:T(8,128)(2,1)S(1)} %get-tuple-element.30), channel_id=1, source_target_pairs={{0,2},{2,0},{1,3},{3,1},{4,6},{6,4},{5,7},{7,5},{8,10},{10,8},{9,1... | collective-permute-start | bytes 196616 | tf_op jit(solution)/shard_map/ppermute | solution.py:153
  22.7 6.4 %collective-permute-start.9 = (bf16[32,2048]{1,0:T(8,128)(2,1)S(1)}, bf16[32,2048]{1,0:T(8,128)(2,1)S(1)}, u32[]{:S(2)}, u32[]{:S(2)}) collective-permute-start(bf16[32,2048]{1,0:T(8,128)(2,1)S(1)} %get-tuple-element.26), channel_id=1, source_target_pairs={{0,4},{4,0},{8,12},{12,8},{1,5},{5,1},{9,13},{13,9},{2,6},{6,2},{1... | collective-permute-start | bytes 393224 | tf_op jit(solution)/shard_map/ppermute | solution.py:153
  25.6 7.4 %collective-permute-start.12 = (bf16[16,2048]{1,0:T(8,128)(2,1)S(1)}, bf16[16,2048]{1,0:T(8,128)(2,1)S(1)}, u32[]{:S(2)}, u32[]{:S(2)}) collective-permute-start(bf16[16,2048]{1,0:T(8,128)(2,1)S(1)} %add_convert_fusion.1), channel_id=1, source_target_pairs={{0,8},{4,12},{8,0},{12,4},{1,9},{5,13},{9,1},{13,5},{2,10},{6,14},... | collective-permute-start | bytes 196616 | tf_op jit(solution)/shard_map/ppermute | solution.py:153
  29.0 6.1 %collective-permute-start.14 = (bf16[16,2048]{1,0:T(8,128)(2,1)S(1)}, bf16[16,2048]{1,0:T(8,128)(2,1)S(1)}, u32[]{:S(2)}, u32[]{:S(2)}) collective-permute-start(bf16[16,2048]{1,0:T(8,128)(2,1)S(1)} %add_convert_fusion), channel_id=1, source_target_pairs={{0,12},{4,8},{8,4},{12,0},{1,13},{5,9},{9,5},{13,1},{2,14},{6,10},... | collective-permute-start | bytes 196616 | tf_op jit(solution)/shard_map/ppermute | solution.py:153
  29.2 7.3 %copy-start.3 = (bf16[16,4096]{1,0:T(8,128)(2,1)S(1)}, bf16[16,4096]{1,0:T(8,128)(2,1)}, u32[]{:S(2)}) copy-start(bf16[16,4096]{1,0:T(8,128)(2,1)} %core_ref.1) | copy-start | bytes 393220
  29.2 5.9 %collective-permute-start.10 = (bf16[16,2048]{1,0:T(8,128)(2,1)S(1)}, bf16[16,2048]{1,0:T(8,128)(2,1)S(1)}, u32[]{:S(2)}, u32[]{:S(2)}) collective-permute-start(bf16[16,2048]{1,0:T(8,128)(2,1)S(1)} %slice.17), channel_id=1, source_target_pairs={{0,2},{2,0},{1,3},{3,1},{4,6},{6,4},{5,7},{7,5},{8,10},{10,8},{9,1... | collective-permute-start | bytes 196616 | tf_op jit(solution)/shard_map/ppermute | solution.py:153
  35.2 1.4 %collective-permute-start.15 = (f32[16,2048]{1,0:T(8,128)S(1)}, f32[16,2048]{1,0:T(8,128)S(1)}, u32[]{:S(2)}, u32[]{:S(2)}) collective-permute-start(f32[16,2048]{1,0:T(8,128)S(1)} %fusion.1.mine_ref), channel_id=1, source_target_pairs={{0,1},{1,0},{2,3},{3,2},{4,5},{5,4},{6,7},{7,6},{8,9},{9,8},{10,11... | collective-permute-start | bytes 393224 | tf_op jit(solution)/shard_map/ppermute | solution.py:153

commit v14 on v13

--- a/solution.py
+++ b/solution.py
@@ -153,6 +153,11 @@
     return lax.ppermute(array, axis, [(i, i ^ step) for i in range(count)])
 
 
+def swap_both(array, sizes, dz, dx):
+    step = dz * sizes[1] + dx
+    return lax.ppermute(array, ("batch", "pair"), [(i, i ^ step) for i in range(sizes[0] * sizes[1])])
+
+
 def per_device(basis_values, point_weights, slot_ids, fetch_rows, density_blocks, core_blocks):
     rows_z, rows_x = lax.axis_size("batch"), lax.axis_size("pair")
     z, x, half = lax.axis_index("batch"), lax.axis_index("pair"), lax.axis_index("orb")
@@ -182,17 +187,20 @@
     direct = {dz: swap(mine, "batch", rows_z, dz) for dz in far}
     beside = [swap(mine, "pair", rows_x, dx) for dx in side]
     *beside, own_rows = lax.optimization_barrier((*beside, own_rows))
-    arrays, places = [mine, *beside], [[dx] for dx in range(rows_x)]
+    cluster = jnp.concatenate([mine, *beside], axis=0)
+    arrays, places = [cluster], [list(range(rows_x))]
     for dz in near:
-        for dx, piece in enumerate([mine, *beside]):
-            arrays.append(swap(piece, "batch", rows_z, dz))
-            places.append([dz * rows_x + dx])
+        arrays.append(swap(cluster, "batch", rows_z, dz))
+        places.append(list(range(dz * rows_x, (dz + 1) * rows_x)))
     direct[far[0]], other_rows = lax.optimization_barrier((direct[far[0]], other_rows))
-    for dz in far:
-        arrays.append(direct[dz])
-        places.append([dz * rows_x])
-        for dx in side:
-            arrays.append(swap(direct[dz], "pair", rows_x, dx))
+    arrays.append(direct[far[0]])
+    places.append([far[0] * rows_x])
+    for dx in side:
+        arrays.append(swap(direct[far[0]], "pair", rows_x, dx))
+        places.append([far[0] * rows_x + dx])
+    for dz in far[1:]:
+        for dx in [0] + side:
+            arrays.append(direct[dz] if dx == 0 else swap_both(mine, (rows_z, rows_x), dz, dx))
             places.append([dz * rows_x + dx])
 
     half_at, _ = lax.optimization_barrier((half.reshape(1).astype(jnp.int32), direct[far[-1]]))
@@ -235,12 +243,14 @@
     )(place, core_at, partial, partial_other, point_weights, basis_values, left_t, own_rows, other_rows)
 
     clusters, singles = sums[:len(near) + 1], sums[len(near) + 1:]
-    landed = []
-    for i, dz in enumerate(far):
-        joined = singles[i * rows_x].astype(f32)
-        for dx in side:
-            joined = joined + swap(singles[i * rows_x + dx], "pair", rows_x, dx).astype(f32)
-        landed.append(swap(joined.astype(bf16), "batch", rows_z, dz).astype(f32))
+    joined = singles[0].astype(f32)
+    for dx in side:
+        joined = joined + swap(singles[dx], "pair", rows_x, dx).astype(f32)
+    landed = [swap(joined.astype(bf16), "batch", rows_z, far[0]).astype(f32)]
+    for i, dz in enumerate(far[1:]):
+        for dx in [0] + side:
+            array = singles[(i + 1) * rows_x + dx]
+            landed.append(swap_both(array, (rows_z, rows_x), dz, dx).astype(f32))
     cluster = clusters[0].astype(f32)
     for dz, array in zip(near, clusters[1:]):
         cluster = cluster + swap(array, "batch", rows_z, dz).astype(f32)

time: 37.5 us -> 42.3 us (1.13)
  starting transfers between devices: 17 us -> 22.3 us
  waiting for transfers between devices: 13.1 us -> 12.6 us
    ppermute x0 -> x3, starting transfers between devices: none -> 6.31 us  [swap_both(): lax.ppermute(array, ('batch', 'pair'), [(i, i ^ step) for i in range(size...]
    ppermute x16 -> x12, waiting for transfers between devices: 13.1 us -> 11.6 us  [swap(): return lax.ppermute(array, axis, [(i, i ^ step) for i in range(count)])]
    ppermute x16 -> x12, starting transfers between devices: 17 us -> 16 us  [swap(): return lax.ppermute(array, axis, [(i, i ^ step) for i in range(count)])]
    ppermute x0 -> x3, waiting for transfers between devices: none -> 1.01 us  [swap_both(): lax.ppermute(array, ('batch', 'pair'), [(i, i ^ step) for i in range(size...]
  transfers between devices with their start and end apart: 16 -> 15, of which waited for: 9 -> 7; matrix products, arithmetic and copies ran while one was open for 0% -> 0% of each run, Pallas kernels for 3% -> 2%
where the time goes in v14:
time: 42.3 us; the launch traced here: 42.1 us
  starting transfers between devices  22.3 us (53%)
  waiting for transfers between devices  12.6 us (30%)
  Pallas kernels  4.15 us (10%)
  local copies, waits for them, and re-layouts  2.85 us (7%)
    ppermute x12, starting transfers between devices, swap(): return lax.ppermute(array, axis, [(i, i ^ step) for i in range(count)])  16 us
    ppermute x12, waiting for transfers between devices, swap(): return lax.ppermute(array, axis, [(i, i ^ step) for i in range(count)])  11.6 us
    ppermute x3, starting transfers between devices, swap_both(): lax.ppermute(array, ('batch', 'pair'), [(i, i ^ step) for i in range(size...  6.31 us
    unnamed x14, local copies, waits for them, and re-layouts  2.74 us
    pallas_call x1, Pallas kernels, per_device(): call(functools.partial(scatter_kernel, out_places), [jax.ShapeDtypeStruct...  1.41 us
    pallas_call x1, Pallas kernels, per_device(): call(functools.partial(density_kernel, places), jax.ShapeDtypeStruct((bat...  1.07 us
    ppermute x3, waiting for transfers between devices, swap_both(): lax.ppermute(array, ('batch', 'pair'), [(i, i ^ step) for i in range(size...  1.01 us
  transfers between devices with their start and end apart: 15, of which 7 were waited for; matrix products, arithmetic and copies ran while one was open for 0% of the time, Pallas kernels for 2%

profile of v14, /device:TPU:0, one launch (start us, length us, event | category | flops | bytes accessed | tf_op | source)
XLA Modules:
  0.0 42.1 jit_solution(16097473067822157898)
XLA Ops:
  0.0 0.0 copy-start
  0.0 0.9 %copy-done = bf16[16,4096]{1,0:T(8,128)(2,1)S(1)} copy-done((bf16[16,4096]{1,0:T(8,128)(2,1)S(1)}, bf16[16,4096]{1,0:T(8,128)(2,1)}, u32[]{:S(2)}) %copy-start) | copy-done | bytes 131096
  0.9 0.0 copy-start.6
  0.9 3.0 %collective-permute-start.1 = (bf16[16,2048]{1,0:T(8,128)(2,1)S(1)}, bf16[16,2048]{1,0:T(8,128)(2,1)S(1)}, u32[]{:S(2)}, u32[]{:S(2)}) collective-permute-start(bf16[16,2048]{1,0:T(8,128)(2,1)S(1)} %constant_dynamic-slice_fusion), channel_id=1, source_target_pairs={{0,2},{2,0},{1,3},{3,1},{4,6},{6,4},{5,7},{7,5},{8,10},{10,8},{9,1... | collective-permute-start | bytes 196616 | tf_op jit(solution)/shard_map/ppermute | solution.py:153
  3.9 2.6 %collective-permute-start.3 = (bf16[16,2048]{1,0:T(8,128)(2,1)S(1)}, bf16[16,2048]{1,0:T(8,128)(2,1)S(1)}, u32[]{:S(2)}, u32[]{:S(2)}) collective-permute-start(bf16[16,2048]{1,0:T(8,128)(2,1)S(1)} %constant_dynamic-slice_fusion), channel_id=1, source_target_pairs={{0,8},{4,12},{8,0},{12,4},{1,9},{5,13},{9,1},{13,5},{2,10},{6,14},... | collective-permute-start | bytes 196616 | tf_op jit(solution)/shard_map/ppermute | solution.py:153
  6.5 0.0 copy-done.6
  6.5 0.0 copy-start.5
  6.5 0.1 reshape.16.slots_ref
  6.6 0.6 %copy-done.5 = s32[1,1,8,8]{3,2,1,0:T(8,128)S(1)} copy-done((s32[1,1,8,8]{3,2,1,0:T(8,128)S(1)}, s32[1,1,8,8]{3,2,1,0:T(8,128)}, u32[]{:S(2)}) %copy-start.5) | copy-done | bytes 280
  7.2 0.2 shard_map.64.refs_6_.refs_5_
  7.4 0.0 collective-permute-done.1
  7.4 1.6 %collective-permute-start.2 = (bf16[32,2048]{1,0:T(8,128)(2,1)S(1)}, bf16[32,2048]{1,0:T(8,128)(2,1)S(1)}, u32[]{:S(2)}, u32[]{:S(2)}) collective-permute-start(bf16[32,2048]{1,0:T(8,128)(2,1)S(1)} %pad_maximum_fusion.refs_0_), channel_id=1, source_target_pairs={{0,4},{4,0},{8,12},{12,8},{1,5},{5,1},{9,13},{13,9},{2,6},{6,2},{1... | collective-permute-start | bytes 393224 | tf_op jit(solution)/shard_map/ppermute | solution.py:153
  9.0 1.8 %collective-permute-start = (bf16[16,2048]{1,0:T(8,128)(2,1)S(1)}, bf16[16,2048]{1,0:T(8,128)(2,1)S(1)}, u32[]{:S(2)}, u32[]{:S(2)}) collective-permute-start(bf16[16,2048]{1,0:T(8,128)(2,1)S(1)} %constant_dynamic-slice_fusion), channel_id=1, source_target_pairs={{0,12},{4,8},{8,4},{12,0},{1,13},{5,9},{9,5},{13,1},{2,14},{6,10},... | collective-permute-start | bytes 196616 | tf_op jit(solution)/shard_map/ppermute | solution.py:153
  10.8 0.0 collective-permute-start.4
  10.8 2.3 %collective-permute-start.6 = (bf16[16,2048]{1,0:T(8,128)(2,1)S(1)}, bf16[16,2048]{1,0:T(8,128)(2,1)S(1)}, u32[]{:S(2)}, u32[]{:S(2)}) collective-permute-start(bf16[16,2048]{1,0:T(8,128)(2,1)S(1)} %constant_dynamic-slice_fusion), channel_id=1, source_target_pairs={{0,14},{2,12},{4,10},{6,8},{8,6},{10,4},{12,2},{14,0},{1,15},{3,13... | collective-permute-start | bytes 196616 | tf_op jit(solution)/shard_map/ppermute | solution.py:158
  13.1 0.0 collective-permute-done.4.refs_7_.refs_6_
  13.1 0.0 collective-permute-done.3.refs_2_
  13.1 1.2 %collective-permute-start.5 = (bf16[16,2048]{1,0:T(8,128)(2,1)S(1)}, bf16[16,2048]{1,0:T(8,128)(2,1)S(1)}, u32[]{:S(2)}, u32[]{:S(2)}) collective-permute-start(bf16[16,2048]{1,0:T(8,128)(2,1)S(1)} %collective-permute-done.3.refs_2_), channel_id=1, source_target_pairs={{0,2},{2,0},{1,3},{3,1},{4,6},{6,4},{5,7},{7,5},{8,10},{10,8},{9,1... | collective-permute-start | bytes 196616 | tf_op jit(solution)/shard_map/ppermute | solution.py:153
  14.3 0.8 %collective-permute-done.refs_4_ = bf16[16,2048]{1,0:T(8,128)(2,1)S(1)} collective-permute-done((bf16[16,2048]{1,0:T(8,128)(2,1)S(1)}, bf16[16,2048]{1,0:T(8,128)(2,1)S(1)}, u32[]{:S(2)}, u32[]{:S(2)}) %collective-permute-start) | collective-permute-done | bytes 65568 | tf_op jit(solution)/shard_map/ppermute | solution.py:153
  15.2 0.0 copy-start.1
  15.2 1.2 %copy-done.1 = bf16[4,256,512]{2,1,0:T(8,128)(2,1)S(1)} copy-done((bf16[4,256,512]{2,1,0:T(8,128)(2,1)S(1)}, bf16[4,256,512]{2,1,0:T(8,128)(2,1)}, u32[]{:S(2)}) %copy-start.1) | copy-done | bytes 1048600
  16.4 0.8 %shard_map.65 = (bf16[4,256,256]{2,1,0:T(8,128)(2,1)S(1)}, bf16[4,256,256]{2,1,0:T(8,128)(2,1)S(1)}) custom-call(s32[1]{0:T(128)} %bitcast.half_ref.core_ref, bf16[4,256,512]{2,1,0:T(8,128)(2,1)S(1)} %copy-done.1), custom_call_target="tpu_custom_call" | custom-call | flops 536870912 | bytes 3145728 | tf_op jit(solution)/shard_map/pallas_call | solution.py:207
  17.2 1.0 %collective-permute-done.6.refs_5_ = bf16[16,2048]{1,0:T(8,128)(2,1)S(1)} collective-permute-done((bf16[16,2048]{1,0:T(8,128)(2,1)S(1)}, bf16[16,2048]{1,0:T(8,128)(2,1)S(1)}, u32[]{:S(2)}, u32[]{:S(2)}) %collective-permute-start.6) | collective-permute-done | bytes 65568 | tf_op jit(solution)/shard_map/ppermute | solution.py:158
  18.2 0.6 %collective-permute-done.5.refs_3_ = bf16[16,2048]{1,0:T(8,128)(2,1)S(1)} collective-permute-done((bf16[16,2048]{1,0:T(8,128)(2,1)S(1)}, bf16[16,2048]{1,0:T(8,128)(2,1)S(1)}, u32[]{:S(2)}, u32[]{:S(2)}) %collective-permute-start.5) | collective-permute-done | bytes 65568 | tf_op jit(solution)/shard_map/ppermute | solution.py:153
  18.8 0.0 collective-permute-done.2.refs_1_
  18.8 0.0 copy-done.2
  18.8 1.1 %shard_map.66.refs_0_ = f32[4,256]{1,0:T(4,128)S(1)} custom-call(s32[1]{0:T(128)} %bitcast.1.place_ref, s32[1]{0:T(128)} %bitcast.half_ref.core_ref, bf16[32,2048]{1,0:T(8,128)(2,1)S(1)} %pad_maximum_fusion.refs_0_, bf16[32,2048]{1,0:T(8,128)(2,1)S(1)} %collective-permute-done.2.refs_1_, bf16[16,2048]{1,0:T(8,128)(2,1)S(1)} %collective-permute-done.3.refs_2_, ...), custom_call_target="tpu_custom_call" | custom-call | flops 268435456 | bytes 2097152 | tf_op jit(solution)/shard_map/pallas_call | solution.py:222
  19.8 0.1 collective-permute-start.7
  19.9 1.2 %collective-permute-done.7.refs_1_ = f32[4,256]{1,0:T(4,128)S(1)} collective-permute-done((f32[4,256]{1,0:T(4,128)S(1)}, f32[4,256]{1,0:T(4,128)S(1)}, u32[]{:S(2)}, u32[]{:S(2)}) %collective-permute-start.7) | collective-permute-done | bytes 4128 | tf_op jit(solution)/shard_map/ppermute | solution.py:153
  21.1 0.0 copy-done.4
  21.1 1.4 %shard_map.67 = (bf16[32,2048]{1,0:T(8,128)(2,1)S(1)}, bf16[32,2048]{1,0:T(8,128)(2,1)S(1)}, bf16[16,2048]{1,0:T(8,128)(2,1)S(1)}, bf16[16,2048]{1,0:T(8,128)(2,...) custom-call(s32[1]{0:T(128)} %bitcast.1.place_ref, s32[1]{0:T(128)} %bitcast.half_ref.core_ref, ...), custom_call_target="tpu_custom_call" | custom-call | flops 268435456 | bytes 2097152 | tf_op jit(solution)/shard_map/pallas_call | solution.py:235
  22.5 1.3 %collective-permute-start.10 = (bf16[16,2048]{1,0:T(8,128)(2,1)S(1)}, bf16[16,2048]{1,0:T(8,128)(2,1)S(1)}, u32[]{:S(2)}, u32[]{:S(2)}) collective-permute-start(bf16[16,2048]{1,0:T(8,128)(2,1)S(1)} %get-tuple-element.28), channel_id=1, source_target_pairs={{0,2},{2,0},{1,3},{3,1},{4,6},{6,4},{5,7},{7,5},{8,10},{10,8},{9,1... | collective-permute-start | bytes 196616 | tf_op jit(solution)/shard_map/ppermute | solution.py:153
  23.8 1.7 %collective-permute-start.12 = (bf16[16,2048]{1,0:T(8,128)(2,1)S(1)}, bf16[16,2048]{1,0:T(8,128)(2,1)S(1)}, u32[]{:S(2)}, u32[]{:S(2)}) collective-permute-start(bf16[16,2048]{1,0:T(8,128)(2,1)S(1)} %get-tuple-element.29), channel_id=1, source_target_pairs={{0,12},{2,14},{4,8},{6,10},{8,4},{10,6},{12,0},{14,2},{1,13},{3,15... | collective-permute-start | bytes 196616 | tf_op jit(solution)/shard_map/ppermute | solution.py:158
  25.5 2.3 %collective-permute-start.13 = (bf16[16,2048]{1,0:T(8,128)(2,1)S(1)}, bf16[16,2048]{1,0:T(8,128)(2,1)S(1)}, u32[]{:S(2)}, u32[]{:S(2)}) collective-permute-start(bf16[16,2048]{1,0:T(8,128)(2,1)S(1)} %get-tuple-element.30), channel_id=1, source_target_pairs={{0,14},{2,12},{4,10},{6,8},{8,6},{10,4},{12,2},{14,0},{1,15},{3,13... | collective-permute-start | bytes 196616 | tf_op jit(solution)/shard_map/ppermute | solution.py:158
  27.8 0.0 collective-permute-start.8
  27.8 0.0 collective-permute-done.10
  27.9 3.1 %collective-permute-start.11 = (bf16[16,2048]{1,0:T(8,128)(2,1)S(1)}, bf16[16,2048]{1,0:T(8,128)(2,1)S(1)}, u32[]{:S(2)}, u32[]{:S(2)}) collective-permute-start(bf16[16,2048]{1,0:T(8,128)(2,1)S(1)} %add_convert_fusion), channel_id=1, source_target_pairs={{0,8},{4,12},{8,0},{12,4},{1,9},{5,13},{9,1},{13,5},{2,10},{6,14},... | collective-permute-start | bytes 196616 | tf_op jit(solution)/shard_map/ppermute | solution.py:153
  30.9 4.6 %collective-permute-done.8 = bf16[32,2048]{1,0:T(8,128)(2,1)S(1)} collective-permute-done((bf16[32,2048]{1,0:T(8,128)(2,1)S(1)}, bf16[32,2048]{1,0:T(8,128)(2,1)S(1)}, u32[]{:S(2)}, u32[]{:S(2)}) %collective-permute-start.8) | collective-permute-done | bytes 131104 | tf_op jit(solution)/shard_map/ppermute | solution.py:153
  35.5 0.0 copy-start.3
  35.6 1.2 %collective-permute-start.9 = (bf16[16,2048]{1,0:T(8,128)(2,1)S(1)}, bf16[16,2048]{1,0:T(8,128)(2,1)S(1)}, u32[]{:S(2)}, u32[]{:S(2)}) collective-permute-start(bf16[16,2048]{1,0:T(8,128)(2,1)S(1)} %slice.19), channel_id=1, source_target_pairs={{0,2},{2,0},{1,3},{3,1},{4,6},{6,4},{5,7},{7,5},{8,10},{10,8},{9,1... | collective-permute-start | bytes 196616 | tf_op jit(solution)/shard_map/ppermute | solution.py:153
  36.7 0.0 collective-permute-done.12
  36.7 0.0 collective-permute-done.13
  36.8 0.0 collective-permute-done.11
  36.8 3.1 %collective-permute-done.9 = bf16[16,2048]{1,0:T(8,128)(2,1)S(1)} collective-permute-done((bf16[16,2048]{1,0:T(8,128)(2,1)S(1)}, bf16[16,2048]{1,0:T(8,128)(2,1)S(1)}, u32[]{:S(2)}, u32[]{:S(2)}) %collective-permute-start.9) | collective-permute-done | bytes 65568 | tf_op jit(solution)/shard_map/ppermute | solution.py:153
  39.9 0.1 collective-permute-start.14
  40.0 1.3 %collective-permute-done.14.other_ref = f32[16,2048]{1,0:T(8,128)S(1)} collective-permute-done((f32[16,2048]{1,0:T(8,128)S(1)}, f32[16,2048]{1,0:T(8,128)S(1)}, u32[]{:S(2)}, u32[]{:S(2)}) %collective-permute-start.14) | collective-permute-done | bytes 131104 | tf_op jit(solution)/shard_map/ppermute | solution.py:153
  41.3 0.0 copy-done.3
  41.3 0.7 %shard_map.68 = f32[16,4096]{1,0:T(8,128)} custom-call(s32[1]{0:T(128)} %bitcast.half_ref.core_ref, f32[16,2048]{1,0:T(8,128)S(1)} %fusion.2.mine_ref, f32[16,2048]{1,0:T(8,128)S(1)} %collective-permute-done.14.other_ref, bf16[16,4096]{1,0:T(8,128)(2,1)S(1)} %copy-done.3), custom_call_target="tpu_custom_call" | custom-call | bytes 786432 | tf_op jit(solution)/shard_map/pallas_call | solution.py:263
  (8 shorter events, 0.1 us)
Async XLA Ops:
  0.0 0.9 %copy-start = (bf16[16,4096]{1,0:T(8,128)(2,1)S(1)}, bf16[16,4096]{1,0:T(8,128)(2,1)}, u32[]{:S(2)}) copy-start(bf16[16,4096]{1,0:T(8,128)(2,1)} %param.10) | copy-start | bytes 393220
  0.9 5.6 %copy-start.6 = (s32[4,8,4]{1,2,0:T(4,128)S(1)}, s32[4,8,4]{1,2,0:T(4,128)}, u32[]{:S(2)}) copy-start(s32[4,8,4]{1,2,0:T(4,128)} %param.8) | copy-start | bytes 1540
  0.9 6.5 %collective-permute-start.1 = (bf16[16,2048]{1,0:T(8,128)(2,1)S(1)}, bf16[16,2048]{1,0:T(8,128)(2,1)S(1)}, u32[]{:S(2)}, u32[]{:S(2)}) collective-permute-start(bf16[16,2048]{1,0:T(8,128)(2,1)S(1)} %constant_dynamic-slice_fusion), channel_id=1, source_target_pairs={{0,2},{2,0},{1,3},{3,1},{4,6},{6,4},{5,7},{7,5},{8,10},{10,8},{9,1... | collective-permute-start | bytes 196616 | tf_op jit(solution)/shard_map/ppermute | solution.py:153
  3.9 9.2 %collective-permute-start.3 = (bf16[16,2048]{1,0:T(8,128)(2,1)S(1)}, bf16[16,2048]{1,0:T(8,128)(2,1)S(1)}, u32[]{:S(2)}, u32[]{:S(2)}) collective-permute-start(bf16[16,2048]{1,0:T(8,128)(2,1)S(1)} %constant_dynamic-slice_fusion), channel_id=1, source_target_pairs={{0,8},{4,12},{8,0},{12,4},{1,9},{5,13},{9,1},{13,5},{2,10},{6,14},... | collective-permute-start | bytes 196616 | tf_op jit(solution)/shard_map/ppermute | solution.py:153
  6.5 0.7 %copy-start.5 = (s32[1,1,8,8]{3,2,1,0:T(8,128)S(1)}, s32[1,1,8,8]{3,2,1,0:T(8,128)}, u32[]{:S(2)}) copy-start(s32[1,1,8,8]{3,2,1,0:T(8,128)} %param.9) | copy-start | bytes 772
  7.4 11.4 %collective-permute-start.2 = (bf16[32,2048]{1,0:T(8,128)(2,1)S(1)}, bf16[32,2048]{1,0:T(8,128)(2,1)S(1)}, u32[]{:S(2)}, u32[]{:S(2)}) collective-permute-start(bf16[32,2048]{1,0:T(8,128)(2,1)S(1)} %pad_maximum_fusion.refs_0_), channel_id=1, source_target_pairs={{0,4},{4,0},{8,12},{12,8},{1,5},{5,1},{9,13},{13,9},{2,6},{6,2},{1... | collective-permute-start | bytes 393224 | tf_op jit(solution)/shard_map/ppermute | solution.py:153
  9.0 6.1 %collective-permute-start = (bf16[16,2048]{1,0:T(8,128)(2,1)S(1)}, bf16[16,2048]{1,0:T(8,128)(2,1)S(1)}, u32[]{:S(2)}, u32[]{:S(2)}) collective-permute-start(bf16[16,2048]{1,0:T(8,128)(2,1)S(1)} %constant_dynamic-slice_fusion), channel_id=1, source_target_pairs={{0,12},{4,8},{8,4},{12,0},{1,13},{5,9},{9,5},{13,1},{2,14},{6,10},... | collective-permute-start | bytes 196616 | tf_op jit(solution)/shard_map/ppermute | solution.py:153
  10.8 2.3 %collective-permute-start.4 = (s32[1,128]{1,0:T(1,128)S(1)}, s32[1,128]{1,0:T(1,128)S(1)}, u32[]{:S(2)}, u32[]{:S(2)}) collective-permute-start(s32[1,128]{1,0:T(1,128)S(1)} %shard_map.64.refs_6_.refs_5_), channel_id=1, source_target_pairs={{0,1},{1,0},{2,3},{3,2},{4,5},{5,4},{6,7},{7,6},{8,9},{9,8},{10,11... | collective-permute-start | bytes 1544 | tf_op jit(solution)/shard_map/ppermute | solution.py:153
  10.8 7.4 %collective-permute-start.6 = (bf16[16,2048]{1,0:T(8,128)(2,1)S(1)}, bf16[16,2048]{1,0:T(8,128)(2,1)S(1)}, u32[]{:S(2)}, u32[]{:S(2)}) collective-permute-start(bf16[16,2048]{1,0:T(8,128)(2,1)S(1)} %constant_dynamic-slice_fusion), channel_id=1, source_target_pairs={{0,14},{2,12},{4,10},{6,8},{8,6},{10,4},{12,2},{14,0},{1,15},{3,13... | collective-permute-start | bytes 196616 | tf_op jit(solution)/shard_map/ppermute | solution.py:158
  13.1 5.7 %collective-permute-start.5 = (bf16[16,2048]{1,0:T(8,128)(2,1)S(1)}, bf16[16,2048]{1,0:T(8,128)(2,1)S(1)}, u32[]{:S(2)}, u32[]{:S(2)}) collective-permute-start(bf16[16,2048]{1,0:T(8,128)(2,1)S(1)} %collective-permute-done.3.refs_2_), channel_id=1, source_target_pairs={{0,2},{2,0},{1,3},{3,1},{4,6},{6,4},{5,7},{7,5},{8,10},{10,8},{9,1... | collective-permute-start | bytes 196616 | tf_op jit(solution)/shard_map/ppermute | solution.py:153
  15.2 1.2 %copy-start.1 = (bf16[4,256,512]{2,1,0:T(8,128)(2,1)S(1)}, bf16[4,256,512]{2,1,0:T(8,128)(2,1)}, u32[]{:S(2)}) copy-start(bf16[4,256,512]{2,1,0:T(8,128)(2,1)} %refs_3_.1) | copy-start | bytes 3145732
  16.4 2.4 %copy-start.2 = (bf16[4,256,512]{2,1,0:T(8,128)(2,1)S(1)}, bf16[4,256,512]{2,1,0:T(8,128)(2,1)}, u32[]{:S(2)}) copy-start(bf16[4,256,512]{2,1,0:T(8,128)(2,1)} %refs_3_.1) | copy-start | bytes 3145732
  18.8 2.3 %copy-start.4 = (f32[4,256]{1,0:T(4,128)S(1)}, f32[4,256]{1,0:T(4,128)}, u32[]{:S(2)}) copy-start(f32[4,256]{1,0:T(4,128)} %refs_2_.1) | copy-start | bytes 12292
  19.8 1.2 %collective-permute-start.7 = (f32[4,256]{1,0:T(4,128)S(1)}, f32[4,256]{1,0:T(4,128)S(1)}, u32[]{:S(2)}, u32[]{:S(2)}) collective-permute-start(f32[4,256]{1,0:T(4,128)S(1)} %shard_map.66.refs_0_), channel_id=1, source_target_pairs={{0,1},{1,0},{2,3},{3,2},{4,5},{5,4},{6,7},{7,6},{8,9},{9,8},{10,11... | collective-permute-start | bytes 12296 | tf_op jit(solution)/shard_map/ppermute | solution.py:153
  22.5 5.4 %collective-permute-start.10 = (bf16[16,2048]{1,0:T(8,128)(2,1)S(1)}, bf16[16,2048]{1,0:T(8,128)(2,1)S(1)}, u32[]{:S(2)}, u32[]{:S(2)}) collective-permute-start(bf16[16,2048]{1,0:T(8,128)(2,1)S(1)} %get-tuple-element.28), channel_id=1, source_target_pairs={{0,2},{2,0},{1,3},{3,1},{4,6},{6,4},{5,7},{7,5},{8,10},{10,8},{9,1... | collective-permute-start | bytes 196616 | tf_op jit(solution)/shard_map/ppermute | solution.py:153
  23.8 12.9 %collective-permute-start.12 = (bf16[16,2048]{1,0:T(8,128)(2,1)S(1)}, bf16[16,2048]{1,0:T(8,128)(2,1)S(1)}, u32[]{:S(2)}, u32[]{:S(2)}) collective-permute-start(bf16[16,2048]{1,0:T(8,128)(2,1)S(1)} %get-tuple-element.29), channel_id=1, source_target_pairs={{0,12},{2,14},{4,8},{6,10},{8,4},{10,6},{12,0},{14,2},{1,13},{3,15... | collective-permute-start | bytes 196616 | tf_op jit(solution)/shard_map/ppermute | solution.py:158
  25.5 11.2 %collective-permute-start.13 = (bf16[16,2048]{1,0:T(8,128)(2,1)S(1)}, bf16[16,2048]{1,0:T(8,128)(2,1)S(1)}, u32[]{:S(2)}, u32[]{:S(2)}) collective-permute-start(bf16[16,2048]{1,0:T(8,128)(2,1)S(1)} %get-tuple-element.30), channel_id=1, source_target_pairs={{0,14},{2,12},{4,10},{6,8},{8,6},{10,4},{12,2},{14,0},{1,15},{3,13... | collective-permute-start | bytes 196616 | tf_op jit(solution)/shard_map/ppermute | solution.py:158
  27.8 7.7 %collective-permute-start.8 = (bf16[32,2048]{1,0:T(8,128)(2,1)S(1)}, bf16[32,2048]{1,0:T(8,128)(2,1)S(1)}, u32[]{:S(2)}, u32[]{:S(2)}) collective-permute-start(bf16[32,2048]{1,0:T(8,128)(2,1)S(1)} %get-tuple-element.26), channel_id=1, source_target_pairs={{0,4},{4,0},{8,12},{12,8},{1,5},{5,1},{9,13},{13,9},{2,6},{6,2},{1... | collective-permute-start | bytes 393224 | tf_op jit(solution)/shard_map/ppermute | solution.py:153
  27.9 8.9 %collective-permute-start.11 = (bf16[16,2048]{1,0:T(8,128)(2,1)S(1)}, bf16[16,2048]{1,0:T(8,128)(2,1)S(1)}, u32[]{:S(2)}, u32[]{:S(2)}) collective-permute-start(bf16[16,2048]{1,0:T(8,128)(2,1)S(1)} %add_convert_fusion), channel_id=1, source_target_pairs={{0,8},{4,12},{8,0},{12,4},{1,9},{5,13},{9,1},{13,5},{2,10},{6,14},... | collective-permute-start | bytes 196616 | tf_op jit(solution)/shard_map/ppermute | solution.py:153
  35.5 5.8 %copy-start.3 = (bf16[16,4096]{1,0:T(8,128)(2,1)S(1)}, bf16[16,4096]{1,0:T(8,128)(2,1)}, u32[]{:S(2)}) copy-start(bf16[16,4096]{1,0:T(8,128)(2,1)} %core_ref.1) | copy-start | bytes 393220
  35.6 4.3 %collective-permute-start.9 = (bf16[16,2048]{1,0:T(8,128)(2,1)S(1)}, bf16[16,2048]{1,0:T(8,128)(2,1)S(1)}, u32[]{:S(2)}, u32[]{:S(2)}) collective-permute-start(bf16[16,2048]{1,0:T(8,128)(2,1)S(1)} %slice.19), channel_id=1, source_target_pairs={{0,2},{2,0},{1,3},{3,1},{4,6},{6,4},{5,7},{7,5},{8,10},{10,8},{9,1... | collective-permute-start | bytes 196616 | tf_op jit(solution)/shard_map/ppermute | solution.py:153
  39.9 1.4 %collective-permute-start.14 = (f32[16,2048]{1,0:T(8,128)S(1)}, f32[16,2048]{1,0:T(8,128)S(1)}, u32[]{:S(2)}, u32[]{:S(2)}) collective-permute-start(f32[16,2048]{1,0:T(8,128)S(1)} %fusion.2.mine_ref), channel_id=1, source_target_pairs={{0,1},{1,0},{2,3},{3,2},{4,5},{5,4},{6,7},{7,6},{8,9},{9,8},{10,11... | collective-permute-start | bytes 393224 | tf_op jit(solution)/shard_map/ppermute | solution.py:153

commit v15 on v13

--- a/solution.py
+++ b/solution.py
@@ -27,7 +27,9 @@
     lane = lax.broadcasted_iota(jnp.int32, (kept, columns), 1)
     wanted = (at % groups) * GO + first + at // groups
     select = jnp.where(lane == wanted, 1.0, 0.0).astype(jnp.bfloat16)
-    for t in range(batches):
+
+    @pl.loop(0, batches)
+    def _(t):
         left_ref[t] = split_dot(values_ref[t], select, NT).astype(jnp.bfloat16)
         left_t_ref[t] = split_dot(select, values_ref[t], NT).astype(jnp.bfloat16)
 
@@ -66,30 +68,34 @@
         table[blocks[0] * held:(blocks[-1] + 1) * held, :] = ref[...]
     pick = row_table(place_ref, core_ref, own_ref, other_ref, held, owners).T.astype(jnp.bfloat16)
     low = lax.broadcasted_iota(jnp.int32, (1, 1, 1, groups, 128), 4) < GO
-    for chunk in range(table.shape[1] // 256):
-        wide = split_dot(pick, table[:, chunk * 256:(chunk + 1) * 256])
-        for j in (2 * chunk, 2 * chunk + 1):
-            got = wide[:, (j % 2) * 128:(j % 2 + 1) * 128].reshape(2, batches, groups // 4, 2, groups, 128)
+    @pl.loop(0, table.shape[1] // 256)
+    def _(chunk):
+        wide = split_dot(pick, table[:, pl.ds(pl.multiple_of(chunk * 256, 256), 256)])
+        for j in range(2):
+            got = wide[:, j * 128:(j + 1) * 128].reshape(2, batches, groups // 4, 2, groups, 128)
             even, odd = got[:, :, :, 0], got[:, :, :, 1]
             first = jnp.where(low, even, pltpu.roll(odd, GO, 4))
             second = jnp.where(low, pltpu.roll(even, GO, 4), odd)
+            rows = pl.ds(pl.multiple_of((2 * chunk + j) * 2 * groups, 2 * groups), 2 * groups)
             for t in range(batches):
                 for q in range(groups // 2):
                     at = (q // (groups // 4), t, q % (groups // 4))
                     both = jnp.concatenate([first[at], second[at]], axis=0)
-                    dense[t, j * 2 * groups:(j + 1) * 2 * groups, q * 128:(q + 1) * 128] = both.astype(jnp.bfloat16)
-    for t in range(batches):
+                    dense[t, rows, q * 128:(q + 1) * 128] = both.astype(jnp.bfloat16)
+
+    @pl.loop(0, batches)
+    def _(t):
         product = split_dot(left_ref[t], dense[t]) * values_ref[t].astype(jnp.float32)
         folded = product[:, :128]
         for q in range(1, columns // 128):
             folded = folded + product[:, q * 128:(q + 1) * 128]
-        out_ref[t:t + 1, :] = jnp.sum(folded.T, axis=0, keepdims=True)
+        out_ref[pl.ds(t, 1), :] = jnp.sum(folded.T, axis=0, keepdims=True)
 
 
 def scatter_kernel(places, place_ref, core_ref, *refs):
     mine_ref, far_ref, weight_ref, values_ref, left_t_ref, own_ref, other_ref = refs[:7]
-    out_refs = refs[7:-2]
-    high, rest = refs[-2:]
+    out_refs = refs[7:-3]
+    high, rest, potential = refs[-3:]
     target = {k: (ref, i) for ref, blocks in zip(out_refs, places) for i, k in enumerate(blocks)}
     pieces = len(target)
     held = out_refs[0].shape[0] // len(places[0])
@@ -98,10 +104,12 @@
     groups = columns // GO
     kept = left_t_ref.shape[1]
     steps = kept // (2 * groups)
-    potential = weight_ref[...] * jnp.tanh(mine_ref[...] + far_ref[...])
+    potential[...] = weight_ref[...] * jnp.tanh(mine_ref[...] + far_ref[...])
     low = lax.broadcasted_iota(jnp.int32, (1, groups, 128), 2) < GO
-    for t in range(batches):
-        factor = jnp.broadcast_to(potential[t:t + 1, :], (128, points)).T
+
+    @pl.loop(0, batches)
+    def _(t):
+        factor = jnp.broadcast_to(potential[pl.ds(t, 1), :], (128, points)).T
         factor = jnp.concatenate([factor] * (columns // 128), axis=1)
         weighted = (values_ref[t].astype(jnp.float32) * factor).astype(jnp.bfloat16)
         part = split_dot(left_t_ref[t], weighted)
@@ -112,18 +120,24 @@
             odd = jnp.where(low, pltpu.roll(first, GO, 2), second)
             side, pair = q // (groups // 4), q % (groups // 4)
             at = ((side * batches + t) * (groups // 2) + 2 * pair) * groups
+            rows = pl.ds(pl.multiple_of(at, 2 * groups), 2 * groups)
             for j in range(steps):
                 both = jnp.concatenate([even[j], odd[j]], axis=0)
                 top = both.astype(jnp.bfloat16)
-                high[at:at + 2 * groups, j * 128:(j + 1) * 128] = top
-                rest[at:at + 2 * groups, j * 128:(j + 1) * 128] = (both - top.astype(jnp.float32)).astype(jnp.bfloat16)
+                high[rows, j * 128:(j + 1) * 128] = top
+                rest[rows, j * 128:(j + 1) * 128] = (both - top.astype(jnp.float32)).astype(jnp.bfloat16)
+
     step = max(1, min(pieces, 128 // held))
     for k in range(0, pieces, step):
-        some = put[k * held:(k + step) * held, :]
-        total = split_dot(some, high[...]) + split_dot(some, rest[...])
-        for i in range(step):
-            ref, at = target[k + i]
-            ref[at * held:(at + 1) * held, :] = total[i * held:(i + 1) * held, :].astype(jnp.bfloat16)
+
+        @pl.loop(0, high.shape[1] // 512)
+        def _(chunk):
+            lanes = pl.ds(pl.multiple_of(chunk * 512, 512), 512)
+            some = put[k * held:(k + step) * held, :]
+            total = split_dot(some, high[:, lanes]) + split_dot(some, rest[:, lanes])
+            for i in range(step):
+                ref, at = target[k + i]
+                ref[at * held:(at + 1) * held, lanes] = total[i * held:(i + 1) * held, :].astype(jnp.bfloat16)
 
 
 def finish_kernel(half_ref, mine_ref, other_ref, core_ref, out_ref):
@@ -182,11 +196,11 @@
     direct = {dz: swap(mine, "batch", rows_z, dz) for dz in far}
     beside = [swap(mine, "pair", rows_x, dx) for dx in side]
     *beside, own_rows = lax.optimization_barrier((*beside, own_rows))
-    arrays, places = [mine, *beside], [[dx] for dx in range(rows_x)]
+    cluster = jnp.concatenate([mine, *beside], axis=0)
+    arrays, places = [cluster], [list(range(rows_x))]
     for dz in near:
-        for dx, piece in enumerate([mine, *beside]):
-            arrays.append(swap(piece, "batch", rows_z, dz))
-            places.append([dz * rows_x + dx])
+        arrays.append(swap(cluster, "batch", rows_z, dz))
+        places.append(list(range(dz * rows_x, (dz + 1) * rows_x)))
     direct[far[0]], other_rows = lax.optimization_barrier((direct[far[0]], other_rows))
     for dz in far:
         arrays.append(direct[dz])
@@ -229,7 +243,7 @@
         [jax.ShapeDtypeStruct((held * len(blocks), wide), bf16) for blocks in out_places],
         7,
         scalars=2,
-        scratch=(pltpu.VMEM((entries, wide), bf16), pltpu.VMEM((entries, wide), bf16)),
+        scratch=(pltpu.VMEM((entries, wide), bf16), pltpu.VMEM((entries, wide), bf16), pltpu.VMEM((batches, points), f32)),
         flops=2 * batches * points * columns * kept,
         moved=2 * batches * points * columns * 2,
     )(place, core_at, partial, partial_other, point_weights, basis_values, left_t, own_rows, other_rows)

time: 37.5 us -> 40.7 us (1.085)
  Pallas kernels: 4.15 us -> 8.85 us
  starting transfers between devices: 17 us -> 15.6 us
    pallas_call x1, Pallas kernels: 1.06 us -> 3.44 us  [per_device(): call(functools.partial(density_kernel, places), jax.ShapeDtypeStruct((bat...]
    pallas_call x1, Pallas kernels: 1.4 us -> 3.03 us  [per_device(): call(functools.partial(scatter_kernel, out_places), [jax.ShapeDtypeStruct...]
    ppermute x16 -> x15, starting transfers between devices: 17 us -> 15.6 us  [swap(): return lax.ppermute(array, axis, [(i, i ^ step) for i in range(count)])]
    pallas_call x1, Pallas kernels: 0.76 us -> 1.46 us  [per_device(): call(prepare_kernel, (jax.ShapeDtypeStruct((batches, points, kept), bf16)...]
    ppermute x16 -> x15, waiting for transfers between devices: 13.1 us -> 13 us  [swap(): return lax.ppermute(array, axis, [(i, i ^ step) for i in range(count)])]
  transfers between devices with their start and end apart: 16 -> 15, of which waited for: 9 -> 8; matrix products, arithmetic and copies ran while one was open for 0% -> 0% of each run, Pallas kernels for 3% -> 4%
where the time goes in v15:
time: 40.7 us; the launch traced here: 40.5 us
  starting transfers between devices  15.6 us (38%)
  waiting for transfers between devices  13 us (32%)
  Pallas kernels  8.85 us (22%)
  local copies, waits for them, and re-layouts  2.84 us (7%)
    ppermute x15, starting transfers between devices, swap(): return lax.ppermute(array, axis, [(i, i ^ step) for i in range(count)])  15.6 us
    ppermute x15, waiting for transfers between devices, swap(): return lax.ppermute(array, axis, [(i, i ^ step) for i in range(count)])  13 us
    pallas_call x1, Pallas kernels, per_device(): call(functools.partial(density_kernel, places), jax.ShapeDtypeStruct((bat...  3.44 us
    pallas_call x1, Pallas kernels, per_device(): call(functools.partial(scatter_kernel, out_places), [jax.ShapeDtypeStruct...  3.03 us
    unnamed x14, local copies, waits for them, and re-layouts  2.74 us
    pallas_call x1, Pallas kernels, per_device(): call(prepare_kernel, (jax.ShapeDtypeStruct((batches, points, kept), bf16)...  1.46 us
  transfers between devices with their start and end apart: 15, of which 8 were waited for; matrix products, arithmetic and copies ran while one was open for 0% of the time, Pallas kernels for 4%

profile of v15, /device:TPU:0, one launch (start us, length us, event | category | flops | bytes accessed | tf_op | source)
XLA Modules:
  0.0 40.5 jit_solution(238749757261481324)
XLA Ops:
  0.0 0.0 copy-start
  0.0 0.9 %copy-done = bf16[16,4096]{1,0:T(8,128)(2,1)S(1)} copy-done((bf16[16,4096]{1,0:T(8,128)(2,1)S(1)}, bf16[16,4096]{1,0:T(8,128)(2,1)}, u32[]{:S(2)}) %copy-start) | copy-done | bytes 131096
  0.9 0.0 copy-start.6
  0.9 3.0 %collective-permute-start.1 = (bf16[16,2048]{1,0:T(8,128)(2,1)S(1)}, bf16[16,2048]{1,0:T(8,128)(2,1)S(1)}, u32[]{:S(2)}, u32[]{:S(2)}) collective-permute-start(bf16[16,2048]{1,0:T(8,128)(2,1)S(1)} %constant_dynamic-slice_fusion), channel_id=1, source_target_pairs={{0,2},{2,0},{1,3},{3,1},{4,6},{6,4},{5,7},{7,5},{8,10},{10,8},{9,1... | collective-permute-start | bytes 196616 | tf_op jit(solution)/shard_map/ppermute | solution.py:167
  3.9 2.6 %collective-permute-start.3 = (bf16[16,2048]{1,0:T(8,128)(2,1)S(1)}, bf16[16,2048]{1,0:T(8,128)(2,1)S(1)}, u32[]{:S(2)}, u32[]{:S(2)}) collective-permute-start(bf16[16,2048]{1,0:T(8,128)(2,1)S(1)} %constant_dynamic-slice_fusion), channel_id=1, source_target_pairs={{0,8},{4,12},{8,0},{12,4},{1,9},{5,13},{9,1},{13,5},{2,10},{6,14},... | collective-permute-start | bytes 196616 | tf_op jit(solution)/shard_map/ppermute | solution.py:167
  6.5 1.3 %collective-permute-start = (bf16[16,2048]{1,0:T(8,128)(2,1)S(1)}, bf16[16,2048]{1,0:T(8,128)(2,1)S(1)}, u32[]{:S(2)}, u32[]{:S(2)}) collective-permute-start(bf16[16,2048]{1,0:T(8,128)(2,1)S(1)} %constant_dynamic-slice_fusion), channel_id=1, source_target_pairs={{0,12},{4,8},{8,4},{12,0},{1,13},{5,9},{9,5},{13,1},{2,14},{6,10},... | collective-permute-start | bytes 196616 | tf_op jit(solution)/shard_map/ppermute | solution.py:167
  7.9 0.0 copy-done.6
  7.9 0.1 reshape.16.slots_ref
  7.9 0.6 %copy-done.5 = s32[1,1,8,8]{3,2,1,0:T(8,128)S(1)} copy-done((s32[1,1,8,8]{3,2,1,0:T(8,128)S(1)}, s32[1,1,8,8]{3,2,1,0:T(8,128)}, u32[]{:S(2)}) %copy-start.5) | copy-done | bytes 280
  8.5 0.2 shard_map.64.refs_6_.refs_5_
  8.7 0.0 collective-permute-done.1
  8.8 0.3 collective-permute-start.2
  9.1 0.0 collective-permute-start.4
  9.1 1.1 %collective-permute-done.4.refs_7_.refs_6_ = s32[1,128]{1,0:T(1,128)S(1)} collective-permute-done((s32[1,128]{1,0:T(1,128)S(1)}, s32[1,128]{1,0:T(1,128)S(1)}, u32[]{:S(2)}, u32[]{:S(2)}) %collective-permute-start.4) | collective-permute-done | bytes 544 | tf_op jit(solution)/shard_map/ppermute | solution.py:167
  10.2 0.0 collective-permute-done.3.refs_2_
  10.2 0.8 %collective-permute-start.5 = (bf16[16,2048]{1,0:T(8,128)(2,1)S(1)}, bf16[16,2048]{1,0:T(8,128)(2,1)S(1)}, u32[]{:S(2)}, u32[]{:S(2)}) collective-permute-start(bf16[16,2048]{1,0:T(8,128)(2,1)S(1)} %collective-permute-done.3.refs_2_), channel_id=1, source_target_pairs={{0,2},{2,0},{1,3},{3,1},{4,6},{6,4},{5,7},{7,5},{8,10},{10,8},{9,1... | collective-permute-start | bytes 196616 | tf_op jit(solution)/shard_map/ppermute | solution.py:167
  11.0 2.3 %collective-permute-done.refs_4_ = bf16[16,2048]{1,0:T(8,128)(2,1)S(1)} collective-permute-done((bf16[16,2048]{1,0:T(8,128)(2,1)S(1)}, bf16[16,2048]{1,0:T(8,128)(2,1)S(1)}, u32[]{:S(2)}, u32[]{:S(2)}) %collective-permute-start) | collective-permute-done | bytes 65568 | tf_op jit(solution)/shard_map/ppermute | solution.py:167
  13.3 0.5 %collective-permute-start.6 = (bf16[16,2048]{1,0:T(8,128)(2,1)S(1)}, bf16[16,2048]{1,0:T(8,128)(2,1)S(1)}, u32[]{:S(2)}, u32[]{:S(2)}) collective-permute-start(bf16[16,2048]{1,0:T(8,128)(2,1)S(1)} %collective-permute-done.refs_4_), channel_id=1, source_target_pairs={{0,2},{2,0},{1,3},{3,1},{4,6},{6,4},{5,7},{7,5},{8,10},{10,8},{9,1... | collective-permute-start | bytes 196616 | tf_op jit(solution)/shard_map/ppermute | solution.py:167
  13.8 0.0 copy-start.1
  13.8 1.2 %copy-done.1 = bf16[4,256,512]{2,1,0:T(8,128)(2,1)S(1)} copy-done((bf16[4,256,512]{2,1,0:T(8,128)(2,1)S(1)}, bf16[4,256,512]{2,1,0:T(8,128)(2,1)}, u32[]{:S(2)}) %copy-start.1) | copy-done | bytes 1048600
  15.0 0.0 copy-start.2
  15.0 1.5 %shard_map.65 = (bf16[4,256,256]{2,1,0:T(8,128)(2,1)S(1)}, bf16[4,256,256]{2,1,0:T(8,128)(2,1)S(1)}) custom-call(s32[1]{0:T(128)} %bitcast.half_ref.core_ref, bf16[4,256,512]{2,1,0:T(8,128)(2,1)S(1)} %copy-done.1), custom_call_target="tpu_custom_call" | custom-call | flops 536870912 | bytes 3145728 | tf_op jit(solution)/shard_map/pallas_call | solution.py:213
  16.5 0.0 collective-permute-done.5.refs_3_
  16.5 1.0 %collective-permute-done.6.refs_5_ = bf16[16,2048]{1,0:T(8,128)(2,1)S(1)} collective-permute-done((bf16[16,2048]{1,0:T(8,128)(2,1)S(1)}, bf16[16,2048]{1,0:T(8,128)(2,1)S(1)}, u32[]{:S(2)}, u32[]{:S(2)}) %collective-permute-start.6) | collective-permute-done | bytes 65568 | tf_op jit(solution)/shard_map/ppermute | solution.py:167
  17.5 0.0 collective-permute-done.2.refs_1_
  17.5 0.0 copy-done.2
  17.5 3.4 %shard_map.66.refs_0_ = f32[4,256]{1,0:T(4,128)S(1)} custom-call(s32[1]{0:T(128)} %bitcast.1.place_ref, s32[1]{0:T(128)} %bitcast.half_ref.core_ref, bf16[32,2048]{1,0:T(8,128)(2,1)S(1)} %pad_maximum_fusion.refs_0_, bf16[32,2048]{1,0:T(8,128)(2,1)S(1)} %collective-permute-done.2.refs_1_, bf16[16,2048]{1,0:T(8,128)(2,1)S(1)} %collective-permute-done.3.refs_2_, ...), custom_call_target="tpu_custom_call" | custom-call | flops 268435456 | bytes 2097152 | tf_op jit(solution)/shard_map/pallas_call | solution.py:228
  21.0 0.1 collective-permute-start.7
  21.1 1.2 %collective-permute-done.7.refs_1_ = f32[4,256]{1,0:T(4,128)S(1)} collective-permute-done((f32[4,256]{1,0:T(4,128)S(1)}, f32[4,256]{1,0:T(4,128)S(1)}, u32[]{:S(2)}, u32[]{:S(2)}) %collective-permute-start.7) | collective-permute-done | bytes 4128 | tf_op jit(solution)/shard_map/ppermute | solution.py:167
  22.2 0.0 copy-done.4
  22.2 3.0 %shard_map.67 = (bf16[32,2048]{1,0:T(8,128)(2,1)S(1)}, bf16[32,2048]{1,0:T(8,128)(2,1)S(1)}, bf16[16,2048]{1,0:T(8,128)(2,1)S(1)}, bf16[16,2048]{1,0:T(8,128)(2,...) custom-call(s32[1]{0:T(128)} %bitcast.1.place_ref, s32[1]{0:T(128)} %bitcast.half_ref.core_ref, ...), custom_call_target="tpu_custom_call" | custom-call | flops 268435456 | bytes 2097152 | tf_op jit(solution)/shard_map/pallas_call | solution.py:241
  25.3 0.6 %collective-permute-start.10 = (bf16[16,2048]{1,0:T(8,128)(2,1)S(1)}, bf16[16,2048]{1,0:T(8,128)(2,1)S(1)}, u32[]{:S(2)}, u32[]{:S(2)}) collective-permute-start(bf16[16,2048]{1,0:T(8,128)(2,1)S(1)} %get-tuple-element.28), channel_id=1, source_target_pairs={{0,2},{2,0},{1,3},{3,1},{4,6},{6,4},{5,7},{7,5},{8,10},{10,8},{9,1... | collective-permute-start | bytes 196616 | tf_op jit(solution)/shard_map/ppermute | solution.py:167
  25.8 1.5 %collective-permute-start.12 = (bf16[16,2048]{1,0:T(8,128)(2,1)S(1)}, bf16[16,2048]{1,0:T(8,128)(2,1)S(1)}, u32[]{:S(2)}, u32[]{:S(2)}) collective-permute-start(bf16[16,2048]{1,0:T(8,128)(2,1)S(1)} %get-tuple-element.30), channel_id=1, source_target_pairs={{0,2},{2,0},{1,3},{3,1},{4,6},{6,4},{5,7},{7,5},{8,10},{10,8},{9,1... | collective-permute-start | bytes 196616 | tf_op jit(solution)/shard_map/ppermute | solution.py:167
  27.4 0.1 collective-permute-start.8
  27.5 2.7 %collective-permute-done.10 = bf16[16,2048]{1,0:T(8,128)(2,1)S(1)} collective-permute-done((bf16[16,2048]{1,0:T(8,128)(2,1)S(1)}, bf16[16,2048]{1,0:T(8,128)(2,1)S(1)}, u32[]{:S(2)}, u32[]{:S(2)}) %collective-permute-start.10) | collective-permute-done | bytes 65568 | tf_op jit(solution)/shard_map/ppermute | solution.py:167
  30.2 2.0 %collective-permute-start.11 = (bf16[16,2048]{1,0:T(8,128)(2,1)S(1)}, bf16[16,2048]{1,0:T(8,128)(2,1)S(1)}, u32[]{:S(2)}, u32[]{:S(2)}) collective-permute-start(bf16[16,2048]{1,0:T(8,128)(2,1)S(1)} %add_convert_fusion.1), channel_id=1, source_target_pairs={{0,8},{4,12},{8,0},{12,4},{1,9},{5,13},{9,1},{13,5},{2,10},{6,14},... | collective-permute-start | bytes 196616 | tf_op jit(solution)/shard_map/ppermute | solution.py:167
  32.1 0.0 collective-permute-done.12
  32.2 1.4 %collective-permute-start.13 = (bf16[16,2048]{1,0:T(8,128)(2,1)S(1)}, bf16[16,2048]{1,0:T(8,128)(2,1)S(1)}, u32[]{:S(2)}, u32[]{:S(2)}) collective-permute-start(bf16[16,2048]{1,0:T(8,128)(2,1)S(1)} %add_convert_fusion), channel_id=1, source_target_pairs={{0,12},{4,8},{8,4},{12,0},{1,13},{5,9},{9,5},{13,1},{2,14},{6,10},... | collective-permute-start | bytes 196616 | tf_op jit(solution)/shard_map/ppermute | solution.py:167
  33.6 0.0 collective-permute-done.8
  33.6 0.0 copy-start.3
  33.6 1.3 %collective-permute-start.9 = (bf16[16,2048]{1,0:T(8,128)(2,1)S(1)}, bf16[16,2048]{1,0:T(8,128)(2,1)S(1)}, u32[]{:S(2)}, u32[]{:S(2)}) collective-permute-start(bf16[16,2048]{1,0:T(8,128)(2,1)S(1)} %slice.17), channel_id=1, source_target_pairs={{0,2},{2,0},{1,3},{3,1},{4,6},{6,4},{5,7},{7,5},{8,10},{10,8},{9,1... | collective-permute-start | bytes 196616 | tf_op jit(solution)/shard_map/ppermute | solution.py:167
  34.9 1.5 %collective-permute-done.11 = bf16[16,2048]{1,0:T(8,128)(2,1)S(1)} collective-permute-done((bf16[16,2048]{1,0:T(8,128)(2,1)S(1)}, bf16[16,2048]{1,0:T(8,128)(2,1)S(1)}, u32[]{:S(2)}, u32[]{:S(2)}) %collective-permute-start.11) | collective-permute-done | bytes 65568 | tf_op jit(solution)/shard_map/ppermute | solution.py:167
  36.5 1.8 %collective-permute-done.13 = bf16[16,2048]{1,0:T(8,128)(2,1)S(1)} collective-permute-done((bf16[16,2048]{1,0:T(8,128)(2,1)S(1)}, bf16[16,2048]{1,0:T(8,128)(2,1)S(1)}, u32[]{:S(2)}, u32[]{:S(2)}) %collective-permute-start.13) | collective-permute-done | bytes 65568 | tf_op jit(solution)/shard_map/ppermute | solution.py:167
  38.3 0.0 collective-permute-done.9
  38.3 0.1 collective-permute-start.14
  38.4 1.3 %collective-permute-done.14.other_ref = f32[16,2048]{1,0:T(8,128)S(1)} collective-permute-done((f32[16,2048]{1,0:T(8,128)S(1)}, f32[16,2048]{1,0:T(8,128)S(1)}, u32[]{:S(2)}, u32[]{:S(2)}) %collective-permute-start.14) | collective-permute-done | bytes 131104 | tf_op jit(solution)/shard_map/ppermute | solution.py:167
  39.8 0.0 copy-done.3
  39.8 0.7 %shard_map.68 = f32[16,4096]{1,0:T(8,128)} custom-call(s32[1]{0:T(128)} %bitcast.half_ref.core_ref, f32[16,2048]{1,0:T(8,128)S(1)} %fusion.1.mine_ref, f32[16,2048]{1,0:T(8,128)S(1)} %collective-permute-done.14.other_ref, bf16[16,4096]{1,0:T(8,128)(2,1)S(1)} %copy-done.3), custom_call_target="tpu_custom_call" | custom-call | bytes 786432 | tf_op jit(solution)/shard_map/pallas_call | solution.py:267
  (9 shorter events, 0.1 us)
Async XLA Ops:
  0.0 0.9 %copy-start = (bf16[16,4096]{1,0:T(8,128)(2,1)S(1)}, bf16[16,4096]{1,0:T(8,128)(2,1)}, u32[]{:S(2)}) copy-start(bf16[16,4096]{1,0:T(8,128)(2,1)} %param.10) | copy-start | bytes 393220
  0.9 6.9 %copy-start.6 = (s32[4,8,4]{1,2,0:T(4,128)S(1)}, s32[4,8,4]{1,2,0:T(4,128)}, u32[]{:S(2)}) copy-start(s32[4,8,4]{1,2,0:T(4,128)} %param.8) | copy-start | bytes 1540
  0.9 7.8 %collective-permute-start.1 = (bf16[16,2048]{1,0:T(8,128)(2,1)S(1)}, bf16[16,2048]{1,0:T(8,128)(2,1)S(1)}, u32[]{:S(2)}, u32[]{:S(2)}) collective-permute-start(bf16[16,2048]{1,0:T(8,128)(2,1)S(1)} %constant_dynamic-slice_fusion), channel_id=1, source_target_pairs={{0,2},{2,0},{1,3},{3,1},{4,6},{6,4},{5,7},{7,5},{8,10},{10,8},{9,1... | collective-permute-start | bytes 196616 | tf_op jit(solution)/shard_map/ppermute | solution.py:167
  3.9 6.3 %collective-permute-start.3 = (bf16[16,2048]{1,0:T(8,128)(2,1)S(1)}, bf16[16,2048]{1,0:T(8,128)(2,1)S(1)}, u32[]{:S(2)}, u32[]{:S(2)}) collective-permute-start(bf16[16,2048]{1,0:T(8,128)(2,1)S(1)} %constant_dynamic-slice_fusion), channel_id=1, source_target_pairs={{0,8},{4,12},{8,0},{12,4},{1,9},{5,13},{9,1},{13,5},{2,10},{6,14},... | collective-permute-start | bytes 196616 | tf_op jit(solution)/shard_map/ppermute | solution.py:167
  6.5 6.8 %collective-permute-start = (bf16[16,2048]{1,0:T(8,128)(2,1)S(1)}, bf16[16,2048]{1,0:T(8,128)(2,1)S(1)}, u32[]{:S(2)}, u32[]{:S(2)}) collective-permute-start(bf16[16,2048]{1,0:T(8,128)(2,1)S(1)} %constant_dynamic-slice_fusion), channel_id=1, source_target_pairs={{0,12},{4,8},{8,4},{12,0},{1,13},{5,9},{9,5},{13,1},{2,14},{6,10},... | collective-permute-start | bytes 196616 | tf_op jit(solution)/shard_map/ppermute | solution.py:167
  7.9 0.7 %copy-start.5 = (s32[1,1,8,8]{3,2,1,0:T(8,128)S(1)}, s32[1,1,8,8]{3,2,1,0:T(8,128)}, u32[]{:S(2)}) copy-start(s32[1,1,8,8]{3,2,1,0:T(8,128)} %param.9) | copy-start | bytes 772
  8.8 8.8 %collective-permute-start.2 = (bf16[32,2048]{1,0:T(8,128)(2,1)S(1)}, bf16[32,2048]{1,0:T(8,128)(2,1)S(1)}, u32[]{:S(2)}, u32[]{:S(2)}) collective-permute-start(bf16[32,2048]{1,0:T(8,128)(2,1)S(1)} %pad_maximum_fusion.refs_0_), channel_id=1, source_target_pairs={{0,4},{4,0},{8,12},{12,8},{1,5},{5,1},{9,13},{13,9},{2,6},{6,2},{1... | collective-permute-start | bytes 393224 | tf_op jit(solution)/shard_map/ppermute | solution.py:167
  9.1 1.1 %collective-permute-start.4 = (s32[1,128]{1,0:T(1,128)S(1)}, s32[1,128]{1,0:T(1,128)S(1)}, u32[]{:S(2)}, u32[]{:S(2)}) collective-permute-start(s32[1,128]{1,0:T(1,128)S(1)} %shard_map.64.refs_6_.refs_5_), channel_id=1, source_target_pairs={{0,1},{1,0},{2,3},{3,2},{4,5},{5,4},{6,7},{7,6},{8,9},{9,8},{10,11... | collective-permute-start | bytes 1544 | tf_op jit(solution)/shard_map/ppermute | solution.py:167
  10.2 6.3 %collective-permute-start.5 = (bf16[16,2048]{1,0:T(8,128)(2,1)S(1)}, bf16[16,2048]{1,0:T(8,128)(2,1)S(1)}, u32[]{:S(2)}, u32[]{:S(2)}) collective-permute-start(bf16[16,2048]{1,0:T(8,128)(2,1)S(1)} %collective-permute-done.3.refs_2_), channel_id=1, source_target_pairs={{0,2},{2,0},{1,3},{3,1},{4,6},{6,4},{5,7},{7,5},{8,10},{10,8},{9,1... | collective-permute-start | bytes 196616 | tf_op jit(solution)/shard_map/ppermute | solution.py:167
  13.3 4.3 %collective-permute-start.6 = (bf16[16,2048]{1,0:T(8,128)(2,1)S(1)}, bf16[16,2048]{1,0:T(8,128)(2,1)S(1)}, u32[]{:S(2)}, u32[]{:S(2)}) collective-permute-start(bf16[16,2048]{1,0:T(8,128)(2,1)S(1)} %collective-permute-done.refs_4_), channel_id=1, source_target_pairs={{0,2},{2,0},{1,3},{3,1},{4,6},{6,4},{5,7},{7,5},{8,10},{10,8},{9,1... | collective-permute-start | bytes 196616 | tf_op jit(solution)/shard_map/ppermute | solution.py:167
  13.8 1.2 %copy-start.1 = (bf16[4,256,512]{2,1,0:T(8,128)(2,1)S(1)}, bf16[4,256,512]{2,1,0:T(8,128)(2,1)}, u32[]{:S(2)}) copy-start(bf16[4,256,512]{2,1,0:T(8,128)(2,1)} %refs_3_.1) | copy-start | bytes 3145732
  15.0 2.5 %copy-start.2 = (bf16[4,256,512]{2,1,0:T(8,128)(2,1)S(1)}, bf16[4,256,512]{2,1,0:T(8,128)(2,1)}, u32[]{:S(2)}) copy-start(bf16[4,256,512]{2,1,0:T(8,128)(2,1)} %refs_3_.1) | copy-start | bytes 3145732
  17.5 4.7 %copy-start.4 = (f32[4,256]{1,0:T(4,128)S(1)}, f32[4,256]{1,0:T(4,128)}, u32[]{:S(2)}) copy-start(f32[4,256]{1,0:T(4,128)} %refs_2_.1) | copy-start | bytes 12292
  21.0 1.2 %collective-permute-start.7 = (f32[4,256]{1,0:T(4,128)S(1)}, f32[4,256]{1,0:T(4,128)S(1)}, u32[]{:S(2)}, u32[]{:S(2)}) collective-permute-start(f32[4,256]{1,0:T(4,128)S(1)} %shard_map.66.refs_0_), channel_id=1, source_target_pairs={{0,1},{1,0},{2,3},{3,2},{4,5},{5,4},{6,7},{7,6},{8,9},{9,8},{10,11... | collective-permute-start | bytes 12296 | tf_op jit(solution)/shard_map/ppermute | solution.py:167
  25.3 4.9 %collective-permute-start.10 = (bf16[16,2048]{1,0:T(8,128)(2,1)S(1)}, bf16[16,2048]{1,0:T(8,128)(2,1)S(1)}, u32[]{:S(2)}, u32[]{:S(2)}) collective-permute-start(bf16[16,2048]{1,0:T(8,128)(2,1)S(1)} %get-tuple-element.28), channel_id=1, source_target_pairs={{0,2},{2,0},{1,3},{3,1},{4,6},{6,4},{5,7},{7,5},{8,10},{10,8},{9,1... | collective-permute-start | bytes 196616 | tf_op jit(solution)/shard_map/ppermute | solution.py:167
  25.8 6.3 %collective-permute-start.12 = (bf16[16,2048]{1,0:T(8,128)(2,1)S(1)}, bf16[16,2048]{1,0:T(8,128)(2,1)S(1)}, u32[]{:S(2)}, u32[]{:S(2)}) collective-permute-start(bf16[16,2048]{1,0:T(8,128)(2,1)S(1)} %get-tuple-element.30), channel_id=1, source_target_pairs={{0,2},{2,0},{1,3},{3,1},{4,6},{6,4},{5,7},{7,5},{8,10},{10,8},{9,1... | collective-permute-start | bytes 196616 | tf_op jit(solution)/shard_map/ppermute | solution.py:167
  27.4 6.2 %collective-permute-start.8 = (bf16[32,2048]{1,0:T(8,128)(2,1)S(1)}, bf16[32,2048]{1,0:T(8,128)(2,1)S(1)}, u32[]{:S(2)}, u32[]{:S(2)}) collective-permute-start(bf16[32,2048]{1,0:T(8,128)(2,1)S(1)} %get-tuple-element.26), channel_id=1, source_target_pairs={{0,4},{4,0},{8,12},{12,8},{1,5},{5,1},{9,13},{13,9},{2,6},{6,2},{1... | collective-permute-start | bytes 393224 | tf_op jit(solution)/shard_map/ppermute | solution.py:167
  30.2 6.3 %collective-permute-start.11 = (bf16[16,2048]{1,0:T(8,128)(2,1)S(1)}, bf16[16,2048]{1,0:T(8,128)(2,1)S(1)}, u32[]{:S(2)}, u32[]{:S(2)}) collective-permute-start(bf16[16,2048]{1,0:T(8,128)(2,1)S(1)} %add_convert_fusion.1), channel_id=1, source_target_pairs={{0,8},{4,12},{8,0},{12,4},{1,9},{5,13},{9,1},{13,5},{2,10},{6,14},... | collective-permute-start | bytes 196616 | tf_op jit(solution)/shard_map/ppermute | solution.py:167
  32.2 6.1 %collective-permute-start.13 = (bf16[16,2048]{1,0:T(8,128)(2,1)S(1)}, bf16[16,2048]{1,0:T(8,128)(2,1)S(1)}, u32[]{:S(2)}, u32[]{:S(2)}) collective-permute-start(bf16[16,2048]{1,0:T(8,128)(2,1)S(1)} %add_convert_fusion), channel_id=1, source_target_pairs={{0,12},{4,8},{8,4},{12,0},{1,13},{5,9},{9,5},{13,1},{2,14},{6,10},... | collective-permute-start | bytes 196616 | tf_op jit(solution)/shard_map/ppermute | solution.py:167
  33.6 6.1 %copy-start.3 = (bf16[16,4096]{1,0:T(8,128)(2,1)S(1)}, bf16[16,4096]{1,0:T(8,128)(2,1)}, u32[]{:S(2)}) copy-start(bf16[16,4096]{1,0:T(8,128)(2,1)} %core_ref.1) | copy-start | bytes 393220
  33.6 4.7 %collective-permute-start.9 = (bf16[16,2048]{1,0:T(8,128)(2,1)S(1)}, bf16[16,2048]{1,0:T(8,128)(2,1)S(1)}, u32[]{:S(2)}, u32[]{:S(2)}) collective-permute-start(bf16[16,2048]{1,0:T(8,128)(2,1)S(1)} %slice.17), channel_id=1, source_target_pairs={{0,2},{2,0},{1,3},{3,1},{4,6},{6,4},{5,7},{7,5},{8,10},{10,8},{9,1... | collective-permute-start | bytes 196616 | tf_op jit(solution)/shard_map/ppermute | solution.py:167
  38.3 1.4 %collective-permute-start.14 = (f32[16,2048]{1,0:T(8,128)S(1)}, f32[16,2048]{1,0:T(8,128)S(1)}, u32[]{:S(2)}, u32[]{:S(2)}) collective-permute-start(f32[16,2048]{1,0:T(8,128)S(1)} %fusion.1.mine_ref), channel_id=1, source_target_pairs={{0,1},{1,0},{2,3},{3,2},{4,5},{5,4},{6,7},{7,6},{8,9},{9,8},{10,11... | collective-permute-start | bytes 393224 | tf_op jit(solution)/shard_map/ppermute | solution.py:167

commit v16 on v13

--- a/solution.py
+++ b/solution.py
@@ -182,11 +182,11 @@
     direct = {dz: swap(mine, "batch", rows_z, dz) for dz in far}
     beside = [swap(mine, "pair", rows_x, dx) for dx in side]
     *beside, own_rows = lax.optimization_barrier((*beside, own_rows))
-    arrays, places = [mine, *beside], [[dx] for dx in range(rows_x)]
+    cluster = jnp.concatenate([mine, *beside], axis=0)
+    arrays, places = [cluster], [list(range(rows_x))]
     for dz in near:
-        for dx, piece in enumerate([mine, *beside]):
-            arrays.append(swap(piece, "batch", rows_z, dz))
-            places.append([dz * rows_x + dx])
+        arrays.append(swap(cluster, "batch", rows_z, dz))
+        places.append(list(range(dz * rows_x, (dz + 1) * rows_x)))
     direct[far[0]], other_rows = lax.optimization_barrier((direct[far[0]], other_rows))
     for dz in far:
         arrays.append(direct[dz])
@@ -223,7 +223,7 @@
     partial_other = swap(partial, "orb", 2, 1)
 
     out_places = [list(range(dz * rows_x, (dz + 1) * rows_x)) for dz in [0] + near]
-    out_places += [[dz * rows_x + dx] for dz in far for dx in [0] + side]
+    out_places += [[dz * rows_x + dx for dz in far] for dx in [0] + side]
     sums = call(
         functools.partial(scatter_kernel, out_places),
         [jax.ShapeDtypeStruct((held * len(blocks), wide), bf16) for blocks in out_places],
@@ -234,14 +234,14 @@
         moved=2 * batches * points * columns * 2,
     )(place, core_at, partial, partial_other, point_weights, basis_values, left_t, own_rows, other_rows)
 
-    clusters, singles = sums[:len(near) + 1], sums[len(near) + 1:]
-    landed = []
-    for i, dz in enumerate(far):
-        joined = singles[i * rows_x].astype(f32)
-        for dx in side:
-            joined = joined + swap(singles[i * rows_x + dx], "pair", rows_x, dx).astype(f32)
-        landed.append(swap(joined.astype(bf16), "batch", rows_z, dz).astype(f32))
-    cluster = clusters[0].astype(f32)
+    clusters, middles = sums[:len(near) + 1], sums[len(near) + 1:]
+    joined = middles[0].astype(f32)
+    for dx in side:
+        joined = joined + swap(middles[dx], "pair", rows_x, dx).astype(f32)
+    joined = joined.astype(bf16)
+    joined, cluster = lax.optimization_barrier((joined, clusters[0]))
+    landed = [swap(joined[i * held:(i + 1) * held], "batch", rows_z, dz).astype(f32) for i, dz in enumerate(far)]
+    cluster = cluster.astype(f32)
     for dz, array in zip(near, clusters[1:]):
         cluster = cluster + swap(array, "batch", rows_z, dz).astype(f32)
     total = cluster[:held]

time: 37.5 us -> 37.5 us (level)
  starting transfers between devices: 17 us -> 13.7 us
  waiting for transfers between devices: 13.1 us -> 16.4 us
    ppermute x16 -> x14, starting transfers between devices: 17 us -> 13.7 us  [swap(): return lax.ppermute(array, axis, [(i, i ^ step) for i in range(count)])]
    ppermute x16 -> x14, waiting for transfers between devices: 13.1 us -> 16.4 us  [swap(): return lax.ppermute(array, axis, [(i, i ^ step) for i in range(count)])]
  transfers between devices with their start and end apart: 16 -> 14, of which waited for: 9 -> 8; matrix products, arithmetic and copies ran while one was open for 0% -> 0% of each run, Pallas kernels for 3% -> 3%
where the time goes in v16:
time: 37.5 us; the launch traced here: 37.3 us
  waiting for transfers between devices  16.4 us (44%)
  starting transfers between devices  13.7 us (37%)
  Pallas kernels  4.15 us (11%)
  local copies, waits for them, and re-layouts  2.86 us (8%)
    ppermute x14, waiting for transfers between devices, swap(): return lax.ppermute(array, axis, [(i, i ^ step) for i in range(count)])  16.4 us
    ppermute x14, starting transfers between devices, swap(): return lax.ppermute(array, axis, [(i, i ^ step) for i in range(count)])  13.7 us
    unnamed x14, local copies, waits for them, and re-layouts  2.74 us
    pallas_call x1, Pallas kernels, per_device(): call(functools.partial(scatter_kernel, out_places), [jax.ShapeDtypeStruct...  1.4 us
    pallas_call x1, Pallas kernels, per_device(): call(functools.partial(density_kernel, places), jax.ShapeDtypeStruct((bat...  1.07 us
    pallas_call x1, Pallas kernels, per_device(): call(prepare_kernel, (jax.ShapeDtypeStruct((batches, points, kept), bf16)...  0.76 us
  transfers between devices with their start and end apart: 14, of which 8 were waited for; matrix products, arithmetic and copies ran while one was open for 0% of the time, Pallas kernels for 3%

profile of v16, /device:TPU:0, one launch (start us, length us, event | category | flops | bytes accessed | tf_op | source)
XLA Modules:
  0.0 37.3 jit_solution(17257794609267005127)
XLA Ops:
  0.0 0.0 copy-start
  0.0 0.9 %copy-done = bf16[16,4096]{1,0:T(8,128)(2,1)S(1)} copy-done((bf16[16,4096]{1,0:T(8,128)(2,1)S(1)}, bf16[16,4096]{1,0:T(8,128)(2,1)}, u32[]{:S(2)}) %copy-start) | copy-done | bytes 131096
  0.9 0.0 copy-start.6
  0.9 3.0 %collective-permute-start.1 = (bf16[16,2048]{1,0:T(8,128)(2,1)S(1)}, bf16[16,2048]{1,0:T(8,128)(2,1)S(1)}, u32[]{:S(2)}, u32[]{:S(2)}) collective-permute-start(bf16[16,2048]{1,0:T(8,128)(2,1)S(1)} %constant_dynamic-slice_fusion), channel_id=1, source_target_pairs={{0,2},{2,0},{1,3},{3,1},{4,6},{6,4},{5,7},{7,5},{8,10},{10,8},{9,1... | collective-permute-start | bytes 196616 | tf_op jit(solution)/shard_map/ppermute | solution.py:153
  3.9 2.6 %collective-permute-start.3 = (bf16[16,2048]{1,0:T(8,128)(2,1)S(1)}, bf16[16,2048]{1,0:T(8,128)(2,1)S(1)}, u32[]{:S(2)}, u32[]{:S(2)}) collective-permute-start(bf16[16,2048]{1,0:T(8,128)(2,1)S(1)} %constant_dynamic-slice_fusion), channel_id=1, source_target_pairs={{0,8},{4,12},{8,0},{12,4},{1,9},{5,13},{9,1},{13,5},{2,10},{6,14},... | collective-permute-start | bytes 196616 | tf_op jit(solution)/shard_map/ppermute | solution.py:153
  6.5 1.3 %collective-permute-start = (bf16[16,2048]{1,0:T(8,128)(2,1)S(1)}, bf16[16,2048]{1,0:T(8,128)(2,1)S(1)}, u32[]{:S(2)}, u32[]{:S(2)}) collective-permute-start(bf16[16,2048]{1,0:T(8,128)(2,1)S(1)} %constant_dynamic-slice_fusion), channel_id=1, source_target_pairs={{0,12},{4,8},{8,4},{12,0},{1,13},{5,9},{9,5},{13,1},{2,14},{6,10},... | collective-permute-start | bytes 196616 | tf_op jit(solution)/shard_map/ppermute | solution.py:153
  7.9 0.0 copy-done.6
  7.9 0.0 copy-start.5
  7.9 0.1 reshape.16.slots_ref
  7.9 0.6 %copy-done.5 = s32[1,1,8,8]{3,2,1,0:T(8,128)S(1)} copy-done((s32[1,1,8,8]{3,2,1,0:T(8,128)S(1)}, s32[1,1,8,8]{3,2,1,0:T(8,128)}, u32[]{:S(2)}) %copy-start.5) | copy-done | bytes 280
  8.5 0.2 shard_map.64.refs_6_.refs_5_
  8.7 0.0 collective-permute-done.1
  8.8 0.3 collective-permute-start.2
  9.1 0.0 collective-permute-start.4
  9.1 1.1 %collective-permute-done.4.refs_7_.refs_6_ = s32[1,128]{1,0:T(1,128)S(1)} collective-permute-done((s32[1,128]{1,0:T(1,128)S(1)}, s32[1,128]{1,0:T(1,128)S(1)}, u32[]{:S(2)}, u32[]{:S(2)}) %collective-permute-start.4) | collective-permute-done | bytes 544 | tf_op jit(solution)/shard_map/ppermute | solution.py:153
  10.2 0.0 collective-permute-done.3.refs_2_
  10.2 0.8 %collective-permute-start.5 = (bf16[16,2048]{1,0:T(8,128)(2,1)S(1)}, bf16[16,2048]{1,0:T(8,128)(2,1)S(1)}, u32[]{:S(2)}, u32[]{:S(2)}) collective-permute-start(bf16[16,2048]{1,0:T(8,128)(2,1)S(1)} %collective-permute-done.3.refs_2_), channel_id=1, source_target_pairs={{0,2},{2,0},{1,3},{3,1},{4,6},{6,4},{5,7},{7,5},{8,10},{10,8},{9,1... | collective-permute-start | bytes 196616 | tf_op jit(solution)/shard_map/ppermute | solution.py:153
  11.0 2.3 %collective-permute-done.refs_4_ = bf16[16,2048]{1,0:T(8,128)(2,1)S(1)} collective-permute-done((bf16[16,2048]{1,0:T(8,128)(2,1)S(1)}, bf16[16,2048]{1,0:T(8,128)(2,1)S(1)}, u32[]{:S(2)}, u32[]{:S(2)}) %collective-permute-start) | collective-permute-done | bytes 65568 | tf_op jit(solution)/shard_map/ppermute | solution.py:153
  13.3 0.5 %collective-permute-start.6 = (bf16[16,2048]{1,0:T(8,128)(2,1)S(1)}, bf16[16,2048]{1,0:T(8,128)(2,1)S(1)}, u32[]{:S(2)}, u32[]{:S(2)}) collective-permute-start(bf16[16,2048]{1,0:T(8,128)(2,1)S(1)} %collective-permute-done.refs_4_), channel_id=1, source_target_pairs={{0,2},{2,0},{1,3},{3,1},{4,6},{6,4},{5,7},{7,5},{8,10},{10,8},{9,1... | collective-permute-start | bytes 196616 | tf_op jit(solution)/shard_map/ppermute | solution.py:153
  13.8 0.0 copy-start.1
  13.8 1.2 %copy-done.1 = bf16[4,256,512]{2,1,0:T(8,128)(2,1)S(1)} copy-done((bf16[4,256,512]{2,1,0:T(8,128)(2,1)S(1)}, bf16[4,256,512]{2,1,0:T(8,128)(2,1)}, u32[]{:S(2)}) %copy-start.1) | copy-done | bytes 1048600
  15.0 0.0 copy-start.2
  15.0 0.8 %shard_map.65 = (bf16[4,256,256]{2,1,0:T(8,128)(2,1)S(1)}, bf16[4,256,256]{2,1,0:T(8,128)(2,1)S(1)}) custom-call(s32[1]{0:T(128)} %bitcast.half_ref.core_ref, bf16[4,256,512]{2,1,0:T(8,128)(2,1)S(1)} %copy-done.1), custom_call_target="tpu_custom_call" | custom-call | flops 536870912 | bytes 3145728 | tf_op jit(solution)/shard_map/pallas_call | solution.py:199
  15.8 0.0 collective-permute-done.5.refs_3_
  15.8 1.7 %collective-permute-done.6.refs_5_ = bf16[16,2048]{1,0:T(8,128)(2,1)S(1)} collective-permute-done((bf16[16,2048]{1,0:T(8,128)(2,1)S(1)}, bf16[16,2048]{1,0:T(8,128)(2,1)S(1)}, u32[]{:S(2)}, u32[]{:S(2)}) %collective-permute-start.6) | collective-permute-done | bytes 65568 | tf_op jit(solution)/shard_map/ppermute | solution.py:153
  17.5 0.0 collective-permute-done.2.refs_1_
  17.5 0.0 copy-done.2
  17.5 0.0 copy-start.4
  17.5 1.1 %shard_map.66.refs_0_ = f32[4,256]{1,0:T(4,128)S(1)} custom-call(s32[1]{0:T(128)} %bitcast.1.place_ref, s32[1]{0:T(128)} %bitcast.half_ref.core_ref, bf16[32,2048]{1,0:T(8,128)(2,1)S(1)} %pad_maximum_fusion.refs_0_, bf16[32,2048]{1,0:T(8,128)(2,1)S(1)} %collective-permute-done.2.refs_1_, bf16[16,2048]{1,0:T(8,128)(2,1)S(1)} %collective-permute-done.3.refs_2_, ...), custom_call_target="tpu_custom_call" | custom-call | flops 268435456 | bytes 2097152 | tf_op jit(solution)/shard_map/pallas_call | solution.py:214
  18.6 0.1 collective-permute-start.7
  18.7 1.2 %collective-permute-done.7.refs_1_ = f32[4,256]{1,0:T(4,128)S(1)} collective-permute-done((f32[4,256]{1,0:T(4,128)S(1)}, f32[4,256]{1,0:T(4,128)S(1)}, u32[]{:S(2)}, u32[]{:S(2)}) %collective-permute-start.7) | collective-permute-done | bytes 4128 | tf_op jit(solution)/shard_map/ppermute | solution.py:153
  19.8 0.0 copy-done.4
  19.8 1.4 %shard_map.67 = (bf16[32,2048]{1,0:T(8,128)(2,1)S(1)}, bf16[32,2048]{1,0:T(8,128)(2,1)S(1)}, bf16[32,2048]{1,0:T(8,128)(2,1)S(1)}, bf16[32,2048]{1,0:T(8,128)(2,1)S(1)}) custom-call(s32[1]{0:T(128)} %bitcast.1.place_ref, s32[1]{0:T(128)} %bitcast.half_ref.core_ref, f32[4,256]{1,0:T(4,128)S(1)} %shard_map.66.refs_0_, ...), custom_call_target="tpu_custom_call" | custom-call | flops 268435456 | bytes 2097152 | tf_op jit(solution)/shard_map/pallas_call | solution.py:227
  21.3 0.6 %collective-permute-start.8 = (bf16[32,2048]{1,0:T(8,128)(2,1)S(1)}, bf16[32,2048]{1,0:T(8,128)(2,1)S(1)}, u32[]{:S(2)}, u32[]{:S(2)}) collective-permute-start(bf16[32,2048]{1,0:T(8,128)(2,1)S(1)} %get-tuple-element.26), channel_id=1, source_target_pairs={{0,2},{2,0},{1,3},{3,1},{4,6},{6,4},{5,7},{7,5},{8,10},{10,8},{9,1... | collective-permute-start | bytes 393224 | tf_op jit(solution)/shard_map/ppermute | solution.py:153
  21.9 0.3 collective-permute-start.9
  22.2 4.7 %collective-permute-done.8 = bf16[32,2048]{1,0:T(8,128)(2,1)S(1)} collective-permute-done((bf16[32,2048]{1,0:T(8,128)(2,1)S(1)}, bf16[32,2048]{1,0:T(8,128)(2,1)S(1)}, u32[]{:S(2)}, u32[]{:S(2)}) %collective-permute-start.8) | collective-permute-done | bytes 131104 | tf_op jit(solution)/shard_map/ppermute | solution.py:153
  27.0 2.0 %collective-permute-start.11 = (bf16[16,2048]{1,0:T(8,128)(2,1)S(1)}, bf16[16,2048]{1,0:T(8,128)(2,1)S(1)}, u32[]{:S(2)}, u32[]{:S(2)}) collective-permute-start(bf16[16,2048]{1,0:T(8,128)(2,1)S(1)} %get-tuple-element.31), channel_id=1, source_target_pairs={{0,8},{4,12},{8,0},{12,4},{1,9},{5,13},{9,1},{13,5},{2,10},{6,14},... | collective-permute-start | bytes 196616 | tf_op jit(solution)/shard_map/ppermute | solution.py:153
  28.9 0.7 %collective-permute-start.12 = (bf16[16,2048]{1,0:T(8,128)(2,1)S(1)}, bf16[16,2048]{1,0:T(8,128)(2,1)S(1)}, u32[]{:S(2)}, u32[]{:S(2)}) collective-permute-start(bf16[16,2048]{1,0:T(8,128)(2,1)S(1)} %get-tuple-element.32), channel_id=1, source_target_pairs={{0,12},{4,8},{8,4},{12,0},{1,13},{5,9},{9,5},{13,1},{2,14},{6,10},... | collective-permute-start | bytes 196616 | tf_op jit(solution)/shard_map/ppermute | solution.py:153
  29.6 0.0 collective-permute-done.9
  29.7 0.0 copy-start.3
  29.7 1.4 %collective-permute-start.10 = (bf16[16,2048]{1,0:T(8,128)(2,1)S(1)}, bf16[16,2048]{1,0:T(8,128)(2,1)S(1)}, u32[]{:S(2)}, u32[]{:S(2)}) collective-permute-start(bf16[16,2048]{1,0:T(8,128)(2,1)S(1)} %slice.25), channel_id=1, source_target_pairs={{0,2},{2,0},{1,3},{3,1},{4,6},{6,4},{5,7},{7,5},{8,10},{10,8},{9,1... | collective-permute-start | bytes 196616 | tf_op jit(solution)/shard_map/ppermute | solution.py:153
  31.1 2.9 %collective-permute-done.11 = bf16[16,2048]{1,0:T(8,128)(2,1)S(1)} collective-permute-done((bf16[16,2048]{1,0:T(8,128)(2,1)S(1)}, bf16[16,2048]{1,0:T(8,128)(2,1)S(1)}, u32[]{:S(2)}, u32[]{:S(2)}) %collective-permute-start.11) | collective-permute-done | bytes 65568 | tf_op jit(solution)/shard_map/ppermute | solution.py:153
  33.9 1.2 %collective-permute-done.12 = bf16[16,2048]{1,0:T(8,128)(2,1)S(1)} collective-permute-done((bf16[16,2048]{1,0:T(8,128)(2,1)S(1)}, bf16[16,2048]{1,0:T(8,128)(2,1)S(1)}, u32[]{:S(2)}, u32[]{:S(2)}) %collective-permute-start.12) | collective-permute-done | bytes 65568 | tf_op jit(solution)/shard_map/ppermute | solution.py:153
  35.1 0.0 collective-permute-done.10
  35.1 0.1 collective-permute-start.13
  35.2 1.3 %collective-permute-done.13.other_ref = f32[16,2048]{1,0:T(8,128)S(1)} collective-permute-done((f32[16,2048]{1,0:T(8,128)S(1)}, f32[16,2048]{1,0:T(8,128)S(1)}, u32[]{:S(2)}, u32[]{:S(2)}) %collective-permute-start.13) | collective-permute-done | bytes 131104 | tf_op jit(solution)/shard_map/ppermute | solution.py:153
  36.5 0.0 copy-done.3
  36.5 0.7 %shard_map.68 = f32[16,4096]{1,0:T(8,128)} custom-call(s32[1]{0:T(128)} %bitcast.half_ref.core_ref, f32[16,2048]{1,0:T(8,128)S(1)} %fusion.1.mine_ref, f32[16,2048]{1,0:T(8,128)S(1)} %collective-permute-done.13.other_ref, bf16[16,4096]{1,0:T(8,128)(2,1)S(1)} %copy-done.3), custom_call_target="tpu_custom_call" | custom-call | bytes 786432 | tf_op jit(solution)/shard_map/pallas_call | solution.py:253
  (7 shorter events, 0.1 us)
Async XLA Ops:
  0.0 0.9 %copy-start = (bf16[16,4096]{1,0:T(8,128)(2,1)S(1)}, bf16[16,4096]{1,0:T(8,128)(2,1)}, u32[]{:S(2)}) copy-start(bf16[16,4096]{1,0:T(8,128)(2,1)} %param.10) | copy-start | bytes 393220
  0.9 6.9 %copy-start.6 = (s32[4,8,4]{1,2,0:T(4,128)S(1)}, s32[4,8,4]{1,2,0:T(4,128)}, u32[]{:S(2)}) copy-start(s32[4,8,4]{1,2,0:T(4,128)} %param.8) | copy-start | bytes 1540
  0.9 7.8 %collective-permute-start.1 = (bf16[16,2048]{1,0:T(8,128)(2,1)S(1)}, bf16[16,2048]{1,0:T(8,128)(2,1)S(1)}, u32[]{:S(2)}, u32[]{:S(2)}) collective-permute-start(bf16[16,2048]{1,0:T(8,128)(2,1)S(1)} %constant_dynamic-slice_fusion), channel_id=1, source_target_pairs={{0,2},{2,0},{1,3},{3,1},{4,6},{6,4},{5,7},{7,5},{8,10},{10,8},{9,1... | collective-permute-start | bytes 196616 | tf_op jit(solution)/shard_map/ppermute | solution.py:153
  3.9 6.3 %collective-permute-start.3 = (bf16[16,2048]{1,0:T(8,128)(2,1)S(1)}, bf16[16,2048]{1,0:T(8,128)(2,1)S(1)}, u32[]{:S(2)}, u32[]{:S(2)}) collective-permute-start(bf16[16,2048]{1,0:T(8,128)(2,1)S(1)} %constant_dynamic-slice_fusion), channel_id=1, source_target_pairs={{0,8},{4,12},{8,0},{12,4},{1,9},{5,13},{9,1},{13,5},{2,10},{6,14},... | collective-permute-start | bytes 196616 | tf_op jit(solution)/shard_map/ppermute | solution.py:153
  6.5 6.8 %collective-permute-start = (bf16[16,2048]{1,0:T(8,128)(2,1)S(1)}, bf16[16,2048]{1,0:T(8,128)(2,1)S(1)}, u32[]{:S(2)}, u32[]{:S(2)}) collective-permute-start(bf16[16,2048]{1,0:T(8,128)(2,1)S(1)} %constant_dynamic-slice_fusion), channel_id=1, source_target_pairs={{0,12},{4,8},{8,4},{12,0},{1,13},{5,9},{9,5},{13,1},{2,14},{6,10},... | collective-permute-start | bytes 196616 | tf_op jit(solution)/shard_map/ppermute | solution.py:153
  7.9 0.7 %copy-start.5 = (s32[1,1,8,8]{3,2,1,0:T(8,128)S(1)}, s32[1,1,8,8]{3,2,1,0:T(8,128)}, u32[]{:S(2)}) copy-start(s32[1,1,8,8]{3,2,1,0:T(8,128)} %param.9) | copy-start | bytes 772
  8.8 8.8 %collective-permute-start.2 = (bf16[32,2048]{1,0:T(8,128)(2,1)S(1)}, bf16[32,2048]{1,0:T(8,128)(2,1)S(1)}, u32[]{:S(2)}, u32[]{:S(2)}) collective-permute-start(bf16[32,2048]{1,0:T(8,128)(2,1)S(1)} %pad_maximum_fusion.refs_0_), channel_id=1, source_target_pairs={{0,4},{4,0},{8,12},{12,8},{1,5},{5,1},{9,13},{13,9},{2,6},{6,2},{1... | collective-permute-start | bytes 393224 | tf_op jit(solution)/shard_map/ppermute | solution.py:153
  9.1 1.1 %collective-permute-start.4 = (s32[1,128]{1,0:T(1,128)S(1)}, s32[1,128]{1,0:T(1,128)S(1)}, u32[]{:S(2)}, u32[]{:S(2)}) collective-permute-start(s32[1,128]{1,0:T(1,128)S(1)} %shard_map.64.refs_6_.refs_5_), channel_id=1, source_target_pairs={{0,1},{1,0},{2,3},{3,2},{4,5},{5,4},{6,7},{7,6},{8,9},{9,8},{10,11... | collective-permute-start | bytes 1544 | tf_op jit(solution)/shard_map/ppermute | solution.py:153
  10.2 5.6 %collective-permute-start.5 = (bf16[16,2048]{1,0:T(8,128)(2,1)S(1)}, bf16[16,2048]{1,0:T(8,128)(2,1)S(1)}, u32[]{:S(2)}, u32[]{:S(2)}) collective-permute-start(bf16[16,2048]{1,0:T(8,128)(2,1)S(1)} %collective-permute-done.3.refs_2_), channel_id=1, source_target_pairs={{0,2},{2,0},{1,3},{3,1},{4,6},{6,4},{5,7},{7,5},{8,10},{10,8},{9,1... | collective-permute-start | bytes 196616 | tf_op jit(solution)/shard_map/ppermute | solution.py:153
  13.3 4.3 %collective-permute-start.6 = (bf16[16,2048]{1,0:T(8,128)(2,1)S(1)}, bf16[16,2048]{1,0:T(8,128)(2,1)S(1)}, u32[]{:S(2)}, u32[]{:S(2)}) collective-permute-start(bf16[16,2048]{1,0:T(8,128)(2,1)S(1)} %collective-permute-done.refs_4_), channel_id=1, source_target_pairs={{0,2},{2,0},{1,3},{3,1},{4,6},{6,4},{5,7},{7,5},{8,10},{10,8},{9,1... | collective-permute-start | bytes 196616 | tf_op jit(solution)/shard_map/ppermute | solution.py:153
  13.8 1.2 %copy-start.1 = (bf16[4,256,512]{2,1,0:T(8,128)(2,1)S(1)}, bf16[4,256,512]{2,1,0:T(8,128)(2,1)}, u32[]{:S(2)}) copy-start(bf16[4,256,512]{2,1,0:T(8,128)(2,1)} %refs_3_.1) | copy-start | bytes 3145732
  15.0 2.5 %copy-start.2 = (bf16[4,256,512]{2,1,0:T(8,128)(2,1)S(1)}, bf16[4,256,512]{2,1,0:T(8,128)(2,1)}, u32[]{:S(2)}) copy-start(bf16[4,256,512]{2,1,0:T(8,128)(2,1)} %refs_3_.1) | copy-start | bytes 3145732
  17.5 2.3 %copy-start.4 = (f32[4,256]{1,0:T(4,128)S(1)}, f32[4,256]{1,0:T(4,128)}, u32[]{:S(2)}) copy-start(f32[4,256]{1,0:T(4,128)} %refs_2_.1) | copy-start | bytes 12292
  18.6 1.2 %collective-permute-start.7 = (f32[4,256]{1,0:T(4,128)S(1)}, f32[4,256]{1,0:T(4,128)S(1)}, u32[]{:S(2)}, u32[]{:S(2)}) collective-permute-start(f32[4,256]{1,0:T(4,128)S(1)} %shard_map.66.refs_0_), channel_id=1, source_target_pairs={{0,1},{1,0},{2,3},{3,2},{4,5},{5,4},{6,7},{7,6},{8,9},{9,8},{10,11... | collective-permute-start | bytes 12296 | tf_op jit(solution)/shard_map/ppermute | solution.py:153
  21.3 5.6 %collective-permute-start.8 = (bf16[32,2048]{1,0:T(8,128)(2,1)S(1)}, bf16[32,2048]{1,0:T(8,128)(2,1)S(1)}, u32[]{:S(2)}, u32[]{:S(2)}) collective-permute-start(bf16[32,2048]{1,0:T(8,128)(2,1)S(1)} %get-tuple-element.26), channel_id=1, source_target_pairs={{0,2},{2,0},{1,3},{3,1},{4,6},{6,4},{5,7},{7,5},{8,10},{10,8},{9,1... | collective-permute-start | bytes 393224 | tf_op jit(solution)/shard_map/ppermute | solution.py:153
  21.9 7.8 %collective-permute-start.9 = (bf16[32,2048]{1,0:T(8,128)(2,1)S(1)}, bf16[32,2048]{1,0:T(8,128)(2,1)S(1)}, u32[]{:S(2)}, u32[]{:S(2)}) collective-permute-start(bf16[32,2048]{1,0:T(8,128)(2,1)S(1)} %get-tuple-element.29), channel_id=1, source_target_pairs={{0,4},{4,0},{8,12},{12,8},{1,5},{5,1},{9,13},{13,9},{2,6},{6,2},{1... | collective-permute-start | bytes 393224 | tf_op jit(solution)/shard_map/ppermute | solution.py:153
  27.0 7.0 %collective-permute-start.11 = (bf16[16,2048]{1,0:T(8,128)(2,1)S(1)}, bf16[16,2048]{1,0:T(8,128)(2,1)S(1)}, u32[]{:S(2)}, u32[]{:S(2)}) collective-permute-start(bf16[16,2048]{1,0:T(8,128)(2,1)S(1)} %get-tuple-element.31), channel_id=1, source_target_pairs={{0,8},{4,12},{8,0},{12,4},{1,9},{5,13},{9,1},{13,5},{2,10},{6,14},... | collective-permute-start | bytes 196616 | tf_op jit(solution)/shard_map/ppermute | solution.py:153
  28.9 6.2 %collective-permute-start.12 = (bf16[16,2048]{1,0:T(8,128)(2,1)S(1)}, bf16[16,2048]{1,0:T(8,128)(2,1)S(1)}, u32[]{:S(2)}, u32[]{:S(2)}) collective-permute-start(bf16[16,2048]{1,0:T(8,128)(2,1)S(1)} %get-tuple-element.32), channel_id=1, source_target_pairs={{0,12},{4,8},{8,4},{12,0},{1,13},{5,9},{9,5},{13,1},{2,14},{6,10},... | collective-permute-start | bytes 196616 | tf_op jit(solution)/shard_map/ppermute | solution.py:153
  29.7 6.9 %copy-start.3 = (bf16[16,4096]{1,0:T(8,128)(2,1)S(1)}, bf16[16,4096]{1,0:T(8,128)(2,1)}, u32[]{:S(2)}) copy-start(bf16[16,4096]{1,0:T(8,128)(2,1)} %core_ref.1) | copy-start | bytes 393220
  29.7 5.4 %collective-permute-start.10 = (bf16[16,2048]{1,0:T(8,128)(2,1)S(1)}, bf16[16,2048]{1,0:T(8,128)(2,1)S(1)}, u32[]{:S(2)}, u32[]{:S(2)}) collective-permute-start(bf16[16,2048]{1,0:T(8,128)(2,1)S(1)} %slice.25), channel_id=1, source_target_pairs={{0,2},{2,0},{1,3},{3,1},{4,6},{6,4},{5,7},{7,5},{8,10},{10,8},{9,1... | collective-permute-start | bytes 196616 | tf_op jit(solution)/shard_map/ppermute | solution.py:153
  35.1 1.4 %collective-permute-start.13 = (f32[16,2048]{1,0:T(8,128)S(1)}, f32[16,2048]{1,0:T(8,128)S(1)}, u32[]{:S(2)}, u32[]{:S(2)}) collective-permute-start(f32[16,2048]{1,0:T(8,128)S(1)} %fusion.1.mine_ref), channel_id=1, source_target_pairs={{0,1},{1,0},{2,3},{3,2},{4,5},{5,4},{6,7},{7,6},{8,9},{9,8},{10,11... | collective-permute-start | bytes 393224 | tf_op jit(solution)/shard_map/ppermute | solution.py:153

commit v17 on v13

--- a/solution.py
+++ b/solution.py
@@ -86,13 +86,13 @@
         out_ref[t:t + 1, :] = jnp.sum(folded.T, axis=0, keepdims=True)
 
 
-def scatter_kernel(places, place_ref, core_ref, *refs):
+def scatter_kernel(places, owners, place_ref, core_ref, *refs):
     mine_ref, far_ref, weight_ref, values_ref, left_t_ref, own_ref, other_ref = refs[:7]
     out_refs = refs[7:-2]
     high, rest = refs[-2:]
     target = {k: (ref, i) for ref, blocks in zip(out_refs, places) for i, k in enumerate(blocks)}
-    pieces = len(target)
     held = out_refs[0].shape[0] // len(places[0])
+    pieces = owners
     put = row_table(place_ref, core_ref, own_ref, other_ref, held, pieces).astype(jnp.bfloat16)
     batches, points, columns = values_ref.shape
     groups = columns // GO
@@ -122,8 +122,18 @@
         some = put[k * held:(k + step) * held, :]
         total = split_dot(some, high[...]) + split_dot(some, rest[...])
         for i in range(step):
-            ref, at = target[k + i]
-            ref[at * held:(at + 1) * held, :] = total[i * held:(i + 1) * held, :].astype(jnp.bfloat16)
+            if k + i in target:
+                ref, at = target[k + i]
+                ref[at * held:(at + 1) * held, :] = total[i * held:(i + 1) * held, :].astype(jnp.bfloat16)
+
+
+def late_kernel(first, place_ref, core_ref, high_ref, rest_ref, own_ref, other_ref, *out_refs):
+    held = out_refs[0].shape[0]
+    owners = first + len(out_refs)
+    put = row_table(place_ref, core_ref, own_ref, other_ref, held, owners)[first * held:].astype(jnp.bfloat16)
+    total = split_dot(put, high_ref[...]) + split_dot(put, rest_ref[...])
+    for i, ref in enumerate(out_refs):
+        ref[...] = total[i * held:(i + 1) * held, :].astype(jnp.bfloat16)
 
 
 def finish_kernel(half_ref, mine_ref, other_ref, core_ref, out_ref):
@@ -182,11 +192,11 @@
     direct = {dz: swap(mine, "batch", rows_z, dz) for dz in far}
     beside = [swap(mine, "pair", rows_x, dx) for dx in side]
     *beside, own_rows = lax.optimization_barrier((*beside, own_rows))
-    arrays, places = [mine, *beside], [[dx] for dx in range(rows_x)]
+    cluster = jnp.concatenate([mine, *beside], axis=0)
+    arrays, places = [cluster], [list(range(rows_x))]
     for dz in near:
-        for dx, piece in enumerate([mine, *beside]):
-            arrays.append(swap(piece, "batch", rows_z, dz))
-            places.append([dz * rows_x + dx])
+        arrays.append(swap(cluster, "batch", rows_z, dz))
+        places.append(list(range(dz * rows_x, (dz + 1) * rows_x)))
     direct[far[0]], other_rows = lax.optimization_barrier((direct[far[0]], other_rows))
     for dz in far:
         arrays.append(direct[dz])
@@ -223,16 +233,24 @@
     partial_other = swap(partial, "orb", 2, 1)
 
     out_places = [list(range(dz * rows_x, (dz + 1) * rows_x)) for dz in [0] + near]
-    out_places += [[dz * rows_x + dx] for dz in far for dx in [0] + side]
-    sums = call(
-        functools.partial(scatter_kernel, out_places),
-        [jax.ShapeDtypeStruct((held * len(blocks), wide), bf16) for blocks in out_places],
+    out_places += [[dz * rows_x + dx] for dz in far[:-1] for dx in [0] + side]
+    outs = [jax.ShapeDtypeStruct((held * len(blocks), wide), bf16) for blocks in out_places]
+    *sums, high, rest = call(
+        functools.partial(scatter_kernel, out_places, owners),
+        outs + [jax.ShapeDtypeStruct((entries, wide), bf16)] * 2,
         7,
         scalars=2,
-        scratch=(pltpu.VMEM((entries, wide), bf16), pltpu.VMEM((entries, wide), bf16)),
         flops=2 * batches * points * columns * kept,
         moved=2 * batches * points * columns * 2,
     )(place, core_at, partial, partial_other, point_weights, basis_values, left_t, own_rows, other_rows)
+    sums += call(
+        functools.partial(late_kernel, owners - rows_x),
+        [jax.ShapeDtypeStruct((held, wide), bf16)] * rows_x,
+        4,
+        scalars=2,
+        flops=4 * rows_x * held * entries * wide,
+        moved=2 * entries * wide * 2,
+    )(place, core_at, high, rest, own_rows, other_rows)
 
     clusters, singles = sums[:len(near) + 1], sums[len(near) + 1:]
     landed = []

time: 37.5 us -> 36.8 us (0.981)
  starting transfers between devices: 17 us -> 15.6 us
  Pallas kernels: 4.15 us -> 4.59 us
    ppermute x16 -> x15, starting transfers between devices: 17 us -> 15.6 us  [swap(): return lax.ppermute(array, axis, [(i, i ^ step) for i in range(count)])]
    pallas_call x1 -> x2, Pallas kernels: 1.4 us -> 1.84 us  [the longest x1 1.39 us: per_device(): call(functools.partial(scatter_kernel, out_places, owners), outs + [jax.S...]
    ppermute x16 -> x15, waiting for transfers between devices: 13.1 us -> 13.3 us  [swap(): return lax.ppermute(array, axis, [(i, i ^ step) for i in range(count)])]
  transfers between devices with their start and end apart: 16 -> 15, of which waited for: 9 -> 8; matrix products, arithmetic and copies ran while one was open for 0% -> 0% of each run, Pallas kernels for 3% -> 4%
where the time goes in v17:
time: 36.8 us; the launch traced here: 36.6 us
  starting transfers between devices  15.6 us (42%)
  waiting for transfers between devices  13.3 us (36%)
  Pallas kernels  4.59 us (12%)
  local copies, waits for them, and re-layouts  2.84 us (8%)
    ppermute x15, starting transfers between devices, swap(): return lax.ppermute(array, axis, [(i, i ^ step) for i in range(count)])  15.6 us
    ppermute x15, waiting for transfers between devices, swap(): return lax.ppermute(array, axis, [(i, i ^ step) for i in range(count)])  13.3 us
    unnamed x14, local copies, waits for them, and re-layouts  2.74 us
    pallas_call x1, Pallas kernels, per_device(): call(functools.partial(scatter_kernel, out_places, owners), outs + [jax.S...  1.39 us
    pallas_call x1, Pallas kernels, per_device(): call(functools.partial(density_kernel, places), jax.ShapeDtypeStruct((bat...  1.07 us
    pallas_call x1, Pallas kernels, per_device(): call(prepare_kernel, (jax.ShapeDtypeStruct((batches, points, kept), bf16)...  0.76 us
  transfers between devices with their start and end apart: 15, of which 8 were waited for; matrix products, arithmetic and copies ran while one was open for 0% of the time, Pallas kernels for 4%

profile of v17, /device:TPU:0, one launch (start us, length us, event | category | flops | bytes accessed | tf_op | source)
XLA Modules:
  0.0 36.6 jit_solution(12899058024350747224)
XLA Ops:
  0.0 0.0 copy-start
  0.0 0.9 %copy-done = bf16[16,4096]{1,0:T(8,128)(2,1)S(1)} copy-done((bf16[16,4096]{1,0:T(8,128)(2,1)S(1)}, bf16[16,4096]{1,0:T(8,128)(2,1)}, u32[]{:S(2)}) %copy-start) | copy-done | bytes 131096
  0.9 0.0 copy-start.6
  0.9 3.0 %collective-permute-start.1 = (bf16[16,2048]{1,0:T(8,128)(2,1)S(1)}, bf16[16,2048]{1,0:T(8,128)(2,1)S(1)}, u32[]{:S(2)}, u32[]{:S(2)}) collective-permute-start(bf16[16,2048]{1,0:T(8,128)(2,1)S(1)} %constant_dynamic-slice_fusion), channel_id=1, source_target_pairs={{0,2},{2,0},{1,3},{3,1},{4,6},{6,4},{5,7},{7,5},{8,10},{10,8},{9,1... | collective-permute-start | bytes 196616 | tf_op jit(solution)/shard_map/ppermute | solution.py:163
  3.9 2.6 %collective-permute-start.3 = (bf16[16,2048]{1,0:T(8,128)(2,1)S(1)}, bf16[16,2048]{1,0:T(8,128)(2,1)S(1)}, u32[]{:S(2)}, u32[]{:S(2)}) collective-permute-start(bf16[16,2048]{1,0:T(8,128)(2,1)S(1)} %constant_dynamic-slice_fusion), channel_id=1, source_target_pairs={{0,8},{4,12},{8,0},{12,4},{1,9},{5,13},{9,1},{13,5},{2,10},{6,14},... | collective-permute-start | bytes 196616 | tf_op jit(solution)/shard_map/ppermute | solution.py:163
  6.5 1.3 %collective-permute-start = (bf16[16,2048]{1,0:T(8,128)(2,1)S(1)}, bf16[16,2048]{1,0:T(8,128)(2,1)S(1)}, u32[]{:S(2)}, u32[]{:S(2)}) collective-permute-start(bf16[16,2048]{1,0:T(8,128)(2,1)S(1)} %constant_dynamic-slice_fusion), channel_id=1, source_target_pairs={{0,12},{4,8},{8,4},{12,0},{1,13},{5,9},{9,5},{13,1},{2,14},{6,10},... | collective-permute-start | bytes 196616 | tf_op jit(solution)/shard_map/ppermute | solution.py:163
  7.9 0.0 copy-done.6
  7.9 0.0 copy-start.5
  7.9 0.1 reshape.16.slots_ref
  7.9 0.6 %copy-done.5 = s32[1,1,8,8]{3,2,1,0:T(8,128)S(1)} copy-done((s32[1,1,8,8]{3,2,1,0:T(8,128)S(1)}, s32[1,1,8,8]{3,2,1,0:T(8,128)}, u32[]{:S(2)}) %copy-start.5) | copy-done | bytes 280
  8.5 0.2 shard_map.64.refs_6_.refs_5_.own_ref
  8.7 0.0 collective-permute-done.1
  8.8 0.3 collective-permute-start.2
  9.1 0.0 collective-permute-start.4
  9.1 1.1 %collective-permute-done.4.refs_7_.refs_6_.other_ref = s32[1,128]{1,0:T(1,128)S(1)} collective-permute-done((s32[1,128]{1,0:T(1,128)S(1)}, s32[1,128]{1,0:T(1,128)S(1)}, u32[]{:S(2)}, u32[]{:S(2)}) %collective-permute-start.4) | collective-permute-done | bytes 544 | tf_op jit(solution)/shard_map/ppermute | solution.py:163
  10.2 0.0 collective-permute-done.3.refs_2_
  10.2 0.8 %collective-permute-start.5 = (bf16[16,2048]{1,0:T(8,128)(2,1)S(1)}, bf16[16,2048]{1,0:T(8,128)(2,1)S(1)}, u32[]{:S(2)}, u32[]{:S(2)}) collective-permute-start(bf16[16,2048]{1,0:T(8,128)(2,1)S(1)} %collective-permute-done.3.refs_2_), channel_id=1, source_target_pairs={{0,2},{2,0},{1,3},{3,1},{4,6},{6,4},{5,7},{7,5},{8,10},{10,8},{9,1... | collective-permute-start | bytes 196616 | tf_op jit(solution)/shard_map/ppermute | solution.py:163
  11.0 2.3 %collective-permute-done.refs_4_ = bf16[16,2048]{1,0:T(8,128)(2,1)S(1)} collective-permute-done((bf16[16,2048]{1,0:T(8,128)(2,1)S(1)}, bf16[16,2048]{1,0:T(8,128)(2,1)S(1)}, u32[]{:S(2)}, u32[]{:S(2)}) %collective-permute-start) | collective-permute-done | bytes 65568 | tf_op jit(solution)/shard_map/ppermute | solution.py:163
  13.3 0.5 %collective-permute-start.6 = (bf16[16,2048]{1,0:T(8,128)(2,1)S(1)}, bf16[16,2048]{1,0:T(8,128)(2,1)S(1)}, u32[]{:S(2)}, u32[]{:S(2)}) collective-permute-start(bf16[16,2048]{1,0:T(8,128)(2,1)S(1)} %collective-permute-done.refs_4_), channel_id=1, source_target_pairs={{0,2},{2,0},{1,3},{3,1},{4,6},{6,4},{5,7},{7,5},{8,10},{10,8},{9,1... | collective-permute-start | bytes 196616 | tf_op jit(solution)/shard_map/ppermute | solution.py:163
  13.8 1.2 %copy-done.1 = bf16[4,256,512]{2,1,0:T(8,128)(2,1)S(1)} copy-done((bf16[4,256,512]{2,1,0:T(8,128)(2,1)S(1)}, bf16[4,256,512]{2,1,0:T(8,128)(2,1)}, u32[]{:S(2)}) %copy-start.1) | copy-done | bytes 1048600
  15.0 0.8 %shard_map.65 = (bf16[4,256,256]{2,1,0:T(8,128)(2,1)S(1)}, bf16[4,256,256]{2,1,0:T(8,128)(2,1)S(1)}) custom-call(s32[1]{0:T(128)} %bitcast.half_ref.core_ref, bf16[4,256,512]{2,1,0:T(8,128)(2,1)S(1)} %copy-done.1), custom_call_target="tpu_custom_call" | custom-call | flops 536870912 | bytes 3145728 | tf_op jit(solution)/shard_map/pallas_call | solution.py:209
  15.8 0.0 collective-permute-done.5.refs_3_
  15.8 1.7 %collective-permute-done.6.refs_5_ = bf16[16,2048]{1,0:T(8,128)(2,1)S(1)} collective-permute-done((bf16[16,2048]{1,0:T(8,128)(2,1)S(1)}, bf16[16,2048]{1,0:T(8,128)(2,1)S(1)}, u32[]{:S(2)}, u32[]{:S(2)}) %collective-permute-start.6) | collective-permute-done | bytes 65568 | tf_op jit(solution)/shard_map/ppermute | solution.py:163
  17.5 0.0 collective-permute-done.2.refs_1_
  17.5 0.0 copy-done.2
  17.5 1.1 %shard_map.66.refs_0_ = f32[4,256]{1,0:T(4,128)S(1)} custom-call(s32[1]{0:T(128)} %bitcast.1.place_ref, s32[1]{0:T(128)} %bitcast.half_ref.core_ref, bf16[32,2048]{1,0:T(8,128)(2,1)S(1)} %pad_maximum_fusion.refs_0_, bf16[32,2048]{1,0:T(8,128)(2,1)S(1)} %collective-permute-done.2.refs_1_, bf16[16,2048]{1,0:T(8,128)(2,1)S(1)} %collective-permute-done.3.refs_2_, ...), custom_call_target="tpu_custom_call" | custom-call | flops 268435456 | bytes 2097152 | tf_op jit(solution)/shard_map/pallas_call | solution.py:224
  18.6 0.1 collective-permute-start.7
  18.7 1.2 %collective-permute-done.7.refs_1_ = f32[4,256]{1,0:T(4,128)S(1)} collective-permute-done((f32[4,256]{1,0:T(4,128)S(1)}, f32[4,256]{1,0:T(4,128)S(1)}, u32[]{:S(2)}, u32[]{:S(2)}) %collective-permute-start.7) | collective-permute-done | bytes 4128 | tf_op jit(solution)/shard_map/ppermute | solution.py:163
  19.8 0.0 copy-done.4
  19.8 1.4 %shard_map.67 = (bf16[32,2048]{1,0:T(8,128)(2,1)S(1)}, bf16[32,2048]{1,0:T(8,128)(2,1)S(1)}, bf16[16,2048]{1,0:T(8,128)(2,1)S(1)}, bf16[16,2048]{1,0:T(8,128)(2,...) custom-call(s32[1]{0:T(128)} %bitcast.1.place_ref, s32[1]{0:T(128)} %bitcast.half_ref.core_ref, ...), custom_call_target="tpu_custom_call" | custom-call | flops 268435456 | bytes 2097152 | tf_op jit(solution)/shard_map/pallas_call | solution.py:238
  21.2 0.6 %collective-permute-start.10 = (bf16[16,2048]{1,0:T(8,128)(2,1)S(1)}, bf16[16,2048]{1,0:T(8,128)(2,1)S(1)}, u32[]{:S(2)}, u32[]{:S(2)}) collective-permute-start(bf16[16,2048]{1,0:T(8,128)(2,1)S(1)} %get-tuple-element.30), channel_id=1, source_target_pairs={{0,2},{2,0},{1,3},{3,1},{4,6},{6,4},{5,7},{7,5},{8,10},{10,8},{9,1... | collective-permute-start | bytes 196616 | tf_op jit(solution)/shard_map/ppermute | solution.py:163
  21.8 0.5 %shard_map.68 = (bf16[16,2048]{1,0:T(8,128)(2,1)S(1)}, bf16[16,2048]{1,0:T(8,128)(2,1)S(1)}) custom-call(s32[1]{0:T(128)} %bitcast.1.place_ref, s32[1]{0:T(128)} %bitcast.half_ref.core_ref, bf16[256,2048]{1,0:T(8,128)(2,1)S(1)} %get-tuple-element.31.high_ref, bf16[256,2048]{1,0:T(8,128)(2,1)S(1)} %get-tuple-element.32.rest_ref, ...), custom_call_target="tpu_custom_call" | custom-call | flops 67108864 | bytes 2097152 | tf_op jit(solution)/shard_map/pallas_call | solution.py:246
  22.3 1.5 %collective-permute-start.12 = (bf16[16,2048]{1,0:T(8,128)(2,1)S(1)}, bf16[16,2048]{1,0:T(8,128)(2,1)S(1)}, u32[]{:S(2)}, u32[]{:S(2)}) collective-permute-start(bf16[16,2048]{1,0:T(8,128)(2,1)S(1)} %get-tuple-element.34), channel_id=1, source_target_pairs={{0,2},{2,0},{1,3},{3,1},{4,6},{6,4},{5,7},{7,5},{8,10},{10,8},{9,1... | collective-permute-start | bytes 196616 | tf_op jit(solution)/shard_map/ppermute | solution.py:163
  23.8 0.1 collective-permute-start.8
  24.0 2.3 %collective-permute-done.10 = bf16[16,2048]{1,0:T(8,128)(2,1)S(1)} collective-permute-done((bf16[16,2048]{1,0:T(8,128)(2,1)S(1)}, bf16[16,2048]{1,0:T(8,128)(2,1)S(1)}, u32[]{:S(2)}, u32[]{:S(2)}) %collective-permute-start.10) | collective-permute-done | bytes 65568 | tf_op jit(solution)/shard_map/ppermute | solution.py:163
  26.3 2.0 %collective-permute-start.11 = (bf16[16,2048]{1,0:T(8,128)(2,1)S(1)}, bf16[16,2048]{1,0:T(8,128)(2,1)S(1)}, u32[]{:S(2)}, u32[]{:S(2)}) collective-permute-start(bf16[16,2048]{1,0:T(8,128)(2,1)S(1)} %add_convert_fusion.1), channel_id=1, source_target_pairs={{0,8},{4,12},{8,0},{12,4},{1,9},{5,13},{9,1},{13,5},{2,10},{6,14},... | collective-permute-start | bytes 196616 | tf_op jit(solution)/shard_map/ppermute | solution.py:163
  28.2 0.0 collective-permute-done.12
  28.2 1.8 %collective-permute-start.13 = (bf16[16,2048]{1,0:T(8,128)(2,1)S(1)}, bf16[16,2048]{1,0:T(8,128)(2,1)S(1)}, u32[]{:S(2)}, u32[]{:S(2)}) collective-permute-start(bf16[16,2048]{1,0:T(8,128)(2,1)S(1)} %add_convert_fusion), channel_id=1, source_target_pairs={{0,12},{4,8},{8,4},{12,0},{1,13},{5,9},{9,5},{13,1},{2,14},{6,10},... | collective-permute-start | bytes 196616 | tf_op jit(solution)/shard_map/ppermute | solution.py:163
  30.0 0.0 collective-permute-done.8
  30.1 0.0 copy-start.3
  30.1 1.0 %collective-permute-start.9 = (bf16[16,2048]{1,0:T(8,128)(2,1)S(1)}, bf16[16,2048]{1,0:T(8,128)(2,1)S(1)}, u32[]{:S(2)}, u32[]{:S(2)}) collective-permute-start(bf16[16,2048]{1,0:T(8,128)(2,1)S(1)} %slice.17), channel_id=1, source_target_pairs={{0,2},{2,0},{1,3},{3,1},{4,6},{6,4},{5,7},{7,5},{8,10},{10,8},{9,1... | collective-permute-start | bytes 196616 | tf_op jit(solution)/shard_map/ppermute | solution.py:163
  31.0 1.8 %collective-permute-done.11 = bf16[16,2048]{1,0:T(8,128)(2,1)S(1)} collective-permute-done((bf16[16,2048]{1,0:T(8,128)(2,1)S(1)}, bf16[16,2048]{1,0:T(8,128)(2,1)S(1)}, u32[]{:S(2)}, u32[]{:S(2)}) %collective-permute-start.11) | collective-permute-done | bytes 65568 | tf_op jit(solution)/shard_map/ppermute | solution.py:163
  32.9 1.5 %collective-permute-done.13 = bf16[16,2048]{1,0:T(8,128)(2,1)S(1)} collective-permute-done((bf16[16,2048]{1,0:T(8,128)(2,1)S(1)}, bf16[16,2048]{1,0:T(8,128)(2,1)S(1)}, u32[]{:S(2)}, u32[]{:S(2)}) %collective-permute-start.13) | collective-permute-done | bytes 65568 | tf_op jit(solution)/shard_map/ppermute | solution.py:163
  34.4 0.0 collective-permute-done.9
  34.4 0.1 collective-permute-start.14
  34.5 1.3 %collective-permute-done.14.other_ref = f32[16,2048]{1,0:T(8,128)S(1)} collective-permute-done((f32[16,2048]{1,0:T(8,128)S(1)}, f32[16,2048]{1,0:T(8,128)S(1)}, u32[]{:S(2)}, u32[]{:S(2)}) %collective-permute-start.14) | collective-permute-done | bytes 131104 | tf_op jit(solution)/shard_map/ppermute | solution.py:163
  35.9 0.0 copy-done.3
  35.9 0.7 %shard_map.69 = f32[16,4096]{1,0:T(8,128)} custom-call(s32[1]{0:T(128)} %bitcast.half_ref.core_ref, f32[16,2048]{1,0:T(8,128)S(1)} %fusion.1.mine_ref, f32[16,2048]{1,0:T(8,128)S(1)} %collective-permute-done.14.other_ref, bf16[16,4096]{1,0:T(8,128)(2,1)S(1)} %copy-done.3), custom_call_target="tpu_custom_call" | custom-call | bytes 786432 | tf_op jit(solution)/shard_map/pallas_call | solution.py:271
  (10 shorter events, 0.1 us)
Async XLA Ops:
  0.0 0.9 %copy-start = (bf16[16,4096]{1,0:T(8,128)(2,1)S(1)}, bf16[16,4096]{1,0:T(8,128)(2,1)}, u32[]{:S(2)}) copy-start(bf16[16,4096]{1,0:T(8,128)(2,1)} %param.10) | copy-start | bytes 393220
  0.9 6.9 %copy-start.6 = (s32[4,8,4]{1,2,0:T(4,128)S(1)}, s32[4,8,4]{1,2,0:T(4,128)}, u32[]{:S(2)}) copy-start(s32[4,8,4]{1,2,0:T(4,128)} %param.8) | copy-start | bytes 1540
  0.9 7.8 %collective-permute-start.1 = (bf16[16,2048]{1,0:T(8,128)(2,1)S(1)}, bf16[16,2048]{1,0:T(8,128)(2,1)S(1)}, u32[]{:S(2)}, u32[]{:S(2)}) collective-permute-start(bf16[16,2048]{1,0:T(8,128)(2,1)S(1)} %constant_dynamic-slice_fusion), channel_id=1, source_target_pairs={{0,2},{2,0},{1,3},{3,1},{4,6},{6,4},{5,7},{7,5},{8,10},{10,8},{9,1... | collective-permute-start | bytes 196616 | tf_op jit(solution)/shard_map/ppermute | solution.py:163
  3.9 6.3 %collective-permute-start.3 = (bf16[16,2048]{1,0:T(8,128)(2,1)S(1)}, bf16[16,2048]{1,0:T(8,128)(2,1)S(1)}, u32[]{:S(2)}, u32[]{:S(2)}) collective-permute-start(bf16[16,2048]{1,0:T(8,128)(2,1)S(1)} %constant_dynamic-slice_fusion), channel_id=1, source_target_pairs={{0,8},{4,12},{8,0},{12,4},{1,9},{5,13},{9,1},{13,5},{2,10},{6,14},... | collective-permute-start | bytes 196616 | tf_op jit(solution)/shard_map/ppermute | solution.py:163
  6.5 6.8 %collective-permute-start = (bf16[16,2048]{1,0:T(8,128)(2,1)S(1)}, bf16[16,2048]{1,0:T(8,128)(2,1)S(1)}, u32[]{:S(2)}, u32[]{:S(2)}) collective-permute-start(bf16[16,2048]{1,0:T(8,128)(2,1)S(1)} %constant_dynamic-slice_fusion), channel_id=1, source_target_pairs={{0,12},{4,8},{8,4},{12,0},{1,13},{5,9},{9,5},{13,1},{2,14},{6,10},... | collective-permute-start | bytes 196616 | tf_op jit(solution)/shard_map/ppermute | solution.py:163
  7.9 0.7 %copy-start.5 = (s32[1,1,8,8]{3,2,1,0:T(8,128)S(1)}, s32[1,1,8,8]{3,2,1,0:T(8,128)}, u32[]{:S(2)}) copy-start(s32[1,1,8,8]{3,2,1,0:T(8,128)} %param.9) | copy-start | bytes 772
  8.8 8.8 %collective-permute-start.2 = (bf16[32,2048]{1,0:T(8,128)(2,1)S(1)}, bf16[32,2048]{1,0:T(8,128)(2,1)S(1)}, u32[]{:S(2)}, u32[]{:S(2)}) collective-permute-start(bf16[32,2048]{1,0:T(8,128)(2,1)S(1)} %pad_maximum_fusion.refs_0_), channel_id=1, source_target_pairs={{0,4},{4,0},{8,12},{12,8},{1,5},{5,1},{9,13},{13,9},{2,6},{6,2},{1... | collective-permute-start | bytes 393224 | tf_op jit(solution)/shard_map/ppermute | solution.py:163
  9.1 1.1 %collective-permute-start.4 = (s32[1,128]{1,0:T(1,128)S(1)}, s32[1,128]{1,0:T(1,128)S(1)}, u32[]{:S(2)}, u32[]{:S(2)}) collective-permute-start(s32[1,128]{1,0:T(1,128)S(1)} %shard_map.64.refs_6_.refs_5_.own_ref), channel_id=1, source_target_pairs={{0,1},{1,0},{2,3},{3,2},{4,5},{5,4},{6,7},{7,6},{8,9},{9,8},{10,11... | collective-permute-start | bytes 1544 | tf_op jit(solution)/shard_map/ppermute | solution.py:163
  10.2 5.6 %collective-permute-start.5 = (bf16[16,2048]{1,0:T(8,128)(2,1)S(1)}, bf16[16,2048]{1,0:T(8,128)(2,1)S(1)}, u32[]{:S(2)}, u32[]{:S(2)}) collective-permute-start(bf16[16,2048]{1,0:T(8,128)(2,1)S(1)} %collective-permute-done.3.refs_2_), channel_id=1, source_target_pairs={{0,2},{2,0},{1,3},{3,1},{4,6},{6,4},{5,7},{7,5},{8,10},{10,8},{9,1... | collective-permute-start | bytes 196616 | tf_op jit(solution)/shard_map/ppermute | solution.py:163
  13.3 4.3 %collective-permute-start.6 = (bf16[16,2048]{1,0:T(8,128)(2,1)S(1)}, bf16[16,2048]{1,0:T(8,128)(2,1)S(1)}, u32[]{:S(2)}, u32[]{:S(2)}) collective-permute-start(bf16[16,2048]{1,0:T(8,128)(2,1)S(1)} %collective-permute-done.refs_4_), channel_id=1, source_target_pairs={{0,2},{2,0},{1,3},{3,1},{4,6},{6,4},{5,7},{7,5},{8,10},{10,8},{9,1... | collective-permute-start | bytes 196616 | tf_op jit(solution)/shard_map/ppermute | solution.py:163
  13.8 1.2 %copy-start.1 = (bf16[4,256,512]{2,1,0:T(8,128)(2,1)S(1)}, bf16[4,256,512]{2,1,0:T(8,128)(2,1)}, u32[]{:S(2)}) copy-start(bf16[4,256,512]{2,1,0:T(8,128)(2,1)} %refs_3_.1) | copy-start | bytes 3145732
  15.0 2.5 %copy-start.2 = (bf16[4,256,512]{2,1,0:T(8,128)(2,1)S(1)}, bf16[4,256,512]{2,1,0:T(8,128)(2,1)}, u32[]{:S(2)}) copy-start(bf16[4,256,512]{2,1,0:T(8,128)(2,1)} %refs_3_.1) | copy-start | bytes 3145732
  17.5 2.3 %copy-start.4 = (f32[4,256]{1,0:T(4,128)S(1)}, f32[4,256]{1,0:T(4,128)}, u32[]{:S(2)}) copy-start(f32[4,256]{1,0:T(4,128)} %refs_2_.1) | copy-start | bytes 12292
  18.6 1.2 %collective-permute-start.7 = (f32[4,256]{1,0:T(4,128)S(1)}, f32[4,256]{1,0:T(4,128)S(1)}, u32[]{:S(2)}, u32[]{:S(2)}) collective-permute-start(f32[4,256]{1,0:T(4,128)S(1)} %shard_map.66.refs_0_), channel_id=1, source_target_pairs={{0,1},{1,0},{2,3},{3,2},{4,5},{5,4},{6,7},{7,6},{8,9},{9,8},{10,11... | collective-permute-start | bytes 12296 | tf_op jit(solution)/shard_map/ppermute | solution.py:163
  21.2 5.0 %collective-permute-start.10 = (bf16[16,2048]{1,0:T(8,128)(2,1)S(1)}, bf16[16,2048]{1,0:T(8,128)(2,1)S(1)}, u32[]{:S(2)}, u32[]{:S(2)}) collective-permute-start(bf16[16,2048]{1,0:T(8,128)(2,1)S(1)} %get-tuple-element.30), channel_id=1, source_target_pairs={{0,2},{2,0},{1,3},{3,1},{4,6},{6,4},{5,7},{7,5},{8,10},{10,8},{9,1... | collective-permute-start | bytes 196616 | tf_op jit(solution)/shard_map/ppermute | solution.py:163
  22.3 5.9 %collective-permute-start.12 = (bf16[16,2048]{1,0:T(8,128)(2,1)S(1)}, bf16[16,2048]{1,0:T(8,128)(2,1)S(1)}, u32[]{:S(2)}, u32[]{:S(2)}) collective-permute-start(bf16[16,2048]{1,0:T(8,128)(2,1)S(1)} %get-tuple-element.34), channel_id=1, source_target_pairs={{0,2},{2,0},{1,3},{3,1},{4,6},{6,4},{5,7},{7,5},{8,10},{10,8},{9,1... | collective-permute-start | bytes 196616 | tf_op jit(solution)/shard_map/ppermute | solution.py:163
  23.8 6.2 %collective-permute-start.8 = (bf16[32,2048]{1,0:T(8,128)(2,1)S(1)}, bf16[32,2048]{1,0:T(8,128)(2,1)S(1)}, u32[]{:S(2)}, u32[]{:S(2)}) collective-permute-start(bf16[32,2048]{1,0:T(8,128)(2,1)S(1)} %get-tuple-element.28), channel_id=1, source_target_pairs={{0,4},{4,0},{8,12},{12,8},{1,5},{5,1},{9,13},{13,9},{2,6},{6,2},{1... | collective-permute-start | bytes 393224 | tf_op jit(solution)/shard_map/ppermute | solution.py:163
  26.3 6.6 %collective-permute-start.11 = (bf16[16,2048]{1,0:T(8,128)(2,1)S(1)}, bf16[16,2048]{1,0:T(8,128)(2,1)S(1)}, u32[]{:S(2)}, u32[]{:S(2)}) collective-permute-start(bf16[16,2048]{1,0:T(8,128)(2,1)S(1)} %add_convert_fusion.1), channel_id=1, source_target_pairs={{0,8},{4,12},{8,0},{12,4},{1,9},{5,13},{9,1},{13,5},{2,10},{6,14},... | collective-permute-start | bytes 196616 | tf_op jit(solution)/shard_map/ppermute | solution.py:163
  28.2 6.1 %collective-permute-start.13 = (bf16[16,2048]{1,0:T(8,128)(2,1)S(1)}, bf16[16,2048]{1,0:T(8,128)(2,1)S(1)}, u32[]{:S(2)}, u32[]{:S(2)}) collective-permute-start(bf16[16,2048]{1,0:T(8,128)(2,1)S(1)} %add_convert_fusion), channel_id=1, source_target_pairs={{0,12},{4,8},{8,4},{12,0},{1,13},{5,9},{9,5},{13,1},{2,14},{6,10},... | collective-permute-start | bytes 196616 | tf_op jit(solution)/shard_map/ppermute | solution.py:163
  30.1 5.8 %copy-start.3 = (bf16[16,4096]{1,0:T(8,128)(2,1)S(1)}, bf16[16,4096]{1,0:T(8,128)(2,1)}, u32[]{:S(2)}) copy-start(bf16[16,4096]{1,0:T(8,128)(2,1)} %core_ref.1) | copy-start | bytes 393220
  30.1 4.3 %collective-permute-start.9 = (bf16[16,2048]{1,0:T(8,128)(2,1)S(1)}, bf16[16,2048]{1,0:T(8,128)(2,1)S(1)}, u32[]{:S(2)}, u32[]{:S(2)}) collective-permute-start(bf16[16,2048]{1,0:T(8,128)(2,1)S(1)} %slice.17), channel_id=1, source_target_pairs={{0,2},{2,0},{1,3},{3,1},{4,6},{6,4},{5,7},{7,5},{8,10},{10,8},{9,1... | collective-permute-start | bytes 196616 | tf_op jit(solution)/shard_map/ppermute | solution.py:163
  34.4 1.4 %collective-permute-start.14 = (f32[16,2048]{1,0:T(8,128)S(1)}, f32[16,2048]{1,0:T(8,128)S(1)}, u32[]{:S(2)}, u32[]{:S(2)}) collective-permute-start(f32[16,2048]{1,0:T(8,128)S(1)} %fusion.1.mine_ref), channel_id=1, source_target_pairs={{0,1},{1,0},{2,3},{3,2},{4,5},{5,4},{6,7},{7,6},{8,9},{9,8},{10,11... | collective-permute-start | bytes 393224 | tf_op jit(solution)/shard_map/ppermute | solution.py:163

commit v18 on v13

--- a/solution.py
+++ b/solution.py
@@ -182,11 +182,11 @@
     direct = {dz: swap(mine, "batch", rows_z, dz) for dz in far}
     beside = [swap(mine, "pair", rows_x, dx) for dx in side]
     *beside, own_rows = lax.optimization_barrier((*beside, own_rows))
-    arrays, places = [mine, *beside], [[dx] for dx in range(rows_x)]
+    cluster = jnp.concatenate([mine, *beside], axis=0)
+    arrays, places = [cluster], [list(range(rows_x))]
     for dz in near:
-        for dx, piece in enumerate([mine, *beside]):
-            arrays.append(swap(piece, "batch", rows_z, dz))
-            places.append([dz * rows_x + dx])
+        arrays.append(swap(cluster, "batch", rows_z, dz))
+        places.append(list(range(dz * rows_x, (dz + 1) * rows_x)))
     direct[far[0]], other_rows = lax.optimization_barrier((direct[far[0]], other_rows))
     for dz in far:
         arrays.append(direct[dz])
@@ -244,11 +244,10 @@
     cluster = clusters[0].astype(f32)
     for dz, array in zip(near, clusters[1:]):
         cluster = cluster + swap(array, "batch", rows_z, dz).astype(f32)
-    total = cluster[:held]
+    mine_total = cluster[:held]
     for dx in side:
-        total = total + swap(cluster[dx * held:(dx + 1) * held].astype(bf16), "pair", rows_x, dx).astype(f32)
-    for term in landed:
-        total = total + term
+        mine_total = mine_total + swap(cluster[dx * held:(dx + 1) * held].astype(bf16), "pair", rows_x, dx).astype(f32)
+    total = mine_total + landed[1] + landed[0]
     total_other = swap(total, "orb", 2, 1)
     return call(
         finish_kernel, jax.ShapeDtypeStruct((held, square), f32), 3, scalars=1, moved=held * square * 12

time: 37.5 us -> 36.7 us (0.979)
  starting transfers between devices: 17 us -> 15 us
  waiting for transfers between devices: 13.1 us -> 14.3 us
    ppermute x16 -> x15, starting transfers between devices: 17 us -> 15 us  [swap(): return lax.ppermute(array, axis, [(i, i ^ step) for i in range(count)])]
    ppermute x16 -> x15, waiting for transfers between devices: 13.1 us -> 14.3 us  [swap(): return lax.ppermute(array, axis, [(i, i ^ step) for i in range(count)])]
  transfers between devices with their start and end apart: 16 -> 15, of which waited for: 9 -> 8; matrix products, arithmetic and copies ran while one was open for 0% -> 0% of each run, Pallas kernels for 3% -> 3%
where the time goes in v18:
time: 36.7 us; the launch traced here: 36.5 us
  starting transfers between devices  15 us (41%)
  waiting for transfers between devices  14.3 us (39%)
  Pallas kernels  4.15 us (11%)
  local copies, waits for them, and re-layouts  2.84 us (8%)
    ppermute x15, starting transfers between devices, swap(): return lax.ppermute(array, axis, [(i, i ^ step) for i in range(count)])  15 us
    ppermute x15, waiting for transfers between devices, swap(): return lax.ppermute(array, axis, [(i, i ^ step) for i in range(count)])  14.3 us
    unnamed x14, local copies, waits for them, and re-layouts  2.74 us
    pallas_call x1, Pallas kernels, per_device(): call(functools.partial(scatter_kernel, out_places), [jax.ShapeDtypeStruct...  1.4 us
    pallas_call x1, Pallas kernels, per_device(): call(functools.partial(density_kernel, places), jax.ShapeDtypeStruct((bat...  1.07 us
    pallas_call x1, Pallas kernels, per_device(): call(prepare_kernel, (jax.ShapeDtypeStruct((batches, points, kept), bf16)...  0.76 us
  transfers between devices with their start and end apart: 15, of which 8 were waited for; matrix products, arithmetic and copies ran while one was open for 0% of the time, Pallas kernels for 3%

profile of v18, /device:TPU:0, one launch (start us, length us, event | category | flops | bytes accessed | tf_op | source)
XLA Modules:
  0.0 36.5 jit_solution(15444159110470802722)
XLA Ops:
  0.0 0.0 copy-start
  0.0 0.9 %copy-done = bf16[16,4096]{1,0:T(8,128)(2,1)S(1)} copy-done((bf16[16,4096]{1,0:T(8,128)(2,1)S(1)}, bf16[16,4096]{1,0:T(8,128)(2,1)}, u32[]{:S(2)}) %copy-start) | copy-done | bytes 131096
  0.9 3.0 %collective-permute-start.1 = (bf16[16,2048]{1,0:T(8,128)(2,1)S(1)}, bf16[16,2048]{1,0:T(8,128)(2,1)S(1)}, u32[]{:S(2)}, u32[]{:S(2)}) collective-permute-start(bf16[16,2048]{1,0:T(8,128)(2,1)S(1)} %constant_dynamic-slice_fusion), channel_id=1, source_target_pairs={{0,2},{2,0},{1,3},{3,1},{4,6},{6,4},{5,7},{7,5},{8,10},{10,8},{9,1... | collective-permute-start | bytes 196616 | tf_op jit(solution)/shard_map/ppermute | solution.py:153
  3.9 2.6 %collective-permute-start.3 = (bf16[16,2048]{1,0:T(8,128)(2,1)S(1)}, bf16[16,2048]{1,0:T(8,128)(2,1)S(1)}, u32[]{:S(2)}, u32[]{:S(2)}) collective-permute-start(bf16[16,2048]{1,0:T(8,128)(2,1)S(1)} %constant_dynamic-slice_fusion), channel_id=1, source_target_pairs={{0,8},{4,12},{8,0},{12,4},{1,9},{5,13},{9,1},{13,5},{2,10},{6,14},... | collective-permute-start | bytes 196616 | tf_op jit(solution)/shard_map/ppermute | solution.py:153
  6.5 1.3 %collective-permute-start = (bf16[16,2048]{1,0:T(8,128)(2,1)S(1)}, bf16[16,2048]{1,0:T(8,128)(2,1)S(1)}, u32[]{:S(2)}, u32[]{:S(2)}) collective-permute-start(bf16[16,2048]{1,0:T(8,128)(2,1)S(1)} %constant_dynamic-slice_fusion), channel_id=1, source_target_pairs={{0,12},{4,8},{8,4},{12,0},{1,13},{5,9},{9,5},{13,1},{2,14},{6,10},... | collective-permute-start | bytes 196616 | tf_op jit(solution)/shard_map/ppermute | solution.py:153
  7.9 0.0 copy-done.6
  7.9 0.0 copy-start.5
  7.9 0.1 reshape.16.slots_ref
  7.9 0.6 %copy-done.5 = s32[1,1,8,8]{3,2,1,0:T(8,128)S(1)} copy-done((s32[1,1,8,8]{3,2,1,0:T(8,128)S(1)}, s32[1,1,8,8]{3,2,1,0:T(8,128)}, u32[]{:S(2)}) %copy-start.5) | copy-done | bytes 280
  8.5 0.2 shard_map.64.refs_6_.refs_5_
  8.7 0.0 collective-permute-done.1
  8.8 0.3 collective-permute-start.2
  9.1 0.0 collective-permute-start.4
  9.1 1.1 %collective-permute-done.4.refs_7_.refs_6_ = s32[1,128]{1,0:T(1,128)S(1)} collective-permute-done((s32[1,128]{1,0:T(1,128)S(1)}, s32[1,128]{1,0:T(1,128)S(1)}, u32[]{:S(2)}, u32[]{:S(2)}) %collective-permute-start.4) | collective-permute-done | bytes 544 | tf_op jit(solution)/shard_map/ppermute | solution.py:153
  10.2 0.0 collective-permute-done.3.refs_2_
  10.2 0.8 %collective-permute-start.5 = (bf16[16,2048]{1,0:T(8,128)(2,1)S(1)}, bf16[16,2048]{1,0:T(8,128)(2,1)S(1)}, u32[]{:S(2)}, u32[]{:S(2)}) collective-permute-start(bf16[16,2048]{1,0:T(8,128)(2,1)S(1)} %collective-permute-done.3.refs_2_), channel_id=1, source_target_pairs={{0,2},{2,0},{1,3},{3,1},{4,6},{6,4},{5,7},{7,5},{8,10},{10,8},{9,1... | collective-permute-start | bytes 196616 | tf_op jit(solution)/shard_map/ppermute | solution.py:153
  11.0 2.3 %collective-permute-done.refs_4_ = bf16[16,2048]{1,0:T(8,128)(2,1)S(1)} collective-permute-done((bf16[16,2048]{1,0:T(8,128)(2,1)S(1)}, bf16[16,2048]{1,0:T(8,128)(2,1)S(1)}, u32[]{:S(2)}, u32[]{:S(2)}) %collective-permute-start) | collective-permute-done | bytes 65568 | tf_op jit(solution)/shard_map/ppermute | solution.py:153
  13.3 0.5 %collective-permute-start.6 = (bf16[16,2048]{1,0:T(8,128)(2,1)S(1)}, bf16[16,2048]{1,0:T(8,128)(2,1)S(1)}, u32[]{:S(2)}, u32[]{:S(2)}) collective-permute-start(bf16[16,2048]{1,0:T(8,128)(2,1)S(1)} %collective-permute-done.refs_4_), channel_id=1, source_target_pairs={{0,2},{2,0},{1,3},{3,1},{4,6},{6,4},{5,7},{7,5},{8,10},{10,8},{9,1... | collective-permute-start | bytes 196616 | tf_op jit(solution)/shard_map/ppermute | solution.py:153
  13.8 0.0 copy-start.1
  13.8 1.2 %copy-done.1 = bf16[4,256,512]{2,1,0:T(8,128)(2,1)S(1)} copy-done((bf16[4,256,512]{2,1,0:T(8,128)(2,1)S(1)}, bf16[4,256,512]{2,1,0:T(8,128)(2,1)}, u32[]{:S(2)}) %copy-start.1) | copy-done | bytes 1048600
  15.0 0.0 copy-start.2
  15.0 0.8 %shard_map.65 = (bf16[4,256,256]{2,1,0:T(8,128)(2,1)S(1)}, bf16[4,256,256]{2,1,0:T(8,128)(2,1)S(1)}) custom-call(s32[1]{0:T(128)} %bitcast.half_ref.core_ref, bf16[4,256,512]{2,1,0:T(8,128)(2,1)S(1)} %copy-done.1), custom_call_target="tpu_custom_call" | custom-call | flops 536870912 | bytes 3145728 | tf_op jit(solution)/shard_map/pallas_call | solution.py:199
  15.8 0.0 collective-permute-done.5.refs_3_
  15.8 1.7 %collective-permute-done.6.refs_5_ = bf16[16,2048]{1,0:T(8,128)(2,1)S(1)} collective-permute-done((bf16[16,2048]{1,0:T(8,128)(2,1)S(1)}, bf16[16,2048]{1,0:T(8,128)(2,1)S(1)}, u32[]{:S(2)}, u32[]{:S(2)}) %collective-permute-start.6) | collective-permute-done | bytes 65568 | tf_op jit(solution)/shard_map/ppermute | solution.py:153
  17.5 0.0 collective-permute-done.2.refs_1_
  17.5 0.0 copy-done.2
  17.5 1.1 %shard_map.66.refs_0_ = f32[4,256]{1,0:T(4,128)S(1)} custom-call(s32[1]{0:T(128)} %bitcast.1.place_ref, s32[1]{0:T(128)} %bitcast.half_ref.core_ref, bf16[32,2048]{1,0:T(8,128)(2,1)S(1)} %pad_maximum_fusion.refs_0_, bf16[32,2048]{1,0:T(8,128)(2,1)S(1)} %collective-permute-done.2.refs_1_, bf16[16,2048]{1,0:T(8,128)(2,1)S(1)} %collective-permute-done.3.refs_2_, ...), custom_call_target="tpu_custom_call" | custom-call | flops 268435456 | bytes 2097152 | tf_op jit(solution)/shard_map/pallas_call | solution.py:214
  18.6 0.1 collective-permute-start.7
  18.7 1.2 %collective-permute-done.7.refs_1_ = f32[4,256]{1,0:T(4,128)S(1)} collective-permute-done((f32[4,256]{1,0:T(4,128)S(1)}, f32[4,256]{1,0:T(4,128)S(1)}, u32[]{:S(2)}, u32[]{:S(2)}) %collective-permute-start.7) | collective-permute-done | bytes 4128 | tf_op jit(solution)/shard_map/ppermute | solution.py:153
  19.8 0.0 copy-done.4
  19.8 1.4 %shard_map.67 = (bf16[32,2048]{1,0:T(8,128)(2,1)S(1)}, bf16[32,2048]{1,0:T(8,128)(2,1)S(1)}, bf16[16,2048]{1,0:T(8,128)(2,1)S(1)}, bf16[16,2048]{1,0:T(8,128)(2,...) custom-call(s32[1]{0:T(128)} %bitcast.1.place_ref, s32[1]{0:T(128)} %bitcast.half_ref.core_ref, ...), custom_call_target="tpu_custom_call" | custom-call | flops 268435456 | bytes 2097152 | tf_op jit(solution)/shard_map/pallas_call | solution.py:227
  21.3 0.6 %collective-permute-start.10 = (bf16[16,2048]{1,0:T(8,128)(2,1)S(1)}, bf16[16,2048]{1,0:T(8,128)(2,1)S(1)}, u32[]{:S(2)}, u32[]{:S(2)}) collective-permute-start(bf16[16,2048]{1,0:T(8,128)(2,1)S(1)} %get-tuple-element.28), channel_id=1, source_target_pairs={{0,2},{2,0},{1,3},{3,1},{4,6},{6,4},{5,7},{7,5},{8,10},{10,8},{9,1... | collective-permute-start | bytes 196616 | tf_op jit(solution)/shard_map/ppermute | solution.py:153
  21.9 1.5 %collective-permute-start.12 = (bf16[16,2048]{1,0:T(8,128)(2,1)S(1)}, bf16[16,2048]{1,0:T(8,128)(2,1)S(1)}, u32[]{:S(2)}, u32[]{:S(2)}) collective-permute-start(bf16[16,2048]{1,0:T(8,128)(2,1)S(1)} %get-tuple-element.30), channel_id=1, source_target_pairs={{0,2},{2,0},{1,3},{3,1},{4,6},{6,4},{5,7},{7,5},{8,10},{10,8},{9,1... | collective-permute-start | bytes 196616 | tf_op jit(solution)/shard_map/ppermute | solution.py:153
  23.3 0.1 collective-permute-start.8
  23.5 2.7 %collective-permute-done.10 = bf16[16,2048]{1,0:T(8,128)(2,1)S(1)} collective-permute-done((bf16[16,2048]{1,0:T(8,128)(2,1)S(1)}, bf16[16,2048]{1,0:T(8,128)(2,1)S(1)}, u32[]{:S(2)}, u32[]{:S(2)}) %collective-permute-start.10) | collective-permute-done | bytes 65568 | tf_op jit(solution)/shard_map/ppermute | solution.py:153
  26.2 2.4 %collective-permute-start.11 = (bf16[16,2048]{1,0:T(8,128)(2,1)S(1)}, bf16[16,2048]{1,0:T(8,128)(2,1)S(1)}, u32[]{:S(2)}, u32[]{:S(2)}) collective-permute-start(bf16[16,2048]{1,0:T(8,128)(2,1)S(1)} %add_convert_fusion.1), channel_id=1, source_target_pairs={{0,12},{4,8},{8,4},{12,0},{1,13},{5,9},{9,5},{13,1},{2,14},{6,10},... | collective-permute-start | bytes 196616 | tf_op jit(solution)/shard_map/ppermute | solution.py:153
  28.6 0.0 collective-permute-done.12
  28.7 0.2 collective-permute-start.13
  28.9 0.0 collective-permute-done.8
  28.9 0.0 copy-start.3
  28.9 1.4 %collective-permute-start.9 = (bf16[16,2048]{1,0:T(8,128)(2,1)S(1)}, bf16[16,2048]{1,0:T(8,128)(2,1)S(1)}, u32[]{:S(2)}, u32[]{:S(2)}) collective-permute-start(bf16[16,2048]{1,0:T(8,128)(2,1)S(1)} %slice.17), channel_id=1, source_target_pairs={{0,2},{2,0},{1,3},{3,1},{4,6},{6,4},{5,7},{7,5},{8,10},{10,8},{9,1... | collective-permute-start | bytes 196616 | tf_op jit(solution)/shard_map/ppermute | solution.py:153
  30.4 2.0 %collective-permute-done.11 = bf16[16,2048]{1,0:T(8,128)(2,1)S(1)} collective-permute-done((bf16[16,2048]{1,0:T(8,128)(2,1)S(1)}, bf16[16,2048]{1,0:T(8,128)(2,1)S(1)}, u32[]{:S(2)}, u32[]{:S(2)}) %collective-permute-start.11) | collective-permute-done | bytes 65568 | tf_op jit(solution)/shard_map/ppermute | solution.py:153
  32.3 2.0 %collective-permute-done.13 = bf16[16,2048]{1,0:T(8,128)(2,1)S(1)} collective-permute-done((bf16[16,2048]{1,0:T(8,128)(2,1)S(1)}, bf16[16,2048]{1,0:T(8,128)(2,1)S(1)}, u32[]{:S(2)}, u32[]{:S(2)}) %collective-permute-start.13) | collective-permute-done | bytes 65568 | tf_op jit(solution)/shard_map/ppermute | solution.py:153
  34.3 0.0 collective-permute-done.9
  34.3 0.1 collective-permute-start.14
  34.4 1.3 %collective-permute-done.14.other_ref = f32[16,2048]{1,0:T(8,128)S(1)} collective-permute-done((f32[16,2048]{1,0:T(8,128)S(1)}, f32[16,2048]{1,0:T(8,128)S(1)}, u32[]{:S(2)}, u32[]{:S(2)}) %collective-permute-start.14) | collective-permute-done | bytes 131104 | tf_op jit(solution)/shard_map/ppermute | solution.py:153
  35.8 0.0 copy-done.3
  35.8 0.7 %shard_map.68 = f32[16,4096]{1,0:T(8,128)} custom-call(s32[1]{0:T(128)} %bitcast.half_ref.core_ref, f32[16,2048]{1,0:T(8,128)S(1)} %fusion.1.mine_ref, f32[16,2048]{1,0:T(8,128)S(1)} %collective-permute-done.14.other_ref, bf16[16,4096]{1,0:T(8,128)(2,1)S(1)} %copy-done.3), custom_call_target="tpu_custom_call" | custom-call | bytes 786432 | tf_op jit(solution)/shard_map/pallas_call | solution.py:252
  (9 shorter events, 0.1 us)
Async XLA Ops:
  0.0 0.9 %copy-start = (bf16[16,4096]{1,0:T(8,128)(2,1)S(1)}, bf16[16,4096]{1,0:T(8,128)(2,1)}, u32[]{:S(2)}) copy-start(bf16[16,4096]{1,0:T(8,128)(2,1)} %param.10) | copy-start | bytes 393220
  0.9 6.9 %copy-start.6 = (s32[4,8,4]{1,2,0:T(4,128)S(1)}, s32[4,8,4]{1,2,0:T(4,128)}, u32[]{:S(2)}) copy-start(s32[4,8,4]{1,2,0:T(4,128)} %param.8) | copy-start | bytes 1540
  0.9 7.8 %collective-permute-start.1 = (bf16[16,2048]{1,0:T(8,128)(2,1)S(1)}, bf16[16,2048]{1,0:T(8,128)(2,1)S(1)}, u32[]{:S(2)}, u32[]{:S(2)}) collective-permute-start(bf16[16,2048]{1,0:T(8,128)(2,1)S(1)} %constant_dynamic-slice_fusion), channel_id=1, source_target_pairs={{0,2},{2,0},{1,3},{3,1},{4,6},{6,4},{5,7},{7,5},{8,10},{10,8},{9,1... | collective-permute-start | bytes 196616 | tf_op jit(solution)/shard_map/ppermute | solution.py:153
  3.9 6.3 %collective-permute-start.3 = (bf16[16,2048]{1,0:T(8,128)(2,1)S(1)}, bf16[16,2048]{1,0:T(8,128)(2,1)S(1)}, u32[]{:S(2)}, u32[]{:S(2)}) collective-permute-start(bf16[16,2048]{1,0:T(8,128)(2,1)S(1)} %constant_dynamic-slice_fusion), channel_id=1, source_target_pairs={{0,8},{4,12},{8,0},{12,4},{1,9},{5,13},{9,1},{13,5},{2,10},{6,14},... | collective-permute-start | bytes 196616 | tf_op jit(solution)/shard_map/ppermute | solution.py:153
  6.5 6.8 %collective-permute-start = (bf16[16,2048]{1,0:T(8,128)(2,1)S(1)}, bf16[16,2048]{1,0:T(8,128)(2,1)S(1)}, u32[]{:S(2)}, u32[]{:S(2)}) collective-permute-start(bf16[16,2048]{1,0:T(8,128)(2,1)S(1)} %constant_dynamic-slice_fusion), channel_id=1, source_target_pairs={{0,12},{4,8},{8,4},{12,0},{1,13},{5,9},{9,5},{13,1},{2,14},{6,10},... | collective-permute-start | bytes 196616 | tf_op jit(solution)/shard_map/ppermute | solution.py:153
  7.9 0.7 %copy-start.5 = (s32[1,1,8,8]{3,2,1,0:T(8,128)S(1)}, s32[1,1,8,8]{3,2,1,0:T(8,128)}, u32[]{:S(2)}) copy-start(s32[1,1,8,8]{3,2,1,0:T(8,128)} %param.9) | copy-start | bytes 772
  8.8 8.8 %collective-permute-start.2 = (bf16[32,2048]{1,0:T(8,128)(2,1)S(1)}, bf16[32,2048]{1,0:T(8,128)(2,1)S(1)}, u32[]{:S(2)}, u32[]{:S(2)}) collective-permute-start(bf16[32,2048]{1,0:T(8,128)(2,1)S(1)} %pad_maximum_fusion.refs_0_), channel_id=1, source_target_pairs={{0,4},{4,0},{8,12},{12,8},{1,5},{5,1},{9,13},{13,9},{2,6},{6,2},{1... | collective-permute-start | bytes 393224 | tf_op jit(solution)/shard_map/ppermute | solution.py:153
  9.1 1.1 %collective-permute-start.4 = (s32[1,128]{1,0:T(1,128)S(1)}, s32[1,128]{1,0:T(1,128)S(1)}, u32[]{:S(2)}, u32[]{:S(2)}) collective-permute-start(s32[1,128]{1,0:T(1,128)S(1)} %shard_map.64.refs_6_.refs_5_), channel_id=1, source_target_pairs={{0,1},{1,0},{2,3},{3,2},{4,5},{5,4},{6,7},{7,6},{8,9},{9,8},{10,11... | collective-permute-start | bytes 1544 | tf_op jit(solution)/shard_map/ppermute | solution.py:153
  10.2 5.6 %collective-permute-start.5 = (bf16[16,2048]{1,0:T(8,128)(2,1)S(1)}, bf16[16,2048]{1,0:T(8,128)(2,1)S(1)}, u32[]{:S(2)}, u32[]{:S(2)}) collective-permute-start(bf16[16,2048]{1,0:T(8,128)(2,1)S(1)} %collective-permute-done.3.refs_2_), channel_id=1, source_target_pairs={{0,2},{2,0},{1,3},{3,1},{4,6},{6,4},{5,7},{7,5},{8,10},{10,8},{9,1... | collective-permute-start | bytes 196616 | tf_op jit(solution)/shard_map/ppermute | solution.py:153
  13.3 4.3 %collective-permute-start.6 = (bf16[16,2048]{1,0:T(8,128)(2,1)S(1)}, bf16[16,2048]{1,0:T(8,128)(2,1)S(1)}, u32[]{:S(2)}, u32[]{:S(2)}) collective-permute-start(bf16[16,2048]{1,0:T(8,128)(2,1)S(1)} %collective-permute-done.refs_4_), channel_id=1, source_target_pairs={{0,2},{2,0},{1,3},{3,1},{4,6},{6,4},{5,7},{7,5},{8,10},{10,8},{9,1... | collective-permute-start | bytes 196616 | tf_op jit(solution)/shard_map/ppermute | solution.py:153
  13.8 1.2 %copy-start.1 = (bf16[4,256,512]{2,1,0:T(8,128)(2,1)S(1)}, bf16[4,256,512]{2,1,0:T(8,128)(2,1)}, u32[]{:S(2)}) copy-start(bf16[4,256,512]{2,1,0:T(8,128)(2,1)} %refs_3_.1) | copy-start | bytes 3145732
  15.0 2.5 %copy-start.2 = (bf16[4,256,512]{2,1,0:T(8,128)(2,1)S(1)}, bf16[4,256,512]{2,1,0:T(8,128)(2,1)}, u32[]{:S(2)}) copy-start(bf16[4,256,512]{2,1,0:T(8,128)(2,1)} %refs_3_.1) | copy-start | bytes 3145732
  17.5 2.3 %copy-start.4 = (f32[4,256]{1,0:T(4,128)S(1)}, f32[4,256]{1,0:T(4,128)}, u32[]{:S(2)}) copy-start(f32[4,256]{1,0:T(4,128)} %refs_2_.1) | copy-start | bytes 12292
  18.6 1.2 %collective-permute-start.7 = (f32[4,256]{1,0:T(4,128)S(1)}, f32[4,256]{1,0:T(4,128)S(1)}, u32[]{:S(2)}, u32[]{:S(2)}) collective-permute-start(f32[4,256]{1,0:T(4,128)S(1)} %shard_map.66.refs_0_), channel_id=1, source_target_pairs={{0,1},{1,0},{2,3},{3,2},{4,5},{5,4},{6,7},{7,6},{8,9},{9,8},{10,11... | collective-permute-start | bytes 12296 | tf_op jit(solution)/shard_map/ppermute | solution.py:153
  21.3 4.9 %collective-permute-start.10 = (bf16[16,2048]{1,0:T(8,128)(2,1)S(1)}, bf16[16,2048]{1,0:T(8,128)(2,1)S(1)}, u32[]{:S(2)}, u32[]{:S(2)}) collective-permute-start(bf16[16,2048]{1,0:T(8,128)(2,1)S(1)} %get-tuple-element.28), channel_id=1, source_target_pairs={{0,2},{2,0},{1,3},{3,1},{4,6},{6,4},{5,7},{7,5},{8,10},{10,8},{9,1... | collective-permute-start | bytes 196616 | tf_op jit(solution)/shard_map/ppermute | solution.py:153
  21.9 6.8 %collective-permute-start.12 = (bf16[16,2048]{1,0:T(8,128)(2,1)S(1)}, bf16[16,2048]{1,0:T(8,128)(2,1)S(1)}, u32[]{:S(2)}, u32[]{:S(2)}) collective-permute-start(bf16[16,2048]{1,0:T(8,128)(2,1)S(1)} %get-tuple-element.30), channel_id=1, source_target_pairs={{0,2},{2,0},{1,3},{3,1},{4,6},{6,4},{5,7},{7,5},{8,10},{10,8},{9,1... | collective-permute-start | bytes 196616 | tf_op jit(solution)/shard_map/ppermute | solution.py:153
  23.3 5.5 %collective-permute-start.8 = (bf16[32,2048]{1,0:T(8,128)(2,1)S(1)}, bf16[32,2048]{1,0:T(8,128)(2,1)S(1)}, u32[]{:S(2)}, u32[]{:S(2)}) collective-permute-start(bf16[32,2048]{1,0:T(8,128)(2,1)S(1)} %get-tuple-element.26), channel_id=1, source_target_pairs={{0,4},{4,0},{8,12},{12,8},{1,5},{5,1},{9,13},{13,9},{2,6},{6,2},{1... | collective-permute-start | bytes 393224 | tf_op jit(solution)/shard_map/ppermute | solution.py:153
  26.2 6.1 %collective-permute-start.11 = (bf16[16,2048]{1,0:T(8,128)(2,1)S(1)}, bf16[16,2048]{1,0:T(8,128)(2,1)S(1)}, u32[]{:S(2)}, u32[]{:S(2)}) collective-permute-start(bf16[16,2048]{1,0:T(8,128)(2,1)S(1)} %add_convert_fusion.1), channel_id=1, source_target_pairs={{0,12},{4,8},{8,4},{12,0},{1,13},{5,9},{9,5},{13,1},{2,14},{6,10},... | collective-permute-start | bytes 196616 | tf_op jit(solution)/shard_map/ppermute | solution.py:153
  28.7 5.6 %collective-permute-start.13 = (bf16[16,2048]{1,0:T(8,128)(2,1)S(1)}, bf16[16,2048]{1,0:T(8,128)(2,1)S(1)}, u32[]{:S(2)}, u32[]{:S(2)}) collective-permute-start(bf16[16,2048]{1,0:T(8,128)(2,1)S(1)} %add_convert_fusion), channel_id=1, source_target_pairs={{0,8},{4,12},{8,0},{12,4},{1,9},{5,13},{9,1},{13,5},{2,10},{6,14},... | collective-permute-start | bytes 196616 | tf_op jit(solution)/shard_map/ppermute | solution.py:153
  28.9 6.8 %copy-start.3 = (bf16[16,4096]{1,0:T(8,128)(2,1)S(1)}, bf16[16,4096]{1,0:T(8,128)(2,1)}, u32[]{:S(2)}) copy-start(bf16[16,4096]{1,0:T(8,128)(2,1)} %core_ref.1) | copy-start | bytes 393220
  28.9 5.4 %collective-permute-start.9 = (bf16[16,2048]{1,0:T(8,128)(2,1)S(1)}, bf16[16,2048]{1,0:T(8,128)(2,1)S(1)}, u32[]{:S(2)}, u32[]{:S(2)}) collective-permute-start(bf16[16,2048]{1,0:T(8,128)(2,1)S(1)} %slice.17), channel_id=1, source_target_pairs={{0,2},{2,0},{1,3},{3,1},{4,6},{6,4},{5,7},{7,5},{8,10},{10,8},{9,1... | collective-permute-start | bytes 196616 | tf_op jit(solution)/shard_map/ppermute | solution.py:153
  34.3 1.4 %collective-permute-start.14 = (f32[16,2048]{1,0:T(8,128)S(1)}, f32[16,2048]{1,0:T(8,128)S(1)}, u32[]{:S(2)}, u32[]{:S(2)}) collective-permute-start(f32[16,2048]{1,0:T(8,128)S(1)} %fusion.1.mine_ref), channel_id=1, source_target_pairs={{0,1},{1,0},{2,3},{3,2},{4,5},{5,4},{6,7},{7,6},{8,9},{9,8},{10,11... | collective-permute-start | bytes 393224 | tf_op jit(solution)/shard_map/ppermute | solution.py:153

commit v19 on v18

--- a/solution.py
+++ b/solution.py
@@ -180,7 +180,9 @@
 
     mine = lax.dynamic_slice_in_dim(density_blocks, half * wide, wide, 1)
     direct = {dz: swap(mine, "batch", rows_z, dz) for dz in far}
-    beside = [swap(mine, "pair", rows_x, dx) for dx in side]
+    beside = [
+        lax.dynamic_slice_in_dim(swap(density_blocks, "pair", rows_x, dx), half * wide, wide, 1) for dx in side
+    ]
     *beside, own_rows = lax.optimization_barrier((*beside, own_rows))
     cluster = jnp.concatenate([mine, *beside], axis=0)
     arrays, places = [cluster], [list(range(rows_x))]
@@ -244,10 +246,11 @@
     cluster = clusters[0].astype(f32)
     for dz, array in zip(near, clusters[1:]):
         cluster = cluster + swap(array, "batch", rows_z, dz).astype(f32)
-    mine_total = cluster[:held]
+    total = cluster[:held]
     for dx in side:
-        mine_total = mine_total + swap(cluster[dx * held:(dx + 1) * held].astype(bf16), "pair", rows_x, dx).astype(f32)
-    total = mine_total + landed[1] + landed[0]
+        total = total + swap(cluster[dx * held:(dx + 1) * held].astype(bf16), "pair", rows_x, dx).astype(f32)
+    for term in landed:
+        total = total + term
     total_other = swap(total, "orb", 2, 1)
     return call(
         finish_kernel, jax.ShapeDtypeStruct((held, square), f32), 3, scalars=1, moved=held * square * 12

time: 36.7 us -> 36.6 us (level)
  starting transfers between devices: 15 us -> 15.8 us
  waiting for transfers between devices: 14.3 us -> 13.5 us
    unnamed x14 -> x12, local copies, waits for them, and re-layouts: 2.74 us -> 1.84 us
    dynamic_slice x1, local copies, waits for them, and re-layouts: 0.01 us -> 0.88 us  [per_device(): mine = lax.dynamic_slice_in_dim(density_blocks, half * wide, wide, 1)]
    ppermute x15, waiting for transfers between devices: 14.3 us -> 13.5 us  [swap(): return lax.ppermute(array, axis, [(i, i ^ step) for i in range(count)])]
    ppermute x15, starting transfers between devices: 15 us -> 15.8 us  [swap(): return lax.ppermute(array, axis, [(i, i ^ step) for i in range(count)])]
  transfers between devices with their start and end apart: 15 -> 15, of which waited for: 8 -> 8; matrix products, arithmetic and copies ran while one was open for 0% -> 3% of each run, Pallas kernels for 3% -> 3%
where the time goes in v19:
time: 36.6 us; the launch traced here: 36.4 us
  starting transfers between devices  15.8 us (43%)
  waiting for transfers between devices  13.5 us (37%)
  Pallas kernels  4.15 us (11%)
  local copies, waits for them, and re-layouts  2.82 us (8%)
    ppermute x15, starting transfers between devices, swap(): return lax.ppermute(array, axis, [(i, i ^ step) for i in range(count)])  15.8 us
    ppermute x15, waiting for transfers between devices, swap(): return lax.ppermute(array, axis, [(i, i ^ step) for i in range(count)])  13.5 us
    unnamed x12, local copies, waits for them, and re-layouts  1.84 us
    pallas_call x1, Pallas kernels, per_device(): call(functools.partial(scatter_kernel, out_places), [jax.ShapeDtypeStruct...  1.4 us
    pallas_call x1, Pallas kernels, per_device(): call(functools.partial(density_kernel, places), jax.ShapeDtypeStruct((bat...  1.07 us
    dynamic_slice x1, local copies, waits for them, and re-layouts, per_device(): mine = lax.dynamic_slice_in_dim(density_blocks, half * wide, wide, 1)  0.88 us
    pallas_call x1, Pallas kernels, per_device(): call(prepare_kernel, (jax.ShapeDtypeStruct((batches, points, kept), bf16)...  0.76 us
  transfers between devices with their start and end apart: 15, of which 8 were waited for; matrix products, arithmetic and copies ran while one was open for 3% of the time, Pallas kernels for 3%

profile of v19, /device:TPU:0, one launch (start us, length us, event | category | flops | bytes accessed | tf_op | source)
XLA Modules:
  0.0 36.4 jit_solution(5566247545818687003)
XLA Ops:
  0.0 2.9 %collective-permute-start.1 = (bf16[16,4096]{1,0:T(8,128)(2,1)}, bf16[16,4096]{1,0:T(8,128)(2,1)S(1)}, u32[]{:S(2)}, u32[]{:S(2)}) collective-permute-start(bf16[16,4096]{1,0:T(8,128)(2,1)} %param.10), channel_id=1, source_target_pairs={{0,2},{2,0},{1,3},{3,1},{4,6},{6,4},{5,7},{7,5},{8,10},{10,8},{9,1... | collective-permute-start | bytes 393224 | tf_op jit(solution)/shard_map/ppermute | solution.py:153
  2.9 0.0 copy-start.5
  2.9 0.9 %constant_dynamic-slice_fusion.1 = bf16[16,2048]{1,0:T(8,128)(2,1)S(1)} fusion(bf16[16,4096]{1,0:T(8,128)(2,1)} %param.10, s32[]{:T(128)S(6)} %select_n.4), kind=kLoop, calls=%fused_computation.9 | loop fusion | bytes 131076 | tf_op jit(solution)/shard_map/dynamic_slice | solution.py:181
  3.8 2.6 %collective-permute-start.3 = (bf16[16,2048]{1,0:T(8,128)(2,1)S(1)}, bf16[16,2048]{1,0:T(8,128)(2,1)S(1)}, u32[]{:S(2)}, u32[]{:S(2)}) collective-permute-start(bf16[16,2048]{1,0:T(8,128)(2,1)S(1)} %constant_dynamic-slice_fusion.1), channel_id=1, source_target_pairs={{0,8},{4,12},{8,0},{12,4},{1,9},{5,13},{9,1},{13,5},{2,10},{6,14},... | collective-permute-start | bytes 196616 | tf_op jit(solution)/shard_map/ppermute | solution.py:153
  6.4 1.3 %collective-permute-start = (bf16[16,2048]{1,0:T(8,128)(2,1)S(1)}, bf16[16,2048]{1,0:T(8,128)(2,1)S(1)}, u32[]{:S(2)}, u32[]{:S(2)}) collective-permute-start(bf16[16,2048]{1,0:T(8,128)(2,1)S(1)} %constant_dynamic-slice_fusion.1), channel_id=1, source_target_pairs={{0,12},{4,8},{8,4},{12,0},{1,13},{5,9},{9,5},{13,1},{2,14},{6,10},... | collective-permute-start | bytes 196616 | tf_op jit(solution)/shard_map/ppermute | solution.py:153
  7.8 0.0 copy-done.5
  7.8 0.0 copy-start.4
  7.8 0.1 reshape.16.slots_ref
  7.9 0.6 %copy-done.4 = s32[1,1,8,8]{3,2,1,0:T(8,128)S(1)} copy-done((s32[1,1,8,8]{3,2,1,0:T(8,128)S(1)}, s32[1,1,8,8]{3,2,1,0:T(8,128)}, u32[]{:S(2)}) %copy-start.4) | copy-done | bytes 280
  8.4 0.2 shard_map.64.refs_6_.refs_5_
  8.6 0.0 collective-permute-done.1
  8.7 0.3 collective-permute-start.2
  9.0 0.0 collective-permute-start.4
  9.0 1.1 %collective-permute-done.4.refs_7_.refs_6_ = s32[1,128]{1,0:T(1,128)S(1)} collective-permute-done((s32[1,128]{1,0:T(1,128)S(1)}, s32[1,128]{1,0:T(1,128)S(1)}, u32[]{:S(2)}, u32[]{:S(2)}) %collective-permute-start.4) | collective-permute-done | bytes 544 | tf_op jit(solution)/shard_map/ppermute | solution.py:153
  10.1 0.0 collective-permute-done.3.refs_2_
  10.1 1.1 %collective-permute-start.5 = (bf16[16,2048]{1,0:T(8,128)(2,1)S(1)}, bf16[16,2048]{1,0:T(8,128)(2,1)S(1)}, u32[]{:S(2)}, u32[]{:S(2)}) collective-permute-start(bf16[16,2048]{1,0:T(8,128)(2,1)S(1)} %collective-permute-done.3.refs_2_), channel_id=1, source_target_pairs={{0,2},{2,0},{1,3},{3,1},{4,6},{6,4},{5,7},{7,5},{8,10},{10,8},{9,1... | collective-permute-start | bytes 196616 | tf_op jit(solution)/shard_map/ppermute | solution.py:153
  11.2 2.0 %collective-permute-done.refs_4_ = bf16[16,2048]{1,0:T(8,128)(2,1)S(1)} collective-permute-done((bf16[16,2048]{1,0:T(8,128)(2,1)S(1)}, bf16[16,2048]{1,0:T(8,128)(2,1)S(1)}, u32[]{:S(2)}, u32[]{:S(2)}) %collective-permute-start) | collective-permute-done | bytes 65568 | tf_op jit(solution)/shard_map/ppermute | solution.py:153
  13.2 0.5 %collective-permute-start.6 = (bf16[16,2048]{1,0:T(8,128)(2,1)S(1)}, bf16[16,2048]{1,0:T(8,128)(2,1)S(1)}, u32[]{:S(2)}, u32[]{:S(2)}) collective-permute-start(bf16[16,2048]{1,0:T(8,128)(2,1)S(1)} %collective-permute-done.refs_4_), channel_id=1, source_target_pairs={{0,2},{2,0},{1,3},{3,1},{4,6},{6,4},{5,7},{7,5},{8,10},{10,8},{9,1... | collective-permute-start | bytes 196616 | tf_op jit(solution)/shard_map/ppermute | solution.py:153
  13.7 0.0 copy-start
  13.7 1.2 %copy-done = bf16[4,256,512]{2,1,0:T(8,128)(2,1)S(1)} copy-done((bf16[4,256,512]{2,1,0:T(8,128)(2,1)S(1)}, bf16[4,256,512]{2,1,0:T(8,128)(2,1)}, u32[]{:S(2)}) %copy-start) | copy-done | bytes 1048600
  14.9 0.0 copy-start.1
  14.9 0.8 %shard_map.65 = (bf16[4,256,256]{2,1,0:T(8,128)(2,1)S(1)}, bf16[4,256,256]{2,1,0:T(8,128)(2,1)S(1)}) custom-call(s32[1]{0:T(128)} %bitcast.half_ref.core_ref, bf16[4,256,512]{2,1,0:T(8,128)(2,1)S(1)} %copy-done), custom_call_target="tpu_custom_call" | custom-call | flops 536870912 | bytes 3145728 | tf_op jit(solution)/shard_map/pallas_call | solution.py:201
  15.7 0.0 collective-permute-done.5.refs_3_
  15.7 1.7 %collective-permute-done.6.refs_5_ = bf16[16,2048]{1,0:T(8,128)(2,1)S(1)} collective-permute-done((bf16[16,2048]{1,0:T(8,128)(2,1)S(1)}, bf16[16,2048]{1,0:T(8,128)(2,1)S(1)}, u32[]{:S(2)}, u32[]{:S(2)}) %collective-permute-start.6) | collective-permute-done | bytes 65568 | tf_op jit(solution)/shard_map/ppermute | solution.py:153
  17.4 0.0 collective-permute-done.2.refs_1_
  17.4 0.0 copy-done.1
  17.4 1.1 %shard_map.66.refs_0_ = f32[4,256]{1,0:T(4,128)S(1)} custom-call(s32[1]{0:T(128)} %bitcast.1.place_ref, s32[1]{0:T(128)} %bitcast.half_ref.core_ref, bf16[32,2048]{1,0:T(8,128)(2,1)S(1)} %pad_maximum_fusion.refs_0_, bf16[32,2048]{1,0:T(8,128)(2,1)S(1)} %collective-permute-done.2.refs_1_, bf16[16,2048]{1,0:T(8,128)(2,1)S(1)} %collective-permute-done.3.refs_2_, ...), custom_call_target="tpu_custom_call" | custom-call | flops 268435456 | bytes 2097152 | tf_op jit(solution)/shard_map/pallas_call | solution.py:216
  18.5 0.1 collective-permute-start.7
  18.6 1.2 %collective-permute-done.7.refs_1_ = f32[4,256]{1,0:T(4,128)S(1)} collective-permute-done((f32[4,256]{1,0:T(4,128)S(1)}, f32[4,256]{1,0:T(4,128)S(1)}, u32[]{:S(2)}, u32[]{:S(2)}) %collective-permute-start.7) | collective-permute-done | bytes 4128 | tf_op jit(solution)/shard_map/ppermute | solution.py:153
  19.8 0.0 copy-done.3
  19.8 1.4 %shard_map.67 = (bf16[32,2048]{1,0:T(8,128)(2,1)S(1)}, bf16[32,2048]{1,0:T(8,128)(2,1)S(1)}, bf16[16,2048]{1,0:T(8,128)(2,1)S(1)}, bf16[16,2048]{1,0:T(8,128)(2,...) custom-call(s32[1]{0:T(128)} %bitcast.1.place_ref, s32[1]{0:T(128)} %bitcast.half_ref.core_ref, ...), custom_call_target="tpu_custom_call" | custom-call | flops 268435456 | bytes 2097152 | tf_op jit(solution)/shard_map/pallas_call | solution.py:229
  21.2 0.6 %collective-permute-start.10 = (bf16[16,2048]{1,0:T(8,128)(2,1)S(1)}, bf16[16,2048]{1,0:T(8,128)(2,1)S(1)}, u32[]{:S(2)}, u32[]{:S(2)}) collective-permute-start(bf16[16,2048]{1,0:T(8,128)(2,1)S(1)} %get-tuple-element.28), channel_id=1, source_target_pairs={{0,2},{2,0},{1,3},{3,1},{4,6},{6,4},{5,7},{7,5},{8,10},{10,8},{9,1... | collective-permute-start | bytes 196616 | tf_op jit(solution)/shard_map/ppermute | solution.py:153
  21.8 1.5 %collective-permute-start.12 = (bf16[16,2048]{1,0:T(8,128)(2,1)S(1)}, bf16[16,2048]{1,0:T(8,128)(2,1)S(1)}, u32[]{:S(2)}, u32[]{:S(2)}) collective-permute-start(bf16[16,2048]{1,0:T(8,128)(2,1)S(1)} %get-tuple-element.30), channel_id=1, source_target_pairs={{0,2},{2,0},{1,3},{3,1},{4,6},{6,4},{5,7},{7,5},{8,10},{10,8},{9,1... | collective-permute-start | bytes 196616 | tf_op jit(solution)/shard_map/ppermute | solution.py:153
  23.3 0.1 collective-permute-start.8
  23.4 2.7 %collective-permute-done.10 = bf16[16,2048]{1,0:T(8,128)(2,1)S(1)} collective-permute-done((bf16[16,2048]{1,0:T(8,128)(2,1)S(1)}, bf16[16,2048]{1,0:T(8,128)(2,1)S(1)}, u32[]{:S(2)}, u32[]{:S(2)}) %collective-permute-start.10) | collective-permute-done | bytes 65568 | tf_op jit(solution)/shard_map/ppermute | solution.py:153
  26.1 2.0 %collective-permute-start.11 = (bf16[16,2048]{1,0:T(8,128)(2,1)S(1)}, bf16[16,2048]{1,0:T(8,128)(2,1)S(1)}, u32[]{:S(2)}, u32[]{:S(2)}) collective-permute-start(bf16[16,2048]{1,0:T(8,128)(2,1)S(1)} %add_convert_fusion.1), channel_id=1, source_target_pairs={{0,8},{4,12},{8,0},{12,4},{1,9},{5,13},{9,1},{13,5},{2,10},{6,14},... | collective-permute-start | bytes 196616 | tf_op jit(solution)/shard_map/ppermute | solution.py:153
  28.1 0.0 collective-permute-done.12
  28.1 1.4 %collective-permute-start.13 = (bf16[16,2048]{1,0:T(8,128)(2,1)S(1)}, bf16[16,2048]{1,0:T(8,128)(2,1)S(1)}, u32[]{:S(2)}, u32[]{:S(2)}) collective-permute-start(bf16[16,2048]{1,0:T(8,128)(2,1)S(1)} %add_convert_fusion), channel_id=1, source_target_pairs={{0,12},{4,8},{8,4},{12,0},{1,13},{5,9},{9,5},{13,1},{2,14},{6,10},... | collective-permute-start | bytes 196616 | tf_op jit(solution)/shard_map/ppermute | solution.py:153
  29.5 0.0 collective-permute-done.8
  29.6 0.0 copy-start.2
  29.6 1.3 %collective-permute-start.9 = (bf16[16,2048]{1,0:T(8,128)(2,1)S(1)}, bf16[16,2048]{1,0:T(8,128)(2,1)S(1)}, u32[]{:S(2)}, u32[]{:S(2)}) collective-permute-start(bf16[16,2048]{1,0:T(8,128)(2,1)S(1)} %slice.17), channel_id=1, source_target_pairs={{0,2},{2,0},{1,3},{3,1},{4,6},{6,4},{5,7},{7,5},{8,10},{10,8},{9,1... | collective-permute-start | bytes 196616 | tf_op jit(solution)/shard_map/ppermute | solution.py:153
  30.9 1.6 %collective-permute-done.11 = bf16[16,2048]{1,0:T(8,128)(2,1)S(1)} collective-permute-done((bf16[16,2048]{1,0:T(8,128)(2,1)S(1)}, bf16[16,2048]{1,0:T(8,128)(2,1)S(1)}, u32[]{:S(2)}, u32[]{:S(2)}) %collective-permute-start.11) | collective-permute-done | bytes 65568 | tf_op jit(solution)/shard_map/ppermute | solution.py:153
  32.4 1.8 %collective-permute-done.13 = bf16[16,2048]{1,0:T(8,128)(2,1)S(1)} collective-permute-done((bf16[16,2048]{1,0:T(8,128)(2,1)S(1)}, bf16[16,2048]{1,0:T(8,128)(2,1)S(1)}, u32[]{:S(2)}, u32[]{:S(2)}) %collective-permute-start.13) | collective-permute-done | bytes 65568 | tf_op jit(solution)/shard_map/ppermute | solution.py:153
  34.2 0.0 collective-permute-done.9
  34.3 0.1 collective-permute-start.14
  34.4 1.3 %collective-permute-done.14.other_ref = f32[16,2048]{1,0:T(8,128)S(1)} collective-permute-done((f32[16,2048]{1,0:T(8,128)S(1)}, f32[16,2048]{1,0:T(8,128)S(1)}, u32[]{:S(2)}, u32[]{:S(2)}) %collective-permute-start.14) | collective-permute-done | bytes 131104 | tf_op jit(solution)/shard_map/ppermute | solution.py:153
  35.7 0.0 copy-done.2
  35.7 0.7 %shard_map.68 = f32[16,4096]{1,0:T(8,128)} custom-call(s32[1]{0:T(128)} %bitcast.half_ref.core_ref, f32[16,2048]{1,0:T(8,128)S(1)} %fusion.1.mine_ref, f32[16,2048]{1,0:T(8,128)S(1)} %collective-permute-done.14.other_ref, bf16[16,4096]{1,0:T(8,128)(2,1)S(1)} %copy-done.2), custom_call_target="tpu_custom_call" | custom-call | bytes 786432 | tf_op jit(solution)/shard_map/pallas_call | solution.py:255
  (8 shorter events, 0.1 us)
Async XLA Ops:
  0.0 8.6 %collective-permute-start.1 = (bf16[16,4096]{1,0:T(8,128)(2,1)}, bf16[16,4096]{1,0:T(8,128)(2,1)S(1)}, u32[]{:S(2)}, u32[]{:S(2)}) collective-permute-start(bf16[16,4096]{1,0:T(8,128)(2,1)} %param.10), channel_id=1, source_target_pairs={{0,2},{2,0},{1,3},{3,1},{4,6},{6,4},{5,7},{7,5},{8,10},{10,8},{9,1... | collective-permute-start | bytes 393224 | tf_op jit(solution)/shard_map/ppermute | solution.py:153
  2.9 4.8 %copy-start.5 = (s32[4,8,4]{1,2,0:T(4,128)S(1)}, s32[4,8,4]{1,2,0:T(4,128)}, u32[]{:S(2)}) copy-start(s32[4,8,4]{1,2,0:T(4,128)} %param.8) | copy-start | bytes 1540
  3.8 6.3 %collective-permute-start.3 = (bf16[16,2048]{1,0:T(8,128)(2,1)S(1)}, bf16[16,2048]{1,0:T(8,128)(2,1)S(1)}, u32[]{:S(2)}, u32[]{:S(2)}) collective-permute-start(bf16[16,2048]{1,0:T(8,128)(2,1)S(1)} %constant_dynamic-slice_fusion.1), channel_id=1, source_target_pairs={{0,8},{4,12},{8,0},{12,4},{1,9},{5,13},{9,1},{13,5},{2,10},{6,14},... | collective-permute-start | bytes 196616 | tf_op jit(solution)/shard_map/ppermute | solution.py:153
  6.4 6.8 %collective-permute-start = (bf16[16,2048]{1,0:T(8,128)(2,1)S(1)}, bf16[16,2048]{1,0:T(8,128)(2,1)S(1)}, u32[]{:S(2)}, u32[]{:S(2)}) collective-permute-start(bf16[16,2048]{1,0:T(8,128)(2,1)S(1)} %constant_dynamic-slice_fusion.1), channel_id=1, source_target_pairs={{0,12},{4,8},{8,4},{12,0},{1,13},{5,9},{9,5},{13,1},{2,14},{6,10},... | collective-permute-start | bytes 196616 | tf_op jit(solution)/shard_map/ppermute | solution.py:153
  7.8 0.7 %copy-start.4 = (s32[1,1,8,8]{3,2,1,0:T(8,128)S(1)}, s32[1,1,8,8]{3,2,1,0:T(8,128)}, u32[]{:S(2)}) copy-start(s32[1,1,8,8]{3,2,1,0:T(8,128)} %param.9) | copy-start | bytes 772
  8.7 8.8 %collective-permute-start.2 = (bf16[32,2048]{1,0:T(8,128)(2,1)S(1)}, bf16[32,2048]{1,0:T(8,128)(2,1)S(1)}, u32[]{:S(2)}, u32[]{:S(2)}) collective-permute-start(bf16[32,2048]{1,0:T(8,128)(2,1)S(1)} %pad_maximum_fusion.refs_0_), channel_id=1, source_target_pairs={{0,4},{4,0},{8,12},{12,8},{1,5},{5,1},{9,13},{13,9},{2,6},{6,2},{1... | collective-permute-start | bytes 393224 | tf_op jit(solution)/shard_map/ppermute | solution.py:153
  9.0 1.1 %collective-permute-start.4 = (s32[1,128]{1,0:T(1,128)S(1)}, s32[1,128]{1,0:T(1,128)S(1)}, u32[]{:S(2)}, u32[]{:S(2)}) collective-permute-start(s32[1,128]{1,0:T(1,128)S(1)} %shard_map.64.refs_6_.refs_5_), channel_id=1, source_target_pairs={{0,1},{1,0},{2,3},{3,2},{4,5},{5,4},{6,7},{7,6},{8,9},{9,8},{10,11... | collective-permute-start | bytes 1544 | tf_op jit(solution)/shard_map/ppermute | solution.py:153
  10.1 5.6 %collective-permute-start.5 = (bf16[16,2048]{1,0:T(8,128)(2,1)S(1)}, bf16[16,2048]{1,0:T(8,128)(2,1)S(1)}, u32[]{:S(2)}, u32[]{:S(2)}) collective-permute-start(bf16[16,2048]{1,0:T(8,128)(2,1)S(1)} %collective-permute-done.3.refs_2_), channel_id=1, source_target_pairs={{0,2},{2,0},{1,3},{3,1},{4,6},{6,4},{5,7},{7,5},{8,10},{10,8},{9,1... | collective-permute-start | bytes 196616 | tf_op jit(solution)/shard_map/ppermute | solution.py:153
  13.2 4.3 %collective-permute-start.6 = (bf16[16,2048]{1,0:T(8,128)(2,1)S(1)}, bf16[16,2048]{1,0:T(8,128)(2,1)S(1)}, u32[]{:S(2)}, u32[]{:S(2)}) collective-permute-start(bf16[16,2048]{1,0:T(8,128)(2,1)S(1)} %collective-permute-done.refs_4_), channel_id=1, source_target_pairs={{0,2},{2,0},{1,3},{3,1},{4,6},{6,4},{5,7},{7,5},{8,10},{10,8},{9,1... | collective-permute-start | bytes 196616 | tf_op jit(solution)/shard_map/ppermute | solution.py:153
  13.7 1.2 %copy-start = (bf16[4,256,512]{2,1,0:T(8,128)(2,1)S(1)}, bf16[4,256,512]{2,1,0:T(8,128)(2,1)}, u32[]{:S(2)}) copy-start(bf16[4,256,512]{2,1,0:T(8,128)(2,1)} %refs_3_.1) | copy-start | bytes 3145732
  14.9 2.5 %copy-start.1 = (bf16[4,256,512]{2,1,0:T(8,128)(2,1)S(1)}, bf16[4,256,512]{2,1,0:T(8,128)(2,1)}, u32[]{:S(2)}) copy-start(bf16[4,256,512]{2,1,0:T(8,128)(2,1)} %refs_3_.1) | copy-start | bytes 3145732
  17.4 2.3 %copy-start.3 = (f32[4,256]{1,0:T(4,128)S(1)}, f32[4,256]{1,0:T(4,128)}, u32[]{:S(2)}) copy-start(f32[4,256]{1,0:T(4,128)} %refs_2_.1) | copy-start | bytes 12292
  18.5 1.2 %collective-permute-start.7 = (f32[4,256]{1,0:T(4,128)S(1)}, f32[4,256]{1,0:T(4,128)S(1)}, u32[]{:S(2)}, u32[]{:S(2)}) collective-permute-start(f32[4,256]{1,0:T(4,128)S(1)} %shard_map.66.refs_0_), channel_id=1, source_target_pairs={{0,1},{1,0},{2,3},{3,2},{4,5},{5,4},{6,7},{7,6},{8,9},{9,8},{10,11... | collective-permute-start | bytes 12296 | tf_op jit(solution)/shard_map/ppermute | solution.py:153
  21.2 4.9 %collective-permute-start.10 = (bf16[16,2048]{1,0:T(8,128)(2,1)S(1)}, bf16[16,2048]{1,0:T(8,128)(2,1)S(1)}, u32[]{:S(2)}, u32[]{:S(2)}) collective-permute-start(bf16[16,2048]{1,0:T(8,128)(2,1)S(1)} %get-tuple-element.28), channel_id=1, source_target_pairs={{0,2},{2,0},{1,3},{3,1},{4,6},{6,4},{5,7},{7,5},{8,10},{10,8},{9,1... | collective-permute-start | bytes 196616 | tf_op jit(solution)/shard_map/ppermute | solution.py:153
  21.8 6.3 %collective-permute-start.12 = (bf16[16,2048]{1,0:T(8,128)(2,1)S(1)}, bf16[16,2048]{1,0:T(8,128)(2,1)S(1)}, u32[]{:S(2)}, u32[]{:S(2)}) collective-permute-start(bf16[16,2048]{1,0:T(8,128)(2,1)S(1)} %get-tuple-element.30), channel_id=1, source_target_pairs={{0,2},{2,0},{1,3},{3,1},{4,6},{6,4},{5,7},{7,5},{8,10},{10,8},{9,1... | collective-permute-start | bytes 196616 | tf_op jit(solution)/shard_map/ppermute | solution.py:153
  23.3 6.3 %collective-permute-start.8 = (bf16[32,2048]{1,0:T(8,128)(2,1)S(1)}, bf16[32,2048]{1,0:T(8,128)(2,1)S(1)}, u32[]{:S(2)}, u32[]{:S(2)}) collective-permute-start(bf16[32,2048]{1,0:T(8,128)(2,1)S(1)} %get-tuple-element.26), channel_id=1, source_target_pairs={{0,4},{4,0},{8,12},{12,8},{1,5},{5,1},{9,13},{13,9},{2,6},{6,2},{1... | collective-permute-start | bytes 393224 | tf_op jit(solution)/shard_map/ppermute | solution.py:153
  26.1 6.3 %collective-permute-start.11 = (bf16[16,2048]{1,0:T(8,128)(2,1)S(1)}, bf16[16,2048]{1,0:T(8,128)(2,1)S(1)}, u32[]{:S(2)}, u32[]{:S(2)}) collective-permute-start(bf16[16,2048]{1,0:T(8,128)(2,1)S(1)} %add_convert_fusion.1), channel_id=1, source_target_pairs={{0,8},{4,12},{8,0},{12,4},{1,9},{5,13},{9,1},{13,5},{2,10},{6,14},... | collective-permute-start | bytes 196616 | tf_op jit(solution)/shard_map/ppermute | solution.py:153
  28.1 6.1 %collective-permute-start.13 = (bf16[16,2048]{1,0:T(8,128)(2,1)S(1)}, bf16[16,2048]{1,0:T(8,128)(2,1)S(1)}, u32[]{:S(2)}, u32[]{:S(2)}) collective-permute-start(bf16[16,2048]{1,0:T(8,128)(2,1)S(1)} %add_convert_fusion), channel_id=1, source_target_pairs={{0,12},{4,8},{8,4},{12,0},{1,13},{5,9},{9,5},{13,1},{2,14},{6,10},... | collective-permute-start | bytes 196616 | tf_op jit(solution)/shard_map/ppermute | solution.py:153
  29.6 6.1 %copy-start.2 = (bf16[16,4096]{1,0:T(8,128)(2,1)S(1)}, bf16[16,4096]{1,0:T(8,128)(2,1)}, u32[]{:S(2)}) copy-start(bf16[16,4096]{1,0:T(8,128)(2,1)} %core_ref.1) | copy-start | bytes 393220
  29.6 4.7 %collective-permute-start.9 = (bf16[16,2048]{1,0:T(8,128)(2,1)S(1)}, bf16[16,2048]{1,0:T(8,128)(2,1)S(1)}, u32[]{:S(2)}, u32[]{:S(2)}) collective-permute-start(bf16[16,2048]{1,0:T(8,128)(2,1)S(1)} %slice.17), channel_id=1, source_target_pairs={{0,2},{2,0},{1,3},{3,1},{4,6},{6,4},{5,7},{7,5},{8,10},{10,8},{9,1... | collective-permute-start | bytes 196616 | tf_op jit(solution)/shard_map/ppermute | solution.py:153
  34.3 1.4 %collective-permute-start.14 = (f32[16,2048]{1,0:T(8,128)S(1)}, f32[16,2048]{1,0:T(8,128)S(1)}, u32[]{:S(2)}, u32[]{:S(2)}) collective-permute-start(f32[16,2048]{1,0:T(8,128)S(1)} %fusion.1.mine_ref), channel_id=1, source_target_pairs={{0,1},{1,0},{2,3},{3,2},{4,5},{5,4},{6,7},{7,6},{8,9},{9,8},{10,11... | collective-permute-start | bytes 393224 | tf_op jit(solution)/shard_map/ppermute | solution.py:153

commit v20 on v19

--- a/solution.py
+++ b/solution.py
@@ -63,7 +63,8 @@
     owners = sum(len(blocks) for blocks in places)
     held = table.shape[0] // owners
     for ref, blocks in zip(piece_refs, places):
-        table[blocks[0] * held:(blocks[-1] + 1) * held, :] = ref[...]
+        for i, k in enumerate(blocks):
+            table[k * held:(k + 1) * held, :] = ref[i * held:(i + 1) * held, :]
     pick = row_table(place_ref, core_ref, own_ref, other_ref, held, owners).T.astype(jnp.bfloat16)
     low = lax.broadcasted_iota(jnp.int32, (1, 1, 1, groups, 128), 4) < GO
     for chunk in range(table.shape[1] // 256):
@@ -180,24 +181,19 @@
 
     mine = lax.dynamic_slice_in_dim(density_blocks, half * wide, wide, 1)
     direct = {dz: swap(mine, "batch", rows_z, dz) for dz in far}
-    beside = [
-        lax.dynamic_slice_in_dim(swap(density_blocks, "pair", rows_x, dx), half * wide, wide, 1) for dx in side
-    ]
+    beside = [swap(mine, "pair", rows_x, dx) for dx in side]
     *beside, own_rows = lax.optimization_barrier((*beside, own_rows))
     cluster = jnp.concatenate([mine, *beside], axis=0)
     arrays, places = [cluster], [list(range(rows_x))]
     for dz in near:
         arrays.append(swap(cluster, "batch", rows_z, dz))
         places.append(list(range(dz * rows_x, (dz + 1) * rows_x)))
-    direct[far[0]], other_rows = lax.optimization_barrier((direct[far[0]], other_rows))
-    for dz in far:
-        arrays.append(direct[dz])
-        places.append([dz * rows_x])
-        for dx in side:
-            arrays.append(swap(direct[dz], "pair", rows_x, dx))
-            places.append([dz * rows_x + dx])
-
-    half_at, _ = lax.optimization_barrier((half.reshape(1).astype(jnp.int32), direct[far[-1]]))
+    middle = jnp.concatenate([direct[dz] for dz in far], axis=0)
+    for dx in [0] + side:
+        arrays.append(middle if dx == 0 else swap(middle, "pair", rows_x, dx))
+        places.append([dz * rows_x + dx for dz in far])
+
+    half_at, _ = lax.optimization_barrier((half.reshape(1).astype(jnp.int32), arrays[len(near)]))
     left, left_t = call(
         prepare_kernel,
         (

time: 36.6 us -> 37.2 us (1.016)
  waiting for transfers between devices: 13.5 us -> 15.6 us
  starting transfers between devices: 15.8 us -> 14.1 us
    ppermute x15 -> x14, waiting for transfers between devices: 13.5 us -> 15.6 us  [swap(): return lax.ppermute(array, axis, [(i, i ^ step) for i in range(count)])]
    ppermute x15 -> x14, starting transfers between devices: 15.8 us -> 14.1 us  [swap(): return lax.ppermute(array, axis, [(i, i ^ step) for i in range(count)])]
    unnamed x12 -> x15, local copies, waits for them, and re-layouts: 1.84 us -> 2.75 us
    dynamic_slice x1, local copies, waits for them, and re-layouts: 0.88 us -> 0.01 us  [per_device(): mine = lax.dynamic_slice_in_dim(density_blocks, half * wide, wide, 1)]
  transfers between devices with their start and end apart: 15 -> 14, of which waited for: 8 -> 8; matrix products, arithmetic and copies ran while one was open for 3% -> 1% of each run, Pallas kernels for 3% -> 3%
where the time goes in v20:
time: 37.2 us; the launch traced here: 37 us
  waiting for transfers between devices  15.6 us (42%)
  starting transfers between devices  14.1 us (38%)
  Pallas kernels  4.15 us (11%)
  local copies, waits for them, and re-layouts  2.86 us (8%)
    ppermute x14, waiting for transfers between devices, swap(): return lax.ppermute(array, axis, [(i, i ^ step) for i in range(count)])  15.6 us
    ppermute x14, starting transfers between devices, swap(): return lax.ppermute(array, axis, [(i, i ^ step) for i in range(count)])  14.1 us
    unnamed x15, local copies, waits for them, and re-layouts  2.75 us
    pallas_call x1, Pallas kernels, per_device(): call(functools.partial(scatter_kernel, out_places), [jax.ShapeDtypeStruct...  1.4 us
    pallas_call x1, Pallas kernels, per_device(): call(functools.partial(density_kernel, places), jax.ShapeDtypeStruct((bat...  1.06 us
    pallas_call x1, Pallas kernels, per_device(): call(prepare_kernel, (jax.ShapeDtypeStruct((batches, points, kept), bf16)...  0.76 us
  transfers between devices with their start and end apart: 14, of which 8 were waited for; matrix products, arithmetic and copies ran while one was open for 1% of the time, Pallas kernels for 3%

profile of v20, /device:TPU:0, one launch (start us, length us, event | category | flops | bytes accessed | tf_op | source)
XLA Modules:
  0.0 37.0 jit_solution(312922113666363155)
XLA Ops:
  0.0 0.0 copy-start
  0.0 0.9 %copy-done = bf16[16,4096]{1,0:T(8,128)(2,1)S(1)} copy-done((bf16[16,4096]{1,0:T(8,128)(2,1)S(1)}, bf16[16,4096]{1,0:T(8,128)(2,1)}, u32[]{:S(2)}) %copy-start) | copy-done | bytes 131096
  0.9 0.0 copy-start.6
  0.9 3.0 %collective-permute-start = (bf16[16,2048]{1,0:T(8,128)(2,1)S(1)}, bf16[16,2048]{1,0:T(8,128)(2,1)S(1)}, u32[]{:S(2)}, u32[]{:S(2)}) collective-permute-start(bf16[16,2048]{1,0:T(8,128)(2,1)S(1)} %constant_dynamic-slice_fusion), channel_id=1, source_target_pairs={{0,2},{2,0},{1,3},{3,1},{4,6},{6,4},{5,7},{7,5},{8,10},{10,8},{9,1... | collective-permute-start | bytes 196616 | tf_op jit(solution)/shard_map/ppermute | solution.py:154
  3.9 3.6 %collective-permute-start.3 = (bf16[16,2048]{1,0:T(8,128)(2,1)S(1)}, bf16[16,2048]{1,0:T(8,128)(2,1)S(1)}, u32[]{:S(2)}, u32[]{:S(2)}) collective-permute-start(bf16[16,2048]{1,0:T(8,128)(2,1)S(1)} %constant_dynamic-slice_fusion), channel_id=1, source_target_pairs={{0,12},{4,8},{8,4},{12,0},{1,13},{5,9},{9,5},{13,1},{2,14},{6,10},... | collective-permute-start | bytes 196616 | tf_op jit(solution)/shard_map/ppermute | solution.py:154
  7.5 0.0 collective-permute-start.2
  7.5 0.0 copy-done.6
  7.5 0.0 copy-start.5
  7.5 0.1 reshape.15.slots_ref
  7.6 0.6 %copy-done.5 = s32[1,1,8,8]{3,2,1,0:T(8,128)S(1)} copy-done((s32[1,1,8,8]{3,2,1,0:T(8,128)S(1)}, s32[1,1,8,8]{3,2,1,0:T(8,128)}, u32[]{:S(2)}) %copy-start.5) | copy-done | bytes 280
  8.2 0.2 shard_map.64.refs_4_.refs_5_
  8.4 0.0 collective-permute-done
  8.4 0.8 %collective-permute-start.1 = (bf16[32,2048]{1,0:T(8,128)(2,1)S(1)}, bf16[32,2048]{1,0:T(8,128)(2,1)S(1)}, u32[]{:S(2)}, u32[]{:S(2)}) collective-permute-start(bf16[32,2048]{1,0:T(8,128)(2,1)S(1)} %pad_maximum_fusion.refs_0_), channel_id=1, source_target_pairs={{0,4},{4,0},{8,12},{12,8},{1,5},{5,1},{9,13},{13,9},{2,6},{6,2},{1... | collective-permute-start | bytes 393224 | tf_op jit(solution)/shard_map/ppermute | solution.py:154
  9.3 3.7 %collective-permute-done.2 = bf16[16,2048]{1,0:T(8,128)(2,1)S(1)} collective-permute-done((bf16[16,2048]{1,0:T(8,128)(2,1)S(1)}, bf16[16,2048]{1,0:T(8,128)(2,1)S(1)}, u32[]{:S(2)}, u32[]{:S(2)}) %collective-permute-start.2) | collective-permute-done | bytes 65568 | tf_op jit(solution)/shard_map/ppermute | solution.py:154
  12.9 0.0 collective-permute-done.3
  13.0 0.6 %collective-permute-start.4 = (bf16[32,2048]{1,0:T(8,128)(2,1)S(1)}, bf16[32,2048]{1,0:T(8,128)(2,1)S(1)}, u32[]{:S(2)}, u32[]{:S(2)}) collective-permute-start(bf16[32,2048]{1,0:T(8,128)(2,1)S(1)} %constant_dynamic-update-slice_fusion.refs_2_), channel_id=1, source_target_pairs={{0,2},{2,0},{1,3},{3,1},{4,6},{6,4},{5,7},{7,5},{8,10},{10,8},{9,1... | collective-permute-start | bytes 393224 | tf_op jit(solution)/shard_map/ppermute | solution.py:154
  13.6 0.0 collective-permute-start.5
  13.6 1.2 %collective-permute-done.1.refs_1_ = bf16[32,2048]{1,0:T(8,128)(2,1)S(1)} collective-permute-done((bf16[32,2048]{1,0:T(8,128)(2,1)S(1)}, bf16[32,2048]{1,0:T(8,128)(2,1)S(1)}, u32[]{:S(2)}, u32[]{:S(2)}) %collective-permute-start.1) | collective-permute-done | bytes 131104 | tf_op jit(solution)/shard_map/ppermute | solution.py:154
  14.8 0.0 copy-start.1
  14.8 1.2 %copy-done.1 = bf16[4,256,512]{2,1,0:T(8,128)(2,1)S(1)} copy-done((bf16[4,256,512]{2,1,0:T(8,128)(2,1)S(1)}, bf16[4,256,512]{2,1,0:T(8,128)(2,1)}, u32[]{:S(2)}) %copy-start.1) | copy-done | bytes 1048600
  16.0 0.0 copy-start.2
  16.0 0.8 %shard_map.65 = (bf16[4,256,256]{2,1,0:T(8,128)(2,1)S(1)}, bf16[4,256,256]{2,1,0:T(8,128)(2,1)S(1)}) custom-call(s32[1]{0:T(128)} %bitcast.half_ref.core_ref, bf16[4,256,512]{2,1,0:T(8,128)(2,1)S(1)} %copy-done.1), custom_call_target="tpu_custom_call" | custom-call | flops 536870912 | bytes 3145728 | tf_op jit(solution)/shard_map/pallas_call | solution.py:197
  16.7 0.0 collective-permute-done.5.refs_5_.refs_6_
  16.8 1.2 %collective-permute-done.4.refs_3_ = bf16[32,2048]{1,0:T(8,128)(2,1)S(1)} collective-permute-done((bf16[32,2048]{1,0:T(8,128)(2,1)S(1)}, bf16[32,2048]{1,0:T(8,128)(2,1)S(1)}, u32[]{:S(2)}, u32[]{:S(2)}) %collective-permute-start.4) | collective-permute-done | bytes 131104 | tf_op jit(solution)/shard_map/ppermute | solution.py:154
  18.0 0.0 copy-done.2
  18.0 0.0 copy-start.4
  18.0 1.1 %shard_map.66.refs_0_ = f32[4,256]{1,0:T(4,128)S(1)} custom-call(s32[1]{0:T(128)} %bitcast.3.place_ref, s32[1]{0:T(128)} %bitcast.half_ref.core_ref, bf16[32,2048]{1,0:T(8,128)(2,1)S(1)} %pad_maximum_fusion.refs_0_, bf16[32,2048]{1,0:T(8,128)(2,1)S(1)} %collective-permute-done.1.refs_1_, bf16[32,2048]{1,0:T(8,128)(2,1)S(1)} %constant_dynamic-update-slice_fusion.refs_2_, ...), custom_call_target="tpu_custom_call" | custom-call | flops 268435456 | bytes 2097152 | tf_op jit(solution)/shard_map/pallas_call | solution.py:212
  19.1 0.1 collective-permute-start.6
  19.1 1.2 %collective-permute-done.6.refs_1_ = f32[4,256]{1,0:T(4,128)S(1)} collective-permute-done((f32[4,256]{1,0:T(4,128)S(1)}, f32[4,256]{1,0:T(4,128)S(1)}, u32[]{:S(2)}, u32[]{:S(2)}) %collective-permute-start.6) | collective-permute-done | bytes 4128 | tf_op jit(solution)/shard_map/ppermute | solution.py:154
  20.3 0.0 copy-done.4
  20.3 1.4 %shard_map.67 = (bf16[32,2048]{1,0:T(8,128)(2,1)S(1)}, bf16[32,2048]{1,0:T(8,128)(2,1)S(1)}, bf16[16,2048]{1,0:T(8,128)(2,1)S(1)}, bf16[16,2048]{1,0:T(8,128)(2,...) custom-call(s32[1]{0:T(128)} %bitcast.3.place_ref, s32[1]{0:T(128)} %bitcast.half_ref.core_ref, ...), custom_call_target="tpu_custom_call" | custom-call | flops 268435456 | bytes 2097152 | tf_op jit(solution)/shard_map/pallas_call | solution.py:225
  21.7 0.6 %collective-permute-start.9 = (bf16[16,2048]{1,0:T(8,128)(2,1)S(1)}, bf16[16,2048]{1,0:T(8,128)(2,1)S(1)}, u32[]{:S(2)}, u32[]{:S(2)}) collective-permute-start(bf16[16,2048]{1,0:T(8,128)(2,1)S(1)} %get-tuple-element.24), channel_id=1, source_target_pairs={{0,2},{2,0},{1,3},{3,1},{4,6},{6,4},{5,7},{7,5},{8,10},{10,8},{9,1... | collective-permute-start | bytes 196616 | tf_op jit(solution)/shard_map/ppermute | solution.py:154
  22.3 1.5 %collective-permute-start.11 = (bf16[16,2048]{1,0:T(8,128)(2,1)S(1)}, bf16[16,2048]{1,0:T(8,128)(2,1)S(1)}, u32[]{:S(2)}, u32[]{:S(2)}) collective-permute-start(bf16[16,2048]{1,0:T(8,128)(2,1)S(1)} %get-tuple-element.26), channel_id=1, source_target_pairs={{0,2},{2,0},{1,3},{3,1},{4,6},{6,4},{5,7},{7,5},{8,10},{10,8},{9,1... | collective-permute-start | bytes 196616 | tf_op jit(solution)/shard_map/ppermute | solution.py:154
  23.8 0.0 collective-permute-start.7
  23.8 2.8 %collective-permute-done.9 = bf16[16,2048]{1,0:T(8,128)(2,1)S(1)} collective-permute-done((bf16[16,2048]{1,0:T(8,128)(2,1)S(1)}, bf16[16,2048]{1,0:T(8,128)(2,1)S(1)}, u32[]{:S(2)}, u32[]{:S(2)}) %collective-permute-start.9) | collective-permute-done | bytes 65568 | tf_op jit(solution)/shard_map/ppermute | solution.py:154
  26.7 1.9 %collective-permute-start.10 = (bf16[16,2048]{1,0:T(8,128)(2,1)S(1)}, bf16[16,2048]{1,0:T(8,128)(2,1)S(1)}, u32[]{:S(2)}, u32[]{:S(2)}) collective-permute-start(bf16[16,2048]{1,0:T(8,128)(2,1)S(1)} %add_convert_fusion.1), channel_id=1, source_target_pairs={{0,8},{4,12},{8,0},{12,4},{1,9},{5,13},{9,1},{13,5},{2,10},{6,14},... | collective-permute-start | bytes 196616 | tf_op jit(solution)/shard_map/ppermute | solution.py:154
  28.6 0.0 collective-permute-done.11
  28.6 1.1 %collective-permute-start.12 = (bf16[16,2048]{1,0:T(8,128)(2,1)S(1)}, bf16[16,2048]{1,0:T(8,128)(2,1)S(1)}, u32[]{:S(2)}, u32[]{:S(2)}) collective-permute-start(bf16[16,2048]{1,0:T(8,128)(2,1)S(1)} %add_convert_fusion), channel_id=1, source_target_pairs={{0,12},{4,8},{8,4},{12,0},{1,13},{5,9},{9,5},{13,1},{2,14},{6,10},... | collective-permute-start | bytes 196616 | tf_op jit(solution)/shard_map/ppermute | solution.py:154
  29.7 0.0 collective-permute-done.7
  29.8 0.0 copy-start.3
  29.8 0.8 %collective-permute-start.8 = (bf16[16,2048]{1,0:T(8,128)(2,1)S(1)}, bf16[16,2048]{1,0:T(8,128)(2,1)S(1)}, u32[]{:S(2)}, u32[]{:S(2)}) collective-permute-start(bf16[16,2048]{1,0:T(8,128)(2,1)S(1)} %slice.17), channel_id=1, source_target_pairs={{0,2},{2,0},{1,3},{3,1},{4,6},{6,4},{5,7},{7,5},{8,10},{10,8},{9,1... | collective-permute-start | bytes 196616 | tf_op jit(solution)/shard_map/ppermute | solution.py:154
  30.6 2.4 %collective-permute-done.10 = bf16[16,2048]{1,0:T(8,128)(2,1)S(1)} collective-permute-done((bf16[16,2048]{1,0:T(8,128)(2,1)S(1)}, bf16[16,2048]{1,0:T(8,128)(2,1)S(1)}, u32[]{:S(2)}, u32[]{:S(2)}) %collective-permute-start.10) | collective-permute-done | bytes 65568 | tf_op jit(solution)/shard_map/ppermute | solution.py:154
  32.9 1.8 %collective-permute-done.12 = bf16[16,2048]{1,0:T(8,128)(2,1)S(1)} collective-permute-done((bf16[16,2048]{1,0:T(8,128)(2,1)S(1)}, bf16[16,2048]{1,0:T(8,128)(2,1)S(1)}, u32[]{:S(2)}, u32[]{:S(2)}) %collective-permute-start.12) | collective-permute-done | bytes 65568 | tf_op jit(solution)/shard_map/ppermute | solution.py:154
  34.8 0.0 collective-permute-done.8
  34.8 0.1 collective-permute-start.13
  34.9 1.3 %collective-permute-done.13.other_ref = f32[16,2048]{1,0:T(8,128)S(1)} collective-permute-done((f32[16,2048]{1,0:T(8,128)S(1)}, f32[16,2048]{1,0:T(8,128)S(1)}, u32[]{:S(2)}, u32[]{:S(2)}) %collective-permute-start.13) | collective-permute-done | bytes 131104 | tf_op jit(solution)/shard_map/ppermute | solution.py:154
  36.2 0.0 copy-done.3
  36.2 0.7 %shard_map.68 = f32[16,4096]{1,0:T(8,128)} custom-call(s32[1]{0:T(128)} %bitcast.half_ref.core_ref, f32[16,2048]{1,0:T(8,128)S(1)} %fusion.1.mine_ref, f32[16,2048]{1,0:T(8,128)S(1)} %collective-permute-done.13.other_ref, bf16[16,4096]{1,0:T(8,128)(2,1)S(1)} %copy-done.3), custom_call_target="tpu_custom_call" | custom-call | bytes 786432 | tf_op jit(solution)/shard_map/pallas_call | solution.py:251
  (9 shorter events, 0.1 us)
Async XLA Ops:
  0.0 0.9 %copy-start = (bf16[16,4096]{1,0:T(8,128)(2,1)S(1)}, bf16[16,4096]{1,0:T(8,128)(2,1)}, u32[]{:S(2)}) copy-start(bf16[16,4096]{1,0:T(8,128)(2,1)} %param.10) | copy-start | bytes 393220
  0.9 6.6 %copy-start.6 = (s32[4,8,4]{1,2,0:T(4,128)S(1)}, s32[4,8,4]{1,2,0:T(4,128)}, u32[]{:S(2)}) copy-start(s32[4,8,4]{1,2,0:T(4,128)} %param.8) | copy-start | bytes 1540
  0.9 7.5 %collective-permute-start = (bf16[16,2048]{1,0:T(8,128)(2,1)S(1)}, bf16[16,2048]{1,0:T(8,128)(2,1)S(1)}, u32[]{:S(2)}, u32[]{:S(2)}) collective-permute-start(bf16[16,2048]{1,0:T(8,128)(2,1)S(1)} %constant_dynamic-slice_fusion), channel_id=1, source_target_pairs={{0,2},{2,0},{1,3},{3,1},{4,6},{6,4},{5,7},{7,5},{8,10},{10,8},{9,1... | collective-permute-start | bytes 196616 | tf_op jit(solution)/shard_map/ppermute | solution.py:154
  3.9 9.0 %collective-permute-start.3 = (bf16[16,2048]{1,0:T(8,128)(2,1)S(1)}, bf16[16,2048]{1,0:T(8,128)(2,1)S(1)}, u32[]{:S(2)}, u32[]{:S(2)}) collective-permute-start(bf16[16,2048]{1,0:T(8,128)(2,1)S(1)} %constant_dynamic-slice_fusion), channel_id=1, source_target_pairs={{0,12},{4,8},{8,4},{12,0},{1,13},{5,9},{9,5},{13,1},{2,14},{6,10},... | collective-permute-start | bytes 196616 | tf_op jit(solution)/shard_map/ppermute | solution.py:154
  7.5 5.4 %collective-permute-start.2 = (bf16[16,2048]{1,0:T(8,128)(2,1)S(1)}, bf16[16,2048]{1,0:T(8,128)(2,1)S(1)}, u32[]{:S(2)}, u32[]{:S(2)}) collective-permute-start(bf16[16,2048]{1,0:T(8,128)(2,1)S(1)} %constant_dynamic-slice_fusion), channel_id=1, source_target_pairs={{0,8},{4,12},{8,0},{12,4},{1,9},{5,13},{9,1},{13,5},{2,10},{6,14},... | collective-permute-start | bytes 196616 | tf_op jit(solution)/shard_map/ppermute | solution.py:154
  7.5 0.7 %copy-start.5 = (s32[1,1,8,8]{3,2,1,0:T(8,128)S(1)}, s32[1,1,8,8]{3,2,1,0:T(8,128)}, u32[]{:S(2)}) copy-start(s32[1,1,8,8]{3,2,1,0:T(8,128)} %param.9) | copy-start | bytes 772
  8.4 6.3 %collective-permute-start.1 = (bf16[32,2048]{1,0:T(8,128)(2,1)S(1)}, bf16[32,2048]{1,0:T(8,128)(2,1)S(1)}, u32[]{:S(2)}, u32[]{:S(2)}) collective-permute-start(bf16[32,2048]{1,0:T(8,128)(2,1)S(1)} %pad_maximum_fusion.refs_0_), channel_id=1, source_target_pairs={{0,4},{4,0},{8,12},{12,8},{1,5},{5,1},{9,13},{13,9},{2,6},{6,2},{1... | collective-permute-start | bytes 393224 | tf_op jit(solution)/shard_map/ppermute | solution.py:154
  13.0 5.0 %collective-permute-start.4 = (bf16[32,2048]{1,0:T(8,128)(2,1)S(1)}, bf16[32,2048]{1,0:T(8,128)(2,1)S(1)}, u32[]{:S(2)}, u32[]{:S(2)}) collective-permute-start(bf16[32,2048]{1,0:T(8,128)(2,1)S(1)} %constant_dynamic-update-slice_fusion.refs_2_), channel_id=1, source_target_pairs={{0,2},{2,0},{1,3},{3,1},{4,6},{6,4},{5,7},{7,5},{8,10},{10,8},{9,1... | collective-permute-start | bytes 393224 | tf_op jit(solution)/shard_map/ppermute | solution.py:154
  13.6 3.2 %collective-permute-start.5 = (s32[1,128]{1,0:T(1,128)S(1)}, s32[1,128]{1,0:T(1,128)S(1)}, u32[]{:S(2)}, u32[]{:S(2)}) collective-permute-start(s32[1,128]{1,0:T(1,128)S(1)} %shard_map.64.refs_4_.refs_5_), channel_id=1, source_target_pairs={{0,1},{1,0},{2,3},{3,2},{4,5},{5,4},{6,7},{7,6},{8,9},{9,8},{10,11... | collective-permute-start | bytes 1544 | tf_op jit(solution)/shard_map/ppermute | solution.py:154
  14.8 1.2 %copy-start.1 = (bf16[4,256,512]{2,1,0:T(8,128)(2,1)S(1)}, bf16[4,256,512]{2,1,0:T(8,128)(2,1)}, u32[]{:S(2)}) copy-start(bf16[4,256,512]{2,1,0:T(8,128)(2,1)} %refs_3_.1) | copy-start | bytes 3145732
  16.0 2.0 %copy-start.2 = (bf16[4,256,512]{2,1,0:T(8,128)(2,1)S(1)}, bf16[4,256,512]{2,1,0:T(8,128)(2,1)}, u32[]{:S(2)}) copy-start(bf16[4,256,512]{2,1,0:T(8,128)(2,1)} %refs_3_.1) | copy-start | bytes 3145732
  18.0 2.3 %copy-start.4 = (f32[4,256]{1,0:T(4,128)S(1)}, f32[4,256]{1,0:T(4,128)}, u32[]{:S(2)}) copy-start(f32[4,256]{1,0:T(4,128)} %refs_2_.1) | copy-start | bytes 12292
  19.1 1.2 %collective-permute-start.6 = (f32[4,256]{1,0:T(4,128)S(1)}, f32[4,256]{1,0:T(4,128)S(1)}, u32[]{:S(2)}, u32[]{:S(2)}) collective-permute-start(f32[4,256]{1,0:T(4,128)S(1)} %shard_map.66.refs_0_), channel_id=1, source_target_pairs={{0,1},{1,0},{2,3},{3,2},{4,5},{5,4},{6,7},{7,6},{8,9},{9,8},{10,11... | collective-permute-start | bytes 12296 | tf_op jit(solution)/shard_map/ppermute | solution.py:154
  21.7 4.9 %collective-permute-start.9 = (bf16[16,2048]{1,0:T(8,128)(2,1)S(1)}, bf16[16,2048]{1,0:T(8,128)(2,1)S(1)}, u32[]{:S(2)}, u32[]{:S(2)}) collective-permute-start(bf16[16,2048]{1,0:T(8,128)(2,1)S(1)} %get-tuple-element.24), channel_id=1, source_target_pairs={{0,2},{2,0},{1,3},{3,1},{4,6},{6,4},{5,7},{7,5},{8,10},{10,8},{9,1... | collective-permute-start | bytes 196616 | tf_op jit(solution)/shard_map/ppermute | solution.py:154
  22.3 6.3 %collective-permute-start.11 = (bf16[16,2048]{1,0:T(8,128)(2,1)S(1)}, bf16[16,2048]{1,0:T(8,128)(2,1)S(1)}, u32[]{:S(2)}, u32[]{:S(2)}) collective-permute-start(bf16[16,2048]{1,0:T(8,128)(2,1)S(1)} %get-tuple-element.26), channel_id=1, source_target_pairs={{0,2},{2,0},{1,3},{3,1},{4,6},{6,4},{5,7},{7,5},{8,10},{10,8},{9,1... | collective-permute-start | bytes 196616 | tf_op jit(solution)/shard_map/ppermute | solution.py:154
  23.8 5.9 %collective-permute-start.7 = (bf16[32,2048]{1,0:T(8,128)(2,1)S(1)}, bf16[32,2048]{1,0:T(8,128)(2,1)S(1)}, u32[]{:S(2)}, u32[]{:S(2)}) collective-permute-start(bf16[32,2048]{1,0:T(8,128)(2,1)S(1)} %get-tuple-element.22), channel_id=1, source_target_pairs={{0,4},{4,0},{8,12},{12,8},{1,5},{5,1},{9,13},{13,9},{2,6},{6,2},{1... | collective-permute-start | bytes 393224 | tf_op jit(solution)/shard_map/ppermute | solution.py:154
  26.7 6.3 %collective-permute-start.10 = (bf16[16,2048]{1,0:T(8,128)(2,1)S(1)}, bf16[16,2048]{1,0:T(8,128)(2,1)S(1)}, u32[]{:S(2)}, u32[]{:S(2)}) collective-permute-start(bf16[16,2048]{1,0:T(8,128)(2,1)S(1)} %add_convert_fusion.1), channel_id=1, source_target_pairs={{0,8},{4,12},{8,0},{12,4},{1,9},{5,13},{9,1},{13,5},{2,10},{6,14},... | collective-permute-start | bytes 196616 | tf_op jit(solution)/shard_map/ppermute | solution.py:154
  28.6 6.1 %collective-permute-start.12 = (bf16[16,2048]{1,0:T(8,128)(2,1)S(1)}, bf16[16,2048]{1,0:T(8,128)(2,1)S(1)}, u32[]{:S(2)}, u32[]{:S(2)}) collective-permute-start(bf16[16,2048]{1,0:T(8,128)(2,1)S(1)} %add_convert_fusion), channel_id=1, source_target_pairs={{0,12},{4,8},{8,4},{12,0},{1,13},{5,9},{9,5},{13,1},{2,14},{6,10},... | collective-permute-start | bytes 196616 | tf_op jit(solution)/shard_map/ppermute | solution.py:154
  29.8 6.5 %copy-start.3 = (bf16[16,4096]{1,0:T(8,128)(2,1)S(1)}, bf16[16,4096]{1,0:T(8,128)(2,1)}, u32[]{:S(2)}) copy-start(bf16[16,4096]{1,0:T(8,128)(2,1)} %core_ref.1) | copy-start | bytes 393220
  29.8 5.0 %collective-permute-start.8 = (bf16[16,2048]{1,0:T(8,128)(2,1)S(1)}, bf16[16,2048]{1,0:T(8,128)(2,1)S(1)}, u32[]{:S(2)}, u32[]{:S(2)}) collective-permute-start(bf16[16,2048]{1,0:T(8,128)(2,1)S(1)} %slice.17), channel_id=1, source_target_pairs={{0,2},{2,0},{1,3},{3,1},{4,6},{6,4},{5,7},{7,5},{8,10},{10,8},{9,1... | collective-permute-start | bytes 196616 | tf_op jit(solution)/shard_map/ppermute | solution.py:154
  34.8 1.4 %collective-permute-start.13 = (f32[16,2048]{1,0:T(8,128)S(1)}, f32[16,2048]{1,0:T(8,128)S(1)}, u32[]{:S(2)}, u32[]{:S(2)}) collective-permute-start(f32[16,2048]{1,0:T(8,128)S(1)} %fusion.1.mine_ref), channel_id=1, source_target_pairs={{0,1},{1,0},{2,3},{3,2},{4,5},{5,4},{6,7},{7,6},{8,9},{9,8},{10,11... | collective-permute-start | bytes 393224 | tf_op jit(solution)/shard_map/ppermute | solution.py:154

commit v21 on v19

--- a/solution.py
+++ b/solution.py
@@ -126,12 +126,21 @@
             ref[at * held:(at + 1) * held, :] = total[i * held:(i + 1) * held, :].astype(jnp.bfloat16)
 
 
-def finish_kernel(half_ref, mine_ref, other_ref, core_ref, out_ref):
+def finish_kernel(half_ref, mine_ref, other_ref, core_ref, out_hbm, total, sent):
     wide = mine_ref.shape[1]
-    own = pl.multiple_of(half_ref[0] * wide, wide)
-    far = pl.multiple_of((1 - half_ref[0]) * wide, wide)
-    out_ref[:, pl.ds(own, wide)] = core_ref[:, pl.ds(own, wide)].astype(jnp.float32) + mine_ref[...]
-    out_ref[:, pl.ds(far, wide)] = core_ref[:, pl.ds(far, wide)].astype(jnp.float32) + other_ref[...]
+    size = wide // 2
+    own = half_ref[0] * wide
+    far = (1 - half_ref[0]) * wide
+    copies = []
+    for first, term_ref in ((own, mine_ref), (far, other_ref)):
+        for i in range(2):
+            lanes = pl.ds(pl.multiple_of(first + i * size, size), size)
+            total[:, lanes] = core_ref[:, lanes].astype(jnp.float32) + term_ref[:, i * size:(i + 1) * size]
+            copy = pltpu.make_async_copy(total.at[:, lanes], out_hbm.at[:, lanes], sent.at[len(copies)])
+            copy.start()
+            copies.append(copy)
+    for copy in copies:
+        copy.wait()
 
 
 def call(kernel, outs, count, scratch=(), scalars=0, flops=0, moved=0):
@@ -180,9 +189,7 @@
 
     mine = lax.dynamic_slice_in_dim(density_blocks, half * wide, wide, 1)
     direct = {dz: swap(mine, "batch", rows_z, dz) for dz in far}
-    beside = [
-        lax.dynamic_slice_in_dim(swap(density_blocks, "pair", rows_x, dx), half * wide, wide, 1) for dx in side
-    ]
+    beside = [swap(mine, "pair", rows_x, dx) for dx in side]
     *beside, own_rows = lax.optimization_barrier((*beside, own_rows))
     cluster = jnp.concatenate([mine, *beside], axis=0)
     arrays, places = [cluster], [list(range(rows_x))]
@@ -252,8 +259,14 @@
     for term in landed:
         total = total + term
     total_other = swap(total, "orb", 2, 1)
-    return call(
-        finish_kernel, jax.ShapeDtypeStruct((held, square), f32), 3, scalars=1, moved=held * square * 12
+    return pl.pallas_call(
+        finish_kernel,
+        out_shape=jax.ShapeDtypeStruct((held, square), f32),
+        in_specs=[pl.BlockSpec(memory_space=pltpu.SMEM)] + [pl.BlockSpec(memory_space=pltpu.VMEM)] * 3,
+        out_specs=pl.BlockSpec(memory_space=pl.ANY),
+        scratch_shapes=[pltpu.VMEM((held, square), f32), pltpu.SemaphoreType.DMA((4,))],
+        compiler_params=pltpu.CompilerParams(vmem_limit_bytes=VMEM_LIMIT),
+        cost_estimate=pl.CostEstimate(flops=0, bytes_accessed=held * square * 12, transcendentals=0),
     )(half_at, total, total_other, core_blocks)
 
 

time: 36.6 us -> 36.7 us (level)
    unnamed x12 -> x14, local copies, waits for them, and re-layouts: 1.84 us -> 2.74 us
    dynamic_slice x1, local copies, waits for them, and re-layouts: 0.88 us -> 0.01 us  [per_device(): mine = lax.dynamic_slice_in_dim(density_blocks, half * wide, wide, 1)]
  transfers between devices with their start and end apart: 15 -> 15, of which waited for: 8 -> 8; matrix products, arithmetic and copies ran while one was open for 3% -> 0% of each run, Pallas kernels for 3% -> 3%
where the time goes in v21:
time: 36.7 us; the launch traced here: 36.5 us
  starting transfers between devices  15.5 us (42%)
  waiting for transfers between devices  13.8 us (38%)
  Pallas kernels  4.17 us (11%)
  local copies, waits for them, and re-layouts  2.84 us (8%)
    ppermute x15, starting transfers between devices, swap(): return lax.ppermute(array, axis, [(i, i ^ step) for i in range(count)])  15.5 us
    ppermute x15, waiting for transfers between devices, swap(): return lax.ppermute(array, axis, [(i, i ^ step) for i in range(count)])  13.8 us
    unnamed x14, local copies, waits for them, and re-layouts  2.74 us
    pallas_call x1, Pallas kernels, per_device(): call(functools.partial(scatter_kernel, out_places), [jax.ShapeDtypeStruct...  1.4 us
    pallas_call x1, Pallas kernels, per_device(): call(functools.partial(density_kernel, places), jax.ShapeDtypeStruct((bat...  1.07 us
    pallas_call x1, Pallas kernels, per_device(): call(prepare_kernel, (jax.ShapeDtypeStruct((batches, points, kept), bf16)...  0.76 us
    pallas_call x1, Pallas kernels, per_device(): pl.pallas_call(finish_kernel, out_shape=jax.ShapeDtypeStruct((held, squar...  0.75 us
  transfers between devices with their start and end apart: 15, of which 8 were waited for; matrix products, arithmetic and copies ran while one was open for 0% of the time, Pallas kernels for 3%

profile of v21, /device:TPU:0, one launch (start us, length us, event | category | flops | bytes accessed | tf_op | source)
XLA Modules:
  0.0 36.5 jit_solution(6745572369894542457)
XLA Ops:
  0.0 0.0 copy-start
  0.0 0.9 %copy-done = bf16[16,4096]{1,0:T(8,128)(2,1)S(1)} copy-done((bf16[16,4096]{1,0:T(8,128)(2,1)S(1)}, bf16[16,4096]{1,0:T(8,128)(2,1)}, u32[]{:S(2)}) %copy-start) | copy-done | bytes 131096
  0.9 0.0 copy-start.6
  0.9 3.0 %collective-permute-start.1 = (bf16[16,2048]{1,0:T(8,128)(2,1)S(1)}, bf16[16,2048]{1,0:T(8,128)(2,1)S(1)}, u32[]{:S(2)}, u32[]{:S(2)}) collective-permute-start(bf16[16,2048]{1,0:T(8,128)(2,1)S(1)} %constant_dynamic-slice_fusion), channel_id=1, source_target_pairs={{0,2},{2,0},{1,3},{3,1},{4,6},{6,4},{5,7},{7,5},{8,10},{10,8},{9,1... | collective-permute-start | bytes 196616 | tf_op jit(solution)/shard_map/ppermute | solution.py:162
  3.9 2.6 %collective-permute-start.3 = (bf16[16,2048]{1,0:T(8,128)(2,1)S(1)}, bf16[16,2048]{1,0:T(8,128)(2,1)S(1)}, u32[]{:S(2)}, u32[]{:S(2)}) collective-permute-start(bf16[16,2048]{1,0:T(8,128)(2,1)S(1)} %constant_dynamic-slice_fusion), channel_id=1, source_target_pairs={{0,8},{4,12},{8,0},{12,4},{1,9},{5,13},{9,1},{13,5},{2,10},{6,14},... | collective-permute-start | bytes 196616 | tf_op jit(solution)/shard_map/ppermute | solution.py:162
  6.5 1.3 %collective-permute-start = (bf16[16,2048]{1,0:T(8,128)(2,1)S(1)}, bf16[16,2048]{1,0:T(8,128)(2,1)S(1)}, u32[]{:S(2)}, u32[]{:S(2)}) collective-permute-start(bf16[16,2048]{1,0:T(8,128)(2,1)S(1)} %constant_dynamic-slice_fusion), channel_id=1, source_target_pairs={{0,12},{4,8},{8,4},{12,0},{1,13},{5,9},{9,5},{13,1},{2,14},{6,10},... | collective-permute-start | bytes 196616 | tf_op jit(solution)/shard_map/ppermute | solution.py:162
  7.9 0.0 copy-done.6
  7.9 0.0 copy-start.5
  7.9 0.1 reshape.16.slots_ref
  7.9 0.6 %copy-done.5 = s32[1,1,8,8]{3,2,1,0:T(8,128)S(1)} copy-done((s32[1,1,8,8]{3,2,1,0:T(8,128)S(1)}, s32[1,1,8,8]{3,2,1,0:T(8,128)}, u32[]{:S(2)}) %copy-start.5) | copy-done | bytes 280
  8.5 0.2 shard_map.64.refs_6_.refs_5_
  8.7 0.0 collective-permute-done.1
  8.8 0.3 collective-permute-start.2
  9.1 0.0 collective-permute-start.4
  9.1 1.1 %collective-permute-done.4.refs_7_.refs_6_ = s32[1,128]{1,0:T(1,128)S(1)} collective-permute-done((s32[1,128]{1,0:T(1,128)S(1)}, s32[1,128]{1,0:T(1,128)S(1)}, u32[]{:S(2)}, u32[]{:S(2)}) %collective-permute-start.4) | collective-permute-done | bytes 544 | tf_op jit(solution)/shard_map/ppermute | solution.py:162
  10.2 0.0 collective-permute-done.3.refs_2_
  10.2 0.8 %collective-permute-start.5 = (bf16[16,2048]{1,0:T(8,128)(2,1)S(1)}, bf16[16,2048]{1,0:T(8,128)(2,1)S(1)}, u32[]{:S(2)}, u32[]{:S(2)}) collective-permute-start(bf16[16,2048]{1,0:T(8,128)(2,1)S(1)} %collective-permute-done.3.refs_2_), channel_id=1, source_target_pairs={{0,2},{2,0},{1,3},{3,1},{4,6},{6,4},{5,7},{7,5},{8,10},{10,8},{9,1... | collective-permute-start | bytes 196616 | tf_op jit(solution)/shard_map/ppermute | solution.py:162
  11.0 2.3 %collective-permute-done.refs_4_ = bf16[16,2048]{1,0:T(8,128)(2,1)S(1)} collective-permute-done((bf16[16,2048]{1,0:T(8,128)(2,1)S(1)}, bf16[16,2048]{1,0:T(8,128)(2,1)S(1)}, u32[]{:S(2)}, u32[]{:S(2)}) %collective-permute-start) | collective-permute-done | bytes 65568 | tf_op jit(solution)/shard_map/ppermute | solution.py:162
  13.3 0.5 %collective-permute-start.6 = (bf16[16,2048]{1,0:T(8,128)(2,1)S(1)}, bf16[16,2048]{1,0:T(8,128)(2,1)S(1)}, u32[]{:S(2)}, u32[]{:S(2)}) collective-permute-start(bf16[16,2048]{1,0:T(8,128)(2,1)S(1)} %collective-permute-done.refs_4_), channel_id=1, source_target_pairs={{0,2},{2,0},{1,3},{3,1},{4,6},{6,4},{5,7},{7,5},{8,10},{10,8},{9,1... | collective-permute-start | bytes 196616 | tf_op jit(solution)/shard_map/ppermute | solution.py:162
  13.8 1.2 %copy-done.1 = bf16[4,256,512]{2,1,0:T(8,128)(2,1)S(1)} copy-done((bf16[4,256,512]{2,1,0:T(8,128)(2,1)S(1)}, bf16[4,256,512]{2,1,0:T(8,128)(2,1)}, u32[]{:S(2)}) %copy-start.1) | copy-done | bytes 1048600
  15.0 0.0 copy-start.2
  15.0 0.8 %shard_map.65 = (bf16[4,256,256]{2,1,0:T(8,128)(2,1)S(1)}, bf16[4,256,256]{2,1,0:T(8,128)(2,1)S(1)}) custom-call(s32[1]{0:T(128)} %bitcast.half_ref.core_ref, bf16[4,256,512]{2,1,0:T(8,128)(2,1)S(1)} %copy-done.1), custom_call_target="tpu_custom_call" | custom-call | flops 536870912 | bytes 3145728 | tf_op jit(solution)/shard_map/pallas_call | solution.py:208
  15.8 0.0 collective-permute-done.5.refs_3_
  15.8 1.7 %collective-permute-done.6.refs_5_ = bf16[16,2048]{1,0:T(8,128)(2,1)S(1)} collective-permute-done((bf16[16,2048]{1,0:T(8,128)(2,1)S(1)}, bf16[16,2048]{1,0:T(8,128)(2,1)S(1)}, u32[]{:S(2)}, u32[]{:S(2)}) %collective-permute-start.6) | collective-permute-done | bytes 65568 | tf_op jit(solution)/shard_map/ppermute | solution.py:162
  17.5 0.0 collective-permute-done.2.refs_1_
  17.5 0.0 copy-done.2
  17.5 1.1 %shard_map.66.refs_0_ = f32[4,256]{1,0:T(4,128)S(1)} custom-call(s32[1]{0:T(128)} %bitcast.1.place_ref, s32[1]{0:T(128)} %bitcast.half_ref.core_ref, bf16[32,2048]{1,0:T(8,128)(2,1)S(1)} %pad_maximum_fusion.refs_0_, bf16[32,2048]{1,0:T(8,128)(2,1)S(1)} %collective-permute-done.2.refs_1_, bf16[16,2048]{1,0:T(8,128)(2,1)S(1)} %collective-permute-done.3.refs_2_, ...), custom_call_target="tpu_custom_call" | custom-call | flops 268435456 | bytes 2097152 | tf_op jit(solution)/shard_map/pallas_call | solution.py:223
  18.6 0.1 collective-permute-start.7
  18.7 1.2 %collective-permute-done.7.refs_1_ = f32[4,256]{1,0:T(4,128)S(1)} collective-permute-done((f32[4,256]{1,0:T(4,128)S(1)}, f32[4,256]{1,0:T(4,128)S(1)}, u32[]{:S(2)}, u32[]{:S(2)}) %collective-permute-start.7) | collective-permute-done | bytes 4128 | tf_op jit(solution)/shard_map/ppermute | solution.py:162
  19.8 0.0 copy-done.4
  19.8 1.4 %shard_map.67 = (bf16[32,2048]{1,0:T(8,128)(2,1)S(1)}, bf16[32,2048]{1,0:T(8,128)(2,1)S(1)}, bf16[16,2048]{1,0:T(8,128)(2,1)S(1)}, bf16[16,2048]{1,0:T(8,128)(2,...) custom-call(s32[1]{0:T(128)} %bitcast.1.place_ref, s32[1]{0:T(128)} %bitcast.half_ref.core_ref, ...), custom_call_target="tpu_custom_call" | custom-call | flops 268435456 | bytes 2097152 | tf_op jit(solution)/shard_map/pallas_call | solution.py:236
  21.3 0.6 %collective-permute-start.10 = (bf16[16,2048]{1,0:T(8,128)(2,1)S(1)}, bf16[16,2048]{1,0:T(8,128)(2,1)S(1)}, u32[]{:S(2)}, u32[]{:S(2)}) collective-permute-start(bf16[16,2048]{1,0:T(8,128)(2,1)S(1)} %get-tuple-element.28), channel_id=1, source_target_pairs={{0,2},{2,0},{1,3},{3,1},{4,6},{6,4},{5,7},{7,5},{8,10},{10,8},{9,1... | collective-permute-start | bytes 196616 | tf_op jit(solution)/shard_map/ppermute | solution.py:162
  21.9 1.5 %collective-permute-start.12 = (bf16[16,2048]{1,0:T(8,128)(2,1)S(1)}, bf16[16,2048]{1,0:T(8,128)(2,1)S(1)}, u32[]{:S(2)}, u32[]{:S(2)}) collective-permute-start(bf16[16,2048]{1,0:T(8,128)(2,1)S(1)} %get-tuple-element.30), channel_id=1, source_target_pairs={{0,2},{2,0},{1,3},{3,1},{4,6},{6,4},{5,7},{7,5},{8,10},{10,8},{9,1... | collective-permute-start | bytes 196616 | tf_op jit(solution)/shard_map/ppermute | solution.py:162
  23.3 0.1 collective-permute-start.8
  23.5 2.7 %collective-permute-done.10 = bf16[16,2048]{1,0:T(8,128)(2,1)S(1)} collective-permute-done((bf16[16,2048]{1,0:T(8,128)(2,1)S(1)}, bf16[16,2048]{1,0:T(8,128)(2,1)S(1)}, u32[]{:S(2)}, u32[]{:S(2)}) %collective-permute-start.10) | collective-permute-done | bytes 65568 | tf_op jit(solution)/shard_map/ppermute | solution.py:162
  26.2 2.0 %collective-permute-start.11 = (bf16[16,2048]{1,0:T(8,128)(2,1)S(1)}, bf16[16,2048]{1,0:T(8,128)(2,1)S(1)}, u32[]{:S(2)}, u32[]{:S(2)}) collective-permute-start(bf16[16,2048]{1,0:T(8,128)(2,1)S(1)} %add_convert_fusion.1), channel_id=1, source_target_pairs={{0,8},{4,12},{8,0},{12,4},{1,9},{5,13},{9,1},{13,5},{2,10},{6,14},... | collective-permute-start | bytes 196616 | tf_op jit(solution)/shard_map/ppermute | solution.py:162
  28.2 0.0 collective-permute-done.12
  28.2 1.4 %collective-permute-start.13 = (bf16[16,2048]{1,0:T(8,128)(2,1)S(1)}, bf16[16,2048]{1,0:T(8,128)(2,1)S(1)}, u32[]{:S(2)}, u32[]{:S(2)}) collective-permute-start(bf16[16,2048]{1,0:T(8,128)(2,1)S(1)} %add_convert_fusion), channel_id=1, source_target_pairs={{0,12},{4,8},{8,4},{12,0},{1,13},{5,9},{9,5},{13,1},{2,14},{6,10},... | collective-permute-start | bytes 196616 | tf_op jit(solution)/shard_map/ppermute | solution.py:162
  29.6 0.0 collective-permute-done.8
  29.7 0.0 copy-start.3
  29.7 1.3 %collective-permute-start.9 = (bf16[16,2048]{1,0:T(8,128)(2,1)S(1)}, bf16[16,2048]{1,0:T(8,128)(2,1)S(1)}, u32[]{:S(2)}, u32[]{:S(2)}) collective-permute-start(bf16[16,2048]{1,0:T(8,128)(2,1)S(1)} %slice.17), channel_id=1, source_target_pairs={{0,2},{2,0},{1,3},{3,1},{4,6},{6,4},{5,7},{7,5},{8,10},{10,8},{9,1... | collective-permute-start | bytes 196616 | tf_op jit(solution)/shard_map/ppermute | solution.py:162
  31.0 1.6 %collective-permute-done.11 = bf16[16,2048]{1,0:T(8,128)(2,1)S(1)} collective-permute-done((bf16[16,2048]{1,0:T(8,128)(2,1)S(1)}, bf16[16,2048]{1,0:T(8,128)(2,1)S(1)}, u32[]{:S(2)}, u32[]{:S(2)}) %collective-permute-start.11) | collective-permute-done | bytes 65568 | tf_op jit(solution)/shard_map/ppermute | solution.py:162
  32.5 1.8 %collective-permute-done.13 = bf16[16,2048]{1,0:T(8,128)(2,1)S(1)} collective-permute-done((bf16[16,2048]{1,0:T(8,128)(2,1)S(1)}, bf16[16,2048]{1,0:T(8,128)(2,1)S(1)}, u32[]{:S(2)}, u32[]{:S(2)}) %collective-permute-start.13) | collective-permute-done | bytes 65568 | tf_op jit(solution)/shard_map/ppermute | solution.py:162
  34.3 0.0 collective-permute-done.9
  34.4 0.1 collective-permute-start.14
  34.5 1.3 %collective-permute-done.14.other_ref = f32[16,2048]{1,0:T(8,128)S(1)} collective-permute-done((f32[16,2048]{1,0:T(8,128)S(1)}, f32[16,2048]{1,0:T(8,128)S(1)}, u32[]{:S(2)}, u32[]{:S(2)}) %collective-permute-start.14) | collective-permute-done | bytes 131104 | tf_op jit(solution)/shard_map/ppermute | solution.py:162
  35.8 0.0 copy-done.3
  35.8 0.7 %shard_map.68 = f32[16,4096]{1,0:T(8,128)} custom-call(s32[1]{0:T(128)} %bitcast.half_ref.core_ref, f32[16,2048]{1,0:T(8,128)S(1)} %fusion.1.mine_ref, f32[16,2048]{1,0:T(8,128)S(1)} %collective-permute-done.14.other_ref, bf16[16,4096]{1,0:T(8,128)(2,1)S(1)} %copy-done.3), custom_call_target="tpu_custom_call" | custom-call | bytes 786432 | tf_op jit(solution)/shard_map/pallas_call | solution.py:262
  (9 shorter events, 0.1 us)
Async XLA Ops:
  0.0 0.9 %copy-start = (bf16[16,4096]{1,0:T(8,128)(2,1)S(1)}, bf16[16,4096]{1,0:T(8,128)(2,1)}, u32[]{:S(2)}) copy-start(bf16[16,4096]{1,0:T(8,128)(2,1)} %param.10) | copy-start | bytes 393220
  0.9 6.9 %copy-start.6 = (s32[4,8,4]{1,2,0:T(4,128)S(1)}, s32[4,8,4]{1,2,0:T(4,128)}, u32[]{:S(2)}) copy-start(s32[4,8,4]{1,2,0:T(4,128)} %param.8) | copy-start | bytes 1540
  0.9 7.8 %collective-permute-start.1 = (bf16[16,2048]{1,0:T(8,128)(2,1)S(1)}, bf16[16,2048]{1,0:T(8,128)(2,1)S(1)}, u32[]{:S(2)}, u32[]{:S(2)}) collective-permute-start(bf16[16,2048]{1,0:T(8,128)(2,1)S(1)} %constant_dynamic-slice_fusion), channel_id=1, source_target_pairs={{0,2},{2,0},{1,3},{3,1},{4,6},{6,4},{5,7},{7,5},{8,10},{10,8},{9,1... | collective-permute-start | bytes 196616 | tf_op jit(solution)/shard_map/ppermute | solution.py:162
  3.9 6.3 %collective-permute-start.3 = (bf16[16,2048]{1,0:T(8,128)(2,1)S(1)}, bf16[16,2048]{1,0:T(8,128)(2,1)S(1)}, u32[]{:S(2)}, u32[]{:S(2)}) collective-permute-start(bf16[16,2048]{1,0:T(8,128)(2,1)S(1)} %constant_dynamic-slice_fusion), channel_id=1, source_target_pairs={{0,8},{4,12},{8,0},{12,4},{1,9},{5,13},{9,1},{13,5},{2,10},{6,14},... | collective-permute-start | bytes 196616 | tf_op jit(solution)/shard_map/ppermute | solution.py:162
  6.5 6.8 %collective-permute-start = (bf16[16,2048]{1,0:T(8,128)(2,1)S(1)}, bf16[16,2048]{1,0:T(8,128)(2,1)S(1)}, u32[]{:S(2)}, u32[]{:S(2)}) collective-permute-start(bf16[16,2048]{1,0:T(8,128)(2,1)S(1)} %constant_dynamic-slice_fusion), channel_id=1, source_target_pairs={{0,12},{4,8},{8,4},{12,0},{1,13},{5,9},{9,5},{13,1},{2,14},{6,10},... | collective-permute-start | bytes 196616 | tf_op jit(solution)/shard_map/ppermute | solution.py:162
  7.9 0.7 %copy-start.5 = (s32[1,1,8,8]{3,2,1,0:T(8,128)S(1)}, s32[1,1,8,8]{3,2,1,0:T(8,128)}, u32[]{:S(2)}) copy-start(s32[1,1,8,8]{3,2,1,0:T(8,128)} %param.9) | copy-start | bytes 772
  8.8 8.8 %collective-permute-start.2 = (bf16[32,2048]{1,0:T(8,128)(2,1)S(1)}, bf16[32,2048]{1,0:T(8,128)(2,1)S(1)}, u32[]{:S(2)}, u32[]{:S(2)}) collective-permute-start(bf16[32,2048]{1,0:T(8,128)(2,1)S(1)} %pad_maximum_fusion.refs_0_), channel_id=1, source_target_pairs={{0,4},{4,0},{8,12},{12,8},{1,5},{5,1},{9,13},{13,9},{2,6},{6,2},{1... | collective-permute-start | bytes 393224 | tf_op jit(solution)/shard_map/ppermute | solution.py:162
  9.1 1.1 %collective-permute-start.4 = (s32[1,128]{1,0:T(1,128)S(1)}, s32[1,128]{1,0:T(1,128)S(1)}, u32[]{:S(2)}, u32[]{:S(2)}) collective-permute-start(s32[1,128]{1,0:T(1,128)S(1)} %shard_map.64.refs_6_.refs_5_), channel_id=1, source_target_pairs={{0,1},{1,0},{2,3},{3,2},{4,5},{5,4},{6,7},{7,6},{8,9},{9,8},{10,11... | collective-permute-start | bytes 1544 | tf_op jit(solution)/shard_map/ppermute | solution.py:162
  10.2 5.6 %collective-permute-start.5 = (bf16[16,2048]{1,0:T(8,128)(2,1)S(1)}, bf16[16,2048]{1,0:T(8,128)(2,1)S(1)}, u32[]{:S(2)}, u32[]{:S(2)}) collective-permute-start(bf16[16,2048]{1,0:T(8,128)(2,1)S(1)} %collective-permute-done.3.refs_2_), channel_id=1, source_target_pairs={{0,2},{2,0},{1,3},{3,1},{4,6},{6,4},{5,7},{7,5},{8,10},{10,8},{9,1... | collective-permute-start | bytes 196616 | tf_op jit(solution)/shard_map/ppermute | solution.py:162
  13.3 4.3 %collective-permute-start.6 = (bf16[16,2048]{1,0:T(8,128)(2,1)S(1)}, bf16[16,2048]{1,0:T(8,128)(2,1)S(1)}, u32[]{:S(2)}, u32[]{:S(2)}) collective-permute-start(bf16[16,2048]{1,0:T(8,128)(2,1)S(1)} %collective-permute-done.refs_4_), channel_id=1, source_target_pairs={{0,2},{2,0},{1,3},{3,1},{4,6},{6,4},{5,7},{7,5},{8,10},{10,8},{9,1... | collective-permute-start | bytes 196616 | tf_op jit(solution)/shard_map/ppermute | solution.py:162
  13.8 1.2 %copy-start.1 = (bf16[4,256,512]{2,1,0:T(8,128)(2,1)S(1)}, bf16[4,256,512]{2,1,0:T(8,128)(2,1)}, u32[]{:S(2)}) copy-start(bf16[4,256,512]{2,1,0:T(8,128)(2,1)} %refs_3_.1) | copy-start | bytes 3145732
  15.0 2.5 %copy-start.2 = (bf16[4,256,512]{2,1,0:T(8,128)(2,1)S(1)}, bf16[4,256,512]{2,1,0:T(8,128)(2,1)}, u32[]{:S(2)}) copy-start(bf16[4,256,512]{2,1,0:T(8,128)(2,1)} %refs_3_.1) | copy-start | bytes 3145732
  17.5 2.3 %copy-start.4 = (f32[4,256]{1,0:T(4,128)S(1)}, f32[4,256]{1,0:T(4,128)}, u32[]{:S(2)}) copy-start(f32[4,256]{1,0:T(4,128)} %refs_2_.1) | copy-start | bytes 12292
  18.6 1.2 %collective-permute-start.7 = (f32[4,256]{1,0:T(4,128)S(1)}, f32[4,256]{1,0:T(4,128)S(1)}, u32[]{:S(2)}, u32[]{:S(2)}) collective-permute-start(f32[4,256]{1,0:T(4,128)S(1)} %shard_map.66.refs_0_), channel_id=1, source_target_pairs={{0,1},{1,0},{2,3},{3,2},{4,5},{5,4},{6,7},{7,6},{8,9},{9,8},{10,11... | collective-permute-start | bytes 12296 | tf_op jit(solution)/shard_map/ppermute | solution.py:162
  21.3 4.9 %collective-permute-start.10 = (bf16[16,2048]{1,0:T(8,128)(2,1)S(1)}, bf16[16,2048]{1,0:T(8,128)(2,1)S(1)}, u32[]{:S(2)}, u32[]{:S(2)}) collective-permute-start(bf16[16,2048]{1,0:T(8,128)(2,1)S(1)} %get-tuple-element.28), channel_id=1, source_target_pairs={{0,2},{2,0},{1,3},{3,1},{4,6},{6,4},{5,7},{7,5},{8,10},{10,8},{9,1... | collective-permute-start | bytes 196616 | tf_op jit(solution)/shard_map/ppermute | solution.py:162
  21.9 6.3 %collective-permute-start.12 = (bf16[16,2048]{1,0:T(8,128)(2,1)S(1)}, bf16[16,2048]{1,0:T(8,128)(2,1)S(1)}, u32[]{:S(2)}, u32[]{:S(2)}) collective-permute-start(bf16[16,2048]{1,0:T(8,128)(2,1)S(1)} %get-tuple-element.30), channel_id=1, source_target_pairs={{0,2},{2,0},{1,3},{3,1},{4,6},{6,4},{5,7},{7,5},{8,10},{10,8},{9,1... | collective-permute-start | bytes 196616 | tf_op jit(solution)/shard_map/ppermute | solution.py:162
  23.3 6.3 %collective-permute-start.8 = (bf16[32,2048]{1,0:T(8,128)(2,1)S(1)}, bf16[32,2048]{1,0:T(8,128)(2,1)S(1)}, u32[]{:S(2)}, u32[]{:S(2)}) collective-permute-start(bf16[32,2048]{1,0:T(8,128)(2,1)S(1)} %get-tuple-element.26), channel_id=1, source_target_pairs={{0,4},{4,0},{8,12},{12,8},{1,5},{5,1},{9,13},{13,9},{2,6},{6,2},{1... | collective-permute-start | bytes 393224 | tf_op jit(solution)/shard_map/ppermute | solution.py:162
  26.2 6.3 %collective-permute-start.11 = (bf16[16,2048]{1,0:T(8,128)(2,1)S(1)}, bf16[16,2048]{1,0:T(8,128)(2,1)S(1)}, u32[]{:S(2)}, u32[]{:S(2)}) collective-permute-start(bf16[16,2048]{1,0:T(8,128)(2,1)S(1)} %add_convert_fusion.1), channel_id=1, source_target_pairs={{0,8},{4,12},{8,0},{12,4},{1,9},{5,13},{9,1},{13,5},{2,10},{6,14},... | collective-permute-start | bytes 196616 | tf_op jit(solution)/shard_map/ppermute | solution.py:162
  28.2 6.1 %collective-permute-start.13 = (bf16[16,2048]{1,0:T(8,128)(2,1)S(1)}, bf16[16,2048]{1,0:T(8,128)(2,1)S(1)}, u32[]{:S(2)}, u32[]{:S(2)}) collective-permute-start(bf16[16,2048]{1,0:T(8,128)(2,1)S(1)} %add_convert_fusion), channel_id=1, source_target_pairs={{0,12},{4,8},{8,4},{12,0},{1,13},{5,9},{9,5},{13,1},{2,14},{6,10},... | collective-permute-start | bytes 196616 | tf_op jit(solution)/shard_map/ppermute | solution.py:162
  29.7 6.1 %copy-start.3 = (bf16[16,4096]{1,0:T(8,128)(2,1)S(1)}, bf16[16,4096]{1,0:T(8,128)(2,1)}, u32[]{:S(2)}) copy-start(bf16[16,4096]{1,0:T(8,128)(2,1)} %core_ref.1) | copy-start | bytes 393220
  29.7 4.7 %collective-permute-start.9 = (bf16[16,2048]{1,0:T(8,128)(2,1)S(1)}, bf16[16,2048]{1,0:T(8,128)(2,1)S(1)}, u32[]{:S(2)}, u32[]{:S(2)}) collective-permute-start(bf16[16,2048]{1,0:T(8,128)(2,1)S(1)} %slice.17), channel_id=1, source_target_pairs={{0,2},{2,0},{1,3},{3,1},{4,6},{6,4},{5,7},{7,5},{8,10},{10,8},{9,1... | collective-permute-start | bytes 196616 | tf_op jit(solution)/shard_map/ppermute | solution.py:162
  34.4 1.4 %collective-permute-start.14 = (f32[16,2048]{1,0:T(8,128)S(1)}, f32[16,2048]{1,0:T(8,128)S(1)}, u32[]{:S(2)}, u32[]{:S(2)}) collective-permute-start(f32[16,2048]{1,0:T(8,128)S(1)} %fusion.1.mine_ref), channel_id=1, source_target_pairs={{0,1},{1,0},{2,3},{3,2},{4,5},{5,4},{6,7},{7,6},{8,9},{9,8},{10,11... | collective-permute-start | bytes 393224 | tf_op jit(solution)/shard_map/ppermute | solution.py:162

commit v22 on v19

--- a/solution.py
+++ b/solution.py
@@ -78,12 +78,15 @@
                     at = (q // (groups // 4), t, q % (groups // 4))
                     both = jnp.concatenate([first[at], second[at]], axis=0)
                     dense[t, j * 2 * groups:(j + 1) * 2 * groups, q * 128:(q + 1) * 128] = both.astype(jnp.bfloat16)
+    at_lane = lax.broadcasted_iota(jnp.int32, (points, 128), 1)
+    columns_out = jnp.zeros((points, 128), jnp.float32)
     for t in range(batches):
         product = split_dot(left_ref[t], dense[t]) * values_ref[t].astype(jnp.float32)
         folded = product[:, :128]
         for q in range(1, columns // 128):
             folded = folded + product[:, q * 128:(q + 1) * 128]
-        out_ref[t:t + 1, :] = jnp.sum(folded.T, axis=0, keepdims=True)
+        columns_out = jnp.where(at_lane == t, jnp.sum(folded, axis=1, keepdims=True), columns_out)
+    out_ref[...] = columns_out.T[:batches]
 
 
 def scatter_kernel(places, place_ref, core_ref, *refs):
@@ -100,8 +103,9 @@
     steps = kept // (2 * groups)
     potential = weight_ref[...] * jnp.tanh(mine_ref[...] + far_ref[...])
     low = lax.broadcasted_iota(jnp.int32, (1, groups, 128), 2) < GO
+    upright = jnp.concatenate([potential] * (8 // batches), axis=0).T
     for t in range(batches):
-        factor = jnp.broadcast_to(potential[t:t + 1, :], (128, points)).T
+        factor = jnp.broadcast_to(upright[:, t:t + 1], (points, 128))
         factor = jnp.concatenate([factor] * (columns // 128), axis=1)
         weighted = (values_ref[t].astype(jnp.float32) * factor).astype(jnp.bfloat16)
         part = split_dot(left_t_ref[t], weighted)
@@ -180,9 +184,7 @@
 
     mine = lax.dynamic_slice_in_dim(density_blocks, half * wide, wide, 1)
     direct = {dz: swap(mine, "batch", rows_z, dz) for dz in far}
-    beside = [
-        lax.dynamic_slice_in_dim(swap(density_blocks, "pair", rows_x, dx), half * wide, wide, 1) for dx in side
-    ]
+    beside = [swap(mine, "pair", rows_x, dx) for dx in side]
     *beside, own_rows = lax.optimization_barrier((*beside, own_rows))
     cluster = jnp.concatenate([mine, *beside], axis=0)
     arrays, places = [cluster], [list(range(rows_x))]

time: 36.6 us -> 36.8 us (level)
    unnamed x12 -> x14, local copies, waits for them, and re-layouts: 1.84 us -> 2.74 us
    dynamic_slice x1, local copies, waits for them, and re-layouts: 0.88 us -> 0.01 us  [per_device(): mine = lax.dynamic_slice_in_dim(density_blocks, half * wide, wide, 1)]
  transfers between devices with their start and end apart: 15 -> 15, of which waited for: 8 -> 8; matrix products, arithmetic and copies ran while one was open for 3% -> 0% of each run, Pallas kernels for 3% -> 3%
where the time goes in v22:
time: 36.8 us; the launch traced here: 36.6 us
  starting transfers between devices  15.5 us (42%)
  waiting for transfers between devices  13.7 us (37%)
  Pallas kernels  4.31 us (12%)
  local copies, waits for them, and re-layouts  2.84 us (8%)
    ppermute x15, starting transfers between devices, swap(): return lax.ppermute(array, axis, [(i, i ^ step) for i in range(count)])  15.5 us
    ppermute x15, waiting for transfers between devices, swap(): return lax.ppermute(array, axis, [(i, i ^ step) for i in range(count)])  13.7 us
    unnamed x14, local copies, waits for them, and re-layouts  2.74 us
    pallas_call x1, Pallas kernels, per_device(): call(functools.partial(scatter_kernel, out_places), [jax.ShapeDtypeStruct...  1.52 us
    pallas_call x1, Pallas kernels, per_device(): call(functools.partial(density_kernel, places), jax.ShapeDtypeStruct((bat...  1.1 us
    pallas_call x1, Pallas kernels, per_device(): call(prepare_kernel, (jax.ShapeDtypeStruct((batches, points, kept), bf16)...  0.76 us
  transfers between devices with their start and end apart: 15, of which 8 were waited for; matrix products, arithmetic and copies ran while one was open for 0% of the time, Pallas kernels for 3%

profile of v22, /device:TPU:0, one launch (start us, length us, event | category | flops | bytes accessed | tf_op | source)
XLA Modules:
  0.0 36.6 jit_solution(17002040437832523557)
XLA Ops:
  0.0 0.0 copy-start
  0.0 0.9 %copy-done = bf16[16,4096]{1,0:T(8,128)(2,1)S(1)} copy-done((bf16[16,4096]{1,0:T(8,128)(2,1)S(1)}, bf16[16,4096]{1,0:T(8,128)(2,1)}, u32[]{:S(2)}) %copy-start) | copy-done | bytes 131096
  0.9 0.0 copy-start.6
  0.9 3.0 %collective-permute-start.1 = (bf16[16,2048]{1,0:T(8,128)(2,1)S(1)}, bf16[16,2048]{1,0:T(8,128)(2,1)S(1)}, u32[]{:S(2)}, u32[]{:S(2)}) collective-permute-start(bf16[16,2048]{1,0:T(8,128)(2,1)S(1)} %constant_dynamic-slice_fusion), channel_id=1, source_target_pairs={{0,2},{2,0},{1,3},{3,1},{4,6},{6,4},{5,7},{7,5},{8,10},{10,8},{9,1... | collective-permute-start | bytes 196616 | tf_op jit(solution)/shard_map/ppermute | solution.py:157
  3.9 2.6 %collective-permute-start.3 = (bf16[16,2048]{1,0:T(8,128)(2,1)S(1)}, bf16[16,2048]{1,0:T(8,128)(2,1)S(1)}, u32[]{:S(2)}, u32[]{:S(2)}) collective-permute-start(bf16[16,2048]{1,0:T(8,128)(2,1)S(1)} %constant_dynamic-slice_fusion), channel_id=1, source_target_pairs={{0,8},{4,12},{8,0},{12,4},{1,9},{5,13},{9,1},{13,5},{2,10},{6,14},... | collective-permute-start | bytes 196616 | tf_op jit(solution)/shard_map/ppermute | solution.py:157
  6.5 1.3 %collective-permute-start = (bf16[16,2048]{1,0:T(8,128)(2,1)S(1)}, bf16[16,2048]{1,0:T(8,128)(2,1)S(1)}, u32[]{:S(2)}, u32[]{:S(2)}) collective-permute-start(bf16[16,2048]{1,0:T(8,128)(2,1)S(1)} %constant_dynamic-slice_fusion), channel_id=1, source_target_pairs={{0,12},{4,8},{8,4},{12,0},{1,13},{5,9},{9,5},{13,1},{2,14},{6,10},... | collective-permute-start | bytes 196616 | tf_op jit(solution)/shard_map/ppermute | solution.py:157
  7.9 0.0 copy-done.6
  7.9 0.1 reshape.16.slots_ref
  7.9 0.6 %copy-done.5 = s32[1,1,8,8]{3,2,1,0:T(8,128)S(1)} copy-done((s32[1,1,8,8]{3,2,1,0:T(8,128)S(1)}, s32[1,1,8,8]{3,2,1,0:T(8,128)}, u32[]{:S(2)}) %copy-start.5) | copy-done | bytes 280
  8.5 0.2 shard_map.64.refs_6_.refs_5_
  8.7 0.0 collective-permute-done.1
  8.8 0.3 collective-permute-start.2
  9.1 0.0 collective-permute-start.4
  9.1 1.1 %collective-permute-done.4.refs_7_.refs_6_ = s32[1,128]{1,0:T(1,128)S(1)} collective-permute-done((s32[1,128]{1,0:T(1,128)S(1)}, s32[1,128]{1,0:T(1,128)S(1)}, u32[]{:S(2)}, u32[]{:S(2)}) %collective-permute-start.4) | collective-permute-done | bytes 544 | tf_op jit(solution)/shard_map/ppermute | solution.py:157
  10.2 0.0 collective-permute-done.3.refs_2_
  10.2 0.8 %collective-permute-start.5 = (bf16[16,2048]{1,0:T(8,128)(2,1)S(1)}, bf16[16,2048]{1,0:T(8,128)(2,1)S(1)}, u32[]{:S(2)}, u32[]{:S(2)}) collective-permute-start(bf16[16,2048]{1,0:T(8,128)(2,1)S(1)} %collective-permute-done.3.refs_2_), channel_id=1, source_target_pairs={{0,2},{2,0},{1,3},{3,1},{4,6},{6,4},{5,7},{7,5},{8,10},{10,8},{9,1... | collective-permute-start | bytes 196616 | tf_op jit(solution)/shard_map/ppermute | solution.py:157
  11.0 2.3 %collective-permute-done.refs_4_ = bf16[16,2048]{1,0:T(8,128)(2,1)S(1)} collective-permute-done((bf16[16,2048]{1,0:T(8,128)(2,1)S(1)}, bf16[16,2048]{1,0:T(8,128)(2,1)S(1)}, u32[]{:S(2)}, u32[]{:S(2)}) %collective-permute-start) | collective-permute-done | bytes 65568 | tf_op jit(solution)/shard_map/ppermute | solution.py:157
  13.3 0.5 %collective-permute-start.6 = (bf16[16,2048]{1,0:T(8,128)(2,1)S(1)}, bf16[16,2048]{1,0:T(8,128)(2,1)S(1)}, u32[]{:S(2)}, u32[]{:S(2)}) collective-permute-start(bf16[16,2048]{1,0:T(8,128)(2,1)S(1)} %collective-permute-done.refs_4_), channel_id=1, source_target_pairs={{0,2},{2,0},{1,3},{3,1},{4,6},{6,4},{5,7},{7,5},{8,10},{10,8},{9,1... | collective-permute-start | bytes 196616 | tf_op jit(solution)/shard_map/ppermute | solution.py:157
  13.8 0.0 copy-start.1
  13.8 1.2 %copy-done.1 = bf16[4,256,512]{2,1,0:T(8,128)(2,1)S(1)} copy-done((bf16[4,256,512]{2,1,0:T(8,128)(2,1)S(1)}, bf16[4,256,512]{2,1,0:T(8,128)(2,1)}, u32[]{:S(2)}) %copy-start.1) | copy-done | bytes 1048600
  15.0 0.0 copy-start.2
  15.0 0.8 %shard_map.65 = (bf16[4,256,256]{2,1,0:T(8,128)(2,1)S(1)}, bf16[4,256,256]{2,1,0:T(8,128)(2,1)S(1)}) custom-call(s32[1]{0:T(128)} %bitcast.half_ref.core_ref, bf16[4,256,512]{2,1,0:T(8,128)(2,1)S(1)} %copy-done.1), custom_call_target="tpu_custom_call" | custom-call | flops 536870912 | bytes 3145728 | tf_op jit(solution)/shard_map/pallas_call | solution.py:203
  15.8 0.0 collective-permute-done.5.refs_3_
  15.8 1.7 %collective-permute-done.6.refs_5_ = bf16[16,2048]{1,0:T(8,128)(2,1)S(1)} collective-permute-done((bf16[16,2048]{1,0:T(8,128)(2,1)S(1)}, bf16[16,2048]{1,0:T(8,128)(2,1)S(1)}, u32[]{:S(2)}, u32[]{:S(2)}) %collective-permute-start.6) | collective-permute-done | bytes 65568 | tf_op jit(solution)/shard_map/ppermute | solution.py:157
  17.5 0.0 collective-permute-done.2.refs_1_
  17.5 0.0 copy-done.2
  17.5 1.1 %shard_map.66.refs_0_ = f32[4,256]{1,0:T(4,128)S(1)} custom-call(s32[1]{0:T(128)} %bitcast.1.place_ref, s32[1]{0:T(128)} %bitcast.half_ref.core_ref, bf16[32,2048]{1,0:T(8,128)(2,1)S(1)} %pad_maximum_fusion.refs_0_, bf16[32,2048]{1,0:T(8,128)(2,1)S(1)} %collective-permute-done.2.refs_1_, bf16[16,2048]{1,0:T(8,128)(2,1)S(1)} %collective-permute-done.3.refs_2_, ...), custom_call_target="tpu_custom_call" | custom-call | flops 268435456 | bytes 2097152 | tf_op jit(solution)/shard_map/pallas_call | solution.py:218
  18.6 0.0 collective-permute-start.7
  18.7 1.2 %collective-permute-done.7.refs_1_ = f32[4,256]{1,0:T(4,128)S(1)} collective-permute-done((f32[4,256]{1,0:T(4,128)S(1)}, f32[4,256]{1,0:T(4,128)S(1)}, u32[]{:S(2)}, u32[]{:S(2)}) %collective-permute-start.7) | collective-permute-done | bytes 4128 | tf_op jit(solution)/shard_map/ppermute | solution.py:157
  19.9 0.0 copy-done.4
  19.9 1.5 %shard_map.67 = (bf16[32,2048]{1,0:T(8,128)(2,1)S(1)}, bf16[32,2048]{1,0:T(8,128)(2,1)S(1)}, bf16[16,2048]{1,0:T(8,128)(2,1)S(1)}, bf16[16,2048]{1,0:T(8,128)(2,...) custom-call(s32[1]{0:T(128)} %bitcast.1.place_ref, s32[1]{0:T(128)} %bitcast.half_ref.core_ref, ...), custom_call_target="tpu_custom_call" | custom-call | flops 268435456 | bytes 2097152 | tf_op jit(solution)/shard_map/pallas_call | solution.py:231
  21.4 0.6 %collective-permute-start.10 = (bf16[16,2048]{1,0:T(8,128)(2,1)S(1)}, bf16[16,2048]{1,0:T(8,128)(2,1)S(1)}, u32[]{:S(2)}, u32[]{:S(2)}) collective-permute-start(bf16[16,2048]{1,0:T(8,128)(2,1)S(1)} %get-tuple-element.28), channel_id=1, source_target_pairs={{0,2},{2,0},{1,3},{3,1},{4,6},{6,4},{5,7},{7,5},{8,10},{10,8},{9,1... | collective-permute-start | bytes 196616 | tf_op jit(solution)/shard_map/ppermute | solution.py:157
  22.0 1.5 %collective-permute-start.12 = (bf16[16,2048]{1,0:T(8,128)(2,1)S(1)}, bf16[16,2048]{1,0:T(8,128)(2,1)S(1)}, u32[]{:S(2)}, u32[]{:S(2)}) collective-permute-start(bf16[16,2048]{1,0:T(8,128)(2,1)S(1)} %get-tuple-element.30), channel_id=1, source_target_pairs={{0,2},{2,0},{1,3},{3,1},{4,6},{6,4},{5,7},{7,5},{8,10},{10,8},{9,1... | collective-permute-start | bytes 196616 | tf_op jit(solution)/shard_map/ppermute | solution.py:157
  23.5 0.1 collective-permute-start.8
  23.6 2.7 %collective-permute-done.10 = bf16[16,2048]{1,0:T(8,128)(2,1)S(1)} collective-permute-done((bf16[16,2048]{1,0:T(8,128)(2,1)S(1)}, bf16[16,2048]{1,0:T(8,128)(2,1)S(1)}, u32[]{:S(2)}, u32[]{:S(2)}) %collective-permute-start.10) | collective-permute-done | bytes 65568 | tf_op jit(solution)/shard_map/ppermute | solution.py:157
  26.3 2.0 %collective-permute-start.11 = (bf16[16,2048]{1,0:T(8,128)(2,1)S(1)}, bf16[16,2048]{1,0:T(8,128)(2,1)S(1)}, u32[]{:S(2)}, u32[]{:S(2)}) collective-permute-start(bf16[16,2048]{1,0:T(8,128)(2,1)S(1)} %add_convert_fusion.1), channel_id=1, source_target_pairs={{0,8},{4,12},{8,0},{12,4},{1,9},{5,13},{9,1},{13,5},{2,10},{6,14},... | collective-permute-start | bytes 196616 | tf_op jit(solution)/shard_map/ppermute | solution.py:157
  28.3 0.0 collective-permute-done.12
  28.3 1.4 %collective-permute-start.13 = (bf16[16,2048]{1,0:T(8,128)(2,1)S(1)}, bf16[16,2048]{1,0:T(8,128)(2,1)S(1)}, u32[]{:S(2)}, u32[]{:S(2)}) collective-permute-start(bf16[16,2048]{1,0:T(8,128)(2,1)S(1)} %add_convert_fusion), channel_id=1, source_target_pairs={{0,12},{4,8},{8,4},{12,0},{1,13},{5,9},{9,5},{13,1},{2,14},{6,10},... | collective-permute-start | bytes 196616 | tf_op jit(solution)/shard_map/ppermute | solution.py:157
  29.7 0.0 collective-permute-done.8
  29.8 0.0 copy-start.3
  29.8 1.3 %collective-permute-start.9 = (bf16[16,2048]{1,0:T(8,128)(2,1)S(1)}, bf16[16,2048]{1,0:T(8,128)(2,1)S(1)}, u32[]{:S(2)}, u32[]{:S(2)}) collective-permute-start(bf16[16,2048]{1,0:T(8,128)(2,1)S(1)} %slice.17), channel_id=1, source_target_pairs={{0,2},{2,0},{1,3},{3,1},{4,6},{6,4},{5,7},{7,5},{8,10},{10,8},{9,1... | collective-permute-start | bytes 196616 | tf_op jit(solution)/shard_map/ppermute | solution.py:157
  31.1 1.5 %collective-permute-done.11 = bf16[16,2048]{1,0:T(8,128)(2,1)S(1)} collective-permute-done((bf16[16,2048]{1,0:T(8,128)(2,1)S(1)}, bf16[16,2048]{1,0:T(8,128)(2,1)S(1)}, u32[]{:S(2)}, u32[]{:S(2)}) %collective-permute-start.11) | collective-permute-done | bytes 65568 | tf_op jit(solution)/shard_map/ppermute | solution.py:157
  32.6 1.8 %collective-permute-done.13 = bf16[16,2048]{1,0:T(8,128)(2,1)S(1)} collective-permute-done((bf16[16,2048]{1,0:T(8,128)(2,1)S(1)}, bf16[16,2048]{1,0:T(8,128)(2,1)S(1)}, u32[]{:S(2)}, u32[]{:S(2)}) %collective-permute-start.13) | collective-permute-done | bytes 65568 | tf_op jit(solution)/shard_map/ppermute | solution.py:157
  34.5 0.0 collective-permute-done.9
  34.5 0.1 collective-permute-start.14
  34.6 1.3 %collective-permute-done.14.other_ref = f32[16,2048]{1,0:T(8,128)S(1)} collective-permute-done((f32[16,2048]{1,0:T(8,128)S(1)}, f32[16,2048]{1,0:T(8,128)S(1)}, u32[]{:S(2)}, u32[]{:S(2)}) %collective-permute-start.14) | collective-permute-done | bytes 131104 | tf_op jit(solution)/shard_map/ppermute | solution.py:157
  35.9 0.0 copy-done.3
  35.9 0.7 %shard_map.68 = f32[16,4096]{1,0:T(8,128)} custom-call(s32[1]{0:T(128)} %bitcast.half_ref.core_ref, f32[16,2048]{1,0:T(8,128)S(1)} %fusion.1.mine_ref, f32[16,2048]{1,0:T(8,128)S(1)} %collective-permute-done.14.other_ref, bf16[16,4096]{1,0:T(8,128)(2,1)S(1)} %copy-done.3), custom_call_target="tpu_custom_call" | custom-call | bytes 786432 | tf_op jit(solution)/shard_map/pallas_call | solution.py:257
  (9 shorter events, 0.1 us)
Async XLA Ops:
  0.0 0.9 %copy-start = (bf16[16,4096]{1,0:T(8,128)(2,1)S(1)}, bf16[16,4096]{1,0:T(8,128)(2,1)}, u32[]{:S(2)}) copy-start(bf16[16,4096]{1,0:T(8,128)(2,1)} %param.10) | copy-start | bytes 393220
  0.9 6.9 %copy-start.6 = (s32[4,8,4]{1,2,0:T(4,128)S(1)}, s32[4,8,4]{1,2,0:T(4,128)}, u32[]{:S(2)}) copy-start(s32[4,8,4]{1,2,0:T(4,128)} %param.8) | copy-start | bytes 1540
  0.9 7.8 %collective-permute-start.1 = (bf16[16,2048]{1,0:T(8,128)(2,1)S(1)}, bf16[16,2048]{1,0:T(8,128)(2,1)S(1)}, u32[]{:S(2)}, u32[]{:S(2)}) collective-permute-start(bf16[16,2048]{1,0:T(8,128)(2,1)S(1)} %constant_dynamic-slice_fusion), channel_id=1, source_target_pairs={{0,2},{2,0},{1,3},{3,1},{4,6},{6,4},{5,7},{7,5},{8,10},{10,8},{9,1... | collective-permute-start | bytes 196616 | tf_op jit(solution)/shard_map/ppermute | solution.py:157
  3.9 6.3 %collective-permute-start.3 = (bf16[16,2048]{1,0:T(8,128)(2,1)S(1)}, bf16[16,2048]{1,0:T(8,128)(2,1)S(1)}, u32[]{:S(2)}, u32[]{:S(2)}) collective-permute-start(bf16[16,2048]{1,0:T(8,128)(2,1)S(1)} %constant_dynamic-slice_fusion), channel_id=1, source_target_pairs={{0,8},{4,12},{8,0},{12,4},{1,9},{5,13},{9,1},{13,5},{2,10},{6,14},... | collective-permute-start | bytes 196616 | tf_op jit(solution)/shard_map/ppermute | solution.py:157
  6.5 6.8 %collective-permute-start = (bf16[16,2048]{1,0:T(8,128)(2,1)S(1)}, bf16[16,2048]{1,0:T(8,128)(2,1)S(1)}, u32[]{:S(2)}, u32[]{:S(2)}) collective-permute-start(bf16[16,2048]{1,0:T(8,128)(2,1)S(1)} %constant_dynamic-slice_fusion), channel_id=1, source_target_pairs={{0,12},{4,8},{8,4},{12,0},{1,13},{5,9},{9,5},{13,1},{2,14},{6,10},... | collective-permute-start | bytes 196616 | tf_op jit(solution)/shard_map/ppermute | solution.py:157
  7.9 0.7 %copy-start.5 = (s32[1,1,8,8]{3,2,1,0:T(8,128)S(1)}, s32[1,1,8,8]{3,2,1,0:T(8,128)}, u32[]{:S(2)}) copy-start(s32[1,1,8,8]{3,2,1,0:T(8,128)} %param.9) | copy-start | bytes 772
  8.8 8.8 %collective-permute-start.2 = (bf16[32,2048]{1,0:T(8,128)(2,1)S(1)}, bf16[32,2048]{1,0:T(8,128)(2,1)S(1)}, u32[]{:S(2)}, u32[]{:S(2)}) collective-permute-start(bf16[32,2048]{1,0:T(8,128)(2,1)S(1)} %pad_maximum_fusion.refs_0_), channel_id=1, source_target_pairs={{0,4},{4,0},{8,12},{12,8},{1,5},{5,1},{9,13},{13,9},{2,6},{6,2},{1... | collective-permute-start | bytes 393224 | tf_op jit(solution)/shard_map/ppermute | solution.py:157
  9.1 1.1 %collective-permute-start.4 = (s32[1,128]{1,0:T(1,128)S(1)}, s32[1,128]{1,0:T(1,128)S(1)}, u32[]{:S(2)}, u32[]{:S(2)}) collective-permute-start(s32[1,128]{1,0:T(1,128)S(1)} %shard_map.64.refs_6_.refs_5_), channel_id=1, source_target_pairs={{0,1},{1,0},{2,3},{3,2},{4,5},{5,4},{6,7},{7,6},{8,9},{9,8},{10,11... | collective-permute-start | bytes 1544 | tf_op jit(solution)/shard_map/ppermute | solution.py:157
  10.2 5.6 %collective-permute-start.5 = (bf16[16,2048]{1,0:T(8,128)(2,1)S(1)}, bf16[16,2048]{1,0:T(8,128)(2,1)S(1)}, u32[]{:S(2)}, u32[]{:S(2)}) collective-permute-start(bf16[16,2048]{1,0:T(8,128)(2,1)S(1)} %collective-permute-done.3.refs_2_), channel_id=1, source_target_pairs={{0,2},{2,0},{1,3},{3,1},{4,6},{6,4},{5,7},{7,5},{8,10},{10,8},{9,1... | collective-permute-start | bytes 196616 | tf_op jit(solution)/shard_map/ppermute | solution.py:157
  13.3 4.3 %collective-permute-start.6 = (bf16[16,2048]{1,0:T(8,128)(2,1)S(1)}, bf16[16,2048]{1,0:T(8,128)(2,1)S(1)}, u32[]{:S(2)}, u32[]{:S(2)}) collective-permute-start(bf16[16,2048]{1,0:T(8,128)(2,1)S(1)} %collective-permute-done.refs_4_), channel_id=1, source_target_pairs={{0,2},{2,0},{1,3},{3,1},{4,6},{6,4},{5,7},{7,5},{8,10},{10,8},{9,1... | collective-permute-start | bytes 196616 | tf_op jit(solution)/shard_map/ppermute | solution.py:157
  13.8 1.2 %copy-start.1 = (bf16[4,256,512]{2,1,0:T(8,128)(2,1)S(1)}, bf16[4,256,512]{2,1,0:T(8,128)(2,1)}, u32[]{:S(2)}) copy-start(bf16[4,256,512]{2,1,0:T(8,128)(2,1)} %refs_3_.1) | copy-start | bytes 3145732
  15.0 2.5 %copy-start.2 = (bf16[4,256,512]{2,1,0:T(8,128)(2,1)S(1)}, bf16[4,256,512]{2,1,0:T(8,128)(2,1)}, u32[]{:S(2)}) copy-start(bf16[4,256,512]{2,1,0:T(8,128)(2,1)} %refs_3_.1) | copy-start | bytes 3145732
  17.5 2.3 %copy-start.4 = (f32[4,256]{1,0:T(4,128)S(1)}, f32[4,256]{1,0:T(4,128)}, u32[]{:S(2)}) copy-start(f32[4,256]{1,0:T(4,128)} %refs_2_.1) | copy-start | bytes 12292
  18.6 1.2 %collective-permute-start.7 = (f32[4,256]{1,0:T(4,128)S(1)}, f32[4,256]{1,0:T(4,128)S(1)}, u32[]{:S(2)}, u32[]{:S(2)}) collective-permute-start(f32[4,256]{1,0:T(4,128)S(1)} %shard_map.66.refs_0_), channel_id=1, source_target_pairs={{0,1},{1,0},{2,3},{3,2},{4,5},{5,4},{6,7},{7,6},{8,9},{9,8},{10,11... | collective-permute-start | bytes 12296 | tf_op jit(solution)/shard_map/ppermute | solution.py:157
  21.4 4.9 %collective-permute-start.10 = (bf16[16,2048]{1,0:T(8,128)(2,1)S(1)}, bf16[16,2048]{1,0:T(8,128)(2,1)S(1)}, u32[]{:S(2)}, u32[]{:S(2)}) collective-permute-start(bf16[16,2048]{1,0:T(8,128)(2,1)S(1)} %get-tuple-element.28), channel_id=1, source_target_pairs={{0,2},{2,0},{1,3},{3,1},{4,6},{6,4},{5,7},{7,5},{8,10},{10,8},{9,1... | collective-permute-start | bytes 196616 | tf_op jit(solution)/shard_map/ppermute | solution.py:157
  22.0 6.3 %collective-permute-start.12 = (bf16[16,2048]{1,0:T(8,128)(2,1)S(1)}, bf16[16,2048]{1,0:T(8,128)(2,1)S(1)}, u32[]{:S(2)}, u32[]{:S(2)}) collective-permute-start(bf16[16,2048]{1,0:T(8,128)(2,1)S(1)} %get-tuple-element.30), channel_id=1, source_target_pairs={{0,2},{2,0},{1,3},{3,1},{4,6},{6,4},{5,7},{7,5},{8,10},{10,8},{9,1... | collective-permute-start | bytes 196616 | tf_op jit(solution)/shard_map/ppermute | solution.py:157
  23.5 6.3 %collective-permute-start.8 = (bf16[32,2048]{1,0:T(8,128)(2,1)S(1)}, bf16[32,2048]{1,0:T(8,128)(2,1)S(1)}, u32[]{:S(2)}, u32[]{:S(2)}) collective-permute-start(bf16[32,2048]{1,0:T(8,128)(2,1)S(1)} %get-tuple-element.26), channel_id=1, source_target_pairs={{0,4},{4,0},{8,12},{12,8},{1,5},{5,1},{9,13},{13,9},{2,6},{6,2},{1... | collective-permute-start | bytes 393224 | tf_op jit(solution)/shard_map/ppermute | solution.py:157
  26.3 6.3 %collective-permute-start.11 = (bf16[16,2048]{1,0:T(8,128)(2,1)S(1)}, bf16[16,2048]{1,0:T(8,128)(2,1)S(1)}, u32[]{:S(2)}, u32[]{:S(2)}) collective-permute-start(bf16[16,2048]{1,0:T(8,128)(2,1)S(1)} %add_convert_fusion.1), channel_id=1, source_target_pairs={{0,8},{4,12},{8,0},{12,4},{1,9},{5,13},{9,1},{13,5},{2,10},{6,14},... | collective-permute-start | bytes 196616 | tf_op jit(solution)/shard_map/ppermute | solution.py:157
  28.3 6.1 %collective-permute-start.13 = (bf16[16,2048]{1,0:T(8,128)(2,1)S(1)}, bf16[16,2048]{1,0:T(8,128)(2,1)S(1)}, u32[]{:S(2)}, u32[]{:S(2)}) collective-permute-start(bf16[16,2048]{1,0:T(8,128)(2,1)S(1)} %add_convert_fusion), channel_id=1, source_target_pairs={{0,12},{4,8},{8,4},{12,0},{1,13},{5,9},{9,5},{13,1},{2,14},{6,10},... | collective-permute-start | bytes 196616 | tf_op jit(solution)/shard_map/ppermute | solution.py:157
  29.8 6.1 %copy-start.3 = (bf16[16,4096]{1,0:T(8,128)(2,1)S(1)}, bf16[16,4096]{1,0:T(8,128)(2,1)}, u32[]{:S(2)}) copy-start(bf16[16,4096]{1,0:T(8,128)(2,1)} %core_ref.1) | copy-start | bytes 393220
  29.8 4.7 %collective-permute-start.9 = (bf16[16,2048]{1,0:T(8,128)(2,1)S(1)}, bf16[16,2048]{1,0:T(8,128)(2,1)S(1)}, u32[]{:S(2)}, u32[]{:S(2)}) collective-permute-start(bf16[16,2048]{1,0:T(8,128)(2,1)S(1)} %slice.17), channel_id=1, source_target_pairs={{0,2},{2,0},{1,3},{3,1},{4,6},{6,4},{5,7},{7,5},{8,10},{10,8},{9,1... | collective-permute-start | bytes 196616 | tf_op jit(solution)/shard_map/ppermute | solution.py:157
  34.5 1.4 %collective-permute-start.14 = (f32[16,2048]{1,0:T(8,128)S(1)}, f32[16,2048]{1,0:T(8,128)S(1)}, u32[]{:S(2)}, u32[]{:S(2)}) collective-permute-start(f32[16,2048]{1,0:T(8,128)S(1)} %fusion.1.mine_ref), channel_id=1, source_target_pairs={{0,1},{1,0},{2,3},{3,2},{4,5},{5,4},{6,7},{7,6},{8,9},{9,8},{10,11... | collective-permute-start | bytes 393224 | tf_op jit(solution)/shard_map/ppermute | solution.py:157

commit v23 on v19

--- a/solution.py
+++ b/solution.py
@@ -66,10 +66,10 @@
         table[blocks[0] * held:(blocks[-1] + 1) * held, :] = ref[...]
     pick = row_table(place_ref, core_ref, own_ref, other_ref, held, owners).T.astype(jnp.bfloat16)
     low = lax.broadcasted_iota(jnp.int32, (1, 1, 1, groups, 128), 4) < GO
-    for chunk in range(table.shape[1] // 256):
-        wide = split_dot(pick, table[:, chunk * 256:(chunk + 1) * 256])
-        for j in (2 * chunk, 2 * chunk + 1):
-            got = wide[:, (j % 2) * 128:(j % 2 + 1) * 128].reshape(2, batches, groups // 4, 2, groups, 128)
+    for chunk in range(table.shape[1] // 512):
+        wide = split_dot(pick, table[:, chunk * 512:(chunk + 1) * 512])
+        for j in range(4 * chunk, 4 * chunk + 4):
+            got = wide[:, (j % 4) * 128:(j % 4 + 1) * 128].reshape(2, batches, groups // 4, 2, groups, 128)
             even, odd = got[:, :, :, 0], got[:, :, :, 1]
             first = jnp.where(low, even, pltpu.roll(odd, GO, 4))
             second = jnp.where(low, pltpu.roll(even, GO, 4), odd)
@@ -88,8 +88,8 @@
 
 def scatter_kernel(places, place_ref, core_ref, *refs):
     mine_ref, far_ref, weight_ref, values_ref, left_t_ref, own_ref, other_ref = refs[:7]
-    out_refs = refs[7:-2]
-    high, rest = refs[-2:]
+    out_refs = refs[7:-1]
+    terms = refs[-1]
     target = {k: (ref, i) for ref, blocks in zip(out_refs, places) for i, k in enumerate(blocks)}
     pieces = len(target)
     held = out_refs[0].shape[0] // len(places[0])
@@ -98,6 +98,7 @@
     groups = columns // GO
     kept = left_t_ref.shape[1]
     steps = kept // (2 * groups)
+    entries = batches * groups * groups
     potential = weight_ref[...] * jnp.tanh(mine_ref[...] + far_ref[...])
     low = lax.broadcasted_iota(jnp.int32, (1, groups, 128), 2) < GO
     for t in range(batches):
@@ -115,12 +116,14 @@
             for j in range(steps):
                 both = jnp.concatenate([even[j], odd[j]], axis=0)
                 top = both.astype(jnp.bfloat16)
-                high[at:at + 2 * groups, j * 128:(j + 1) * 128] = top
-                rest[at:at + 2 * groups, j * 128:(j + 1) * 128] = (both - top.astype(jnp.float32)).astype(jnp.bfloat16)
+                terms[at:at + 2 * groups, j * 128:(j + 1) * 128] = top
+                left = (both - top.astype(jnp.float32)).astype(jnp.bfloat16)
+                terms[entries + at:entries + at + 2 * groups, j * 128:(j + 1) * 128] = left
+    put = jnp.concatenate([put, put], axis=1)
     step = max(1, min(pieces, 128 // held))
     for k in range(0, pieces, step):
         some = put[k * held:(k + step) * held, :]
-        total = split_dot(some, high[...]) + split_dot(some, rest[...])
+        total = split_dot(some, terms[...])
         for i in range(step):
             ref, at = target[k + i]
             ref[at * held:(at + 1) * held, :] = total[i * held:(i + 1) * held, :].astype(jnp.bfloat16)
@@ -180,9 +183,7 @@
 
     mine = lax.dynamic_slice_in_dim(density_blocks, half * wide, wide, 1)
     direct = {dz: swap(mine, "batch", rows_z, dz) for dz in far}
-    beside = [
-        lax.dynamic_slice_in_dim(swap(density_blocks, "pair", rows_x, dx), half * wide, wide, 1) for dx in side
-    ]
+    beside = [swap(mine, "pair", rows_x, dx) for dx in side]
     *beside, own_rows = lax.optimization_barrier((*beside, own_rows))
     cluster = jnp.concatenate([mine, *beside], axis=0)
     arrays, places = [cluster], [list(range(rows_x))]
@@ -231,7 +232,7 @@
         [jax.ShapeDtypeStruct((held * len(blocks), wide), bf16) for blocks in out_places],
         7,
         scalars=2,
-        scratch=(pltpu.VMEM((entries, wide), bf16), pltpu.VMEM((entries, wide), bf16)),
+        scratch=(pltpu.VMEM((2 * entries, wide), bf16),),
         flops=2 * batches * points * columns * kept,
         moved=2 * batches * points * columns * 2,
     )(place, core_at, partial, partial_other, point_weights, basis_values, left_t, own_rows, other_rows)

time: 36.6 us -> 36.6 us (level)
    unnamed x12 -> x14, local copies, waits for them, and re-layouts: 1.84 us -> 2.74 us
    dynamic_slice x1, local copies, waits for them, and re-layouts: 0.88 us -> 0.01 us  [per_device(): mine = lax.dynamic_slice_in_dim(density_blocks, half * wide, wide, 1)]
  transfers between devices with their start and end apart: 15 -> 15, of which waited for: 8 -> 8; matrix products, arithmetic and copies ran while one was open for 3% -> 0% of each run, Pallas kernels for 3% -> 3%
where the time goes in v23:
time: 36.6 us; the launch traced here: 36.4 us
  starting transfers between devices  15.5 us (42%)
  waiting for transfers between devices  13.8 us (38%)
  Pallas kernels  4.05 us (11%)
  local copies, waits for them, and re-layouts  2.84 us (8%)
    ppermute x15, starting transfers between devices, swap(): return lax.ppermute(array, axis, [(i, i ^ step) for i in range(count)])  15.5 us
    ppermute x15, waiting for transfers between devices, swap(): return lax.ppermute(array, axis, [(i, i ^ step) for i in range(count)])  13.8 us
    unnamed x14, local copies, waits for them, and re-layouts  2.74 us
    pallas_call x1, Pallas kernels, per_device(): call(functools.partial(scatter_kernel, out_places), [jax.ShapeDtypeStruct...  1.3 us
    pallas_call x1, Pallas kernels, per_device(): call(functools.partial(density_kernel, places), jax.ShapeDtypeStruct((bat...  1.07 us
    pallas_call x1, Pallas kernels, per_device(): call(prepare_kernel, (jax.ShapeDtypeStruct((batches, points, kept), bf16)...  0.76 us
  transfers between devices with their start and end apart: 15, of which 8 were waited for; matrix products, arithmetic and copies ran while one was open for 0% of the time, Pallas kernels for 3%

profile of v23, /device:TPU:0, one launch (start us, length us, event | category | flops | bytes accessed | tf_op | source)
XLA Modules:
  0.0 36.4 jit_solution(17242085920167463218)
XLA Ops:
  0.0 0.0 copy-start
  0.0 0.9 %copy-done = bf16[16,4096]{1,0:T(8,128)(2,1)S(1)} copy-done((bf16[16,4096]{1,0:T(8,128)(2,1)S(1)}, bf16[16,4096]{1,0:T(8,128)(2,1)}, u32[]{:S(2)}) %copy-start) | copy-done | bytes 131096
  0.9 0.0 copy-start.6
  0.9 3.0 %collective-permute-start.1 = (bf16[16,2048]{1,0:T(8,128)(2,1)S(1)}, bf16[16,2048]{1,0:T(8,128)(2,1)S(1)}, u32[]{:S(2)}, u32[]{:S(2)}) collective-permute-start(bf16[16,2048]{1,0:T(8,128)(2,1)S(1)} %constant_dynamic-slice_fusion), channel_id=1, source_target_pairs={{0,2},{2,0},{1,3},{3,1},{4,6},{6,4},{5,7},{7,5},{8,10},{10,8},{9,1... | collective-permute-start | bytes 196616 | tf_op jit(solution)/shard_map/ppermute | solution.py:156
  3.9 2.6 %collective-permute-start.3 = (bf16[16,2048]{1,0:T(8,128)(2,1)S(1)}, bf16[16,2048]{1,0:T(8,128)(2,1)S(1)}, u32[]{:S(2)}, u32[]{:S(2)}) collective-permute-start(bf16[16,2048]{1,0:T(8,128)(2,1)S(1)} %constant_dynamic-slice_fusion), channel_id=1, source_target_pairs={{0,8},{4,12},{8,0},{12,4},{1,9},{5,13},{9,1},{13,5},{2,10},{6,14},... | collective-permute-start | bytes 196616 | tf_op jit(solution)/shard_map/ppermute | solution.py:156
  6.5 1.3 %collective-permute-start = (bf16[16,2048]{1,0:T(8,128)(2,1)S(1)}, bf16[16,2048]{1,0:T(8,128)(2,1)S(1)}, u32[]{:S(2)}, u32[]{:S(2)}) collective-permute-start(bf16[16,2048]{1,0:T(8,128)(2,1)S(1)} %constant_dynamic-slice_fusion), channel_id=1, source_target_pairs={{0,12},{4,8},{8,4},{12,0},{1,13},{5,9},{9,5},{13,1},{2,14},{6,10},... | collective-permute-start | bytes 196616 | tf_op jit(solution)/shard_map/ppermute | solution.py:156
  7.9 0.0 copy-done.6
  7.9 0.1 reshape.16.slots_ref
  7.9 0.6 %copy-done.5 = s32[1,1,8,8]{3,2,1,0:T(8,128)S(1)} copy-done((s32[1,1,8,8]{3,2,1,0:T(8,128)S(1)}, s32[1,1,8,8]{3,2,1,0:T(8,128)}, u32[]{:S(2)}) %copy-start.5) | copy-done | bytes 280
  8.5 0.2 shard_map.64.refs_6_.refs_5_
  8.7 0.0 collective-permute-done.1
  8.8 0.3 collective-permute-start.2
  9.1 0.0 collective-permute-start.4
  9.1 1.1 %collective-permute-done.4.refs_7_.refs_6_ = s32[1,128]{1,0:T(1,128)S(1)} collective-permute-done((s32[1,128]{1,0:T(1,128)S(1)}, s32[1,128]{1,0:T(1,128)S(1)}, u32[]{:S(2)}, u32[]{:S(2)}) %collective-permute-start.4) | collective-permute-done | bytes 544 | tf_op jit(solution)/shard_map/ppermute | solution.py:156
  10.2 0.0 collective-permute-done.3.refs_2_
  10.2 0.8 %collective-permute-start.5 = (bf16[16,2048]{1,0:T(8,128)(2,1)S(1)}, bf16[16,2048]{1,0:T(8,128)(2,1)S(1)}, u32[]{:S(2)}, u32[]{:S(2)}) collective-permute-start(bf16[16,2048]{1,0:T(8,128)(2,1)S(1)} %collective-permute-done.3.refs_2_), channel_id=1, source_target_pairs={{0,2},{2,0},{1,3},{3,1},{4,6},{6,4},{5,7},{7,5},{8,10},{10,8},{9,1... | collective-permute-start | bytes 196616 | tf_op jit(solution)/shard_map/ppermute | solution.py:156
  11.0 2.3 %collective-permute-done.refs_4_ = bf16[16,2048]{1,0:T(8,128)(2,1)S(1)} collective-permute-done((bf16[16,2048]{1,0:T(8,128)(2,1)S(1)}, bf16[16,2048]{1,0:T(8,128)(2,1)S(1)}, u32[]{:S(2)}, u32[]{:S(2)}) %collective-permute-start) | collective-permute-done | bytes 65568 | tf_op jit(solution)/shard_map/ppermute | solution.py:156
  13.3 0.5 %collective-permute-start.6 = (bf16[16,2048]{1,0:T(8,128)(2,1)S(1)}, bf16[16,2048]{1,0:T(8,128)(2,1)S(1)}, u32[]{:S(2)}, u32[]{:S(2)}) collective-permute-start(bf16[16,2048]{1,0:T(8,128)(2,1)S(1)} %collective-permute-done.refs_4_), channel_id=1, source_target_pairs={{0,2},{2,0},{1,3},{3,1},{4,6},{6,4},{5,7},{7,5},{8,10},{10,8},{9,1... | collective-permute-start | bytes 196616 | tf_op jit(solution)/shard_map/ppermute | solution.py:156
  13.8 0.0 copy-start.1
  13.8 1.2 %copy-done.1 = bf16[4,256,512]{2,1,0:T(8,128)(2,1)S(1)} copy-done((bf16[4,256,512]{2,1,0:T(8,128)(2,1)S(1)}, bf16[4,256,512]{2,1,0:T(8,128)(2,1)}, u32[]{:S(2)}) %copy-start.1) | copy-done | bytes 1048600
  15.0 0.0 copy-start.2
  15.0 0.8 %shard_map.65 = (bf16[4,256,256]{2,1,0:T(8,128)(2,1)S(1)}, bf16[4,256,256]{2,1,0:T(8,128)(2,1)S(1)}) custom-call(s32[1]{0:T(128)} %bitcast.half_ref.core_ref, bf16[4,256,512]{2,1,0:T(8,128)(2,1)S(1)} %copy-done.1), custom_call_target="tpu_custom_call" | custom-call | flops 536870912 | bytes 3145728 | tf_op jit(solution)/shard_map/pallas_call | solution.py:202
  15.8 0.0 collective-permute-done.5.refs_3_
  15.8 1.7 %collective-permute-done.6.refs_5_ = bf16[16,2048]{1,0:T(8,128)(2,1)S(1)} collective-permute-done((bf16[16,2048]{1,0:T(8,128)(2,1)S(1)}, bf16[16,2048]{1,0:T(8,128)(2,1)S(1)}, u32[]{:S(2)}, u32[]{:S(2)}) %collective-permute-start.6) | collective-permute-done | bytes 65568 | tf_op jit(solution)/shard_map/ppermute | solution.py:156
  17.5 0.0 collective-permute-done.2.refs_1_
  17.5 0.0 copy-done.2
  17.5 1.1 %shard_map.66.refs_0_ = f32[4,256]{1,0:T(4,128)S(1)} custom-call(s32[1]{0:T(128)} %bitcast.1.place_ref, s32[1]{0:T(128)} %bitcast.half_ref.core_ref, bf16[32,2048]{1,0:T(8,128)(2,1)S(1)} %pad_maximum_fusion.refs_0_, bf16[32,2048]{1,0:T(8,128)(2,1)S(1)} %collective-permute-done.2.refs_1_, bf16[16,2048]{1,0:T(8,128)(2,1)S(1)} %collective-permute-done.3.refs_2_, ...), custom_call_target="tpu_custom_call" | custom-call | flops 268435456 | bytes 2097152 | tf_op jit(solution)/shard_map/pallas_call | solution.py:217
  18.6 0.1 collective-permute-start.7
  18.7 1.2 %collective-permute-done.7.refs_1_ = f32[4,256]{1,0:T(4,128)S(1)} collective-permute-done((f32[4,256]{1,0:T(4,128)S(1)}, f32[4,256]{1,0:T(4,128)S(1)}, u32[]{:S(2)}, u32[]{:S(2)}) %collective-permute-start.7) | collective-permute-done | bytes 4128 | tf_op jit(solution)/shard_map/ppermute | solution.py:156
  19.8 0.0 copy-done.4
  19.8 1.3 %shard_map.67 = (bf16[32,2048]{1,0:T(8,128)(2,1)S(1)}, bf16[32,2048]{1,0:T(8,128)(2,1)S(1)}, bf16[16,2048]{1,0:T(8,128)(2,1)S(1)}, bf16[16,2048]{1,0:T(8,128)(2,...) custom-call(s32[1]{0:T(128)} %bitcast.1.place_ref, s32[1]{0:T(128)} %bitcast.half_ref.core_ref, ...), custom_call_target="tpu_custom_call" | custom-call | flops 268435456 | bytes 2097152 | tf_op jit(solution)/shard_map/pallas_call | solution.py:230
  21.2 0.6 %collective-permute-start.10 = (bf16[16,2048]{1,0:T(8,128)(2,1)S(1)}, bf16[16,2048]{1,0:T(8,128)(2,1)S(1)}, u32[]{:S(2)}, u32[]{:S(2)}) collective-permute-start(bf16[16,2048]{1,0:T(8,128)(2,1)S(1)} %get-tuple-element.28), channel_id=1, source_target_pairs={{0,2},{2,0},{1,3},{3,1},{4,6},{6,4},{5,7},{7,5},{8,10},{10,8},{9,1... | collective-permute-start | bytes 196616 | tf_op jit(solution)/shard_map/ppermute | solution.py:156
  21.8 1.5 %collective-permute-start.12 = (bf16[16,2048]{1,0:T(8,128)(2,1)S(1)}, bf16[16,2048]{1,0:T(8,128)(2,1)S(1)}, u32[]{:S(2)}, u32[]{:S(2)}) collective-permute-start(bf16[16,2048]{1,0:T(8,128)(2,1)S(1)} %get-tuple-element.30), channel_id=1, source_target_pairs={{0,2},{2,0},{1,3},{3,1},{4,6},{6,4},{5,7},{7,5},{8,10},{10,8},{9,1... | collective-permute-start | bytes 196616 | tf_op jit(solution)/shard_map/ppermute | solution.py:156
  23.3 0.1 collective-permute-start.8
  23.4 2.7 %collective-permute-done.10 = bf16[16,2048]{1,0:T(8,128)(2,1)S(1)} collective-permute-done((bf16[16,2048]{1,0:T(8,128)(2,1)S(1)}, bf16[16,2048]{1,0:T(8,128)(2,1)S(1)}, u32[]{:S(2)}, u32[]{:S(2)}) %collective-permute-start.10) | collective-permute-done | bytes 65568 | tf_op jit(solution)/shard_map/ppermute | solution.py:156
  26.1 2.0 %collective-permute-start.11 = (bf16[16,2048]{1,0:T(8,128)(2,1)S(1)}, bf16[16,2048]{1,0:T(8,128)(2,1)S(1)}, u32[]{:S(2)}, u32[]{:S(2)}) collective-permute-start(bf16[16,2048]{1,0:T(8,128)(2,1)S(1)} %add_convert_fusion.1), channel_id=1, source_target_pairs={{0,8},{4,12},{8,0},{12,4},{1,9},{5,13},{9,1},{13,5},{2,10},{6,14},... | collective-permute-start | bytes 196616 | tf_op jit(solution)/shard_map/ppermute | solution.py:156
  28.1 0.0 collective-permute-done.12
  28.1 1.4 %collective-permute-start.13 = (bf16[16,2048]{1,0:T(8,128)(2,1)S(1)}, bf16[16,2048]{1,0:T(8,128)(2,1)S(1)}, u32[]{:S(2)}, u32[]{:S(2)}) collective-permute-start(bf16[16,2048]{1,0:T(8,128)(2,1)S(1)} %add_convert_fusion), channel_id=1, source_target_pairs={{0,12},{4,8},{8,4},{12,0},{1,13},{5,9},{9,5},{13,1},{2,14},{6,10},... | collective-permute-start | bytes 196616 | tf_op jit(solution)/shard_map/ppermute | solution.py:156
  29.5 0.0 collective-permute-done.8
  29.5 0.0 copy-start.3
  29.6 1.3 %collective-permute-start.9 = (bf16[16,2048]{1,0:T(8,128)(2,1)S(1)}, bf16[16,2048]{1,0:T(8,128)(2,1)S(1)}, u32[]{:S(2)}, u32[]{:S(2)}) collective-permute-start(bf16[16,2048]{1,0:T(8,128)(2,1)S(1)} %slice.17), channel_id=1, source_target_pairs={{0,2},{2,0},{1,3},{3,1},{4,6},{6,4},{5,7},{7,5},{8,10},{10,8},{9,1... | collective-permute-start | bytes 196616 | tf_op jit(solution)/shard_map/ppermute | solution.py:156
  30.8 1.6 %collective-permute-done.11 = bf16[16,2048]{1,0:T(8,128)(2,1)S(1)} collective-permute-done((bf16[16,2048]{1,0:T(8,128)(2,1)S(1)}, bf16[16,2048]{1,0:T(8,128)(2,1)S(1)}, u32[]{:S(2)}, u32[]{:S(2)}) %collective-permute-start.11) | collective-permute-done | bytes 65568 | tf_op jit(solution)/shard_map/ppermute | solution.py:156
  32.4 1.8 %collective-permute-done.13 = bf16[16,2048]{1,0:T(8,128)(2,1)S(1)} collective-permute-done((bf16[16,2048]{1,0:T(8,128)(2,1)S(1)}, bf16[16,2048]{1,0:T(8,128)(2,1)S(1)}, u32[]{:S(2)}, u32[]{:S(2)}) %collective-permute-start.13) | collective-permute-done | bytes 65568 | tf_op jit(solution)/shard_map/ppermute | solution.py:156
  34.2 0.0 collective-permute-done.9
  34.3 0.1 collective-permute-start.14
  34.4 1.3 %collective-permute-done.14.other_ref = f32[16,2048]{1,0:T(8,128)S(1)} collective-permute-done((f32[16,2048]{1,0:T(8,128)S(1)}, f32[16,2048]{1,0:T(8,128)S(1)}, u32[]{:S(2)}, u32[]{:S(2)}) %collective-permute-start.14) | collective-permute-done | bytes 131104 | tf_op jit(solution)/shard_map/ppermute | solution.py:156
  35.7 0.0 copy-done.3
  35.7 0.7 %shard_map.68 = f32[16,4096]{1,0:T(8,128)} custom-call(s32[1]{0:T(128)} %bitcast.half_ref.core_ref, f32[16,2048]{1,0:T(8,128)S(1)} %fusion.1.mine_ref, f32[16,2048]{1,0:T(8,128)S(1)} %collective-permute-done.14.other_ref, bf16[16,4096]{1,0:T(8,128)(2,1)S(1)} %copy-done.3), custom_call_target="tpu_custom_call" | custom-call | bytes 786432 | tf_op jit(solution)/shard_map/pallas_call | solution.py:256
  (9 shorter events, 0.1 us)
Async XLA Ops:
  0.0 0.9 %copy-start = (bf16[16,4096]{1,0:T(8,128)(2,1)S(1)}, bf16[16,4096]{1,0:T(8,128)(2,1)}, u32[]{:S(2)}) copy-start(bf16[16,4096]{1,0:T(8,128)(2,1)} %param.10) | copy-start | bytes 393220
  0.9 6.9 %copy-start.6 = (s32[4,8,4]{1,2,0:T(4,128)S(1)}, s32[4,8,4]{1,2,0:T(4,128)}, u32[]{:S(2)}) copy-start(s32[4,8,4]{1,2,0:T(4,128)} %param.8) | copy-start | bytes 1540
  0.9 7.8 %collective-permute-start.1 = (bf16[16,2048]{1,0:T(8,128)(2,1)S(1)}, bf16[16,2048]{1,0:T(8,128)(2,1)S(1)}, u32[]{:S(2)}, u32[]{:S(2)}) collective-permute-start(bf16[16,2048]{1,0:T(8,128)(2,1)S(1)} %constant_dynamic-slice_fusion), channel_id=1, source_target_pairs={{0,2},{2,0},{1,3},{3,1},{4,6},{6,4},{5,7},{7,5},{8,10},{10,8},{9,1... | collective-permute-start | bytes 196616 | tf_op jit(solution)/shard_map/ppermute | solution.py:156
  3.9 6.3 %collective-permute-start.3 = (bf16[16,2048]{1,0:T(8,128)(2,1)S(1)}, bf16[16,2048]{1,0:T(8,128)(2,1)S(1)}, u32[]{:S(2)}, u32[]{:S(2)}) collective-permute-start(bf16[16,2048]{1,0:T(8,128)(2,1)S(1)} %constant_dynamic-slice_fusion), channel_id=1, source_target_pairs={{0,8},{4,12},{8,0},{12,4},{1,9},{5,13},{9,1},{13,5},{2,10},{6,14},... | collective-permute-start | bytes 196616 | tf_op jit(solution)/shard_map/ppermute | solution.py:156
  6.5 6.8 %collective-permute-start = (bf16[16,2048]{1,0:T(8,128)(2,1)S(1)}, bf16[16,2048]{1,0:T(8,128)(2,1)S(1)}, u32[]{:S(2)}, u32[]{:S(2)}) collective-permute-start(bf16[16,2048]{1,0:T(8,128)(2,1)S(1)} %constant_dynamic-slice_fusion), channel_id=1, source_target_pairs={{0,12},{4,8},{8,4},{12,0},{1,13},{5,9},{9,5},{13,1},{2,14},{6,10},... | collective-permute-start | bytes 196616 | tf_op jit(solution)/shard_map/ppermute | solution.py:156
  7.9 0.7 %copy-start.5 = (s32[1,1,8,8]{3,2,1,0:T(8,128)S(1)}, s32[1,1,8,8]{3,2,1,0:T(8,128)}, u32[]{:S(2)}) copy-start(s32[1,1,8,8]{3,2,1,0:T(8,128)} %param.9) | copy-start | bytes 772
  8.8 8.8 %collective-permute-start.2 = (bf16[32,2048]{1,0:T(8,128)(2,1)S(1)}, bf16[32,2048]{1,0:T(8,128)(2,1)S(1)}, u32[]{:S(2)}, u32[]{:S(2)}) collective-permute-start(bf16[32,2048]{1,0:T(8,128)(2,1)S(1)} %pad_maximum_fusion.refs_0_), channel_id=1, source_target_pairs={{0,4},{4,0},{8,12},{12,8},{1,5},{5,1},{9,13},{13,9},{2,6},{6,2},{1... | collective-permute-start | bytes 393224 | tf_op jit(solution)/shard_map/ppermute | solution.py:156
  9.1 1.1 %collective-permute-start.4 = (s32[1,128]{1,0:T(1,128)S(1)}, s32[1,128]{1,0:T(1,128)S(1)}, u32[]{:S(2)}, u32[]{:S(2)}) collective-permute-start(s32[1,128]{1,0:T(1,128)S(1)} %shard_map.64.refs_6_.refs_5_), channel_id=1, source_target_pairs={{0,1},{1,0},{2,3},{3,2},{4,5},{5,4},{6,7},{7,6},{8,9},{9,8},{10,11... | collective-permute-start | bytes 1544 | tf_op jit(solution)/shard_map/ppermute | solution.py:156
  10.2 5.6 %collective-permute-start.5 = (bf16[16,2048]{1,0:T(8,128)(2,1)S(1)}, bf16[16,2048]{1,0:T(8,128)(2,1)S(1)}, u32[]{:S(2)}, u32[]{:S(2)}) collective-permute-start(bf16[16,2048]{1,0:T(8,128)(2,1)S(1)} %collective-permute-done.3.refs_2_), channel_id=1, source_target_pairs={{0,2},{2,0},{1,3},{3,1},{4,6},{6,4},{5,7},{7,5},{8,10},{10,8},{9,1... | collective-permute-start | bytes 196616 | tf_op jit(solution)/shard_map/ppermute | solution.py:156
  13.3 4.3 %collective-permute-start.6 = (bf16[16,2048]{1,0:T(8,128)(2,1)S(1)}, bf16[16,2048]{1,0:T(8,128)(2,1)S(1)}, u32[]{:S(2)}, u32[]{:S(2)}) collective-permute-start(bf16[16,2048]{1,0:T(8,128)(2,1)S(1)} %collective-permute-done.refs_4_), channel_id=1, source_target_pairs={{0,2},{2,0},{1,3},{3,1},{4,6},{6,4},{5,7},{7,5},{8,10},{10,8},{9,1... | collective-permute-start | bytes 196616 | tf_op jit(solution)/shard_map/ppermute | solution.py:156
  13.8 1.2 %copy-start.1 = (bf16[4,256,512]{2,1,0:T(8,128)(2,1)S(1)}, bf16[4,256,512]{2,1,0:T(8,128)(2,1)}, u32[]{:S(2)}) copy-start(bf16[4,256,512]{2,1,0:T(8,128)(2,1)} %refs_3_.1) | copy-start | bytes 3145732
  15.0 2.5 %copy-start.2 = (bf16[4,256,512]{2,1,0:T(8,128)(2,1)S(1)}, bf16[4,256,512]{2,1,0:T(8,128)(2,1)}, u32[]{:S(2)}) copy-start(bf16[4,256,512]{2,1,0:T(8,128)(2,1)} %refs_3_.1) | copy-start | bytes 3145732
  17.5 2.3 %copy-start.4 = (f32[4,256]{1,0:T(4,128)S(1)}, f32[4,256]{1,0:T(4,128)}, u32[]{:S(2)}) copy-start(f32[4,256]{1,0:T(4,128)} %refs_2_.1) | copy-start | bytes 12292
  18.6 1.2 %collective-permute-start.7 = (f32[4,256]{1,0:T(4,128)S(1)}, f32[4,256]{1,0:T(4,128)S(1)}, u32[]{:S(2)}, u32[]{:S(2)}) collective-permute-start(f32[4,256]{1,0:T(4,128)S(1)} %shard_map.66.refs_0_), channel_id=1, source_target_pairs={{0,1},{1,0},{2,3},{3,2},{4,5},{5,4},{6,7},{7,6},{8,9},{9,8},{10,11... | collective-permute-start | bytes 12296 | tf_op jit(solution)/shard_map/ppermute | solution.py:156
  21.2 4.9 %collective-permute-start.10 = (bf16[16,2048]{1,0:T(8,128)(2,1)S(1)}, bf16[16,2048]{1,0:T(8,128)(2,1)S(1)}, u32[]{:S(2)}, u32[]{:S(2)}) collective-permute-start(bf16[16,2048]{1,0:T(8,128)(2,1)S(1)} %get-tuple-element.28), channel_id=1, source_target_pairs={{0,2},{2,0},{1,3},{3,1},{4,6},{6,4},{5,7},{7,5},{8,10},{10,8},{9,1... | collective-permute-start | bytes 196616 | tf_op jit(solution)/shard_map/ppermute | solution.py:156
  21.8 6.3 %collective-permute-start.12 = (bf16[16,2048]{1,0:T(8,128)(2,1)S(1)}, bf16[16,2048]{1,0:T(8,128)(2,1)S(1)}, u32[]{:S(2)}, u32[]{:S(2)}) collective-permute-start(bf16[16,2048]{1,0:T(8,128)(2,1)S(1)} %get-tuple-element.30), channel_id=1, source_target_pairs={{0,2},{2,0},{1,3},{3,1},{4,6},{6,4},{5,7},{7,5},{8,10},{10,8},{9,1... | collective-permute-start | bytes 196616 | tf_op jit(solution)/shard_map/ppermute | solution.py:156
  23.3 6.2 %collective-permute-start.8 = (bf16[32,2048]{1,0:T(8,128)(2,1)S(1)}, bf16[32,2048]{1,0:T(8,128)(2,1)S(1)}, u32[]{:S(2)}, u32[]{:S(2)}) collective-permute-start(bf16[32,2048]{1,0:T(8,128)(2,1)S(1)} %get-tuple-element.26), channel_id=1, source_target_pairs={{0,4},{4,0},{8,12},{12,8},{1,5},{5,1},{9,13},{13,9},{2,6},{6,2},{1... | collective-permute-start | bytes 393224 | tf_op jit(solution)/shard_map/ppermute | solution.py:156
  26.1 6.3 %collective-permute-start.11 = (bf16[16,2048]{1,0:T(8,128)(2,1)S(1)}, bf16[16,2048]{1,0:T(8,128)(2,1)S(1)}, u32[]{:S(2)}, u32[]{:S(2)}) collective-permute-start(bf16[16,2048]{1,0:T(8,128)(2,1)S(1)} %add_convert_fusion.1), channel_id=1, source_target_pairs={{0,8},{4,12},{8,0},{12,4},{1,9},{5,13},{9,1},{13,5},{2,10},{6,14},... | collective-permute-start | bytes 196616 | tf_op jit(solution)/shard_map/ppermute | solution.py:156
  28.1 6.1 %collective-permute-start.13 = (bf16[16,2048]{1,0:T(8,128)(2,1)S(1)}, bf16[16,2048]{1,0:T(8,128)(2,1)S(1)}, u32[]{:S(2)}, u32[]{:S(2)}) collective-permute-start(bf16[16,2048]{1,0:T(8,128)(2,1)S(1)} %add_convert_fusion), channel_id=1, source_target_pairs={{0,12},{4,8},{8,4},{12,0},{1,13},{5,9},{9,5},{13,1},{2,14},{6,10},... | collective-permute-start | bytes 196616 | tf_op jit(solution)/shard_map/ppermute | solution.py:156
  29.5 6.1 %copy-start.3 = (bf16[16,4096]{1,0:T(8,128)(2,1)S(1)}, bf16[16,4096]{1,0:T(8,128)(2,1)}, u32[]{:S(2)}) copy-start(bf16[16,4096]{1,0:T(8,128)(2,1)} %core_ref.1) | copy-start | bytes 393220
  29.6 4.7 %collective-permute-start.9 = (bf16[16,2048]{1,0:T(8,128)(2,1)S(1)}, bf16[16,2048]{1,0:T(8,128)(2,1)S(1)}, u32[]{:S(2)}, u32[]{:S(2)}) collective-permute-start(bf16[16,2048]{1,0:T(8,128)(2,1)S(1)} %slice.17), channel_id=1, source_target_pairs={{0,2},{2,0},{1,3},{3,1},{4,6},{6,4},{5,7},{7,5},{8,10},{10,8},{9,1... | collective-permute-start | bytes 196616 | tf_op jit(solution)/shard_map/ppermute | solution.py:156
  34.3 1.4 %collective-permute-start.14 = (f32[16,2048]{1,0:T(8,128)S(1)}, f32[16,2048]{1,0:T(8,128)S(1)}, u32[]{:S(2)}, u32[]{:S(2)}) collective-permute-start(f32[16,2048]{1,0:T(8,128)S(1)} %fusion.1.mine_ref), channel_id=1, source_target_pairs={{0,1},{1,0},{2,3},{3,2},{4,5},{5,4},{6,7},{7,6},{8,9},{9,8},{10,11... | collective-permute-start | bytes 393224 | tf_op jit(solution)/shard_map/ppermute | solution.py:156

commit v24 on v12

--- a/solution.py
+++ b/solution.py
@@ -10,20 +10,12 @@
 GO = 64
 VMEM_LIMIT = 50 * 1024 * 1024
 NT = (((1,), (1,)), ((), ()))
-TN = (((0,), (0,)), ((), ()))
 
 
 def split_dot(left, right, dims=None):
     if dims is None:
         return jnp.dot(left, right, preferred_element_type=jnp.float32)
     return lax.dot_general(left, right, dims, preferred_element_type=jnp.float32)
-
-
-def three_parts(values):
-    top = values.astype(jnp.bfloat16)
-    left = values - top.astype(jnp.float32)
-    middle = left.astype(jnp.bfloat16)
-    return top, middle, (left - middle.astype(jnp.float32)).astype(jnp.bfloat16)
 
 
 def prepare_kernel(place_ref, half_ref, values_ref, own_ref, other_ref, left_ref, left_t_ref, pick_ref, put_ref):
@@ -39,8 +31,9 @@
         left_ref[t] = split_dot(values_ref[t], select, NT).astype(jnp.bfloat16)
         left_t_ref[t] = split_dot(select, values_ref[t], NT).astype(jnp.bfloat16)
     hot = row_table(place_ref, half_ref, own_ref, other_ref, put_ref.shape[0])
-    put_ref[...] = hot.astype(jnp.bfloat16)
     pick_ref[...] = hot.T.astype(jnp.bfloat16)
+    hot = hot.astype(jnp.bfloat16)
+    put_ref[...] = jnp.concatenate([hot, hot], axis=1)
 
 
 def index_kernel(held, fetch_ref, slots_ref, rows_ref):
@@ -75,11 +68,12 @@
     held = table.shape[0] // owners
     for ref, blocks in zip(piece_refs, places):
         table[blocks[0] * held:(blocks[-1] + 1) * held, :] = ref[...]
+    pick = pick_ref[...]
     low = lax.broadcasted_iota(jnp.int32, (1, 1, 1, groups, 128), 4) < GO
-    for chunk in range(table.shape[1] // 256):
-        wide = split_dot(pick_ref[...], table[:, chunk * 256:(chunk + 1) * 256])
-        for j in (2 * chunk, 2 * chunk + 1):
-            got = wide[:, (j % 2) * 128:(j % 2 + 1) * 128].reshape(2, batches, groups // 4, 2, groups, 128)
+    for chunk in range(table.shape[1] // 512):
+        wide = split_dot(pick, table[:, chunk * 512:(chunk + 1) * 512])
+        for j in range(4 * chunk, 4 * chunk + 4):
+            got = wide[:, (j % 4) * 128:(j % 4 + 1) * 128].reshape(2, batches, groups // 4, 2, groups, 128)
             even, odd = got[:, :, :, 0], got[:, :, :, 1]
             first = jnp.where(low, even, pltpu.roll(odd, GO, 4))
             second = jnp.where(low, pltpu.roll(even, GO, 4), odd)
@@ -88,20 +82,18 @@
                     at = (q // (groups // 4), t, q % (groups // 4))
                     both = jnp.concatenate([first[at], second[at]], axis=0)
                     dense[t, j * 2 * groups:(j + 1) * 2 * groups, q * 128:(q + 1) * 128] = both.astype(jnp.bfloat16)
-    ones = jnp.ones((8, 128), jnp.bfloat16)
     for t in range(batches):
         product = split_dot(left_ref[t], dense[t]) * values_ref[t].astype(jnp.float32)
         folded = product[:, :128]
         for q in range(1, columns // 128):
             folded = folded + product[:, q * 128:(q + 1) * 128]
-        top, middle, last = [split_dot(ones, part, NT) for part in three_parts(folded)]
-        out_ref[t:t + 1, :] = (top + middle + last)[:1]
+        out_ref[t:t + 1, :] = jnp.sum(folded.T, axis=0, keepdims=True)
 
 
 def scatter_kernel(places, *refs):
     mine_ref, far_ref, weight_ref, values_ref, left_t_ref, put_ref = refs[:6]
-    out_refs = refs[6:-2]
-    high, rest = refs[-2:]
+    out_refs = refs[6:-1]
+    terms = refs[-1]
     target = {k: (ref, i) for ref, blocks in zip(out_refs, places) for i, k in enumerate(blocks)}
     pieces = len(target)
     held = out_refs[0].shape[0] // len(places[0])
@@ -109,14 +101,11 @@
     groups = columns // GO
     kept = left_t_ref.shape[1]
     steps = kept // (2 * groups)
+    entries = batches * groups * groups
     potential = weight_ref[...] * jnp.tanh(mine_ref[...] + far_ref[...])
     low = lax.broadcasted_iota(jnp.int32, (1, groups, 128), 2) < GO
-    row = lax.broadcasted_iota(jnp.int32, (8, points), 0)
-    ones = jnp.ones((8, 128), jnp.bfloat16)
     for t in range(batches):
-        top, middle, last = [part.astype(jnp.float32) for part in three_parts(potential[t:t + 1, :])]
-        stacked = jnp.where(row == 0, top, jnp.where(row == 1, middle, jnp.where(row == 2, last, 0.0)))
-        factor = split_dot(stacked.astype(jnp.bfloat16), ones, TN)
+        factor = jnp.broadcast_to(potential[t:t + 1, :], (128, points)).T
         factor = jnp.concatenate([factor] * (columns // 128), axis=1)
         weighted = (values_ref[t].astype(jnp.float32) * factor).astype(jnp.bfloat16)
         part = split_dot(left_t_ref[t], weighted)
@@ -130,12 +119,13 @@
             for j in range(steps):
                 both = jnp.concatenate([even[j], odd[j]], axis=0)
                 top = both.astype(jnp.bfloat16)
-                high[at:at + 2 * groups, j * 128:(j + 1) * 128] = top
-                rest[at:at + 2 * groups, j * 128:(j + 1) * 128] = (both - top.astype(jnp.float32)).astype(jnp.bfloat16)
+                terms[at:at + 2 * groups, j * 128:(j + 1) * 128] = top
+                left = (both - top.astype(jnp.float32)).astype(jnp.bfloat16)
+                terms[entries + at:entries + at + 2 * groups, j * 128:(j + 1) * 128] = left
     step = max(1, min(pieces, 128 // held))
     for k in range(0, pieces, step):
         some = put_ref[k * held:(k + step) * held, :]
-        total = split_dot(some, high[...]) + split_dot(some, rest[...])
+        total = split_dot(some, terms[...])
         for i in range(step):
             ref, at = target[k + i]
             ref[at * held:(at + 1) * held, :] = total[i * held:(i + 1) * held, :].astype(jnp.bfloat16)
@@ -218,7 +208,7 @@
             jax.ShapeDtypeStruct((batches, points, kept), bf16),
             jax.ShapeDtypeStruct((batches, kept, points), bf16),
             jax.ShapeDtypeStruct((entries, table_rows), bf16),
-            jax.ShapeDtypeStruct((table_rows, entries), bf16),
+            jax.ShapeDtypeStruct((table_rows, 2 * entries), bf16),
         ),
         3,
         scalars=2,
@@ -243,7 +233,7 @@
         functools.partial(scatter_kernel, out_places),
         [jax.ShapeDtypeStruct((held * len(blocks), wide), bf16) for blocks in out_places],
         6,
-        scratch=(pltpu.VMEM((entries, wide), bf16), pltpu.VMEM((entries, wide), bf16)),
+        scratch=(pltpu.VMEM((2 * entries, wide), bf16),),
         flops=2 * batches * points * columns * kept,
         moved=2 * batches * points * columns * 2,
     )(partial, partial_other, point_weights, basis_values, left_t, put)

time: 37.6 us -> 36.5 us (0.971)
  Pallas kernels: 5.05 us -> 3.95 us
    pallas_call x1, Pallas kernels: 1.57 us -> 0.97 us  [per_device(): call(functools.partial(density_kernel, places), jax.ShapeDtypeStruct((bat...]
    pallas_call x1, Pallas kernels: 1.79 us -> 1.29 us  [per_device(): call(functools.partial(scatter_kernel, out_places), [jax.ShapeDtypeStruct...]
where the time goes in v24:
time: 36.5 us; the launch traced here: 36.3 us
  starting transfers between devices  15.5 us (42%)
  waiting for transfers between devices  13.8 us (38%)
  Pallas kernels  3.95 us (11%)
  local copies, waits for them, and re-layouts  2.84 us (8%)
    ppermute x15, starting transfers between devices, swap(): return lax.ppermute(array, axis, [(i, i ^ step) for i in range(count)])  15.5 us
    ppermute x15, waiting for transfers between devices, swap(): return lax.ppermute(array, axis, [(i, i ^ step) for i in range(count)])  13.8 us
    unnamed x14, local copies, waits for them, and re-layouts  2.74 us
    pallas_call x1, Pallas kernels, per_device(): call(functools.partial(scatter_kernel, out_places), [jax.ShapeDtypeStruct...  1.29 us
    pallas_call x1, Pallas kernels, per_device(): call(functools.partial(density_kernel, places), jax.ShapeDtypeStruct((bat...  0.97 us
    pallas_call x1, Pallas kernels, per_device(): call(prepare_kernel, (jax.ShapeDtypeStruct((batches, points, kept), bf16)...  0.77 us
  transfers between devices with their start and end apart: 15, of which 8 were waited for; matrix products, arithmetic and copies ran while one was open for 0% of the time, Pallas kernels for 3%

profile of v24, /device:TPU:0, one launch (start us, length us, event | category | flops | bytes accessed | tf_op | source)
XLA Modules:
  0.0 36.3 jit_solution(11940280457137314931)
XLA Ops:
  0.0 0.0 copy-start
  0.0 0.9 %copy-done = bf16[16,4096]{1,0:T(8,128)(2,1)S(1)} copy-done((bf16[16,4096]{1,0:T(8,128)(2,1)S(1)}, bf16[16,4096]{1,0:T(8,128)(2,1)}, u32[]{:S(2)}) %copy-start) | copy-done | bytes 131096
  0.9 0.0 copy-start.6
  0.9 3.0 %collective-permute-start.1 = (bf16[16,2048]{1,0:T(8,128)(2,1)S(1)}, bf16[16,2048]{1,0:T(8,128)(2,1)S(1)}, u32[]{:S(2)}, u32[]{:S(2)}) collective-permute-start(bf16[16,2048]{1,0:T(8,128)(2,1)S(1)} %constant_dynamic-slice_fusion), channel_id=1, source_target_pairs={{0,2},{2,0},{1,3},{3,1},{4,6},{6,4},{5,7},{7,5},{8,10},{10,8},{9,1... | collective-permute-start | bytes 196616 | tf_op jit(solution)/shard_map/ppermute | solution.py:158
  3.9 2.6 %collective-permute-start.3 = (bf16[16,2048]{1,0:T(8,128)(2,1)S(1)}, bf16[16,2048]{1,0:T(8,128)(2,1)S(1)}, u32[]{:S(2)}, u32[]{:S(2)}) collective-permute-start(bf16[16,2048]{1,0:T(8,128)(2,1)S(1)} %constant_dynamic-slice_fusion), channel_id=1, source_target_pairs={{0,8},{4,12},{8,0},{12,4},{1,9},{5,13},{9,1},{13,5},{2,10},{6,14},... | collective-permute-start | bytes 196616 | tf_op jit(solution)/shard_map/ppermute | solution.py:158
  6.5 1.3 %collective-permute-start = (bf16[16,2048]{1,0:T(8,128)(2,1)S(1)}, bf16[16,2048]{1,0:T(8,128)(2,1)S(1)}, u32[]{:S(2)}, u32[]{:S(2)}) collective-permute-start(bf16[16,2048]{1,0:T(8,128)(2,1)S(1)} %constant_dynamic-slice_fusion), channel_id=1, source_target_pairs={{0,12},{4,8},{8,4},{12,0},{1,13},{5,9},{9,5},{13,1},{2,14},{6,10},... | collective-permute-start | bytes 196616 | tf_op jit(solution)/shard_map/ppermute | solution.py:158
  7.9 0.0 copy-done.6
  7.9 0.1 reshape.14.slots_ref
  7.9 0.6 %copy-done.5 = s32[1,1,8,8]{3,2,1,0:T(8,128)S(1)} copy-done((s32[1,1,8,8]{3,2,1,0:T(8,128)S(1)}, s32[1,1,8,8]{3,2,1,0:T(8,128)}, u32[]{:S(2)}) %copy-start.5) | copy-done | bytes 280
  8.5 0.2 shard_map.64.own_ref
  8.7 0.0 collective-permute-done.1
  8.8 0.3 collective-permute-start.2
  9.1 0.0 collective-permute-start.4
  9.1 1.1 %collective-permute-done.4.other_ref = s32[1,128]{1,0:T(1,128)S(1)} collective-permute-done((s32[1,128]{1,0:T(1,128)S(1)}, s32[1,128]{1,0:T(1,128)S(1)}, u32[]{:S(2)}, u32[]{:S(2)}) %collective-permute-start.4) | collective-permute-done | bytes 544 | tf_op jit(solution)/shard_map/ppermute | solution.py:158
  10.2 0.0 collective-permute-done.3.refs_2_
  10.2 0.8 %collective-permute-start.5 = (bf16[16,2048]{1,0:T(8,128)(2,1)S(1)}, bf16[16,2048]{1,0:T(8,128)(2,1)S(1)}, u32[]{:S(2)}, u32[]{:S(2)}) collective-permute-start(bf16[16,2048]{1,0:T(8,128)(2,1)S(1)} %collective-permute-done.3.refs_2_), channel_id=1, source_target_pairs={{0,2},{2,0},{1,3},{3,1},{4,6},{6,4},{5,7},{7,5},{8,10},{10,8},{9,1... | collective-permute-start | bytes 196616 | tf_op jit(solution)/shard_map/ppermute | solution.py:158
  11.0 2.3 %collective-permute-done.refs_4_ = bf16[16,2048]{1,0:T(8,128)(2,1)S(1)} collective-permute-done((bf16[16,2048]{1,0:T(8,128)(2,1)S(1)}, bf16[16,2048]{1,0:T(8,128)(2,1)S(1)}, u32[]{:S(2)}, u32[]{:S(2)}) %collective-permute-start) | collective-permute-done | bytes 65568 | tf_op jit(solution)/shard_map/ppermute | solution.py:158
  13.3 0.5 %collective-permute-start.6 = (bf16[16,2048]{1,0:T(8,128)(2,1)S(1)}, bf16[16,2048]{1,0:T(8,128)(2,1)S(1)}, u32[]{:S(2)}, u32[]{:S(2)}) collective-permute-start(bf16[16,2048]{1,0:T(8,128)(2,1)S(1)} %collective-permute-done.refs_4_), channel_id=1, source_target_pairs={{0,2},{2,0},{1,3},{3,1},{4,6},{6,4},{5,7},{7,5},{8,10},{10,8},{9,1... | collective-permute-start | bytes 196616 | tf_op jit(solution)/shard_map/ppermute | solution.py:158
  13.8 0.0 copy-start.1
  13.8 1.2 %copy-done.1 = bf16[4,256,512]{2,1,0:T(8,128)(2,1)S(1)} copy-done((bf16[4,256,512]{2,1,0:T(8,128)(2,1)S(1)}, bf16[4,256,512]{2,1,0:T(8,128)(2,1)}, u32[]{:S(2)}) %copy-start.1) | copy-done | bytes 1048600
  15.0 0.0 copy-start.2
  15.0 0.8 %shard_map.65 = (bf16[4,256,256]{2,1,0:T(8,128)(2,1)S(1)}, bf16[4,256,256]{2,1,0:T(8,128)(2,1)S(1)}, bf16[256,128]{1,0:T(8,128)(2,1)S(1)}, bf16[128,512]{1,0:T(8,128)(2,1)S(1)}) custom-call(s32[1]{0:T(128)} %bitcast.3.place_ref, s32[1]{0:T(128)} %bitcast.half_ref, bf16[4,256,512]{2,1,0:T(8,128)(2,1)S(1)} %copy-done.1, s32[1,128]{1,0:T(1,128)S(1)} %shard_map.64.own_ref, ...), custom_call_target="tpu_custom_call" | custom-call | flops 536870912 | bytes 3145728 | tf_op jit(solution)/shard_map/pallas_call | solution.py:205
  15.8 0.0 collective-permute-done.5.refs_3_
  15.8 1.7 %collective-permute-done.6.refs_5_ = bf16[16,2048]{1,0:T(8,128)(2,1)S(1)} collective-permute-done((bf16[16,2048]{1,0:T(8,128)(2,1)S(1)}, bf16[16,2048]{1,0:T(8,128)(2,1)S(1)}, u32[]{:S(2)}, u32[]{:S(2)}) %collective-permute-start.6) | collective-permute-done | bytes 65568 | tf_op jit(solution)/shard_map/ppermute | solution.py:158
  17.5 0.0 collective-permute-done.2.refs_1_
  17.5 0.0 copy-done.2
  17.5 1.0 %shard_map.66.refs_0_ = f32[4,256]{1,0:T(4,128)S(1)} custom-call(bf16[32,2048]{1,0:T(8,128)(2,1)S(1)} %pad_maximum_fusion.refs_0_, bf16[32,2048]{1,0:T(8,128)(2,1)S(1)} %collective-permute-done.2.refs_1_, bf16[16,2048]{1,0:T(8,128)(2,1)S(1)} %collective-permute-done.3.refs_2_, bf16[16,2048]{1,0:T(8,128)(2,1)S(1)} %collective-permute-done.5.refs_3_, ...), custom_call_target="tpu_custom_call" | custom-call | flops 268435456 | bytes 2097152 | tf_op jit(solution)/shard_map/pallas_call | solution.py:220
  18.5 0.1 collective-permute-start.7
  18.6 1.2 %collective-permute-done.7.refs_1_ = f32[4,256]{1,0:T(4,128)S(1)} collective-permute-done((f32[4,256]{1,0:T(4,128)S(1)}, f32[4,256]{1,0:T(4,128)S(1)}, u32[]{:S(2)}, u32[]{:S(2)}) %collective-permute-start.7) | collective-permute-done | bytes 4128 | tf_op jit(solution)/shard_map/ppermute | solution.py:158
  19.7 0.0 copy-done.4
  19.7 1.3 %shard_map.67 = (bf16[32,2048]{1,0:T(8,128)(2,1)S(1)}, bf16[32,2048]{1,0:T(8,128)(2,1)S(1)}, bf16[16,2048]{1,0:T(8,128)(2,1)S(1)}, bf16[16,2048]{1,0:T(8,128)(2,...) custom-call(f32[4,256]{1,0:T(4,128)S(1)} %shard_map.66.refs_0_, ...), custom_call_target="tpu_custom_call" | custom-call | flops 268435456 | bytes 2097152 | tf_op jit(solution)/shard_map/pallas_call | solution.py:232
  21.0 0.6 %collective-permute-start.10 = (bf16[16,2048]{1,0:T(8,128)(2,1)S(1)}, bf16[16,2048]{1,0:T(8,128)(2,1)S(1)}, u32[]{:S(2)}, u32[]{:S(2)}) collective-permute-start(bf16[16,2048]{1,0:T(8,128)(2,1)S(1)} %get-tuple-element.32), channel_id=1, source_target_pairs={{0,2},{2,0},{1,3},{3,1},{4,6},{6,4},{5,7},{7,5},{8,10},{10,8},{9,1... | collective-permute-start | bytes 196616 | tf_op jit(solution)/shard_map/ppermute | solution.py:158
  21.6 1.5 %collective-permute-start.12 = (bf16[16,2048]{1,0:T(8,128)(2,1)S(1)}, bf16[16,2048]{1,0:T(8,128)(2,1)S(1)}, u32[]{:S(2)}, u32[]{:S(2)}) collective-permute-start(bf16[16,2048]{1,0:T(8,128)(2,1)S(1)} %get-tuple-element.34), channel_id=1, source_target_pairs={{0,2},{2,0},{1,3},{3,1},{4,6},{6,4},{5,7},{7,5},{8,10},{10,8},{9,1... | collective-permute-start | bytes 196616 | tf_op jit(solution)/shard_map/ppermute | solution.py:158
  23.1 0.1 collective-permute-start.8
  23.2 2.7 %collective-permute-done.10 = bf16[16,2048]{1,0:T(8,128)(2,1)S(1)} collective-permute-done((bf16[16,2048]{1,0:T(8,128)(2,1)S(1)}, bf16[16,2048]{1,0:T(8,128)(2,1)S(1)}, u32[]{:S(2)}, u32[]{:S(2)}) %collective-permute-start.10) | collective-permute-done | bytes 65568 | tf_op jit(solution)/shard_map/ppermute | solution.py:158
  26.0 2.0 %collective-permute-start.11 = (bf16[16,2048]{1,0:T(8,128)(2,1)S(1)}, bf16[16,2048]{1,0:T(8,128)(2,1)S(1)}, u32[]{:S(2)}, u32[]{:S(2)}) collective-permute-start(bf16[16,2048]{1,0:T(8,128)(2,1)S(1)} %add_convert_fusion.1), channel_id=1, source_target_pairs={{0,8},{4,12},{8,0},{12,4},{1,9},{5,13},{9,1},{13,5},{2,10},{6,14},... | collective-permute-start | bytes 196616 | tf_op jit(solution)/shard_map/ppermute | solution.py:158
  28.0 0.0 collective-permute-done.12
  28.0 1.4 %collective-permute-start.13 = (bf16[16,2048]{1,0:T(8,128)(2,1)S(1)}, bf16[16,2048]{1,0:T(8,128)(2,1)S(1)}, u32[]{:S(2)}, u32[]{:S(2)}) collective-permute-start(bf16[16,2048]{1,0:T(8,128)(2,1)S(1)} %add_convert_fusion), channel_id=1, source_target_pairs={{0,12},{4,8},{8,4},{12,0},{1,13},{5,9},{9,5},{13,1},{2,14},{6,10},... | collective-permute-start | bytes 196616 | tf_op jit(solution)/shard_map/ppermute | solution.py:158
  29.4 0.0 collective-permute-done.8
  29.4 0.0 copy-start.3
  29.4 1.3 %collective-permute-start.9 = (bf16[16,2048]{1,0:T(8,128)(2,1)S(1)}, bf16[16,2048]{1,0:T(8,128)(2,1)S(1)}, u32[]{:S(2)}, u32[]{:S(2)}) collective-permute-start(bf16[16,2048]{1,0:T(8,128)(2,1)S(1)} %slice.17), channel_id=1, source_target_pairs={{0,2},{2,0},{1,3},{3,1},{4,6},{6,4},{5,7},{7,5},{8,10},{10,8},{9,1... | collective-permute-start | bytes 196616 | tf_op jit(solution)/shard_map/ppermute | solution.py:158
  30.7 1.5 %collective-permute-done.11 = bf16[16,2048]{1,0:T(8,128)(2,1)S(1)} collective-permute-done((bf16[16,2048]{1,0:T(8,128)(2,1)S(1)}, bf16[16,2048]{1,0:T(8,128)(2,1)S(1)}, u32[]{:S(2)}, u32[]{:S(2)}) %collective-permute-start.11) | collective-permute-done | bytes 65568 | tf_op jit(solution)/shard_map/ppermute | solution.py:158
  32.3 1.8 %collective-permute-done.13 = bf16[16,2048]{1,0:T(8,128)(2,1)S(1)} collective-permute-done((bf16[16,2048]{1,0:T(8,128)(2,1)S(1)}, bf16[16,2048]{1,0:T(8,128)(2,1)S(1)}, u32[]{:S(2)}, u32[]{:S(2)}) %collective-permute-start.13) | collective-permute-done | bytes 65568 | tf_op jit(solution)/shard_map/ppermute | solution.py:158
  34.1 0.0 collective-permute-done.9
  34.2 0.1 collective-permute-start.14
  34.2 1.3 %collective-permute-done.14.other_ref = f32[16,2048]{1,0:T(8,128)S(1)} collective-permute-done((f32[16,2048]{1,0:T(8,128)S(1)}, f32[16,2048]{1,0:T(8,128)S(1)}, u32[]{:S(2)}, u32[]{:S(2)}) %collective-permute-start.14) | collective-permute-done | bytes 131104 | tf_op jit(solution)/shard_map/ppermute | solution.py:158
  35.6 0.0 copy-done.3
  35.6 0.7 %shard_map.68 = f32[16,4096]{1,0:T(8,128)} custom-call(s32[1]{0:T(128)} %bitcast.half_ref, f32[16,2048]{1,0:T(8,128)S(1)} %fusion.1.mine_ref, f32[16,2048]{1,0:T(8,128)S(1)} %collective-permute-done.14.other_ref, bf16[16,4096]{1,0:T(8,128)(2,1)S(1)} %copy-done.3), custom_call_target="tpu_custom_call" | custom-call | bytes 786432 | tf_op jit(solution)/shard_map/pallas_call | solution.py:257
  (9 shorter events, 0.1 us)
Async XLA Ops:
  0.0 0.9 %copy-start = (bf16[16,4096]{1,0:T(8,128)(2,1)S(1)}, bf16[16,4096]{1,0:T(8,128)(2,1)}, u32[]{:S(2)}) copy-start(bf16[16,4096]{1,0:T(8,128)(2,1)} %param.10) | copy-start | bytes 393220
  0.9 6.9 %copy-start.6 = (s32[4,8,4]{1,2,0:T(4,128)S(1)}, s32[4,8,4]{1,2,0:T(4,128)}, u32[]{:S(2)}) copy-start(s32[4,8,4]{1,2,0:T(4,128)} %param.8) | copy-start | bytes 1540
  0.9 7.8 %collective-permute-start.1 = (bf16[16,2048]{1,0:T(8,128)(2,1)S(1)}, bf16[16,2048]{1,0:T(8,128)(2,1)S(1)}, u32[]{:S(2)}, u32[]{:S(2)}) collective-permute-start(bf16[16,2048]{1,0:T(8,128)(2,1)S(1)} %constant_dynamic-slice_fusion), channel_id=1, source_target_pairs={{0,2},{2,0},{1,3},{3,1},{4,6},{6,4},{5,7},{7,5},{8,10},{10,8},{9,1... | collective-permute-start | bytes 196616 | tf_op jit(solution)/shard_map/ppermute | solution.py:158
  3.9 6.3 %collective-permute-start.3 = (bf16[16,2048]{1,0:T(8,128)(2,1)S(1)}, bf16[16,2048]{1,0:T(8,128)(2,1)S(1)}, u32[]{:S(2)}, u32[]{:S(2)}) collective-permute-start(bf16[16,2048]{1,0:T(8,128)(2,1)S(1)} %constant_dynamic-slice_fusion), channel_id=1, source_target_pairs={{0,8},{4,12},{8,0},{12,4},{1,9},{5,13},{9,1},{13,5},{2,10},{6,14},... | collective-permute-start | bytes 196616 | tf_op jit(solution)/shard_map/ppermute | solution.py:158
  6.5 6.8 %collective-permute-start = (bf16[16,2048]{1,0:T(8,128)(2,1)S(1)}, bf16[16,2048]{1,0:T(8,128)(2,1)S(1)}, u32[]{:S(2)}, u32[]{:S(2)}) collective-permute-start(bf16[16,2048]{1,0:T(8,128)(2,1)S(1)} %constant_dynamic-slice_fusion), channel_id=1, source_target_pairs={{0,12},{4,8},{8,4},{12,0},{1,13},{5,9},{9,5},{13,1},{2,14},{6,10},... | collective-permute-start | bytes 196616 | tf_op jit(solution)/shard_map/ppermute | solution.py:158
  7.9 0.7 %copy-start.5 = (s32[1,1,8,8]{3,2,1,0:T(8,128)S(1)}, s32[1,1,8,8]{3,2,1,0:T(8,128)}, u32[]{:S(2)}) copy-start(s32[1,1,8,8]{3,2,1,0:T(8,128)} %param.9) | copy-start | bytes 772
  8.8 8.8 %collective-permute-start.2 = (bf16[32,2048]{1,0:T(8,128)(2,1)S(1)}, bf16[32,2048]{1,0:T(8,128)(2,1)S(1)}, u32[]{:S(2)}, u32[]{:S(2)}) collective-permute-start(bf16[32,2048]{1,0:T(8,128)(2,1)S(1)} %pad_maximum_fusion.refs_0_), channel_id=1, source_target_pairs={{0,4},{4,0},{8,12},{12,8},{1,5},{5,1},{9,13},{13,9},{2,6},{6,2},{1... | collective-permute-start | bytes 393224 | tf_op jit(solution)/shard_map/ppermute | solution.py:158
  9.1 1.1 %collective-permute-start.4 = (s32[1,128]{1,0:T(1,128)S(1)}, s32[1,128]{1,0:T(1,128)S(1)}, u32[]{:S(2)}, u32[]{:S(2)}) collective-permute-start(s32[1,128]{1,0:T(1,128)S(1)} %shard_map.64.own_ref), channel_id=1, source_target_pairs={{0,1},{1,0},{2,3},{3,2},{4,5},{5,4},{6,7},{7,6},{8,9},{9,8},{10,11... | collective-permute-start | bytes 1544 | tf_op jit(solution)/shard_map/ppermute | solution.py:158
  10.2 5.6 %collective-permute-start.5 = (bf16[16,2048]{1,0:T(8,128)(2,1)S(1)}, bf16[16,2048]{1,0:T(8,128)(2,1)S(1)}, u32[]{:S(2)}, u32[]{:S(2)}) collective-permute-start(bf16[16,2048]{1,0:T(8,128)(2,1)S(1)} %collective-permute-done.3.refs_2_), channel_id=1, source_target_pairs={{0,2},{2,0},{1,3},{3,1},{4,6},{6,4},{5,7},{7,5},{8,10},{10,8},{9,1... | collective-permute-start | bytes 196616 | tf_op jit(solution)/shard_map/ppermute | solution.py:158
  13.3 4.3 %collective-permute-start.6 = (bf16[16,2048]{1,0:T(8,128)(2,1)S(1)}, bf16[16,2048]{1,0:T(8,128)(2,1)S(1)}, u32[]{:S(2)}, u32[]{:S(2)}) collective-permute-start(bf16[16,2048]{1,0:T(8,128)(2,1)S(1)} %collective-permute-done.refs_4_), channel_id=1, source_target_pairs={{0,2},{2,0},{1,3},{3,1},{4,6},{6,4},{5,7},{7,5},{8,10},{10,8},{9,1... | collective-permute-start | bytes 196616 | tf_op jit(solution)/shard_map/ppermute | solution.py:158
  13.8 1.2 %copy-start.1 = (bf16[4,256,512]{2,1,0:T(8,128)(2,1)S(1)}, bf16[4,256,512]{2,1,0:T(8,128)(2,1)}, u32[]{:S(2)}) copy-start(bf16[4,256,512]{2,1,0:T(8,128)(2,1)} %refs_3_.1) | copy-start | bytes 3145732
  15.0 2.5 %copy-start.2 = (bf16[4,256,512]{2,1,0:T(8,128)(2,1)S(1)}, bf16[4,256,512]{2,1,0:T(8,128)(2,1)}, u32[]{:S(2)}) copy-start(bf16[4,256,512]{2,1,0:T(8,128)(2,1)} %refs_3_.1) | copy-start | bytes 3145732
  17.5 2.2 %copy-start.4 = (f32[4,256]{1,0:T(4,128)S(1)}, f32[4,256]{1,0:T(4,128)}, u32[]{:S(2)}) copy-start(f32[4,256]{1,0:T(4,128)} %refs_2_.1) | copy-start | bytes 12292
  18.5 1.2 %collective-permute-start.7 = (f32[4,256]{1,0:T(4,128)S(1)}, f32[4,256]{1,0:T(4,128)S(1)}, u32[]{:S(2)}, u32[]{:S(2)}) collective-permute-start(f32[4,256]{1,0:T(4,128)S(1)} %shard_map.66.refs_0_), channel_id=1, source_target_pairs={{0,1},{1,0},{2,3},{3,2},{4,5},{5,4},{6,7},{7,6},{8,9},{9,8},{10,11... | collective-permute-start | bytes 12296 | tf_op jit(solution)/shard_map/ppermute | solution.py:158
  21.0 4.9 %collective-permute-start.10 = (bf16[16,2048]{1,0:T(8,128)(2,1)S(1)}, bf16[16,2048]{1,0:T(8,128)(2,1)S(1)}, u32[]{:S(2)}, u32[]{:S(2)}) collective-permute-start(bf16[16,2048]{1,0:T(8,128)(2,1)S(1)} %get-tuple-element.32), channel_id=1, source_target_pairs={{0,2},{2,0},{1,3},{3,1},{4,6},{6,4},{5,7},{7,5},{8,10},{10,8},{9,1... | collective-permute-start | bytes 196616 | tf_op jit(solution)/shard_map/ppermute | solution.py:158
  21.6 6.3 %collective-permute-start.12 = (bf16[16,2048]{1,0:T(8,128)(2,1)S(1)}, bf16[16,2048]{1,0:T(8,128)(2,1)S(1)}, u32[]{:S(2)}, u32[]{:S(2)}) collective-permute-start(bf16[16,2048]{1,0:T(8,128)(2,1)S(1)} %get-tuple-element.34), channel_id=1, source_target_pairs={{0,2},{2,0},{1,3},{3,1},{4,6},{6,4},{5,7},{7,5},{8,10},{10,8},{9,1... | collective-permute-start | bytes 196616 | tf_op jit(solution)/shard_map/ppermute | solution.py:158
  23.1 6.3 %collective-permute-start.8 = (bf16[32,2048]{1,0:T(8,128)(2,1)S(1)}, bf16[32,2048]{1,0:T(8,128)(2,1)S(1)}, u32[]{:S(2)}, u32[]{:S(2)}) collective-permute-start(bf16[32,2048]{1,0:T(8,128)(2,1)S(1)} %get-tuple-element.30), channel_id=1, source_target_pairs={{0,4},{4,0},{8,12},{12,8},{1,5},{5,1},{9,13},{13,9},{2,6},{6,2},{1... | collective-permute-start | bytes 393224 | tf_op jit(solution)/shard_map/ppermute | solution.py:158
  26.0 6.3 %collective-permute-start.11 = (bf16[16,2048]{1,0:T(8,128)(2,1)S(1)}, bf16[16,2048]{1,0:T(8,128)(2,1)S(1)}, u32[]{:S(2)}, u32[]{:S(2)}) collective-permute-start(bf16[16,2048]{1,0:T(8,128)(2,1)S(1)} %add_convert_fusion.1), channel_id=1, source_target_pairs={{0,8},{4,12},{8,0},{12,4},{1,9},{5,13},{9,1},{13,5},{2,10},{6,14},... | collective-permute-start | bytes 196616 | tf_op jit(solution)/shard_map/ppermute | solution.py:158
  28.0 6.1 %collective-permute-start.13 = (bf16[16,2048]{1,0:T(8,128)(2,1)S(1)}, bf16[16,2048]{1,0:T(8,128)(2,1)S(1)}, u32[]{:S(2)}, u32[]{:S(2)}) collective-permute-start(bf16[16,2048]{1,0:T(8,128)(2,1)S(1)} %add_convert_fusion), channel_id=1, source_target_pairs={{0,12},{4,8},{8,4},{12,0},{1,13},{5,9},{9,5},{13,1},{2,14},{6,10},... | collective-permute-start | bytes 196616 | tf_op jit(solution)/shard_map/ppermute | solution.py:158
  29.4 6.1 %copy-start.3 = (bf16[16,4096]{1,0:T(8,128)(2,1)S(1)}, bf16[16,4096]{1,0:T(8,128)(2,1)}, u32[]{:S(2)}) copy-start(bf16[16,4096]{1,0:T(8,128)(2,1)} %core_ref.1) | copy-start | bytes 393220
  29.4 4.7 %collective-permute-start.9 = (bf16[16,2048]{1,0:T(8,128)(2,1)S(1)}, bf16[16,2048]{1,0:T(8,128)(2,1)S(1)}, u32[]{:S(2)}, u32[]{:S(2)}) collective-permute-start(bf16[16,2048]{1,0:T(8,128)(2,1)S(1)} %slice.17), channel_id=1, source_target_pairs={{0,2},{2,0},{1,3},{3,1},{4,6},{6,4},{5,7},{7,5},{8,10},{10,8},{9,1... | collective-permute-start | bytes 196616 | tf_op jit(solution)/shard_map/ppermute | solution.py:158
  34.2 1.4 %collective-permute-start.14 = (f32[16,2048]{1,0:T(8,128)S(1)}, f32[16,2048]{1,0:T(8,128)S(1)}, u32[]{:S(2)}, u32[]{:S(2)}) collective-permute-start(f32[16,2048]{1,0:T(8,128)S(1)} %fusion.1.mine_ref), channel_id=1, source_target_pairs={{0,1},{1,0},{2,3},{3,2},{4,5},{5,4},{6,7},{7,6},{8,9},{9,8},{10,11... | collective-permute-start | bytes 393224 | tf_op jit(solution)/shard_map/ppermute | solution.py:158

commit v25 on v24

--- a/solution.py
+++ b/solution.py
@@ -61,17 +61,15 @@
 
 def density_kernel(places, *refs):
     piece_refs = refs[:len(places)]
-    pick_ref, left_ref, values_ref, out_ref, table, dense = refs[len(places):]
+    pick_ref, left_ref, values_ref, out_ref, dense = refs[len(places):]
     batches, points, columns = values_ref.shape
     groups = columns // GO
-    owners = sum(len(blocks) for blocks in places)
-    held = table.shape[0] // owners
-    for ref, blocks in zip(piece_refs, places):
-        table[blocks[0] * held:(blocks[-1] + 1) * held, :] = ref[...]
+    assert [k for blocks in places for k in blocks] == list(range(sum(len(blocks) for blocks in places)))
     pick = pick_ref[...]
     low = lax.broadcasted_iota(jnp.int32, (1, 1, 1, groups, 128), 4) < GO
-    for chunk in range(table.shape[1] // 512):
-        wide = split_dot(pick, table[:, chunk * 512:(chunk + 1) * 512])
+    for chunk in range(piece_refs[0].shape[1] // 512):
+        table = jnp.concatenate([ref[:, chunk * 512:(chunk + 1) * 512] for ref in piece_refs], axis=0)
+        wide = split_dot(pick, table)
         for j in range(4 * chunk, 4 * chunk + 4):
             got = wide[:, (j % 4) * 128:(j % 4 + 1) * 128].reshape(2, batches, groups // 4, 2, groups, 128)
             even, odd = got[:, :, :, 0], got[:, :, :, 1]
@@ -221,7 +219,7 @@
         functools.partial(density_kernel, places),
         jax.ShapeDtypeStruct((batches, points), f32),
         len(arrays) + 3,
-        scratch=(pltpu.VMEM((table_rows, wide), bf16), pltpu.VMEM((batches, kept, columns), bf16)),
+        scratch=(pltpu.VMEM((batches, kept, columns), bf16),),
         flops=2 * batches * points * columns * kept,
         moved=2 * batches * points * columns * 2,
     )(*arrays, pick, left, basis_values)

time: 36.5 us -> 36.5 us (level)
  no operation moved by 1% of the time
where the time goes in v25:
time: 36.5 us; the launch traced here: 36.3 us
  starting transfers between devices  15.5 us (42%)
  waiting for transfers between devices  13.8 us (38%)
  Pallas kernels  3.95 us (11%)
  local copies, waits for them, and re-layouts  2.84 us (8%)
    ppermute x15, starting transfers between devices, swap(): return lax.ppermute(array, axis, [(i, i ^ step) for i in range(count)])  15.5 us
    ppermute x15, waiting for transfers between devices, swap(): return lax.ppermute(array, axis, [(i, i ^ step) for i in range(count)])  13.8 us
    unnamed x14, local copies, waits for them, and re-layouts  2.74 us
    pallas_call x1, Pallas kernels, per_device(): call(functools.partial(scatter_kernel, out_places), [jax.ShapeDtypeStruct...  1.29 us
    pallas_call x1, Pallas kernels, per_device(): call(functools.partial(density_kernel, places), jax.ShapeDtypeStruct((bat...  0.97 us
    pallas_call x1, Pallas kernels, per_device(): call(prepare_kernel, (jax.ShapeDtypeStruct((batches, points, kept), bf16)...  0.77 us
  transfers between devices with their start and end apart: 15, of which 8 were waited for; matrix products, arithmetic and copies ran while one was open for 0% of the time, Pallas kernels for 3%

profile of v25, /device:TPU:0, one launch (start us, length us, event | category | flops | bytes accessed | tf_op | source)
XLA Modules:
  0.0 36.3 jit_solution(11940280457137314931)
XLA Ops:
  0.0 0.0 copy-start
  0.0 0.9 %copy-done = bf16[16,4096]{1,0:T(8,128)(2,1)S(1)} copy-done((bf16[16,4096]{1,0:T(8,128)(2,1)S(1)}, bf16[16,4096]{1,0:T(8,128)(2,1)}, u32[]{:S(2)}) %copy-start) | copy-done | bytes 131096
  0.9 0.0 copy-start.6
  0.9 3.0 %collective-permute-start.1 = (bf16[16,2048]{1,0:T(8,128)(2,1)S(1)}, bf16[16,2048]{1,0:T(8,128)(2,1)S(1)}, u32[]{:S(2)}, u32[]{:S(2)}) collective-permute-start(bf16[16,2048]{1,0:T(8,128)(2,1)S(1)} %constant_dynamic-slice_fusion), channel_id=1, source_target_pairs={{0,2},{2,0},{1,3},{3,1},{4,6},{6,4},{5,7},{7,5},{8,10},{10,8},{9,1... | collective-permute-start | bytes 196616 | tf_op jit(solution)/shard_map/ppermute | solution.py:156
  3.9 2.6 %collective-permute-start.3 = (bf16[16,2048]{1,0:T(8,128)(2,1)S(1)}, bf16[16,2048]{1,0:T(8,128)(2,1)S(1)}, u32[]{:S(2)}, u32[]{:S(2)}) collective-permute-start(bf16[16,2048]{1,0:T(8,128)(2,1)S(1)} %constant_dynamic-slice_fusion), channel_id=1, source_target_pairs={{0,8},{4,12},{8,0},{12,4},{1,9},{5,13},{9,1},{13,5},{2,10},{6,14},... | collective-permute-start | bytes 196616 | tf_op jit(solution)/shard_map/ppermute | solution.py:156
  6.5 1.3 %collective-permute-start = (bf16[16,2048]{1,0:T(8,128)(2,1)S(1)}, bf16[16,2048]{1,0:T(8,128)(2,1)S(1)}, u32[]{:S(2)}, u32[]{:S(2)}) collective-permute-start(bf16[16,2048]{1,0:T(8,128)(2,1)S(1)} %constant_dynamic-slice_fusion), channel_id=1, source_target_pairs={{0,12},{4,8},{8,4},{12,0},{1,13},{5,9},{9,5},{13,1},{2,14},{6,10},... | collective-permute-start | bytes 196616 | tf_op jit(solution)/shard_map/ppermute | solution.py:156
  7.9 0.0 copy-done.6
  7.9 0.1 reshape.14.slots_ref
  7.9 0.6 %copy-done.5 = s32[1,1,8,8]{3,2,1,0:T(8,128)S(1)} copy-done((s32[1,1,8,8]{3,2,1,0:T(8,128)S(1)}, s32[1,1,8,8]{3,2,1,0:T(8,128)}, u32[]{:S(2)}) %copy-start.5) | copy-done | bytes 280
  8.5 0.2 shard_map.64.own_ref
  8.7 0.0 collective-permute-done.1
  8.8 0.3 collective-permute-start.2
  9.1 0.0 collective-permute-start.4
  9.1 1.1 %collective-permute-done.4.other_ref = s32[1,128]{1,0:T(1,128)S(1)} collective-permute-done((s32[1,128]{1,0:T(1,128)S(1)}, s32[1,128]{1,0:T(1,128)S(1)}, u32[]{:S(2)}, u32[]{:S(2)}) %collective-permute-start.4) | collective-permute-done | bytes 544 | tf_op jit(solution)/shard_map/ppermute | solution.py:156
  10.2 0.0 collective-permute-done.3.refs_2_
  10.2 0.8 %collective-permute-start.5 = (bf16[16,2048]{1,0:T(8,128)(2,1)S(1)}, bf16[16,2048]{1,0:T(8,128)(2,1)S(1)}, u32[]{:S(2)}, u32[]{:S(2)}) collective-permute-start(bf16[16,2048]{1,0:T(8,128)(2,1)S(1)} %collective-permute-done.3.refs_2_), channel_id=1, source_target_pairs={{0,2},{2,0},{1,3},{3,1},{4,6},{6,4},{5,7},{7,5},{8,10},{10,8},{9,1... | collective-permute-start | bytes 196616 | tf_op jit(solution)/shard_map/ppermute | solution.py:156
  11.0 2.3 %collective-permute-done.refs_4_ = bf16[16,2048]{1,0:T(8,128)(2,1)S(1)} collective-permute-done((bf16[16,2048]{1,0:T(8,128)(2,1)S(1)}, bf16[16,2048]{1,0:T(8,128)(2,1)S(1)}, u32[]{:S(2)}, u32[]{:S(2)}) %collective-permute-start) | collective-permute-done | bytes 65568 | tf_op jit(solution)/shard_map/ppermute | solution.py:156
  13.3 0.5 %collective-permute-start.6 = (bf16[16,2048]{1,0:T(8,128)(2,1)S(1)}, bf16[16,2048]{1,0:T(8,128)(2,1)S(1)}, u32[]{:S(2)}, u32[]{:S(2)}) collective-permute-start(bf16[16,2048]{1,0:T(8,128)(2,1)S(1)} %collective-permute-done.refs_4_), channel_id=1, source_target_pairs={{0,2},{2,0},{1,3},{3,1},{4,6},{6,4},{5,7},{7,5},{8,10},{10,8},{9,1... | collective-permute-start | bytes 196616 | tf_op jit(solution)/shard_map/ppermute | solution.py:156
  13.8 0.0 copy-start.1
  13.8 1.2 %copy-done.1 = bf16[4,256,512]{2,1,0:T(8,128)(2,1)S(1)} copy-done((bf16[4,256,512]{2,1,0:T(8,128)(2,1)S(1)}, bf16[4,256,512]{2,1,0:T(8,128)(2,1)}, u32[]{:S(2)}) %copy-start.1) | copy-done | bytes 1048600
  15.0 0.0 copy-start.2
  15.0 0.8 %shard_map.65 = (bf16[4,256,256]{2,1,0:T(8,128)(2,1)S(1)}, bf16[4,256,256]{2,1,0:T(8,128)(2,1)S(1)}, bf16[256,128]{1,0:T(8,128)(2,1)S(1)}, bf16[128,512]{1,0:T(8,128)(2,1)S(1)}) custom-call(s32[1]{0:T(128)} %bitcast.3.place_ref, s32[1]{0:T(128)} %bitcast.half_ref, bf16[4,256,512]{2,1,0:T(8,128)(2,1)S(1)} %copy-done.1, s32[1,128]{1,0:T(1,128)S(1)} %shard_map.64.own_ref, ...), custom_call_target="tpu_custom_call" | custom-call | flops 536870912 | bytes 3145728 | tf_op jit(solution)/shard_map/pallas_call | solution.py:203
  15.8 0.0 collective-permute-done.5.refs_3_
  15.8 1.7 %collective-permute-done.6.refs_5_ = bf16[16,2048]{1,0:T(8,128)(2,1)S(1)} collective-permute-done((bf16[16,2048]{1,0:T(8,128)(2,1)S(1)}, bf16[16,2048]{1,0:T(8,128)(2,1)S(1)}, u32[]{:S(2)}, u32[]{:S(2)}) %collective-permute-start.6) | collective-permute-done | bytes 65568 | tf_op jit(solution)/shard_map/ppermute | solution.py:156
  17.5 0.0 collective-permute-done.2.refs_1_
  17.5 0.0 copy-done.2
  17.5 1.0 %shard_map.66.refs_0_ = f32[4,256]{1,0:T(4,128)S(1)} custom-call(bf16[32,2048]{1,0:T(8,128)(2,1)S(1)} %pad_maximum_fusion.refs_0_, bf16[32,2048]{1,0:T(8,128)(2,1)S(1)} %collective-permute-done.2.refs_1_, bf16[16,2048]{1,0:T(8,128)(2,1)S(1)} %collective-permute-done.3.refs_2_, bf16[16,2048]{1,0:T(8,128)(2,1)S(1)} %collective-permute-done.5.refs_3_, ...), custom_call_target="tpu_custom_call" | custom-call | flops 268435456 | bytes 2097152 | tf_op jit(solution)/shard_map/pallas_call | solution.py:218
  18.5 0.1 collective-permute-start.7
  18.6 1.2 %collective-permute-done.7.refs_1_ = f32[4,256]{1,0:T(4,128)S(1)} collective-permute-done((f32[4,256]{1,0:T(4,128)S(1)}, f32[4,256]{1,0:T(4,128)S(1)}, u32[]{:S(2)}, u32[]{:S(2)}) %collective-permute-start.7) | collective-permute-done | bytes 4128 | tf_op jit(solution)/shard_map/ppermute | solution.py:156
  19.7 0.0 copy-done.4
  19.7 1.3 %shard_map.67 = (bf16[32,2048]{1,0:T(8,128)(2,1)S(1)}, bf16[32,2048]{1,0:T(8,128)(2,1)S(1)}, bf16[16,2048]{1,0:T(8,128)(2,1)S(1)}, bf16[16,2048]{1,0:T(8,128)(2,...) custom-call(f32[4,256]{1,0:T(4,128)S(1)} %shard_map.66.refs_0_, ...), custom_call_target="tpu_custom_call" | custom-call | flops 268435456 | bytes 2097152 | tf_op jit(solution)/shard_map/pallas_call | solution.py:230
  21.0 0.6 %collective-permute-start.10 = (bf16[16,2048]{1,0:T(8,128)(2,1)S(1)}, bf16[16,2048]{1,0:T(8,128)(2,1)S(1)}, u32[]{:S(2)}, u32[]{:S(2)}) collective-permute-start(bf16[16,2048]{1,0:T(8,128)(2,1)S(1)} %get-tuple-element.32), channel_id=1, source_target_pairs={{0,2},{2,0},{1,3},{3,1},{4,6},{6,4},{5,7},{7,5},{8,10},{10,8},{9,1... | collective-permute-start | bytes 196616 | tf_op jit(solution)/shard_map/ppermute | solution.py:156
  21.6 1.5 %collective-permute-start.12 = (bf16[16,2048]{1,0:T(8,128)(2,1)S(1)}, bf16[16,2048]{1,0:T(8,128)(2,1)S(1)}, u32[]{:S(2)}, u32[]{:S(2)}) collective-permute-start(bf16[16,2048]{1,0:T(8,128)(2,1)S(1)} %get-tuple-element.34), channel_id=1, source_target_pairs={{0,2},{2,0},{1,3},{3,1},{4,6},{6,4},{5,7},{7,5},{8,10},{10,8},{9,1... | collective-permute-start | bytes 196616 | tf_op jit(solution)/shard_map/ppermute | solution.py:156
  23.1 0.1 collective-permute-start.8
  23.2 2.7 %collective-permute-done.10 = bf16[16,2048]{1,0:T(8,128)(2,1)S(1)} collective-permute-done((bf16[16,2048]{1,0:T(8,128)(2,1)S(1)}, bf16[16,2048]{1,0:T(8,128)(2,1)S(1)}, u32[]{:S(2)}, u32[]{:S(2)}) %collective-permute-start.10) | collective-permute-done | bytes 65568 | tf_op jit(solution)/shard_map/ppermute | solution.py:156
  26.0 2.0 %collective-permute-start.11 = (bf16[16,2048]{1,0:T(8,128)(2,1)S(1)}, bf16[16,2048]{1,0:T(8,128)(2,1)S(1)}, u32[]{:S(2)}, u32[]{:S(2)}) collective-permute-start(bf16[16,2048]{1,0:T(8,128)(2,1)S(1)} %add_convert_fusion.1), channel_id=1, source_target_pairs={{0,8},{4,12},{8,0},{12,4},{1,9},{5,13},{9,1},{13,5},{2,10},{6,14},... | collective-permute-start | bytes 196616 | tf_op jit(solution)/shard_map/ppermute | solution.py:156
  28.0 0.0 collective-permute-done.12
  28.0 1.4 %collective-permute-start.13 = (bf16[16,2048]{1,0:T(8,128)(2,1)S(1)}, bf16[16,2048]{1,0:T(8,128)(2,1)S(1)}, u32[]{:S(2)}, u32[]{:S(2)}) collective-permute-start(bf16[16,2048]{1,0:T(8,128)(2,1)S(1)} %add_convert_fusion), channel_id=1, source_target_pairs={{0,12},{4,8},{8,4},{12,0},{1,13},{5,9},{9,5},{13,1},{2,14},{6,10},... | collective-permute-start | bytes 196616 | tf_op jit(solution)/shard_map/ppermute | solution.py:156
  29.4 0.0 collective-permute-done.8
  29.4 0.0 copy-start.3
  29.4 1.3 %collective-permute-start.9 = (bf16[16,2048]{1,0:T(8,128)(2,1)S(1)}, bf16[16,2048]{1,0:T(8,128)(2,1)S(1)}, u32[]{:S(2)}, u32[]{:S(2)}) collective-permute-start(bf16[16,2048]{1,0:T(8,128)(2,1)S(1)} %slice.17), channel_id=1, source_target_pairs={{0,2},{2,0},{1,3},{3,1},{4,6},{6,4},{5,7},{7,5},{8,10},{10,8},{9,1... | collective-permute-start | bytes 196616 | tf_op jit(solution)/shard_map/ppermute | solution.py:156
  30.7 1.5 %collective-permute-done.11 = bf16[16,2048]{1,0:T(8,128)(2,1)S(1)} collective-permute-done((bf16[16,2048]{1,0:T(8,128)(2,1)S(1)}, bf16[16,2048]{1,0:T(8,128)(2,1)S(1)}, u32[]{:S(2)}, u32[]{:S(2)}) %collective-permute-start.11) | collective-permute-done | bytes 65568 | tf_op jit(solution)/shard_map/ppermute | solution.py:156
  32.3 1.8 %collective-permute-done.13 = bf16[16,2048]{1,0:T(8,128)(2,1)S(1)} collective-permute-done((bf16[16,2048]{1,0:T(8,128)(2,1)S(1)}, bf16[16,2048]{1,0:T(8,128)(2,1)S(1)}, u32[]{:S(2)}, u32[]{:S(2)}) %collective-permute-start.13) | collective-permute-done | bytes 65568 | tf_op jit(solution)/shard_map/ppermute | solution.py:156
  34.1 0.0 collective-permute-done.9
  34.2 0.1 collective-permute-start.14
  34.2 1.3 %collective-permute-done.14.other_ref = f32[16,2048]{1,0:T(8,128)S(1)} collective-permute-done((f32[16,2048]{1,0:T(8,128)S(1)}, f32[16,2048]{1,0:T(8,128)S(1)}, u32[]{:S(2)}, u32[]{:S(2)}) %collective-permute-start.14) | collective-permute-done | bytes 131104 | tf_op jit(solution)/shard_map/ppermute | solution.py:156
  35.6 0.0 copy-done.3
  35.6 0.7 %shard_map.68 = f32[16,4096]{1,0:T(8,128)} custom-call(s32[1]{0:T(128)} %bitcast.half_ref, f32[16,2048]{1,0:T(8,128)S(1)} %fusion.1.mine_ref, f32[16,2048]{1,0:T(8,128)S(1)} %collective-permute-done.14.other_ref, bf16[16,4096]{1,0:T(8,128)(2,1)S(1)} %copy-done.3), custom_call_target="tpu_custom_call" | custom-call | bytes 786432 | tf_op jit(solution)/shard_map/pallas_call | solution.py:255
  (9 shorter events, 0.1 us)
Async XLA Ops:
  0.0 0.9 %copy-start = (bf16[16,4096]{1,0:T(8,128)(2,1)S(1)}, bf16[16,4096]{1,0:T(8,128)(2,1)}, u32[]{:S(2)}) copy-start(bf16[16,4096]{1,0:T(8,128)(2,1)} %param.10) | copy-start | bytes 393220
  0.9 6.9 %copy-start.6 = (s32[4,8,4]{1,2,0:T(4,128)S(1)}, s32[4,8,4]{1,2,0:T(4,128)}, u32[]{:S(2)}) copy-start(s32[4,8,4]{1,2,0:T(4,128)} %param.8) | copy-start | bytes 1540
  0.9 7.8 %collective-permute-start.1 = (bf16[16,2048]{1,0:T(8,128)(2,1)S(1)}, bf16[16,2048]{1,0:T(8,128)(2,1)S(1)}, u32[]{:S(2)}, u32[]{:S(2)}) collective-permute-start(bf16[16,2048]{1,0:T(8,128)(2,1)S(1)} %constant_dynamic-slice_fusion), channel_id=1, source_target_pairs={{0,2},{2,0},{1,3},{3,1},{4,6},{6,4},{5,7},{7,5},{8,10},{10,8},{9,1... | collective-permute-start | bytes 196616 | tf_op jit(solution)/shard_map/ppermute | solution.py:156
  3.9 6.3 %collective-permute-start.3 = (bf16[16,2048]{1,0:T(8,128)(2,1)S(1)}, bf16[16,2048]{1,0:T(8,128)(2,1)S(1)}, u32[]{:S(2)}, u32[]{:S(2)}) collective-permute-start(bf16[16,2048]{1,0:T(8,128)(2,1)S(1)} %constant_dynamic-slice_fusion), channel_id=1, source_target_pairs={{0,8},{4,12},{8,0},{12,4},{1,9},{5,13},{9,1},{13,5},{2,10},{6,14},... | collective-permute-start | bytes 196616 | tf_op jit(solution)/shard_map/ppermute | solution.py:156
  6.5 6.8 %collective-permute-start = (bf16[16,2048]{1,0:T(8,128)(2,1)S(1)}, bf16[16,2048]{1,0:T(8,128)(2,1)S(1)}, u32[]{:S(2)}, u32[]{:S(2)}) collective-permute-start(bf16[16,2048]{1,0:T(8,128)(2,1)S(1)} %constant_dynamic-slice_fusion), channel_id=1, source_target_pairs={{0,12},{4,8},{8,4},{12,0},{1,13},{5,9},{9,5},{13,1},{2,14},{6,10},... | collective-permute-start | bytes 196616 | tf_op jit(solution)/shard_map/ppermute | solution.py:156
  7.9 0.7 %copy-start.5 = (s32[1,1,8,8]{3,2,1,0:T(8,128)S(1)}, s32[1,1,8,8]{3,2,1,0:T(8,128)}, u32[]{:S(2)}) copy-start(s32[1,1,8,8]{3,2,1,0:T(8,128)} %param.9) | copy-start | bytes 772
  8.8 8.8 %collective-permute-start.2 = (bf16[32,2048]{1,0:T(8,128)(2,1)S(1)}, bf16[32,2048]{1,0:T(8,128)(2,1)S(1)}, u32[]{:S(2)}, u32[]{:S(2)}) collective-permute-start(bf16[32,2048]{1,0:T(8,128)(2,1)S(1)} %pad_maximum_fusion.refs_0_), channel_id=1, source_target_pairs={{0,4},{4,0},{8,12},{12,8},{1,5},{5,1},{9,13},{13,9},{2,6},{6,2},{1... | collective-permute-start | bytes 393224 | tf_op jit(solution)/shard_map/ppermute | solution.py:156
  9.1 1.1 %collective-permute-start.4 = (s32[1,128]{1,0:T(1,128)S(1)}, s32[1,128]{1,0:T(1,128)S(1)}, u32[]{:S(2)}, u32[]{:S(2)}) collective-permute-start(s32[1,128]{1,0:T(1,128)S(1)} %shard_map.64.own_ref), channel_id=1, source_target_pairs={{0,1},{1,0},{2,3},{3,2},{4,5},{5,4},{6,7},{7,6},{8,9},{9,8},{10,11... | collective-permute-start | bytes 1544 | tf_op jit(solution)/shard_map/ppermute | solution.py:156
  10.2 5.6 %collective-permute-start.5 = (bf16[16,2048]{1,0:T(8,128)(2,1)S(1)}, bf16[16,2048]{1,0:T(8,128)(2,1)S(1)}, u32[]{:S(2)}, u32[]{:S(2)}) collective-permute-start(bf16[16,2048]{1,0:T(8,128)(2,1)S(1)} %collective-permute-done.3.refs_2_), channel_id=1, source_target_pairs={{0,2},{2,0},{1,3},{3,1},{4,6},{6,4},{5,7},{7,5},{8,10},{10,8},{9,1... | collective-permute-start | bytes 196616 | tf_op jit(solution)/shard_map/ppermute | solution.py:156
  13.3 4.3 %collective-permute-start.6 = (bf16[16,2048]{1,0:T(8,128)(2,1)S(1)}, bf16[16,2048]{1,0:T(8,128)(2,1)S(1)}, u32[]{:S(2)}, u32[]{:S(2)}) collective-permute-start(bf16[16,2048]{1,0:T(8,128)(2,1)S(1)} %collective-permute-done.refs_4_), channel_id=1, source_target_pairs={{0,2},{2,0},{1,3},{3,1},{4,6},{6,4},{5,7},{7,5},{8,10},{10,8},{9,1... | collective-permute-start | bytes 196616 | tf_op jit(solution)/shard_map/ppermute | solution.py:156
  13.8 1.2 %copy-start.1 = (bf16[4,256,512]{2,1,0:T(8,128)(2,1)S(1)}, bf16[4,256,512]{2,1,0:T(8,128)(2,1)}, u32[]{:S(2)}) copy-start(bf16[4,256,512]{2,1,0:T(8,128)(2,1)} %refs_3_.1) | copy-start | bytes 3145732
  15.0 2.5 %copy-start.2 = (bf16[4,256,512]{2,1,0:T(8,128)(2,1)S(1)}, bf16[4,256,512]{2,1,0:T(8,128)(2,1)}, u32[]{:S(2)}) copy-start(bf16[4,256,512]{2,1,0:T(8,128)(2,1)} %refs_3_.1) | copy-start | bytes 3145732
  17.5 2.2 %copy-start.4 = (f32[4,256]{1,0:T(4,128)S(1)}, f32[4,256]{1,0:T(4,128)}, u32[]{:S(2)}) copy-start(f32[4,256]{1,0:T(4,128)} %refs_2_.1) | copy-start | bytes 12292
  18.5 1.2 %collective-permute-start.7 = (f32[4,256]{1,0:T(4,128)S(1)}, f32[4,256]{1,0:T(4,128)S(1)}, u32[]{:S(2)}, u32[]{:S(2)}) collective-permute-start(f32[4,256]{1,0:T(4,128)S(1)} %shard_map.66.refs_0_), channel_id=1, source_target_pairs={{0,1},{1,0},{2,3},{3,2},{4,5},{5,4},{6,7},{7,6},{8,9},{9,8},{10,11... | collective-permute-start | bytes 12296 | tf_op jit(solution)/shard_map/ppermute | solution.py:156
  21.0 4.9 %collective-permute-start.10 = (bf16[16,2048]{1,0:T(8,128)(2,1)S(1)}, bf16[16,2048]{1,0:T(8,128)(2,1)S(1)}, u32[]{:S(2)}, u32[]{:S(2)}) collective-permute-start(bf16[16,2048]{1,0:T(8,128)(2,1)S(1)} %get-tuple-element.32), channel_id=1, source_target_pairs={{0,2},{2,0},{1,3},{3,1},{4,6},{6,4},{5,7},{7,5},{8,10},{10,8},{9,1... | collective-permute-start | bytes 196616 | tf_op jit(solution)/shard_map/ppermute | solution.py:156
  21.6 6.3 %collective-permute-start.12 = (bf16[16,2048]{1,0:T(8,128)(2,1)S(1)}, bf16[16,2048]{1,0:T(8,128)(2,1)S(1)}, u32[]{:S(2)}, u32[]{:S(2)}) collective-permute-start(bf16[16,2048]{1,0:T(8,128)(2,1)S(1)} %get-tuple-element.34), channel_id=1, source_target_pairs={{0,2},{2,0},{1,3},{3,1},{4,6},{6,4},{5,7},{7,5},{8,10},{10,8},{9,1... | collective-permute-start | bytes 196616 | tf_op jit(solution)/shard_map/ppermute | solution.py:156
  23.1 6.3 %collective-permute-start.8 = (bf16[32,2048]{1,0:T(8,128)(2,1)S(1)}, bf16[32,2048]{1,0:T(8,128)(2,1)S(1)}, u32[]{:S(2)}, u32[]{:S(2)}) collective-permute-start(bf16[32,2048]{1,0:T(8,128)(2,1)S(1)} %get-tuple-element.30), channel_id=1, source_target_pairs={{0,4},{4,0},{8,12},{12,8},{1,5},{5,1},{9,13},{13,9},{2,6},{6,2},{1... | collective-permute-start | bytes 393224 | tf_op jit(solution)/shard_map/ppermute | solution.py:156
  26.0 6.3 %collective-permute-start.11 = (bf16[16,2048]{1,0:T(8,128)(2,1)S(1)}, bf16[16,2048]{1,0:T(8,128)(2,1)S(1)}, u32[]{:S(2)}, u32[]{:S(2)}) collective-permute-start(bf16[16,2048]{1,0:T(8,128)(2,1)S(1)} %add_convert_fusion.1), channel_id=1, source_target_pairs={{0,8},{4,12},{8,0},{12,4},{1,9},{5,13},{9,1},{13,5},{2,10},{6,14},... | collective-permute-start | bytes 196616 | tf_op jit(solution)/shard_map/ppermute | solution.py:156
  28.0 6.1 %collective-permute-start.13 = (bf16[16,2048]{1,0:T(8,128)(2,1)S(1)}, bf16[16,2048]{1,0:T(8,128)(2,1)S(1)}, u32[]{:S(2)}, u32[]{:S(2)}) collective-permute-start(bf16[16,2048]{1,0:T(8,128)(2,1)S(1)} %add_convert_fusion), channel_id=1, source_target_pairs={{0,12},{4,8},{8,4},{12,0},{1,13},{5,9},{9,5},{13,1},{2,14},{6,10},... | collective-permute-start | bytes 196616 | tf_op jit(solution)/shard_map/ppermute | solution.py:156
  29.4 6.1 %copy-start.3 = (bf16[16,4096]{1,0:T(8,128)(2,1)S(1)}, bf16[16,4096]{1,0:T(8,128)(2,1)}, u32[]{:S(2)}) copy-start(bf16[16,4096]{1,0:T(8,128)(2,1)} %core_ref.1) | copy-start | bytes 393220
  29.4 4.7 %collective-permute-start.9 = (bf16[16,2048]{1,0:T(8,128)(2,1)S(1)}, bf16[16,2048]{1,0:T(8,128)(2,1)S(1)}, u32[]{:S(2)}, u32[]{:S(2)}) collective-permute-start(bf16[16,2048]{1,0:T(8,128)(2,1)S(1)} %slice.17), channel_id=1, source_target_pairs={{0,2},{2,0},{1,3},{3,1},{4,6},{6,4},{5,7},{7,5},{8,10},{10,8},{9,1... | collective-permute-start | bytes 196616 | tf_op jit(solution)/shard_map/ppermute | solution.py:156
  34.2 1.4 %collective-permute-start.14 = (f32[16,2048]{1,0:T(8,128)S(1)}, f32[16,2048]{1,0:T(8,128)S(1)}, u32[]{:S(2)}, u32[]{:S(2)}) collective-permute-start(f32[16,2048]{1,0:T(8,128)S(1)} %fusion.1.mine_ref), channel_id=1, source_target_pairs={{0,1},{1,0},{2,3},{3,2},{4,5},{5,4},{6,7},{7,6},{8,9},{9,8},{10,11... | collective-permute-start | bytes 393224 | tf_op jit(solution)/shard_map/ppermute | solution.py:156

commit v26 on v24

--- a/solution.py
+++ b/solution.py
@@ -185,7 +185,9 @@
 
     mine = lax.dynamic_slice_in_dim(density_blocks, half * wide, wide, 1)
     direct = {dz: swap(mine, "batch", rows_z, dz) for dz in far}
-    beside = [swap(mine, "pair", rows_x, dx) for dx in side]
+    beside = [
+        lax.dynamic_slice_in_dim(swap(density_blocks, "pair", rows_x, dx), half * wide, wide, 1) for dx in side
+    ]
     *beside, own_rows = lax.optimization_barrier((*beside, own_rows))
     cluster = jnp.concatenate([mine, *beside], axis=0)
     arrays, places = [cluster], [list(range(rows_x))]
@@ -251,7 +253,7 @@
     total = cluster[:held]
     for dx in side:
         total = total + swap(cluster[dx * held:(dx + 1) * held].astype(bf16), "pair", rows_x, dx).astype(f32)
-    for term in landed:
+    for term in reversed(landed):
         total = total + term
     total_other = swap(total, "orb", 2, 1)
     return call(

time: 36.5 us -> 36.4 us (level)
    unnamed x14 -> x12, local copies, waits for them, and re-layouts: 2.74 us -> 1.84 us
    dynamic_slice x1, local copies, waits for them, and re-layouts: 0.01 us -> 0.88 us  [per_device(): mine = lax.dynamic_slice_in_dim(density_blocks, half * wide, wide, 1)]
    ppermute x15, starting transfers between devices: 15.5 us -> 15.2 us  [swap(): return lax.ppermute(array, axis, [(i, i ^ step) for i in range(count)])]
  transfers between devices with their start and end apart: 15 -> 15, of which waited for: 8 -> 8; matrix products, arithmetic and copies ran while one was open for 0% -> 3% of each run, Pallas kernels for 3% -> 3%
where the time goes in v26:
time: 36.4 us; the launch traced here: 36.2 us
  starting transfers between devices  15.2 us (42%)
  waiting for transfers between devices  14 us (38%)
  Pallas kernels  3.95 us (11%)
  local copies, waits for them, and re-layouts  2.82 us (8%)
    ppermute x15, starting transfers between devices, swap(): return lax.ppermute(array, axis, [(i, i ^ step) for i in range(count)])  15.2 us
    ppermute x15, waiting for transfers between devices, swap(): return lax.ppermute(array, axis, [(i, i ^ step) for i in range(count)])  14 us
    unnamed x12, local copies, waits for them, and re-layouts  1.84 us
    pallas_call x1, Pallas kernels, per_device(): call(functools.partial(scatter_kernel, out_places), [jax.ShapeDtypeStruct...  1.29 us
    pallas_call x1, Pallas kernels, per_device(): call(functools.partial(density_kernel, places), jax.ShapeDtypeStruct((bat...  0.97 us
    dynamic_slice x1, local copies, waits for them, and re-layouts, per_device(): mine = lax.dynamic_slice_in_dim(density_blocks, half * wide, wide, 1)  0.88 us
    pallas_call x1, Pallas kernels, per_device(): call(prepare_kernel, (jax.ShapeDtypeStruct((batches, points, kept), bf16)...  0.77 us
    pallas_call x1, Pallas kernels, per_device(): call(finish_kernel, jax.ShapeDtypeStruct((held, square), f32), 3, scalars...  0.73 us
  transfers between devices with their start and end apart: 15, of which 8 were waited for; matrix products, arithmetic and copies ran while one was open for 3% of the time, Pallas kernels for 3%

profile of v26, /device:TPU:0, one launch (start us, length us, event | category | flops | bytes accessed | tf_op | source)
XLA Modules:
  0.0 36.2 jit_solution(359481081825360442)
XLA Ops:
  0.0 2.9 %collective-permute-start.1 = (bf16[16,4096]{1,0:T(8,128)(2,1)}, bf16[16,4096]{1,0:T(8,128)(2,1)S(1)}, u32[]{:S(2)}, u32[]{:S(2)}) collective-permute-start(bf16[16,4096]{1,0:T(8,128)(2,1)} %param.10), channel_id=1, source_target_pairs={{0,2},{2,0},{1,3},{3,1},{4,6},{6,4},{5,7},{7,5},{8,10},{10,8},{9,1... | collective-permute-start | bytes 393224 | tf_op jit(solution)/shard_map/ppermute | solution.py:158
  2.9 0.0 copy-start.5
  2.9 0.9 %constant_dynamic-slice_fusion.1 = bf16[16,2048]{1,0:T(8,128)(2,1)S(1)} fusion(bf16[16,4096]{1,0:T(8,128)(2,1)} %param.10, s32[]{:T(128)S(6)} %select_n.4), kind=kLoop, calls=%fused_computation.9 | loop fusion | bytes 131076 | tf_op jit(solution)/shard_map/dynamic_slice | solution.py:186
  3.8 2.6 %collective-permute-start.3 = (bf16[16,2048]{1,0:T(8,128)(2,1)S(1)}, bf16[16,2048]{1,0:T(8,128)(2,1)S(1)}, u32[]{:S(2)}, u32[]{:S(2)}) collective-permute-start(bf16[16,2048]{1,0:T(8,128)(2,1)S(1)} %constant_dynamic-slice_fusion.1), channel_id=1, source_target_pairs={{0,8},{4,12},{8,0},{12,4},{1,9},{5,13},{9,1},{13,5},{2,10},{6,14},... | collective-permute-start | bytes 196616 | tf_op jit(solution)/shard_map/ppermute | solution.py:158
  6.4 1.3 %collective-permute-start = (bf16[16,2048]{1,0:T(8,128)(2,1)S(1)}, bf16[16,2048]{1,0:T(8,128)(2,1)S(1)}, u32[]{:S(2)}, u32[]{:S(2)}) collective-permute-start(bf16[16,2048]{1,0:T(8,128)(2,1)S(1)} %constant_dynamic-slice_fusion.1), channel_id=1, source_target_pairs={{0,12},{4,8},{8,4},{12,0},{1,13},{5,9},{9,5},{13,1},{2,14},{6,10},... | collective-permute-start | bytes 196616 | tf_op jit(solution)/shard_map/ppermute | solution.py:158
  7.8 0.0 copy-done.5
  7.8 0.0 copy-start.4
  7.8 0.1 reshape.14.slots_ref
  7.9 0.6 %copy-done.4 = s32[1,1,8,8]{3,2,1,0:T(8,128)S(1)} copy-done((s32[1,1,8,8]{3,2,1,0:T(8,128)S(1)}, s32[1,1,8,8]{3,2,1,0:T(8,128)}, u32[]{:S(2)}) %copy-start.4) | copy-done | bytes 280
  8.4 0.2 shard_map.64.own_ref
  8.6 0.0 collective-permute-done.1
  8.7 0.3 collective-permute-start.2
  9.0 0.0 collective-permute-start.4
  9.0 1.1 %collective-permute-done.4.other_ref = s32[1,128]{1,0:T(1,128)S(1)} collective-permute-done((s32[1,128]{1,0:T(1,128)S(1)}, s32[1,128]{1,0:T(1,128)S(1)}, u32[]{:S(2)}, u32[]{:S(2)}) %collective-permute-start.4) | collective-permute-done | bytes 544 | tf_op jit(solution)/shard_map/ppermute | solution.py:158
  10.1 0.0 collective-permute-done.3.refs_2_
  10.1 1.1 %collective-permute-start.5 = (bf16[16,2048]{1,0:T(8,128)(2,1)S(1)}, bf16[16,2048]{1,0:T(8,128)(2,1)S(1)}, u32[]{:S(2)}, u32[]{:S(2)}) collective-permute-start(bf16[16,2048]{1,0:T(8,128)(2,1)S(1)} %collective-permute-done.3.refs_2_), channel_id=1, source_target_pairs={{0,2},{2,0},{1,3},{3,1},{4,6},{6,4},{5,7},{7,5},{8,10},{10,8},{9,1... | collective-permute-start | bytes 196616 | tf_op jit(solution)/shard_map/ppermute | solution.py:158
  11.2 2.0 %collective-permute-done.refs_4_ = bf16[16,2048]{1,0:T(8,128)(2,1)S(1)} collective-permute-done((bf16[16,2048]{1,0:T(8,128)(2,1)S(1)}, bf16[16,2048]{1,0:T(8,128)(2,1)S(1)}, u32[]{:S(2)}, u32[]{:S(2)}) %collective-permute-start) | collective-permute-done | bytes 65568 | tf_op jit(solution)/shard_map/ppermute | solution.py:158
  13.2 0.5 %collective-permute-start.6 = (bf16[16,2048]{1,0:T(8,128)(2,1)S(1)}, bf16[16,2048]{1,0:T(8,128)(2,1)S(1)}, u32[]{:S(2)}, u32[]{:S(2)}) collective-permute-start(bf16[16,2048]{1,0:T(8,128)(2,1)S(1)} %collective-permute-done.refs_4_), channel_id=1, source_target_pairs={{0,2},{2,0},{1,3},{3,1},{4,6},{6,4},{5,7},{7,5},{8,10},{10,8},{9,1... | collective-permute-start | bytes 196616 | tf_op jit(solution)/shard_map/ppermute | solution.py:158
  13.7 0.0 copy-start
  13.7 1.2 %copy-done = bf16[4,256,512]{2,1,0:T(8,128)(2,1)S(1)} copy-done((bf16[4,256,512]{2,1,0:T(8,128)(2,1)S(1)}, bf16[4,256,512]{2,1,0:T(8,128)(2,1)}, u32[]{:S(2)}) %copy-start) | copy-done | bytes 1048600
  14.9 0.0 copy-start.1
  14.9 0.8 %shard_map.65 = (bf16[4,256,256]{2,1,0:T(8,128)(2,1)S(1)}, bf16[4,256,256]{2,1,0:T(8,128)(2,1)S(1)}, bf16[256,128]{1,0:T(8,128)(2,1)S(1)}, bf16[128,512]{1,0:T(8,128)(2,1)S(1)}) custom-call(s32[1]{0:T(128)} %bitcast.3.place_ref, s32[1]{0:T(128)} %bitcast.half_ref, bf16[4,256,512]{2,1,0:T(8,128)(2,1)S(1)} %copy-done, s32[1,128]{1,0:T(1,128)S(1)} %shard_map.64.own_ref, ...), custom_call_target="tpu_custom_call" | custom-call | flops 536870912 | bytes 3145728 | tf_op jit(solution)/shard_map/pallas_call | solution.py:207
  15.7 0.0 collective-permute-done.5.refs_3_
  15.7 1.7 %collective-permute-done.6.refs_5_ = bf16[16,2048]{1,0:T(8,128)(2,1)S(1)} collective-permute-done((bf16[16,2048]{1,0:T(8,128)(2,1)S(1)}, bf16[16,2048]{1,0:T(8,128)(2,1)S(1)}, u32[]{:S(2)}, u32[]{:S(2)}) %collective-permute-start.6) | collective-permute-done | bytes 65568 | tf_op jit(solution)/shard_map/ppermute | solution.py:158
  17.4 0.0 collective-permute-done.2.refs_1_
  17.4 0.0 copy-done.1
  17.4 1.0 %shard_map.66.refs_0_ = f32[4,256]{1,0:T(4,128)S(1)} custom-call(bf16[32,2048]{1,0:T(8,128)(2,1)S(1)} %pad_maximum_fusion.refs_0_, bf16[32,2048]{1,0:T(8,128)(2,1)S(1)} %collective-permute-done.2.refs_1_, bf16[16,2048]{1,0:T(8,128)(2,1)S(1)} %collective-permute-done.3.refs_2_, bf16[16,2048]{1,0:T(8,128)(2,1)S(1)} %collective-permute-done.5.refs_3_, ...), custom_call_target="tpu_custom_call" | custom-call | flops 268435456 | bytes 2097152 | tf_op jit(solution)/shard_map/pallas_call | solution.py:222
  18.4 0.1 collective-permute-start.7
  18.5 1.2 %collective-permute-done.7.refs_1_ = f32[4,256]{1,0:T(4,128)S(1)} collective-permute-done((f32[4,256]{1,0:T(4,128)S(1)}, f32[4,256]{1,0:T(4,128)S(1)}, u32[]{:S(2)}, u32[]{:S(2)}) %collective-permute-start.7) | collective-permute-done | bytes 4128 | tf_op jit(solution)/shard_map/ppermute | solution.py:158
  19.7 0.0 copy-done.3
  19.7 1.3 %shard_map.67 = (bf16[32,2048]{1,0:T(8,128)(2,1)S(1)}, bf16[32,2048]{1,0:T(8,128)(2,1)S(1)}, bf16[16,2048]{1,0:T(8,128)(2,1)S(1)}, bf16[16,2048]{1,0:T(8,128)(2,...) custom-call(f32[4,256]{1,0:T(4,128)S(1)} %shard_map.66.refs_0_, ...), custom_call_target="tpu_custom_call" | custom-call | flops 268435456 | bytes 2097152 | tf_op jit(solution)/shard_map/pallas_call | solution.py:234
  20.9 0.6 %collective-permute-start.10 = (bf16[16,2048]{1,0:T(8,128)(2,1)S(1)}, bf16[16,2048]{1,0:T(8,128)(2,1)S(1)}, u32[]{:S(2)}, u32[]{:S(2)}) collective-permute-start(bf16[16,2048]{1,0:T(8,128)(2,1)S(1)} %get-tuple-element.32), channel_id=1, source_target_pairs={{0,2},{2,0},{1,3},{3,1},{4,6},{6,4},{5,7},{7,5},{8,10},{10,8},{9,1... | collective-permute-start | bytes 196616 | tf_op jit(solution)/shard_map/ppermute | solution.py:158
  21.5 1.5 %collective-permute-start.12 = (bf16[16,2048]{1,0:T(8,128)(2,1)S(1)}, bf16[16,2048]{1,0:T(8,128)(2,1)S(1)}, u32[]{:S(2)}, u32[]{:S(2)}) collective-permute-start(bf16[16,2048]{1,0:T(8,128)(2,1)S(1)} %get-tuple-element.34), channel_id=1, source_target_pairs={{0,2},{2,0},{1,3},{3,1},{4,6},{6,4},{5,7},{7,5},{8,10},{10,8},{9,1... | collective-permute-start | bytes 196616 | tf_op jit(solution)/shard_map/ppermute | solution.py:158
  23.0 0.1 collective-permute-start.8
  23.1 2.7 %collective-permute-done.10 = bf16[16,2048]{1,0:T(8,128)(2,1)S(1)} collective-permute-done((bf16[16,2048]{1,0:T(8,128)(2,1)S(1)}, bf16[16,2048]{1,0:T(8,128)(2,1)S(1)}, u32[]{:S(2)}, u32[]{:S(2)}) %collective-permute-start.10) | collective-permute-done | bytes 65568 | tf_op jit(solution)/shard_map/ppermute | solution.py:158
  25.9 2.4 %collective-permute-start.11 = (bf16[16,2048]{1,0:T(8,128)(2,1)S(1)}, bf16[16,2048]{1,0:T(8,128)(2,1)S(1)}, u32[]{:S(2)}, u32[]{:S(2)}) collective-permute-start(bf16[16,2048]{1,0:T(8,128)(2,1)S(1)} %add_convert_fusion.1), channel_id=1, source_target_pairs={{0,12},{4,8},{8,4},{12,0},{1,13},{5,9},{9,5},{13,1},{2,14},{6,10},... | collective-permute-start | bytes 196616 | tf_op jit(solution)/shard_map/ppermute | solution.py:158
  28.3 0.0 collective-permute-done.12
  28.4 0.2 collective-permute-start.13
  28.6 0.0 collective-permute-done.8
  28.6 0.0 copy-start.2
  28.6 1.4 %collective-permute-start.9 = (bf16[16,2048]{1,0:T(8,128)(2,1)S(1)}, bf16[16,2048]{1,0:T(8,128)(2,1)S(1)}, u32[]{:S(2)}, u32[]{:S(2)}) collective-permute-start(bf16[16,2048]{1,0:T(8,128)(2,1)S(1)} %slice.17), channel_id=1, source_target_pairs={{0,2},{2,0},{1,3},{3,1},{4,6},{6,4},{5,7},{7,5},{8,10},{10,8},{9,1... | collective-permute-start | bytes 196616 | tf_op jit(solution)/shard_map/ppermute | solution.py:158
  30.1 2.1 %collective-permute-done.11 = bf16[16,2048]{1,0:T(8,128)(2,1)S(1)} collective-permute-done((bf16[16,2048]{1,0:T(8,128)(2,1)S(1)}, bf16[16,2048]{1,0:T(8,128)(2,1)S(1)}, u32[]{:S(2)}, u32[]{:S(2)}) %collective-permute-start.11) | collective-permute-done | bytes 65568 | tf_op jit(solution)/shard_map/ppermute | solution.py:158
  32.1 1.9 %collective-permute-done.13 = bf16[16,2048]{1,0:T(8,128)(2,1)S(1)} collective-permute-done((bf16[16,2048]{1,0:T(8,128)(2,1)S(1)}, bf16[16,2048]{1,0:T(8,128)(2,1)S(1)}, u32[]{:S(2)}, u32[]{:S(2)}) %collective-permute-start.13) | collective-permute-done | bytes 65568 | tf_op jit(solution)/shard_map/ppermute | solution.py:158
  34.0 0.0 collective-permute-done.9
  34.0 0.1 collective-permute-start.14
  34.1 1.3 %collective-permute-done.14.other_ref = f32[16,2048]{1,0:T(8,128)S(1)} collective-permute-done((f32[16,2048]{1,0:T(8,128)S(1)}, f32[16,2048]{1,0:T(8,128)S(1)}, u32[]{:S(2)}, u32[]{:S(2)}) %collective-permute-start.14) | collective-permute-done | bytes 131104 | tf_op jit(solution)/shard_map/ppermute | solution.py:158
  35.5 0.0 copy-done.2
  35.5 0.7 %shard_map.68 = f32[16,4096]{1,0:T(8,128)} custom-call(s32[1]{0:T(128)} %bitcast.half_ref, f32[16,2048]{1,0:T(8,128)S(1)} %fusion.1.mine_ref, f32[16,2048]{1,0:T(8,128)S(1)} %collective-permute-done.14.other_ref, bf16[16,4096]{1,0:T(8,128)(2,1)S(1)} %copy-done.2), custom_call_target="tpu_custom_call" | custom-call | bytes 786432 | tf_op jit(solution)/shard_map/pallas_call | solution.py:259
  (8 shorter events, 0.1 us)
Async XLA Ops:
  0.0 8.6 %collective-permute-start.1 = (bf16[16,4096]{1,0:T(8,128)(2,1)}, bf16[16,4096]{1,0:T(8,128)(2,1)S(1)}, u32[]{:S(2)}, u32[]{:S(2)}) collective-permute-start(bf16[16,4096]{1,0:T(8,128)(2,1)} %param.10), channel_id=1, source_target_pairs={{0,2},{2,0},{1,3},{3,1},{4,6},{6,4},{5,7},{7,5},{8,10},{10,8},{9,1... | collective-permute-start | bytes 393224 | tf_op jit(solution)/shard_map/ppermute | solution.py:158
  2.9 4.8 %copy-start.5 = (s32[4,8,4]{1,2,0:T(4,128)S(1)}, s32[4,8,4]{1,2,0:T(4,128)}, u32[]{:S(2)}) copy-start(s32[4,8,4]{1,2,0:T(4,128)} %param.8) | copy-start | bytes 1540
  3.8 6.3 %collective-permute-start.3 = (bf16[16,2048]{1,0:T(8,128)(2,1)S(1)}, bf16[16,2048]{1,0:T(8,128)(2,1)S(1)}, u32[]{:S(2)}, u32[]{:S(2)}) collective-permute-start(bf16[16,2048]{1,0:T(8,128)(2,1)S(1)} %constant_dynamic-slice_fusion.1), channel_id=1, source_target_pairs={{0,8},{4,12},{8,0},{12,4},{1,9},{5,13},{9,1},{13,5},{2,10},{6,14},... | collective-permute-start | bytes 196616 | tf_op jit(solution)/shard_map/ppermute | solution.py:158
  6.4 6.8 %collective-permute-start = (bf16[16,2048]{1,0:T(8,128)(2,1)S(1)}, bf16[16,2048]{1,0:T(8,128)(2,1)S(1)}, u32[]{:S(2)}, u32[]{:S(2)}) collective-permute-start(bf16[16,2048]{1,0:T(8,128)(2,1)S(1)} %constant_dynamic-slice_fusion.1), channel_id=1, source_target_pairs={{0,12},{4,8},{8,4},{12,0},{1,13},{5,9},{9,5},{13,1},{2,14},{6,10},... | collective-permute-start | bytes 196616 | tf_op jit(solution)/shard_map/ppermute | solution.py:158
  7.8 0.7 %copy-start.4 = (s32[1,1,8,8]{3,2,1,0:T(8,128)S(1)}, s32[1,1,8,8]{3,2,1,0:T(8,128)}, u32[]{:S(2)}) copy-start(s32[1,1,8,8]{3,2,1,0:T(8,128)} %param.9) | copy-start | bytes 772
  8.7 8.8 %collective-permute-start.2 = (bf16[32,2048]{1,0:T(8,128)(2,1)S(1)}, bf16[32,2048]{1,0:T(8,128)(2,1)S(1)}, u32[]{:S(2)}, u32[]{:S(2)}) collective-permute-start(bf16[32,2048]{1,0:T(8,128)(2,1)S(1)} %pad_maximum_fusion.refs_0_), channel_id=1, source_target_pairs={{0,4},{4,0},{8,12},{12,8},{1,5},{5,1},{9,13},{13,9},{2,6},{6,2},{1... | collective-permute-start | bytes 393224 | tf_op jit(solution)/shard_map/ppermute | solution.py:158
  9.0 1.1 %collective-permute-start.4 = (s32[1,128]{1,0:T(1,128)S(1)}, s32[1,128]{1,0:T(1,128)S(1)}, u32[]{:S(2)}, u32[]{:S(2)}) collective-permute-start(s32[1,128]{1,0:T(1,128)S(1)} %shard_map.64.own_ref), channel_id=1, source_target_pairs={{0,1},{1,0},{2,3},{3,2},{4,5},{5,4},{6,7},{7,6},{8,9},{9,8},{10,11... | collective-permute-start | bytes 1544 | tf_op jit(solution)/shard_map/ppermute | solution.py:158
  10.1 5.6 %collective-permute-start.5 = (bf16[16,2048]{1,0:T(8,128)(2,1)S(1)}, bf16[16,2048]{1,0:T(8,128)(2,1)S(1)}, u32[]{:S(2)}, u32[]{:S(2)}) collective-permute-start(bf16[16,2048]{1,0:T(8,128)(2,1)S(1)} %collective-permute-done.3.refs_2_), channel_id=1, source_target_pairs={{0,2},{2,0},{1,3},{3,1},{4,6},{6,4},{5,7},{7,5},{8,10},{10,8},{9,1... | collective-permute-start | bytes 196616 | tf_op jit(solution)/shard_map/ppermute | solution.py:158
  13.2 4.3 %collective-permute-start.6 = (bf16[16,2048]{1,0:T(8,128)(2,1)S(1)}, bf16[16,2048]{1,0:T(8,128)(2,1)S(1)}, u32[]{:S(2)}, u32[]{:S(2)}) collective-permute-start(bf16[16,2048]{1,0:T(8,128)(2,1)S(1)} %collective-permute-done.refs_4_), channel_id=1, source_target_pairs={{0,2},{2,0},{1,3},{3,1},{4,6},{6,4},{5,7},{7,5},{8,10},{10,8},{9,1... | collective-permute-start | bytes 196616 | tf_op jit(solution)/shard_map/ppermute | solution.py:158
  13.7 1.2 %copy-start = (bf16[4,256,512]{2,1,0:T(8,128)(2,1)S(1)}, bf16[4,256,512]{2,1,0:T(8,128)(2,1)}, u32[]{:S(2)}) copy-start(bf16[4,256,512]{2,1,0:T(8,128)(2,1)} %refs_3_.1) | copy-start | bytes 3145732
  14.9 2.5 %copy-start.1 = (bf16[4,256,512]{2,1,0:T(8,128)(2,1)S(1)}, bf16[4,256,512]{2,1,0:T(8,128)(2,1)}, u32[]{:S(2)}) copy-start(bf16[4,256,512]{2,1,0:T(8,128)(2,1)} %refs_3_.1) | copy-start | bytes 3145732
  17.4 2.2 %copy-start.3 = (f32[4,256]{1,0:T(4,128)S(1)}, f32[4,256]{1,0:T(4,128)}, u32[]{:S(2)}) copy-start(f32[4,256]{1,0:T(4,128)} %refs_2_.1) | copy-start | bytes 12292
  18.4 1.2 %collective-permute-start.7 = (f32[4,256]{1,0:T(4,128)S(1)}, f32[4,256]{1,0:T(4,128)S(1)}, u32[]{:S(2)}, u32[]{:S(2)}) collective-permute-start(f32[4,256]{1,0:T(4,128)S(1)} %shard_map.66.refs_0_), channel_id=1, source_target_pairs={{0,1},{1,0},{2,3},{3,2},{4,5},{5,4},{6,7},{7,6},{8,9},{9,8},{10,11... | collective-permute-start | bytes 12296 | tf_op jit(solution)/shard_map/ppermute | solution.py:158
  20.9 4.9 %collective-permute-start.10 = (bf16[16,2048]{1,0:T(8,128)(2,1)S(1)}, bf16[16,2048]{1,0:T(8,128)(2,1)S(1)}, u32[]{:S(2)}, u32[]{:S(2)}) collective-permute-start(bf16[16,2048]{1,0:T(8,128)(2,1)S(1)} %get-tuple-element.32), channel_id=1, source_target_pairs={{0,2},{2,0},{1,3},{3,1},{4,6},{6,4},{5,7},{7,5},{8,10},{10,8},{9,1... | collective-permute-start | bytes 196616 | tf_op jit(solution)/shard_map/ppermute | solution.py:158
  21.5 6.8 %collective-permute-start.12 = (bf16[16,2048]{1,0:T(8,128)(2,1)S(1)}, bf16[16,2048]{1,0:T(8,128)(2,1)S(1)}, u32[]{:S(2)}, u32[]{:S(2)}) collective-permute-start(bf16[16,2048]{1,0:T(8,128)(2,1)S(1)} %get-tuple-element.34), channel_id=1, source_target_pairs={{0,2},{2,0},{1,3},{3,1},{4,6},{6,4},{5,7},{7,5},{8,10},{10,8},{9,1... | collective-permute-start | bytes 196616 | tf_op jit(solution)/shard_map/ppermute | solution.py:158
  23.0 5.5 %collective-permute-start.8 = (bf16[32,2048]{1,0:T(8,128)(2,1)S(1)}, bf16[32,2048]{1,0:T(8,128)(2,1)S(1)}, u32[]{:S(2)}, u32[]{:S(2)}) collective-permute-start(bf16[32,2048]{1,0:T(8,128)(2,1)S(1)} %get-tuple-element.30), channel_id=1, source_target_pairs={{0,4},{4,0},{8,12},{12,8},{1,5},{5,1},{9,13},{13,9},{2,6},{6,2},{1... | collective-permute-start | bytes 393224 | tf_op jit(solution)/shard_map/ppermute | solution.py:158
  25.9 6.2 %collective-permute-start.11 = (bf16[16,2048]{1,0:T(8,128)(2,1)S(1)}, bf16[16,2048]{1,0:T(8,128)(2,1)S(1)}, u32[]{:S(2)}, u32[]{:S(2)}) collective-permute-start(bf16[16,2048]{1,0:T(8,128)(2,1)S(1)} %add_convert_fusion.1), channel_id=1, source_target_pairs={{0,12},{4,8},{8,4},{12,0},{1,13},{5,9},{9,5},{13,1},{2,14},{6,10},... | collective-permute-start | bytes 196616 | tf_op jit(solution)/shard_map/ppermute | solution.py:158
  28.4 5.6 %collective-permute-start.13 = (bf16[16,2048]{1,0:T(8,128)(2,1)S(1)}, bf16[16,2048]{1,0:T(8,128)(2,1)S(1)}, u32[]{:S(2)}, u32[]{:S(2)}) collective-permute-start(bf16[16,2048]{1,0:T(8,128)(2,1)S(1)} %add_convert_fusion), channel_id=1, source_target_pairs={{0,8},{4,12},{8,0},{12,4},{1,9},{5,13},{9,1},{13,5},{2,10},{6,14},... | collective-permute-start | bytes 196616 | tf_op jit(solution)/shard_map/ppermute | solution.py:158
  28.6 6.8 %copy-start.2 = (bf16[16,4096]{1,0:T(8,128)(2,1)S(1)}, bf16[16,4096]{1,0:T(8,128)(2,1)}, u32[]{:S(2)}) copy-start(bf16[16,4096]{1,0:T(8,128)(2,1)} %core_ref.1) | copy-start | bytes 393220
  28.6 5.4 %collective-permute-start.9 = (bf16[16,2048]{1,0:T(8,128)(2,1)S(1)}, bf16[16,2048]{1,0:T(8,128)(2,1)S(1)}, u32[]{:S(2)}, u32[]{:S(2)}) collective-permute-start(bf16[16,2048]{1,0:T(8,128)(2,1)S(1)} %slice.17), channel_id=1, source_target_pairs={{0,2},{2,0},{1,3},{3,1},{4,6},{6,4},{5,7},{7,5},{8,10},{10,8},{9,1... | collective-permute-start | bytes 196616 | tf_op jit(solution)/shard_map/ppermute | solution.py:158
  34.0 1.4 %collective-permute-start.14 = (f32[16,2048]{1,0:T(8,128)S(1)}, f32[16,2048]{1,0:T(8,128)S(1)}, u32[]{:S(2)}, u32[]{:S(2)}) collective-permute-start(f32[16,2048]{1,0:T(8,128)S(1)} %fusion.1.mine_ref), channel_id=1, source_target_pairs={{0,1},{1,0},{2,3},{3,2},{4,5},{5,4},{6,7},{7,6},{8,9},{9,8},{10,11... | collective-permute-start | bytes 393224 | tf_op jit(solution)/shard_map/ppermute | solution.py:158

commit v27 on v26

--- a/solution.py
+++ b/solution.py
@@ -194,7 +194,7 @@
     for dz in near:
         arrays.append(swap(cluster, "batch", rows_z, dz))
         places.append(list(range(dz * rows_x, (dz + 1) * rows_x)))
-    direct[far[0]], other_rows = lax.optimization_barrier((direct[far[0]], other_rows))
+    direct[far[-1]], other_rows = lax.optimization_barrier((direct[far[-1]], other_rows))
     for dz in far:
         arrays.append(direct[dz])
         places.append([dz * rows_x])

time: 36.4 us -> 37.2 us (1.022)
  starting transfers between devices: 15.2 us -> 15.7 us
    ppermute x15, starting transfers between devices: 15.2 us -> 15.7 us  [swap(): return lax.ppermute(array, axis, [(i, i ^ step) for i in range(count)])]
  transfers between devices with their start and end apart: 15 -> 15, of which waited for: 8 -> 9; matrix products, arithmetic and copies ran while one was open for 3% -> 3% of each run, Pallas kernels for 3% -> 3%
where the time goes in v27:
time: 37.2 us; the launch traced here: 36.9 us
  starting transfers between devices  15.7 us (42%)
  waiting for transfers between devices  14.2 us (38%)
  Pallas kernels  3.95 us (11%)
  local copies, waits for them, and re-layouts  2.82 us (8%)
    ppermute x15, starting transfers between devices, swap(): return lax.ppermute(array, axis, [(i, i ^ step) for i in range(count)])  15.7 us
    ppermute x15, waiting for transfers between devices, swap(): return lax.ppermute(array, axis, [(i, i ^ step) for i in range(count)])  14.2 us
    unnamed x12, local copies, waits for them, and re-layouts  1.84 us
    pallas_call x1, Pallas kernels, per_device(): call(functools.partial(scatter_kernel, out_places), [jax.ShapeDtypeStruct...  1.29 us
    pallas_call x1, Pallas kernels, per_device(): call(functools.partial(density_kernel, places), jax.ShapeDtypeStruct((bat...  0.97 us
    dynamic_slice x1, local copies, waits for them, and re-layouts, per_device(): mine = lax.dynamic_slice_in_dim(density_blocks, half * wide, wide, 1)  0.88 us
    pallas_call x1, Pallas kernels, per_device(): call(prepare_kernel, (jax.ShapeDtypeStruct((batches, points, kept), bf16)...  0.76 us
  transfers between devices with their start and end apart: 15, of which 9 were waited for; matrix products, arithmetic and copies ran while one was open for 3% of the time, Pallas kernels for 3%

profile of v27, /device:TPU:0, one launch (start us, length us, event | category | flops | bytes accessed | tf_op | source)
XLA Modules:
  0.0 36.9 jit_solution(100393987045630811)
XLA Ops:
  0.0 2.9 %collective-permute-start.2 = (bf16[16,4096]{1,0:T(8,128)(2,1)}, bf16[16,4096]{1,0:T(8,128)(2,1)S(1)}, u32[]{:S(2)}, u32[]{:S(2)}) collective-permute-start(bf16[16,4096]{1,0:T(8,128)(2,1)} %param.10), channel_id=1, source_target_pairs={{0,2},{2,0},{1,3},{3,1},{4,6},{6,4},{5,7},{7,5},{8,10},{10,8},{9,1... | collective-permute-start | bytes 393224 | tf_op jit(solution)/shard_map/ppermute | solution.py:158
  2.9 0.0 copy-start.5
  2.9 0.9 %constant_dynamic-slice_fusion.1 = bf16[16,2048]{1,0:T(8,128)(2,1)S(1)} fusion(bf16[16,4096]{1,0:T(8,128)(2,1)} %param.10, s32[]{:T(128)S(6)} %select_n.4), kind=kLoop, calls=%fused_computation.9 | loop fusion | bytes 131076 | tf_op jit(solution)/shard_map/dynamic_slice | solution.py:186
  3.8 2.6 %collective-permute-start.4 = (bf16[16,2048]{1,0:T(8,128)(2,1)S(1)}, bf16[16,2048]{1,0:T(8,128)(2,1)S(1)}, u32[]{:S(2)}, u32[]{:S(2)}) collective-permute-start(bf16[16,2048]{1,0:T(8,128)(2,1)S(1)} %constant_dynamic-slice_fusion.1), channel_id=1, source_target_pairs={{0,8},{4,12},{8,0},{12,4},{1,9},{5,13},{9,1},{13,5},{2,10},{6,14},... | collective-permute-start | bytes 196616 | tf_op jit(solution)/shard_map/ppermute | solution.py:158
  6.4 1.3 %collective-permute-start = (bf16[16,2048]{1,0:T(8,128)(2,1)S(1)}, bf16[16,2048]{1,0:T(8,128)(2,1)S(1)}, u32[]{:S(2)}, u32[]{:S(2)}) collective-permute-start(bf16[16,2048]{1,0:T(8,128)(2,1)S(1)} %constant_dynamic-slice_fusion.1), channel_id=1, source_target_pairs={{0,12},{4,8},{8,4},{12,0},{1,13},{5,9},{9,5},{13,1},{2,14},{6,10},... | collective-permute-start | bytes 196616 | tf_op jit(solution)/shard_map/ppermute | solution.py:158
  7.8 0.0 copy-done.5
  7.8 0.0 copy-start.4
  7.8 0.1 reshape.14.slots_ref
  7.9 0.6 %copy-done.4 = s32[1,1,8,8]{3,2,1,0:T(8,128)S(1)} copy-done((s32[1,1,8,8]{3,2,1,0:T(8,128)S(1)}, s32[1,1,8,8]{3,2,1,0:T(8,128)}, u32[]{:S(2)}) %copy-start.4) | copy-done | bytes 280
  8.4 0.2 shard_map.64.own_ref
  8.6 0.0 collective-permute-done.2
  8.7 0.3 collective-permute-start.3
  9.0 0.0 collective-permute-start.1
  9.0 1.1 %collective-permute-done.1.other_ref = s32[1,128]{1,0:T(1,128)S(1)} collective-permute-done((s32[1,128]{1,0:T(1,128)S(1)}, s32[1,128]{1,0:T(1,128)S(1)}, u32[]{:S(2)}, u32[]{:S(2)}) %collective-permute-start.1) | collective-permute-done | bytes 544 | tf_op jit(solution)/shard_map/ppermute | solution.py:158
  10.1 3.1 %collective-permute-done.refs_4_ = bf16[16,2048]{1,0:T(8,128)(2,1)S(1)} collective-permute-done((bf16[16,2048]{1,0:T(8,128)(2,1)S(1)}, bf16[16,2048]{1,0:T(8,128)(2,1)S(1)}, u32[]{:S(2)}, u32[]{:S(2)}) %collective-permute-start) | collective-permute-done | bytes 65568 | tf_op jit(solution)/shard_map/ppermute | solution.py:158
  13.2 0.0 collective-permute-done.4.refs_2_
  13.2 0.5 %collective-permute-start.5 = (bf16[16,2048]{1,0:T(8,128)(2,1)S(1)}, bf16[16,2048]{1,0:T(8,128)(2,1)S(1)}, u32[]{:S(2)}, u32[]{:S(2)}) collective-permute-start(bf16[16,2048]{1,0:T(8,128)(2,1)S(1)} %collective-permute-done.4.refs_2_), channel_id=1, source_target_pairs={{0,2},{2,0},{1,3},{3,1},{4,6},{6,4},{5,7},{7,5},{8,10},{10,8},{9,1... | collective-permute-start | bytes 196616 | tf_op jit(solution)/shard_map/ppermute | solution.py:158
  13.7 1.5 %collective-permute-start.6 = (bf16[16,2048]{1,0:T(8,128)(2,1)S(1)}, bf16[16,2048]{1,0:T(8,128)(2,1)S(1)}, u32[]{:S(2)}, u32[]{:S(2)}) collective-permute-start(bf16[16,2048]{1,0:T(8,128)(2,1)S(1)} %collective-permute-done.refs_4_), channel_id=1, source_target_pairs={{0,2},{2,0},{1,3},{3,1},{4,6},{6,4},{5,7},{7,5},{8,10},{10,8},{9,1... | collective-permute-start | bytes 196616 | tf_op jit(solution)/shard_map/ppermute | solution.py:158
  15.2 0.0 copy-start
  15.2 1.2 %copy-done = bf16[4,256,512]{2,1,0:T(8,128)(2,1)S(1)} copy-done((bf16[4,256,512]{2,1,0:T(8,128)(2,1)S(1)}, bf16[4,256,512]{2,1,0:T(8,128)(2,1)}, u32[]{:S(2)}) %copy-start) | copy-done | bytes 1048600
  16.4 0.0 copy-start.1
  16.4 0.8 %shard_map.65 = (bf16[4,256,256]{2,1,0:T(8,128)(2,1)S(1)}, bf16[4,256,256]{2,1,0:T(8,128)(2,1)S(1)}, bf16[256,128]{1,0:T(8,128)(2,1)S(1)}, bf16[128,512]{1,0:T(8,128)(2,1)S(1)}) custom-call(s32[1]{0:T(128)} %bitcast.3.place_ref, s32[1]{0:T(128)} %bitcast.half_ref, bf16[4,256,512]{2,1,0:T(8,128)(2,1)S(1)} %copy-done, s32[1,128]{1,0:T(1,128)S(1)} %shard_map.64.own_ref, ...), custom_call_target="tpu_custom_call" | custom-call | flops 536870912 | bytes 3145728 | tf_op jit(solution)/shard_map/pallas_call | solution.py:207
  17.2 0.2 collective-permute-done.5.refs_3_
  17.4 0.7 %collective-permute-done.6.refs_5_ = bf16[16,2048]{1,0:T(8,128)(2,1)S(1)} collective-permute-done((bf16[16,2048]{1,0:T(8,128)(2,1)S(1)}, bf16[16,2048]{1,0:T(8,128)(2,1)S(1)}, u32[]{:S(2)}, u32[]{:S(2)}) %collective-permute-start.6) | collective-permute-done | bytes 65568 | tf_op jit(solution)/shard_map/ppermute | solution.py:158
  18.1 0.0 collective-permute-done.3.refs_1_
  18.1 0.0 copy-done.1
  18.2 1.0 %shard_map.66.refs_0_ = f32[4,256]{1,0:T(4,128)S(1)} custom-call(bf16[32,2048]{1,0:T(8,128)(2,1)S(1)} %pad_maximum_fusion.refs_0_, bf16[32,2048]{1,0:T(8,128)(2,1)S(1)} %collective-permute-done.3.refs_1_, bf16[16,2048]{1,0:T(8,128)(2,1)S(1)} %collective-permute-done.4.refs_2_, bf16[16,2048]{1,0:T(8,128)(2,1)S(1)} %collective-permute-done.5.refs_3_, ...), custom_call_target="tpu_custom_call" | custom-call | flops 268435456 | bytes 2097152 | tf_op jit(solution)/shard_map/pallas_call | solution.py:222
  19.1 0.1 collective-permute-start.7
  19.2 1.2 %collective-permute-done.7.refs_1_ = f32[4,256]{1,0:T(4,128)S(1)} collective-permute-done((f32[4,256]{1,0:T(4,128)S(1)}, f32[4,256]{1,0:T(4,128)S(1)}, u32[]{:S(2)}, u32[]{:S(2)}) %collective-permute-start.7) | collective-permute-done | bytes 4128 | tf_op jit(solution)/shard_map/ppermute | solution.py:158
  20.4 0.0 copy-done.3
  20.4 1.3 %shard_map.67 = (bf16[32,2048]{1,0:T(8,128)(2,1)S(1)}, bf16[32,2048]{1,0:T(8,128)(2,1)S(1)}, bf16[16,2048]{1,0:T(8,128)(2,1)S(1)}, bf16[16,2048]{1,0:T(8,128)(2,...) custom-call(f32[4,256]{1,0:T(4,128)S(1)} %shard_map.66.refs_0_, ...), custom_call_target="tpu_custom_call" | custom-call | flops 268435456 | bytes 2097152 | tf_op jit(solution)/shard_map/pallas_call | solution.py:234
  21.7 1.4 %collective-permute-start.10 = (bf16[16,2048]{1,0:T(8,128)(2,1)S(1)}, bf16[16,2048]{1,0:T(8,128)(2,1)S(1)}, u32[]{:S(2)}, u32[]{:S(2)}) collective-permute-start(bf16[16,2048]{1,0:T(8,128)(2,1)S(1)} %get-tuple-element.32), channel_id=1, source_target_pairs={{0,2},{2,0},{1,3},{3,1},{4,6},{6,4},{5,7},{7,5},{8,10},{10,8},{9,1... | collective-permute-start | bytes 196616 | tf_op jit(solution)/shard_map/ppermute | solution.py:158
  23.0 0.7 %collective-permute-start.12 = (bf16[16,2048]{1,0:T(8,128)(2,1)S(1)}, bf16[16,2048]{1,0:T(8,128)(2,1)S(1)}, u32[]{:S(2)}, u32[]{:S(2)}) collective-permute-start(bf16[16,2048]{1,0:T(8,128)(2,1)S(1)} %get-tuple-element.34), channel_id=1, source_target_pairs={{0,2},{2,0},{1,3},{3,1},{4,6},{6,4},{5,7},{7,5},{8,10},{10,8},{9,1... | collective-permute-start | bytes 196616 | tf_op jit(solution)/shard_map/ppermute | solution.py:158
  23.7 0.1 collective-permute-start.8
  23.9 2.6 %collective-permute-done.10 = bf16[16,2048]{1,0:T(8,128)(2,1)S(1)} collective-permute-done((bf16[16,2048]{1,0:T(8,128)(2,1)S(1)}, bf16[16,2048]{1,0:T(8,128)(2,1)S(1)}, u32[]{:S(2)}, u32[]{:S(2)}) %collective-permute-start.10) | collective-permute-done | bytes 65568 | tf_op jit(solution)/shard_map/ppermute | solution.py:158
  26.5 1.9 %collective-permute-start.11 = (bf16[16,2048]{1,0:T(8,128)(2,1)S(1)}, bf16[16,2048]{1,0:T(8,128)(2,1)S(1)}, u32[]{:S(2)}, u32[]{:S(2)}) collective-permute-start(bf16[16,2048]{1,0:T(8,128)(2,1)S(1)} %add_convert_fusion.1), channel_id=1, source_target_pairs={{0,12},{4,8},{8,4},{12,0},{1,13},{5,9},{9,5},{13,1},{2,14},{6,10},... | collective-permute-start | bytes 196616 | tf_op jit(solution)/shard_map/ppermute | solution.py:158
  28.3 0.0 collective-permute-done.12
  28.4 1.1 %collective-permute-start.13 = (bf16[16,2048]{1,0:T(8,128)(2,1)S(1)}, bf16[16,2048]{1,0:T(8,128)(2,1)S(1)}, u32[]{:S(2)}, u32[]{:S(2)}) collective-permute-start(bf16[16,2048]{1,0:T(8,128)(2,1)S(1)} %add_convert_fusion), channel_id=1, source_target_pairs={{0,8},{4,12},{8,0},{12,4},{1,9},{5,13},{9,1},{13,5},{2,10},{6,14},... | collective-permute-start | bytes 196616 | tf_op jit(solution)/shard_map/ppermute | solution.py:158
  29.5 0.0 collective-permute-done.8
  29.6 0.0 copy-start.2
  29.6 1.2 %collective-permute-start.9 = (bf16[16,2048]{1,0:T(8,128)(2,1)S(1)}, bf16[16,2048]{1,0:T(8,128)(2,1)S(1)}, u32[]{:S(2)}, u32[]{:S(2)}) collective-permute-start(bf16[16,2048]{1,0:T(8,128)(2,1)S(1)} %slice.17), channel_id=1, source_target_pairs={{0,2},{2,0},{1,3},{3,1},{4,6},{6,4},{5,7},{7,5},{8,10},{10,8},{9,1... | collective-permute-start | bytes 196616 | tf_op jit(solution)/shard_map/ppermute | solution.py:158
  30.7 1.9 %collective-permute-done.11 = bf16[16,2048]{1,0:T(8,128)(2,1)S(1)} collective-permute-done((bf16[16,2048]{1,0:T(8,128)(2,1)S(1)}, bf16[16,2048]{1,0:T(8,128)(2,1)S(1)}, u32[]{:S(2)}, u32[]{:S(2)}) %collective-permute-start.11) | collective-permute-done | bytes 65568 | tf_op jit(solution)/shard_map/ppermute | solution.py:158
  32.6 2.1 %collective-permute-done.13 = bf16[16,2048]{1,0:T(8,128)(2,1)S(1)} collective-permute-done((bf16[16,2048]{1,0:T(8,128)(2,1)S(1)}, bf16[16,2048]{1,0:T(8,128)(2,1)S(1)}, u32[]{:S(2)}, u32[]{:S(2)}) %collective-permute-start.13) | collective-permute-done | bytes 65568 | tf_op jit(solution)/shard_map/ppermute | solution.py:158
  34.7 0.0 collective-permute-done.9
  34.8 0.1 collective-permute-start.14
  34.9 1.3 %collective-permute-done.14.other_ref = f32[16,2048]{1,0:T(8,128)S(1)} collective-permute-done((f32[16,2048]{1,0:T(8,128)S(1)}, f32[16,2048]{1,0:T(8,128)S(1)}, u32[]{:S(2)}, u32[]{:S(2)}) %collective-permute-start.14) | collective-permute-done | bytes 131104 | tf_op jit(solution)/shard_map/ppermute | solution.py:158
  36.2 0.0 copy-done.2
  36.2 0.7 %shard_map.68 = f32[16,4096]{1,0:T(8,128)} custom-call(s32[1]{0:T(128)} %bitcast.half_ref, f32[16,2048]{1,0:T(8,128)S(1)} %fusion.1.mine_ref, f32[16,2048]{1,0:T(8,128)S(1)} %collective-permute-done.14.other_ref, bf16[16,4096]{1,0:T(8,128)(2,1)S(1)} %copy-done.2), custom_call_target="tpu_custom_call" | custom-call | bytes 786432 | tf_op jit(solution)/shard_map/pallas_call | solution.py:259
  (8 shorter events, 0.1 us)
Async XLA Ops:
  0.0 8.6 %collective-permute-start.2 = (bf16[16,4096]{1,0:T(8,128)(2,1)}, bf16[16,4096]{1,0:T(8,128)(2,1)S(1)}, u32[]{:S(2)}, u32[]{:S(2)}) collective-permute-start(bf16[16,4096]{1,0:T(8,128)(2,1)} %param.10), channel_id=1, source_target_pairs={{0,2},{2,0},{1,3},{3,1},{4,6},{6,4},{5,7},{7,5},{8,10},{10,8},{9,1... | collective-permute-start | bytes 393224 | tf_op jit(solution)/shard_map/ppermute | solution.py:158
  2.9 4.8 %copy-start.5 = (s32[4,8,4]{1,2,0:T(4,128)S(1)}, s32[4,8,4]{1,2,0:T(4,128)}, u32[]{:S(2)}) copy-start(s32[4,8,4]{1,2,0:T(4,128)} %param.8) | copy-start | bytes 1540
  3.8 9.4 %collective-permute-start.4 = (bf16[16,2048]{1,0:T(8,128)(2,1)S(1)}, bf16[16,2048]{1,0:T(8,128)(2,1)S(1)}, u32[]{:S(2)}, u32[]{:S(2)}) collective-permute-start(bf16[16,2048]{1,0:T(8,128)(2,1)S(1)} %constant_dynamic-slice_fusion.1), channel_id=1, source_target_pairs={{0,8},{4,12},{8,0},{12,4},{1,9},{5,13},{9,1},{13,5},{2,10},{6,14},... | collective-permute-start | bytes 196616 | tf_op jit(solution)/shard_map/ppermute | solution.py:158
  6.4 6.8 %collective-permute-start = (bf16[16,2048]{1,0:T(8,128)(2,1)S(1)}, bf16[16,2048]{1,0:T(8,128)(2,1)S(1)}, u32[]{:S(2)}, u32[]{:S(2)}) collective-permute-start(bf16[16,2048]{1,0:T(8,128)(2,1)S(1)} %constant_dynamic-slice_fusion.1), channel_id=1, source_target_pairs={{0,12},{4,8},{8,4},{12,0},{1,13},{5,9},{9,5},{13,1},{2,14},{6,10},... | collective-permute-start | bytes 196616 | tf_op jit(solution)/shard_map/ppermute | solution.py:158
  7.8 0.7 %copy-start.4 = (s32[1,1,8,8]{3,2,1,0:T(8,128)S(1)}, s32[1,1,8,8]{3,2,1,0:T(8,128)}, u32[]{:S(2)}) copy-start(s32[1,1,8,8]{3,2,1,0:T(8,128)} %param.9) | copy-start | bytes 772
  8.7 9.5 %collective-permute-start.3 = (bf16[32,2048]{1,0:T(8,128)(2,1)S(1)}, bf16[32,2048]{1,0:T(8,128)(2,1)S(1)}, u32[]{:S(2)}, u32[]{:S(2)}) collective-permute-start(bf16[32,2048]{1,0:T(8,128)(2,1)S(1)} %pad_maximum_fusion.refs_0_), channel_id=1, source_target_pairs={{0,4},{4,0},{8,12},{12,8},{1,5},{5,1},{9,13},{13,9},{2,6},{6,2},{1... | collective-permute-start | bytes 393224 | tf_op jit(solution)/shard_map/ppermute | solution.py:158
  9.0 1.1 %collective-permute-start.1 = (s32[1,128]{1,0:T(1,128)S(1)}, s32[1,128]{1,0:T(1,128)S(1)}, u32[]{:S(2)}, u32[]{:S(2)}) collective-permute-start(s32[1,128]{1,0:T(1,128)S(1)} %shard_map.64.own_ref), channel_id=1, source_target_pairs={{0,1},{1,0},{2,3},{3,2},{4,5},{5,4},{6,7},{7,6},{8,9},{9,8},{10,11... | collective-permute-start | bytes 1544 | tf_op jit(solution)/shard_map/ppermute | solution.py:158
  13.2 4.3 %collective-permute-start.5 = (bf16[16,2048]{1,0:T(8,128)(2,1)S(1)}, bf16[16,2048]{1,0:T(8,128)(2,1)S(1)}, u32[]{:S(2)}, u32[]{:S(2)}) collective-permute-start(bf16[16,2048]{1,0:T(8,128)(2,1)S(1)} %collective-permute-done.4.refs_2_), channel_id=1, source_target_pairs={{0,2},{2,0},{1,3},{3,1},{4,6},{6,4},{5,7},{7,5},{8,10},{10,8},{9,1... | collective-permute-start | bytes 196616 | tf_op jit(solution)/shard_map/ppermute | solution.py:158
  13.7 4.4 %collective-permute-start.6 = (bf16[16,2048]{1,0:T(8,128)(2,1)S(1)}, bf16[16,2048]{1,0:T(8,128)(2,1)S(1)}, u32[]{:S(2)}, u32[]{:S(2)}) collective-permute-start(bf16[16,2048]{1,0:T(8,128)(2,1)S(1)} %collective-permute-done.refs_4_), channel_id=1, source_target_pairs={{0,2},{2,0},{1,3},{3,1},{4,6},{6,4},{5,7},{7,5},{8,10},{10,8},{9,1... | collective-permute-start | bytes 196616 | tf_op jit(solution)/shard_map/ppermute | solution.py:158
  15.2 1.2 %copy-start = (bf16[4,256,512]{2,1,0:T(8,128)(2,1)S(1)}, bf16[4,256,512]{2,1,0:T(8,128)(2,1)}, u32[]{:S(2)}) copy-start(bf16[4,256,512]{2,1,0:T(8,128)(2,1)} %refs_3_.1) | copy-start | bytes 3145732
  16.4 1.7 %copy-start.1 = (bf16[4,256,512]{2,1,0:T(8,128)(2,1)S(1)}, bf16[4,256,512]{2,1,0:T(8,128)(2,1)}, u32[]{:S(2)}) copy-start(bf16[4,256,512]{2,1,0:T(8,128)(2,1)} %refs_3_.1) | copy-start | bytes 3145732
  18.2 2.2 %copy-start.3 = (f32[4,256]{1,0:T(4,128)S(1)}, f32[4,256]{1,0:T(4,128)}, u32[]{:S(2)}) copy-start(f32[4,256]{1,0:T(4,128)} %refs_2_.1) | copy-start | bytes 12292
  19.1 1.2 %collective-permute-start.7 = (f32[4,256]{1,0:T(4,128)S(1)}, f32[4,256]{1,0:T(4,128)S(1)}, u32[]{:S(2)}, u32[]{:S(2)}) collective-permute-start(f32[4,256]{1,0:T(4,128)S(1)} %shard_map.66.refs_0_), channel_id=1, source_target_pairs={{0,1},{1,0},{2,3},{3,2},{4,5},{5,4},{6,7},{7,6},{8,9},{9,8},{10,11... | collective-permute-start | bytes 12296 | tf_op jit(solution)/shard_map/ppermute | solution.py:158
  21.7 4.8 %collective-permute-start.10 = (bf16[16,2048]{1,0:T(8,128)(2,1)S(1)}, bf16[16,2048]{1,0:T(8,128)(2,1)S(1)}, u32[]{:S(2)}, u32[]{:S(2)}) collective-permute-start(bf16[16,2048]{1,0:T(8,128)(2,1)S(1)} %get-tuple-element.32), channel_id=1, source_target_pairs={{0,2},{2,0},{1,3},{3,1},{4,6},{6,4},{5,7},{7,5},{8,10},{10,8},{9,1... | collective-permute-start | bytes 196616 | tf_op jit(solution)/shard_map/ppermute | solution.py:158
  23.0 5.3 %collective-permute-start.12 = (bf16[16,2048]{1,0:T(8,128)(2,1)S(1)}, bf16[16,2048]{1,0:T(8,128)(2,1)S(1)}, u32[]{:S(2)}, u32[]{:S(2)}) collective-permute-start(bf16[16,2048]{1,0:T(8,128)(2,1)S(1)} %get-tuple-element.34), channel_id=1, source_target_pairs={{0,2},{2,0},{1,3},{3,1},{4,6},{6,4},{5,7},{7,5},{8,10},{10,8},{9,1... | collective-permute-start | bytes 196616 | tf_op jit(solution)/shard_map/ppermute | solution.py:158
  23.7 5.8 %collective-permute-start.8 = (bf16[32,2048]{1,0:T(8,128)(2,1)S(1)}, bf16[32,2048]{1,0:T(8,128)(2,1)S(1)}, u32[]{:S(2)}, u32[]{:S(2)}) collective-permute-start(bf16[32,2048]{1,0:T(8,128)(2,1)S(1)} %get-tuple-element.30), channel_id=1, source_target_pairs={{0,4},{4,0},{8,12},{12,8},{1,5},{5,1},{9,13},{13,9},{2,6},{6,2},{1... | collective-permute-start | bytes 393224 | tf_op jit(solution)/shard_map/ppermute | solution.py:158
  26.5 6.1 %collective-permute-start.11 = (bf16[16,2048]{1,0:T(8,128)(2,1)S(1)}, bf16[16,2048]{1,0:T(8,128)(2,1)S(1)}, u32[]{:S(2)}, u32[]{:S(2)}) collective-permute-start(bf16[16,2048]{1,0:T(8,128)(2,1)S(1)} %add_convert_fusion.1), channel_id=1, source_target_pairs={{0,12},{4,8},{8,4},{12,0},{1,13},{5,9},{9,5},{13,1},{2,14},{6,10},... | collective-permute-start | bytes 196616 | tf_op jit(solution)/shard_map/ppermute | solution.py:158
  28.4 6.4 %collective-permute-start.13 = (bf16[16,2048]{1,0:T(8,128)(2,1)S(1)}, bf16[16,2048]{1,0:T(8,128)(2,1)S(1)}, u32[]{:S(2)}, u32[]{:S(2)}) collective-permute-start(bf16[16,2048]{1,0:T(8,128)(2,1)S(1)} %add_convert_fusion), channel_id=1, source_target_pairs={{0,8},{4,12},{8,0},{12,4},{1,9},{5,13},{9,1},{13,5},{2,10},{6,14},... | collective-permute-start | bytes 196616 | tf_op jit(solution)/shard_map/ppermute | solution.py:158
  29.6 6.6 %copy-start.2 = (bf16[16,4096]{1,0:T(8,128)(2,1)S(1)}, bf16[16,4096]{1,0:T(8,128)(2,1)}, u32[]{:S(2)}) copy-start(bf16[16,4096]{1,0:T(8,128)(2,1)} %core_ref.1) | copy-start | bytes 393220
  29.6 5.2 %collective-permute-start.9 = (bf16[16,2048]{1,0:T(8,128)(2,1)S(1)}, bf16[16,2048]{1,0:T(8,128)(2,1)S(1)}, u32[]{:S(2)}, u32[]{:S(2)}) collective-permute-start(bf16[16,2048]{1,0:T(8,128)(2,1)S(1)} %slice.17), channel_id=1, source_target_pairs={{0,2},{2,0},{1,3},{3,1},{4,6},{6,4},{5,7},{7,5},{8,10},{10,8},{9,1... | collective-permute-start | bytes 196616 | tf_op jit(solution)/shard_map/ppermute | solution.py:158
  34.8 1.4 %collective-permute-start.14 = (f32[16,2048]{1,0:T(8,128)S(1)}, f32[16,2048]{1,0:T(8,128)S(1)}, u32[]{:S(2)}, u32[]{:S(2)}) collective-permute-start(f32[16,2048]{1,0:T(8,128)S(1)} %fusion.1.mine_ref), channel_id=1, source_target_pairs={{0,1},{1,0},{2,3},{3,2},{4,5},{5,4},{6,7},{7,6},{8,9},{9,8},{10,11... | collective-permute-start | bytes 393224 | tf_op jit(solution)/shard_map/ppermute | solution.py:158
